TPU v7x, 32 devices: a whole 2x2x4 slice. The times are simulated.
32 devices in a mesh: elem: 8 (over z, y), orb: 4 (over x, core).
Axes of the slice: x: 2, y: 2, z: 4, core: 2. Of those that a mesh axis runs over, the one named last changes fastest.
Arguments:
- orbitals: bfloat16 [6144, 4096], P('elem', 'orb')
- hamiltonian: bfloat16 [96, 7, 64, 64], P('elem'), may hold values from -0.25 to 0.25
- neighbours: int32 [96, 7], P('elem'), may hold values from 0 to 95, as said below
Outputs:
- updated: bfloat16 [6144, 4096], P('elem', 'orb')
Inputs may be any that keep to these rules, and one draw needn't show every extreme that they name: Elements form tiles of 12 consecutive indices, each tile a periodic 3 x 4 plane of elements in some order, tiles stacked periodically. An element's row lists itself, its two neighbours along each in-plane direction, then the element at the same place in the previous tile and in the next tile.
All inputs are finite; a program needn't handle non-finite values.
Results may differ from a plain program's by a relative error of at most 0.0062.
Values may be sent and summed in bfloat16 or wider, within the bound.
No kernel may reach another device: no remote copies, remote signals or barrier semaphores. Data moves between devices by JAX's collectives and lax.ppermute only.
A program may use at most 64 MiB of HBM per device.

v0:
```python
import jax
import jax.numpy as jnp
from jax import lax
from jax.sharding import PartitionSpec as P


def extended_2(value, sides, width):
    for axis, dim in sides:
        peers, length = (lax.axis_size(axis), value.shape[dim])
        up = [(i, (i + 1) % peers) for i in range(peers)]
        down = [(j, i) for i, j in up]
        last = lax.slice_in_dim(value, length - width, length, axis=dim)
        initial = lax.slice_in_dim(value, 0, width, axis=dim)
        before = lax.ppermute(last, axis, up)
        after = lax.ppermute(initial, axis, down)
        value = jnp.concatenate([before, value, after], axis=dim)
    return value


def neighbour_product(hamiltonian, local_index, field):
    rows, width = field.shape
    elements = hamiltonian.shape[0]
    block_size = hamiltonian.shape[2]
    extended = extended_2(field, (("elem", 0),), rows)
    blocks = extended.reshape(3 * elements, block_size, width)
    picked = blocks[local_index]
    result = jnp.einsum("enab,enbc->eac", hamiltonian, picked, preferred_element_type=jnp.float32)
    return result.reshape(rows, width)


def local(orbitals, hamiltonian, neighbours):
    elements = hamiltonian.shape[0]
    tiles = lax.axis_size("elem")
    my_tile = lax.axis_index("elem")
    other_tile = neighbours // elements
    relative = (other_tile - my_tile + tiles) % tiles
    slot = jnp.where(relative == 0, 1, jnp.where(relative == 1, 2, 0)).astype(jnp.int32)
    local_index = slot * elements + neighbours % elements
    start_field = orbitals.astype(jnp.float32)
    first = neighbour_product(hamiltonian, local_index, orbitals)
    first_half = first.astype(jnp.bfloat16)
    second = 2.0 * neighbour_product(hamiltonian, local_index, first_half) - start_field
    second_half = second.astype(jnp.bfloat16)
    third = 2.0 * neighbour_product(hamiltonian, local_index, second_half) - first
    filtered = third.astype(jnp.bfloat16)
    rows_total = filtered.shape[0] * tiles
    columns = filtered.shape[1]
    groups = lax.axis_size("orb")
    orbital_count = columns * groups
    panel = lax.all_gather(filtered, "orb", axis=1, tiled=True)
    own_squares = jnp.sum(jnp.square(filtered.astype(jnp.float32)))
    total = lax.psum(own_squares, ("elem", "orb"))
    partial_gram = lax.dot_general(
        panel, filtered, (((0,), (0,)), ((), ())), preferred_element_type=jnp.float32
    )
    gram_part = lax.psum_scatter(partial_gram, "elem", scatter_dimension=0, tiled=True)
    level = total / (orbital_count * rows_total)
    scaled_part = (gram_part / (level * rows_total)).astype(jnp.bfloat16)
    scaled = lax.all_gather(scaled_part, "elem", axis=0, tiled=True)
    mixed = jnp.dot(panel, scaled, preferred_element_type=jnp.float32)
    result = (1.5 * filtered.astype(jnp.float32) - 0.5 * mixed) / jnp.sqrt(level)
    return result.astype(jnp.bfloat16)


def solution(mesh):
    return jax.shard_map(
        local,
        mesh=mesh,
        in_specs=(P("elem", "orb"), P("elem", None, None, None), P("elem", None)),
        out_specs=P("elem", "orb"),
        check_vma=False,
    )
```

profile of v0, /device:TPU:0, one launch (start us, length us, event | category | flops | bytes accessed | tf_op | source)
XLA Modules:
  0.0 766.9 jit_solution(16788620688457175232)
XLA Ops:
  6.5 0.0 copy-start
  6.5 0.0 all-gather.3.cloned.1.call-start
  6.5 3.0 collective-permute-start
  9.5 3.0 collective-permute-start.1
  12.5 0.7 compare_select_fusion
  13.3 0.1 copy.5
  13.4 0.1 reshape.24
  13.5 63.7 %collective-permute-done = bf16[768,1024]{1,0:T(8,128)(2,1)S(1)} collective-permute-done((bf16[768,1024]{1,0:T(8,128)(2,1)}, bf16[768,1024]{1,0:T(8,128)(2,1)S(1)}, u32[]{:S(2)}, u32[]{:S(2)}) %collective-permute-start) | collective-permute-done | bytes 1572896 | tf_op jit(solution)/shard_map/ppermute | solution.py:14
  77.2 2.2 collective-permute-done.1
  79.4 3.8 pad_maximum_fusion
  83.2 8.8 %gather_fusion = bf16[84,64,1024]{2,1,0:T(8,128)(2,1)} fusion(bf16[36,64,1024]{2,1,0:T(8,128)(2,1)} %bitcast.47, s32[1024]{0:T(1024)S(1)} %pad_clamp_fusion), kind=kCustom, calls=%fused_computation | custom fusion | bytes 22020432 | tf_op jit(solution)/shard_map/gather | solution.py:26
  92.0 0.0 copy-done
  92.0 7.8 %bitcast_convert_fusion = (bf16[12,1024,64]{1,2,0:T(8,128)(2,1)S(1)}, f32[12,1024,64,1]{1,2,3,0:T(8,128)}) fusion(bf16[12,7,64,64]{3,2,1,0:T(8,128)(2,1)S(1)} %copy-done, bf16[12,7,64,1024]{3,2,1,0:T(8,128)(2,1)} %bitcast.43), kind=kOutput, calls=%fused_computation.12 | convolution fusion | flops 705429504 | bytes 16416768 | tf_op jit(solution)/shard_map/enab,enbc->eac/dot_general | solution.py:27
  99.8 0.2 collective-permute-start.2
  100.0 4.5 collective-permute-start.3
  104.5 62.0 %collective-permute-done.2 = bf16[768,1024]{1,0:T(8,128)(2,1)S(1)} collective-permute-done((bf16[768,1024]{1,0:T(8,128)(2,1)S(1)}, bf16[768,1024]{1,0:T(8,128)(2,1)S(1)}, u32[]{:S(2)}, u32[]{:S(2)}) %collective-permute-start.2) | collective-permute-done | bytes 1572896 | tf_op jit(solution)/shard_map/ppermute | solution.py:14
  166.5 4.0 collective-permute-done.3
  170.5 2.5 pad_maximum_fusion.1
  172.9 8.8 %gather_fusion.1 = bf16[84,64,1024]{2,1,0:T(8,128)(2,1)} fusion(bf16[36,64,1024]{2,1,0:T(8,128)(2,1)} %bitcast.46, s32[1024]{0:T(1024)S(1)} %pad_clamp_fusion), kind=kCustom, calls=%fused_computation.1 | custom fusion | bytes 22020432 | tf_op jit(solution)/shard_map/gather | solution.py:26
  181.7 0.0 copy-start.2
  181.7 6.3 bitcast_multiply_fusion.1
  188.0 0.0 copy-done.2
  188.0 0.6 fusion
  188.7 0.1 collective-permute-start.4
  188.7 4.7 collective-permute-start.5
  193.4 62.5 %collective-permute-done.4 = bf16[768,1024]{1,0:T(8,128)(2,1)S(1)} collective-permute-done((bf16[768,1024]{1,0:T(8,128)(2,1)S(1)}, bf16[768,1024]{1,0:T(8,128)(2,1)S(1)}, u32[]{:S(2)}, u32[]{:S(2)}) %collective-permute-start.4) | collective-permute-done | bytes 1572896 | tf_op jit(solution)/shard_map/ppermute | solution.py:14
  255.9 3.7 collective-permute-done.5
  259.6 2.5 pad_maximum_fusion.2
  262.1 8.8 %gather_fusion.2 = bf16[84,64,1024]{2,1,0:T(8,128)(2,1)} fusion(bf16[36,64,1024]{2,1,0:T(8,128)(2,1)} %bitcast.45, s32[1024]{0:T(1024)S(1)} %pad_clamp_fusion), kind=kCustom, calls=%fused_computation.2 | custom fusion | bytes 22020432 | tf_op jit(solution)/shard_map/gather | solution.py:26
  270.9 8.9 %multiply_reduce_fusion = (f32[]{:T(128)}, bf16[12,1024,64]{1,2,0:T(8,128)(2,1)}) fusion(f32[12,1024,64,1]{1,2,3,0:T(8,128)} %get-tuple-element.6, bf16[12,7,64,64]{3,2,1,0:T(8,128)(2,1)S(1)} %copy-done, bf16[12,7,64,1024]{3,2,1,0:T(8,128)(2,1)} %bitcast.48), kind=kOutput, calls=%fused_computation.14 | convolution fusion | flops 709361664 | bytes 16416772 | tf_op jit(solution)/shard_map/enab,enbc->eac/dot_general | solution.py:27
  279.8 0.0 all-gather.3.cloned.1.call-update
  279.8 0.2 reduce-scatter.2.cloned.1.call-start
  280.1 44.7 %all-gather.3.cloned.1.call-done = bf16[768,4096]{1,0:T(8,128)(2,1)} async-done(((bf16[768,1024]{1,0:T(8,128)(2,1)}), bf16[768,4096]{1,0:T(8,128)(2,1)}) %all-gather.3.cloned.1.call-update) | async-done | bytes 6291472 | tf_op jit(solution)/shard_map/all_gather | solution.py:50
  324.8 12.6 %fusion.8 = f32[4096,1024]{1,0:T(8,128)} fusion(bf16[768,4096]{1,0:T(8,128)(2,1)} %all-gather.3.cloned.1.call-done, bf16[768,1024]{1,0:T(8,128)(2,1)} %bitcast.53), kind=kOutput, calls=%fused_computation.29 | convolution fusion | flops 6442450944 | bytes 24641536 | tf_op jit(solution)/shard_map/dot_general | solution.py:53
  337.3 0.0 reduce-scatter.2.cloned.1.call-update
  337.4 0.0 copy-start.3
  337.4 0.0 all-gather.5.cloned.1.call-start
  337.4 42.2 %psum.7 = f32[]{:T(128)} all-reduce(f32[]{:T(128)} %get-tuple-element.7), channel_id=1, replica_groups=mesh['elem'=8,'orb'=4] {'elem','orb'}, use_global_device_ids=true, to_apply=%region_2.3 | all-reduce | flops 1 | bytes 8 | tf_op jit(solution)/shard_map/psum | solution.py:52
  380.2 241.0 %reduce-scatter.2.cloned.1.call-done = f32[512,1024]{1,0:T(8,128)} async-done(((f32[4096,1024]{1,0:T(8,128)}), f32[512,1024]{1,0:T(8,128)}) %reduce-scatter.2.cloned.1.call-update) | async-done | bytes 2097168 | tf_op jit(solution)/shard_map/reduce_scatter | solution.py:56
  621.2 2.9 divide_convert_fusion.1
  624.1 0.0 all-gather.5.cloned.1.call-update
  624.7 123.5 %all-gather.5.cloned.1.call-done = bf16[4096,1024]{1,0:T(8,128)(2,1)} async-done(((bf16[512,1024]{1,0:T(8,128)(2,1)}), bf16[4096,1024]{1,0:T(8,128)(2,1)}) %all-gather.5.cloned.1.call-update) | async-done | bytes 8388624 | tf_op jit(solution)/shard_map/all_gather | solution.py:59
  748.2 0.0 copy-done.3
  748.2 0.0 copy-start.1
  748.2 12.2 %divide_convert_fusion = bf16[768,1024]{1,0:T(8,128)(2,1)} fusion(bf16[768,1024]{1,0:T(8,128)(2,1)S(1)} %bitcast.54, bf16[768,4096]{1,0:T(8,128)(2,1)} %all-gather.3.cloned.1.call-done, bf16[4096,1024]{1,0:T(8,128)(2,1)} %all-gather.5.cloned.1.call-done, f32[]{:T(128)S(6)} %sqrt.3), kind=kOutput, calls=%fused_computation.13 | convolution fusion | flops 6447169536 | bytes 17825796 | tf_op jit(solution)/shard_map/dot_general | solution.py:60
  760.4 0.0 copy-done.1
  (1 shorter events, 0.0 us)
Async XLA Ops:
  6.5 85.4 %copy-start = (bf16[12,7,64,64]{3,2,1,0:T(8,128)(2,1)S(1)}, bf16[12,7,64,64]{3,2,1,0:T(8,128)(2,1)}, u32[]{:S(2)}) copy-start(bf16[12,7,64,64]{3,2,1,0:T(8,128)(2,1)} %param.4) | copy-start | bytes 2064388
  6.5 318.2 %all-gather.3.cloned.1.call-start = ((), (), s32[]{:S(2)}) async-start(), calls=%async_computation.1 | async-start | bytes 7864320 | tf_op jit(solution)/shard_map/all_gather | solution.py:50
  6.5 70.6 %collective-permute-start = (bf16[768,1024]{1,0:T(8,128)(2,1)}, bf16[768,1024]{1,0:T(8,128)(2,1)S(1)}, u32[]{:S(2)}, u32[]{:S(2)}) collective-permute-start(bf16[768,1024]{1,0:T(8,128)(2,1)} %param.3), channel_id=1, source_target_pairs={{0,4},{4,8},{8,12},{12,16},{16,20},{20,24},{24,28},{28,0},{1,5},{5... | collective-permute-start | bytes 4718600 | tf_op jit(solution)/shard_map/ppermute | solution.py:14
  9.5 69.9 %collective-permute-start.1 = (bf16[768,1024]{1,0:T(8,128)(2,1)}, bf16[768,1024]{1,0:T(8,128)(2,1)}, u32[]{:S(2)}, u32[]{:S(2)}) collective-permute-start(bf16[768,1024]{1,0:T(8,128)(2,1)} %param.3), channel_id=1, source_target_pairs={{4,0},{8,4},{12,8},{16,12},{20,16},{24,20},{28,24},{0,28},{5,1},{9... | collective-permute-start | bytes 4718600 | tf_op jit(solution)/shard_map/ppermute | solution.py:15
  99.8 66.7 %collective-permute-start.2 = (bf16[768,1024]{1,0:T(8,128)(2,1)S(1)}, bf16[768,1024]{1,0:T(8,128)(2,1)S(1)}, u32[]{:S(2)}, u32[]{:S(2)}) collective-permute-start(bf16[768,1024]{1,0:T(8,128)(2,1)S(1)} %bitcast.49), channel_id=1, source_target_pairs={{0,4},{4,8},{8,12},{12,16},{16,20},{20,24},{24,28},{28,0},{1,5},{5... | collective-permute-start | bytes 4718600 | tf_op jit(solution)/shard_map/ppermute | solution.py:14
  100.0 70.5 %collective-permute-start.3 = (bf16[768,1024]{1,0:T(8,128)(2,1)S(1)}, bf16[768,1024]{1,0:T(8,128)(2,1)S(1)}, u32[]{:S(2)}, u32[]{:S(2)}) collective-permute-start(bf16[768,1024]{1,0:T(8,128)(2,1)S(1)} %bitcast.50), channel_id=1, source_target_pairs={{4,0},{8,4},{12,8},{16,12},{20,16},{24,20},{28,24},{0,28},{5,1},{9... | collective-permute-start | bytes 4718600 | tf_op jit(solution)/shard_map/ppermute | solution.py:15
  181.7 6.3 copy-start.2
  188.7 67.2 %collective-permute-start.4 = (bf16[768,1024]{1,0:T(8,128)(2,1)S(1)}, bf16[768,1024]{1,0:T(8,128)(2,1)S(1)}, u32[]{:S(2)}, u32[]{:S(2)}) collective-permute-start(bf16[768,1024]{1,0:T(8,128)(2,1)S(1)} %fusion), channel_id=1, source_target_pairs={{0,4},{4,8},{8,12},{12,16},{16,20},{20,24},{24,28},{28,0},{1,5},{5... | collective-permute-start | bytes 4718600 | tf_op jit(solution)/shard_map/ppermute | solution.py:14
  188.7 70.9 %collective-permute-start.5 = (bf16[768,1024]{1,0:T(8,128)(2,1)S(1)}, bf16[768,1024]{1,0:T(8,128)(2,1)S(1)}, u32[]{:S(2)}, u32[]{:S(2)}) collective-permute-start(bf16[768,1024]{1,0:T(8,128)(2,1)S(1)} %fusion), channel_id=1, source_target_pairs={{4,0},{8,4},{12,8},{16,12},{20,16},{24,20},{28,24},{0,28},{5,1},{9... | collective-permute-start | bytes 4718600 | tf_op jit(solution)/shard_map/ppermute | solution.py:15
  279.8 341.4 %reduce-scatter.2.cloned.1.call-start = ((), (), s32[]{:S(2)}) async-start(), calls=%async_computation.2 | async-start | bytes 18874368 | tf_op jit(solution)/shard_map/reduce_scatter | solution.py:56
  337.4 410.8 %copy-start.3 = (bf16[12,1024,64]{1,2,0:T(8,128)(2,1)S(1)}, bf16[12,1024,64]{1,2,0:T(8,128)(2,1)}, u32[]{:S(2)}) copy-start(bf16[12,1024,64]{1,2,0:T(8,128)(2,1)} %get-tuple-element.8) | copy-start | bytes 4718596
  337.4 410.8 %all-gather.5.cloned.1.call-start = ((), (), s32[]{:S(2)}) async-start(), calls=%async_computation.3 | async-start | bytes 9437184 | tf_op jit(solution)/shard_map/all_gather | solution.py:59
  748.2 12.2 %copy-start.1 = (bf16[12,7,64,64]{3,2,1,0:T(8,128)(2,1)S(1)}, bf16[12,7,64,64]{3,2,1,0:T(8,128)(2,1)}, u32[]{:S(2)}) copy-start(bf16[12,7,64,64]{3,2,1,0:T(8,128)(2,1)} %param.4) | copy-start | bytes 2064388
Sparse Core Ops, SparseCore 0:
  280.0 44.7 all-gather.2
  337.5 283.6 reduce-scatter.1
  624.2 123.9 all-gather.4
where the time goes:
time: 767 us
  waiting for transfers between devices  607 us (79%)
  matrix products  47.8 us (6%)
  blocking collectives  42.2 us (6%)
  local copies, waits for them, and re-layouts  26.6 us (3%)
  starting transfers between devices  15.8 us (2%)
  between operations  14.4 us (2%)
  other arithmetic  12.9 us (2%)
    reduce_scatter x1, waiting for transfers between devices, local(): lax.psum_scatter(partial_gram, 'elem', scatter_dimension=0, tiled=True)  241 us
    ppermute x3, waiting for transfers between devices, extended_2(): before = lax.ppermute(last, axis, up)  188 us
    all_gather x1, waiting for transfers between devices, local(): scaled = lax.all_gather(scaled_part, 'elem', axis=0, tiled=True)  123 us
    all_gather x1, waiting for transfers between devices, local(): panel = lax.all_gather(filtered, 'orb', axis=1, tiled=True)  44.7 us
    psum x1, blocking collectives, local(): total = lax.psum(own_squares, ('elem', 'orb'))  42.2 us
    gather x3, local copies, waits for them, and re-layouts, neighbour_product(): picked = blocks[local_index]  26.4 us
    dot_general x3, matrix products, neighbour_product(): jnp.einsum('enab,enbc->eac', hamiltonian, picked, preferred_element_type=...  23 us
  transfers between devices with their start and end apart: 9, of which 9 were waited for; matrix products, arithmetic and copies ran while one was open for 0% of the time, Pallas kernels for 0%

commit v1 on v0

v1 whole, which is shorter than its diff:
```python
import functools

import jax
import jax.numpy as jnp
from jax import lax
from jax.experimental import pallas as pl
from jax.experimental.pallas import tpu as pltpu
from jax.sharding import PartitionSpec as P

CHUNKS = 4
F32 = jnp.float32
BF16 = jnp.bfloat16


def dense_operator(blocks, place):
    elements, slots, size, _ = blocks.shape
    hot = place[:, :, None] == jnp.arange(elements, dtype=place.dtype)
    full = jnp.zeros((elements, size, elements, size), blocks.dtype)
    for slot in range(slots):
        mask = hot[:, slot][:, None, :, None]
        full = jnp.where(mask, blocks[:, slot][:, :, None, :], full)
    return full.reshape(elements * size, elements * size)


def product_kernel(stage, own_ref, near_ref, far_ref, field_ref, by_near_ref, by_far_ref, *refs):
    def accumulate(operator_ref, value_ref):
        return jnp.dot(operator_ref[...], value_ref[...], preferred_element_type=F32)

    total = accumulate(own_ref, field_ref) + accumulate(near_ref, by_near_ref) + accumulate(far_ref, by_far_ref)
    if stage == 0:
        wide_ref, half_ref = refs
        wide_ref[...] = total
        half_ref[...] = total.astype(BF16)
    elif stage == 1:
        before_ref, half_ref = refs
        half_ref[...] = (2.0 * total - before_ref[...].astype(F32)).astype(BF16)
    else:
        before_ref, half_ref, squares_ref = refs
        value = (2.0 * total - before_ref[...]).astype(BF16)
        half_ref[...] = value
        wide = value.astype(F32)
        squares_ref[...] = jnp.sum((wide * wide).reshape(-1, 8, wide.shape[1]), axis=0)


def product(stage, operators, field, by_near, by_far, before=None):
    rows, width = field.shape
    half = jax.ShapeDtypeStruct((rows, width), BF16)
    wide = jax.ShapeDtypeStruct((rows, width), F32)
    squares = jax.ShapeDtypeStruct((8, width), F32)
    outs = ((wide, half), half, (half, squares))[stage]
    args = (*operators, field, by_near, by_far) + (() if before is None else (before,))
    return pl.pallas_call(
        functools.partial(product_kernel, stage),
        out_shape=outs,
        in_specs=[pl.BlockSpec(memory_space=pltpu.VMEM)] * len(args),
        compiler_params=pltpu.CompilerParams(vmem_limit_bytes=32 * 1024 * 1024),
        cost_estimate=pl.CostEstimate(
            flops=6 * rows * rows * width, bytes_accessed=6 * rows * rows + 16 * rows * width, transcendentals=0
        ),
        name=f"product_{stage}",
    )(*args)


def local(orbitals, hamiltonian, neighbours):
    elements = hamiltonian.shape[0]
    rows, columns = orbitals.shape
    tiles = lax.axis_size("elem")
    groups = lax.axis_size("orb")
    lines = tiles // 2
    odd = lax.axis_index("elem") % 2

    swap = [(i, i ^ 1) for i in range(tiles)]
    forward = []
    for line in range(lines):
        forward.append((2 * line, 2 * ((line + 1) % lines)))
        forward.append((2 * line + 1, 2 * ((line - 1) % lines) + 1))

    place = neighbours % elements
    own = dense_operator(hamiltonian[:, :5], place[:, :5])
    previous, following = (dense_operator(hamiltonian[:, s : s + 1], place[:, s : s + 1]) for s in (5, 6))
    near = jnp.where(odd == 0, following, previous)
    far = jnp.where(odd == 0, previous, following)
    operators = (own, near, far)

    width = columns // CHUNKS
    start = [lax.slice_in_dim(orbitals, c * width, (c + 1) * width, axis=1) for c in range(CHUNKS)]

    def step(stage, fields, before):
        out = []
        for field, old in zip(fields, before):
            by_near = lax.ppermute(field, "elem", swap)
            by_far = lax.ppermute(by_near, "elem", forward)
            out.append(product(stage, operators, field, by_near, by_far, old))
        return out

    firsts = step(0, start, [None] * CHUNKS)
    seconds = step(1, [half for _, half in firsts], start)
    thirds = step(2, seconds, [wide for wide, _ in firsts])

    own_squares = sum(jnp.sum(squares) for _, squares in thirds)
    total = jnp.sum(lax.all_gather(jnp.full((8, 128), own_squares, F32), ("elem", "orb"))[:, 0, 0])

    pieces = []
    for value, _ in thirds:
        have = {0: value}
        bit = groups // 2
        while bit:
            peers = [(i, i ^ bit) for i in range(groups)]
            for known in list(have):
                have[known | bit] = lax.ppermute(have[known], "orb", peers)
            bit //= 2
        pieces.append(have)
    panel = jnp.concatenate([pieces[c][d] for d in range(groups) for c in range(CHUNKS)], axis=1)
    filtered = panel[:, :columns]

    rows_total = rows * tiles
    orbital_count = columns * groups
    level = total / (orbital_count * rows_total)
    partial_gram = lax.dot_general(panel, filtered, (((0,), (0,)), ((), ())), preferred_element_type=F32).astype(BF16)
    gram_part = lax.psum_scatter(partial_gram, "elem", scatter_dimension=0, tiled=True)
    scaled_part = (gram_part.astype(F32) / (level * rows_total)).astype(BF16)
    scaled = lax.all_gather(scaled_part, "elem", axis=0, tiled=True)
    mixed = jnp.dot(panel, scaled, preferred_element_type=F32)
    result = (1.5 * filtered.astype(F32) - 0.5 * mixed) / jnp.sqrt(level)
    return result.astype(BF16)


def solution(mesh):
    return jax.shard_map(
        local,
        mesh=mesh,
        in_specs=(P("elem", "orb"), P("elem", None, None, None), P("elem", None)),
        out_specs=P("elem", "orb"),
        check_vma=False,
    )
```

time: 767 us -> 490 us (0.64)
  waiting for transfers between devices: 607 us -> 326 us
  matrix products: 47.8 us -> 21 us
  starting transfers between devices: 15.8 us -> 36 us
  Pallas kernels: 0 us -> 17.4 us
  local copies, waits for them, and re-layouts: 26.6 us -> 18 us
    reduce_scatter x1, waiting for transfers between devices: 241 us -> 101 us  [local(): lax.psum_scatter(partial_gram, 'elem', scatter_dimension=0, tiled=True)]
    ppermute x6 -> x36, waiting for transfers between devices: 198 us -> 101 us  [the longest x12 64.8 us: step(): by_near = lax.ppermute(field, 'elem', swap)]
    all_gather x1 -> x0, waiting for transfers between devices: 44.7 us -> none  [local(): panel = lax.all_gather(filtered, 'orb', axis=1, tiled=True)]
    psum x1 -> x0, blocking collectives: 42.2 us -> none  [local(): total = lax.psum(own_squares, ('elem', 'orb'))]
    unnamed x0 -> x1, blocking collectives: none -> 41.4 us
    gather x3 -> x0, local copies, waits for them, and re-layouts: 26.4 us -> none  [neighbour_product(): picked = blocks[local_index]]
    dot_general x4 -> x1, matrix products: 35.2 us -> 12.1 us  [local(): mixed = jnp.dot(panel, scaled, preferred_element_type=F32)]
    ppermute x6 -> x36, starting transfers between devices: 15.5 us -> 35.9 us  [the longest x12 15.7 us: step(): by_near = lax.ppermute(field, 'elem', swap)]
  transfers between devices with their start and end apart: 9 -> 38, of which waited for: 9 -> 21; matrix products, arithmetic and copies ran while one was open for 0% -> 5% of each run, Pallas kernels for 0% -> 4%
where the time goes in v1:
time: 490 us; the launch traced here: 489 us
  waiting for transfers between devices  326 us (67%)
  blocking collectives  41.4 us (8%)
  starting transfers between devices  36 us (7%)
  matrix products  21 us (4%)
  local copies, waits for them, and re-layouts  18 us (4%)
  between operations  18 us (4%)
  Pallas kernels  17.4 us (4%)
  other arithmetic  11.9 us (2%)
    all_gather x1, waiting for transfers between devices, local(): scaled = lax.all_gather(scaled_part, 'elem', axis=0, tiled=True)  123 us
    reduce_scatter x1, waiting for transfers between devices, local(): lax.psum_scatter(partial_gram, 'elem', scatter_dimension=0, tiled=True)  101 us
    ppermute x12, waiting for transfers between devices, step(): by_near = lax.ppermute(field, 'elem', swap)  64.8 us
    unnamed x1, blocking collectives  41.4 us
    ppermute x12, waiting for transfers between devices, local(): have[known | bit] = lax.ppermute(have[known], 'orb', peers)  25.8 us
    pallas_call x12, Pallas kernels, product(): pl.pallas_call(functools.partial(product_kernel, stage), out_shape=outs,...  17.4 us
    ppermute x12, starting transfers between devices, step(): by_near = lax.ppermute(field, 'elem', swap)  15.7 us
    ppermute x12, starting transfers between devices, step(): by_far = lax.ppermute(by_near, 'elem', forward)  14.5 us
  transfers between devices with their start and end apart: 38, of which 21 were waited for; matrix products, arithmetic and copies ran while one was open for 5% of the time, Pallas kernels for 4%

profile of v1, /device:TPU:0, one launch (start us, length us, event | category | flops | bytes accessed | tf_op | source)
XLA Modules:
  0.0 489.3 jit_solution(9476111119170367327)
XLA Ops:
  6.5 1.6 fusion
  8.2 3.0 collective-permute-start.6
  11.3 1.9 collective-permute-start.12
  13.6 2.8 select_select_fusion.2
  16.5 4.7 collective-permute-done.6.by_near_ref
  21.2 2.1 collective-permute-start.7
  23.4 6.3 %collective-permute-done.by_near_ref = bf16[768,256]{1,0:T(8,128)(2,1)} collective-permute-done((bf16[768,256]{1,0:T(8,128)(2,1)S(1)}, bf16[768,256]{1,0:T(8,128)(2,1)}, u32[]{:S(2)}, u32[]{:S(2)}) %collective-permute-start) | collective-permute-done | bytes 393248 | tf_op jit(solution)/shard_map/ppermute | solution.py:91
  29.7 2.1 collective-permute-start.1
  31.8 6.3 %collective-permute-done.12.by_near_ref = bf16[768,256]{1,0:T(8,128)(2,1)} collective-permute-done((bf16[768,256]{1,0:T(8,128)(2,1)S(1)}, bf16[768,256]{1,0:T(8,128)(2,1)}, u32[]{:S(2)}, u32[]{:S(2)}) %collective-permute-start.12) | collective-permute-done | bytes 393248 | tf_op jit(solution)/shard_map/ppermute | solution.py:91
  38.1 2.1 collective-permute-start.13
  40.2 5.5 %collective-permute-done.18.by_near_ref = bf16[768,256]{1,0:T(8,128)(2,1)} collective-permute-done((bf16[768,256]{1,0:T(8,128)(2,1)S(1)}, bf16[768,256]{1,0:T(8,128)(2,1)}, u32[]{:S(2)}, u32[]{:S(2)}) %collective-permute-start.18) | collective-permute-done | bytes 393248 | tf_op jit(solution)/shard_map/ppermute | solution.py:91
  45.7 1.8 collective-permute-start.19
  47.5 3.1 select_select_fusion
  50.6 3.8 select_n.78.near_ref
  54.5 3.9 select_n.80.far_ref
  58.3 3.9 reshape.91.own_ref
  62.2 1.0 copy-done.7
  63.2 2.2 product_0.4
  65.5 3.6 collective-permute-start.2
  69.1 2.2 product_0.5
  71.4 2.2 product_0.6
  73.6 2.0 collective-permute-start.14
  75.7 2.2 product_0.7
  78.0 1.1 collective-permute-done.2.by_near_ref
  79.2 8.4 %collective-permute-done.8.by_near_ref = bf16[768,256]{1,0:T(8,128)(2,1)S(1)} collective-permute-done((bf16[768,256]{1,0:T(8,128)(2,1)S(1)}, bf16[768,256]{1,0:T(8,128)(2,1)S(1)}, u32[]{:S(2)}, u32[]{:S(2)}) %collective-permute-start.8) | collective-permute-done | bytes 393248 | tf_op jit(solution)/shard_map/ppermute | solution.py:91
  87.6 8.4 %collective-permute-done.14.by_near_ref = bf16[768,256]{1,0:T(8,128)(2,1)S(1)} collective-permute-done((bf16[768,256]{1,0:T(8,128)(2,1)S(1)}, bf16[768,256]{1,0:T(8,128)(2,1)S(1)}, u32[]{:S(2)}, u32[]{:S(2)}) %collective-permute-start.14) | collective-permute-done | bytes 393248 | tf_op jit(solution)/shard_map/ppermute | solution.py:91
  96.0 6.3 %collective-permute-done.20.by_near_ref = bf16[768,256]{1,0:T(8,128)(2,1)S(1)} collective-permute-done((bf16[768,256]{1,0:T(8,128)(2,1)S(1)}, bf16[768,256]{1,0:T(8,128)(2,1)S(1)}, u32[]{:S(2)}, u32[]{:S(2)}) %collective-permute-start.20) | collective-permute-done | bytes 393248 | tf_op jit(solution)/shard_map/ppermute | solution.py:91
  102.3 1.1 product_1.4.field_ref
  103.4 2.2 collective-permute-start.4
  105.7 1.1 product_1.5.field_ref
  106.8 1.1 product_1.6.field_ref
  107.9 2.1 collective-permute-start.16
  110.0 4.0 collective-permute-done.21.by_far_ref
  114.0 1.1 product_1.7.field_ref
  115.7 1.6 collective-permute-start.5
  117.3 6.9 %collective-permute-done.10.by_near_ref = bf16[768,256]{1,0:T(8,128)(2,1)S(1)} collective-permute-done((bf16[768,256]{1,0:T(8,128)(2,1)S(1)}, bf16[768,256]{1,0:T(8,128)(2,1)S(1)}, u32[]{:S(2)}, u32[]{:S(2)}) %collective-permute-start.10) | collective-permute-done | bytes 393248 | tf_op jit(solution)/shard_map/ppermute | solution.py:91
  124.1 1.6 collective-permute-start.11
  125.7 6.9 %collective-permute-done.16.by_near_ref = bf16[768,256]{1,0:T(8,128)(2,1)S(1)} collective-permute-done((bf16[768,256]{1,0:T(8,128)(2,1)S(1)}, bf16[768,256]{1,0:T(8,128)(2,1)S(1)}, u32[]{:S(2)}, u32[]{:S(2)}) %collective-permute-start.16) | collective-permute-done | bytes 393248 | tf_op jit(solution)/shard_map/ppermute | solution.py:91
  132.5 1.6 collective-permute-start.17
  134.1 3.7 collective-permute-done.22.by_near_ref
  137.8 1.5 collective-permute-start.23
  139.3 1.1 product_2.4
  140.5 1.6 collective-permute-start.28
  142.0 1.1 product_2.5
  143.3 3.1 collective-permute-done.17.by_far_ref
  146.4 1.1 product_2.6
  147.7 3.7 collective-permute-done.23.by_far_ref
  151.3 1.1 product_2.7
  152.9 1.6 collective-permute-start.29
  155.1 1.6 collective-permute-start.31
  156.9 8.0 %collective-permute-done.29 = bf16[768,256]{1,0:T(8,128)(2,1)S(1)} collective-permute-done((bf16[768,256]{1,0:T(8,128)(2,1)S(1)}, bf16[768,256]{1,0:T(8,128)(2,1)S(1)}, u32[]{:S(2)}, u32[]{:S(2)}) %collective-permute-start.29) | collective-permute-done | bytes 393248 | tf_op jit(solution)/shard_map/ppermute | solution.py:110
  164.9 8.4 %collective-permute-done.30 = bf16[768,256]{1,0:T(8,128)(2,1)S(1)} collective-permute-done((bf16[768,256]{1,0:T(8,128)(2,1)S(1)}, bf16[768,256]{1,0:T(8,128)(2,1)S(1)}, u32[]{:S(2)}, u32[]{:S(2)}) %collective-permute-start.30) | collective-permute-done | bytes 393248 | tf_op jit(solution)/shard_map/ppermute | solution.py:110
  173.3 8.0 %collective-permute-done.31 = bf16[768,256]{1,0:T(8,128)(2,1)S(1)} collective-permute-done((bf16[768,256]{1,0:T(8,128)(2,1)S(1)}, bf16[768,256]{1,0:T(8,128)(2,1)S(1)}, u32[]{:S(2)}, u32[]{:S(2)}) %collective-permute-start.31) | collective-permute-done | bytes 393248 | tf_op jit(solution)/shard_map/ppermute | solution.py:110
  181.5 1.5 collective-permute-done.35
  183.1 2.7 copy-done.16
  185.8 8.9 %convolution_convert_fusion = bf16[4096,1024]{1,0:T(8,128)(2,1)} fusion(bf16[768,4096]{1,0:T(8,128)(2,1)S(1)} %constant_dynamic-update-slice_fusion.4, bf16[768,1024]{1,0:T(8,128)(2,1)S(1)} %get-tuple-element.51), kind=kOutput, calls=%fused_computation | convolution fusion | flops 6446645248 | bytes 16252928 | tf_op jit(solution)/shard_map/dot_general | solution.py:119
  194.8 0.7 reduce_sum.46
  196.8 0.7 reduce_sum.48
  200.2 41.4 %all-reduce = f32[32]{0:T(128)S(1)} all-reduce(f32[32]{0:T(128)S(1)} %dynamic-update-slice), channel_id=2, replica_groups=mesh['elem'=8,'orb'=4] {'elem','orb'}, use_global_device_ids=true, to_apply=%add | all-reduce | flops 32 | bytes 256
  241.7 0.7 reduce_sum.49
  243.0 100.8 %reduce-scatter.2.cloned.1.call-done = bf16[512,1024]{1,0:T(8,128)(2,1)} async-done(((bf16[4096,1024]{1,0:T(8,128)(2,1)}), bf16[512,1024]{1,0:T(8,128)(2,1)}) %reduce-scatter.2.cloned.1.call-update) | async-done | bytes 1048592 | tf_op jit(solution)/shard_map/reduce_scatter | solution.py:120
  343.8 2.4 divide_convert_fusion.1
  347.0 123.4 %all-gather.2.cloned.1.call-done = bf16[4096,1024]{1,0:T(8,128)(2,1)} async-done(((bf16[512,1024]{1,0:T(8,128)(2,1)}), bf16[4096,1024]{1,0:T(8,128)(2,1)}) %all-gather.2.cloned.1.call-update) | async-done | bytes 8388624 | tf_op jit(solution)/shard_map/all_gather | solution.py:122
  470.4 12.1 %divide_convert_fusion = bf16[768,1024]{1,0:T(8,128)(2,1)} fusion(bf16[768,1024]{1,0:T(8,128)(2,1)S(1)} %copy-done.15, bf16[768,4096]{1,0:T(8,128)(2,1)} %copy-done.16, bf16[4096,1024]{1,0:T(8,128)(2,1)} %all-gather.2.cloned.1.call-done, f32[]{:T(128)S(6)} %sqrt.3), kind=kOutput, calls=%fused_computation.3 | convolution fusion | flops 6447169536 | bytes 17825796 | tf_op jit(solution)/shard_map/dot_general | solution.py:123
  (101 shorter events, 5.2 us)
Async XLA Ops:
  6.5 6.8 %copy-start.13 = (bf16[12,7,64,64]{3,2,1,0:T(8,128)(2,1)S(1)}, bf16[12,7,64,64]{3,2,1,0:T(8,128)(2,1)}, u32[]{:S(2)}) copy-start(bf16[12,7,64,64]{3,2,1,0:T(8,128)(2,1)} %param.4) | copy-start | bytes 2064388
  6.5 6.9 %copy-start.17 = (s32[12,7]{0,1:T(8,128)S(1)}, s32[12,7]{0,1:T(8,128)}, u32[]{:S(2)}) copy-start(s32[12,7]{0,1:T(8,128)} %param.5) | copy-start | bytes 1012
  6.5 337.3 %reduce-scatter.2.cloned.1.call-start = ((), (), s32[]{:S(2)}) async-start(), calls=%async_computation.1 | async-start | bytes 9437184 | tf_op jit(solution)/shard_map/reduce_scatter | solution.py:120
  8.1 8.3 %copy-start = (bf16[768,256]{1,0:T(8,128)(2,1)}, bf16[768,256]{1,0:T(8,128)(2,1)S(1)}, u32[]{:S(2)}) copy-start(bf16[768,256]{1,0:T(8,128)(2,1)S(1)} %get-tuple-element.37.field_ref.refs_0_) | copy-start | bytes 1179652
  8.1 8.3 %copy-start.2 = (bf16[768,256]{1,0:T(8,128)(2,1)}, bf16[768,256]{1,0:T(8,128)(2,1)S(1)}, u32[]{:S(2)}) copy-start(bf16[768,256]{1,0:T(8,128)(2,1)S(1)} %get-tuple-element.40.field_ref.refs_0_) | copy-start | bytes 1179652
  8.1 8.3 %copy-start.4 = (bf16[768,256]{1,0:T(8,128)(2,1)}, bf16[768,256]{1,0:T(8,128)(2,1)S(1)}, u32[]{:S(2)}) copy-start(bf16[768,256]{1,0:T(8,128)(2,1)S(1)} %get-tuple-element.38.field_ref.refs_0_) | copy-start | bytes 1179652
  8.2 8.3 %copy-start.6 = (bf16[768,256]{1,0:T(8,128)(2,1)}, bf16[768,256]{1,0:T(8,128)(2,1)S(1)}, u32[]{:S(2)}) copy-start(bf16[768,256]{1,0:T(8,128)(2,1)S(1)} %get-tuple-element.39.field_ref.refs_0_) | copy-start | bytes 1179652
  8.2 13.1 %collective-permute-start.6 = (bf16[768,256]{1,0:T(8,128)(2,1)S(1)}, bf16[768,256]{1,0:T(8,128)(2,1)}, u32[]{:S(2)}, u32[]{:S(2)}) collective-permute-start(bf16[768,256]{1,0:T(8,128)(2,1)S(1)} %get-tuple-element.38.field_ref.refs_0_), channel_id=1, source_target_pairs={{0,4},{4,0},{8,12},{12,8},{16,20},{20,16},{24,28},{28,24},{1,5},{5... | collective-permute-start | bytes 1179656 | tf_op jit(solution)/shard_map/ppermute | solution.py:91
  11.2 18.5 %collective-permute-start = (bf16[768,256]{1,0:T(8,128)(2,1)S(1)}, bf16[768,256]{1,0:T(8,128)(2,1)}, u32[]{:S(2)}, u32[]{:S(2)}) collective-permute-start(bf16[768,256]{1,0:T(8,128)(2,1)S(1)} %get-tuple-element.39.field_ref.refs_0_), channel_id=1, source_target_pairs={{0,4},{4,0},{8,12},{12,8},{16,20},{20,16},{24,28},{28,24},{1,5},{5... | collective-permute-start | bytes 1179656 | tf_op jit(solution)/shard_map/ppermute | solution.py:91
  11.3 26.8 %collective-permute-start.12 = (bf16[768,256]{1,0:T(8,128)(2,1)S(1)}, bf16[768,256]{1,0:T(8,128)(2,1)}, u32[]{:S(2)}, u32[]{:S(2)}) collective-permute-start(bf16[768,256]{1,0:T(8,128)(2,1)S(1)} %get-tuple-element.40.field_ref.refs_0_), channel_id=1, source_target_pairs={{0,4},{4,0},{8,12},{12,8},{16,20},{20,16},{24,28},{28,24},{1,5},{5... | collective-permute-start | bytes 1179656 | tf_op jit(solution)/shard_map/ppermute | solution.py:91
  13.2 32.5 %collective-permute-start.18 = (bf16[768,256]{1,0:T(8,128)(2,1)S(1)}, bf16[768,256]{1,0:T(8,128)(2,1)}, u32[]{:S(2)}, u32[]{:S(2)}) collective-permute-start(bf16[768,256]{1,0:T(8,128)(2,1)S(1)} %get-tuple-element.37.field_ref.refs_0_), channel_id=1, source_target_pairs={{0,4},{4,0},{8,12},{12,8},{16,20},{20,16},{24,28},{28,24},{1,5},{5... | collective-permute-start | bytes 1179656 | tf_op jit(solution)/shard_map/ppermute | solution.py:91
  21.2 47.8 %collective-permute-start.7 = (bf16[768,256]{1,0:T(8,128)(2,1)}, bf16[768,256]{1,0:T(8,128)(2,1)}, u32[]{:S(2)}, u32[]{:S(2)}) collective-permute-start(bf16[768,256]{1,0:T(8,128)(2,1)} %collective-permute-done.6.by_near_ref), channel_id=1, source_target_pairs={{0,8},{4,28},{8,16},{12,4},{16,24},{20,12},{24,0},{28,20},{1,9},{5... | collective-permute-start | bytes 1179656 | tf_op jit(solution)/shard_map/ppermute | solution.py:92
  29.7 32.5 %collective-permute-start.1 = (bf16[768,256]{1,0:T(8,128)(2,1)}, bf16[768,256]{1,0:T(8,128)(2,1)}, u32[]{:S(2)}, u32[]{:S(2)}) collective-permute-start(bf16[768,256]{1,0:T(8,128)(2,1)} %collective-permute-done.by_near_ref), channel_id=1, source_target_pairs={{0,8},{4,28},{8,16},{12,4},{16,24},{20,12},{24,0},{28,20},{1,9},{5... | collective-permute-start | bytes 1179656 | tf_op jit(solution)/shard_map/ppermute | solution.py:92
  38.1 33.3 %collective-permute-start.13 = (bf16[768,256]{1,0:T(8,128)(2,1)}, bf16[768,256]{1,0:T(8,128)(2,1)}, u32[]{:S(2)}, u32[]{:S(2)}) collective-permute-start(bf16[768,256]{1,0:T(8,128)(2,1)} %collective-permute-done.12.by_near_ref), channel_id=1, source_target_pairs={{0,8},{4,28},{8,16},{12,4},{16,24},{20,12},{24,0},{28,20},{1,9},{5... | collective-permute-start | bytes 1179656 | tf_op jit(solution)/shard_map/ppermute | solution.py:92
  45.7 30.0 %collective-permute-start.19 = (bf16[768,256]{1,0:T(8,128)(2,1)}, bf16[768,256]{1,0:T(8,128)(2,1)}, u32[]{:S(2)}, u32[]{:S(2)}) collective-permute-start(bf16[768,256]{1,0:T(8,128)(2,1)} %collective-permute-done.18.by_near_ref), channel_id=1, source_target_pairs={{0,8},{4,28},{8,16},{12,4},{16,24},{20,12},{24,0},{28,20},{1,9},{5... | collective-permute-start | bytes 1179656 | tf_op jit(solution)/shard_map/ppermute | solution.py:92
  62.2 6.9 %copy-start.5 = (bf16[768,256]{1,0:T(8,128)(2,1)S(1)}, bf16[768,256]{1,0:T(8,128)(2,1)}, u32[]{:S(2)}) copy-start(bf16[768,256]{1,0:T(8,128)(2,1)} %copy-done.4) | copy-start | bytes 1179652
  62.2 1.0 copy-start.7
  65.4 6.0 %copy-start.3 = (bf16[768,256]{1,0:T(8,128)(2,1)S(1)}, bf16[768,256]{1,0:T(8,128)(2,1)}, u32[]{:S(2)}) copy-start(bf16[768,256]{1,0:T(8,128)(2,1)} %copy-done.2) | copy-start | bytes 1179652
  65.5 13.6 %collective-permute-start.2 = (bf16[768,256]{1,0:T(8,128)(2,1)S(1)}, bf16[768,256]{1,0:T(8,128)(2,1)S(1)}, u32[]{:S(2)}, u32[]{:S(2)}) collective-permute-start(bf16[768,256]{1,0:T(8,128)(2,1)S(1)} %get-tuple-element.21.field_ref), channel_id=1, source_target_pairs={{0,4},{4,0},{8,12},{12,8},{16,20},{20,16},{24,28},{28,24},{1,5},{5... | collective-permute-start | bytes 1179656 | tf_op jit(solution)/shard_map/ppermute | solution.py:91
  71.3 4.4 copy-start.1
  71.3 16.2 %collective-permute-start.8 = (bf16[768,256]{1,0:T(8,128)(2,1)S(1)}, bf16[768,256]{1,0:T(8,128)(2,1)S(1)}, u32[]{:S(2)}, u32[]{:S(2)}) collective-permute-start(bf16[768,256]{1,0:T(8,128)(2,1)S(1)} %get-tuple-element.24.field_ref), channel_id=1, source_target_pairs={{0,4},{4,0},{8,12},{12,8},{16,20},{20,16},{24,28},{28,24},{1,5},{5... | collective-permute-start | bytes 1179656 | tf_op jit(solution)/shard_map/ppermute | solution.py:91
  73.6 28.7 %copy-start.8 = (bf16[768,256]{1,0:T(8,128)(2,1)S(1)}, bf16[768,256]{1,0:T(8,128)(2,1)}, u32[]{:S(2)}) copy-start(bf16[768,256]{1,0:T(8,128)(2,1)} %copy-done.6) | copy-start | bytes 1179652
  73.6 22.3 %collective-permute-start.14 = (bf16[768,256]{1,0:T(8,128)(2,1)S(1)}, bf16[768,256]{1,0:T(8,128)(2,1)S(1)}, u32[]{:S(2)}, u32[]{:S(2)}) collective-permute-start(bf16[768,256]{1,0:T(8,128)(2,1)S(1)} %get-tuple-element.27.field_ref), channel_id=1, source_target_pairs={{0,4},{4,0},{8,12},{12,8},{16,20},{20,16},{24,28},{28,24},{1,5},{5... | collective-permute-start | bytes 1179656 | tf_op jit(solution)/shard_map/ppermute | solution.py:91
  77.9 24.4 %collective-permute-start.20 = (bf16[768,256]{1,0:T(8,128)(2,1)S(1)}, bf16[768,256]{1,0:T(8,128)(2,1)S(1)}, u32[]{:S(2)}, u32[]{:S(2)}) collective-permute-start(bf16[768,256]{1,0:T(8,128)(2,1)S(1)} %get-tuple-element.30.field_ref), channel_id=1, source_target_pairs={{0,4},{4,0},{8,12},{12,8},{16,20},{20,16},{24,28},{28,24},{1,5},{5... | collective-permute-start | bytes 1179656 | tf_op jit(solution)/shard_map/ppermute | solution.py:91
  79.1 23.2 %collective-permute-start.3 = (bf16[768,256]{1,0:T(8,128)(2,1)S(1)}, bf16[768,256]{1,0:T(8,128)(2,1)S(1)}, u32[]{:S(2)}, u32[]{:S(2)}) collective-permute-start(bf16[768,256]{1,0:T(8,128)(2,1)S(1)} %collective-permute-done.2.by_near_ref), channel_id=1, source_target_pairs={{0,8},{4,28},{8,16},{12,4},{16,24},{20,12},{24,0},{28,20},{1,9},{5... | collective-permute-start | bytes 1179656 | tf_op jit(solution)/shard_map/ppermute | solution.py:92
  87.5 18.1 %collective-permute-start.9 = (bf16[768,256]{1,0:T(8,128)(2,1)S(1)}, bf16[768,256]{1,0:T(8,128)(2,1)S(1)}, u32[]{:S(2)}, u32[]{:S(2)}) collective-permute-start(bf16[768,256]{1,0:T(8,128)(2,1)S(1)} %collective-permute-done.8.by_near_ref), channel_id=1, source_target_pairs={{0,8},{4,28},{8,16},{12,4},{16,24},{20,12},{24,0},{28,20},{1,9},{5... | collective-permute-start | bytes 1179656 | tf_op jit(solution)/shard_map/ppermute | solution.py:92
  96.0 10.9 %collective-permute-start.15 = (bf16[768,256]{1,0:T(8,128)(2,1)S(1)}, bf16[768,256]{1,0:T(8,128)(2,1)S(1)}, u32[]{:S(2)}, u32[]{:S(2)}) collective-permute-start(bf16[768,256]{1,0:T(8,128)(2,1)S(1)} %collective-permute-done.14.by_near_ref), channel_id=1, source_target_pairs={{0,8},{4,28},{8,16},{12,4},{16,24},{20,12},{24,0},{28,20},{1,9},{5... | collective-permute-start | bytes 1179656 | tf_op jit(solution)/shard_map/ppermute | solution.py:92
  102.3 11.6 %collective-permute-start.21 = (bf16[768,256]{1,0:T(8,128)(2,1)S(1)}, bf16[768,256]{1,0:T(8,128)(2,1)S(1)}, u32[]{:S(2)}, u32[]{:S(2)}) collective-permute-start(bf16[768,256]{1,0:T(8,128)(2,1)S(1)} %collective-permute-done.20.by_near_ref), channel_id=1, source_target_pairs={{0,8},{4,28},{8,16},{12,4},{16,24},{20,12},{24,0},{28,20},{1,9},{5... | collective-permute-start | bytes 1179656 | tf_op jit(solution)/shard_map/ppermute | solution.py:92
  103.4 12.3 %collective-permute-start.4 = (bf16[768,256]{1,0:T(8,128)(2,1)S(1)}, bf16[768,256]{1,0:T(8,128)(2,1)S(1)}, u32[]{:S(2)}, u32[]{:S(2)}) collective-permute-start(bf16[768,256]{1,0:T(8,128)(2,1)S(1)} %product_1.4.field_ref), channel_id=1, source_target_pairs={{0,4},{4,0},{8,12},{12,8},{16,20},{20,16},{24,28},{28,24},{1,5},{5... | collective-permute-start | bytes 1179656 | tf_op jit(solution)/shard_map/ppermute | solution.py:91
  106.8 17.4 %collective-permute-start.10 = (bf16[768,256]{1,0:T(8,128)(2,1)S(1)}, bf16[768,256]{1,0:T(8,128)(2,1)S(1)}, u32[]{:S(2)}, u32[]{:S(2)}) collective-permute-start(bf16[768,256]{1,0:T(8,128)(2,1)S(1)} %product_1.5.field_ref), channel_id=1, source_target_pairs={{0,4},{4,0},{8,12},{12,8},{16,20},{20,16},{24,28},{28,24},{1,5},{5... | collective-permute-start | bytes 1179656 | tf_op jit(solution)/shard_map/ppermute | solution.py:91
  107.9 24.6 %collective-permute-start.16 = (bf16[768,256]{1,0:T(8,128)(2,1)S(1)}, bf16[768,256]{1,0:T(8,128)(2,1)S(1)}, u32[]{:S(2)}, u32[]{:S(2)}) collective-permute-start(bf16[768,256]{1,0:T(8,128)(2,1)S(1)} %product_1.6.field_ref), channel_id=1, source_target_pairs={{0,4},{4,0},{8,12},{12,8},{16,20},{20,16},{24,28},{28,24},{1,5},{5... | collective-permute-start | bytes 1179656 | tf_op jit(solution)/shard_map/ppermute | solution.py:91
  115.0 22.8 %collective-permute-start.22 = (bf16[768,256]{1,0:T(8,128)(2,1)S(1)}, bf16[768,256]{1,0:T(8,128)(2,1)S(1)}, u32[]{:S(2)}, u32[]{:S(2)}) collective-permute-start(bf16[768,256]{1,0:T(8,128)(2,1)S(1)} %product_1.7.field_ref), channel_id=1, source_target_pairs={{0,4},{4,0},{8,12},{12,8},{16,20},{20,16},{24,28},{28,24},{1,5},{5... | collective-permute-start | bytes 1179656 | tf_op jit(solution)/shard_map/ppermute | solution.py:91
  115.7 23.6 %collective-permute-start.5 = (bf16[768,256]{1,0:T(8,128)(2,1)S(1)}, bf16[768,256]{1,0:T(8,128)(2,1)S(1)}, u32[]{:S(2)}, u32[]{:S(2)}) collective-permute-start(bf16[768,256]{1,0:T(8,128)(2,1)S(1)} %collective-permute-done.4.by_near_ref), channel_id=1, source_target_pairs={{0,8},{4,28},{8,16},{12,4},{16,24},{20,12},{24,0},{28,20},{1,9},{5... | collective-permute-start | bytes 1179656 | tf_op jit(solution)/shard_map/ppermute | solution.py:92
  124.1 17.9 %collective-permute-start.11 = (bf16[768,256]{1,0:T(8,128)(2,1)S(1)}, bf16[768,256]{1,0:T(8,128)(2,1)S(1)}, u32[]{:S(2)}, u32[]{:S(2)}) collective-permute-start(bf16[768,256]{1,0:T(8,128)(2,1)S(1)} %collective-permute-done.10.by_near_ref), channel_id=1, source_target_pairs={{0,8},{4,28},{8,16},{12,4},{16,24},{20,12},{24,0},{28,20},{1,9},{5... | collective-permute-start | bytes 1179656 | tf_op jit(solution)/shard_map/ppermute | solution.py:92
  132.5 13.8 %collective-permute-start.17 = (bf16[768,256]{1,0:T(8,128)(2,1)S(1)}, bf16[768,256]{1,0:T(8,128)(2,1)S(1)}, u32[]{:S(2)}, u32[]{:S(2)}) collective-permute-start(bf16[768,256]{1,0:T(8,128)(2,1)S(1)} %collective-permute-done.16.by_near_ref), channel_id=1, source_target_pairs={{0,8},{4,28},{8,16},{12,4},{16,24},{20,12},{24,0},{28,20},{1,9},{5... | collective-permute-start | bytes 1179656 | tf_op jit(solution)/shard_map/ppermute | solution.py:92
  137.8 13.5 %collective-permute-start.23 = (bf16[768,256]{1,0:T(8,128)(2,1)S(1)}, bf16[768,256]{1,0:T(8,128)(2,1)S(1)}, u32[]{:S(2)}, u32[]{:S(2)}) collective-permute-start(bf16[768,256]{1,0:T(8,128)(2,1)S(1)} %collective-permute-done.22.by_near_ref), channel_id=1, source_target_pairs={{0,8},{4,28},{8,16},{12,4},{16,24},{20,12},{24,0},{28,20},{1,9},{5... | collective-permute-start | bytes 1179656 | tf_op jit(solution)/shard_map/ppermute | solution.py:92
  140.4 12.5 %collective-permute-start.24 = (bf16[768,256]{1,0:T(8,128)(2,1)S(1)}, bf16[768,256]{1,0:T(8,128)(2,1)S(1)}, u32[]{:S(2)}, u32[]{:S(2)}) collective-permute-start(bf16[768,256]{1,0:T(8,128)(2,1)S(1)} %get-tuple-element.23), channel_id=1, source_target_pairs={{0,1},{1,0},{2,3},{3,2},{4,5},{5,4},{6,7},{7,6},{8,9},{9,8},{10,11... | collective-permute-start | bytes 1179656 | tf_op jit(solution)/shard_map/ppermute | solution.py:110
  140.5 16.2 %collective-permute-start.28 = (bf16[768,256]{1,0:T(8,128)(2,1)S(1)}, bf16[768,256]{1,0:T(8,128)(2,1)S(1)}, u32[]{:S(2)}, u32[]{:S(2)}) collective-permute-start(bf16[768,256]{1,0:T(8,128)(2,1)S(1)} %get-tuple-element.23), channel_id=1, source_target_pairs={{0,2},{1,3},{2,0},{3,1},{4,6},{5,7},{6,4},{7,5},{8,10},{9,11},{10,... | collective-permute-start | bytes 1179656 | tf_op jit(solution)/shard_map/ppermute | solution.py:110
  143.1 11.4 %collective-permute-start.25 = (bf16[768,256]{1,0:T(8,128)(2,1)S(1)}, bf16[768,256]{1,0:T(8,128)(2,1)S(1)}, u32[]{:S(2)}, u32[]{:S(2)}) collective-permute-start(bf16[768,256]{1,0:T(8,128)(2,1)S(1)} %get-tuple-element.26), channel_id=1, source_target_pairs={{0,1},{1,0},{2,3},{3,2},{4,5},{5,4},{6,7},{7,6},{8,9},{9,8},{10,11... | collective-permute-start | bytes 1179656 | tf_op jit(solution)/shard_map/ppermute | solution.py:110
  147.5 4.9 %copy-start.9 = (f32[8,256]{1,0:T(8,128)}, f32[8,256]{1,0:T(8,128)S(1)}, u32[]{:S(2)}) copy-start(f32[8,256]{1,0:T(8,128)S(1)} %get-tuple-element.35) | copy-start | bytes 24580
  147.5 7.6 %collective-permute-start.26 = (bf16[768,256]{1,0:T(8,128)(2,1)S(1)}, bf16[768,256]{1,0:T(8,128)(2,1)S(1)}, u32[]{:S(2)}, u32[]{:S(2)}) collective-permute-start(bf16[768,256]{1,0:T(8,128)(2,1)S(1)} %get-tuple-element.29), channel_id=1, source_target_pairs={{0,1},{1,0},{2,3},{3,2},{4,5},{5,4},{6,7},{7,6},{8,9},{9,8},{10,11... | collective-permute-start | bytes 1179656 | tf_op jit(solution)/shard_map/ppermute | solution.py:110
  152.4 4.4 copy-start.11
  152.5 4.3 collective-permute-start.27
  152.8 30.2 %copy-start.14 = (bf16[768,1024]{1,0:T(8,128)(2,1)}, bf16[768,1024]{1,0:T(8,128)(2,1)S(1)}, u32[]{:S(2)}) copy-start(bf16[768,1024]{1,0:T(8,128)(2,1)S(1)} %get-tuple-element.51) | copy-start | bytes 4718596
  152.9 12.0 %collective-permute-start.29 = (bf16[768,256]{1,0:T(8,128)(2,1)S(1)}, bf16[768,256]{1,0:T(8,128)(2,1)S(1)}, u32[]{:S(2)}, u32[]{:S(2)}) collective-permute-start(bf16[768,256]{1,0:T(8,128)(2,1)S(1)} %get-tuple-element.26), channel_id=1, source_target_pairs={{0,2},{1,3},{2,0},{3,1},{4,6},{5,7},{6,4},{7,5},{8,10},{9,11},{10,... | collective-permute-start | bytes 1179656 | tf_op jit(solution)/shard_map/ppermute | solution.py:110
  154.5 18.8 %collective-permute-start.30 = (bf16[768,256]{1,0:T(8,128)(2,1)S(1)}, bf16[768,256]{1,0:T(8,128)(2,1)S(1)}, u32[]{:S(2)}, u32[]{:S(2)}) collective-permute-start(bf16[768,256]{1,0:T(8,128)(2,1)S(1)} %get-tuple-element.29), channel_id=1, source_target_pairs={{0,2},{1,3},{2,0},{3,1},{4,6},{5,7},{6,4},{7,5},{8,10},{9,11},{10,... | collective-permute-start | bytes 1179656 | tf_op jit(solution)/shard_map/ppermute | solution.py:110
  155.1 26.2 %collective-permute-start.31 = (bf16[768,256]{1,0:T(8,128)(2,1)S(1)}, bf16[768,256]{1,0:T(8,128)(2,1)S(1)}, u32[]{:S(2)}, u32[]{:S(2)}) collective-permute-start(bf16[768,256]{1,0:T(8,128)(2,1)S(1)} %get-tuple-element.32), channel_id=1, source_target_pairs={{0,2},{1,3},{2,0},{3,1},{4,6},{5,7},{6,4},{7,5},{8,10},{9,11},{10,... | collective-permute-start | bytes 1179656 | tf_op jit(solution)/shard_map/ppermute | solution.py:110
  156.7 24.7 %collective-permute-start.32 = (bf16[768,256]{1,0:T(8,128)(2,1)S(1)}, bf16[768,256]{1,0:T(8,128)(2,1)S(1)}, u32[]{:S(2)}, u32[]{:S(2)}) collective-permute-start(bf16[768,256]{1,0:T(8,128)(2,1)S(1)} %collective-permute-done.28), channel_id=1, source_target_pairs={{0,1},{1,0},{2,3},{3,2},{4,5},{5,4},{6,7},{7,6},{8,9},{9,8},{10,11... | collective-permute-start | bytes 1179656 | tf_op jit(solution)/shard_map/ppermute | solution.py:110
  164.8 16.6 %collective-permute-start.33 = (bf16[768,256]{1,0:T(8,128)(2,1)S(1)}, bf16[768,256]{1,0:T(8,128)(2,1)S(1)}, u32[]{:S(2)}, u32[]{:S(2)}) collective-permute-start(bf16[768,256]{1,0:T(8,128)(2,1)S(1)} %collective-permute-done.29), channel_id=1, source_target_pairs={{0,1},{1,0},{2,3},{3,2},{4,5},{5,4},{6,7},{7,6},{8,9},{9,8},{10,11... | collective-permute-start | bytes 1179656 | tf_op jit(solution)/shard_map/ppermute | solution.py:110
  173.3 8.2 %collective-permute-start.34 = (bf16[768,256]{1,0:T(8,128)(2,1)S(1)}, bf16[768,256]{1,0:T(8,128)(2,1)S(1)}, u32[]{:S(2)}, u32[]{:S(2)}) collective-permute-start(bf16[768,256]{1,0:T(8,128)(2,1)S(1)} %collective-permute-done.30), channel_id=1, source_target_pairs={{0,1},{1,0},{2,3},{3,2},{4,5},{5,4},{6,7},{7,6},{8,9},{9,8},{10,11... | collective-permute-start | bytes 1179656 | tf_op jit(solution)/shard_map/ppermute | solution.py:110
  181.3 1.7 collective-permute-start.35
  183.1 2.7 copy-start.16
  194.7 1.4 copy-start.10
  194.7 2.1 copy-start.12
  194.7 275.7 %copy-start.15 = (bf16[768,1024]{1,0:T(8,128)(2,1)S(1)}, bf16[768,1024]{1,0:T(8,128)(2,1)}, u32[]{:S(2)}) copy-start(bf16[768,1024]{1,0:T(8,128)(2,1)} %copy-done.14) | copy-start | bytes 4718596
  194.7 275.7 %all-gather.2.cloned.1.call-start = ((), (), s32[]{:S(2)}) async-start(), calls=%async_computation.2 | async-start | bytes 9437184 | tf_op jit(solution)/shard_map/all_gather | solution.py:122
Sparse Core Ops, SparseCore 0:
  194.8 148.9 reduce-scatter.1
  346.4 123.9 all-gather.1

commit v2 on v1

v2 whole, which is shorter than its diff:
```python
import functools

import jax
import jax.numpy as jnp
from jax import lax
from jax.experimental import pallas as pl
from jax.experimental.pallas import tpu as pltpu
from jax.sharding import PartitionSpec as P

CHUNKS = 4
F32 = jnp.float32
BF16 = jnp.bfloat16


def product_kernel(stage, place_ref, blocks_ref, field_ref, near_ref, far_ref, *refs):
    elements, size, _ = blocks_ref.shape
    width = field_ref.shape[1]
    squares = jnp.zeros((8, width), F32)
    filler = jnp.zeros((size, width), BF16)
    for element in range(elements):
        picked = []
        for slot in range(7):
            source = field_ref if slot < 5 else near_ref if slot == 5 else far_ref
            first_row = pl.multiple_of(place_ref[element, slot] * size, size)
            picked.append(source[pl.ds(first_row, size), :])
        stacked = jnp.concatenate(picked + [filler], axis=0)
        total = jnp.dot(blocks_ref[element], stacked, preferred_element_type=F32)
        here = pl.ds(element * size, size)
        if stage == 0:
            wide_ref, half_ref = refs
            wide_ref[here, :] = total
            half_ref[here, :] = total.astype(BF16)
        elif stage == 1:
            before_ref, half_ref = refs
            half_ref[here, :] = (2.0 * total - before_ref[here, :].astype(F32)).astype(BF16)
        else:
            before_ref, half_ref, squares_ref = refs
            value = (2.0 * total - before_ref[here, :]).astype(BF16)
            half_ref[here, :] = value
            wide = value.astype(F32)
            squares += jnp.sum((wide * wide).reshape(-1, 8, width), axis=0)
    if stage == 2:
        squares_ref[...] = squares


def product(stage, place, blocks, field, by_near, by_far, before=None):
    rows, width = field.shape
    half = jax.ShapeDtypeStruct((rows, width), BF16)
    wide = jax.ShapeDtypeStruct((rows, width), F32)
    squares = jax.ShapeDtypeStruct((8, width), F32)
    outs = ((wide, half), half, (half, squares))[stage]
    args = (blocks, field, by_near, by_far) + (() if before is None else (before,))
    return pl.pallas_call(
        functools.partial(product_kernel, stage),
        out_shape=outs,
        in_specs=[pl.BlockSpec(memory_space=pltpu.SMEM)] + [pl.BlockSpec(memory_space=pltpu.VMEM)] * len(args),
        compiler_params=pltpu.CompilerParams(vmem_limit_bytes=32 * 1024 * 1024),
        cost_estimate=pl.CostEstimate(
            flops=2 * blocks.size * width, bytes_accessed=2 * blocks.size + 16 * rows * width, transcendentals=0
        ),
        name=f"product_{stage}",
    )(place, *args)


def local(orbitals, hamiltonian, neighbours):
    elements, slots, size, _ = hamiltonian.shape
    rows, columns = orbitals.shape
    tiles = lax.axis_size("elem")
    groups = lax.axis_size("orb")
    lines = tiles // 2
    my_tile = lax.axis_index("elem")
    my_group = lax.axis_index("orb")
    odd = my_tile % 2
    line = my_tile // 2

    swap = [(i, i ^ 1) for i in range(tiles)]
    around = [(2 * i + side, 2 * ((i + 1) % lines) + side) for i in range(lines) for side in (0, 1)]
    outward = [(2 * i + side, 2 * ((i + 1 - 2 * side) % lines) + side) for i in range(lines) for side in (0, 1)]

    place = neighbours % elements
    last_two = place[:, 5:]
    place = jnp.concatenate([place[:, :5], jnp.where(odd == 0, last_two[:, ::-1], last_two)], axis=1)
    by_slot = [hamiltonian[:, s] for s in range(5)]
    by_slot.append(jnp.where(odd == 0, hamiltonian[:, 6], hamiltonian[:, 5]))
    by_slot.append(jnp.where(odd == 0, hamiltonian[:, 5], hamiltonian[:, 6]))
    by_slot.append(jnp.zeros_like(by_slot[0]))
    blocks = jnp.concatenate(by_slot, axis=2)

    width = columns // CHUNKS
    start = [lax.slice_in_dim(orbitals, c * width, (c + 1) * width, axis=1) for c in range(CHUNKS)]

    def step(stage, fields, before):
        out = []
        for field, old in zip(fields, before):
            by_near = lax.ppermute(field, "elem", swap)
            by_far = lax.ppermute(by_near, "elem", outward)
            out.append(product(stage, place, blocks, field, by_near, by_far, old))
        return out

    firsts = step(0, start, [None] * CHUNKS)
    seconds = step(1, [half for _, half in firsts], start)
    thirds = step(2, seconds, [wide for wide, _ in firsts])

    pieces = []
    for value, _ in thirds:
        have = {0: value}
        bit = groups // 2
        while bit:
            peers = [(i, i ^ bit) for i in range(groups)]
            for known in list(have):
                have[known | bit] = lax.ppermute(have[known], "orb", peers)
            bit //= 2
        pieces.append(have)
    panel = [jnp.concatenate([have[d] for have in pieces], axis=1) for d in range(groups)]
    filtered = panel[0]

    total = sum(squares for _, squares in thirds)
    total = jnp.full((8, 128), jnp.sum(total), F32)
    for axis, peers in (("orb", groups), ("elem", tiles)):
        bit = 1
        while bit < peers:
            total = total + lax.ppermute(total, axis, [(i, i ^ bit) for i in range(peers)])
            bit *= 2
    rows_total = rows * tiles
    level = total[0, 0] / (columns * groups * rows_total)
    divisor = level * rows_total

    def gram_of(left, right):
        return lax.dot_general(left, right, (((0,), (0,)), ((), ())), preferred_element_type=F32).astype(BF16)

    def summed_and_scaled(value):
        height = value.shape[0] // tiles
        value = value.reshape(2, lines, height, value.shape[1])
        other = lax.ppermute(lax.dynamic_index_in_dim(value, 1 - odd, 0, keepdims=False), "elem", swap)
        mine = lax.dynamic_index_in_dim(value, odd, 0, keepdims=False)

        def pair(index):
            return sum(lax.dynamic_index_in_dim(v, index, 0, keepdims=False).astype(F32) for v in (mine, other))

        running = None
        for hop in range(1, lines):
            part = pair((line - hop) % lines)
            if running is not None:
                part = part + running.astype(F32)
            running = lax.ppermute(part.astype(BF16), "elem", around)
        part = pair(line)
        if running is not None:
            part = part + running.astype(F32)
        part = (part / divisor).astype(BF16)
        whole = lax.dynamic_update_index_in_dim(jnp.zeros_like(mine), part, line, 0)
        for hop in range(1, lines):
            part = lax.ppermute(part, "elem", around)
            whole = lax.dynamic_update_index_in_dim(whole, part, (line - hop) % lines, 0)
        far_whole = lax.ppermute(whole, "elem", swap)
        halves = [jnp.where(odd == 0, whole, far_whole), jnp.where(odd == 0, far_whole, whole)]
        return jnp.concatenate(halves, axis=0).reshape(tiles * height, -1)

    mixed = jnp.dot(filtered, summed_and_scaled(gram_of(filtered, filtered)), preferred_element_type=F32)
    middle = columns // 2
    order = sorted(range(1, groups), key=lambda d: (d == 1, d))
    for d in order:
        top_bit = 1 << (d.bit_length() - 1)
        lower = (my_group & top_bit) == 0
        left = jnp.where(lower, panel[d][:, :middle], filtered[:, middle:])
        right = jnp.where(lower, filtered, panel[d])
        half = summed_and_scaled(gram_of(left, right))
        peer_half = lax.ppermute(half, "orb", [(i, i ^ d) for i in range(groups)])
        block = jnp.concatenate(
            [jnp.where(lower, half, peer_half), jnp.where(lower, peer_half, half)], axis=0
        )
        block = jnp.where(lower, block, block.T)
        mixed = mixed + jnp.dot(panel[d], block, preferred_element_type=F32)
    result = (1.5 * filtered.astype(F32) - 0.5 * mixed) / jnp.sqrt(level)
    return result.astype(BF16)


def solution(mesh):
    return jax.shard_map(
        local,
        mesh=mesh,
        in_specs=(P("elem", "orb"), P("elem", None, None, None), P("elem", None)),
        out_specs=P("elem", "orb"),
        check_vma=False,
    )
```

time: 490 us -> 366 us (0.75)
  waiting for transfers between devices: 326 us -> 214 us
  blocking collectives: 41.4 us -> 0 us
  local copies, waits for them, and re-layouts: 18 us -> 37.6 us
  starting transfers between devices: 36 us -> 54.4 us
  between operations: 18 us -> 2.34 us
    all_gather x1 -> x0, waiting for transfers between devices: 123 us -> none  [local(): scaled = lax.all_gather(scaled_part, 'elem', axis=0, tiled=True)]
    ppermute x12 -> x52, waiting for transfers between devices: 10.7 us -> 131 us  [the longest x12 47.1 us: summed_and_scaled(): part = lax.ppermute(part, 'elem', around)]
    reduce_scatter x1 -> x0, waiting for transfers between devices: 101 us -> none  [local(): lax.psum_scatter(partial_gram, 'elem', scatter_dimension=0, tiled=True)]
    unnamed x1 -> x0, blocking collectives: 41.4 us -> none
    ppermute x12 -> x52, starting transfers between devices: 14.5 us -> 34 us  [the longest x12 14.4 us: step(): by_far = lax.ppermute(by_near, 'elem', outward)]
    select_n x3 -> x1, local copies, waits for them, and re-layouts: 11.6 us -> 0.54 us  [local(): jnp.where(lower, half, peer_half)]
    concatenate x1 -> x8, local copies, waits for them, and re-layouts: 0.04 us -> 10.6 us  [the longest x3 7.87 us: local(): jnp.concatenate([jnp.where(lower, half, peer_half), jnp.where(lower, peer...]
    unnamed x53 -> x61, local copies, waits for them, and re-layouts: 4.73 us -> 11.8 us
  transfers between devices with their start and end apart: 38 -> 76, of which waited for: 21 -> 43; matrix products, arithmetic and copies ran while one was open for 5% -> 15% of each run, Pallas kernels for 4% -> 5%
where the time goes in v2:
time: 366 us; the launch traced here: 365 us
  waiting for transfers between devices  214 us (58%)
  starting transfers between devices  54.4 us (15%)
  local copies, waits for them, and re-layouts  37.6 us (10%)
  matrix products  22.4 us (6%)
  Pallas kernels  18.2 us (5%)
  other arithmetic  15.5 us (4%)
    ppermute x12, waiting for transfers between devices, step(): by_near = lax.ppermute(field, 'elem', swap)  59.4 us
    ppermute x12, waiting for transfers between devices, summed_and_scaled(): part = lax.ppermute(part, 'elem', around)  47.1 us
    ppermute x12, waiting for transfers between devices, summed_and_scaled(): running = lax.ppermute(part.astype(BF16), 'elem', around)  33.6 us
    ppermute x12, waiting for transfers between devices, local(): have[known | bit] = lax.ppermute(have[known], 'orb', peers)  24.1 us
    ppermute x4, waiting for transfers between devices, summed_and_scaled(): lax.ppermute(lax.dynamic_index_in_dim(value, 1 - odd, 0, keepdims=False),...  21.4 us
    pallas_call x12, Pallas kernels, product(): pl.pallas_call(functools.partial(product_kernel, stage), out_shape=outs,...  18.2 us
    dot_general x3, matrix products, local(): mixed = mixed + jnp.dot(panel[d], block, preferred_element_type=F32)  15.6 us
    ppermute x12, starting transfers between devices, step(): by_near = lax.ppermute(field, 'elem', swap)  15.1 us
  transfers between devices with their start and end apart: 76, of which 43 were waited for; matrix products, arithmetic and copies ran while one was open for 15% of the time, Pallas kernels for 5%

profile of v2, /device:TPU:0, one launch (start us, length us, event | category | flops | bytes accessed | tf_op | source)
XLA Modules:
  0.0 364.9 jit_solution(1528157904499936886)
XLA Ops:
  1.5 3.0 collective-permute-start
  4.6 1.9 collective-permute-start.12
  6.7 2.2 slice_bitcast_fusion
  9.0 1.8 fusion.66
  10.8 3.7 %collective-permute-done.near_ref = bf16[768,256]{1,0:T(8,128)(2,1)S(1)} collective-permute-done((bf16[768,256]{1,0:T(8,128)(2,1)S(1)}, bf16[768,256]{1,0:T(8,128)(2,1)S(1)}, u32[]{:S(2)}, u32[]{:S(2)}) %collective-permute-start) | collective-permute-done | bytes 393248 | tf_op jit(solution)/shard_map/ppermute | solution.py:95
  14.5 2.1 collective-permute-start.1
  16.6 6.3 %collective-permute-done.6.near_ref = bf16[768,256]{1,0:T(8,128)(2,1)S(1)} collective-permute-done((bf16[768,256]{1,0:T(8,128)(2,1)S(1)}, bf16[768,256]{1,0:T(8,128)(2,1)S(1)}, u32[]{:S(2)}, u32[]{:S(2)}) %collective-permute-start.6) | collective-permute-done | bytes 393248 | tf_op jit(solution)/shard_map/ppermute | solution.py:95
  22.9 2.1 collective-permute-start.7
  25.0 6.4 %collective-permute-done.12.near_ref = bf16[768,256]{1,0:T(8,128)(2,1)} collective-permute-done((bf16[768,256]{1,0:T(8,128)(2,1)S(1)}, bf16[768,256]{1,0:T(8,128)(2,1)}, u32[]{:S(2)}, u32[]{:S(2)}) %collective-permute-start.12) | collective-permute-done | bytes 393248 | tf_op jit(solution)/shard_map/ppermute | solution.py:95
  31.4 2.1 collective-permute-start.13
  34.4 2.5 concatenate.52.blocks_ref
  37.0 2.0 collective-permute-done.18.near_ref
  38.9 1.8 collective-permute-start.19
  42.5 3.6 collective-permute-start.2
  51.6 1.8 collective-permute-start.14
  56.2 8.4 %collective-permute-done.8.near_ref = bf16[768,256]{1,0:T(8,128)(2,1)S(1)} collective-permute-done((bf16[768,256]{1,0:T(8,128)(2,1)S(1)}, bf16[768,256]{1,0:T(8,128)(2,1)S(1)}, u32[]{:S(2)}, u32[]{:S(2)}) %collective-permute-start.8) | collective-permute-done | bytes 393248 | tf_op jit(solution)/shard_map/ppermute | solution.py:95
  64.6 8.4 %collective-permute-done.14.near_ref = bf16[768,256]{1,0:T(8,128)(2,1)S(1)} collective-permute-done((bf16[768,256]{1,0:T(8,128)(2,1)S(1)}, bf16[768,256]{1,0:T(8,128)(2,1)S(1)}, u32[]{:S(2)}, u32[]{:S(2)}) %collective-permute-start.14) | collective-permute-done | bytes 393248 | tf_op jit(solution)/shard_map/ppermute | solution.py:95
  73.0 6.4 %collective-permute-done.20.near_ref = bf16[768,256]{1,0:T(8,128)(2,1)S(1)} collective-permute-done((bf16[768,256]{1,0:T(8,128)(2,1)S(1)}, bf16[768,256]{1,0:T(8,128)(2,1)S(1)}, u32[]{:S(2)}, u32[]{:S(2)}) %collective-permute-start.20) | collective-permute-done | bytes 393248 | tf_op jit(solution)/shard_map/ppermute | solution.py:95
  80.7 2.3 collective-permute-start.4
  87.7 4.2 %collective-permute-done.21.far_ref = bf16[768,256]{1,0:T(8,128)(2,1)S(1)} collective-permute-done((bf16[768,256]{1,0:T(8,128)(2,1)S(1)}, bf16[768,256]{1,0:T(8,128)(2,1)S(1)}, u32[]{:S(2)}, u32[]{:S(2)}) %collective-permute-start.21) | collective-permute-done | bytes 393248 | tf_op jit(solution)/shard_map/ppermute | solution.py:96
  94.7 6.9 %collective-permute-done.10.near_ref = bf16[768,256]{1,0:T(8,128)(2,1)} collective-permute-done((bf16[768,256]{1,0:T(8,128)(2,1)S(1)}, bf16[768,256]{1,0:T(8,128)(2,1)}, u32[]{:S(2)}, u32[]{:S(2)}) %collective-permute-start.10) | collective-permute-done | bytes 393248 | tf_op jit(solution)/shard_map/ppermute | solution.py:95
  103.1 6.9 %collective-permute-done.16.near_ref = bf16[768,256]{1,0:T(8,128)(2,1)} collective-permute-done((bf16[768,256]{1,0:T(8,128)(2,1)S(1)}, bf16[768,256]{1,0:T(8,128)(2,1)}, u32[]{:S(2)}, u32[]{:S(2)}) %collective-permute-start.16) | collective-permute-done | bytes 393248 | tf_op jit(solution)/shard_map/ppermute | solution.py:95
  111.6 3.8 %collective-permute-done.22.near_ref = bf16[768,256]{1,0:T(8,128)(2,1)} collective-permute-done((bf16[768,256]{1,0:T(8,128)(2,1)S(1)}, bf16[768,256]{1,0:T(8,128)(2,1)}, u32[]{:S(2)}, u32[]{:S(2)}) %collective-permute-start.22) | collective-permute-done | bytes 393248 | tf_op jit(solution)/shard_map/ppermute | solution.py:95
  121.5 1.8 product_2.5
  126.1 4.4 %collective-permute-done.23.far_ref = bf16[768,256]{1,0:T(8,128)(2,1)} collective-permute-done((bf16[768,256]{1,0:T(8,128)(2,1)}, bf16[768,256]{1,0:T(8,128)(2,1)}, u32[]{:S(2)}, u32[]{:S(2)}) %collective-permute-start.23) | collective-permute-done | bytes 393248 | tf_op jit(solution)/shard_map/ppermute | solution.py:96
  130.4 1.8 product_2.7
  136.9 2.1 collective-permute-done.29
  139.8 3.5 collective-permute-done.30
  143.4 3.5 collective-permute-done.31
  147.0 1.8 convolution_convert_fusion
  148.8 2.7 collective-permute-done.32
  157.8 5.7 %collective-permute-done.37 = bf16[768,256]{1,0:T(8,128)(2,1)S(1)} collective-permute-done((bf16[768,256]{1,0:T(8,128)(2,1)S(1)}, bf16[768,256]{1,0:T(8,128)(2,1)S(1)}, u32[]{:S(2)}, u32[]{:S(2)}) %collective-permute-start.37) | collective-permute-done | bytes 393248 | tf_op jit(solution)/shard_map/ppermute | solution.py:111
  163.5 8.4 %collective-permute-done.38 = bf16[768,256]{1,0:T(8,128)(2,1)S(1)} collective-permute-done((bf16[768,256]{1,0:T(8,128)(2,1)S(1)}, bf16[768,256]{1,0:T(8,128)(2,1)S(1)}, u32[]{:S(2)}, u32[]{:S(2)}) %collective-permute-start.38) | collective-permute-done | bytes 393248 | tf_op jit(solution)/shard_map/ppermute | solution.py:111
  172.0 7.2 %collective-permute-done.39 = bf16[768,256]{1,0:T(8,128)(2,1)S(1)} collective-permute-done((bf16[768,256]{1,0:T(8,128)(2,1)S(1)}, bf16[768,256]{1,0:T(8,128)(2,1)S(1)}, u32[]{:S(2)}, u32[]{:S(2)}) %collective-permute-start.39) | collective-permute-done | bytes 393248 | tf_op jit(solution)/shard_map/ppermute | solution.py:111
  180.5 2.8 collective-permute-done.40
  185.0 1.8 collective-permute-start.41
  188.2 11.1 %collective-permute-done.67 = bf16[4,64,1024]{2,1,0:T(8,128)(2,1)S(1)} collective-permute-done((bf16[4,64,1024]{2,1,0:T(8,128)(2,1)S(1)}, bf16[4,64,1024]{2,1,0:T(8,128)(2,1)S(1)}, u32[]{:S(2)}, u32[]{:S(2)}) %collective-permute-start.67) | collective-permute-done | bytes 524320 | tf_op jit(solution)/shard_map/ppermute | solution.py:134
  200.4 10.2 %collective-permute-done.41 = bf16[4,64,1024]{2,1,0:T(8,128)(2,1)S(1)} collective-permute-done((bf16[4,64,1024]{2,1,0:T(8,128)(2,1)S(1)}, bf16[4,64,1024]{2,1,0:T(8,128)(2,1)S(1)}, u32[]{:S(2)}, u32[]{:S(2)}) %collective-permute-start.41) | collective-permute-done | bytes 524320 | tf_op jit(solution)/shard_map/ppermute | solution.py:134
  213.0 5.9 %collective-permute-done.42 = bf16[64,1024]{1,0:T(8,128)(2,1)S(1)} collective-permute-done((bf16[64,1024]{1,0:T(8,128)(2,1)S(1)}, bf16[64,1024]{1,0:T(8,128)(2,1)S(1)}, u32[]{:S(2)}, u32[]{:S(2)}) %collective-permute-start.42) | collective-permute-done | bytes 131104 | tf_op jit(solution)/shard_map/ppermute | solution.py:145
  219.1 2.7 collective-permute-done.69
  221.9 8.0 %collective-permute-done.43 = bf16[64,1024]{1,0:T(8,128)(2,1)S(1)} collective-permute-done((bf16[64,1024]{1,0:T(8,128)(2,1)S(1)}, bf16[64,1024]{1,0:T(8,128)(2,1)S(1)}, u32[]{:S(2)}, u32[]{:S(2)}) %collective-permute-start.43) | collective-permute-done | bytes 131104 | tf_op jit(solution)/shard_map/ppermute | solution.py:145
  233.2 2.2 collective-permute-start.55
  235.4 2.7 collective-permute-done.44
  238.4 10.0 %collective-permute-done.55 = bf16[64,1024]{1,0:T(8,128)(2,1)S(1)} collective-permute-done((bf16[64,1024]{1,0:T(8,128)(2,1)S(1)}, bf16[64,1024]{1,0:T(8,128)(2,1)S(1)}, u32[]{:S(2)}, u32[]{:S(2)}) %collective-permute-start.55) | collective-permute-done | bytes 131104 | tf_op jit(solution)/shard_map/ppermute | solution.py:145
  248.6 1.8 collective-permute-done.45
  250.5 3.2 collective-permute-start.27
  253.7 3.0 collective-permute-done.56
  256.8 2.7 collective-permute-done.72
  259.5 2.8 collective-permute-done.46
  262.3 8.5 %collective-permute-done.73 = bf16[64,1024]{1,0:T(8,128)(2,1)S(1)} collective-permute-done((bf16[64,1024]{1,0:T(8,128)(2,1)S(1)}, bf16[64,1024]{1,0:T(8,128)(2,1)S(1)}, u32[]{:S(2)}, u32[]{:S(2)}) %collective-permute-start.73) | collective-permute-done | bytes 131104 | tf_op jit(solution)/shard_map/ppermute | solution.py:152
  275.2 6.1 %collective-permute-done.58 = bf16[64,1024]{1,0:T(8,128)(2,1)S(1)} collective-permute-done((bf16[64,1024]{1,0:T(8,128)(2,1)S(1)}, bf16[64,1024]{1,0:T(8,128)(2,1)S(1)}, u32[]{:S(2)}, u32[]{:S(2)}) %collective-permute-start.58) | collective-permute-done | bytes 131104 | tf_op jit(solution)/shard_map/ppermute | solution.py:152
  281.3 7.2 %collective-permute-done.59 = bf16[64,1024]{1,0:T(8,128)(2,1)S(1)} collective-permute-done((bf16[64,1024]{1,0:T(8,128)(2,1)S(1)}, bf16[64,1024]{1,0:T(8,128)(2,1)S(1)}, u32[]{:S(2)}, u32[]{:S(2)}) %collective-permute-start.59) | collective-permute-done | bytes 131104 | tf_op jit(solution)/shard_map/ppermute | solution.py:152
  288.6 7.6 %collective-permute-done.60 = bf16[64,1024]{1,0:T(8,128)(2,1)S(1)} collective-permute-done((bf16[64,1024]{1,0:T(8,128)(2,1)S(1)}, bf16[64,1024]{1,0:T(8,128)(2,1)S(1)}, u32[]{:S(2)}, u32[]{:S(2)}) %collective-permute-start.60) | collective-permute-done | bytes 131104 | tf_op jit(solution)/shard_map/ppermute | solution.py:152
  296.2 2.3 collective-permute-start.61
  302.6 4.3 %collective-permute-done.34 = bf16[128,1024]{1,0:T(8,128)(2,1)} collective-permute-done((bf16[128,1024]{1,0:T(8,128)(2,1)S(1)}, bf16[128,1024]{1,0:T(8,128)(2,1)}, u32[]{:S(2)}, u32[]{:S(2)}) %collective-permute-start.34) | collective-permute-done | bytes 262176 | tf_op jit(solution)/shard_map/ppermute | solution.py:152
  310.1 5.1 %collective-permute-done.35 = bf16[128,1024]{1,0:T(8,128)(2,1)S(1)} collective-permute-done((bf16[128,1024]{1,0:T(8,128)(2,1)}, bf16[128,1024]{1,0:T(8,128)(2,1)S(1)}, u32[]{:S(2)}, u32[]{:S(2)}) %collective-permute-start.35) | collective-permute-done | bytes 262176 | tf_op jit(solution)/shard_map/ppermute | solution.py:152
  318.9 2.6 copy.54
  321.5 6.1 %fusion = f32[768,1024]{1,0:T(8,128)} fusion(bf16[768,1024]{1,0:T(8,128)(2,1)} %copy-done.19, bf16[1024,1024]{0,1:T(8,128)(2,1)} %copy.54, pred[]{:T(512)S(6)} %eq.50, bf16[512,1024]{1,0:T(8,128)(2,1)} %copy-done.13, bf16[512,1024]{1,0:T(8,128)(2,1)} %copy-done.12), kind=kOutput, calls=%fused_computation.6 | convolution fusion | flops 1615855616 | bytes 8912897 | tf_op jit(solution)/shard_map/dot_general | solution.py:172
  333.5 2.6 copy.49
  336.2 5.8 %fusion.2 = f32[768,1024]{1,0:T(8,128)} fusion(bf16[768,1024]{1,0:T(8,128)(2,1)} %copy-done.20, bf16[1024,1024]{0,1:T(8,128)(2,1)} %copy.49, pred[]{:T(512)S(6)} %eq.49, bf16[512,1024]{1,0:T(8,128)(2,1)} %broadcast_select_fusion, bf16[512,1024]{1,0:T(8,128)(2,1)S(1)} %copy.48), kind=kOutput, calls=%fused_computation.10 | convolution fusion | flops 1615855616 | bytes 8912897 | tf_op jit(solution)/shard_map/dot_general | solution.py:172
  342.0 7.0 %collective-permute-done.62 = bf16[512,1024]{0,1:T(8,128)(2,1)} collective-permute-done((bf16[512,1024]{0,1:T(8,128)(2,1)}, bf16[512,1024]{0,1:T(8,128)(2,1)}, u32[]{:S(2)}, u32[]{:S(2)}) %collective-permute-start.62) | collective-permute-done | bytes 1048608 | tf_op jit(solution)/shard_map/ppermute | solution.py:167
  351.9 2.6 copy.53
  357.7 1.8 fusion.75
  361.2 3.7 %divide_convert_fusion = bf16[768,1024]{1,0:T(8,128)(2,1)} fusion(f32[768,1024]{1,0:T(8,128)S(1)} %copy-done.22, f32[768,1024]{1,0:T(8,128)S(1)} %fusion.75, f32[768,1024]{1,0:T(8,128)S(1)} %copy-done.23, bf16[768,1024]{1,0:T(8,128)(2,1)S(1)} %copy-done.16, f32[]{:T(128)} %bitcast.71, bf16[768,1024]{1,0:T(8,128)(2,1)S(1)} %copy-done.18, ...), kind=kOutput, calls=%fused_computation | convolution fusion | flops 1622933504 | bytes 18350084 | tf_op jit(solution)/shard_map/dot_general | solution.py:172
  (249 shorter events, 84.7 us)
Async XLA Ops:
  1.5 13.0 %collective-permute-start = (bf16[768,256]{1,0:T(8,128)(2,1)S(1)}, bf16[768,256]{1,0:T(8,128)(2,1)S(1)}, u32[]{:S(2)}, u32[]{:S(2)}) collective-permute-start(bf16[768,256]{1,0:T(8,128)(2,1)S(1)} %get-tuple-element.53.field_ref.refs_0_), channel_id=1, source_target_pairs={{0,4},{4,0},{8,12},{12,8},{16,20},{20,16},{24,28},{28,24},{1,5},{5... | collective-permute-start | bytes 1179656 | tf_op jit(solution)/shard_map/ppermute | solution.py:95
  4.5 18.4 %collective-permute-start.6 = (bf16[768,256]{1,0:T(8,128)(2,1)S(1)}, bf16[768,256]{1,0:T(8,128)(2,1)S(1)}, u32[]{:S(2)}, u32[]{:S(2)}) collective-permute-start(bf16[768,256]{1,0:T(8,128)(2,1)S(1)} %get-tuple-element.52.field_ref.refs_0_), channel_id=1, source_target_pairs={{0,4},{4,0},{8,12},{12,8},{16,20},{20,16},{24,28},{28,24},{1,5},{5... | collective-permute-start | bytes 1179656 | tf_op jit(solution)/shard_map/ppermute | solution.py:95
  4.6 26.8 %collective-permute-start.12 = (bf16[768,256]{1,0:T(8,128)(2,1)S(1)}, bf16[768,256]{1,0:T(8,128)(2,1)}, u32[]{:S(2)}, u32[]{:S(2)}) collective-permute-start(bf16[768,256]{1,0:T(8,128)(2,1)S(1)} %get-tuple-element.54.field_ref.refs_0_), channel_id=1, source_target_pairs={{0,4},{4,0},{8,12},{12,8},{16,20},{20,16},{24,28},{28,24},{1,5},{5... | collective-permute-start | bytes 1179656 | tf_op jit(solution)/shard_map/ppermute | solution.py:95
  6.5 32.4 %collective-permute-start.18 = (bf16[768,256]{1,0:T(8,128)(2,1)S(1)}, bf16[768,256]{1,0:T(8,128)(2,1)S(1)}, u32[]{:S(2)}, u32[]{:S(2)}) collective-permute-start(bf16[768,256]{1,0:T(8,128)(2,1)S(1)} %get-tuple-element.51.field_ref.refs_0_), channel_id=1, source_target_pairs={{0,4},{4,0},{8,12},{12,8},{16,20},{20,16},{24,28},{28,24},{1,5},{5... | collective-permute-start | bytes 1179656 | tf_op jit(solution)/shard_map/ppermute | solution.py:95
  14.5 26.4 %collective-permute-start.1 = (bf16[768,256]{1,0:T(8,128)(2,1)S(1)}, bf16[768,256]{1,0:T(8,128)(2,1)}, u32[]{:S(2)}, u32[]{:S(2)}) collective-permute-start(bf16[768,256]{1,0:T(8,128)(2,1)S(1)} %collective-permute-done.near_ref), channel_id=1, source_target_pairs={{0,8},{4,28},{8,16},{12,4},{16,24},{20,12},{24,0},{28,20},{1,9},{5... | collective-permute-start | bytes 1179656 | tf_op jit(solution)/shard_map/ppermute | solution.py:96
  22.9 23.2 %collective-permute-start.7 = (bf16[768,256]{1,0:T(8,128)(2,1)S(1)}, bf16[768,256]{1,0:T(8,128)(2,1)}, u32[]{:S(2)}, u32[]{:S(2)}) collective-permute-start(bf16[768,256]{1,0:T(8,128)(2,1)S(1)} %collective-permute-done.6.near_ref), channel_id=1, source_target_pairs={{0,8},{4,28},{8,16},{12,4},{16,24},{20,12},{24,0},{28,20},{1,9},{5... | collective-permute-start | bytes 1179656 | tf_op jit(solution)/shard_map/ppermute | solution.py:96
  31.4 17.6 %collective-permute-start.13 = (bf16[768,256]{1,0:T(8,128)(2,1)}, bf16[768,256]{1,0:T(8,128)(2,1)}, u32[]{:S(2)}, u32[]{:S(2)}) collective-permute-start(bf16[768,256]{1,0:T(8,128)(2,1)} %collective-permute-done.12.near_ref), channel_id=1, source_target_pairs={{0,8},{4,28},{8,16},{12,4},{16,24},{20,12},{24,0},{28,20},{1,9},{5... | collective-permute-start | bytes 1179656 | tf_op jit(solution)/shard_map/ppermute | solution.py:96
  38.9 14.5 %collective-permute-start.19 = (bf16[768,256]{1,0:T(8,128)(2,1)S(1)}, bf16[768,256]{1,0:T(8,128)(2,1)S(1)}, u32[]{:S(2)}, u32[]{:S(2)}) collective-permute-start(bf16[768,256]{1,0:T(8,128)(2,1)S(1)} %collective-permute-done.18.near_ref), channel_id=1, source_target_pairs={{0,8},{4,28},{8,16},{12,4},{16,24},{20,12},{24,0},{28,20},{1,9},{5... | collective-permute-start | bytes 1179656 | tf_op jit(solution)/shard_map/ppermute | solution.py:96
  42.5 13.6 %collective-permute-start.2 = (bf16[768,256]{1,0:T(8,128)(2,1)S(1)}, bf16[768,256]{1,0:T(8,128)(2,1)S(1)}, u32[]{:S(2)}, u32[]{:S(2)}) collective-permute-start(bf16[768,256]{1,0:T(8,128)(2,1)S(1)} %get-tuple-element.21.field_ref), channel_id=1, source_target_pairs={{0,4},{4,0},{8,12},{12,8},{16,20},{20,16},{24,28},{28,24},{1,5},{5... | collective-permute-start | bytes 1179656 | tf_op jit(solution)/shard_map/ppermute | solution.py:95
  48.7 15.9 %collective-permute-start.8 = (bf16[768,256]{1,0:T(8,128)(2,1)S(1)}, bf16[768,256]{1,0:T(8,128)(2,1)S(1)}, u32[]{:S(2)}, u32[]{:S(2)}) collective-permute-start(bf16[768,256]{1,0:T(8,128)(2,1)S(1)} %get-tuple-element.24.field_ref), channel_id=1, source_target_pairs={{0,4},{4,0},{8,12},{12,8},{16,20},{20,16},{24,28},{28,24},{1,5},{5... | collective-permute-start | bytes 1179656 | tf_op jit(solution)/shard_map/ppermute | solution.py:95
  51.6 21.4 %collective-permute-start.14 = (bf16[768,256]{1,0:T(8,128)(2,1)S(1)}, bf16[768,256]{1,0:T(8,128)(2,1)S(1)}, u32[]{:S(2)}, u32[]{:S(2)}) collective-permute-start(bf16[768,256]{1,0:T(8,128)(2,1)S(1)} %get-tuple-element.27.field_ref), channel_id=1, source_target_pairs={{0,4},{4,0},{8,12},{12,8},{16,20},{20,16},{24,28},{28,24},{1,5},{5... | collective-permute-start | bytes 1179656 | tf_op jit(solution)/shard_map/ppermute | solution.py:95
  55.6 23.8 %collective-permute-start.20 = (bf16[768,256]{1,0:T(8,128)(2,1)S(1)}, bf16[768,256]{1,0:T(8,128)(2,1)S(1)}, u32[]{:S(2)}, u32[]{:S(2)}) collective-permute-start(bf16[768,256]{1,0:T(8,128)(2,1)S(1)} %get-tuple-element.30.field_ref), channel_id=1, source_target_pairs={{0,4},{4,0},{8,12},{12,8},{16,20},{20,16},{24,28},{28,24},{1,5},{5... | collective-permute-start | bytes 1179656 | tf_op jit(solution)/shard_map/ppermute | solution.py:95
  56.1 23.3 %collective-permute-start.3 = (bf16[768,256]{1,0:T(8,128)(2,1)S(1)}, bf16[768,256]{1,0:T(8,128)(2,1)S(1)}, u32[]{:S(2)}, u32[]{:S(2)}) collective-permute-start(bf16[768,256]{1,0:T(8,128)(2,1)S(1)} %collective-permute-done.2.near_ref), channel_id=1, source_target_pairs={{0,8},{4,28},{8,16},{12,4},{16,24},{20,12},{24,0},{28,20},{1,9},{5... | collective-permute-start | bytes 1179656 | tf_op jit(solution)/shard_map/ppermute | solution.py:96
  64.6 18.4 %collective-permute-start.9 = (bf16[768,256]{1,0:T(8,128)(2,1)S(1)}, bf16[768,256]{1,0:T(8,128)(2,1)S(1)}, u32[]{:S(2)}, u32[]{:S(2)}) collective-permute-start(bf16[768,256]{1,0:T(8,128)(2,1)S(1)} %collective-permute-done.8.near_ref), channel_id=1, source_target_pairs={{0,8},{4,28},{8,16},{12,4},{16,24},{20,12},{24,0},{28,20},{1,9},{5... | collective-permute-start | bytes 1179656 | tf_op jit(solution)/shard_map/ppermute | solution.py:96
  73.0 11.8 %collective-permute-start.15 = (bf16[768,256]{1,0:T(8,128)(2,1)S(1)}, bf16[768,256]{1,0:T(8,128)(2,1)S(1)}, u32[]{:S(2)}, u32[]{:S(2)}) collective-permute-start(bf16[768,256]{1,0:T(8,128)(2,1)S(1)} %collective-permute-done.14.near_ref), channel_id=1, source_target_pairs={{0,8},{4,28},{8,16},{12,4},{16,24},{20,12},{24,0},{28,20},{1,9},{5... | collective-permute-start | bytes 1179656 | tf_op jit(solution)/shard_map/ppermute | solution.py:96
  79.5 12.4 %collective-permute-start.21 = (bf16[768,256]{1,0:T(8,128)(2,1)S(1)}, bf16[768,256]{1,0:T(8,128)(2,1)S(1)}, u32[]{:S(2)}, u32[]{:S(2)}) collective-permute-start(bf16[768,256]{1,0:T(8,128)(2,1)S(1)} %collective-permute-done.20.near_ref), channel_id=1, source_target_pairs={{0,8},{4,28},{8,16},{12,4},{16,24},{20,12},{24,0},{28,20},{1,9},{5... | collective-permute-start | bytes 1179656 | tf_op jit(solution)/shard_map/ppermute | solution.py:96
  80.7 12.5 %collective-permute-start.4 = (bf16[768,256]{1,0:T(8,128)(2,1)S(1)}, bf16[768,256]{1,0:T(8,128)(2,1)}, u32[]{:S(2)}, u32[]{:S(2)}) collective-permute-start(bf16[768,256]{1,0:T(8,128)(2,1)S(1)} %product_1.4.field_ref), channel_id=1, source_target_pairs={{0,4},{4,0},{8,12},{12,8},{16,20},{20,16},{24,28},{28,24},{1,5},{5... | collective-permute-start | bytes 1179656 | tf_op jit(solution)/shard_map/ppermute | solution.py:95
  84.3 17.3 %collective-permute-start.10 = (bf16[768,256]{1,0:T(8,128)(2,1)S(1)}, bf16[768,256]{1,0:T(8,128)(2,1)}, u32[]{:S(2)}, u32[]{:S(2)}) collective-permute-start(bf16[768,256]{1,0:T(8,128)(2,1)S(1)} %product_1.5.field_ref), channel_id=1, source_target_pairs={{0,4},{4,0},{8,12},{12,8},{16,20},{20,16},{24,28},{28,24},{1,5},{5... | collective-permute-start | bytes 1179656 | tf_op jit(solution)/shard_map/ppermute | solution.py:95
  86.1 23.9 %collective-permute-start.16 = (bf16[768,256]{1,0:T(8,128)(2,1)S(1)}, bf16[768,256]{1,0:T(8,128)(2,1)}, u32[]{:S(2)}, u32[]{:S(2)}) collective-permute-start(bf16[768,256]{1,0:T(8,128)(2,1)S(1)} %product_1.6.field_ref), channel_id=1, source_target_pairs={{0,4},{4,0},{8,12},{12,8},{16,20},{20,16},{24,28},{28,24},{1,5},{5... | collective-permute-start | bytes 1179656 | tf_op jit(solution)/shard_map/ppermute | solution.py:95
  93.2 22.2 %collective-permute-start.22 = (bf16[768,256]{1,0:T(8,128)(2,1)S(1)}, bf16[768,256]{1,0:T(8,128)(2,1)}, u32[]{:S(2)}, u32[]{:S(2)}) collective-permute-start(bf16[768,256]{1,0:T(8,128)(2,1)S(1)} %product_1.7.field_ref), channel_id=1, source_target_pairs={{0,4},{4,0},{8,12},{12,8},{16,20},{20,16},{24,28},{28,24},{1,5},{5... | collective-permute-start | bytes 1179656 | tf_op jit(solution)/shard_map/ppermute | solution.py:95
  93.2 23.6 %collective-permute-start.5 = (bf16[768,256]{1,0:T(8,128)(2,1)}, bf16[768,256]{1,0:T(8,128)(2,1)S(1)}, u32[]{:S(2)}, u32[]{:S(2)}) collective-permute-start(bf16[768,256]{1,0:T(8,128)(2,1)} %collective-permute-done.4.near_ref), channel_id=1, source_target_pairs={{0,8},{4,28},{8,16},{12,4},{16,24},{20,12},{24,0},{28,20},{1,9},{5... | collective-permute-start | bytes 1179656 | tf_op jit(solution)/shard_map/ppermute | solution.py:96
  101.6 19.9 %collective-permute-start.11 = (bf16[768,256]{1,0:T(8,128)(2,1)}, bf16[768,256]{1,0:T(8,128)(2,1)}, u32[]{:S(2)}, u32[]{:S(2)}) collective-permute-start(bf16[768,256]{1,0:T(8,128)(2,1)} %collective-permute-done.10.near_ref), channel_id=1, source_target_pairs={{0,8},{4,28},{8,16},{12,4},{16,24},{20,12},{24,0},{28,20},{1,9},{5... | collective-permute-start | bytes 1179656 | tf_op jit(solution)/shard_map/ppermute | solution.py:96
  110.0 14.3 %collective-permute-start.17 = (bf16[768,256]{1,0:T(8,128)(2,1)}, bf16[768,256]{1,0:T(8,128)(2,1)}, u32[]{:S(2)}, u32[]{:S(2)}) collective-permute-start(bf16[768,256]{1,0:T(8,128)(2,1)} %collective-permute-done.16.near_ref), channel_id=1, source_target_pairs={{0,8},{4,28},{8,16},{12,4},{16,24},{20,12},{24,0},{28,20},{1,9},{5... | collective-permute-start | bytes 1179656 | tf_op jit(solution)/shard_map/ppermute | solution.py:96
  115.4 15.1 %collective-permute-start.23 = (bf16[768,256]{1,0:T(8,128)(2,1)}, bf16[768,256]{1,0:T(8,128)(2,1)}, u32[]{:S(2)}, u32[]{:S(2)}) collective-permute-start(bf16[768,256]{1,0:T(8,128)(2,1)} %collective-permute-done.22.near_ref), channel_id=1, source_target_pairs={{0,8},{4,28},{8,16},{12,4},{16,24},{20,12},{24,0},{28,20},{1,9},{5... | collective-permute-start | bytes 1179656 | tf_op jit(solution)/shard_map/ppermute | solution.py:96
  121.4 31.6 %collective-permute-start.63 = (bf16[768,256]{1,0:T(8,128)(2,1)S(1)}, bf16[768,256]{1,0:T(8,128)(2,1)S(1)}, u32[]{:S(2)}, u32[]{:S(2)}) collective-permute-start(bf16[768,256]{1,0:T(8,128)(2,1)S(1)} %get-tuple-element.23), channel_id=1, source_target_pairs={{0,1},{1,0},{2,3},{3,2},{4,5},{5,4},{6,7},{7,6},{8,9},{9,8},{10,11... | collective-permute-start | bytes 1179656 | tf_op jit(solution)/shard_map/ppermute | solution.py:111
  133.6 19.9 %collective-permute-start.64 = (bf16[768,256]{1,0:T(8,128)(2,1)S(1)}, bf16[768,256]{1,0:T(8,128)(2,1)S(1)}, u32[]{:S(2)}, u32[]{:S(2)}) collective-permute-start(bf16[768,256]{1,0:T(8,128)(2,1)S(1)} %get-tuple-element.26), channel_id=1, source_target_pairs={{0,1},{1,0},{2,3},{3,2},{4,5},{5,4},{6,7},{7,6},{8,9},{9,8},{10,11... | collective-permute-start | bytes 1179656 | tf_op jit(solution)/shard_map/ppermute | solution.py:111
  134.1 22.9 %collective-permute-start.65 = (bf16[768,256]{1,0:T(8,128)(2,1)S(1)}, bf16[768,256]{1,0:T(8,128)(2,1)S(1)}, u32[]{:S(2)}, u32[]{:S(2)}) collective-permute-start(bf16[768,256]{1,0:T(8,128)(2,1)S(1)} %get-tuple-element.29), channel_id=1, source_target_pairs={{0,1},{1,0},{2,3},{3,2},{4,5},{5,4},{6,7},{7,6},{8,9},{9,8},{10,11... | collective-permute-start | bytes 1179656 | tf_op jit(solution)/shard_map/ppermute | solution.py:111
  134.2 23.5 %collective-permute-start.66 = (bf16[768,256]{1,0:T(8,128)(2,1)S(1)}, bf16[768,256]{1,0:T(8,128)(2,1)S(1)}, u32[]{:S(2)}, u32[]{:S(2)}) collective-permute-start(bf16[768,256]{1,0:T(8,128)(2,1)S(1)} %get-tuple-element.32), channel_id=1, source_target_pairs={{0,1},{1,0},{2,3},{3,2},{4,5},{5,4},{6,7},{7,6},{8,9},{9,8},{10,11... | collective-permute-start | bytes 1179656 | tf_op jit(solution)/shard_map/ppermute | solution.py:111
  151.5 12.1 %collective-permute-start.37 = (bf16[768,256]{1,0:T(8,128)(2,1)S(1)}, bf16[768,256]{1,0:T(8,128)(2,1)S(1)}, u32[]{:S(2)}, u32[]{:S(2)}) collective-permute-start(bf16[768,256]{1,0:T(8,128)(2,1)S(1)} %get-tuple-element.23), channel_id=1, source_target_pairs={{0,2},{1,3},{2,0},{3,1},{4,6},{5,7},{6,4},{7,5},{8,10},{9,11},{10,... | collective-permute-start | bytes 1179656 | tf_op jit(solution)/shard_map/ppermute | solution.py:111
  153.0 19.0 %collective-permute-start.38 = (bf16[768,256]{1,0:T(8,128)(2,1)S(1)}, bf16[768,256]{1,0:T(8,128)(2,1)S(1)}, u32[]{:S(2)}, u32[]{:S(2)}) collective-permute-start(bf16[768,256]{1,0:T(8,128)(2,1)S(1)} %get-tuple-element.26), channel_id=1, source_target_pairs={{0,2},{1,3},{2,0},{3,1},{4,6},{5,7},{6,4},{7,5},{8,10},{9,11},{10,... | collective-permute-start | bytes 1179656 | tf_op jit(solution)/shard_map/ppermute | solution.py:111
  153.5 25.6 %collective-permute-start.39 = (bf16[768,256]{1,0:T(8,128)(2,1)S(1)}, bf16[768,256]{1,0:T(8,128)(2,1)S(1)}, u32[]{:S(2)}, u32[]{:S(2)}) collective-permute-start(bf16[768,256]{1,0:T(8,128)(2,1)S(1)} %get-tuple-element.29), channel_id=1, source_target_pairs={{0,2},{1,3},{2,0},{3,1},{4,6},{5,7},{6,4},{7,5},{8,10},{9,11},{10,... | collective-permute-start | bytes 1179656 | tf_op jit(solution)/shard_map/ppermute | solution.py:111
  157.0 26.3 %collective-permute-start.40 = (bf16[768,256]{1,0:T(8,128)(2,1)S(1)}, bf16[768,256]{1,0:T(8,128)(2,1)S(1)}, u32[]{:S(2)}, u32[]{:S(2)}) collective-permute-start(bf16[768,256]{1,0:T(8,128)(2,1)S(1)} %get-tuple-element.32), channel_id=1, source_target_pairs={{0,2},{1,3},{2,0},{3,1},{4,6},{5,7},{6,4},{7,5},{8,10},{9,11},{10,... | collective-permute-start | bytes 1179656 | tf_op jit(solution)/shard_map/ppermute | solution.py:111
  157.7 54.9 %collective-permute-start.24 = (bf16[4,128,1024]{2,1,0:T(8,128)(2,1)S(1)}, bf16[4,128,1024]{2,1,0:T(8,128)(2,1)S(1)}, u32[]{:S(2)}, u32[]{:S(2)}) collective-permute-start(bf16[4,128,1024]{2,1,0:T(8,128)(2,1)S(1)} %dynamic-slice_bitcast_fusion), channel_id=1, source_target_pairs={{0,4},{4,0},{8,12},{12,8},{16,20},{20,16},{24,28},{28,24},{1,5},{5... | collective-permute-start | bytes 3145736 | tf_op jit(solution)/shard_map/ppermute | solution.py:134
  163.5 21.0 %collective-permute-start.50 = (bf16[768,256]{1,0:T(8,128)(2,1)S(1)}, bf16[768,256]{1,0:T(8,128)(2,1)S(1)}, u32[]{:S(2)}, u32[]{:S(2)}) collective-permute-start(bf16[768,256]{1,0:T(8,128)(2,1)S(1)} %collective-permute-done.37), channel_id=1, source_target_pairs={{0,1},{1,0},{2,3},{3,2},{4,5},{5,4},{6,7},{7,6},{8,9},{9,8},{10,11... | collective-permute-start | bytes 1179656 | tf_op jit(solution)/shard_map/ppermute | solution.py:111
  172.0 13.0 %collective-permute-start.51 = (bf16[768,256]{1,0:T(8,128)(2,1)S(1)}, bf16[768,256]{1,0:T(8,128)(2,1)S(1)}, u32[]{:S(2)}, u32[]{:S(2)}) collective-permute-start(bf16[768,256]{1,0:T(8,128)(2,1)S(1)} %collective-permute-done.38), channel_id=1, source_target_pairs={{0,1},{1,0},{2,3},{3,2},{4,5},{5,4},{6,7},{7,6},{8,9},{9,8},{10,11... | collective-permute-start | bytes 1179656 | tf_op jit(solution)/shard_map/ppermute | solution.py:111
  184.6 14.8 %collective-permute-start.67 = (bf16[4,64,1024]{2,1,0:T(8,128)(2,1)S(1)}, bf16[4,64,1024]{2,1,0:T(8,128)(2,1)S(1)}, u32[]{:S(2)}, u32[]{:S(2)}) collective-permute-start(bf16[4,64,1024]{2,1,0:T(8,128)(2,1)S(1)} %dynamic-slice_bitcast_fusion.1), channel_id=1, source_target_pairs={{0,4},{4,0},{8,12},{12,8},{16,20},{20,16},{24,28},{28,24},{1,5},{5... | collective-permute-start | bytes 1572872 | tf_op jit(solution)/shard_map/ppermute | solution.py:134
  185.0 25.6 %collective-permute-start.41 = (bf16[4,64,1024]{2,1,0:T(8,128)(2,1)S(1)}, bf16[4,64,1024]{2,1,0:T(8,128)(2,1)S(1)}, u32[]{:S(2)}, u32[]{:S(2)}) collective-permute-start(bf16[4,64,1024]{2,1,0:T(8,128)(2,1)S(1)} %dynamic-slice_bitcast_fusion.3), channel_id=1, source_target_pairs={{0,4},{4,0},{8,12},{12,8},{16,20},{20,16},{24,28},{28,24},{1,5},{5... | collective-permute-start | bytes 1572872 | tf_op jit(solution)/shard_map/ppermute | solution.py:134
  199.4 11.6 %collective-permute-start.68 = (bf16[64,1024]{1,0:T(8,128)(2,1)S(1)}, bf16[64,1024]{1,0:T(8,128)(2,1)S(1)}, u32[]{:S(2)}, u32[]{:S(2)}) collective-permute-start(bf16[64,1024]{1,0:T(8,128)(2,1)S(1)} %fusion.41), channel_id=1, source_target_pairs={{0,8},{4,12},{8,16},{12,20},{16,24},{20,28},{24,0},{28,4},{1,9},{5... | collective-permute-start | bytes 393224 | tf_op jit(solution)/shard_map/ppermute | solution.py:145
  199.8 33.4 %collective-permute-start.54 = (bf16[4,64,1024]{2,1,0:T(8,128)(2,1)S(1)}, bf16[4,64,1024]{2,1,0:T(8,128)(2,1)S(1)}, u32[]{:S(2)}, u32[]{:S(2)}) collective-permute-start(bf16[4,64,1024]{2,1,0:T(8,128)(2,1)S(1)} %dynamic-slice_bitcast_fusion.2), channel_id=1, source_target_pairs={{0,4},{4,0},{8,12},{12,8},{16,20},{20,16},{24,28},{28,24},{1,5},{5... | collective-permute-start | bytes 1572872 | tf_op jit(solution)/shard_map/ppermute | solution.py:134
  210.6 8.3 %collective-permute-start.42 = (bf16[64,1024]{1,0:T(8,128)(2,1)S(1)}, bf16[64,1024]{1,0:T(8,128)(2,1)S(1)}, u32[]{:S(2)}, u32[]{:S(2)}) collective-permute-start(bf16[64,1024]{1,0:T(8,128)(2,1)S(1)} %fusion.57), channel_id=1, source_target_pairs={{0,8},{4,12},{8,16},{12,20},{16,24},{20,28},{24,0},{28,4},{1,9},{5... | collective-permute-start | bytes 393224 | tf_op jit(solution)/shard_map/ppermute | solution.py:145
  211.1 10.7 %collective-permute-start.69 = (bf16[64,1024]{1,0:T(8,128)(2,1)S(1)}, bf16[64,1024]{1,0:T(8,128)(2,1)S(1)}, u32[]{:S(2)}, u32[]{:S(2)}) collective-permute-start(bf16[64,1024]{1,0:T(8,128)(2,1)S(1)} %fusion.43), channel_id=1, source_target_pairs={{0,8},{4,12},{8,16},{12,20},{16,24},{20,28},{24,0},{28,4},{1,9},{5... | collective-permute-start | bytes 393224 | tf_op jit(solution)/shard_map/ppermute | solution.py:145
  212.7 18.8 %collective-permute-start.25 = (bf16[128,1024]{1,0:T(8,128)(2,1)S(1)}, bf16[128,1024]{1,0:T(8,128)(2,1)S(1)}, u32[]{:S(2)}, u32[]{:S(2)}) collective-permute-start(bf16[128,1024]{1,0:T(8,128)(2,1)S(1)} %fusion.33), channel_id=1, source_target_pairs={{0,8},{4,12},{8,16},{12,20},{16,24},{20,28},{24,0},{28,4},{1,9},{5... | collective-permute-start | bytes 786440 | tf_op jit(solution)/shard_map/ppermute | solution.py:145
  219.0 10.9 %collective-permute-start.43 = (bf16[64,1024]{1,0:T(8,128)(2,1)S(1)}, bf16[64,1024]{1,0:T(8,128)(2,1)S(1)}, u32[]{:S(2)}, u32[]{:S(2)}) collective-permute-start(bf16[64,1024]{1,0:T(8,128)(2,1)S(1)} %fusion.59), channel_id=1, source_target_pairs={{0,8},{4,12},{8,16},{12,20},{16,24},{20,28},{24,0},{28,4},{1,9},{5... | collective-permute-start | bytes 393224 | tf_op jit(solution)/shard_map/ppermute | solution.py:145
  221.8 9.5 %collective-permute-start.70 = (bf16[64,1024]{1,0:T(8,128)(2,1)S(1)}, bf16[64,1024]{1,0:T(8,128)(2,1)S(1)}, u32[]{:S(2)}, u32[]{:S(2)}) collective-permute-start(bf16[64,1024]{1,0:T(8,128)(2,1)S(1)} %fusion.45), channel_id=1, source_target_pairs={{0,8},{4,12},{8,16},{12,20},{16,24},{20,28},{24,0},{28,4},{1,9},{5... | collective-permute-start | bytes 393224 | tf_op jit(solution)/shard_map/ppermute | solution.py:145
  231.4 17.0 %collective-permute-start.71 = (bf16[64,1024]{1,0:T(8,128)(2,1)S(1)}, bf16[64,1024]{1,0:T(8,128)(2,1)S(1)}, u32[]{:S(2)}, u32[]{:S(2)}) collective-permute-start(bf16[64,1024]{1,0:T(8,128)(2,1)S(1)} %get-tuple-element.44), channel_id=1, source_target_pairs={{0,8},{4,12},{8,16},{12,20},{16,24},{20,28},{24,0},{28,4},{1,9},{5... | collective-permute-start | bytes 393224 | tf_op jit(solution)/shard_map/ppermute | solution.py:152
  231.6 18.7 %collective-permute-start.26 = (bf16[128,1024]{1,0:T(8,128)(2,1)S(1)}, bf16[128,1024]{1,0:T(8,128)(2,1)S(1)}, u32[]{:S(2)}, u32[]{:S(2)}) collective-permute-start(bf16[128,1024]{1,0:T(8,128)(2,1)S(1)} %fusion.35), channel_id=1, source_target_pairs={{0,8},{4,12},{8,16},{12,20},{16,24},{20,28},{24,0},{28,4},{1,9},{5... | collective-permute-start | bytes 786440 | tf_op jit(solution)/shard_map/ppermute | solution.py:145
  233.2 15.1 %collective-permute-start.55 = (bf16[64,1024]{1,0:T(8,128)(2,1)S(1)}, bf16[64,1024]{1,0:T(8,128)(2,1)S(1)}, u32[]{:S(2)}, u32[]{:S(2)}) collective-permute-start(bf16[64,1024]{1,0:T(8,128)(2,1)S(1)} %fusion.49), channel_id=1, source_target_pairs={{0,8},{4,12},{8,16},{12,20},{16,24},{20,28},{24,0},{28,4},{1,9},{5... | collective-permute-start | bytes 393224 | tf_op jit(solution)/shard_map/ppermute | solution.py:145
  238.3 12.0 %collective-permute-start.45 = (bf16[64,1024]{1,0:T(8,128)(2,1)S(1)}, bf16[64,1024]{1,0:T(8,128)(2,1)S(1)}, u32[]{:S(2)}, u32[]{:S(2)}) collective-permute-start(bf16[64,1024]{1,0:T(8,128)(2,1)S(1)} %get-tuple-element.40), channel_id=1, source_target_pairs={{0,8},{4,12},{8,16},{12,20},{16,24},{20,28},{24,0},{28,4},{1,9},{5... | collective-permute-start | bytes 393224 | tf_op jit(solution)/shard_map/ppermute | solution.py:152
  248.4 8.3 %collective-permute-start.56 = (bf16[64,1024]{1,0:T(8,128)(2,1)S(1)}, bf16[64,1024]{1,0:T(8,128)(2,1)S(1)}, u32[]{:S(2)}, u32[]{:S(2)}) collective-permute-start(bf16[64,1024]{1,0:T(8,128)(2,1)S(1)} %fusion.51), channel_id=1, source_target_pairs={{0,8},{4,12},{8,16},{12,20},{16,24},{20,28},{24,0},{28,4},{1,9},{5... | collective-permute-start | bytes 393224 | tf_op jit(solution)/shard_map/ppermute | solution.py:145
  248.5 11.0 %collective-permute-start.72 = (bf16[64,1024]{1,0:T(8,128)(2,1)S(1)}, bf16[64,1024]{1,0:T(8,128)(2,1)S(1)}, u32[]{:S(2)}, u32[]{:S(2)}) collective-permute-start(bf16[64,1024]{1,0:T(8,128)(2,1)S(1)} %collective-permute-done.71), channel_id=1, source_target_pairs={{0,8},{4,12},{8,16},{12,20},{16,24},{20,28},{24,0},{28,4},{1,9},{5... | collective-permute-start | bytes 393224 | tf_op jit(solution)/shard_map/ppermute | solution.py:152
  250.3 12.0 %collective-permute-start.46 = (bf16[64,1024]{1,0:T(8,128)(2,1)S(1)}, bf16[64,1024]{1,0:T(8,128)(2,1)S(1)}, u32[]{:S(2)}, u32[]{:S(2)}) collective-permute-start(bf16[64,1024]{1,0:T(8,128)(2,1)S(1)} %collective-permute-done.45), channel_id=1, source_target_pairs={{0,8},{4,12},{8,16},{12,20},{16,24},{20,28},{24,0},{28,4},{1,9},{5... | collective-permute-start | bytes 393224 | tf_op jit(solution)/shard_map/ppermute | solution.py:152
  250.5 22.7 %collective-permute-start.27 = (bf16[128,1024]{1,0:T(8,128)(2,1)S(1)}, bf16[128,1024]{1,0:T(8,128)(2,1)S(1)}, u32[]{:S(2)}, u32[]{:S(2)}) collective-permute-start(bf16[128,1024]{1,0:T(8,128)(2,1)S(1)} %fusion.37), channel_id=1, source_target_pairs={{0,8},{4,12},{8,16},{12,20},{16,24},{20,28},{24,0},{28,4},{1,9},{5... | collective-permute-start | bytes 786440 | tf_op jit(solution)/shard_map/ppermute | solution.py:145
  256.7 16.3 %collective-permute-start.57 = (bf16[64,1024]{1,0:T(8,128)(2,1)S(1)}, bf16[64,1024]{1,0:T(8,128)(2,1)S(1)}, u32[]{:S(2)}, u32[]{:S(2)}) collective-permute-start(bf16[64,1024]{1,0:T(8,128)(2,1)S(1)} %fusion.53), channel_id=1, source_target_pairs={{0,8},{4,12},{8,16},{12,20},{16,24},{20,28},{24,0},{28,4},{1,9},{5... | collective-permute-start | bytes 393224 | tf_op jit(solution)/shard_map/ppermute | solution.py:145
  259.5 11.3 %collective-permute-start.73 = (bf16[64,1024]{1,0:T(8,128)(2,1)S(1)}, bf16[64,1024]{1,0:T(8,128)(2,1)S(1)}, u32[]{:S(2)}, u32[]{:S(2)}) collective-permute-start(bf16[64,1024]{1,0:T(8,128)(2,1)S(1)} %collective-permute-done.72), channel_id=1, source_target_pairs={{0,8},{4,12},{8,16},{12,20},{16,24},{20,28},{24,0},{28,4},{1,9},{5... | collective-permute-start | bytes 393224 | tf_op jit(solution)/shard_map/ppermute | solution.py:152
  262.3 9.9 %collective-permute-start.47 = (bf16[64,1024]{1,0:T(8,128)(2,1)S(1)}, bf16[64,1024]{1,0:T(8,128)(2,1)S(1)}, u32[]{:S(2)}, u32[]{:S(2)}) collective-permute-start(bf16[64,1024]{1,0:T(8,128)(2,1)S(1)} %collective-permute-done.46), channel_id=1, source_target_pairs={{0,8},{4,12},{8,16},{12,20},{16,24},{20,28},{24,0},{28,4},{1,9},{5... | collective-permute-start | bytes 393224 | tf_op jit(solution)/shard_map/ppermute | solution.py:152
  270.8 28.5 %collective-permute-start.74 = (bf16[4,64,1024]{2,1,0:T(8,128)(2,1)S(1)}, bf16[4,64,1024]{2,1,0:T(8,128)(2,1)S(1)}, u32[]{:S(2)}, u32[]{:S(2)}) collective-permute-start(bf16[4,64,1024]{2,1,0:T(8,128)(2,1)S(1)} %bitcast_dynamic-update-slice_fusion.4), channel_id=1, source_target_pairs={{0,4},{4,0},{8,12},{12,8},{16,20},{20,16},{24,28},{28,24},{1,5},{5... | collective-permute-start | bytes 1572872 | tf_op jit(solution)/shard_map/ppermute | solution.py:154
  272.2 27.3 %collective-permute-start.48 = (bf16[4,64,1024]{2,1,0:T(8,128)(2,1)S(1)}, bf16[4,64,1024]{2,1,0:T(8,128)(2,1)S(1)}, u32[]{:S(2)}, u32[]{:S(2)}) collective-permute-start(bf16[4,64,1024]{2,1,0:T(8,128)(2,1)S(1)} %bitcast_dynamic-update-slice_fusion.12), channel_id=1, source_target_pairs={{0,4},{4,0},{8,12},{12,8},{16,20},{20,16},{24,28},{28,24},{1,5},{5... | collective-permute-start | bytes 1572872 | tf_op jit(solution)/shard_map/ppermute | solution.py:154
  275.2 23.4 %collective-permute-start.33 = (bf16[128,1024]{1,0:T(8,128)(2,1)S(1)}, bf16[128,1024]{1,0:T(8,128)(2,1)S(1)}, u32[]{:S(2)}, u32[]{:S(2)}) collective-permute-start(bf16[128,1024]{1,0:T(8,128)(2,1)S(1)} %get-tuple-element.42), channel_id=1, source_target_pairs={{0,8},{4,12},{8,16},{12,20},{16,24},{20,28},{24,0},{28,4},{1,9},{5... | collective-permute-start | bytes 786440 | tf_op jit(solution)/shard_map/ppermute | solution.py:152
  296.2 12.3 %collective-permute-start.61 = (bf16[4,64,1024]{2,1,0:T(8,128)(2,1)S(1)}, bf16[4,64,1024]{2,1,0:T(8,128)(2,1)S(1)}, u32[]{:S(2)}, u32[]{:S(2)}) collective-permute-start(bf16[4,64,1024]{2,1,0:T(8,128)(2,1)S(1)} %bitcast_dynamic-update-slice_fusion.8), channel_id=1, source_target_pairs={{0,4},{4,0},{8,12},{12,8},{16,20},{20,16},{24,28},{28,24},{1,5},{5... | collective-permute-start | bytes 1572872 | tf_op jit(solution)/shard_map/ppermute | solution.py:154
  299.5 16.5 %collective-permute-start.75 = (bf16[512,1024]{1,0:T(8,128)(2,1)S(1)}, bf16[512,1024]{1,0:T(8,128)(2,1)}, u32[]{:S(2)}, u32[]{:S(2)}) collective-permute-start(bf16[512,1024]{1,0:T(8,128)(2,1)S(1)} %bitcast.211), channel_id=1, source_target_pairs={{0,1},{1,0},{2,3},{3,2},{4,5},{5,4},{6,7},{7,6},{8,9},{9,8},{10,11... | collective-permute-start | bytes 3145736 | tf_op jit(solution)/shard_map/ppermute | solution.py:167
  301.1 26.5 %collective-permute-start.49 = (bf16[512,1024]{0,1:T(8,128)(2,1)}, bf16[512,1024]{0,1:T(8,128)(2,1)}, u32[]{:S(2)}, u32[]{:S(2)}) collective-permute-start(bf16[512,1024]{0,1:T(8,128)(2,1)} %copy.45), channel_id=1, source_target_pairs={{0,2},{1,3},{2,0},{3,1},{4,6},{5,7},{6,4},{7,5},{8,10},{9,11},{10,... | collective-permute-start | bytes 3145736 | tf_op jit(solution)/shard_map/ppermute | solution.py:167
  306.8 8.4 %collective-permute-start.35 = (bf16[128,1024]{1,0:T(8,128)(2,1)}, bf16[128,1024]{1,0:T(8,128)(2,1)S(1)}, u32[]{:S(2)}, u32[]{:S(2)}) collective-permute-start(bf16[128,1024]{1,0:T(8,128)(2,1)} %collective-permute-done.34), channel_id=1, source_target_pairs={{0,8},{4,12},{8,16},{12,20},{16,24},{20,28},{24,0},{28,4},{1,9},{5... | collective-permute-start | bytes 786440 | tf_op jit(solution)/shard_map/ppermute | solution.py:152
  310.1 38.9 %collective-permute-start.62 = (bf16[512,1024]{0,1:T(8,128)(2,1)}, bf16[512,1024]{0,1:T(8,128)(2,1)}, u32[]{:S(2)}, u32[]{:S(2)}) collective-permute-start(bf16[512,1024]{0,1:T(8,128)(2,1)} %copy.51), channel_id=1, source_target_pairs={{0,3},{1,2},{2,1},{3,0},{4,7},{5,6},{6,5},{7,4},{8,11},{9,10},{10,... | collective-permute-start | bytes 3145736 | tf_op jit(solution)/shard_map/ppermute | solution.py:167
  315.9 38.6 %collective-permute-start.36 = (bf16[4,128,1024]{2,1,0:T(8,128)(2,1)}, bf16[4,128,1024]{2,1,0:T(8,128)(2,1)}, u32[]{:S(2)}, u32[]{:S(2)}) collective-permute-start(bf16[4,128,1024]{2,1,0:T(8,128)(2,1)} %bitcast_dynamic-update-slice_fusion), channel_id=1, source_target_pairs={{0,4},{4,0},{8,12},{12,8},{16,20},{20,16},{24,28},{28,24},{1,5},{5... | collective-permute-start | bytes 3145736 | tf_op jit(solution)/shard_map/ppermute | solution.py:154
  (36 other events, 181.2 us)

commit v3 on v2

v3 whole, which is shorter than its diff:
```python
import functools

import jax
import jax.numpy as jnp
from jax import lax
from jax.experimental import pallas as pl
from jax.experimental.pallas import tpu as pltpu
from jax.sharding import PartitionSpec as P

CHUNKS = 4
F32 = jnp.float32
BF16 = jnp.bfloat16
VMEM_LIMIT = 48 * 1024 * 1024


class Order:
    def __init__(self, token):
        self.token = token

    def __call__(self, *values):
        *values, self.token = lax.optimization_barrier((*values, self.token))
        return values[0] if len(values) == 1 else tuple(values)


def product_kernel(stage, place_ref, blocks_ref, field_ref, near_ref, far_ref, *refs):
    elements, size, _ = blocks_ref.shape
    width = field_ref.shape[1]
    squares = jnp.zeros((8, width), F32)
    filler = jnp.zeros((size, width), BF16)
    for element in range(elements):
        picked = []
        for slot in range(7):
            source = field_ref if slot < 5 else near_ref if slot == 5 else far_ref
            first_row = pl.multiple_of(place_ref[element, slot] * size, size)
            picked.append(source[pl.ds(first_row, size), :])
        stacked = jnp.concatenate(picked + [filler], axis=0)
        total = jnp.dot(blocks_ref[element], stacked, preferred_element_type=F32)
        here = pl.ds(element * size, size)
        if stage == 0:
            wide_ref, half_ref = refs
            wide_ref[here, :] = total
            half_ref[here, :] = total.astype(BF16)
        elif stage == 1:
            before_ref, half_ref = refs
            half_ref[here, :] = (2.0 * total - before_ref[here, :].astype(F32)).astype(BF16)
        else:
            before_ref, half_ref, squares_ref = refs
            value = (2.0 * total - before_ref[here, :]).astype(BF16)
            half_ref[here, :] = value
            wide = value.astype(F32)
            squares += jnp.sum((wide * wide).reshape(-1, 8, width), axis=0)
    if stage == 2:
        squares_ref[...] = squares


def call(kernel, name, outs, scalars, args, scratch=(), aliases=None):
    return pl.pallas_call(
        kernel,
        out_shape=outs,
        in_specs=[pl.BlockSpec(memory_space=pltpu.SMEM)] * len(scalars)
        + [pl.BlockSpec(memory_space=pltpu.VMEM)] * len(args),
        scratch_shapes=list(scratch),
        input_output_aliases=aliases or {},
        compiler_params=pltpu.CompilerParams(vmem_limit_bytes=VMEM_LIMIT),
        cost_estimate=pl.CostEstimate(flops=1024, bytes_accessed=1024, transcendentals=0),
        name=name,
    )(*scalars, *args)


def product(stage, place, blocks, field, by_near, by_far, before=None):
    rows, width = field.shape
    half = jax.ShapeDtypeStruct((rows, width), BF16)
    wide = jax.ShapeDtypeStruct((rows, width), F32)
    squares = jax.ShapeDtypeStruct((8, width), F32)
    outs = ((wide, half), half, (half, squares))[stage]
    args = (blocks, field, by_near, by_far) + (() if before is None else (before,))
    kernel = functools.partial(product_kernel, stage)
    return call(kernel, f"product_{stage}", outs, (place,), args)


def put_in_place(where_ref, lines, mine_ref, far_ref, out_ref, base):
    odd, line = where_ref[0], where_ref[1]
    half = mine_ref.shape[0]
    height = half // lines
    for side, ref in ((odd, mine_ref), (1 - odd, far_ref)):
        for j in range(lines):
            number = lax.rem(line - j + lines, lines)
            first_row = pl.multiple_of(base + side * half + number * height, height)
            out_ref[pl.ds(first_row, height), :] = ref[j * height : (j + 1) * height, :]


TRANSPOSED_LEFT = (((0,), (0,)), ((), ()))
TRANSPOSED_RIGHT = (((1,), (1,)), ((), ()))


def side_by_side(refs):
    return jnp.concatenate([ref[...] for ref in refs], axis=1)


def gram_kernel(pair, where_ref, *refs):
    mine_ref, other_ref, whole = refs[-3:]
    fields = refs[:CHUNKS]
    half = whole.shape[0] // 2
    width = fields[0].shape[1]
    middle = CHUNKS * width // 2
    odd = where_ref[0]

    def fill(left, rights, count):
        for c, right in enumerate(rights):
            value = lax.dot_general(left, right[...], TRANSPOSED_LEFT, preferred_element_type=F32)
            whole[:count, c * width : (c + 1) * width] = value.astype(BF16)

    if pair:
        peers = refs[CHUNKS : 2 * CHUNKS]
        used = middle

        @pl.when(where_ref[2] == 0)
        def _():
            fill(side_by_side(peers[: CHUNKS // 2]), fields, middle)

        @pl.when(where_ref[2] == 1)
        def _():
            fill(side_by_side(fields[CHUNKS // 2 :]), peers, middle)
    else:
        used = middle + middle // 2
        upper = side_by_side(fields[CHUNKS // 2 :])
        fill(side_by_side(fields[: CHUNKS // 2]), fields, middle)
        corner = lax.dot_general(upper, upper, TRANSPOSED_LEFT, preferred_element_type=F32).astype(BF16)
        whole[middle:used, :middle] = corner[: middle // 2]
        whole[middle:used, middle:] = corner[middle // 2 :]
    if used < whole.shape[0]:
        whole[used:, :] = jnp.zeros((whole.shape[0] - used, whole.shape[1]), BF16)
    mine_ref[...] = whole[pl.ds(pl.multiple_of(odd * half, half), half), :]
    other_ref[...] = whole[pl.ds(pl.multiple_of((1 - odd) * half, half), half), :]


def own_kernel(lines, where_ref, *refs):
    fields = refs[:CHUNKS]
    mine_ref, far_ref, out_ref, block = refs[CHUNKS:]
    put_in_place(where_ref, lines, mine_ref, far_ref, block, 0)
    middle = CHUNKS * fields[0].shape[1] // 2
    lower, upper = side_by_side(fields[: CHUNKS // 2]), side_by_side(fields[CHUNKS // 2 :])
    corner = jnp.concatenate(
        [block[middle : middle + middle // 2, :middle], block[middle : middle + middle // 2, middle:]], axis=0
    )
    out_ref[:, :middle] = jnp.dot(lower, block[:middle, :middle], preferred_element_type=F32) + lax.dot_general(
        upper, block[:middle, middle:], TRANSPOSED_RIGHT, preferred_element_type=F32
    )
    out_ref[:, middle:] = jnp.dot(lower, block[:middle, middle:], preferred_element_type=F32) + jnp.dot(
        upper, corner, preferred_element_type=F32
    )


def pair_kernel(lines, last, where_ref, *refs):
    if last:
        level_ref, *refs = refs
        own = refs[CHUNKS + 5 : 2 * CHUNKS + 5]
    out_ref, block = refs[-2:]
    total_ref = refs[0]
    fields = refs[1 : CHUNKS + 1]
    mine_ref, far_ref, peer_mine_ref, peer_far_ref = refs[CHUNKS + 1 : CHUNKS + 5]
    height = block.shape[0] // 2
    width = fields[0].shape[1]
    used = CHUNKS * width // 2
    is_upper = where_ref[2]
    put_in_place(where_ref, lines, mine_ref, far_ref, block, is_upper * height)
    put_in_place(where_ref, lines, peer_mine_ref, peer_far_ref, block, (1 - is_upper) * height)

    def finish(mixed, c):
        here = slice(c * width, (c + 1) * width)
        value = total_ref[:, here] + mixed
        if last:
            value = (1.5 * own[c][...].astype(F32) - 0.5 * value) / jnp.sqrt(level_ref[0])
        out_ref[:, here] = value.astype(out_ref.dtype)

    def rows_of_block(c):
        first_row = c * width if c * width < used else height + c * width - used
        return block[first_row : first_row + width, :]

    @pl.when(is_upper == 0)
    def _():
        field = side_by_side(fields)
        for c in range(CHUNKS):
            here = slice(c * width, (c + 1) * width)
            right = jnp.concatenate([block[:used, here], block[height : height + used, here]], axis=0)
            finish(jnp.dot(field, right, preferred_element_type=F32), c)

    @pl.when(is_upper == 1)
    def _():
        field = side_by_side(fields)
        for c in range(CHUNKS):
            finish(lax.dot_general(field, rows_of_block(c), TRANSPOSED_RIGHT, preferred_element_type=F32), c)


def local(orbitals, hamiltonian, neighbours):
    elements, slots, size, _ = hamiltonian.shape
    rows, columns = orbitals.shape
    tiles = lax.axis_size("elem")
    groups = lax.axis_size("orb")
    lines = tiles // 2
    my_tile = lax.axis_index("elem")
    my_group = lax.axis_index("orb")
    odd = my_tile % 2
    line = my_tile // 2

    swap = [(i, i ^ 1) for i in range(tiles)]
    around = [(2 * i + side, 2 * ((i + 1) % lines) + side) for i in range(lines) for side in (0, 1)]
    outward = [(2 * i + side, 2 * ((i + 1 - 2 * side) % lines) + side) for i in range(lines) for side in (0, 1)]

    def to_group(value, d):
        return lax.ppermute(value, "orb", [(i, i ^ d) for i in range(groups)])

    place = neighbours % elements
    last_two = place[:, 5:]
    place = jnp.concatenate([place[:, :5], jnp.where(odd == 0, last_two[:, ::-1], last_two)], axis=1)
    by_slot = [hamiltonian[:, s] for s in range(5)]
    by_slot.append(jnp.where(odd == 0, hamiltonian[:, 6], hamiltonian[:, 5]))
    by_slot.append(jnp.where(odd == 0, hamiltonian[:, 5], hamiltonian[:, 6]))
    by_slot.append(jnp.zeros_like(by_slot[0]))
    blocks = jnp.concatenate(by_slot, axis=2)

    width = columns // CHUNKS
    fields = [lax.slice_in_dim(orbitals, c * width, (c + 1) * width, axis=1) for c in range(CHUNKS)]
    start = fields
    near = [lax.ppermute(field, "elem", swap) for field in fields]
    order = Order(jnp.zeros((8, 128), F32) + place[0, 0].astype(F32))
    blocks, place = order(blocks, place)

    jobs = [(stage, c) for stage in range(3) for c in range(CHUNKS)]
    far = {}
    firsts, squares, pieces = {}, [], [{} for _ in range(CHUNKS)]
    near = {(0, c): near[c] for c in range(CHUNKS)}
    current = {(0, c): fields[c] for c in range(CHUNKS)}

    def send_on(job):
        near[job] = order(near[job])
        far[job] = lax.ppermute(near[job], "elem", outward)

    def more_panel(c):
        for d in range(1, groups):
            if d & (d - 1):
                low = d & -d
                if d ^ low in pieces[c] and d not in pieces[c]:
                    pieces[c][d ^ low] = order(pieces[c][d ^ low])
                    pieces[c][d] = to_group(pieces[c][d ^ low], low)

    def multiply(job):
        stage, c = job
        far[job] = order(far[job])
        old = (None, start[c], firsts.get(c))[stage]
        out = product(stage, place, blocks, current[job], near[job], far[job], old)
        if stage == 0:
            firsts[c], out = order(*out)
        elif stage == 1:
            out = order(out)
        else:
            out, square = order(*out)
            squares.append(square)
            pieces[c][0] = out
            bit = groups // 2
            while bit:
                pieces[c][bit] = to_group(out, bit)
                bit //= 2
            if c:
                more_panel(c - 1)
            return
        current[(stage + 1, c)] = out
        near[(stage + 1, c)] = lax.ppermute(out, "elem", swap)

    for index, job in enumerate(jobs):
        send_on(job)
        if index:
            multiply(jobs[index - 1])
    multiply(jobs[-1])

    squares = sum(squares)
    if width % 128:
        squares = jnp.pad(squares, ((0, 0), (0, -width % 128)))
    squares = sum(squares[:, i : i + 128] for i in range(0, squares.shape[1], 128))
    gathered = lax.all_gather(squares, ("elem", "orb"))
    rows_total = rows * tiles
    level = None
    middle = columns // 2
    unit = 16 * tiles

    def is_upper(d):
        return (my_group & (1 << (d.bit_length() - 1))) != 0

    def where(d):
        return jnp.stack([odd, line, is_upper(d) if d else odd]).astype(jnp.int32)

    def all_chunks(d):
        return [pieces[c][d] for c in range(CHUNKS)]

    def gram_chunk(d):
        height = middle if d else middle + middle // 2
        height += -height % unit
        fields = all_chunks(0)
        if d:
            more_panel(CHUNKS - 1)
            fields += order(*all_chunks(d))
        half = jax.ShapeDtypeStruct((height // 2, columns), BF16)
        scratch = (pltpu.VMEM((height, columns), BF16),)
        name = "gram_pair" if d else "gram_own"
        return call(functools.partial(gram_kernel, d > 0), name, (half, half), (where(d),), fields, scratch)

    exchanged = {}

    def process(d):
        nonlocal level
        mine, other = order(*gram_chunk(d))
        other = lax.ppermute(other, "elem", swap)
        yield
        other = order(other)
        height = mine.shape[0] // lines

        def pair(index):
            return sum(lax.dynamic_slice_in_dim(v, index * height, height, 0).astype(F32) for v in (mine, other))

        running = None
        for hop in range(1, lines):
            part = pair((line - hop) % lines)
            if running is not None:
                part = part + running.astype(F32)
            running = lax.ppermute(part.astype(BF16), "elem", around)
            yield
            running = order(running)
        part = pair(line)
        if running is not None:
            part = part + running.astype(F32)
        if level is None:
            level = jnp.sum(order(gathered)) / (columns * groups * rows_total)
        part = (part / (level * rows_total)).astype(BF16)
        parts = [part]
        for hop in range(1, lines):
            part = lax.ppermute(part, "elem", around)
            yield
            part = order(part)
            parts.append(part)
        whole = jnp.concatenate(parts, axis=0)
        far_whole = lax.ppermute(whole, "elem", swap)
        if d:
            peer_whole = to_group(whole, d)
        yield
        far_whole = order(far_whole)
        if d == 0:
            exchanged[0] = (whole, far_whole)
            return
        peer_far = to_group(far_whole, d)
        yield
        peer_whole = order(peer_whole)
        peer_far = order(peer_far)
        exchanged[d] = (whole, far_whole, peer_whole, peer_far)

    queue = sorted(range(1, groups), key=lambda d: (d == 1, d))
    events = []
    for position, d in enumerate([0] + queue):
        ready = 0.0 if position == 0 else 10.0 + 0.1 * position
        times = [ready]
        reduced = 19.0 + 10.5 * position
        times += [reduced + 6.0 * hop for hop in range(2 * lines - 1)]
        times.append(max(times[-1] + 10.0, 77.0 + 10.5 * position))
        if d:
            times.append(times[-1] + 11.0 if d > 1 else times[-1] + 3.0)
        events += [(time, position, d) for time in times]
    events.sort()
    running = {d: process(d) for d in [0] + queue}
    left_over = {d: sum(1 for event in events if event[2] == d) for d in running}
    done = []
    mixed = None
    for _, _, d in events:
        next(running[d], None)
        left_over[d] -= 1
        if left_over[d]:
            continue
        done.append(d)
        parts = exchanged[d]
        last = len(done) == groups
        shape = jax.ShapeDtypeStruct((rows, columns), BF16 if last else F32)
        scratch = (pltpu.VMEM((len(parts) * parts[0].shape[0], columns), BF16),)
        if d == 0:
            args = (*all_chunks(0), *parts)
            mixed = order(call(functools.partial(own_kernel, lines), "mix_own", shape, (where(0),), args, scratch))
            continue
        args = (mixed, *all_chunks(d), *parts)
        scalars = (where(d),)
        if last:
            scalars += (level.reshape(1),)
            args += tuple(all_chunks(0))
        kernel = functools.partial(pair_kernel, lines, last)
        mixed = call(kernel, "mix_last" if last else "mix_pair", shape, scalars, args, scratch, {} if last else {1: 0})
        if not last:
            mixed = order(mixed)
    return mixed


def solution(mesh):
    return jax.shard_map(
        local,
        mesh=mesh,
        in_specs=(P("elem", "orb"), P("elem", None, None, None), P("elem", None)),
        out_specs=P("elem", "orb"),
        check_vma=False,
    )
```

time: 366 us -> 362 us (0.989)
  blocking collectives: 0 us -> 42.3 us
  waiting for transfers between devices: 214 us -> 176 us
  Pallas kernels: 18.2 us -> 47.8 us
  local copies, waits for them, and re-layouts: 37.6 us -> 12.6 us
  matrix products: 22.4 us -> 0 us
  starting transfers between devices: 54.4 us -> 64.4 us
    all_gather x0 -> x1, blocking collectives: none -> 42.3 us  [local(): gathered = lax.all_gather(squares, ('elem', 'orb'))]
    ppermute x76 -> x74, waiting for transfers between devices: 214 us -> 176 us  [the longest x12 45.7 us: send_on(): far[job] = lax.ppermute(near[job], 'elem', outward)]
    pallas_call x12 -> x20, Pallas kernels: 18.2 us -> 47.8 us  [call(): pl.pallas_call(kernel, out_shape=outs, in_specs=[pl.BlockSpec(memory_spac...]
    dot_general x8 -> x0, matrix products: 22.4 us -> none  [the longest x3 15.6 us: local(): mixed = mixed + jnp.dot(panel[d], block, preferred_element_type=F32)]
    convert_element_type x12 -> x16, other arithmetic: 0.79 us -> 12.8 us  [the longest x12 9.54 us: process(): running = lax.ppermute(part.astype(BF16), 'elem', around)]
    ppermute x76 -> x74, starting transfers between devices: 54.4 us -> 64.4 us  [the longest x8 32.5 us: multiply(): near[stage + 1, c] = lax.ppermute(out, 'elem', swap)]
    concatenate x7 -> x0, local copies, waits for them, and re-layouts: 8.06 us -> none  [the longest x3 7.87 us: local(): jnp.concatenate([jnp.where(lower, half, peer_half), jnp.where(lower, peer...]
    select_n x8 -> x0, other arithmetic: 7.43 us -> none  [the longest x3 4.38 us: local(): jnp.where(lower, half, peer_half)]
  transfers between devices with their start and end apart: 76 -> 74, of which waited for: 43 -> 45; matrix products, arithmetic and copies ran while one was open for 15% -> 6% of each run, Pallas kernels for 5% -> 10%
where the time goes in v3:
time: 362 us; the launch traced here: 361 us
  waiting for transfers between devices  176 us (49%)
  starting transfers between devices  64.4 us (18%)
  Pallas kernels  47.8 us (13%)
  blocking collectives  42.3 us (12%)
  other arithmetic  16.5 us (5%)
  local copies, waits for them, and re-layouts  12.6 us (3%)
    pallas_call x20, Pallas kernels, call(): pl.pallas_call(kernel, out_shape=outs, in_specs=[pl.BlockSpec(memory_spac...  47.8 us
    ppermute x12, waiting for transfers between devices, send_on(): far[job] = lax.ppermute(near[job], 'elem', outward)  45.7 us
    all_gather x1, blocking collectives, local(): gathered = lax.all_gather(squares, ('elem', 'orb'))  42.3 us
    ppermute x8, starting transfers between devices, multiply(): near[stage + 1, c] = lax.ppermute(out, 'elem', swap)  32.5 us
    ppermute x12, waiting for transfers between devices, process(): running = lax.ppermute(part.astype(BF16), 'elem', around)  31 us
    ppermute x4, waiting for transfers between devices, process(): far_whole = lax.ppermute(whole, 'elem', swap)  29.5 us
    ppermute x12, waiting for transfers between devices, process(): part = lax.ppermute(part, 'elem', around)  29 us
    ppermute x4, waiting for transfers between devices, process(): other = lax.ppermute(other, 'elem', swap)  22.9 us
  transfers between devices with their start and end apart: 74, of which 45 were waited for; matrix products, arithmetic and copies ran while one was open for 6% of the time, Pallas kernels for 10%

profile of v3, /device:TPU:0, one launch (start us, length us, event | category | flops | bytes accessed | tf_op | source)
XLA Modules:
  0.0 361.0 jit_solution(13029220747995617435)
XLA Ops:
  0.0 1.5 fusion.2
  1.5 3.0 collective-permute-start.2
  4.6 2.2 slice_bitcast_fusion
  6.8 1.7 fusion.1
  8.9 2.4 concatenate.18.blocks_ref
  11.4 10.6 %collective-permute-done.near_ref = bf16[768,256]{1,0:T(8,128)(2,1)S(1)} collective-permute-done((bf16[768,256]{1,0:T(8,128)(2,1)S(1)}, bf16[768,256]{1,0:T(8,128)(2,1)S(1)}, u32[]{:S(2)}, u32[]{:S(2)}) %collective-permute-start) | collective-permute-done | bytes 393248 | tf_op jit(solution)/shard_map/ppermute | solution.py:225
  22.1 1.8 collective-permute-start.1
  23.9 3.5 collective-permute-start.4
  27.9 8.0 %collective-permute-done.1.far_ref = bf16[768,256]{1,0:T(8,128)(2,1)S(1)} collective-permute-done((bf16[768,256]{1,0:T(8,128)(2,1)S(1)}, bf16[768,256]{1,0:T(8,128)(2,1)S(1)}, u32[]{:S(2)}, u32[]{:S(2)}) %collective-permute-start.1) | collective-permute-done | bytes 393248 | tf_op jit(solution)/shard_map/ppermute | solution.py:237
  37.5 5.1 %collective-permute-start.3 = (bf16[768,256]{1,0:T(8,128)(2,1)S(1)}, bf16[768,256]{1,0:T(8,128)(2,1)S(1)}, u32[]{:S(2)}, u32[]{:S(2)}) collective-permute-start(bf16[768,256]{1,0:T(8,128)(2,1)S(1)} %get-tuple-element.212.field_ref), channel_id=1, source_target_pairs={{0,4},{4,0},{8,12},{12,8},{16,20},{20,16},{24,28},{28,24},{1,5},{5... | collective-permute-start | bytes 1179656 | tf_op jit(solution)/shard_map/ppermute | solution.py:268
  42.6 1.8 collective-permute-done.7.far_ref
  45.9 5.1 %collective-permute-start.9 = (bf16[768,256]{1,0:T(8,128)(2,1)S(1)}, bf16[768,256]{1,0:T(8,128)(2,1)S(1)}, u32[]{:S(2)}, u32[]{:S(2)}) collective-permute-start(bf16[768,256]{1,0:T(8,128)(2,1)S(1)} %get-tuple-element.229.field_ref), channel_id=1, source_target_pairs={{0,4},{4,0},{8,12},{12,8},{16,20},{20,16},{24,28},{28,24},{1,5},{5... | collective-permute-start | bytes 1179656 | tf_op jit(solution)/shard_map/ppermute | solution.py:268
  51.0 1.8 collective-permute-done.5.far_ref
  54.4 5.1 %collective-permute-start.12 = (bf16[768,256]{1,0:T(8,128)(2,1)S(1)}, bf16[768,256]{1,0:T(8,128)(2,1)S(1)}, u32[]{:S(2)}, u32[]{:S(2)}) collective-permute-start(bf16[768,256]{1,0:T(8,128)(2,1)S(1)} %get-tuple-element.241.field_ref), channel_id=1, source_target_pairs={{0,4},{4,0},{8,12},{12,8},{16,20},{20,16},{24,28},{28,24},{1,5},{5... | collective-permute-start | bytes 1179656 | tf_op jit(solution)/shard_map/ppermute | solution.py:268
  59.4 1.8 collective-permute-done.10.far_ref
  62.8 5.1 %collective-permute-start.14 = (bf16[768,256]{1,0:T(8,128)(2,1)S(1)}, bf16[768,256]{1,0:T(8,128)(2,1)S(1)}, u32[]{:S(2)}, u32[]{:S(2)}) collective-permute-start(bf16[768,256]{1,0:T(8,128)(2,1)S(1)} %get-tuple-element.244.field_ref), channel_id=1, source_target_pairs={{0,4},{4,0},{8,12},{12,8},{16,20},{20,16},{24,28},{28,24},{1,5},{5... | collective-permute-start | bytes 1179656 | tf_op jit(solution)/shard_map/ppermute | solution.py:268
  67.9 1.8 collective-permute-done.8.far_ref
  71.2 5.1 %collective-permute-start.11 = (bf16[768,256]{1,0:T(8,128)(2,1)S(1)}, bf16[768,256]{1,0:T(8,128)(2,1)S(1)}, u32[]{:S(2)}, u32[]{:S(2)}) collective-permute-start(bf16[768,256]{1,0:T(8,128)(2,1)S(1)} %product_1.4.field_ref), channel_id=1, source_target_pairs={{0,4},{4,0},{8,12},{12,8},{16,20},{20,16},{24,28},{28,24},{1,5},{5... | collective-permute-start | bytes 1179656 | tf_op jit(solution)/shard_map/ppermute | solution.py:268
  76.3 1.7 collective-permute-done.15.far_ref
  79.6 5.1 %collective-permute-start.17 = (bf16[768,256]{1,0:T(8,128)(2,1)S(1)}, bf16[768,256]{1,0:T(8,128)(2,1)S(1)}, u32[]{:S(2)}, u32[]{:S(2)}) collective-permute-start(bf16[768,256]{1,0:T(8,128)(2,1)S(1)} %product_1.5.field_ref), channel_id=1, source_target_pairs={{0,4},{4,0},{8,12},{12,8},{16,20},{20,16},{24,28},{28,24},{1,5},{5... | collective-permute-start | bytes 1179656 | tf_op jit(solution)/shard_map/ppermute | solution.py:268
  84.7 1.7 collective-permute-done.13.far_ref
  88.1 6.8 %collective-permute-done.18.far_ref = bf16[768,256]{1,0:T(8,128)(2,1)S(1)} collective-permute-done((bf16[768,256]{1,0:T(8,128)(2,1)S(1)}, bf16[768,256]{1,0:T(8,128)(2,1)S(1)}, u32[]{:S(2)}, u32[]{:S(2)}) %collective-permute-start.18) | collective-permute-done | bytes 393248 | tf_op jit(solution)/shard_map/ppermute | solution.py:237
  97.8 5.6 %collective-permute-done.16.far_ref = bf16[768,256]{1,0:T(8,128)(2,1)S(1)} collective-permute-done((bf16[768,256]{1,0:T(8,128)(2,1)S(1)}, bf16[768,256]{1,0:T(8,128)(2,1)S(1)}, u32[]{:S(2)}, u32[]{:S(2)}) %collective-permute-start.16) | collective-permute-done | bytes 393248 | tf_op jit(solution)/shard_map/ppermute | solution.py:237
  104.6 1.8 collective-permute-start.23
  107.2 2.8 collective-permute-done.19.far_ref
  110.0 1.3 product_2.5
  111.9 1.5 collective-permute-start.25
  114.7 9.1 %collective-permute-done.21.far_ref = bf16[768,256]{1,0:T(8,128)(2,1)S(1)} collective-permute-done((bf16[768,256]{1,0:T(8,128)(2,1)S(1)}, bf16[768,256]{1,0:T(8,128)(2,1)S(1)}, u32[]{:S(2)}, u32[]{:S(2)}) %collective-permute-start.21) | collective-permute-done | bytes 393248 | tf_op jit(solution)/shard_map/ppermute | solution.py:237
  125.2 1.5 collective-permute-start.26
  126.7 2.9 collective-permute-done.24.far_ref
  133.3 2.9 gram_own.1
  137.2 4.2 %collective-permute-done.35.refs_7_.refs_4_ = bf16[768,256]{1,0:T(8,128)(2,1)S(1)} collective-permute-done((bf16[768,256]{1,0:T(8,128)(2,1)S(1)}, bf16[768,256]{1,0:T(8,128)(2,1)S(1)}, u32[]{:S(2)}, u32[]{:S(2)}) %collective-permute-start.35) | collective-permute-done | bytes 393248 | tf_op jit(solution)/shard_map/ppermute | solution.py:211
  146.0 1.6 gram_pair.3
  147.8 2.6 gram_pair.4
  151.3 2.4 gram_pair.5
  153.8 8.3 %collective-permute-done.27 = bf16[384,1024]{1,0:T(8,128)(2,1)} collective-permute-done((bf16[384,1024]{1,0:T(8,128)(2,1)}, bf16[384,1024]{1,0:T(8,128)(2,1)}, u32[]{:S(2)}, u32[]{:S(2)}) %collective-permute-start.27) | collective-permute-done | bytes 786464 | tf_op jit(solution)/shard_map/ppermute | solution.py:312
  163.2 7.9 %collective-permute-done.37 = bf16[96,1024]{1,0:T(8,128)(2,1)S(1)} collective-permute-done((bf16[96,1024]{1,0:T(8,128)(2,1)S(1)}, bf16[96,1024]{1,0:T(8,128)(2,1)S(1)}, u32[]{:S(2)}, u32[]{:S(2)}) %collective-permute-start.37) | collective-permute-done | bytes 196640 | tf_op jit(solution)/shard_map/ppermute | solution.py:325
  172.2 42.3 %all-gather = f32[256,128]{1,0:T(8,128)S(1)} all-gather(f32[8,128]{1,0:T(8,128)S(1)} %slice_add_fusion), channel_id=2, replica_groups=mesh['elem'=8,'orb'=4] {'elem','orb'}, dimensions={0}, use_global_device_ids=true | all-gather | bytes 135168 | tf_op jit(solution)/shard_map/all_gather | solution.py:280
  214.4 2.0 collective-permute-start.51
  217.8 7.0 %collective-permute-done.41 = bf16[64,1024]{1,0:T(8,128)(2,1)S(1)} collective-permute-done((bf16[64,1024]{1,0:T(8,128)(2,1)S(1)}, bf16[64,1024]{1,0:T(8,128)(2,1)S(1)}, u32[]{:S(2)}, u32[]{:S(2)}) %collective-permute-start.41) | collective-permute-done | bytes 131104 | tf_op jit(solution)/shard_map/ppermute | solution.py:325
  225.5 14.5 %collective-permute-done.51 = bf16[256,1024]{1,0:T(8,128)(2,1)S(1)} collective-permute-done((bf16[256,1024]{1,0:T(8,128)(2,1)S(1)}, bf16[256,1024]{1,0:T(8,128)(2,1)S(1)}, u32[]{:S(2)}, u32[]{:S(2)}) %collective-permute-start.51) | collective-permute-done | bytes 524320 | tf_op jit(solution)/shard_map/ppermute | solution.py:312
  245.5 4.9 %collective-permute-start.47 = (bf16[64,1024]{1,0:T(8,128)(2,1)S(1)}, bf16[64,1024]{1,0:T(8,128)(2,1)S(1)}, u32[]{:S(2)}, u32[]{:S(2)}) collective-permute-start(bf16[64,1024]{1,0:T(8,128)(2,1)S(1)} %add_convert_fusion.8), channel_id=1, source_target_pairs={{0,8},{4,12},{8,16},{12,20},{16,24},{20,28},{24,0},{28,4},{1,9},{5... | collective-permute-start | bytes 393224 | tf_op jit(solution)/shard_map/ppermute | solution.py:325
  251.5 4.3 %collective-permute-done.46 = bf16[64,1024]{1,0:T(8,128)(2,1)S(1)} collective-permute-done((bf16[64,1024]{1,0:T(8,128)(2,1)S(1)}, bf16[64,1024]{1,0:T(8,128)(2,1)S(1)}, u32[]{:S(2)}, u32[]{:S(2)}) %collective-permute-start.46) | collective-permute-done | bytes 131104 | tf_op jit(solution)/shard_map/ppermute | solution.py:325
  256.9 1.7 collective-permute-done.47
  259.7 1.8 collective-permute-done.56
  261.6 3.4 collective-permute-done.49
  265.0 2.9 collective-permute-done.50
  268.9 1.8 collective-permute-done.59
  270.8 2.7 collective-permute-done.57
  273.5 3.6 %collective-permute-done.53 = bf16[64,1024]{1,0:T(8,128)(2,1)S(1)} collective-permute-done((bf16[64,1024]{1,0:T(8,128)(2,1)S(1)}, bf16[64,1024]{1,0:T(8,128)(2,1)S(1)}, u32[]{:S(2)}, u32[]{:S(2)}) %collective-permute-start.53) | collective-permute-done | bytes 131104 | tf_op jit(solution)/shard_map/ppermute | solution.py:325
  279.7 2.3 collective-permute-done.60
  282.0 4.4 %collective-permute-done.55 = bf16[64,1024]{1,0:T(8,128)(2,1)S(1)} collective-permute-done((bf16[64,1024]{1,0:T(8,128)(2,1)S(1)}, bf16[64,1024]{1,0:T(8,128)(2,1)S(1)}, u32[]{:S(2)}, u32[]{:S(2)}) %collective-permute-start.55) | collective-permute-done | bytes 131104 | tf_op jit(solution)/shard_map/ppermute | solution.py:336
  286.4 2.8 collective-permute-done.69
  289.6 5.0 %collective-permute-done.58 = bf16[64,1024]{1,0:T(8,128)(2,1)S(1)} collective-permute-done((bf16[64,1024]{1,0:T(8,128)(2,1)S(1)}, bf16[64,1024]{1,0:T(8,128)(2,1)S(1)}, u32[]{:S(2)}, u32[]{:S(2)}) %collective-permute-start.58) | collective-permute-done | bytes 131104 | tf_op jit(solution)/shard_map/ppermute | solution.py:336
  294.6 2.7 collective-permute-done.70
  297.6 3.7 %collective-permute-done.61 = bf16[64,1024]{1,0:T(8,128)(2,1)S(1)} collective-permute-done((bf16[64,1024]{1,0:T(8,128)(2,1)S(1)}, bf16[64,1024]{1,0:T(8,128)(2,1)S(1)}, u32[]{:S(2)}, u32[]{:S(2)}) %collective-permute-start.61) | collective-permute-done | bytes 131104 | tf_op jit(solution)/shard_map/ppermute | solution.py:336
  304.3 8.1 %collective-permute-done.71.refs_7_ = bf16[256,1024]{1,0:T(8,128)(2,1)} collective-permute-done((bf16[256,1024]{1,0:T(8,128)(2,1)S(1)}, bf16[256,1024]{1,0:T(8,128)(2,1)}, u32[]{:S(2)}, u32[]{:S(2)}) %collective-permute-start.71) | collective-permute-done | bytes 524320 | tf_op jit(solution)/shard_map/ppermute | solution.py:341
  312.5 11.2 %collective-permute-done.66.refs_6_ = bf16[256,1024]{1,0:T(8,128)(2,1)} collective-permute-done((bf16[256,1024]{1,0:T(8,128)(2,1)}, bf16[256,1024]{1,0:T(8,128)(2,1)}, u32[]{:S(2)}, u32[]{:S(2)}) %collective-permute-start.66) | collective-permute-done | bytes 524320 | tf_op jit(solution)/shard_map/ppermute | solution.py:341
  324.5 1.7 collective-permute-start.68
  327.7 10.2 %collective-permute-done.52.refs_5_ = bf16[384,1024]{1,0:T(8,128)(2,1)} collective-permute-done((bf16[384,1024]{1,0:T(8,128)(2,1)S(1)}, bf16[384,1024]{1,0:T(8,128)(2,1)}, u32[]{:S(2)}, u32[]{:S(2)}) %collective-permute-start.52) | collective-permute-done | bytes 786464 | tf_op jit(solution)/shard_map/ppermute | solution.py:341
  337.9 4.8 %mix_own.1.refs_0_ = f32[768,1024]{1,0:T(8,128)} custom-call(s32[3]{0:T(128)S(1)} %copy-done.33, bf16[768,256]{1,0:T(8,128)(2,1)S(1)} %get-tuple-element.280.refs_0_.refs_10_, bf16[768,256]{1,0:T(8,128)(2,1)S(1)} %get-tuple-element.291.refs_1_.refs_11_, bf16[768,256]{1,0:T(8,128)(2,1)S(1)} %get-tuple-element.300.refs_2_.refs_12_, ...), custom_call_target="tpu_custom_call" | custom-call | flops 1024 | bytes 1024 | tf_op jit(solution)/shard_map/mix_own/pallas_call | solution.py:57
  342.8 6.1 %mix_pair.2.refs_0_ = f32[768,1024]{1,0:T(8,128)} custom-call(s32[3]{0:T(128)S(1)} %pad_add_fusion.4.where_ref, f32[768,1024]{1,0:T(8,128)} %mix_own.1.refs_0_, bf16[768,256]{1,0:T(8,128)(2,1)S(1)} %copy-done.1, bf16[768,256]{1,0:T(8,128)(2,1)S(1)} %copy-done.3, bf16[768,256]{1,0:T(8,128)(2,1)S(1)} %copy-done.5, ...), custom_call_target="tpu_custom_call", output_to_operand_aliasing={{}: (1, {})} | custom-call | flops 1024 | bytes 1024 | tf_op jit(solution)/shard_map/mix_pair/pallas_call | solution.py:57
  348.9 6.1 %mix_pair.3.refs_1_ = f32[768,1024]{1,0:T(8,128)} custom-call(s32[3]{0:T(128)S(1)} %pad_add_fusion.4.where_ref, f32[768,1024]{1,0:T(8,128)} %mix_pair.2.refs_0_, bf16[768,256]{1,0:T(8,128)(2,1)S(1)} %copy-done.9, bf16[768,256]{1,0:T(8,128)(2,1)S(1)} %copy-done.12, bf16[768,256]{1,0:T(8,128)(2,1)S(1)} %copy-done.15, ...), custom_call_target="tpu_custom_call", output_to_operand_aliasing={{}: (1, {})} | custom-call | flops 1024 | bytes 1024 | tf_op jit(solution)/shard_map/mix_pair/pallas_call | solution.py:57
  355.0 5.9 %mix_last.1 = bf16[768,1024]{1,0:T(8,128)(2,1)} custom-call(s32[3]{0:T(128)S(1)} %pad_add_fusion.1.where_ref, f32[1]{0:T(128)} %bitcast.13.refs_0_, f32[768,1024]{1,0:T(8,128)} %mix_pair.3.refs_1_, bf16[768,256]{1,0:T(8,128)(2,1)} %collective-permute-done.28.refs_4_.refs_2_, bf16[768,256]{1,0:T(8,128)(2,1)} %collective-permute-done.29.refs_5_.refs_3_, ...), custom_call_target="tpu_custom_call" | custom-call | flops 1024 | bytes 1024 | tf_op jit(solution)/shard_map/mix_last/pallas_call | solution.py:57
  (218 shorter events, 51.8 us)
Async XLA Ops:
  1.5 25.9 %collective-permute-start.2 = (bf16[768,256]{1,0:T(8,128)(2,1)S(1)}, bf16[768,256]{1,0:T(8,128)(2,1)S(1)}, u32[]{:S(2)}, u32[]{:S(2)}) collective-permute-start(bf16[768,256]{1,0:T(8,128)(2,1)S(1)} %get-tuple-element.400.field_ref.refs_0_), channel_id=1, source_target_pairs={{0,4},{4,0},{8,12},{12,8},{16,20},{20,16},{24,28},{28,24},{1,5},{5... | collective-permute-start | bytes 1179656 | tf_op jit(solution)/shard_map/ppermute | solution.py:225
  4.5 17.5 %collective-permute-start = (bf16[768,256]{1,0:T(8,128)(2,1)S(1)}, bf16[768,256]{1,0:T(8,128)(2,1)S(1)}, u32[]{:S(2)}, u32[]{:S(2)}) collective-permute-start(bf16[768,256]{1,0:T(8,128)(2,1)S(1)} %get-tuple-element.401.field_ref.refs_0_), channel_id=1, source_target_pairs={{0,4},{4,0},{8,12},{12,8},{16,20},{20,16},{24,28},{28,24},{1,5},{5... | collective-permute-start | bytes 1179656 | tf_op jit(solution)/shard_map/ppermute | solution.py:225
  22.1 13.9 %collective-permute-start.1 = (bf16[768,256]{1,0:T(8,128)(2,1)S(1)}, bf16[768,256]{1,0:T(8,128)(2,1)S(1)}, u32[]{:S(2)}, u32[]{:S(2)}) collective-permute-start(bf16[768,256]{1,0:T(8,128)(2,1)S(1)} %collective-permute-done.near_ref), channel_id=1, source_target_pairs={{0,8},{4,28},{8,16},{12,4},{16,24},{20,12},{24,0},{28,20},{1,9},{5... | collective-permute-start | bytes 1179656 | tf_op jit(solution)/shard_map/ppermute | solution.py:237
  23.9 13.6 %collective-permute-start.4 = (bf16[768,256]{1,0:T(8,128)(2,1)S(1)}, bf16[768,256]{1,0:T(8,128)(2,1)S(1)}, u32[]{:S(2)}, u32[]{:S(2)}) collective-permute-start(bf16[768,256]{1,0:T(8,128)(2,1)S(1)} %get-tuple-element.399.field_ref.refs_0_), channel_id=1, source_target_pairs={{0,4},{4,0},{8,12},{12,8},{16,20},{20,16},{24,28},{28,24},{1,5},{5... | collective-permute-start | bytes 1179656 | tf_op jit(solution)/shard_map/ppermute | solution.py:225
  27.4 16.9 %collective-permute-start.7 = (bf16[768,256]{1,0:T(8,128)(2,1)S(1)}, bf16[768,256]{1,0:T(8,128)(2,1)S(1)}, u32[]{:S(2)}, u32[]{:S(2)}) collective-permute-start(bf16[768,256]{1,0:T(8,128)(2,1)S(1)} %collective-permute-done.2.near_ref), channel_id=1, source_target_pairs={{0,8},{4,28},{8,16},{12,4},{16,24},{20,12},{24,0},{28,20},{1,9},{5... | collective-permute-start | bytes 1179656 | tf_op jit(solution)/shard_map/ppermute | solution.py:237
  27.4 18.4 %collective-permute-start.6 = (bf16[768,256]{1,0:T(8,128)(2,1)S(1)}, bf16[768,256]{1,0:T(8,128)(2,1)S(1)}, u32[]{:S(2)}, u32[]{:S(2)}) collective-permute-start(bf16[768,256]{1,0:T(8,128)(2,1)S(1)} %get-tuple-element.402.field_ref.refs_0_), channel_id=1, source_target_pairs={{0,4},{4,0},{8,12},{12,8},{16,20},{20,16},{24,28},{28,24},{1,5},{5... | collective-permute-start | bytes 1179656 | tf_op jit(solution)/shard_map/ppermute | solution.py:225
  37.4 15.3 %collective-permute-start.5 = (bf16[768,256]{1,0:T(8,128)(2,1)S(1)}, bf16[768,256]{1,0:T(8,128)(2,1)S(1)}, u32[]{:S(2)}, u32[]{:S(2)}) collective-permute-start(bf16[768,256]{1,0:T(8,128)(2,1)S(1)} %collective-permute-done.4.near_ref), channel_id=1, source_target_pairs={{0,8},{4,28},{8,16},{12,4},{16,24},{20,12},{24,0},{28,20},{1,9},{5... | collective-permute-start | bytes 1179656 | tf_op jit(solution)/shard_map/ppermute | solution.py:237
  37.5 16.8 %collective-permute-start.3 = (bf16[768,256]{1,0:T(8,128)(2,1)S(1)}, bf16[768,256]{1,0:T(8,128)(2,1)S(1)}, u32[]{:S(2)}, u32[]{:S(2)}) collective-permute-start(bf16[768,256]{1,0:T(8,128)(2,1)S(1)} %get-tuple-element.212.field_ref), channel_id=1, source_target_pairs={{0,4},{4,0},{8,12},{12,8},{16,20},{20,16},{24,28},{28,24},{1,5},{5... | collective-permute-start | bytes 1179656 | tf_op jit(solution)/shard_map/ppermute | solution.py:268
  45.9 15.3 %collective-permute-start.10 = (bf16[768,256]{1,0:T(8,128)(2,1)S(1)}, bf16[768,256]{1,0:T(8,128)(2,1)S(1)}, u32[]{:S(2)}, u32[]{:S(2)}) collective-permute-start(bf16[768,256]{1,0:T(8,128)(2,1)S(1)} %collective-permute-done.6.near_ref), channel_id=1, source_target_pairs={{0,8},{4,28},{8,16},{12,4},{16,24},{20,12},{24,0},{28,20},{1,9},{5... | collective-permute-start | bytes 1179656 | tf_op jit(solution)/shard_map/ppermute | solution.py:237
  45.9 16.8 %collective-permute-start.9 = (bf16[768,256]{1,0:T(8,128)(2,1)S(1)}, bf16[768,256]{1,0:T(8,128)(2,1)S(1)}, u32[]{:S(2)}, u32[]{:S(2)}) collective-permute-start(bf16[768,256]{1,0:T(8,128)(2,1)S(1)} %get-tuple-element.229.field_ref), channel_id=1, source_target_pairs={{0,4},{4,0},{8,12},{12,8},{16,20},{20,16},{24,28},{28,24},{1,5},{5... | collective-permute-start | bytes 1179656 | tf_op jit(solution)/shard_map/ppermute | solution.py:268
  54.3 15.3 %collective-permute-start.8 = (bf16[768,256]{1,0:T(8,128)(2,1)S(1)}, bf16[768,256]{1,0:T(8,128)(2,1)S(1)}, u32[]{:S(2)}, u32[]{:S(2)}) collective-permute-start(bf16[768,256]{1,0:T(8,128)(2,1)S(1)} %collective-permute-done.3.near_ref), channel_id=1, source_target_pairs={{0,8},{4,28},{8,16},{12,4},{16,24},{20,12},{24,0},{28,20},{1,9},{5... | collective-permute-start | bytes 1179656 | tf_op jit(solution)/shard_map/ppermute | solution.py:237
  54.4 16.8 %collective-permute-start.12 = (bf16[768,256]{1,0:T(8,128)(2,1)S(1)}, bf16[768,256]{1,0:T(8,128)(2,1)S(1)}, u32[]{:S(2)}, u32[]{:S(2)}) collective-permute-start(bf16[768,256]{1,0:T(8,128)(2,1)S(1)} %get-tuple-element.241.field_ref), channel_id=1, source_target_pairs={{0,4},{4,0},{8,12},{12,8},{16,20},{20,16},{24,28},{28,24},{1,5},{5... | collective-permute-start | bytes 1179656 | tf_op jit(solution)/shard_map/ppermute | solution.py:268
  62.7 15.3 %collective-permute-start.15 = (bf16[768,256]{1,0:T(8,128)(2,1)S(1)}, bf16[768,256]{1,0:T(8,128)(2,1)S(1)}, u32[]{:S(2)}, u32[]{:S(2)}) collective-permute-start(bf16[768,256]{1,0:T(8,128)(2,1)S(1)} %collective-permute-done.9.near_ref), channel_id=1, source_target_pairs={{0,8},{4,28},{8,16},{12,4},{16,24},{20,12},{24,0},{28,20},{1,9},{5... | collective-permute-start | bytes 1179656 | tf_op jit(solution)/shard_map/ppermute | solution.py:237
  62.8 16.8 %collective-permute-start.14 = (bf16[768,256]{1,0:T(8,128)(2,1)S(1)}, bf16[768,256]{1,0:T(8,128)(2,1)S(1)}, u32[]{:S(2)}, u32[]{:S(2)}) collective-permute-start(bf16[768,256]{1,0:T(8,128)(2,1)S(1)} %get-tuple-element.244.field_ref), channel_id=1, source_target_pairs={{0,4},{4,0},{8,12},{12,8},{16,20},{20,16},{24,28},{28,24},{1,5},{5... | collective-permute-start | bytes 1179656 | tf_op jit(solution)/shard_map/ppermute | solution.py:268
  71.1 15.3 %collective-permute-start.13 = (bf16[768,256]{1,0:T(8,128)(2,1)S(1)}, bf16[768,256]{1,0:T(8,128)(2,1)S(1)}, u32[]{:S(2)}, u32[]{:S(2)}) collective-permute-start(bf16[768,256]{1,0:T(8,128)(2,1)S(1)} %collective-permute-done.12.near_ref), channel_id=1, source_target_pairs={{0,8},{4,28},{8,16},{12,4},{16,24},{20,12},{24,0},{28,20},{1,9},{5... | collective-permute-start | bytes 1179656 | tf_op jit(solution)/shard_map/ppermute | solution.py:237
  71.2 16.8 %collective-permute-start.11 = (bf16[768,256]{1,0:T(8,128)(2,1)S(1)}, bf16[768,256]{1,0:T(8,128)(2,1)S(1)}, u32[]{:S(2)}, u32[]{:S(2)}) collective-permute-start(bf16[768,256]{1,0:T(8,128)(2,1)S(1)} %product_1.4.field_ref), channel_id=1, source_target_pairs={{0,4},{4,0},{8,12},{12,8},{16,20},{20,16},{24,28},{28,24},{1,5},{5... | collective-permute-start | bytes 1179656 | tf_op jit(solution)/shard_map/ppermute | solution.py:268
  79.6 15.3 %collective-permute-start.18 = (bf16[768,256]{1,0:T(8,128)(2,1)S(1)}, bf16[768,256]{1,0:T(8,128)(2,1)S(1)}, u32[]{:S(2)}, u32[]{:S(2)}) collective-permute-start(bf16[768,256]{1,0:T(8,128)(2,1)S(1)} %collective-permute-done.14.near_ref), channel_id=1, source_target_pairs={{0,8},{4,28},{8,16},{12,4},{16,24},{20,12},{24,0},{28,20},{1,9},{5... | collective-permute-start | bytes 1179656 | tf_op jit(solution)/shard_map/ppermute | solution.py:237
  79.6 17.7 %collective-permute-start.17 = (bf16[768,256]{1,0:T(8,128)(2,1)S(1)}, bf16[768,256]{1,0:T(8,128)(2,1)S(1)}, u32[]{:S(2)}, u32[]{:S(2)}) collective-permute-start(bf16[768,256]{1,0:T(8,128)(2,1)S(1)} %product_1.5.field_ref), channel_id=1, source_target_pairs={{0,4},{4,0},{8,12},{12,8},{16,20},{20,16},{24,28},{28,24},{1,5},{5... | collective-permute-start | bytes 1179656 | tf_op jit(solution)/shard_map/ppermute | solution.py:268
  88.0 15.3 %collective-permute-start.16 = (bf16[768,256]{1,0:T(8,128)(2,1)S(1)}, bf16[768,256]{1,0:T(8,128)(2,1)S(1)}, u32[]{:S(2)}, u32[]{:S(2)}) collective-permute-start(bf16[768,256]{1,0:T(8,128)(2,1)S(1)} %collective-permute-done.11.near_ref), channel_id=1, source_target_pairs={{0,8},{4,28},{8,16},{12,4},{16,24},{20,12},{24,0},{28,20},{1,9},{5... | collective-permute-start | bytes 1179656 | tf_op jit(solution)/shard_map/ppermute | solution.py:237
  96.2 11.1 %collective-permute-start.20 = (bf16[768,256]{1,0:T(8,128)(2,1)S(1)}, bf16[768,256]{1,0:T(8,128)(2,1)S(1)}, u32[]{:S(2)}, u32[]{:S(2)}) collective-permute-start(bf16[768,256]{1,0:T(8,128)(2,1)S(1)} %product_1.6.field_ref), channel_id=1, source_target_pairs={{0,4},{4,0},{8,12},{12,8},{16,20},{20,16},{24,28},{28,24},{1,5},{5... | collective-permute-start | bytes 1179656 | tf_op jit(solution)/shard_map/ppermute | solution.py:268
  97.3 12.7 %collective-permute-start.19 = (bf16[768,256]{1,0:T(8,128)(2,1)S(1)}, bf16[768,256]{1,0:T(8,128)(2,1)S(1)}, u32[]{:S(2)}, u32[]{:S(2)}) collective-permute-start(bf16[768,256]{1,0:T(8,128)(2,1)S(1)} %collective-permute-done.17.near_ref), channel_id=1, source_target_pairs={{0,8},{4,28},{8,16},{12,4},{16,24},{20,12},{24,0},{28,20},{1,9},{5... | collective-permute-start | bytes 1179656 | tf_op jit(solution)/shard_map/ppermute | solution.py:237
  104.6 8.7 %collective-permute-start.23 = (bf16[768,256]{1,0:T(8,128)(2,1)S(1)}, bf16[768,256]{1,0:T(8,128)(2,1)S(1)}, u32[]{:S(2)}, u32[]{:S(2)}) collective-permute-start(bf16[768,256]{1,0:T(8,128)(2,1)S(1)} %get-tuple-element.280.refs_0_.refs_10_), channel_id=1, source_target_pairs={{0,2},{1,3},{2,0},{3,1},{4,6},{5,7},{6,4},{7,5},{8,10},{9,11},{10,... | collective-permute-start | bytes 1179656 | tf_op jit(solution)/shard_map/ppermute | solution.py:211
  110.0 13.8 %collective-permute-start.21 = (bf16[768,256]{1,0:T(8,128)(2,1)S(1)}, bf16[768,256]{1,0:T(8,128)(2,1)S(1)}, u32[]{:S(2)}, u32[]{:S(2)}) collective-permute-start(bf16[768,256]{1,0:T(8,128)(2,1)S(1)} %collective-permute-done.20.near_ref), channel_id=1, source_target_pairs={{0,8},{4,28},{8,16},{12,4},{16,24},{20,12},{24,0},{28,20},{1,9},{5... | collective-permute-start | bytes 1179656 | tf_op jit(solution)/shard_map/ppermute | solution.py:237
  111.9 13.3 %collective-permute-start.25 = (bf16[768,256]{1,0:T(8,128)(2,1)S(1)}, bf16[768,256]{1,0:T(8,128)(2,1)S(1)}, u32[]{:S(2)}, u32[]{:S(2)}) collective-permute-start(bf16[768,256]{1,0:T(8,128)(2,1)S(1)} %get-tuple-element.291.refs_1_.refs_11_), channel_id=1, source_target_pairs={{0,2},{1,3},{2,0},{3,1},{4,6},{5,7},{6,4},{7,5},{8,10},{9,11},{10,... | collective-permute-start | bytes 1179656 | tf_op jit(solution)/shard_map/ppermute | solution.py:211
  114.2 15.4 %collective-permute-start.24 = (bf16[768,256]{1,0:T(8,128)(2,1)S(1)}, bf16[768,256]{1,0:T(8,128)(2,1)S(1)}, u32[]{:S(2)}, u32[]{:S(2)}) collective-permute-start(bf16[768,256]{1,0:T(8,128)(2,1)S(1)} %collective-permute-done.22.near_ref), channel_id=1, source_target_pairs={{0,8},{4,28},{8,16},{12,4},{16,24},{20,12},{24,0},{28,20},{1,9},{5... | collective-permute-start | bytes 1179656 | tf_op jit(solution)/shard_map/ppermute | solution.py:237
  125.2 11.9 %collective-permute-start.26 = (bf16[768,256]{1,0:T(8,128)(2,1)S(1)}, bf16[768,256]{1,0:T(8,128)(2,1)S(1)}, u32[]{:S(2)}, u32[]{:S(2)}) collective-permute-start(bf16[768,256]{1,0:T(8,128)(2,1)S(1)} %get-tuple-element.300.refs_2_.refs_12_), channel_id=1, source_target_pairs={{0,2},{1,3},{2,0},{3,1},{4,6},{5,7},{6,4},{7,5},{8,10},{9,11},{10,... | collective-permute-start | bytes 1179656 | tf_op jit(solution)/shard_map/ppermute | solution.py:211
  131.5 10.0 %collective-permute-start.35 = (bf16[768,256]{1,0:T(8,128)(2,1)S(1)}, bf16[768,256]{1,0:T(8,128)(2,1)S(1)}, u32[]{:S(2)}, u32[]{:S(2)}) collective-permute-start(bf16[768,256]{1,0:T(8,128)(2,1)S(1)} %get-tuple-element.301.refs_3_.refs_13_), channel_id=1, source_target_pairs={{0,2},{1,3},{2,0},{3,1},{4,6},{5,7},{6,4},{7,5},{8,10},{9,11},{10,... | collective-permute-start | bytes 1179656 | tf_op jit(solution)/shard_map/ppermute | solution.py:211
  132.8 9.8 %collective-permute-start.32 = (bf16[768,256]{1,0:T(8,128)(2,1)S(1)}, bf16[768,256]{1,0:T(8,128)(2,1)S(1)}, u32[]{:S(2)}, u32[]{:S(2)}) collective-permute-start(bf16[768,256]{1,0:T(8,128)(2,1)S(1)} %collective-permute-done.23.refs_4_.refs_1_), channel_id=1, source_target_pairs={{0,1},{1,0},{2,3},{3,2},{4,5},{5,4},{6,7},{7,6},{8,9},{9,8},{10,11... | collective-permute-start | bytes 1179656 | tf_op jit(solution)/shard_map/ppermute | solution.py:211
  132.8 10.0 %collective-permute-start.33 = (bf16[768,256]{1,0:T(8,128)(2,1)S(1)}, bf16[768,256]{1,0:T(8,128)(2,1)S(1)}, u32[]{:S(2)}, u32[]{:S(2)}) collective-permute-start(bf16[768,256]{1,0:T(8,128)(2,1)S(1)} %collective-permute-done.25.refs_5_.refs_2_), channel_id=1, source_target_pairs={{0,1},{1,0},{2,3},{3,2},{4,5},{5,4},{6,7},{7,6},{8,9},{9,8},{10,11... | collective-permute-start | bytes 1179656 | tf_op jit(solution)/shard_map/ppermute | solution.py:211
  141.4 20.7 %collective-permute-start.27 = (bf16[384,1024]{1,0:T(8,128)(2,1)}, bf16[384,1024]{1,0:T(8,128)(2,1)}, u32[]{:S(2)}, u32[]{:S(2)}) collective-permute-start(bf16[384,1024]{1,0:T(8,128)(2,1)} %get-tuple-element.307), channel_id=1, source_target_pairs={{0,4},{4,0},{8,12},{12,8},{16,20},{20,16},{24,28},{28,24},{1,5},{5... | collective-permute-start | bytes 2359304 | tf_op jit(solution)/shard_map/ppermute | solution.py:312
  150.4 66.1 %collective-permute-start.39 = (bf16[256,1024]{1,0:T(8,128)(2,1)S(1)}, bf16[256,1024]{1,0:T(8,128)(2,1)S(1)}, u32[]{:S(2)}, u32[]{:S(2)}) collective-permute-start(bf16[256,1024]{1,0:T(8,128)(2,1)S(1)} %get-tuple-element.341), channel_id=1, source_target_pairs={{0,4},{4,0},{8,12},{12,8},{16,20},{20,16},{24,28},{28,24},{1,5},{5... | collective-permute-start | bytes 1572872 | tf_op jit(solution)/shard_map/ppermute | solution.py:312
  172.1 44.5 %collective-permute-start.38 = (bf16[96,1024]{1,0:T(8,128)(2,1)S(1)}, bf16[96,1024]{1,0:T(8,128)(2,1)S(1)}, u32[]{:S(2)}, u32[]{:S(2)}) collective-permute-start(bf16[96,1024]{1,0:T(8,128)(2,1)S(1)} %add_convert_fusion.1), channel_id=1, source_target_pairs={{0,8},{4,12},{8,16},{12,20},{16,24},{20,28},{24,0},{28,4},{1,9},{5... | collective-permute-start | bytes 589832 | tf_op jit(solution)/shard_map/ppermute | solution.py:325
  214.4 29.0 %collective-permute-start.44 = (bf16[256,1024]{1,0:T(8,128)(2,1)}, bf16[256,1024]{1,0:T(8,128)(2,1)}, u32[]{:S(2)}, u32[]{:S(2)}) collective-permute-start(bf16[256,1024]{1,0:T(8,128)(2,1)} %get-tuple-element.353), channel_id=1, source_target_pairs={{0,4},{4,0},{8,12},{12,8},{16,20},{20,16},{24,28},{28,24},{1,5},{5... | collective-permute-start | bytes 1572872 | tf_op jit(solution)/shard_map/ppermute | solution.py:312
  214.4 25.6 %collective-permute-start.51 = (bf16[256,1024]{1,0:T(8,128)(2,1)S(1)}, bf16[256,1024]{1,0:T(8,128)(2,1)S(1)}, u32[]{:S(2)}, u32[]{:S(2)}) collective-permute-start(bf16[256,1024]{1,0:T(8,128)(2,1)S(1)} %get-tuple-element.367), channel_id=1, source_target_pairs={{0,4},{4,0},{8,12},{12,8},{16,20},{20,16},{24,28},{28,24},{1,5},{5... | collective-permute-start | bytes 1572872 | tf_op jit(solution)/shard_map/ppermute | solution.py:312
  216.5 8.2 %collective-permute-start.41 = (bf16[64,1024]{1,0:T(8,128)(2,1)S(1)}, bf16[64,1024]{1,0:T(8,128)(2,1)S(1)}, u32[]{:S(2)}, u32[]{:S(2)}) collective-permute-start(bf16[64,1024]{1,0:T(8,128)(2,1)S(1)} %add_convert_fusion.11), channel_id=1, source_target_pairs={{0,8},{4,12},{8,16},{12,20},{16,24},{20,28},{24,0},{28,4},{1,9},{5... | collective-permute-start | bytes 393224 | tf_op jit(solution)/shard_map/ppermute | solution.py:325
  217.7 23.3 %collective-permute-start.40 = (bf16[96,1024]{1,0:T(8,128)(2,1)S(1)}, bf16[96,1024]{1,0:T(8,128)(2,1)}, u32[]{:S(2)}, u32[]{:S(2)}) collective-permute-start(bf16[96,1024]{1,0:T(8,128)(2,1)S(1)} %add_convert_fusion), channel_id=1, source_target_pairs={{0,8},{4,12},{8,16},{12,20},{16,24},{20,28},{24,0},{28,4},{1,9},{5... | collective-permute-start | bytes 589832 | tf_op jit(solution)/shard_map/ppermute | solution.py:325
  225.5 17.9 %collective-permute-start.43 = (bf16[64,1024]{1,0:T(8,128)(2,1)}, bf16[64,1024]{1,0:T(8,128)(2,1)}, u32[]{:S(2)}, u32[]{:S(2)}) collective-permute-start(bf16[64,1024]{1,0:T(8,128)(2,1)} %add_convert_fusion.10), channel_id=1, source_target_pairs={{0,8},{4,12},{8,16},{12,20},{16,24},{20,28},{24,0},{28,4},{1,9},{5... | collective-permute-start | bytes 393224 | tf_op jit(solution)/shard_map/ppermute | solution.py:325
  241.0 9.5 %collective-permute-start.54 = (bf16[64,1024]{1,0:T(8,128)(2,1)}, bf16[64,1024]{1,0:T(8,128)(2,1)}, u32[]{:S(2)}, u32[]{:S(2)}) collective-permute-start(bf16[64,1024]{1,0:T(8,128)(2,1)} %add_convert_fusion.5), channel_id=1, source_target_pairs={{0,8},{4,12},{8,16},{12,20},{16,24},{20,28},{24,0},{28,4},{1,9},{5... | collective-permute-start | bytes 393224 | tf_op jit(solution)/shard_map/ppermute | solution.py:325
  243.3 35.8 %collective-permute-start.42 = (bf16[96,1024]{1,0:T(8,128)(2,1)S(1)}, bf16[96,1024]{1,0:T(8,128)(2,1)S(1)}, u32[]{:S(2)}, u32[]{:S(2)}) collective-permute-start(bf16[96,1024]{1,0:T(8,128)(2,1)S(1)} %divide_convert_fusion), channel_id=1, source_target_pairs={{0,8},{4,12},{8,16},{12,20},{16,24},{20,28},{24,0},{28,4},{1,9},{5... | collective-permute-start | bytes 589832 | tf_op jit(solution)/shard_map/ppermute | solution.py:336
  244.5 11.3 %collective-permute-start.46 = (bf16[64,1024]{1,0:T(8,128)(2,1)S(1)}, bf16[64,1024]{1,0:T(8,128)(2,1)S(1)}, u32[]{:S(2)}, u32[]{:S(2)}) collective-permute-start(bf16[64,1024]{1,0:T(8,128)(2,1)S(1)} %add_convert_fusion.9), channel_id=1, source_target_pairs={{0,8},{4,12},{8,16},{12,20},{16,24},{20,28},{24,0},{28,4},{1,9},{5... | collective-permute-start | bytes 393224 | tf_op jit(solution)/shard_map/ppermute | solution.py:325
  245.5 13.1 %collective-permute-start.47 = (bf16[64,1024]{1,0:T(8,128)(2,1)S(1)}, bf16[64,1024]{1,0:T(8,128)(2,1)S(1)}, u32[]{:S(2)}, u32[]{:S(2)}) collective-permute-start(bf16[64,1024]{1,0:T(8,128)(2,1)S(1)} %add_convert_fusion.8), channel_id=1, source_target_pairs={{0,8},{4,12},{8,16},{12,20},{16,24},{20,28},{24,0},{28,4},{1,9},{5... | collective-permute-start | bytes 393224 | tf_op jit(solution)/shard_map/ppermute | solution.py:325
  251.4 10.0 %collective-permute-start.56 = (bf16[64,1024]{1,0:T(8,128)(2,1)S(1)}, bf16[64,1024]{1,0:T(8,128)(2,1)S(1)}, u32[]{:S(2)}, u32[]{:S(2)}) collective-permute-start(bf16[64,1024]{1,0:T(8,128)(2,1)S(1)} %add_convert_fusion.4), channel_id=1, source_target_pairs={{0,8},{4,12},{8,16},{12,20},{16,24},{20,28},{24,0},{28,4},{1,9},{5... | collective-permute-start | bytes 393224 | tf_op jit(solution)/shard_map/ppermute | solution.py:325
  256.9 8.1 %collective-permute-start.49 = (bf16[64,1024]{1,0:T(8,128)(2,1)S(1)}, bf16[64,1024]{1,0:T(8,128)(2,1)S(1)}, u32[]{:S(2)}, u32[]{:S(2)}) collective-permute-start(bf16[64,1024]{1,0:T(8,128)(2,1)S(1)} %divide_convert_fusion.3), channel_id=1, source_target_pairs={{0,8},{4,12},{8,16},{12,20},{16,24},{20,28},{24,0},{28,4},{1,9},{5... | collective-permute-start | bytes 393224 | tf_op jit(solution)/shard_map/ppermute | solution.py:336
  259.6 8.3 %collective-permute-start.50 = (bf16[64,1024]{1,0:T(8,128)(2,1)S(1)}, bf16[64,1024]{1,0:T(8,128)(2,1)S(1)}, u32[]{:S(2)}, u32[]{:S(2)}) collective-permute-start(bf16[64,1024]{1,0:T(8,128)(2,1)S(1)} %add_convert_fusion.7), channel_id=1, source_target_pairs={{0,8},{4,12},{8,16},{12,20},{16,24},{20,28},{24,0},{28,4},{1,9},{5... | collective-permute-start | bytes 393224 | tf_op jit(solution)/shard_map/ppermute | solution.py:325
  261.5 9.2 %collective-permute-start.59 = (bf16[64,1024]{1,0:T(8,128)(2,1)S(1)}, bf16[64,1024]{1,0:T(8,128)(2,1)S(1)}, u32[]{:S(2)}, u32[]{:S(2)}) collective-permute-start(bf16[64,1024]{1,0:T(8,128)(2,1)S(1)} %add_convert_fusion.3), channel_id=1, source_target_pairs={{0,8},{4,12},{8,16},{12,20},{16,24},{20,28},{24,0},{28,4},{1,9},{5... | collective-permute-start | bytes 393224 | tf_op jit(solution)/shard_map/ppermute | solution.py:325
  265.0 8.5 %collective-permute-start.57 = (bf16[64,1024]{1,0:T(8,128)(2,1)S(1)}, bf16[64,1024]{1,0:T(8,128)(2,1)S(1)}, u32[]{:S(2)}, u32[]{:S(2)}) collective-permute-start(bf16[64,1024]{1,0:T(8,128)(2,1)S(1)} %collective-permute-done.49), channel_id=1, source_target_pairs={{0,8},{4,12},{8,16},{12,20},{16,24},{20,28},{24,0},{28,4},{1,9},{5... | collective-permute-start | bytes 393224 | tf_op jit(solution)/shard_map/ppermute | solution.py:336
  268.8 8.3 %collective-permute-start.53 = (bf16[64,1024]{1,0:T(8,128)(2,1)S(1)}, bf16[64,1024]{1,0:T(8,128)(2,1)S(1)}, u32[]{:S(2)}, u32[]{:S(2)}) collective-permute-start(bf16[64,1024]{1,0:T(8,128)(2,1)S(1)} %add_convert_fusion.6), channel_id=1, source_target_pairs={{0,8},{4,12},{8,16},{12,20},{16,24},{20,28},{24,0},{28,4},{1,9},{5... | collective-permute-start | bytes 393224 | tf_op jit(solution)/shard_map/ppermute | solution.py:325
  270.8 8.4 %collective-permute-start.62 = (bf16[64,1024]{1,0:T(8,128)(2,1)S(1)}, bf16[64,1024]{1,0:T(8,128)(2,1)S(1)}, u32[]{:S(2)}, u32[]{:S(2)}) collective-permute-start(bf16[64,1024]{1,0:T(8,128)(2,1)S(1)} %divide_convert_fusion.1), channel_id=1, source_target_pairs={{0,8},{4,12},{8,16},{12,20},{16,24},{20,28},{24,0},{28,4},{1,9},{5... | collective-permute-start | bytes 393224 | tf_op jit(solution)/shard_map/ppermute | solution.py:336
  273.5 8.5 %collective-permute-start.60 = (bf16[64,1024]{1,0:T(8,128)(2,1)S(1)}, bf16[64,1024]{1,0:T(8,128)(2,1)S(1)}, u32[]{:S(2)}, u32[]{:S(2)}) collective-permute-start(bf16[64,1024]{1,0:T(8,128)(2,1)S(1)} %collective-permute-done.57), channel_id=1, source_target_pairs={{0,8},{4,12},{8,16},{12,20},{16,24},{20,28},{24,0},{28,4},{1,9},{5... | collective-permute-start | bytes 393224 | tf_op jit(solution)/shard_map/ppermute | solution.py:336
  278.1 8.3 %collective-permute-start.55 = (bf16[64,1024]{1,0:T(8,128)(2,1)S(1)}, bf16[64,1024]{1,0:T(8,128)(2,1)S(1)}, u32[]{:S(2)}, u32[]{:S(2)}) collective-permute-start(bf16[64,1024]{1,0:T(8,128)(2,1)S(1)} %divide_convert_fusion.2), channel_id=1, source_target_pairs={{0,8},{4,12},{8,16},{12,20},{16,24},{20,28},{24,0},{28,4},{1,9},{5... | collective-permute-start | bytes 393224 | tf_op jit(solution)/shard_map/ppermute | solution.py:336
  279.2 10.0 %collective-permute-start.69 = (bf16[64,1024]{1,0:T(8,128)(2,1)S(1)}, bf16[64,1024]{1,0:T(8,128)(2,1)S(1)}, u32[]{:S(2)}, u32[]{:S(2)}) collective-permute-start(bf16[64,1024]{1,0:T(8,128)(2,1)S(1)} %collective-permute-done.62), channel_id=1, source_target_pairs={{0,8},{4,12},{8,16},{12,20},{16,24},{20,28},{24,0},{28,4},{1,9},{5... | collective-permute-start | bytes 393224 | tf_op jit(solution)/shard_map/ppermute | solution.py:336
  279.2 15.4 %collective-permute-start.45 = (bf16[96,1024]{1,0:T(8,128)(2,1)S(1)}, bf16[96,1024]{1,0:T(8,128)(2,1)S(1)}, u32[]{:S(2)}, u32[]{:S(2)}) collective-permute-start(bf16[96,1024]{1,0:T(8,128)(2,1)S(1)} %collective-permute-done.42), channel_id=1, source_target_pairs={{0,8},{4,12},{8,16},{12,20},{16,24},{20,28},{24,0},{28,4},{1,9},{5... | collective-permute-start | bytes 589832 | tf_op jit(solution)/shard_map/ppermute | solution.py:336
  286.4 8.2 %collective-permute-start.58 = (bf16[64,1024]{1,0:T(8,128)(2,1)S(1)}, bf16[64,1024]{1,0:T(8,128)(2,1)S(1)}, u32[]{:S(2)}, u32[]{:S(2)}) collective-permute-start(bf16[64,1024]{1,0:T(8,128)(2,1)S(1)} %collective-permute-done.55), channel_id=1, source_target_pairs={{0,8},{4,12},{8,16},{12,20},{16,24},{20,28},{24,0},{28,4},{1,9},{5... | collective-permute-start | bytes 393224 | tf_op jit(solution)/shard_map/ppermute | solution.py:336
  289.2 14.3 %collective-permute-start.63 = (bf16[256,1024]{1,0:T(8,128)(2,1)S(1)}, bf16[256,1024]{1,0:T(8,128)(2,1)}, u32[]{:S(2)}, u32[]{:S(2)}) collective-permute-start(bf16[256,1024]{1,0:T(8,128)(2,1)S(1)} %pad_maximum_fusion.1.refs_5_), channel_id=1, source_target_pairs={{0,4},{4,0},{8,12},{12,8},{16,20},{20,16},{24,28},{28,24},{1,5},{5... | collective-permute-start | bytes 1572872 | tf_op jit(solution)/shard_map/ppermute | solution.py:341
  294.6 8.9 %collective-permute-start.48 = (bf16[96,1024]{1,0:T(8,128)(2,1)S(1)}, bf16[96,1024]{1,0:T(8,128)(2,1)S(1)}, u32[]{:S(2)}, u32[]{:S(2)}) collective-permute-start(bf16[96,1024]{1,0:T(8,128)(2,1)S(1)} %collective-permute-done.45), channel_id=1, source_target_pairs={{0,8},{4,12},{8,16},{12,20},{16,24},{20,28},{24,0},{28,4},{1,9},{5... | collective-permute-start | bytes 589832 | tf_op jit(solution)/shard_map/ppermute | solution.py:336
  297.3 15.2 %collective-permute-start.71 = (bf16[256,1024]{1,0:T(8,128)(2,1)S(1)}, bf16[256,1024]{1,0:T(8,128)(2,1)}, u32[]{:S(2)}, u32[]{:S(2)}) collective-permute-start(bf16[256,1024]{1,0:T(8,128)(2,1)S(1)} %pad_maximum_fusion.3.refs_6_), channel_id=1, source_target_pairs={{0,4},{4,0},{8,12},{12,8},{16,20},{20,16},{24,28},{28,24},{1,5},{5... | collective-permute-start | bytes 1572872 | tf_op jit(solution)/shard_map/ppermute | solution.py:341
  302.2 21.5 %collective-permute-start.66 = (bf16[256,1024]{1,0:T(8,128)(2,1)}, bf16[256,1024]{1,0:T(8,128)(2,1)}, u32[]{:S(2)}, u32[]{:S(2)}) collective-permute-start(bf16[256,1024]{1,0:T(8,128)(2,1)} %pad_maximum_fusion.2.refs_5_), channel_id=1, source_target_pairs={{0,4},{4,0},{8,12},{12,8},{16,20},{20,16},{24,28},{28,24},{1,5},{5... | collective-permute-start | bytes 1572872 | tf_op jit(solution)/shard_map/ppermute | solution.py:341
  302.4 21.3 %collective-permute-start.64 = (bf16[256,1024]{1,0:T(8,128)(2,1)S(1)}, bf16[256,1024]{1,0:T(8,128)(2,1)S(1)}, u32[]{:S(2)}, u32[]{:S(2)}) collective-permute-start(bf16[256,1024]{1,0:T(8,128)(2,1)S(1)} %pad_maximum_fusion.1.refs_5_), channel_id=1, source_target_pairs={{0,2},{1,3},{2,0},{3,1},{4,6},{5,7},{6,4},{7,5},{8,10},{9,11},{10,... | collective-permute-start | bytes 1572872 | tf_op jit(solution)/shard_map/ppermute | solution.py:211
  303.5 22.8 %collective-permute-start.72 = (bf16[256,1024]{1,0:T(8,128)(2,1)S(1)}, bf16[256,1024]{1,0:T(8,128)(2,1)S(1)}, u32[]{:S(2)}, u32[]{:S(2)}) collective-permute-start(bf16[256,1024]{1,0:T(8,128)(2,1)S(1)} %pad_maximum_fusion.3.refs_6_), channel_id=1, source_target_pairs={{0,1},{1,0},{2,3},{3,2},{4,5},{5,4},{6,7},{7,6},{8,9},{9,8},{10,11... | collective-permute-start | bytes 1572872 | tf_op jit(solution)/shard_map/ppermute | solution.py:211
  303.5 34.4 %collective-permute-start.52 = (bf16[384,1024]{1,0:T(8,128)(2,1)S(1)}, bf16[384,1024]{1,0:T(8,128)(2,1)}, u32[]{:S(2)}, u32[]{:S(2)}) collective-permute-start(bf16[384,1024]{1,0:T(8,128)(2,1)S(1)} %pad_maximum_fusion.refs_4_), channel_id=1, source_target_pairs={{0,4},{4,0},{8,12},{12,8},{16,20},{20,16},{24,28},{28,24},{1,5},{5... | collective-permute-start | bytes 2359304 | tf_op jit(solution)/shard_map/ppermute | solution.py:341
  312.5 30.2 %collective-permute-start.65 = (bf16[256,1024]{1,0:T(8,128)(2,1)}, bf16[256,1024]{1,0:T(8,128)(2,1)}, u32[]{:S(2)}, u32[]{:S(2)}) collective-permute-start(bf16[256,1024]{1,0:T(8,128)(2,1)} %collective-permute-done.63.refs_6_), channel_id=1, source_target_pairs={{0,2},{1,3},{2,0},{3,1},{4,6},{5,7},{6,4},{7,5},{8,10},{9,11},{10,... | collective-permute-start | bytes 1572872 | tf_op jit(solution)/shard_map/ppermute | solution.py:211
  323.7 19.0 %collective-permute-start.67 = (bf16[256,1024]{1,0:T(8,128)(2,1)}, bf16[256,1024]{1,0:T(8,128)(2,1)}, u32[]{:S(2)}, u32[]{:S(2)}) collective-permute-start(bf16[256,1024]{1,0:T(8,128)(2,1)} %pad_maximum_fusion.2.refs_5_), channel_id=1, source_target_pairs={{0,3},{1,2},{2,1},{3,0},{4,7},{5,6},{6,5},{7,4},{8,11},{9,10},{10,... | collective-permute-start | bytes 1572872 | tf_op jit(solution)/shard_map/ppermute | solution.py:211
  324.5 24.3 %collective-permute-start.68 = (bf16[256,1024]{1,0:T(8,128)(2,1)}, bf16[256,1024]{1,0:T(8,128)(2,1)}, u32[]{:S(2)}, u32[]{:S(2)}) collective-permute-start(bf16[256,1024]{1,0:T(8,128)(2,1)} %collective-permute-done.66.refs_6_), channel_id=1, source_target_pairs={{0,3},{1,2},{2,1},{3,0},{4,7},{5,6},{6,5},{7,4},{8,11},{9,10},{10,... | collective-permute-start | bytes 1572872 | tf_op jit(solution)/shard_map/ppermute | solution.py:211
  327.1 21.8 %collective-permute-start.73 = (bf16[256,1024]{1,0:T(8,128)(2,1)}, bf16[256,1024]{1,0:T(8,128)(2,1)}, u32[]{:S(2)}, u32[]{:S(2)}) collective-permute-start(bf16[256,1024]{1,0:T(8,128)(2,1)} %collective-permute-done.71.refs_7_), channel_id=1, source_target_pairs={{0,1},{1,0},{2,3},{3,2},{4,5},{5,4},{6,7},{7,6},{8,9},{9,8},{10,11... | collective-permute-start | bytes 1572872 | tf_op jit(solution)/shard_map/ppermute | solution.py:211
  (48 other events, 488.9 us)

commit v4 on v3

--- a/solution.py
+++ b/solution.py
@@ -78,15 +78,22 @@
     return call(kernel, f"product_{stage}", outs, (place,), args)
 
 
+def number_of(line, position, lines):
+    number, bit, weight = 0, 1, lines // 2
+    while bit < lines:
+        number = number + lax.rem(line // bit + (position // weight) % 2, 2) * weight
+        bit, weight = bit * 2, weight // 2
+    return number
+
+
 def put_in_place(where_ref, lines, mine_ref, far_ref, out_ref, base):
     odd, line = where_ref[0], where_ref[1]
     half = mine_ref.shape[0]
     height = half // lines
     for side, ref in ((odd, mine_ref), (1 - odd, far_ref)):
         for j in range(lines):
-            number = lax.rem(line - j + lines, lines)
-            first_row = pl.multiple_of(base + side * half + number * height, height)
-            out_ref[pl.ds(first_row, height), :] = ref[j * height : (j + 1) * height, :]
+            first_row = base + side * half + number_of(line, j, lines) * height
+            out_ref[pl.ds(pl.multiple_of(first_row, height), height), :] = ref[j * height : (j + 1) * height, :]
 
 
 TRANSPOSED_LEFT = (((0,), (0,)), ((), ()))
@@ -204,7 +211,6 @@
     line = my_tile // 2
 
     swap = [(i, i ^ 1) for i in range(tiles)]
-    around = [(2 * i + side, 2 * ((i + 1) % lines) + side) for i in range(lines) for side in (0, 1)]
     outward = [(2 * i + side, 2 * ((i + 1 - 2 * side) % lines) + side) for i in range(lines) for side in (0, 1)]
 
     def to_group(value, d):
@@ -220,17 +226,18 @@
     blocks = jnp.concatenate(by_slot, axis=2)
 
     width = columns // CHUNKS
-    fields = [lax.slice_in_dim(orbitals, c * width, (c + 1) * width, axis=1) for c in range(CHUNKS)]
-    start = fields
-    near = [lax.ppermute(field, "elem", swap) for field in fields]
-    order = Order(jnp.zeros((8, 128), F32) + place[0, 0].astype(F32))
+    start = [lax.slice_in_dim(orbitals, c * width, (c + 1) * width, axis=1) for c in range(CHUNKS)]
+    near = {(0, 0): lax.ppermute(start[0], "elem", swap)}
+    order = Order(jnp.zeros((8, 128), F32))
     blocks, place = order(blocks, place)
+    start = [start[0]] + [order(field) for field in start[1:]]
+    for c in range(1, CHUNKS):
+        near[(0, c)] = lax.ppermute(start[c], "elem", swap)
 
     jobs = [(stage, c) for stage in range(3) for c in range(CHUNKS)]
     far = {}
     firsts, squares, pieces = {}, [], [{} for _ in range(CHUNKS)]
-    near = {(0, c): near[c] for c in range(CHUNKS)}
-    current = {(0, c): fields[c] for c in range(CHUNKS)}
+    current = {(0, c): start[c] for c in range(CHUNKS)}
 
     def send_on(job):
         near[job] = order(near[job])
@@ -274,10 +281,6 @@
     multiply(jobs[-1])
 
     squares = sum(squares)
-    if width % 128:
-        squares = jnp.pad(squares, ((0, 0), (0, -width % 128)))
-    squares = sum(squares[:, i : i + 128] for i in range(0, squares.shape[1], 128))
-    gathered = lax.all_gather(squares, ("elem", "orb"))
     rows_total = rows * tiles
     level = None
     middle = columns // 2
@@ -305,73 +308,97 @@
         return call(functools.partial(gram_kernel, d > 0), name, (half, half), (where(d),), fields, scratch)
 
     exchanged = {}
+    line_bits = [1 << i for i in range(lines.bit_length() - 1)]
+
+    def over_z(value, bit):
+        return lax.ppermute(value, "elem", [(i, i ^ (2 * bit)) for i in range(tiles)])
+
+    def level_process():
+        nonlocal level
+        total = jnp.full((8, 128), jnp.sum(squares), F32)
+        for axis, peers in (("orb", groups), ("elem", tiles)):
+            bit = 1
+            while bit < peers:
+                other = lax.ppermute(total, axis, [(i, i ^ bit) for i in range(peers)])
+                yield
+                total = total + order(other)
+                bit *= 2
+        level = total[0, 0] / (columns * groups * rows_total)
+        yield
 
     def process(d):
-        nonlocal level
         mine, other = order(*gram_chunk(d))
-        other = lax.ppermute(other, "elem", swap)
-        yield
-        other = order(other)
-        height = mine.shape[0] // lines
-
-        def pair(index):
-            return sum(lax.dynamic_slice_in_dim(v, index * height, height, 0).astype(F32) for v in (mine, other))
-
-        running = None
-        for hop in range(1, lines):
-            part = pair((line - hop) % lines)
-            if running is not None:
-                part = part + running.astype(F32)
-            running = lax.ppermute(part.astype(BF16), "elem", around)
+        yield
+        other = lax.ppermute(order(other), "elem", swap)
+        yield
+        terms = [(mine, 0), (order(other), 0)]
+        height = mine.shape[0]
+        offset = 0
+
+        def added(first_row, count):
+            return sum(lax.dynamic_slice_in_dim(v, first_row - row, count, 0).astype(F32) for v, row in terms)
+
+        for bit in line_bits:
+            height //= 2
+            keep = (line // bit) % 2
+            received = over_z(added(offset + (1 - keep) * height, height).astype(BF16), bit)
+            offset = offset + keep * height
             yield
-            running = order(running)
-        part = pair(line)
-        if running is not None:
-            part = part + running.astype(F32)
-        if level is None:
-            level = jnp.sum(order(gathered)) / (columns * groups * rows_total)
-        part = (part / (level * rows_total)).astype(BF16)
-        parts = [part]
-        for hop in range(1, lines):
-            part = lax.ppermute(part, "elem", around)
+            terms.append((order(received), offset))
+        part = (added(offset, height) / (level * rows_total)).astype(BF16)
+        for bit in line_bits[::-1]:
+            received = over_z(part, bit)
             yield
-            part = order(part)
-            parts.append(part)
-        whole = jnp.concatenate(parts, axis=0)
-        far_whole = lax.ppermute(whole, "elem", swap)
+            part = jnp.concatenate([part, order(received)], axis=0)
+        whole = order(part)
         if d:
             peer_whole = to_group(whole, d)
         yield
+        far_whole = lax.ppermute(order(whole), "elem", swap)
+        yield
+        if d:
+            peer_whole = order(peer_whole)
+            yield
         far_whole = order(far_whole)
         if d == 0:
             exchanged[0] = (whole, far_whole)
+            yield
             return
         peer_far = to_group(far_whole, d)
         yield
-        peer_whole = order(peer_whole)
         peer_far = order(peer_far)
         exchanged[d] = (whole, far_whole, peer_whole, peer_far)
+        yield
 
     queue = sorted(range(1, groups), key=lambda d: (d == 1, d))
-    events = []
+    events = [(3.5 * (i + 1), -1, -1) for i in range(groups.bit_length() + tiles.bit_length() - 1)]
+    free = 66.0
     for position, d in enumerate([0] + queue):
-        ready = 0.0 if position == 0 else 10.0 + 0.1 * position
-        times = [ready]
-        reduced = 19.0 + 10.5 * position
-        times += [reduced + 6.0 * hop for hop in range(2 * lines - 1)]
-        times.append(max(times[-1] + 10.0, 77.0 + 10.5 * position))
+        summed = 20.0 + 12.0 * position
+        hop = 9.0 if d else 11.5
+        times = [0.0 if d == 0 else 10.5 if position == 1 else 20.5 + 0.2 * position]
+        times.append(0.0 if d == 0 else summed - 11.9)
+        times += [summed + hop * i for i in range(2 * len(line_bits) + 1)]
+        sent = max(free + 0.1, times[-1])
+        free = sent + (11.0 if d else 16.5)
+        times.append(sent)
         if d:
-            times.append(times[-1] + 11.0 if d > 1 else times[-1] + 3.0)
+            times.append(max(sent, times[-2] + (11.0 if d > 1 else 3.0)))
+            times.append(max(times[-1], free))
+            times.append(times[-1] + (11.0 if d > 1 else 3.0))
+        else:
+            times.append(free)
         events += [(time, position, d) for time in times]
-    events.sort()
+    events.sort(key=lambda event: event[:2])
     running = {d: process(d) for d in [0] + queue}
+    running[-1] = level_process()
     left_over = {d: sum(1 for event in events if event[2] == d) for d in running}
     done = []
     mixed = None
     for _, _, d in events:
         next(running[d], None)
         left_over[d] -= 1
-        if left_over[d]:
+        if left_over[d] or d < 0:
             continue
         done.append(d)
         parts = exchanged[d]

time: 362 us -> 327 us (0.903)
  starting transfers between devices: 64.4 us -> 112 us
  waiting for transfers between devices: 176 us -> 130 us
  blocking collectives: 42.3 us -> 0 us
    all_gather x1 -> x0, blocking collectives: 42.3 us -> none  [local(): gathered = lax.all_gather(squares, ('elem', 'orb'))]
    ppermute x12, waiting for transfers between devices: 45.7 us -> 9.37 us  [send_on(): far[job] = lax.ppermute(near[job], 'elem', outward)]
    ppermute x36 -> x33, starting transfers between devices: 19.3 us -> 46 us  [the longest x16 22.2 us: over_z(): return lax.ppermute(value, 'elem', [(i, i ^ 2 * bit) for i in range(tiles)])]
    ppermute x12, starting transfers between devices: 3.32 us -> 25 us  [send_on(): far[job] = lax.ppermute(near[job], 'elem', outward)]
    ppermute x36 -> x33, waiting for transfers between devices: 124 us -> 104 us  [the longest x16 48.3 us: over_z(): return lax.ppermute(value, 'elem', [(i, i ^ 2 * bit) for i in range(tiles)])]
    ppermute x8, waiting for transfers between devices: 2.01 us -> 10.1 us  [multiply(): near[stage + 1, c] = lax.ppermute(out, 'elem', swap)]
    ppermute x8, starting transfers between devices: 32.5 us -> 27.7 us  [multiply(): near[stage + 1, c] = lax.ppermute(out, 'elem', swap)]
    ppermute x18, starting transfers between devices: 9.32 us -> 13 us  [to_group(): return lax.ppermute(value, 'orb', [(i, i ^ d) for i in range(groups)])]
  transfers between devices with their start and end apart: 74 -> 71, of which waited for: 45 -> 34; matrix products, arithmetic and copies ran while one was open for 6% -> 7% of each run, Pallas kernels for 10% -> 12%
where the time goes in v4:
time: 327 us; the launch traced here: 326 us
  waiting for transfers between devices  130 us (40%)
  starting transfers between devices  112 us (34%)
  Pallas kernels  48.5 us (15%)
  other arithmetic  17.2 us (5%)
  local copies, waits for them, and re-layouts  15.9 us (5%)
    pallas_call x20, Pallas kernels, call(): pl.pallas_call(kernel, out_shape=outs, in_specs=[pl.BlockSpec(memory_spac...  48.5 us
    ppermute x16, waiting for transfers between devices, over_z(): return lax.ppermute(value, 'elem', [(i, i ^ 2 * bit) for i in range(tiles)])  48.3 us
    ppermute x4, waiting for transfers between devices, process(): far_whole = lax.ppermute(order(whole), 'elem', swap)  31.3 us
    ppermute x8, starting transfers between devices, multiply(): near[stage + 1, c] = lax.ppermute(out, 'elem', swap)  27.7 us
    ppermute x12, starting transfers between devices, send_on(): far[job] = lax.ppermute(near[job], 'elem', outward)  25 us
    ppermute x16, starting transfers between devices, over_z(): return lax.ppermute(value, 'elem', [(i, i ^ 2 * bit) for i in range(tiles)])  22.2 us
    ppermute x18, starting transfers between devices, to_group(): return lax.ppermute(value, 'orb', [(i, i ^ d) for i in range(groups)])  13 us
    ppermute x5, waiting for transfers between devices, level_process(): other = lax.ppermute(total, axis, [(i, i ^ bit) for i in range(peers)])  12.3 us
  transfers between devices with their start and end apart: 71, of which 34 were waited for; matrix products, arithmetic and copies ran while one was open for 7% of the time, Pallas kernels for 12%

profile of v4, /device:TPU:0, one launch (start us, length us, event | category | flops | bytes accessed | tf_op | source)
XLA Modules:
  0.0 325.6 jit_solution(1122018895821086779)
XLA Ops:
  1.5 3.0 collective-permute-start
  4.5 2.2 slice_bitcast_fusion
  8.1 2.3 concatenate.34.blocks_ref
  10.5 3.9 %collective-permute-done.near_ref = bf16[768,256]{1,0:T(8,128)(2,1)S(1)} collective-permute-done((bf16[768,256]{1,0:T(8,128)(2,1)S(1)}, bf16[768,256]{1,0:T(8,128)(2,1)S(1)}, u32[]{:S(2)}, u32[]{:S(2)}) %collective-permute-start) | collective-permute-done | bytes 393248 | tf_op jit(solution)/shard_map/ppermute | solution.py:230
  14.5 2.1 collective-permute-start.1
  16.6 3.5 %collective-permute-start.4 = (bf16[768,256]{1,0:T(8,128)(2,1)S(1)}, bf16[768,256]{1,0:T(8,128)(2,1)S(1)}, u32[]{:S(2)}, u32[]{:S(2)}) collective-permute-start(bf16[768,256]{1,0:T(8,128)(2,1)S(1)} %get-tuple-element.238.field_ref.refs_0_), channel_id=1, source_target_pairs={{0,4},{4,0},{8,12},{12,8},{16,20},{20,16},{24,28},{28,24},{1,5},{5... | collective-permute-start | bytes 1179656 | tf_op jit(solution)/shard_map/ppermute | solution.py:235
  20.2 2.7 collective-permute-done.2.near_ref
  22.9 2.1 collective-permute-start.7
  27.0 4.3 %collective-permute-done.4.near_ref = bf16[768,256]{1,0:T(8,128)(2,1)S(1)} collective-permute-done((bf16[768,256]{1,0:T(8,128)(2,1)S(1)}, bf16[768,256]{1,0:T(8,128)(2,1)S(1)}, u32[]{:S(2)}, u32[]{:S(2)}) %collective-permute-start.4) | collective-permute-done | bytes 393248 | tf_op jit(solution)/shard_map/ppermute | solution.py:235
  31.3 2.1 collective-permute-start.5
  33.4 3.5 %collective-permute-start.3 = (bf16[768,256]{1,0:T(8,128)(2,1)S(1)}, bf16[768,256]{1,0:T(8,128)(2,1)S(1)}, u32[]{:S(2)}, u32[]{:S(2)}) collective-permute-start(bf16[768,256]{1,0:T(8,128)(2,1)S(1)} %get-tuple-element.237.field_ref), channel_id=1, source_target_pairs={{0,4},{4,0},{8,12},{12,8},{16,20},{20,16},{24,28},{28,24},{1,5},{5... | collective-permute-start | bytes 1179656 | tf_op jit(solution)/shard_map/ppermute | solution.py:275
  39.7 2.1 collective-permute-start.10
  41.9 3.5 %collective-permute-start.9 = (bf16[768,256]{1,0:T(8,128)(2,1)S(1)}, bf16[768,256]{1,0:T(8,128)(2,1)S(1)}, u32[]{:S(2)}, u32[]{:S(2)}) collective-permute-start(bf16[768,256]{1,0:T(8,128)(2,1)S(1)} %get-tuple-element.256.field_ref), channel_id=1, source_target_pairs={{0,4},{4,0},{8,12},{12,8},{16,20},{20,16},{24,28},{28,24},{1,5},{5... | collective-permute-start | bytes 1179656 | tf_op jit(solution)/shard_map/ppermute | solution.py:275
  48.2 2.1 collective-permute-start.8
  50.3 3.5 %collective-permute-start.12 = (bf16[768,256]{1,0:T(8,128)(2,1)S(1)}, bf16[768,256]{1,0:T(8,128)(2,1)S(1)}, u32[]{:S(2)}, u32[]{:S(2)}) collective-permute-start(bf16[768,256]{1,0:T(8,128)(2,1)S(1)} %get-tuple-element.268.field_ref), channel_id=1, source_target_pairs={{0,4},{4,0},{8,12},{12,8},{16,20},{20,16},{24,28},{28,24},{1,5},{5... | collective-permute-start | bytes 1179656 | tf_op jit(solution)/shard_map/ppermute | solution.py:275
  56.6 2.1 collective-permute-start.15
  58.7 3.5 %collective-permute-start.14 = (bf16[768,256]{1,0:T(8,128)(2,1)S(1)}, bf16[768,256]{1,0:T(8,128)(2,1)S(1)}, u32[]{:S(2)}, u32[]{:S(2)}) collective-permute-start(bf16[768,256]{1,0:T(8,128)(2,1)S(1)} %get-tuple-element.271.field_ref), channel_id=1, source_target_pairs={{0,4},{4,0},{8,12},{12,8},{16,20},{20,16},{24,28},{28,24},{1,5},{5... | collective-permute-start | bytes 1179656 | tf_op jit(solution)/shard_map/ppermute | solution.py:275
  65.0 2.1 collective-permute-start.13
  67.1 3.5 %collective-permute-start.11 = (bf16[768,256]{1,0:T(8,128)(2,1)S(1)}, bf16[768,256]{1,0:T(8,128)(2,1)S(1)}, u32[]{:S(2)}, u32[]{:S(2)}) collective-permute-start(bf16[768,256]{1,0:T(8,128)(2,1)S(1)} %product_1.4.field_ref), channel_id=1, source_target_pairs={{0,4},{4,0},{8,12},{12,8},{16,20},{20,16},{24,28},{28,24},{1,5},{5... | collective-permute-start | bytes 1179656 | tf_op jit(solution)/shard_map/ppermute | solution.py:275
  73.4 2.1 collective-permute-start.18
  75.6 3.5 %collective-permute-start.17 = (bf16[768,256]{1,0:T(8,128)(2,1)S(1)}, bf16[768,256]{1,0:T(8,128)(2,1)S(1)}, u32[]{:S(2)}, u32[]{:S(2)}) collective-permute-start(bf16[768,256]{1,0:T(8,128)(2,1)S(1)} %product_1.5.field_ref), channel_id=1, source_target_pairs={{0,4},{4,0},{8,12},{12,8},{16,20},{20,16},{24,28},{28,24},{1,5},{5... | collective-permute-start | bytes 1179656 | tf_op jit(solution)/shard_map/ppermute | solution.py:275
  81.9 2.1 collective-permute-start.16
  84.0 3.5 %collective-permute-start.20 = (bf16[768,256]{1,0:T(8,128)(2,1)S(1)}, bf16[768,256]{1,0:T(8,128)(2,1)S(1)}, u32[]{:S(2)}, u32[]{:S(2)}) collective-permute-start(bf16[768,256]{1,0:T(8,128)(2,1)S(1)} %product_1.6.field_ref), channel_id=1, source_target_pairs={{0,4},{4,0},{8,12},{12,8},{16,20},{20,16},{24,28},{28,24},{1,5},{5... | collective-permute-start | bytes 1179656 | tf_op jit(solution)/shard_map/ppermute | solution.py:275
  90.3 2.1 collective-permute-start.19
  95.9 2.9 collective-permute-start.22
  98.8 2.0 collective-permute-start.21
  104.4 2.0 collective-permute-done.22.near_ref
  113.4 5.4 %collective-permute-done.24.far_ref = bf16[768,256]{1,0:T(8,128)(2,1)} collective-permute-done((bf16[768,256]{1,0:T(8,128)(2,1)}, bf16[768,256]{1,0:T(8,128)(2,1)}, u32[]{:S(2)}, u32[]{:S(2)}) %collective-permute-start.24) | collective-permute-done | bytes 393248 | tf_op jit(solution)/shard_map/ppermute | solution.py:244
  122.7 2.9 gram_own.1
  131.9 8.1 %collective-permute-done.28 = f32[8,128]{1,0:T(8,128)S(1)} collective-permute-done((f32[8,128]{1,0:T(8,128)S(1)}, f32[8,128]{1,0:T(8,128)S(1)}, u32[]{:S(2)}, u32[]{:S(2)}) %collective-permute-start.28) | collective-permute-done | bytes 4128 | tf_op jit(solution)/shard_map/ppermute | solution.py:322
  142.2 2.6 gram_pair.3
  146.2 3.0 collective-permute-done.31
  151.0 2.8 collective-permute-start.32
  155.5 2.0 add_convert_fusion
  157.5 1.9 collective-permute-start.38
  160.5 3.1 gram_pair.4
  164.4 3.1 gram_pair.5
  173.8 2.9 collective-permute-start.43
  176.8 7.2 %collective-permute-done.45 = bf16[128,1024]{1,0:T(8,128)(2,1)} collective-permute-done((bf16[128,1024]{1,0:T(8,128)(2,1)S(1)}, bf16[128,1024]{1,0:T(8,128)(2,1)}, u32[]{:S(2)}, u32[]{:S(2)}) %collective-permute-start.45) | collective-permute-done | bytes 262176 | tf_op jit(solution)/shard_map/ppermute | solution.py:314
  187.1 2.7 collective-permute-start.49
  191.5 9.8 %collective-permute-done.49 = bf16[64,1024]{1,0:T(8,128)(2,1)S(1)} collective-permute-done((bf16[64,1024]{1,0:T(8,128)(2,1)S(1)}, bf16[64,1024]{1,0:T(8,128)(2,1)S(1)}, u32[]{:S(2)}, u32[]{:S(2)}) %collective-permute-start.49) | collective-permute-done | bytes 131104 | tf_op jit(solution)/shard_map/ppermute | solution.py:314
  203.5 2.1 collective-permute-start.52
  206.7 7.7 %collective-permute-done.48 = bf16[128,1024]{1,0:T(8,128)(2,1)S(1)} collective-permute-done((bf16[128,1024]{1,0:T(8,128)(2,1)S(1)}, bf16[128,1024]{1,0:T(8,128)(2,1)S(1)}, u32[]{:S(2)}, u32[]{:S(2)}) %collective-permute-start.48) | collective-permute-done | bytes 262176 | tf_op jit(solution)/shard_map/ppermute | solution.py:314
  215.5 1.8 collective-permute-start.50
  217.4 5.7 %collective-permute-done.53 = bf16[64,1024]{1,0:T(8,128)(2,1)S(1)} collective-permute-done((bf16[64,1024]{1,0:T(8,128)(2,1)S(1)}, bf16[64,1024]{1,0:T(8,128)(2,1)S(1)}, u32[]{:S(2)}, u32[]{:S(2)}) %collective-permute-start.53) | collective-permute-done | bytes 131104 | tf_op jit(solution)/shard_map/ppermute | solution.py:314
  225.1 3.0 collective-permute-start.56
  228.1 7.7 %collective-permute-done.59 = bf16[64,1024]{1,0:T(8,128)(2,1)S(1)} collective-permute-done((bf16[64,1024]{1,0:T(8,128)(2,1)S(1)}, bf16[64,1024]{1,0:T(8,128)(2,1)S(1)}, u32[]{:S(2)}, u32[]{:S(2)}) %collective-permute-start.59) | collective-permute-done | bytes 131104 | tf_op jit(solution)/shard_map/ppermute | solution.py:314
  236.9 4.3 %collective-permute-start.57 = (bf16[128,1024]{1,0:T(8,128)(2,1)S(1)}, bf16[128,1024]{1,0:T(8,128)(2,1)S(1)}, u32[]{:S(2)}, u32[]{:S(2)}) collective-permute-start(bf16[128,1024]{1,0:T(8,128)(2,1)S(1)} %pad_maximum_fusion.5), channel_id=1, source_target_pairs={{0,8},{4,12},{8,0},{12,4},{16,24},{20,28},{24,16},{28,20},{1,9},{5... | collective-permute-start | bytes 786440 | tf_op jit(solution)/shard_map/ppermute | solution.py:314
  241.3 2.2 collective-permute-done.66
  243.5 2.0 collective-permute-start.67
  248.8 2.2 collective-permute-start.60
  251.0 3.4 %collective-permute-done.58 = bf16[128,1024]{1,0:T(8,128)(2,1)S(1)} collective-permute-done((bf16[128,1024]{1,0:T(8,128)(2,1)S(1)}, bf16[128,1024]{1,0:T(8,128)(2,1)S(1)}, u32[]{:S(2)}, u32[]{:S(2)}) %collective-permute-start.58) | collective-permute-done | bytes 262176 | tf_op jit(solution)/shard_map/ppermute | solution.py:314
  254.4 2.2 collective-permute-start.63
  256.6 2.0 collective-permute-done.67
  258.7 2.2 collective-permute-start.68
  262.6 14.8 %collective-permute-done.60.refs_6_ = bf16[256,1024]{1,0:T(8,128)(2,1)S(1)} collective-permute-done((bf16[256,1024]{1,0:T(8,128)(2,1)S(1)}, bf16[256,1024]{1,0:T(8,128)(2,1)S(1)}, u32[]{:S(2)}, u32[]{:S(2)}) %collective-permute-start.60) | collective-permute-done | bytes 524320 | tf_op jit(solution)/shard_map/ppermute | solution.py:357
  277.4 11.2 %collective-permute-done.63.refs_6_ = bf16[256,1024]{1,0:T(8,128)(2,1)S(1)} collective-permute-done((bf16[256,1024]{1,0:T(8,128)(2,1)S(1)}, bf16[256,1024]{1,0:T(8,128)(2,1)S(1)}, u32[]{:S(2)}, u32[]{:S(2)}) %collective-permute-start.63) | collective-permute-done | bytes 524320 | tf_op jit(solution)/shard_map/ppermute | solution.py:357
  290.2 5.2 %collective-permute-done.68.refs_7_ = bf16[256,1024]{1,0:T(8,128)(2,1)S(1)} collective-permute-done((bf16[256,1024]{1,0:T(8,128)(2,1)S(1)}, bf16[256,1024]{1,0:T(8,128)(2,1)S(1)}, u32[]{:S(2)}, u32[]{:S(2)}) %collective-permute-start.68) | collective-permute-done | bytes 524320 | tf_op jit(solution)/shard_map/ppermute | solution.py:357
  297.3 4.1 %mix_own.1.refs_0_ = f32[768,1024]{1,0:T(8,128)} custom-call(s32[3]{0:T(128)S(1)} %copy-done.18, bf16[768,256]{1,0:T(8,128)(2,1)S(1)} %get-tuple-element.307.refs_0_.refs_10_, bf16[768,256]{1,0:T(8,128)(2,1)S(1)} %get-tuple-element.318.refs_1_.refs_11_, bf16[768,256]{1,0:T(8,128)(2,1)S(1)} %get-tuple-element.327.refs_2_.refs_12_, ...), custom_call_target="tpu_custom_call" | custom-call | flops 1024 | bytes 1024 | tf_op jit(solution)/shard_map/mix_own/pallas_call | solution.py:57
  301.4 2.1 collective-permute-done.62.refs_8_
  303.5 5.5 %mix_pair.2.refs_0_ = f32[768,1024]{1,0:T(8,128)} custom-call(s32[3]{0:T(128)S(1)} %pad_add_fusion.4.where_ref, f32[768,1024]{1,0:T(8,128)} %mix_own.1.refs_0_, bf16[768,256]{1,0:T(8,128)(2,1)S(1)} %collective-permute-done.23.refs_4_.refs_1_, bf16[768,256]{1,0:T(8,128)(2,1)S(1)} %collective-permute-done.25.refs_5_.refs_2_, ...), custom_call_target="tpu_custom_call", output_to_operand_aliasing={{}: (1, {})} | custom-call | flops 1024 | bytes 1024 | tf_op jit(solution)/shard_map/mix_pair/pallas_call | solution.py:57
  309.0 4.5 %collective-permute-done.65.refs_8_ = bf16[256,1024]{1,0:T(8,128)(2,1)S(1)} collective-permute-done((bf16[256,1024]{1,0:T(8,128)(2,1)S(1)}, bf16[256,1024]{1,0:T(8,128)(2,1)S(1)}, u32[]{:S(2)}, u32[]{:S(2)}) %collective-permute-start.65) | collective-permute-done | bytes 524320 | tf_op jit(solution)/shard_map/ppermute | solution.py:217
  314.1 6.0 %mix_pair.3.refs_1_ = f32[768,1024]{1,0:T(8,128)} custom-call(s32[3]{0:T(128)S(1)} %pad_add_fusion.4.where_ref, f32[768,1024]{1,0:T(8,128)} %mix_pair.2.refs_0_, bf16[768,256]{1,0:T(8,128)(2,1)S(1)} %copy-done.2, bf16[768,256]{1,0:T(8,128)(2,1)} %collective-permute-done.34.refs_5_.refs_2_, ...), custom_call_target="tpu_custom_call", output_to_operand_aliasing={{}: (1, {})} | custom-call | flops 1024 | bytes 1024 | tf_op jit(solution)/shard_map/mix_pair/pallas_call | solution.py:57
  320.2 5.5 %mix_last.1 = bf16[768,1024]{1,0:T(8,128)(2,1)} custom-call(s32[3]{0:T(128)S(1)} %pad_add_fusion.1.where_ref, f32[1]{0:T(128)} %bitcast.11.refs_0_, f32[768,1024]{1,0:T(8,128)} %mix_pair.3.refs_1_, bf16[768,256]{1,0:T(8,128)(2,1)S(1)} %collective-permute-done.39.refs_4_.refs_2_, bf16[768,256]{1,0:T(8,128)(2,1)} %collective-permute-done.40.refs_5_.refs_3_, ...), custom_call_target="tpu_custom_call" | custom-call | flops 1024 | bytes 1024 | tf_op jit(solution)/shard_map/mix_last/pallas_call | solution.py:57
  (180 shorter events, 83.8 us)
Async XLA Ops:
  1.5 13.0 %collective-permute-start = (bf16[768,256]{1,0:T(8,128)(2,1)S(1)}, bf16[768,256]{1,0:T(8,128)(2,1)S(1)}, u32[]{:S(2)}, u32[]{:S(2)}) collective-permute-start(bf16[768,256]{1,0:T(8,128)(2,1)S(1)} %get-tuple-element.442.field_ref.refs_0_), channel_id=1, source_target_pairs={{0,4},{4,0},{8,12},{12,8},{16,20},{20,16},{24,28},{28,24},{1,5},{5... | collective-permute-start | bytes 1179656 | tf_op jit(solution)/shard_map/ppermute | solution.py:230
  10.5 12.4 %collective-permute-start.2 = (bf16[768,256]{1,0:T(8,128)(2,1)S(1)}, bf16[768,256]{1,0:T(8,128)(2,1)S(1)}, u32[]{:S(2)}, u32[]{:S(2)}) collective-permute-start(bf16[768,256]{1,0:T(8,128)(2,1)S(1)} %get-tuple-element.230.field_ref.refs_0_), channel_id=1, source_target_pairs={{0,4},{4,0},{8,12},{12,8},{16,20},{20,16},{24,28},{28,24},{1,5},{5... | collective-permute-start | bytes 1179656 | tf_op jit(solution)/shard_map/ppermute | solution.py:235
  14.5 11.3 %collective-permute-start.1 = (bf16[768,256]{1,0:T(8,128)(2,1)S(1)}, bf16[768,256]{1,0:T(8,128)(2,1)S(1)}, u32[]{:S(2)}, u32[]{:S(2)}) collective-permute-start(bf16[768,256]{1,0:T(8,128)(2,1)S(1)} %collective-permute-done.near_ref), channel_id=1, source_target_pairs={{0,8},{4,28},{8,16},{12,4},{16,24},{20,12},{24,0},{28,20},{1,9},{5... | collective-permute-start | bytes 1179656 | tf_op jit(solution)/shard_map/ppermute | solution.py:244
  16.6 14.7 %collective-permute-start.4 = (bf16[768,256]{1,0:T(8,128)(2,1)S(1)}, bf16[768,256]{1,0:T(8,128)(2,1)S(1)}, u32[]{:S(2)}, u32[]{:S(2)}) collective-permute-start(bf16[768,256]{1,0:T(8,128)(2,1)S(1)} %get-tuple-element.238.field_ref.refs_0_), channel_id=1, source_target_pairs={{0,4},{4,0},{8,12},{12,8},{16,20},{20,16},{24,28},{28,24},{1,5},{5... | collective-permute-start | bytes 1179656 | tf_op jit(solution)/shard_map/ppermute | solution.py:235
  20.1 19.6 %collective-permute-start.6 = (bf16[768,256]{1,0:T(8,128)(2,1)S(1)}, bf16[768,256]{1,0:T(8,128)(2,1)S(1)}, u32[]{:S(2)}, u32[]{:S(2)}) collective-permute-start(bf16[768,256]{1,0:T(8,128)(2,1)S(1)} %get-tuple-element.241.field_ref.refs_0_), channel_id=1, source_target_pairs={{0,4},{4,0},{8,12},{12,8},{16,20},{20,16},{24,28},{28,24},{1,5},{5... | collective-permute-start | bytes 1179656 | tf_op jit(solution)/shard_map/ppermute | solution.py:235
  22.9 14.1 %collective-permute-start.7 = (bf16[768,256]{1,0:T(8,128)(2,1)S(1)}, bf16[768,256]{1,0:T(8,128)(2,1)S(1)}, u32[]{:S(2)}, u32[]{:S(2)}) collective-permute-start(bf16[768,256]{1,0:T(8,128)(2,1)S(1)} %collective-permute-done.2.near_ref), channel_id=1, source_target_pairs={{0,8},{4,28},{8,16},{12,4},{16,24},{20,12},{24,0},{28,20},{1,9},{5... | collective-permute-start | bytes 1179656 | tf_op jit(solution)/shard_map/ppermute | solution.py:244
  31.3 14.1 %collective-permute-start.5 = (bf16[768,256]{1,0:T(8,128)(2,1)S(1)}, bf16[768,256]{1,0:T(8,128)(2,1)S(1)}, u32[]{:S(2)}, u32[]{:S(2)}) collective-permute-start(bf16[768,256]{1,0:T(8,128)(2,1)S(1)} %collective-permute-done.4.near_ref), channel_id=1, source_target_pairs={{0,8},{4,28},{8,16},{12,4},{16,24},{20,12},{24,0},{28,20},{1,9},{5... | collective-permute-start | bytes 1179656 | tf_op jit(solution)/shard_map/ppermute | solution.py:244
  33.4 14.7 %collective-permute-start.3 = (bf16[768,256]{1,0:T(8,128)(2,1)S(1)}, bf16[768,256]{1,0:T(8,128)(2,1)S(1)}, u32[]{:S(2)}, u32[]{:S(2)}) collective-permute-start(bf16[768,256]{1,0:T(8,128)(2,1)S(1)} %get-tuple-element.237.field_ref), channel_id=1, source_target_pairs={{0,4},{4,0},{8,12},{12,8},{16,20},{20,16},{24,28},{28,24},{1,5},{5... | collective-permute-start | bytes 1179656 | tf_op jit(solution)/shard_map/ppermute | solution.py:275
  39.7 14.1 %collective-permute-start.10 = (bf16[768,256]{1,0:T(8,128)(2,1)S(1)}, bf16[768,256]{1,0:T(8,128)(2,1)S(1)}, u32[]{:S(2)}, u32[]{:S(2)}) collective-permute-start(bf16[768,256]{1,0:T(8,128)(2,1)S(1)} %collective-permute-done.6.near_ref), channel_id=1, source_target_pairs={{0,8},{4,28},{8,16},{12,4},{16,24},{20,12},{24,0},{28,20},{1,9},{5... | collective-permute-start | bytes 1179656 | tf_op jit(solution)/shard_map/ppermute | solution.py:244
  41.9 14.7 %collective-permute-start.9 = (bf16[768,256]{1,0:T(8,128)(2,1)S(1)}, bf16[768,256]{1,0:T(8,128)(2,1)S(1)}, u32[]{:S(2)}, u32[]{:S(2)}) collective-permute-start(bf16[768,256]{1,0:T(8,128)(2,1)S(1)} %get-tuple-element.256.field_ref), channel_id=1, source_target_pairs={{0,4},{4,0},{8,12},{12,8},{16,20},{20,16},{24,28},{28,24},{1,5},{5... | collective-permute-start | bytes 1179656 | tf_op jit(solution)/shard_map/ppermute | solution.py:275
  48.2 14.1 %collective-permute-start.8 = (bf16[768,256]{1,0:T(8,128)(2,1)S(1)}, bf16[768,256]{1,0:T(8,128)(2,1)S(1)}, u32[]{:S(2)}, u32[]{:S(2)}) collective-permute-start(bf16[768,256]{1,0:T(8,128)(2,1)S(1)} %collective-permute-done.3.near_ref), channel_id=1, source_target_pairs={{0,8},{4,28},{8,16},{12,4},{16,24},{20,12},{24,0},{28,20},{1,9},{5... | collective-permute-start | bytes 1179656 | tf_op jit(solution)/shard_map/ppermute | solution.py:244
  50.3 14.7 %collective-permute-start.12 = (bf16[768,256]{1,0:T(8,128)(2,1)S(1)}, bf16[768,256]{1,0:T(8,128)(2,1)S(1)}, u32[]{:S(2)}, u32[]{:S(2)}) collective-permute-start(bf16[768,256]{1,0:T(8,128)(2,1)S(1)} %get-tuple-element.268.field_ref), channel_id=1, source_target_pairs={{0,4},{4,0},{8,12},{12,8},{16,20},{20,16},{24,28},{28,24},{1,5},{5... | collective-permute-start | bytes 1179656 | tf_op jit(solution)/shard_map/ppermute | solution.py:275
  56.6 14.1 %collective-permute-start.15 = (bf16[768,256]{1,0:T(8,128)(2,1)S(1)}, bf16[768,256]{1,0:T(8,128)(2,1)S(1)}, u32[]{:S(2)}, u32[]{:S(2)}) collective-permute-start(bf16[768,256]{1,0:T(8,128)(2,1)S(1)} %collective-permute-done.9.near_ref), channel_id=1, source_target_pairs={{0,8},{4,28},{8,16},{12,4},{16,24},{20,12},{24,0},{28,20},{1,9},{5... | collective-permute-start | bytes 1179656 | tf_op jit(solution)/shard_map/ppermute | solution.py:244
  58.7 14.7 %collective-permute-start.14 = (bf16[768,256]{1,0:T(8,128)(2,1)S(1)}, bf16[768,256]{1,0:T(8,128)(2,1)S(1)}, u32[]{:S(2)}, u32[]{:S(2)}) collective-permute-start(bf16[768,256]{1,0:T(8,128)(2,1)S(1)} %get-tuple-element.271.field_ref), channel_id=1, source_target_pairs={{0,4},{4,0},{8,12},{12,8},{16,20},{20,16},{24,28},{28,24},{1,5},{5... | collective-permute-start | bytes 1179656 | tf_op jit(solution)/shard_map/ppermute | solution.py:275
  65.0 14.1 %collective-permute-start.13 = (bf16[768,256]{1,0:T(8,128)(2,1)S(1)}, bf16[768,256]{1,0:T(8,128)(2,1)S(1)}, u32[]{:S(2)}, u32[]{:S(2)}) collective-permute-start(bf16[768,256]{1,0:T(8,128)(2,1)S(1)} %collective-permute-done.12.near_ref), channel_id=1, source_target_pairs={{0,8},{4,28},{8,16},{12,4},{16,24},{20,12},{24,0},{28,20},{1,9},{5... | collective-permute-start | bytes 1179656 | tf_op jit(solution)/shard_map/ppermute | solution.py:244
  67.1 14.7 %collective-permute-start.11 = (bf16[768,256]{1,0:T(8,128)(2,1)S(1)}, bf16[768,256]{1,0:T(8,128)(2,1)S(1)}, u32[]{:S(2)}, u32[]{:S(2)}) collective-permute-start(bf16[768,256]{1,0:T(8,128)(2,1)S(1)} %product_1.4.field_ref), channel_id=1, source_target_pairs={{0,4},{4,0},{8,12},{12,8},{16,20},{20,16},{24,28},{28,24},{1,5},{5... | collective-permute-start | bytes 1179656 | tf_op jit(solution)/shard_map/ppermute | solution.py:275
  73.4 14.1 %collective-permute-start.18 = (bf16[768,256]{1,0:T(8,128)(2,1)S(1)}, bf16[768,256]{1,0:T(8,128)(2,1)S(1)}, u32[]{:S(2)}, u32[]{:S(2)}) collective-permute-start(bf16[768,256]{1,0:T(8,128)(2,1)S(1)} %collective-permute-done.14.near_ref), channel_id=1, source_target_pairs={{0,8},{4,28},{8,16},{12,4},{16,24},{20,12},{24,0},{28,20},{1,9},{5... | collective-permute-start | bytes 1179656 | tf_op jit(solution)/shard_map/ppermute | solution.py:244
  75.6 14.7 %collective-permute-start.17 = (bf16[768,256]{1,0:T(8,128)(2,1)S(1)}, bf16[768,256]{1,0:T(8,128)(2,1)S(1)}, u32[]{:S(2)}, u32[]{:S(2)}) collective-permute-start(bf16[768,256]{1,0:T(8,128)(2,1)S(1)} %product_1.5.field_ref), channel_id=1, source_target_pairs={{0,4},{4,0},{8,12},{12,8},{16,20},{20,16},{24,28},{28,24},{1,5},{5... | collective-permute-start | bytes 1179656 | tf_op jit(solution)/shard_map/ppermute | solution.py:275
  81.9 11.3 %collective-permute-start.16 = (bf16[768,256]{1,0:T(8,128)(2,1)S(1)}, bf16[768,256]{1,0:T(8,128)(2,1)S(1)}, u32[]{:S(2)}, u32[]{:S(2)}) collective-permute-start(bf16[768,256]{1,0:T(8,128)(2,1)S(1)} %collective-permute-done.11.near_ref), channel_id=1, source_target_pairs={{0,8},{4,28},{8,16},{12,4},{16,24},{20,12},{24,0},{28,20},{1,9},{5... | collective-permute-start | bytes 1179656 | tf_op jit(solution)/shard_map/ppermute | solution.py:244
  84.0 14.8 %collective-permute-start.20 = (bf16[768,256]{1,0:T(8,128)(2,1)S(1)}, bf16[768,256]{1,0:T(8,128)(2,1)S(1)}, u32[]{:S(2)}, u32[]{:S(2)}) collective-permute-start(bf16[768,256]{1,0:T(8,128)(2,1)S(1)} %product_1.6.field_ref), channel_id=1, source_target_pairs={{0,4},{4,0},{8,12},{12,8},{16,20},{20,16},{24,28},{28,24},{1,5},{5... | collective-permute-start | bytes 1179656 | tf_op jit(solution)/shard_map/ppermute | solution.py:275
  90.3 11.3 %collective-permute-start.19 = (bf16[768,256]{1,0:T(8,128)(2,1)S(1)}, bf16[768,256]{1,0:T(8,128)(2,1)S(1)}, u32[]{:S(2)}, u32[]{:S(2)}) collective-permute-start(bf16[768,256]{1,0:T(8,128)(2,1)S(1)} %collective-permute-done.17.near_ref), channel_id=1, source_target_pairs={{0,8},{4,28},{8,16},{12,4},{16,24},{20,12},{24,0},{28,20},{1,9},{5... | collective-permute-start | bytes 1179656 | tf_op jit(solution)/shard_map/ppermute | solution.py:244
  94.4 10.0 %collective-permute-start.23 = (bf16[768,256]{1,0:T(8,128)(2,1)S(1)}, bf16[768,256]{1,0:T(8,128)(2,1)S(1)}, u32[]{:S(2)}, u32[]{:S(2)}) collective-permute-start(bf16[768,256]{1,0:T(8,128)(2,1)S(1)} %get-tuple-element.307.refs_0_.refs_10_), channel_id=1, source_target_pairs={{0,2},{1,3},{2,0},{3,1},{4,6},{5,7},{6,4},{7,5},{8,10},{9,11},{10,... | collective-permute-start | bytes 1179656 | tf_op jit(solution)/shard_map/ppermute | solution.py:217
  95.9 10.5 %collective-permute-start.22 = (bf16[768,256]{1,0:T(8,128)(2,1)S(1)}, bf16[768,256]{1,0:T(8,128)(2,1)}, u32[]{:S(2)}, u32[]{:S(2)}) collective-permute-start(bf16[768,256]{1,0:T(8,128)(2,1)S(1)} %product_1.7.field_ref), channel_id=1, source_target_pairs={{0,4},{4,0},{8,12},{12,8},{16,20},{20,16},{24,28},{28,24},{1,5},{5... | collective-permute-start | bytes 1179656 | tf_op jit(solution)/shard_map/ppermute | solution.py:275
  98.8 11.2 %collective-permute-start.21 = (bf16[768,256]{1,0:T(8,128)(2,1)S(1)}, bf16[768,256]{1,0:T(8,128)(2,1)S(1)}, u32[]{:S(2)}, u32[]{:S(2)}) collective-permute-start(bf16[768,256]{1,0:T(8,128)(2,1)S(1)} %collective-permute-done.20.near_ref), channel_id=1, source_target_pairs={{0,8},{4,28},{8,16},{12,4},{16,24},{20,12},{24,0},{28,20},{1,9},{5... | collective-permute-start | bytes 1179656 | tf_op jit(solution)/shard_map/ppermute | solution.py:244
  102.9 10.5 %collective-permute-start.25 = (bf16[768,256]{1,0:T(8,128)(2,1)S(1)}, bf16[768,256]{1,0:T(8,128)(2,1)S(1)}, u32[]{:S(2)}, u32[]{:S(2)}) collective-permute-start(bf16[768,256]{1,0:T(8,128)(2,1)S(1)} %get-tuple-element.318.refs_1_.refs_11_), channel_id=1, source_target_pairs={{0,2},{1,3},{2,0},{3,1},{4,6},{5,7},{6,4},{7,5},{8,10},{9,11},{10,... | collective-permute-start | bytes 1179656 | tf_op jit(solution)/shard_map/ppermute | solution.py:217
  106.4 12.4 %collective-permute-start.24 = (bf16[768,256]{1,0:T(8,128)(2,1)}, bf16[768,256]{1,0:T(8,128)(2,1)}, u32[]{:S(2)}, u32[]{:S(2)}) collective-permute-start(bf16[768,256]{1,0:T(8,128)(2,1)} %collective-permute-done.22.near_ref), channel_id=1, source_target_pairs={{0,8},{4,28},{8,16},{12,4},{16,24},{20,12},{24,0},{28,20},{1,9},{5... | collective-permute-start | bytes 1179656 | tf_op jit(solution)/shard_map/ppermute | solution.py:244
  111.9 10.8 %collective-permute-start.27 = (bf16[768,256]{1,0:T(8,128)(2,1)S(1)}, bf16[768,256]{1,0:T(8,128)(2,1)S(1)}, u32[]{:S(2)}, u32[]{:S(2)}) collective-permute-start(bf16[768,256]{1,0:T(8,128)(2,1)S(1)} %get-tuple-element.327.refs_2_.refs_12_), channel_id=1, source_target_pairs={{0,2},{1,3},{2,0},{3,1},{4,6},{5,7},{6,4},{7,5},{8,10},{9,11},{10,... | collective-permute-start | bytes 1179656 | tf_op jit(solution)/shard_map/ppermute | solution.py:217
  126.5 22.6 %collective-permute-start.37 = (bf16[384,1024]{1,0:T(8,128)(2,1)}, bf16[384,1024]{1,0:T(8,128)(2,1)}, u32[]{:S(2)}, u32[]{:S(2)}) collective-permute-start(bf16[384,1024]{1,0:T(8,128)(2,1)} %get-tuple-element.357), channel_id=1, source_target_pairs={{0,4},{4,0},{8,12},{12,8},{16,20},{20,16},{24,28},{28,24},{1,5},{5... | collective-permute-start | bytes 2359304 | tf_op jit(solution)/shard_map/ppermute | solution.py:332
  128.3 13.8 %collective-permute-start.30 = (bf16[768,256]{1,0:T(8,128)(2,1)S(1)}, bf16[768,256]{1,0:T(8,128)(2,1)S(1)}, u32[]{:S(2)}, u32[]{:S(2)}) collective-permute-start(bf16[768,256]{1,0:T(8,128)(2,1)S(1)} %get-tuple-element.328.refs_3_.refs_13_), channel_id=1, source_target_pairs={{0,2},{1,3},{2,0},{3,1},{4,6},{5,7},{6,4},{7,5},{8,10},{9,11},{10,... | collective-permute-start | bytes 1179656 | tf_op jit(solution)/shard_map/ppermute | solution.py:217
  130.7 9.2 %collective-permute-start.28 = (f32[8,128]{1,0:T(8,128)S(1)}, f32[8,128]{1,0:T(8,128)S(1)}, u32[]{:S(2)}, u32[]{:S(2)}) collective-permute-start(f32[8,128]{1,0:T(8,128)S(1)} %broadcast_add_fusion), channel_id=1, source_target_pairs={{0,2},{1,3},{2,0},{3,1},{4,6},{5,7},{6,4},{7,5},{8,10},{9,11},{10,... | collective-permute-start | bytes 12296 | tf_op jit(solution)/shard_map/ppermute | solution.py:322
  131.9 17.8 %collective-permute-start.39 = (bf16[768,256]{1,0:T(8,128)(2,1)S(1)}, bf16[768,256]{1,0:T(8,128)(2,1)S(1)}, u32[]{:S(2)}, u32[]{:S(2)}) collective-permute-start(bf16[768,256]{1,0:T(8,128)(2,1)S(1)} %get-tuple-element.307.refs_0_.refs_10_), channel_id=1, source_target_pairs={{0,1},{1,0},{2,3},{3,2},{4,5},{5,4},{6,7},{7,6},{8,9},{9,8},{10,11... | collective-permute-start | bytes 1179656 | tf_op jit(solution)/shard_map/ppermute | solution.py:217
  145.7 8.2 %collective-permute-start.34 = (bf16[768,256]{1,0:T(8,128)(2,1)S(1)}, bf16[768,256]{1,0:T(8,128)(2,1)}, u32[]{:S(2)}, u32[]{:S(2)}) collective-permute-start(bf16[768,256]{1,0:T(8,128)(2,1)S(1)} %collective-permute-done.25.refs_5_.refs_2_), channel_id=1, source_target_pairs={{0,1},{1,0},{2,3},{3,2},{4,5},{5,4},{6,7},{7,6},{8,9},{9,8},{10,11... | collective-permute-start | bytes 1179656 | tf_op jit(solution)/shard_map/ppermute | solution.py:217
  149.2 8.3 %collective-permute-start.36 = (bf16[768,256]{1,0:T(8,128)(2,1)S(1)}, bf16[768,256]{1,0:T(8,128)(2,1)}, u32[]{:S(2)}, u32[]{:S(2)}) collective-permute-start(bf16[768,256]{1,0:T(8,128)(2,1)S(1)} %collective-permute-done.30.refs_7_.refs_4_), channel_id=1, source_target_pairs={{0,1},{1,0},{2,3},{3,2},{4,5},{5,4},{6,7},{7,6},{8,9},{9,8},{10,11... | collective-permute-start | bytes 1179656 | tf_op jit(solution)/shard_map/ppermute | solution.py:217
  149.7 19.8 %collective-permute-start.44 = (bf16[256,1024]{1,0:T(8,128)(2,1)}, bf16[256,1024]{1,0:T(8,128)(2,1)}, u32[]{:S(2)}, u32[]{:S(2)}) collective-permute-start(bf16[256,1024]{1,0:T(8,128)(2,1)} %get-tuple-element.383), channel_id=1, source_target_pairs={{0,4},{4,0},{8,12},{12,8},{16,20},{20,16},{24,28},{28,24},{1,5},{5... | collective-permute-start | bytes 1572872 | tf_op jit(solution)/shard_map/ppermute | solution.py:332
  153.8 10.6 %collective-permute-start.40 = (bf16[768,256]{1,0:T(8,128)(2,1)S(1)}, bf16[768,256]{1,0:T(8,128)(2,1)}, u32[]{:S(2)}, u32[]{:S(2)}) collective-permute-start(bf16[768,256]{1,0:T(8,128)(2,1)S(1)} %get-tuple-element.318.refs_1_.refs_11_), channel_id=1, source_target_pairs={{0,1},{1,0},{2,3},{3,2},{4,5},{5,4},{6,7},{7,6},{8,9},{9,8},{10,11... | collective-permute-start | bytes 1179656 | tf_op jit(solution)/shard_map/ppermute | solution.py:217
  153.8 10.6 %collective-permute-start.41 = (bf16[768,256]{1,0:T(8,128)(2,1)S(1)}, bf16[768,256]{1,0:T(8,128)(2,1)}, u32[]{:S(2)}, u32[]{:S(2)}) collective-permute-start(bf16[768,256]{1,0:T(8,128)(2,1)S(1)} %get-tuple-element.327.refs_2_.refs_12_), channel_id=1, source_target_pairs={{0,1},{1,0},{2,3},{3,2},{4,5},{5,4},{6,7},{7,6},{8,9},{9,8},{10,11... | collective-permute-start | bytes 1179656 | tf_op jit(solution)/shard_map/ppermute | solution.py:217
  155.5 8.9 %collective-permute-start.42 = (bf16[768,256]{1,0:T(8,128)(2,1)S(1)}, bf16[768,256]{1,0:T(8,128)(2,1)}, u32[]{:S(2)}, u32[]{:S(2)}) collective-permute-start(bf16[768,256]{1,0:T(8,128)(2,1)S(1)} %get-tuple-element.328.refs_3_.refs_13_), channel_id=1, source_target_pairs={{0,1},{1,0},{2,3},{3,2},{4,5},{5,4},{6,7},{7,6},{8,9},{9,8},{10,11... | collective-permute-start | bytes 1179656 | tf_op jit(solution)/shard_map/ppermute | solution.py:217
  157.5 12.0 %collective-permute-start.38 = (bf16[192,1024]{1,0:T(8,128)(2,1)}, bf16[192,1024]{1,0:T(8,128)(2,1)}, u32[]{:S(2)}, u32[]{:S(2)}) collective-permute-start(bf16[192,1024]{1,0:T(8,128)(2,1)} %add_convert_fusion), channel_id=1, source_target_pairs={{0,8},{4,12},{8,0},{12,4},{16,24},{20,28},{24,16},{28,20},{1,9},{5... | collective-permute-start | bytes 1179656 | tf_op jit(solution)/shard_map/ppermute | solution.py:314
  169.5 14.5 %collective-permute-start.47 = (bf16[256,1024]{1,0:T(8,128)(2,1)}, bf16[256,1024]{1,0:T(8,128)(2,1)}, u32[]{:S(2)}, u32[]{:S(2)}) collective-permute-start(bf16[256,1024]{1,0:T(8,128)(2,1)} %get-tuple-element.392), channel_id=1, source_target_pairs={{0,4},{4,0},{8,12},{12,8},{16,20},{20,16},{24,28},{28,24},{1,5},{5... | collective-permute-start | bytes 1572872 | tf_op jit(solution)/shard_map/ppermute | solution.py:332
  172.0 12.0 %collective-permute-start.45 = (bf16[128,1024]{1,0:T(8,128)(2,1)S(1)}, bf16[128,1024]{1,0:T(8,128)(2,1)}, u32[]{:S(2)}, u32[]{:S(2)}) collective-permute-start(bf16[128,1024]{1,0:T(8,128)(2,1)S(1)} %add_convert_fusion.3), channel_id=1, source_target_pairs={{0,8},{4,12},{8,0},{12,4},{16,24},{20,28},{24,16},{28,20},{1,9},{5... | collective-permute-start | bytes 786440 | tf_op jit(solution)/shard_map/ppermute | solution.py:314
  173.8 10.2 %collective-permute-start.43 = (bf16[96,1024]{1,0:T(8,128)(2,1)S(1)}, bf16[96,1024]{1,0:T(8,128)(2,1)}, u32[]{:S(2)}, u32[]{:S(2)}) collective-permute-start(bf16[96,1024]{1,0:T(8,128)(2,1)S(1)} %add_convert_fusion.4), channel_id=1, source_target_pairs={{0,16},{4,20},{8,24},{12,28},{16,0},{20,4},{24,8},{28,12},{1,17},{... | collective-permute-start | bytes 589832 | tf_op jit(solution)/shard_map/ppermute | solution.py:314
  184.0 18.4 %collective-permute-start.51 = (bf16[256,1024]{1,0:T(8,128)(2,1)}, bf16[256,1024]{1,0:T(8,128)(2,1)}, u32[]{:S(2)}, u32[]{:S(2)}) collective-permute-start(bf16[256,1024]{1,0:T(8,128)(2,1)} %get-tuple-element.403), channel_id=1, source_target_pairs={{0,4},{4,0},{8,12},{12,8},{16,20},{20,16},{24,28},{28,24},{1,5},{5... | collective-permute-start | bytes 1572872 | tf_op jit(solution)/shard_map/ppermute | solution.py:332
  187.1 14.2 %collective-permute-start.49 = (bf16[64,1024]{1,0:T(8,128)(2,1)S(1)}, bf16[64,1024]{1,0:T(8,128)(2,1)S(1)}, u32[]{:S(2)}, u32[]{:S(2)}) collective-permute-start(bf16[64,1024]{1,0:T(8,128)(2,1)S(1)} %add_convert_fusion.7), channel_id=1, source_target_pairs={{0,16},{4,20},{8,24},{12,28},{16,0},{20,4},{24,8},{28,12},{1,17},{... | collective-permute-start | bytes 393224 | tf_op jit(solution)/shard_map/ppermute | solution.py:314
  191.1 24.4 %collective-permute-start.46 = (bf16[96,1024]{1,0:T(8,128)(2,1)S(1)}, bf16[96,1024]{1,0:T(8,128)(2,1)S(1)}, u32[]{:S(2)}, u32[]{:S(2)}) collective-permute-start(bf16[96,1024]{1,0:T(8,128)(2,1)S(1)} %divide_convert_fusion), channel_id=1, source_target_pairs={{0,16},{4,20},{8,24},{12,28},{16,0},{20,4},{24,8},{28,12},{1,17},{... | collective-permute-start | bytes 589832 | tf_op jit(solution)/shard_map/ppermute | solution.py:314
  202.3 12.1 %collective-permute-start.48 = (bf16[128,1024]{1,0:T(8,128)(2,1)S(1)}, bf16[128,1024]{1,0:T(8,128)(2,1)S(1)}, u32[]{:S(2)}, u32[]{:S(2)}) collective-permute-start(bf16[128,1024]{1,0:T(8,128)(2,1)S(1)} %add_convert_fusion.2), channel_id=1, source_target_pairs={{0,8},{4,12},{8,0},{12,4},{16,24},{20,28},{24,16},{28,20},{1,9},{5... | collective-permute-start | bytes 786440 | tf_op jit(solution)/shard_map/ppermute | solution.py:314
  203.5 19.6 %collective-permute-start.52 = (bf16[128,1024]{1,0:T(8,128)(2,1)S(1)}, bf16[128,1024]{1,0:T(8,128)(2,1)S(1)}, u32[]{:S(2)}, u32[]{:S(2)}) collective-permute-start(bf16[128,1024]{1,0:T(8,128)(2,1)S(1)} %add_convert_fusion.1), channel_id=1, source_target_pairs={{0,8},{4,12},{8,0},{12,4},{16,24},{20,28},{24,16},{28,20},{1,9},{5... | collective-permute-start | bytes 786440 | tf_op jit(solution)/shard_map/ppermute | solution.py:314
  206.6 10.8 %collective-permute-start.54 = (bf16[64,1024]{1,0:T(8,128)(2,1)S(1)}, bf16[64,1024]{1,0:T(8,128)(2,1)S(1)}, u32[]{:S(2)}, u32[]{:S(2)}) collective-permute-start(bf16[64,1024]{1,0:T(8,128)(2,1)S(1)} %divide_convert_fusion.3), channel_id=1, source_target_pairs={{0,16},{4,20},{8,24},{12,28},{16,0},{20,4},{24,8},{28,12},{1,17},{... | collective-permute-start | bytes 393224 | tf_op jit(solution)/shard_map/ppermute | solution.py:314
  215.4 7.7 %collective-permute-start.53 = (bf16[64,1024]{1,0:T(8,128)(2,1)S(1)}, bf16[64,1024]{1,0:T(8,128)(2,1)S(1)}, u32[]{:S(2)}, u32[]{:S(2)}) collective-permute-start(bf16[64,1024]{1,0:T(8,128)(2,1)S(1)} %add_convert_fusion.6), channel_id=1, source_target_pairs={{0,16},{4,20},{8,24},{12,28},{16,0},{20,4},{24,8},{28,12},{1,17},{... | collective-permute-start | bytes 393224 | tf_op jit(solution)/shard_map/ppermute | solution.py:314
  215.5 25.6 %collective-permute-start.50 = (bf16[192,1024]{1,0:T(8,128)(2,1)S(1)}, bf16[192,1024]{1,0:T(8,128)(2,1)S(1)}, u32[]{:S(2)}, u32[]{:S(2)}) collective-permute-start(bf16[192,1024]{1,0:T(8,128)(2,1)S(1)} %pad_maximum_fusion.4), channel_id=1, source_target_pairs={{0,8},{4,12},{8,0},{12,4},{16,24},{20,28},{24,16},{28,20},{1,9},{5... | collective-permute-start | bytes 1179656 | tf_op jit(solution)/shard_map/ppermute | solution.py:314
  224.0 11.8 %collective-permute-start.59 = (bf16[64,1024]{1,0:T(8,128)(2,1)S(1)}, bf16[64,1024]{1,0:T(8,128)(2,1)S(1)}, u32[]{:S(2)}, u32[]{:S(2)}) collective-permute-start(bf16[64,1024]{1,0:T(8,128)(2,1)S(1)} %add_convert_fusion.5), channel_id=1, source_target_pairs={{0,16},{4,20},{8,24},{12,28},{16,0},{20,4},{24,8},{28,12},{1,17},{... | collective-permute-start | bytes 393224 | tf_op jit(solution)/shard_map/ppermute | solution.py:314
  225.1 16.1 %collective-permute-start.56 = (bf16[64,1024]{1,0:T(8,128)(2,1)S(1)}, bf16[64,1024]{1,0:T(8,128)(2,1)S(1)}, u32[]{:S(2)}, u32[]{:S(2)}) collective-permute-start(bf16[64,1024]{1,0:T(8,128)(2,1)S(1)} %divide_convert_fusion.2), channel_id=1, source_target_pairs={{0,16},{4,20},{8,24},{12,28},{16,0},{20,4},{24,8},{28,12},{1,17},{... | collective-permute-start | bytes 393224 | tf_op jit(solution)/shard_map/ppermute | solution.py:314
  236.9 11.9 %collective-permute-start.57 = (bf16[128,1024]{1,0:T(8,128)(2,1)S(1)}, bf16[128,1024]{1,0:T(8,128)(2,1)S(1)}, u32[]{:S(2)}, u32[]{:S(2)}) collective-permute-start(bf16[128,1024]{1,0:T(8,128)(2,1)S(1)} %pad_maximum_fusion.5), channel_id=1, source_target_pairs={{0,8},{4,12},{8,0},{12,4},{16,24},{20,28},{24,16},{28,20},{1,9},{5... | collective-permute-start | bytes 786440 | tf_op jit(solution)/shard_map/ppermute | solution.py:314
  241.2 13.2 %collective-permute-start.58 = (bf16[128,1024]{1,0:T(8,128)(2,1)S(1)}, bf16[128,1024]{1,0:T(8,128)(2,1)S(1)}, u32[]{:S(2)}, u32[]{:S(2)}) collective-permute-start(bf16[128,1024]{1,0:T(8,128)(2,1)S(1)} %pad_maximum_fusion.6), channel_id=1, source_target_pairs={{0,8},{4,12},{8,0},{12,4},{16,24},{20,28},{24,16},{28,20},{1,9},{5... | collective-permute-start | bytes 786440 | tf_op jit(solution)/shard_map/ppermute | solution.py:314
  243.5 15.1 %collective-permute-start.67 = (bf16[128,1024]{1,0:T(8,128)(2,1)S(1)}, bf16[128,1024]{1,0:T(8,128)(2,1)S(1)}, u32[]{:S(2)}, u32[]{:S(2)}) collective-permute-start(bf16[128,1024]{1,0:T(8,128)(2,1)S(1)} %pad_maximum_fusion.7), channel_id=1, source_target_pairs={{0,8},{4,12},{8,0},{12,4},{16,24},{20,28},{24,16},{28,20},{1,9},{5... | collective-permute-start | bytes 786440 | tf_op jit(solution)/shard_map/ppermute | solution.py:314
  245.6 51.6 %collective-permute-start.55 = (bf16[384,1024]{1,0:T(8,128)(2,1)S(1)}, bf16[384,1024]{1,0:T(8,128)(2,1)S(1)}, u32[]{:S(2)}, u32[]{:S(2)}) collective-permute-start(bf16[384,1024]{1,0:T(8,128)(2,1)S(1)} %pad_maximum_fusion.refs_4_), channel_id=1, source_target_pairs={{0,4},{4,0},{8,12},{12,8},{16,20},{20,16},{24,28},{28,24},{1,5},{5... | collective-permute-start | bytes 2359304 | tf_op jit(solution)/shard_map/ppermute | solution.py:357
  248.8 28.6 %collective-permute-start.60 = (bf16[256,1024]{1,0:T(8,128)(2,1)S(1)}, bf16[256,1024]{1,0:T(8,128)(2,1)S(1)}, u32[]{:S(2)}, u32[]{:S(2)}) collective-permute-start(bf16[256,1024]{1,0:T(8,128)(2,1)S(1)} %pad_maximum_fusion.1.refs_5_), channel_id=1, source_target_pairs={{0,4},{4,0},{8,12},{12,8},{16,20},{20,16},{24,28},{28,24},{1,5},{5... | collective-permute-start | bytes 1572872 | tf_op jit(solution)/shard_map/ppermute | solution.py:357
  254.4 34.2 %collective-permute-start.63 = (bf16[256,1024]{1,0:T(8,128)(2,1)S(1)}, bf16[256,1024]{1,0:T(8,128)(2,1)S(1)}, u32[]{:S(2)}, u32[]{:S(2)}) collective-permute-start(bf16[256,1024]{1,0:T(8,128)(2,1)S(1)} %pad_maximum_fusion.2.refs_5_), channel_id=1, source_target_pairs={{0,4},{4,0},{8,12},{12,8},{16,20},{20,16},{24,28},{28,24},{1,5},{5... | collective-permute-start | bytes 1572872 | tf_op jit(solution)/shard_map/ppermute | solution.py:357
  258.7 36.8 %collective-permute-start.68 = (bf16[256,1024]{1,0:T(8,128)(2,1)S(1)}, bf16[256,1024]{1,0:T(8,128)(2,1)S(1)}, u32[]{:S(2)}, u32[]{:S(2)}) collective-permute-start(bf16[256,1024]{1,0:T(8,128)(2,1)S(1)} %pad_maximum_fusion.3.refs_6_), channel_id=1, source_target_pairs={{0,4},{4,0},{8,12},{12,8},{16,20},{20,16},{24,28},{28,24},{1,5},{5... | collective-permute-start | bytes 1572872 | tf_op jit(solution)/shard_map/ppermute | solution.py:357
  260.9 34.6 %collective-permute-start.61 = (bf16[256,1024]{1,0:T(8,128)(2,1)S(1)}, bf16[256,1024]{1,0:T(8,128)(2,1)S(1)}, u32[]{:S(2)}, u32[]{:S(2)}) collective-permute-start(bf16[256,1024]{1,0:T(8,128)(2,1)S(1)} %pad_maximum_fusion.1.refs_5_), channel_id=1, source_target_pairs={{0,2},{1,3},{2,0},{3,1},{4,6},{5,7},{6,4},{7,5},{8,10},{9,11},{10,... | collective-permute-start | bytes 1572872 | tf_op jit(solution)/shard_map/ppermute | solution.py:217
  277.4 24.0 %collective-permute-start.64 = (bf16[256,1024]{1,0:T(8,128)(2,1)S(1)}, bf16[256,1024]{1,0:T(8,128)(2,1)S(1)}, u32[]{:S(2)}, u32[]{:S(2)}) collective-permute-start(bf16[256,1024]{1,0:T(8,128)(2,1)S(1)} %pad_maximum_fusion.2.refs_5_), channel_id=1, source_target_pairs={{0,3},{1,2},{2,1},{3,0},{4,7},{5,6},{6,5},{7,4},{8,11},{9,10},{10,... | collective-permute-start | bytes 1572872 | tf_op jit(solution)/shard_map/ppermute | solution.py:217
  288.7 14.9 %collective-permute-start.62 = (bf16[256,1024]{1,0:T(8,128)(2,1)S(1)}, bf16[256,1024]{1,0:T(8,128)(2,1)S(1)}, u32[]{:S(2)}, u32[]{:S(2)}) collective-permute-start(bf16[256,1024]{1,0:T(8,128)(2,1)S(1)} %collective-permute-done.60.refs_6_), channel_id=1, source_target_pairs={{0,2},{1,3},{2,0},{3,1},{4,6},{5,7},{6,4},{7,5},{8,10},{9,11},{10,... | collective-permute-start | bytes 1572872 | tf_op jit(solution)/shard_map/ppermute | solution.py:217
  295.5 18.0 %collective-permute-start.65 = (bf16[256,1024]{1,0:T(8,128)(2,1)S(1)}, bf16[256,1024]{1,0:T(8,128)(2,1)S(1)}, u32[]{:S(2)}, u32[]{:S(2)}) collective-permute-start(bf16[256,1024]{1,0:T(8,128)(2,1)S(1)} %collective-permute-done.63.refs_6_), channel_id=1, source_target_pairs={{0,3},{1,2},{2,1},{3,0},{4,7},{5,6},{6,5},{7,4},{8,11},{9,10},{10,... | collective-permute-start | bytes 1572872 | tf_op jit(solution)/shard_map/ppermute | solution.py:217
  295.5 24.7 %collective-permute-start.69 = (bf16[256,1024]{1,0:T(8,128)(2,1)S(1)}, bf16[256,1024]{1,0:T(8,128)(2,1)S(1)}, u32[]{:S(2)}, u32[]{:S(2)}) collective-permute-start(bf16[256,1024]{1,0:T(8,128)(2,1)S(1)} %pad_maximum_fusion.3.refs_6_), channel_id=1, source_target_pairs={{0,1},{1,0},{2,3},{3,2},{4,5},{5,4},{6,7},{7,6},{8,9},{9,8},{10,11... | collective-permute-start | bytes 1572872 | tf_op jit(solution)/shard_map/ppermute | solution.py:217
  297.2 22.9 %collective-permute-start.70 = (bf16[256,1024]{1,0:T(8,128)(2,1)S(1)}, bf16[256,1024]{1,0:T(8,128)(2,1)S(1)}, u32[]{:S(2)}, u32[]{:S(2)}) collective-permute-start(bf16[256,1024]{1,0:T(8,128)(2,1)S(1)} %collective-permute-done.68.refs_7_), channel_id=1, source_target_pairs={{0,1},{1,0},{2,3},{3,2},{4,5},{5,4},{6,7},{7,6},{8,9},{9,8},{10,11... | collective-permute-start | bytes 1572872 | tf_op jit(solution)/shard_map/ppermute | solution.py:217
  (27 other events, 192.0 us)

commit v5 on v4

v5 whole, which is shorter than its diff:
```python
import functools

import jax
import jax.numpy as jnp
from jax import lax
from jax.experimental import pallas as pl
from jax.experimental.pallas import tpu as pltpu
from jax.sharding import PartitionSpec as P

CHUNKS = 4
F32 = jnp.float32
BF16 = jnp.bfloat16
VMEM_LIMIT = 48 * 1024 * 1024


class Order:
    def __init__(self, token):
        self.token = token

    def __call__(self, *values):
        *values, self.token = lax.optimization_barrier((*values, self.token))
        return values[0] if len(values) == 1 else tuple(values)


class Schedule:
    RATE = 94e3
    CORE_RATE = 400e3
    DELAY = 2.5

    def __init__(self):
        self.now = 0.0
        self.free = {}

    def spend(self, time):
        self.now += time

    def transfer(self, value, link, weight=1.0):
        self.spend(1.3)
        size = value.size * value.dtype.itemsize
        time = weight * (size / self.CORE_RATE if link == "core" else 2 * size / self.RATE)
        begin = max(self.now, self.free.get(link, 0.0))
        self.free[link] = begin + time
        return begin + time + self.DELAY

    def run(self, processes):
        ready = [0.0] * len(processes)
        alive = list(range(len(processes)))
        while alive:
            can = [i for i in alive if ready[i] <= self.now]
            if not can:
                self.now = min(ready[i] for i in alive)
                continue
            try:
                ready[can[0]] = next(processes[can[0]])
            except StopIteration:
                alive.remove(can[0])


def product_kernel(stage, place_ref, blocks_ref, field_ref, near_ref, far_ref, *refs):
    elements, size, _ = blocks_ref.shape
    width = field_ref.shape[1]
    squares = jnp.zeros((8, width), F32)
    filler = jnp.zeros((size, width), BF16)
    for element in range(elements):
        picked = []
        for slot in range(7):
            source = field_ref if slot < 5 else near_ref if slot == 5 else far_ref
            first_row = pl.multiple_of(place_ref[element, slot] * size, size)
            picked.append(source[pl.ds(first_row, size), :])
        stacked = jnp.concatenate(picked + [filler], axis=0)
        total = jnp.dot(blocks_ref[element], stacked, preferred_element_type=F32)
        here = pl.ds(element * size, size)
        if stage == 0:
            wide_ref, half_ref = refs
            wide_ref[here, :] = total
            half_ref[here, :] = total.astype(BF16)
        elif stage == 1:
            before_ref, half_ref = refs
            half_ref[here, :] = (2.0 * total - before_ref[here, :].astype(F32)).astype(BF16)
        else:
            before_ref, half_ref, squares_ref = refs
            value = (2.0 * total - before_ref[here, :]).astype(BF16)
            half_ref[here, :] = value
            wide = value.astype(F32)
            squares += jnp.sum((wide * wide).reshape(-1, 8, width), axis=0)
    if stage == 2:
        squares_ref[...] = squares


def call(kernel, name, outs, scalars, args, scratch=(), aliases=None):
    return pl.pallas_call(
        kernel,
        out_shape=outs,
        in_specs=[pl.BlockSpec(memory_space=pltpu.SMEM)] * len(scalars)
        + [pl.BlockSpec(memory_space=pltpu.VMEM)] * len(args),
        scratch_shapes=list(scratch),
        input_output_aliases=aliases or {},
        compiler_params=pltpu.CompilerParams(vmem_limit_bytes=VMEM_LIMIT),
        cost_estimate=pl.CostEstimate(flops=1024, bytes_accessed=1024, transcendentals=0),
        name=name,
    )(*scalars, *args)


def product(stage, place, blocks, field, by_near, by_far, before=None):
    rows, width = field.shape
    half = jax.ShapeDtypeStruct((rows, width), BF16)
    wide = jax.ShapeDtypeStruct((rows, width), F32)
    squares = jax.ShapeDtypeStruct((8, width), F32)
    outs = ((wide, half), half, (half, squares))[stage]
    args = (blocks, field, by_near, by_far) + (() if before is None else (before,))
    kernel = functools.partial(product_kernel, stage)
    return call(kernel, f"product_{stage}", outs, (place,), args)


def put_in_place(where_ref, masks, mine_ref, far_ref, out_ref, base):
    bits = len(masks)
    height = mine_ref.shape[0] >> (bits - 1)
    for side, ref in ((0, mine_ref), (1, far_ref)):
        for position in range(1 << (bits - 1)):
            distance = side << (bits - 1) | position
            number = 0
            for i, mask in enumerate(masks):
                apart = distance >> (bits - 1 - i) & 1
                number = 2 * number + lax.rem(where_ref[0] // mask + apart, 2)
            here = pl.ds(pl.multiple_of(base + number * height, height), height)
            out_ref[here, :] = ref[position * height : (position + 1) * height, :]


TRANSPOSED_LEFT = (((0,), (0,)), ((), ()))
TRANSPOSED_RIGHT = (((1,), (1,)), ((), ()))


def side_by_side(refs):
    return jnp.concatenate([ref[...] for ref in refs], axis=1)


def gram_kernel(pair, mask, where_ref, *refs):
    mine_ref, other_ref, whole = refs[-3:]
    fields = refs[:CHUNKS]
    half = whole.shape[0] // 2
    width = fields[0].shape[1]
    middle = CHUNKS * width // 2
    side = lax.rem(where_ref[0] // mask, 2)

    def fill(left, rights, count):
        for c, right in enumerate(rights):
            value = lax.dot_general(left, right[...], TRANSPOSED_LEFT, preferred_element_type=F32)
            whole[:count, c * width : (c + 1) * width] = value.astype(BF16)

    if pair:
        peers = refs[CHUNKS : 2 * CHUNKS]
        used = middle

        @pl.when(where_ref[1] == 0)
        def _():
            fill(side_by_side(peers[: CHUNKS // 2]), fields, middle)

        @pl.when(where_ref[1] == 1)
        def _():
            fill(side_by_side(fields[CHUNKS // 2 :]), peers, middle)
    else:
        used = middle + middle // 2
        upper = side_by_side(fields[CHUNKS // 2 :])
        fill(side_by_side(fields[: CHUNKS // 2]), fields, middle)
        corner = lax.dot_general(upper, upper, TRANSPOSED_LEFT, preferred_element_type=F32).astype(BF16)
        whole[middle:used, :middle] = corner[: middle // 2]
        whole[middle:used, middle:] = corner[middle // 2 :]
    if used < whole.shape[0]:
        whole[used:, :] = jnp.zeros((whole.shape[0] - used, whole.shape[1]), BF16)
    mine_ref[...] = whole[pl.ds(pl.multiple_of(side * half, half), half), :]
    other_ref[...] = whole[pl.ds(pl.multiple_of((1 - side) * half, half), half), :]


def mix_kernel(pair, masks, first, last, where_ref, *refs):
    level_ref, *refs = refs if last else (None, *refs)
    total_ref, *refs = (None, *refs) if first else refs
    fields, refs = refs[:CHUNKS], refs[CHUNKS:]
    out_ref, block = refs[-2:]
    own = refs[-2 - CHUNKS : -2]
    width = fields[0].shape[1]
    middle = CHUNKS * width // 2

    def finish(mixed, here):
        value = mixed if first else total_ref[:, here] + mixed
        if last:
            filtered = side_by_side(own)[:, here].astype(F32)
            value = (1.5 * filtered - 0.5 * value) / jnp.sqrt(level_ref[0])
        out_ref[:, here] = value.astype(out_ref.dtype)

    def times(left, right):
        return jnp.dot(left, right, preferred_element_type=F32)

    def times_transposed(left, right):
        return lax.dot_general(left, right, TRANSPOSED_RIGHT, preferred_element_type=F32)

    if not pair:
        put_in_place(where_ref, masks, refs[0], refs[1], block, 0)
        lower, upper = side_by_side(fields[: CHUNKS // 2]), side_by_side(fields[CHUNKS // 2 :])
        corner = block[middle : middle + middle // 2, :]
        corner = jnp.concatenate([corner[:, :middle], corner[:, middle:]], axis=0)
        finish(
            times(lower, block[:middle, :middle]) + times_transposed(upper, block[:middle, middle:]),
            slice(0, middle),
        )
        finish(times(lower, block[:middle, middle:]) + times(upper, corner), slice(middle, 2 * middle))
        return
    height = block.shape[0] // 2
    is_upper = where_ref[1]
    put_in_place(where_ref, masks, refs[0], refs[1], block, is_upper * height)
    put_in_place(where_ref, masks, refs[2], refs[3], block, (1 - is_upper) * height)

    @pl.when(is_upper == 0)
    def _():
        field = side_by_side(fields)
        for c in range(CHUNKS):
            here = slice(c * width, (c + 1) * width)
            finish(times(field, jnp.concatenate([block[:middle, here], block[height : height + middle, here]])), here)

    @pl.when(is_upper == 1)
    def _():
        field = side_by_side(fields)
        for c in range(CHUNKS):
            row = c * width if c * width < middle else height + c * width - middle
            finish(times_transposed(field, block[row : row + width, :]), slice(c * width, (c + 1) * width))


def local(orbitals, hamiltonian, neighbours):
    elements, slots, size, _ = hamiltonian.shape
    rows, columns = orbitals.shape
    tiles = lax.axis_size("elem")
    groups = lax.axis_size("orb")
    lines = tiles // 2
    my_tile = lax.axis_index("elem")
    my_group = lax.axis_index("orb")
    odd = my_tile % 2
    line = my_tile // 2

    swap = [(i, i ^ 1) for i in range(tiles)]
    outward = [(2 * i + side, 2 * ((i + 1 - 2 * side) % lines) + side) for i in range(lines) for side in (0, 1)]

    def to_group(value, d):
        return lax.ppermute(value, "orb", [(i, i ^ d) for i in range(groups)])

    place = neighbours % elements
    last_two = place[:, 5:]
    place = jnp.concatenate([place[:, :5], jnp.where(odd == 0, last_two[:, ::-1], last_two)], axis=1)
    by_slot = [hamiltonian[:, s] for s in range(5)]
    by_slot.append(jnp.where(odd == 0, hamiltonian[:, 6], hamiltonian[:, 5]))
    by_slot.append(jnp.where(odd == 0, hamiltonian[:, 5], hamiltonian[:, 6]))
    by_slot.append(jnp.zeros_like(by_slot[0]))
    blocks = jnp.concatenate(by_slot, axis=2)

    width = columns // CHUNKS
    start = [lax.slice_in_dim(orbitals, c * width, (c + 1) * width, axis=1) for c in range(CHUNKS)]
    near = {(0, 0): lax.ppermute(start[0], "elem", swap)}
    order = Order(jnp.zeros((8, 128), F32))
    blocks, place = order(blocks, place)
    start = [start[0]] + [order(field) for field in start[1:]]
    for c in range(1, CHUNKS):
        near[(0, c)] = lax.ppermute(start[c], "elem", swap)

    jobs = [(stage, c) for stage in range(3) for c in range(CHUNKS)]
    far = {}
    firsts, squares, pieces = {}, [], [{} for _ in range(CHUNKS)]
    current = {(0, c): start[c] for c in range(CHUNKS)}

    def send_on(job):
        near[job] = order(near[job])
        far[job] = lax.ppermute(near[job], "elem", outward)

    def more_panel(c):
        for d in range(1, groups):
            if d & (d - 1):
                low = d & -d
                if d ^ low in pieces[c] and d not in pieces[c]:
                    pieces[c][d ^ low] = order(pieces[c][d ^ low])
                    pieces[c][d] = to_group(pieces[c][d ^ low], low)

    def multiply(job):
        stage, c = job
        far[job] = order(far[job])
        old = (None, start[c], firsts.get(c))[stage]
        out = product(stage, place, blocks, current[job], near[job], far[job], old)
        if stage == 0:
            firsts[c], out = order(*out)
        elif stage == 1:
            out = order(out)
        else:
            out, square = order(*out)
            squares.append(square)
            pieces[c][0] = out
            bit = groups // 2
            while bit:
                pieces[c][bit] = to_group(out, bit)
                bit //= 2
            if c:
                more_panel(c - 1)
            return
        current[(stage + 1, c)] = out
        near[(stage + 1, c)] = lax.ppermute(out, "elem", swap)

    for index, job in enumerate(jobs):
        send_on(job)
        if index:
            multiply(jobs[index - 1])
    multiply(jobs[-1])

    squares = sum(squares)
    rows_total = rows * tiles
    level = None
    middle = columns // 2
    unit = 16 * tiles
    clock = Schedule()
    z_masks = [2 << i for i in range(lines.bit_length() - 1)]
    there = {d: 3.0 if d == 1 else 10.5 for d in range(1, groups)}
    mixed, mixes = None, 0

    def is_upper(d):
        return (my_group & (1 << (d.bit_length() - 1))) != 0

    def where(d):
        return jnp.stack([my_tile, is_upper(d) if d else odd]).astype(jnp.int32)

    def all_chunks(d):
        return [pieces[c][d] for c in range(CHUNKS)]

    def over_tiles(value, mask):
        sent = lax.ppermute(value, "elem", [(i, i ^ mask) for i in range(tiles)])
        if mask <= 2:
            return sent, clock.transfer(value, "y" if mask == 1 else "z")
        clock.spend(-1.3)
        return sent, max(clock.transfer(value, "z", mask / 4), clock.transfer(value, "middle", mask / 2))

    def over_groups(value, d):
        return to_group(value, d), clock.transfer(value, "core" if d == 1 else "x")

    def panel_process():
        yield 10.5
        more_panel(CHUNKS - 1)
        clock.spend(1.3)
        for d in range(1, groups):
            if d & (d - 1):
                there[d] = clock.now + 3.5

    def gram_chunk(d, mask):
        height = middle if d else middle + middle // 2
        height += -height % unit
        fields = all_chunks(0)
        if d:
            fields += order(*all_chunks(d))
        half = jax.ShapeDtypeStruct((height // 2, columns), BF16)
        scratch = (pltpu.VMEM((height, columns), BF16),)
        name = "gram_pair" if d else "gram_own"
        clock.spend(3.2 if d else 3.0)
        return call(functools.partial(gram_kernel, d > 0, mask), name, (half, half), (where(d),), fields, scratch)

    def level_process():
        nonlocal level
        yield 4.0
        total = jnp.full((8, 128), jnp.sum(squares), F32)
        for axis, peers in (("elem", tiles), ("orb", groups)):
            bit = 1
            while bit < peers:
                total = order(total)
                other = lax.ppermute(total, axis, [(i, i ^ bit) for i in range(peers)])
                clock.spend(1.5)
                yield clock.now + 3.5
                total = total + order(other)
                clock.spend(0.6)
                bit *= 2
        level = total[0, 0] / (columns * groups * rows_total)

    def process(d, masks):
        nonlocal mixed, mixes
        while d and (d not in pieces[-1] or there[d] > clock.now):
            yield max(there[d], clock.now + 0.5)
        mine, value = order(*gram_chunk(d, masks[0]))
        terms = [(mine, 0)]
        height, offset = mine.shape[0], 0

        def added(first_row, count):
            clock.spend(1.0)
            return sum(lax.dynamic_slice_in_dim(v, first_row - row, count, 0).astype(F32) for v, row in terms)

        for i, mask in enumerate(masks):
            if i:
                height //= 2
                keep = (my_tile // mask) % 2
                value = added(offset + (1 - keep) * height, height).astype(BF16)
                offset = offset + keep * height
            received, arrival = over_tiles(value, mask)
            yield arrival
            terms.append((order(received), offset))
        while level is None:
            yield clock.now + 0.5
        part = (added(offset, height) / (level * rows_total)).astype(BF16)
        for mask in masks[:0:-1]:
            received, arrival = over_tiles(part, mask)
            yield arrival
            part = jnp.concatenate([part, order(received)], axis=0)
            clock.spend(0.7)
        part = order(part)
        far, arrival = over_tiles(part, masks[0])
        if d:
            peer, peer_arrival = over_groups(part, d)
        yield arrival
        far = order(far)
        parts = (part, far)
        if d:
            peer_far, arrival = over_groups(far, d)
            yield peer_arrival
            peer = order(peer)
            yield arrival
            peer_far = order(peer_far)
            parts += (peer, peer_far)
        first, last = mixes == 0, mixes == groups - 1
        mixes += 1
        shape = jax.ShapeDtypeStruct((rows, columns), BF16 if last else F32)
        scratch = (pltpu.VMEM((len(parts) * part.shape[0], columns), BF16),)
        args = (() if first else (mixed,)) + (*all_chunks(d), *parts)
        scalars = (where(d),)
        if last:
            scalars += (level.reshape(1),)
            args += tuple(all_chunks(0))
        kernel = functools.partial(mix_kernel, d > 0, masks, first, last)
        name = "mix_pair" if d else "mix_own"
        clock.spend(5.7 if d else 4.5)
        mixed = call(kernel, name, shape, scalars, args, scratch, {} if first or last else {1: 0})
        if not last:
            mixed = order(mixed)

    y_first, z_first, z_then_y = (1, *z_masks), (*z_masks, 1), (*z_masks[:1], 1, *z_masks[1:])
    queue = sorted(range(1, groups), key=lambda d: (d == 1, d))
    processes = [panel_process(), level_process(), process(0, z_first)]
    processes += [process(d, z_then_y if i == 0 else y_first) for i, d in enumerate(queue)]
    clock.run(processes)
    return mixed


def solution(mesh):
    return jax.shard_map(
        local,
        mesh=mesh,
        in_specs=(P("elem", "orb"), P("elem", None, None, None), P("elem", None)),
        out_specs=P("elem", "orb"),
        check_vma=False,
    )
```

time: 327 us -> 307 us (0.939)
  waiting for transfers between devices: 130 us -> 115 us
    ppermute x24, waiting for transfers between devices: 79.6 us -> 51.7 us  [over_tiles(): sent = lax.ppermute(value, 'elem', [(i, i ^ mask) for i in range(tiles)])]
    ppermute x18, waiting for transfers between devices: 6.6 us -> 21.2 us  [to_group(): return lax.ppermute(value, 'orb', [(i, i ^ d) for i in range(groups)])]
    ppermute x5, waiting for transfers between devices: 12.3 us -> 8.81 us  [level_process(): other = lax.ppermute(total, axis, [(i, i ^ bit) for i in range(peers)])]
    unnamed x41 -> x43, local copies, waits for them, and re-layouts: 8.73 us -> 6.8 us
  transfers between devices with their start and end apart: 71 -> 71, of which waited for: 34 -> 34; matrix products, arithmetic and copies ran while one was open for 7% -> 6% of each run, Pallas kernels for 12% -> 14%
where the time goes in v5:
time: 307 us; the launch traced here: 304 us
  waiting for transfers between devices  115 us (37%)
  starting transfers between devices  110 us (36%)
  Pallas kernels  47.9 us (16%)
  other arithmetic  14.9 us (5%)
  local copies, waits for them, and re-layouts  13.1 us (4%)
    ppermute x24, waiting for transfers between devices, over_tiles(): sent = lax.ppermute(value, 'elem', [(i, i ^ mask) for i in range(tiles)])  51.7 us
    pallas_call x20, Pallas kernels, call(): pl.pallas_call(kernel, out_shape=outs, in_specs=[pl.BlockSpec(memory_spac...  47.9 us
    ppermute x24, starting transfers between devices, over_tiles(): sent = lax.ppermute(value, 'elem', [(i, i ^ mask) for i in range(tiles)])  33.3 us
    ppermute x8, starting transfers between devices, multiply(): near[stage + 1, c] = lax.ppermute(out, 'elem', swap)  27.7 us
    ppermute x12, starting transfers between devices, send_on(): far[job] = lax.ppermute(near[job], 'elem', outward)  25 us
    ppermute x18, waiting for transfers between devices, to_group(): return lax.ppermute(value, 'orb', [(i, i ^ d) for i in range(groups)])  21.2 us
    ppermute x18, starting transfers between devices, to_group(): return lax.ppermute(value, 'orb', [(i, i ^ d) for i in range(groups)])  11.4 us
    ppermute x8, waiting for transfers between devices, multiply(): near[stage + 1, c] = lax.ppermute(out, 'elem', swap)  10.9 us
  transfers between devices with their start and end apart: 71, of which 34 were waited for; matrix products, arithmetic and copies ran while one was open for 6% of the time, Pallas kernels for 14%

profile of v5, /device:TPU:0, one launch (start us, length us, event | category | flops | bytes accessed | tf_op | source)
XLA Modules:
  0.0 303.6 jit_solution(10402888090507137193)
XLA Ops:
  1.6 3.0 collective-permute-start
  6.7 2.5 concatenate.34.blocks_ref
  9.5 5.1 %collective-permute-done.near_ref = bf16[768,256]{1,0:T(8,128)(2,1)S(1)} collective-permute-done((bf16[768,256]{1,0:T(8,128)(2,1)S(1)}, bf16[768,256]{1,0:T(8,128)(2,1)S(1)}, u32[]{:S(2)}, u32[]{:S(2)}) %collective-permute-start) | collective-permute-done | bytes 393248 | tf_op jit(solution)/shard_map/ppermute | solution.py:255
  14.6 2.1 collective-permute-start.1
  16.7 3.5 %collective-permute-start.4 = (bf16[768,256]{1,0:T(8,128)(2,1)S(1)}, bf16[768,256]{1,0:T(8,128)(2,1)S(1)}, u32[]{:S(2)}, u32[]{:S(2)}) collective-permute-start(bf16[768,256]{1,0:T(8,128)(2,1)S(1)} %get-tuple-element.233.field_ref.refs_0_), channel_id=1, source_target_pairs={{0,4},{4,0},{8,12},{12,8},{16,20},{20,16},{24,28},{28,24},{1,5},{5... | collective-permute-start | bytes 1179656 | tf_op jit(solution)/shard_map/ppermute | solution.py:260
  20.3 2.7 collective-permute-done.2.near_ref
  23.0 2.1 collective-permute-start.7
  27.1 4.3 %collective-permute-done.4.near_ref = bf16[768,256]{1,0:T(8,128)(2,1)S(1)} collective-permute-done((bf16[768,256]{1,0:T(8,128)(2,1)S(1)}, bf16[768,256]{1,0:T(8,128)(2,1)S(1)}, u32[]{:S(2)}, u32[]{:S(2)}) %collective-permute-start.4) | collective-permute-done | bytes 393248 | tf_op jit(solution)/shard_map/ppermute | solution.py:260
  31.4 2.1 collective-permute-start.5
  33.5 3.5 %collective-permute-start.3 = (bf16[768,256]{1,0:T(8,128)(2,1)S(1)}, bf16[768,256]{1,0:T(8,128)(2,1)S(1)}, u32[]{:S(2)}, u32[]{:S(2)}) collective-permute-start(bf16[768,256]{1,0:T(8,128)(2,1)S(1)} %get-tuple-element.232.field_ref), channel_id=1, source_target_pairs={{0,4},{4,0},{8,12},{12,8},{16,20},{20,16},{24,28},{28,24},{1,5},{5... | collective-permute-start | bytes 1179656 | tf_op jit(solution)/shard_map/ppermute | solution.py:300
  39.9 2.1 collective-permute-start.10
  42.0 3.5 %collective-permute-start.9 = (bf16[768,256]{1,0:T(8,128)(2,1)S(1)}, bf16[768,256]{1,0:T(8,128)(2,1)S(1)}, u32[]{:S(2)}, u32[]{:S(2)}) collective-permute-start(bf16[768,256]{1,0:T(8,128)(2,1)S(1)} %get-tuple-element.251.field_ref), channel_id=1, source_target_pairs={{0,4},{4,0},{8,12},{12,8},{16,20},{20,16},{24,28},{28,24},{1,5},{5... | collective-permute-start | bytes 1179656 | tf_op jit(solution)/shard_map/ppermute | solution.py:300
  48.3 2.1 collective-permute-start.8
  50.4 3.5 %collective-permute-start.12 = (bf16[768,256]{1,0:T(8,128)(2,1)S(1)}, bf16[768,256]{1,0:T(8,128)(2,1)S(1)}, u32[]{:S(2)}, u32[]{:S(2)}) collective-permute-start(bf16[768,256]{1,0:T(8,128)(2,1)S(1)} %get-tuple-element.263.field_ref), channel_id=1, source_target_pairs={{0,4},{4,0},{8,12},{12,8},{16,20},{20,16},{24,28},{28,24},{1,5},{5... | collective-permute-start | bytes 1179656 | tf_op jit(solution)/shard_map/ppermute | solution.py:300
  56.7 2.1 collective-permute-start.15
  58.8 3.5 %collective-permute-start.14 = (bf16[768,256]{1,0:T(8,128)(2,1)S(1)}, bf16[768,256]{1,0:T(8,128)(2,1)S(1)}, u32[]{:S(2)}, u32[]{:S(2)}) collective-permute-start(bf16[768,256]{1,0:T(8,128)(2,1)S(1)} %get-tuple-element.266.field_ref), channel_id=1, source_target_pairs={{0,4},{4,0},{8,12},{12,8},{16,20},{20,16},{24,28},{28,24},{1,5},{5... | collective-permute-start | bytes 1179656 | tf_op jit(solution)/shard_map/ppermute | solution.py:300
  65.1 2.1 collective-permute-start.13
  67.2 3.5 %collective-permute-start.11 = (bf16[768,256]{1,0:T(8,128)(2,1)S(1)}, bf16[768,256]{1,0:T(8,128)(2,1)S(1)}, u32[]{:S(2)}, u32[]{:S(2)}) collective-permute-start(bf16[768,256]{1,0:T(8,128)(2,1)S(1)} %product_1.4.field_ref), channel_id=1, source_target_pairs={{0,4},{4,0},{8,12},{12,8},{16,20},{20,16},{24,28},{28,24},{1,5},{5... | collective-permute-start | bytes 1179656 | tf_op jit(solution)/shard_map/ppermute | solution.py:300
  73.6 2.1 collective-permute-start.18
  75.7 3.5 %collective-permute-start.17 = (bf16[768,256]{1,0:T(8,128)(2,1)S(1)}, bf16[768,256]{1,0:T(8,128)(2,1)S(1)}, u32[]{:S(2)}, u32[]{:S(2)}) collective-permute-start(bf16[768,256]{1,0:T(8,128)(2,1)S(1)} %product_1.5.field_ref), channel_id=1, source_target_pairs={{0,4},{4,0},{8,12},{12,8},{16,20},{20,16},{24,28},{28,24},{1,5},{5... | collective-permute-start | bytes 1179656 | tf_op jit(solution)/shard_map/ppermute | solution.py:300
  82.0 2.1 collective-permute-start.16
  84.1 3.5 %collective-permute-start.20 = (bf16[768,256]{1,0:T(8,128)(2,1)S(1)}, bf16[768,256]{1,0:T(8,128)(2,1)S(1)}, u32[]{:S(2)}, u32[]{:S(2)}) collective-permute-start(bf16[768,256]{1,0:T(8,128)(2,1)S(1)} %product_1.6.field_ref), channel_id=1, source_target_pairs={{0,4},{4,0},{8,12},{12,8},{16,20},{20,16},{24,28},{28,24},{1,5},{5... | collective-permute-start | bytes 1179656 | tf_op jit(solution)/shard_map/ppermute | solution.py:300
  90.4 2.1 collective-permute-start.19
  96.1 2.9 collective-permute-start.22
  98.9 2.0 collective-permute-start.21
  104.5 1.9 collective-permute-done.22.near_ref
  106.4 1.8 collective-permute-start.24
  108.2 1.9 collective-permute-done.21.far_ref
  113.5 5.1 %collective-permute-done.24.far_ref = bf16[768,256]{1,0:T(8,128)(2,1)S(1)} collective-permute-done((bf16[768,256]{1,0:T(8,128)(2,1)S(1)}, bf16[768,256]{1,0:T(8,128)(2,1)S(1)}, u32[]{:S(2)}, u32[]{:S(2)}) %collective-permute-start.24) | collective-permute-done | bytes 393248 | tf_op jit(solution)/shard_map/ppermute | solution.py:269
  123.3 3.0 gram_own.1
  130.9 2.0 collective-permute-start.27
  135.0 3.2 %gram_pair.3 = (bf16[256,1024]{1,0:T(8,128)(2,1)S(1)}, bf16[256,1024]{1,0:T(8,128)(2,1)}) custom-call(s32[2]{0:T(128)S(1)} %pad_add_fusion.3.where_ref, bf16[768,256]{1,0:T(8,128)(2,1)S(1)} %get-tuple-element.302.refs_0_.refs_1_.refs_10_, bf16[768,256]{1,0:T(8,128)(2,1)S(1)} %get-tuple-element.313.refs_1_.refs_2_.refs_11_, ...), custom_call_target="tpu_custom_call" | custom-call | flops 1024 | bytes 1024 | tf_op jit(solution)/shard_map/gram_pair/pallas_call | solution.py:91
  139.6 2.0 collective-permute-start.32
  141.7 2.4 gram_pair.4
  144.9 2.6 collective-permute-done.32
  149.8 2.4 gram_pair.5
  152.3 6.2 %collective-permute-done.34 = f32[8,128]{1,0:T(8,128)} collective-permute-done((f32[8,128]{1,0:T(8,128)S(1)}, f32[8,128]{1,0:T(8,128)}, u32[]{:S(2)}, u32[]{:S(2)}) %collective-permute-start.34) | collective-permute-done | bytes 4128 | tf_op jit(solution)/shard_map/ppermute | solution.py:365
  160.9 3.5 %collective-permute-start.44 = (bf16[128,1024]{1,0:T(8,128)(2,1)}, bf16[128,1024]{1,0:T(8,128)(2,1)}, u32[]{:S(2)}, u32[]{:S(2)}) collective-permute-start(bf16[128,1024]{1,0:T(8,128)(2,1)} %add_convert_fusion.3), channel_id=1, source_target_pairs={{0,8},{4,12},{8,0},{12,4},{16,24},{20,28},{24,16},{28,20},{1,9},{5... | collective-permute-start | bytes 786440 | tf_op jit(solution)/shard_map/ppermute | solution.py:328
  164.4 1.9 add_convert_fusion
  166.5 2.9 collective-permute-start.47
  172.6 2.3 collective-permute-start.48
  176.1 2.6 collective-permute-start.46
  179.8 8.2 %collective-permute-done.45 = bf16[192,1024]{1,0:T(8,128)(2,1)} collective-permute-done((bf16[192,1024]{1,0:T(8,128)(2,1)}, bf16[192,1024]{1,0:T(8,128)(2,1)}, u32[]{:S(2)}, u32[]{:S(2)}) %collective-permute-start.45) | collective-permute-done | bytes 393248 | tf_op jit(solution)/shard_map/ppermute | solution.py:328
  189.2 3.6 %collective-permute-start.49 = (bf16[96,1024]{1,0:T(8,128)(2,1)S(1)}, bf16[96,1024]{1,0:T(8,128)(2,1)S(1)}, u32[]{:S(2)}, u32[]{:S(2)}) collective-permute-start(bf16[96,1024]{1,0:T(8,128)(2,1)S(1)} %add_convert_fusion.4), channel_id=1, source_target_pairs={{0,4},{4,0},{8,12},{12,8},{16,20},{20,16},{24,28},{28,24},{1,5},{5... | collective-permute-start | bytes 589832 | tf_op jit(solution)/shard_map/ppermute | solution.py:328
  195.0 3.0 collective-permute-start.50
  198.1 3.9 %collective-permute-done.52 = bf16[64,1024]{1,0:T(8,128)(2,1)S(1)} collective-permute-done((bf16[64,1024]{1,0:T(8,128)(2,1)S(1)}, bf16[64,1024]{1,0:T(8,128)(2,1)S(1)}, u32[]{:S(2)}, u32[]{:S(2)}) %collective-permute-start.52) | collective-permute-done | bytes 131104 | tf_op jit(solution)/shard_map/ppermute | solution.py:328
  202.1 2.1 collective-permute-done.50
  206.4 5.7 %collective-permute-done.51 = bf16[128,1024]{1,0:T(8,128)(2,1)S(1)} collective-permute-done((bf16[128,1024]{1,0:T(8,128)(2,1)S(1)}, bf16[128,1024]{1,0:T(8,128)(2,1)S(1)}, u32[]{:S(2)}, u32[]{:S(2)}) %collective-permute-start.51) | collective-permute-done | bytes 262176 | tf_op jit(solution)/shard_map/ppermute | solution.py:328
  214.4 2.3 collective-permute-done.56
  216.7 3.4 %collective-permute-done.55 = bf16[64,1024]{1,0:T(8,128)(2,1)S(1)} collective-permute-done((bf16[64,1024]{1,0:T(8,128)(2,1)S(1)}, bf16[64,1024]{1,0:T(8,128)(2,1)S(1)}, u32[]{:S(2)}, u32[]{:S(2)}) %collective-permute-start.55) | collective-permute-done | bytes 131104 | tf_op jit(solution)/shard_map/ppermute | solution.py:328
  220.3 2.3 collective-permute-start.59
  222.7 5.4 %collective-permute-done.57 = bf16[64,1024]{1,0:T(8,128)(2,1)S(1)} collective-permute-done((bf16[64,1024]{1,0:T(8,128)(2,1)S(1)}, bf16[64,1024]{1,0:T(8,128)(2,1)S(1)}, u32[]{:S(2)}, u32[]{:S(2)}) %collective-permute-start.57) | collective-permute-done | bytes 131104 | tf_op jit(solution)/shard_map/ppermute | solution.py:328
  228.1 4.6 %collective-permute-start.67 = (bf16[128,1024]{1,0:T(8,128)(2,1)S(1)}, bf16[128,1024]{1,0:T(8,128)(2,1)S(1)}, u32[]{:S(2)}, u32[]{:S(2)}) collective-permute-start(bf16[128,1024]{1,0:T(8,128)(2,1)S(1)} %pad_maximum_fusion.7), channel_id=1, source_target_pairs={{0,8},{4,12},{8,0},{12,4},{16,24},{20,28},{24,16},{28,20},{1,9},{5... | collective-permute-start | bytes 786440 | tf_op jit(solution)/shard_map/ppermute | solution.py:328
  232.8 3.4 %collective-permute-start.65 = (bf16[192,1024]{1,0:T(8,128)(2,1)S(1)}, bf16[192,1024]{1,0:T(8,128)(2,1)S(1)}, u32[]{:S(2)}, u32[]{:S(2)}) collective-permute-start(bf16[192,1024]{1,0:T(8,128)(2,1)S(1)} %pad_maximum_fusion.4), channel_id=1, source_target_pairs={{0,16},{4,20},{8,24},{12,28},{16,0},{20,4},{24,8},{28,12},{1,17},{... | collective-permute-start | bytes 1179656 | tf_op jit(solution)/shard_map/ppermute | solution.py:328
  236.2 3.3 %collective-permute-done.58 = bf16[128,1024]{1,0:T(8,128)(2,1)S(1)} collective-permute-done((bf16[128,1024]{1,0:T(8,128)(2,1)S(1)}, bf16[128,1024]{1,0:T(8,128)(2,1)S(1)}, u32[]{:S(2)}, u32[]{:S(2)}) %collective-permute-start.58) | collective-permute-done | bytes 262176 | tf_op jit(solution)/shard_map/ppermute | solution.py:328
  241.6 4.8 %collective-permute-done.65 = bf16[192,1024]{1,0:T(8,128)(2,1)S(1)} collective-permute-done((bf16[192,1024]{1,0:T(8,128)(2,1)S(1)}, bf16[192,1024]{1,0:T(8,128)(2,1)S(1)}, u32[]{:S(2)}, u32[]{:S(2)}) %collective-permute-start.65) | collective-permute-done | bytes 393248 | tf_op jit(solution)/shard_map/ppermute | solution.py:328
  246.5 9.9 %collective-permute-done.62.refs_6_ = bf16[256,1024]{1,0:T(8,128)(2,1)S(1)} collective-permute-done((bf16[256,1024]{1,0:T(8,128)(2,1)S(1)}, bf16[256,1024]{1,0:T(8,128)(2,1)S(1)}, u32[]{:S(2)}, u32[]{:S(2)}) %collective-permute-start.62) | collective-permute-done | bytes 524320 | tf_op jit(solution)/shard_map/ppermute | solution.py:328
  260.8 10.4 %collective-permute-done.63.refs_7_ = bf16[256,1024]{1,0:T(8,128)(2,1)S(1)} collective-permute-done((bf16[256,1024]{1,0:T(8,128)(2,1)S(1)}, bf16[256,1024]{1,0:T(8,128)(2,1)S(1)}, u32[]{:S(2)}, u32[]{:S(2)}) %collective-permute-start.63) | collective-permute-done | bytes 524320 | tf_op jit(solution)/shard_map/ppermute | solution.py:242
  271.2 4.8 %mix_pair.3.refs_0_ = f32[768,1024]{1,0:T(8,128)} custom-call(s32[2]{0:T(128)S(1)} %pad_add_fusion.3.where_ref, bf16[768,256]{1,0:T(8,128)(2,1)S(1)} %copy-done.2, bf16[768,256]{1,0:T(8,128)(2,1)S(1)} %copy-done.5, bf16[768,256]{1,0:T(8,128)(2,1)} %collective-permute-done.30.refs_6_.refs_2_, bf16[768,256]{1,0:T(8,128)(2,1)} %collective-permute-done.31.refs_7_.refs_3_, ...), custom_call_target="tpu_custom_call" | custom-call | flops 1024 | bytes 1024 | tf_op jit(solution)/shard_map/mix_pair/pallas_call | solution.py:91
  276.0 6.4 %collective-permute-done.64.refs_8_ = bf16[256,1024]{1,0:T(8,128)(2,1)S(1)} collective-permute-done((bf16[256,1024]{1,0:T(8,128)(2,1)S(1)}, bf16[256,1024]{1,0:T(8,128)(2,1)S(1)}, u32[]{:S(2)}, u32[]{:S(2)}) %collective-permute-start.64) | collective-permute-done | bytes 524320 | tf_op jit(solution)/shard_map/ppermute | solution.py:242
  282.4 5.8 %mix_pair.4.refs_0_ = f32[768,1024]{1,0:T(8,128)} custom-call(s32[2]{0:T(128)S(1)} %pad_add_fusion.1.where_ref, f32[768,1024]{1,0:T(8,128)} %mix_pair.3.refs_0_, bf16[768,256]{1,0:T(8,128)(2,1)S(1)} %collective-permute-done.23.refs_4_.refs_1_, bf16[768,256]{1,0:T(8,128)(2,1)S(1)} %collective-permute-done.25.refs_5_.refs_2_, ...), custom_call_target="tpu_custom_call", output_to_operand_aliasing={{}: (1, {})} | custom-call | flops 1024 | bytes 1024 | tf_op jit(solution)/shard_map/mix_pair/pallas_call | solution.py:91
  288.2 3.5 %collective-permute-done.69.refs_8_ = bf16[256,1024]{1,0:T(8,128)(2,1)S(1)} collective-permute-done((bf16[256,1024]{1,0:T(8,128)(2,1)S(1)}, bf16[256,1024]{1,0:T(8,128)(2,1)S(1)}, u32[]{:S(2)}, u32[]{:S(2)}) %collective-permute-start.69) | collective-permute-done | bytes 524320 | tf_op jit(solution)/shard_map/ppermute | solution.py:242
  291.7 5.5 %mix_own.1.refs_1_ = f32[768,1024]{1,0:T(8,128)} custom-call(s32[2]{0:T(128)S(1)} %copy-done.17, f32[768,1024]{1,0:T(8,128)} %mix_pair.4.refs_0_, bf16[768,256]{1,0:T(8,128)(2,1)S(1)} %get-tuple-element.302.refs_0_.refs_1_.refs_10_, bf16[768,256]{1,0:T(8,128)(2,1)S(1)} %get-tuple-element.313.refs_1_.refs_2_.refs_11_, ...), custom_call_target="tpu_custom_call", output_to_operand_aliasing={{}: (1, {})} | custom-call | flops 1024 | bytes 1024 | tf_op jit(solution)/shard_map/mix_own/pallas_call | solution.py:91
  298.0 5.5 %mix_pair.5 = bf16[768,1024]{1,0:T(8,128)(2,1)} custom-call(s32[2]{0:T(128)S(1)} %pad_add_fusion.1.where_ref, f32[1]{0:T(128)} %bitcast.11.refs_0_, f32[768,1024]{1,0:T(8,128)} %mix_own.1.refs_1_, bf16[768,256]{1,0:T(8,128)(2,1)S(1)} %collective-permute-done.35.refs_4_.refs_2_, bf16[768,256]{1,0:T(8,128)(2,1)} %collective-permute-done.36.refs_5_.refs_3_, ...), custom_call_target="tpu_custom_call" | custom-call | flops 1024 | bytes 1024 | tf_op jit(solution)/shard_map/mix_pair/pallas_call | solution.py:91
  (182 shorter events, 74.2 us)
Async XLA Ops:
  1.6 13.0 %collective-permute-start = (bf16[768,256]{1,0:T(8,128)(2,1)S(1)}, bf16[768,256]{1,0:T(8,128)(2,1)S(1)}, u32[]{:S(2)}, u32[]{:S(2)}) collective-permute-start(bf16[768,256]{1,0:T(8,128)(2,1)S(1)} %get-tuple-element.431.field_ref.refs_0_), channel_id=1, source_target_pairs={{0,4},{4,0},{8,12},{12,8},{16,20},{20,16},{24,28},{28,24},{1,5},{5... | collective-permute-start | bytes 1179656 | tf_op jit(solution)/shard_map/ppermute | solution.py:255
  9.3 13.7 %collective-permute-start.2 = (bf16[768,256]{1,0:T(8,128)(2,1)S(1)}, bf16[768,256]{1,0:T(8,128)(2,1)S(1)}, u32[]{:S(2)}, u32[]{:S(2)}) collective-permute-start(bf16[768,256]{1,0:T(8,128)(2,1)S(1)} %get-tuple-element.225.field_ref.refs_0_), channel_id=1, source_target_pairs={{0,4},{4,0},{8,12},{12,8},{16,20},{20,16},{24,28},{28,24},{1,5},{5... | collective-permute-start | bytes 1179656 | tf_op jit(solution)/shard_map/ppermute | solution.py:260
  14.6 11.3 %collective-permute-start.1 = (bf16[768,256]{1,0:T(8,128)(2,1)S(1)}, bf16[768,256]{1,0:T(8,128)(2,1)S(1)}, u32[]{:S(2)}, u32[]{:S(2)}) collective-permute-start(bf16[768,256]{1,0:T(8,128)(2,1)S(1)} %collective-permute-done.near_ref), channel_id=1, source_target_pairs={{0,8},{4,28},{8,16},{12,4},{16,24},{20,12},{24,0},{28,20},{1,9},{5... | collective-permute-start | bytes 1179656 | tf_op jit(solution)/shard_map/ppermute | solution.py:269
  16.7 14.7 %collective-permute-start.4 = (bf16[768,256]{1,0:T(8,128)(2,1)S(1)}, bf16[768,256]{1,0:T(8,128)(2,1)S(1)}, u32[]{:S(2)}, u32[]{:S(2)}) collective-permute-start(bf16[768,256]{1,0:T(8,128)(2,1)S(1)} %get-tuple-element.233.field_ref.refs_0_), channel_id=1, source_target_pairs={{0,4},{4,0},{8,12},{12,8},{16,20},{20,16},{24,28},{28,24},{1,5},{5... | collective-permute-start | bytes 1179656 | tf_op jit(solution)/shard_map/ppermute | solution.py:260
  20.2 19.6 %collective-permute-start.6 = (bf16[768,256]{1,0:T(8,128)(2,1)S(1)}, bf16[768,256]{1,0:T(8,128)(2,1)S(1)}, u32[]{:S(2)}, u32[]{:S(2)}) collective-permute-start(bf16[768,256]{1,0:T(8,128)(2,1)S(1)} %get-tuple-element.236.field_ref.refs_0_), channel_id=1, source_target_pairs={{0,4},{4,0},{8,12},{12,8},{16,20},{20,16},{24,28},{28,24},{1,5},{5... | collective-permute-start | bytes 1179656 | tf_op jit(solution)/shard_map/ppermute | solution.py:260
  23.0 14.1 %collective-permute-start.7 = (bf16[768,256]{1,0:T(8,128)(2,1)S(1)}, bf16[768,256]{1,0:T(8,128)(2,1)S(1)}, u32[]{:S(2)}, u32[]{:S(2)}) collective-permute-start(bf16[768,256]{1,0:T(8,128)(2,1)S(1)} %collective-permute-done.2.near_ref), channel_id=1, source_target_pairs={{0,8},{4,28},{8,16},{12,4},{16,24},{20,12},{24,0},{28,20},{1,9},{5... | collective-permute-start | bytes 1179656 | tf_op jit(solution)/shard_map/ppermute | solution.py:269
  31.4 14.1 %collective-permute-start.5 = (bf16[768,256]{1,0:T(8,128)(2,1)S(1)}, bf16[768,256]{1,0:T(8,128)(2,1)S(1)}, u32[]{:S(2)}, u32[]{:S(2)}) collective-permute-start(bf16[768,256]{1,0:T(8,128)(2,1)S(1)} %collective-permute-done.4.near_ref), channel_id=1, source_target_pairs={{0,8},{4,28},{8,16},{12,4},{16,24},{20,12},{24,0},{28,20},{1,9},{5... | collective-permute-start | bytes 1179656 | tf_op jit(solution)/shard_map/ppermute | solution.py:269
  33.5 14.7 %collective-permute-start.3 = (bf16[768,256]{1,0:T(8,128)(2,1)S(1)}, bf16[768,256]{1,0:T(8,128)(2,1)S(1)}, u32[]{:S(2)}, u32[]{:S(2)}) collective-permute-start(bf16[768,256]{1,0:T(8,128)(2,1)S(1)} %get-tuple-element.232.field_ref), channel_id=1, source_target_pairs={{0,4},{4,0},{8,12},{12,8},{16,20},{20,16},{24,28},{28,24},{1,5},{5... | collective-permute-start | bytes 1179656 | tf_op jit(solution)/shard_map/ppermute | solution.py:300
  39.9 14.1 %collective-permute-start.10 = (bf16[768,256]{1,0:T(8,128)(2,1)S(1)}, bf16[768,256]{1,0:T(8,128)(2,1)S(1)}, u32[]{:S(2)}, u32[]{:S(2)}) collective-permute-start(bf16[768,256]{1,0:T(8,128)(2,1)S(1)} %collective-permute-done.6.near_ref), channel_id=1, source_target_pairs={{0,8},{4,28},{8,16},{12,4},{16,24},{20,12},{24,0},{28,20},{1,9},{5... | collective-permute-start | bytes 1179656 | tf_op jit(solution)/shard_map/ppermute | solution.py:269
  42.0 14.7 %collective-permute-start.9 = (bf16[768,256]{1,0:T(8,128)(2,1)S(1)}, bf16[768,256]{1,0:T(8,128)(2,1)S(1)}, u32[]{:S(2)}, u32[]{:S(2)}) collective-permute-start(bf16[768,256]{1,0:T(8,128)(2,1)S(1)} %get-tuple-element.251.field_ref), channel_id=1, source_target_pairs={{0,4},{4,0},{8,12},{12,8},{16,20},{20,16},{24,28},{28,24},{1,5},{5... | collective-permute-start | bytes 1179656 | tf_op jit(solution)/shard_map/ppermute | solution.py:300
  48.3 14.1 %collective-permute-start.8 = (bf16[768,256]{1,0:T(8,128)(2,1)S(1)}, bf16[768,256]{1,0:T(8,128)(2,1)S(1)}, u32[]{:S(2)}, u32[]{:S(2)}) collective-permute-start(bf16[768,256]{1,0:T(8,128)(2,1)S(1)} %collective-permute-done.3.near_ref), channel_id=1, source_target_pairs={{0,8},{4,28},{8,16},{12,4},{16,24},{20,12},{24,0},{28,20},{1,9},{5... | collective-permute-start | bytes 1179656 | tf_op jit(solution)/shard_map/ppermute | solution.py:269
  50.4 14.7 %collective-permute-start.12 = (bf16[768,256]{1,0:T(8,128)(2,1)S(1)}, bf16[768,256]{1,0:T(8,128)(2,1)S(1)}, u32[]{:S(2)}, u32[]{:S(2)}) collective-permute-start(bf16[768,256]{1,0:T(8,128)(2,1)S(1)} %get-tuple-element.263.field_ref), channel_id=1, source_target_pairs={{0,4},{4,0},{8,12},{12,8},{16,20},{20,16},{24,28},{28,24},{1,5},{5... | collective-permute-start | bytes 1179656 | tf_op jit(solution)/shard_map/ppermute | solution.py:300
  56.7 14.1 %collective-permute-start.15 = (bf16[768,256]{1,0:T(8,128)(2,1)S(1)}, bf16[768,256]{1,0:T(8,128)(2,1)S(1)}, u32[]{:S(2)}, u32[]{:S(2)}) collective-permute-start(bf16[768,256]{1,0:T(8,128)(2,1)S(1)} %collective-permute-done.9.near_ref), channel_id=1, source_target_pairs={{0,8},{4,28},{8,16},{12,4},{16,24},{20,12},{24,0},{28,20},{1,9},{5... | collective-permute-start | bytes 1179656 | tf_op jit(solution)/shard_map/ppermute | solution.py:269
  58.8 14.7 %collective-permute-start.14 = (bf16[768,256]{1,0:T(8,128)(2,1)S(1)}, bf16[768,256]{1,0:T(8,128)(2,1)S(1)}, u32[]{:S(2)}, u32[]{:S(2)}) collective-permute-start(bf16[768,256]{1,0:T(8,128)(2,1)S(1)} %get-tuple-element.266.field_ref), channel_id=1, source_target_pairs={{0,4},{4,0},{8,12},{12,8},{16,20},{20,16},{24,28},{28,24},{1,5},{5... | collective-permute-start | bytes 1179656 | tf_op jit(solution)/shard_map/ppermute | solution.py:300
  65.1 14.1 %collective-permute-start.13 = (bf16[768,256]{1,0:T(8,128)(2,1)S(1)}, bf16[768,256]{1,0:T(8,128)(2,1)S(1)}, u32[]{:S(2)}, u32[]{:S(2)}) collective-permute-start(bf16[768,256]{1,0:T(8,128)(2,1)S(1)} %collective-permute-done.12.near_ref), channel_id=1, source_target_pairs={{0,8},{4,28},{8,16},{12,4},{16,24},{20,12},{24,0},{28,20},{1,9},{5... | collective-permute-start | bytes 1179656 | tf_op jit(solution)/shard_map/ppermute | solution.py:269
  67.2 14.7 %collective-permute-start.11 = (bf16[768,256]{1,0:T(8,128)(2,1)S(1)}, bf16[768,256]{1,0:T(8,128)(2,1)S(1)}, u32[]{:S(2)}, u32[]{:S(2)}) collective-permute-start(bf16[768,256]{1,0:T(8,128)(2,1)S(1)} %product_1.4.field_ref), channel_id=1, source_target_pairs={{0,4},{4,0},{8,12},{12,8},{16,20},{20,16},{24,28},{28,24},{1,5},{5... | collective-permute-start | bytes 1179656 | tf_op jit(solution)/shard_map/ppermute | solution.py:300
  73.6 14.1 %collective-permute-start.18 = (bf16[768,256]{1,0:T(8,128)(2,1)S(1)}, bf16[768,256]{1,0:T(8,128)(2,1)S(1)}, u32[]{:S(2)}, u32[]{:S(2)}) collective-permute-start(bf16[768,256]{1,0:T(8,128)(2,1)S(1)} %collective-permute-done.14.near_ref), channel_id=1, source_target_pairs={{0,8},{4,28},{8,16},{12,4},{16,24},{20,12},{24,0},{28,20},{1,9},{5... | collective-permute-start | bytes 1179656 | tf_op jit(solution)/shard_map/ppermute | solution.py:269
  75.7 14.7 %collective-permute-start.17 = (bf16[768,256]{1,0:T(8,128)(2,1)S(1)}, bf16[768,256]{1,0:T(8,128)(2,1)S(1)}, u32[]{:S(2)}, u32[]{:S(2)}) collective-permute-start(bf16[768,256]{1,0:T(8,128)(2,1)S(1)} %product_1.5.field_ref), channel_id=1, source_target_pairs={{0,4},{4,0},{8,12},{12,8},{16,20},{20,16},{24,28},{28,24},{1,5},{5... | collective-permute-start | bytes 1179656 | tf_op jit(solution)/shard_map/ppermute | solution.py:300
  82.0 11.3 %collective-permute-start.16 = (bf16[768,256]{1,0:T(8,128)(2,1)S(1)}, bf16[768,256]{1,0:T(8,128)(2,1)S(1)}, u32[]{:S(2)}, u32[]{:S(2)}) collective-permute-start(bf16[768,256]{1,0:T(8,128)(2,1)S(1)} %collective-permute-done.11.near_ref), channel_id=1, source_target_pairs={{0,8},{4,28},{8,16},{12,4},{16,24},{20,12},{24,0},{28,20},{1,9},{5... | collective-permute-start | bytes 1179656 | tf_op jit(solution)/shard_map/ppermute | solution.py:269
  84.1 14.8 %collective-permute-start.20 = (bf16[768,256]{1,0:T(8,128)(2,1)S(1)}, bf16[768,256]{1,0:T(8,128)(2,1)S(1)}, u32[]{:S(2)}, u32[]{:S(2)}) collective-permute-start(bf16[768,256]{1,0:T(8,128)(2,1)S(1)} %product_1.6.field_ref), channel_id=1, source_target_pairs={{0,4},{4,0},{8,12},{12,8},{16,20},{20,16},{24,28},{28,24},{1,5},{5... | collective-permute-start | bytes 1179656 | tf_op jit(solution)/shard_map/ppermute | solution.py:300
  90.4 11.3 %collective-permute-start.19 = (bf16[768,256]{1,0:T(8,128)(2,1)S(1)}, bf16[768,256]{1,0:T(8,128)(2,1)S(1)}, u32[]{:S(2)}, u32[]{:S(2)}) collective-permute-start(bf16[768,256]{1,0:T(8,128)(2,1)S(1)} %collective-permute-done.17.near_ref), channel_id=1, source_target_pairs={{0,8},{4,28},{8,16},{12,4},{16,24},{20,12},{24,0},{28,20},{1,9},{5... | collective-permute-start | bytes 1179656 | tf_op jit(solution)/shard_map/ppermute | solution.py:269
  94.5 10.0 %collective-permute-start.23 = (bf16[768,256]{1,0:T(8,128)(2,1)S(1)}, bf16[768,256]{1,0:T(8,128)(2,1)S(1)}, u32[]{:S(2)}, u32[]{:S(2)}) collective-permute-start(bf16[768,256]{1,0:T(8,128)(2,1)S(1)} %get-tuple-element.302.refs_0_.refs_1_.refs_10_), channel_id=1, source_target_pairs={{0,2},{1,3},{2,0},{3,1},{4,6},{5,7},{6,4},{7,5},{8,10},{9,11},{10,... | collective-permute-start | bytes 1179656 | tf_op jit(solution)/shard_map/ppermute | solution.py:242
  96.1 10.4 %collective-permute-start.22 = (bf16[768,256]{1,0:T(8,128)(2,1)S(1)}, bf16[768,256]{1,0:T(8,128)(2,1)S(1)}, u32[]{:S(2)}, u32[]{:S(2)}) collective-permute-start(bf16[768,256]{1,0:T(8,128)(2,1)S(1)} %product_1.7.field_ref), channel_id=1, source_target_pairs={{0,4},{4,0},{8,12},{12,8},{16,20},{20,16},{24,28},{28,24},{1,5},{5... | collective-permute-start | bytes 1179656 | tf_op jit(solution)/shard_map/ppermute | solution.py:300
  98.9 11.2 %collective-permute-start.21 = (bf16[768,256]{1,0:T(8,128)(2,1)S(1)}, bf16[768,256]{1,0:T(8,128)(2,1)S(1)}, u32[]{:S(2)}, u32[]{:S(2)}) collective-permute-start(bf16[768,256]{1,0:T(8,128)(2,1)S(1)} %collective-permute-done.20.near_ref), channel_id=1, source_target_pairs={{0,8},{4,28},{8,16},{12,4},{16,24},{20,12},{24,0},{28,20},{1,9},{5... | collective-permute-start | bytes 1179656 | tf_op jit(solution)/shard_map/ppermute | solution.py:269
  103.0 10.0 %collective-permute-start.25 = (bf16[768,256]{1,0:T(8,128)(2,1)S(1)}, bf16[768,256]{1,0:T(8,128)(2,1)S(1)}, u32[]{:S(2)}, u32[]{:S(2)}) collective-permute-start(bf16[768,256]{1,0:T(8,128)(2,1)S(1)} %get-tuple-element.313.refs_1_.refs_2_.refs_11_), channel_id=1, source_target_pairs={{0,2},{1,3},{2,0},{3,1},{4,6},{5,7},{6,4},{7,5},{8,10},{9,11},{10,... | collective-permute-start | bytes 1179656 | tf_op jit(solution)/shard_map/ppermute | solution.py:242
  106.4 12.1 %collective-permute-start.24 = (bf16[768,256]{1,0:T(8,128)(2,1)S(1)}, bf16[768,256]{1,0:T(8,128)(2,1)S(1)}, u32[]{:S(2)}, u32[]{:S(2)}) collective-permute-start(bf16[768,256]{1,0:T(8,128)(2,1)S(1)} %collective-permute-done.22.near_ref), channel_id=1, source_target_pairs={{0,8},{4,28},{8,16},{12,4},{16,24},{20,12},{24,0},{28,20},{1,9},{5... | collective-permute-start | bytes 1179656 | tf_op jit(solution)/shard_map/ppermute | solution.py:269
  108.2 12.2 %collective-permute-start.28 = (bf16[768,256]{1,0:T(8,128)(2,1)S(1)}, bf16[768,256]{1,0:T(8,128)(2,1)S(1)}, u32[]{:S(2)}, u32[]{:S(2)}) collective-permute-start(bf16[768,256]{1,0:T(8,128)(2,1)S(1)} %get-tuple-element.302.refs_0_.refs_1_.refs_10_), channel_id=1, source_target_pairs={{0,1},{1,0},{2,3},{3,2},{4,5},{5,4},{6,7},{7,6},{8,9},{9,8},{10,11... | collective-permute-start | bytes 1179656 | tf_op jit(solution)/shard_map/ppermute | solution.py:242
  111.4 10.3 %collective-permute-start.26 = (bf16[768,256]{1,0:T(8,128)(2,1)S(1)}, bf16[768,256]{1,0:T(8,128)(2,1)S(1)}, u32[]{:S(2)}, u32[]{:S(2)}) collective-permute-start(bf16[768,256]{1,0:T(8,128)(2,1)S(1)} %get-tuple-element.322.refs_2_.refs_3_.refs_12_), channel_id=1, source_target_pairs={{0,2},{1,3},{2,0},{3,1},{4,6},{5,7},{6,4},{7,5},{8,10},{9,11},{10,... | collective-permute-start | bytes 1179656 | tf_op jit(solution)/shard_map/ppermute | solution.py:242
  112.9 14.2 %collective-permute-start.29 = (bf16[768,256]{1,0:T(8,128)(2,1)S(1)}, bf16[768,256]{1,0:T(8,128)(2,1)S(1)}, u32[]{:S(2)}, u32[]{:S(2)}) collective-permute-start(bf16[768,256]{1,0:T(8,128)(2,1)S(1)} %get-tuple-element.313.refs_1_.refs_2_.refs_11_), channel_id=1, source_target_pairs={{0,1},{1,0},{2,3},{3,2},{4,5},{5,4},{6,7},{7,6},{8,9},{9,8},{10,11... | collective-permute-start | bytes 1179656 | tf_op jit(solution)/shard_map/ppermute | solution.py:242
  112.9 17.9 %collective-permute-start.30 = (bf16[768,256]{1,0:T(8,128)(2,1)S(1)}, bf16[768,256]{1,0:T(8,128)(2,1)}, u32[]{:S(2)}, u32[]{:S(2)}) collective-permute-start(bf16[768,256]{1,0:T(8,128)(2,1)S(1)} %get-tuple-element.322.refs_2_.refs_3_.refs_12_), channel_id=1, source_target_pairs={{0,1},{1,0},{2,3},{3,2},{4,5},{5,4},{6,7},{7,6},{8,9},{9,8},{10,11... | collective-permute-start | bytes 1179656 | tf_op jit(solution)/shard_map/ppermute | solution.py:242
  120.4 10.5 %collective-permute-start.31 = (bf16[768,256]{1,0:T(8,128)(2,1)S(1)}, bf16[768,256]{1,0:T(8,128)(2,1)}, u32[]{:S(2)}, u32[]{:S(2)}) collective-permute-start(bf16[768,256]{1,0:T(8,128)(2,1)S(1)} %get-tuple-element.323.refs_3_.refs_4_.refs_13_), channel_id=1, source_target_pairs={{0,1},{1,0},{2,3},{3,2},{4,5},{5,4},{6,7},{7,6},{8,9},{9,8},{10,11... | collective-permute-start | bytes 1179656 | tf_op jit(solution)/shard_map/ppermute | solution.py:242
  121.2 18.0 %collective-permute-start.35 = (bf16[768,256]{1,0:T(8,128)(2,1)S(1)}, bf16[768,256]{1,0:T(8,128)(2,1)S(1)}, u32[]{:S(2)}, u32[]{:S(2)}) collective-permute-start(bf16[768,256]{1,0:T(8,128)(2,1)S(1)} %collective-permute-done.23.refs_4_.refs_1_), channel_id=1, source_target_pairs={{0,1},{1,0},{2,3},{3,2},{4,5},{5,4},{6,7},{7,6},{8,9},{9,8},{10,11... | collective-permute-start | bytes 1179656 | tf_op jit(solution)/shard_map/ppermute | solution.py:242
  121.8 17.3 %collective-permute-start.33 = (bf16[768,256]{1,0:T(8,128)(2,1)S(1)}, bf16[768,256]{1,0:T(8,128)(2,1)S(1)}, u32[]{:S(2)}, u32[]{:S(2)}) collective-permute-start(bf16[768,256]{1,0:T(8,128)(2,1)S(1)} %get-tuple-element.323.refs_3_.refs_4_.refs_13_), channel_id=1, source_target_pairs={{0,2},{1,3},{2,0},{3,1},{4,6},{5,7},{6,4},{7,5},{8,10},{9,11},{10,... | collective-permute-start | bytes 1179656 | tf_op jit(solution)/shard_map/ppermute | solution.py:242
  127.9 31.2 %collective-permute-start.41 = (bf16[384,1024]{1,0:T(8,128)(2,1)}, bf16[384,1024]{1,0:T(8,128)(2,1)}, u32[]{:S(2)}, u32[]{:S(2)}) collective-permute-start(bf16[384,1024]{1,0:T(8,128)(2,1)} %get-tuple-element.372), channel_id=1, source_target_pairs={{0,8},{4,12},{8,0},{12,4},{16,24},{20,28},{24,16},{28,20},{1,9},{5... | collective-permute-start | bytes 2359304 | tf_op jit(solution)/shard_map/ppermute | solution.py:328
  139.0 20.2 %collective-permute-start.40 = (bf16[256,1024]{1,0:T(8,128)(2,1)}, bf16[256,1024]{1,0:T(8,128)(2,1)}, u32[]{:S(2)}, u32[]{:S(2)}) collective-permute-start(bf16[256,1024]{1,0:T(8,128)(2,1)} %get-tuple-element.371), channel_id=1, source_target_pairs={{0,4},{4,0},{8,12},{12,8},{16,20},{20,16},{24,28},{28,24},{1,5},{5... | collective-permute-start | bytes 1572872 | tf_op jit(solution)/shard_map/ppermute | solution.py:328
  139.1 9.2 %collective-permute-start.37 = (bf16[768,256]{1,0:T(8,128)(2,1)S(1)}, bf16[768,256]{1,0:T(8,128)(2,1)}, u32[]{:S(2)}, u32[]{:S(2)}) collective-permute-start(bf16[768,256]{1,0:T(8,128)(2,1)S(1)} %collective-permute-done.26.refs_6_.refs_3_), channel_id=1, source_target_pairs={{0,1},{1,0},{2,3},{3,2},{4,5},{5,4},{6,7},{7,6},{8,9},{9,8},{10,11... | collective-permute-start | bytes 1179656 | tf_op jit(solution)/shard_map/ppermute | solution.py:242
  139.2 10.6 %collective-permute-start.38 = (bf16[768,256]{1,0:T(8,128)(2,1)S(1)}, bf16[768,256]{1,0:T(8,128)(2,1)}, u32[]{:S(2)}, u32[]{:S(2)}) collective-permute-start(bf16[768,256]{1,0:T(8,128)(2,1)S(1)} %collective-permute-done.33.refs_7_.refs_4_), channel_id=1, source_target_pairs={{0,1},{1,0},{2,3},{3,2},{4,5},{5,4},{6,7},{7,6},{8,9},{9,8},{10,11... | collective-permute-start | bytes 1179656 | tf_op jit(solution)/shard_map/ppermute | solution.py:242
  147.5 22.5 %collective-permute-start.43 = (bf16[256,1024]{1,0:T(8,128)(2,1)}, bf16[256,1024]{1,0:T(8,128)(2,1)}, u32[]{:S(2)}, u32[]{:S(2)}) collective-permute-start(bf16[256,1024]{1,0:T(8,128)(2,1)} %get-tuple-element.379), channel_id=1, source_target_pairs={{0,8},{4,12},{8,0},{12,4},{16,24},{20,28},{24,16},{28,20},{1,9},{5... | collective-permute-start | bytes 1572872 | tf_op jit(solution)/shard_map/ppermute | solution.py:328
  148.2 10.3 %collective-permute-start.34 = (f32[8,128]{1,0:T(8,128)S(1)}, f32[8,128]{1,0:T(8,128)}, u32[]{:S(2)}, u32[]{:S(2)}) collective-permute-start(f32[8,128]{1,0:T(8,128)S(1)} %add.205), channel_id=1, source_target_pairs={{0,16},{4,20},{8,24},{12,28},{16,0},{20,4},{24,8},{28,12},{1,17},{... | collective-permute-start | bytes 12296 | tf_op jit(solution)/shard_map/ppermute | solution.py:365
  160.9 10.6 %collective-permute-start.44 = (bf16[128,1024]{1,0:T(8,128)(2,1)}, bf16[128,1024]{1,0:T(8,128)(2,1)}, u32[]{:S(2)}, u32[]{:S(2)}) collective-permute-start(bf16[128,1024]{1,0:T(8,128)(2,1)} %add_convert_fusion.3), channel_id=1, source_target_pairs={{0,8},{4,12},{8,0},{12,4},{16,24},{20,28},{24,16},{28,20},{1,9},{5... | collective-permute-start | bytes 786440 | tf_op jit(solution)/shard_map/ppermute | solution.py:328
  166.3 21.7 %collective-permute-start.45 = (bf16[192,1024]{1,0:T(8,128)(2,1)}, bf16[192,1024]{1,0:T(8,128)(2,1)}, u32[]{:S(2)}, u32[]{:S(2)}) collective-permute-start(bf16[192,1024]{1,0:T(8,128)(2,1)} %add_convert_fusion), channel_id=1, source_target_pairs={{0,16},{4,20},{8,24},{12,28},{16,0},{20,4},{24,8},{28,12},{1,17},{... | collective-permute-start | bytes 1179656 | tf_op jit(solution)/shard_map/ppermute | solution.py:328
  166.5 27.5 %collective-permute-start.47 = (bf16[256,1024]{1,0:T(8,128)(2,1)}, bf16[256,1024]{1,0:T(8,128)(2,1)S(1)}, u32[]{:S(2)}, u32[]{:S(2)}) collective-permute-start(bf16[256,1024]{1,0:T(8,128)(2,1)} %copy-done.18), channel_id=1, source_target_pairs={{0,4},{4,0},{8,12},{12,8},{16,20},{20,16},{24,28},{28,24},{1,5},{5... | collective-permute-start | bytes 1572872 | tf_op jit(solution)/shard_map/ppermute | solution.py:328
  169.4 9.2 %collective-permute-start.42 = (f32[8,128]{1,0:T(8,128)S(1)}, f32[8,128]{1,0:T(8,128)S(1)}, u32[]{:S(2)}, u32[]{:S(2)}) collective-permute-start(f32[8,128]{1,0:T(8,128)S(1)} %add.207), channel_id=1, source_target_pairs={{0,2},{1,3},{2,0},{3,1},{4,6},{5,7},{6,4},{7,5},{8,10},{9,11},{10,... | collective-permute-start | bytes 12296 | tf_op jit(solution)/shard_map/ppermute | solution.py:365
  172.6 20.2 %collective-permute-start.48 = (bf16[64,1024]{1,0:T(8,128)(2,1)S(1)}, bf16[64,1024]{1,0:T(8,128)(2,1)S(1)}, u32[]{:S(2)}, u32[]{:S(2)}) collective-permute-start(bf16[64,1024]{1,0:T(8,128)(2,1)S(1)} %add_convert_fusion.7), channel_id=1, source_target_pairs={{0,16},{4,20},{8,24},{12,28},{16,0},{20,4},{24,8},{28,12},{1,17},{... | collective-permute-start | bytes 393224 | tf_op jit(solution)/shard_map/ppermute | solution.py:328
  176.1 18.0 %collective-permute-start.46 = (bf16[128,1024]{1,0:T(8,128)(2,1)S(1)}, bf16[128,1024]{1,0:T(8,128)(2,1)S(1)}, u32[]{:S(2)}, u32[]{:S(2)}) collective-permute-start(bf16[128,1024]{1,0:T(8,128)(2,1)S(1)} %add_convert_fusion.2), channel_id=1, source_target_pairs={{0,4},{4,0},{8,12},{12,8},{16,20},{20,16},{24,28},{28,24},{1,5},{5... | collective-permute-start | bytes 786440 | tf_op jit(solution)/shard_map/ppermute | solution.py:328
  189.2 9.0 %collective-permute-start.49 = (bf16[96,1024]{1,0:T(8,128)(2,1)S(1)}, bf16[96,1024]{1,0:T(8,128)(2,1)S(1)}, u32[]{:S(2)}, u32[]{:S(2)}) collective-permute-start(bf16[96,1024]{1,0:T(8,128)(2,1)S(1)} %add_convert_fusion.4), channel_id=1, source_target_pairs={{0,4},{4,0},{8,12},{12,8},{16,20},{20,16},{24,28},{28,24},{1,5},{5... | collective-permute-start | bytes 589832 | tf_op jit(solution)/shard_map/ppermute | solution.py:328
  195.0 9.1 %collective-permute-start.50 = (bf16[64,1024]{1,0:T(8,128)(2,1)S(1)}, bf16[64,1024]{1,0:T(8,128)(2,1)S(1)}, u32[]{:S(2)}, u32[]{:S(2)}) collective-permute-start(bf16[64,1024]{1,0:T(8,128)(2,1)S(1)} %add_convert_fusion.6), channel_id=1, source_target_pairs={{0,16},{4,20},{8,24},{12,28},{16,0},{20,4},{24,8},{28,12},{1,17},{... | collective-permute-start | bytes 393224 | tf_op jit(solution)/shard_map/ppermute | solution.py:328
  198.0 14.1 %collective-permute-start.51 = (bf16[128,1024]{1,0:T(8,128)(2,1)S(1)}, bf16[128,1024]{1,0:T(8,128)(2,1)S(1)}, u32[]{:S(2)}, u32[]{:S(2)}) collective-permute-start(bf16[128,1024]{1,0:T(8,128)(2,1)S(1)} %add_convert_fusion.1), channel_id=1, source_target_pairs={{0,8},{4,12},{8,0},{12,4},{16,24},{20,28},{24,16},{28,20},{1,9},{5... | collective-permute-start | bytes 786440 | tf_op jit(solution)/shard_map/ppermute | solution.py:328
  202.0 14.7 %collective-permute-start.56 = (bf16[128,1024]{1,0:T(8,128)(2,1)S(1)}, bf16[128,1024]{1,0:T(8,128)(2,1)S(1)}, u32[]{:S(2)}, u32[]{:S(2)}) collective-permute-start(bf16[128,1024]{1,0:T(8,128)(2,1)S(1)} %pad_maximum_fusion.5), channel_id=1, source_target_pairs={{0,8},{4,12},{8,0},{12,4},{16,24},{20,28},{24,16},{28,20},{1,9},{5... | collective-permute-start | bytes 786440 | tf_op jit(solution)/shard_map/ppermute | solution.py:328
  205.1 9.3 %collective-permute-start.53 = (bf16[64,1024]{1,0:T(8,128)(2,1)S(1)}, bf16[64,1024]{1,0:T(8,128)(2,1)S(1)}, u32[]{:S(2)}, u32[]{:S(2)}) collective-permute-start(bf16[64,1024]{1,0:T(8,128)(2,1)S(1)} %divide_convert_fusion.2), channel_id=1, source_target_pairs={{0,16},{4,20},{8,24},{12,28},{16,0},{20,4},{24,8},{28,12},{1,17},{... | collective-permute-start | bytes 393224 | tf_op jit(solution)/shard_map/ppermute | solution.py:328
  213.5 19.2 %collective-permute-start.54 = (bf16[96,1024]{1,0:T(8,128)(2,1)S(1)}, bf16[96,1024]{1,0:T(8,128)(2,1)S(1)}, u32[]{:S(2)}, u32[]{:S(2)}) collective-permute-start(bf16[96,1024]{1,0:T(8,128)(2,1)S(1)} %divide_convert_fusion), channel_id=1, source_target_pairs={{0,4},{4,0},{8,12},{12,8},{16,20},{20,16},{24,28},{28,24},{1,5},{5... | collective-permute-start | bytes 589832 | tf_op jit(solution)/shard_map/ppermute | solution.py:328
  220.3 21.3 %collective-permute-start.59 = (bf16[256,1024]{1,0:T(8,128)(2,1)S(1)}, bf16[256,1024]{1,0:T(8,128)(2,1)S(1)}, u32[]{:S(2)}, u32[]{:S(2)}) collective-permute-start(bf16[256,1024]{1,0:T(8,128)(2,1)S(1)} %pad_maximum_fusion.1.refs_4_), channel_id=1, source_target_pairs={{0,4},{4,0},{8,12},{12,8},{16,20},{20,16},{24,28},{28,24},{1,5},{5... | collective-permute-start | bytes 1572872 | tf_op jit(solution)/shard_map/ppermute | solution.py:328
  222.6 16.9 %collective-permute-start.58 = (bf16[128,1024]{1,0:T(8,128)(2,1)S(1)}, bf16[128,1024]{1,0:T(8,128)(2,1)S(1)}, u32[]{:S(2)}, u32[]{:S(2)}) collective-permute-start(bf16[128,1024]{1,0:T(8,128)(2,1)S(1)} %pad_maximum_fusion.6), channel_id=1, source_target_pairs={{0,4},{4,0},{8,12},{12,8},{16,20},{20,16},{24,28},{28,24},{1,5},{5... | collective-permute-start | bytes 786440 | tf_op jit(solution)/shard_map/ppermute | solution.py:328
  228.1 12.8 %collective-permute-start.67 = (bf16[128,1024]{1,0:T(8,128)(2,1)S(1)}, bf16[128,1024]{1,0:T(8,128)(2,1)S(1)}, u32[]{:S(2)}, u32[]{:S(2)}) collective-permute-start(bf16[128,1024]{1,0:T(8,128)(2,1)S(1)} %pad_maximum_fusion.7), channel_id=1, source_target_pairs={{0,8},{4,12},{8,0},{12,4},{16,24},{20,28},{24,16},{28,20},{1,9},{5... | collective-permute-start | bytes 786440 | tf_op jit(solution)/shard_map/ppermute | solution.py:328
  232.8 13.6 %collective-permute-start.65 = (bf16[192,1024]{1,0:T(8,128)(2,1)S(1)}, bf16[192,1024]{1,0:T(8,128)(2,1)S(1)}, u32[]{:S(2)}, u32[]{:S(2)}) collective-permute-start(bf16[192,1024]{1,0:T(8,128)(2,1)S(1)} %pad_maximum_fusion.4), channel_id=1, source_target_pairs={{0,16},{4,20},{8,24},{12,28},{16,0},{20,4},{24,8},{28,12},{1,17},{... | collective-permute-start | bytes 1179656 | tf_op jit(solution)/shard_map/ppermute | solution.py:328
  236.2 20.6 %collective-permute-start.60 = (bf16[256,1024]{1,0:T(8,128)(2,1)S(1)}, bf16[256,1024]{1,0:T(8,128)(2,1)S(1)}, u32[]{:S(2)}, u32[]{:S(2)}) collective-permute-start(bf16[256,1024]{1,0:T(8,128)(2,1)S(1)} %pad_maximum_fusion.1.refs_4_), channel_id=1, source_target_pairs={{0,1},{1,0},{2,3},{3,2},{4,5},{5,4},{6,7},{7,6},{8,9},{9,8},{10,11... | collective-permute-start | bytes 1572872 | tf_op jit(solution)/shard_map/ppermute | solution.py:242
  239.6 16.7 %collective-permute-start.62 = (bf16[256,1024]{1,0:T(8,128)(2,1)S(1)}, bf16[256,1024]{1,0:T(8,128)(2,1)S(1)}, u32[]{:S(2)}, u32[]{:S(2)}) collective-permute-start(bf16[256,1024]{1,0:T(8,128)(2,1)S(1)} %pad_maximum_fusion.2.refs_5_), channel_id=1, source_target_pairs={{0,8},{4,12},{8,0},{12,4},{16,24},{20,28},{24,16},{28,20},{1,9},{5... | collective-permute-start | bytes 1572872 | tf_op jit(solution)/shard_map/ppermute | solution.py:328
  241.0 17.4 %collective-permute-start.68 = (bf16[256,1024]{1,0:T(8,128)(2,1)S(1)}, bf16[256,1024]{1,0:T(8,128)(2,1)S(1)}, u32[]{:S(2)}, u32[]{:S(2)}) collective-permute-start(bf16[256,1024]{1,0:T(8,128)(2,1)S(1)} %pad_maximum_fusion.3.refs_6_), channel_id=1, source_target_pairs={{0,4},{4,0},{8,12},{12,8},{16,20},{20,16},{24,28},{28,24},{1,5},{5... | collective-permute-start | bytes 1572872 | tf_op jit(solution)/shard_map/ppermute | solution.py:328
  241.6 16.8 %collective-permute-start.61 = (bf16[256,1024]{1,0:T(8,128)(2,1)S(1)}, bf16[256,1024]{1,0:T(8,128)(2,1)S(1)}, u32[]{:S(2)}, u32[]{:S(2)}) collective-permute-start(bf16[256,1024]{1,0:T(8,128)(2,1)S(1)} %collective-permute-done.59.refs_5_), channel_id=1, source_target_pairs={{0,1},{1,0},{2,3},{3,2},{4,5},{5,4},{6,7},{7,6},{8,9},{9,8},{10,11... | collective-permute-start | bytes 1572872 | tf_op jit(solution)/shard_map/ppermute | solution.py:242
  246.4 36.1 %collective-permute-start.66 = (bf16[384,1024]{1,0:T(8,128)(2,1)S(1)}, bf16[384,1024]{1,0:T(8,128)(2,1)S(1)}, u32[]{:S(2)}, u32[]{:S(2)}) collective-permute-start(bf16[384,1024]{1,0:T(8,128)(2,1)S(1)} %pad_maximum_fusion.refs_5_), channel_id=1, source_target_pairs={{0,8},{4,12},{8,0},{12,4},{16,24},{20,28},{24,16},{28,20},{1,9},{5... | collective-permute-start | bytes 2359304 | tf_op jit(solution)/shard_map/ppermute | solution.py:328
  256.3 14.9 %collective-permute-start.63 = (bf16[256,1024]{1,0:T(8,128)(2,1)S(1)}, bf16[256,1024]{1,0:T(8,128)(2,1)S(1)}, u32[]{:S(2)}, u32[]{:S(2)}) collective-permute-start(bf16[256,1024]{1,0:T(8,128)(2,1)S(1)} %pad_maximum_fusion.2.refs_5_), channel_id=1, source_target_pairs={{0,2},{1,3},{2,0},{3,1},{4,6},{5,7},{6,4},{7,5},{8,10},{9,11},{10,... | collective-permute-start | bytes 1572872 | tf_op jit(solution)/shard_map/ppermute | solution.py:242
  256.8 25.6 %collective-permute-start.64 = (bf16[256,1024]{1,0:T(8,128)(2,1)S(1)}, bf16[256,1024]{1,0:T(8,128)(2,1)S(1)}, u32[]{:S(2)}, u32[]{:S(2)}) collective-permute-start(bf16[256,1024]{1,0:T(8,128)(2,1)S(1)} %collective-permute-done.62.refs_6_), channel_id=1, source_target_pairs={{0,2},{1,3},{2,0},{3,1},{4,6},{5,7},{6,4},{7,5},{8,10},{9,11},{10,... | collective-permute-start | bytes 1572872 | tf_op jit(solution)/shard_map/ppermute | solution.py:242
  258.4 33.3 %collective-permute-start.69 = (bf16[256,1024]{1,0:T(8,128)(2,1)S(1)}, bf16[256,1024]{1,0:T(8,128)(2,1)S(1)}, u32[]{:S(2)}, u32[]{:S(2)}) collective-permute-start(bf16[256,1024]{1,0:T(8,128)(2,1)S(1)} %pad_maximum_fusion.3.refs_6_), channel_id=1, source_target_pairs={{0,3},{1,2},{2,1},{3,0},{4,7},{5,6},{6,5},{7,4},{8,11},{9,10},{10,... | collective-permute-start | bytes 1572872 | tf_op jit(solution)/shard_map/ppermute | solution.py:242
  258.4 39.7 %collective-permute-start.70 = (bf16[256,1024]{1,0:T(8,128)(2,1)S(1)}, bf16[256,1024]{1,0:T(8,128)(2,1)S(1)}, u32[]{:S(2)}, u32[]{:S(2)}) collective-permute-start(bf16[256,1024]{1,0:T(8,128)(2,1)S(1)} %collective-permute-done.68.refs_7_), channel_id=1, source_target_pairs={{0,3},{1,2},{2,1},{3,0},{4,7},{5,6},{6,5},{7,4},{8,11},{9,10},{10,... | collective-permute-start | bytes 1572872 | tf_op jit(solution)/shard_map/ppermute | solution.py:242
  (28 other events, 273.7 us)

commit v6 on v5

--- a/solution.py
+++ b/solution.py
@@ -10,7 +10,8 @@
 CHUNKS = 4
 F32 = jnp.float32
 BF16 = jnp.bfloat16
-VMEM_LIMIT = 48 * 1024 * 1024
+MIB = 1024 * 1024
+EXTRA = 16
 
 
 class Order:
@@ -78,16 +79,16 @@
             before_ref, half_ref = refs
             half_ref[here, :] = (2.0 * total - before_ref[here, :].astype(F32)).astype(BF16)
         else:
-            before_ref, half_ref, squares_ref = refs
+            before_ref, earlier_ref, half_ref, squares_ref = refs
             value = (2.0 * total - before_ref[here, :]).astype(BF16)
             half_ref[here, :] = value
             wide = value.astype(F32)
             squares += jnp.sum((wide * wide).reshape(-1, 8, width), axis=0)
     if stage == 2:
-        squares_ref[...] = squares
-
-
-def call(kernel, name, outs, scalars, args, scratch=(), aliases=None):
+        squares_ref[...] = earlier_ref[...] + squares
+
+
+def call(kernel, name, outs, scalars, args, scratch=(), aliases=None, vmem=16):
     return pl.pallas_call(
         kernel,
         out_shape=outs,
@@ -95,19 +96,19 @@
         + [pl.BlockSpec(memory_space=pltpu.VMEM)] * len(args),
         scratch_shapes=list(scratch),
         input_output_aliases=aliases or {},
-        compiler_params=pltpu.CompilerParams(vmem_limit_bytes=VMEM_LIMIT),
+        compiler_params=pltpu.CompilerParams(vmem_limit_bytes=vmem * MIB),
         cost_estimate=pl.CostEstimate(flops=1024, bytes_accessed=1024, transcendentals=0),
         name=name,
     )(*scalars, *args)
 
 
-def product(stage, place, blocks, field, by_near, by_far, before=None):
+def product(stage, place, blocks, field, by_near, by_far, *before):
     rows, width = field.shape
     half = jax.ShapeDtypeStruct((rows, width), BF16)
     wide = jax.ShapeDtypeStruct((rows, width), F32)
     squares = jax.ShapeDtypeStruct((8, width), F32)
     outs = ((wide, half), half, (half, squares))[stage]
-    args = (blocks, field, by_near, by_far) + (() if before is None else (before,))
+    args = (blocks, field, by_near, by_far, *before)
     kernel = functools.partial(product_kernel, stage)
     return call(kernel, f"product_{stage}", outs, (place,), args)
 
@@ -130,6 +131,15 @@
 TRANSPOSED_RIGHT = (((1,), (1,)), ((), ()))
 
 
+def extra_rows(value):
+    first = lax.reduce_precision(value, 8, 7)
+    second = lax.reduce_precision(value - first, 8, 7)
+    third = value - first - second
+    row = lax.broadcasted_iota(jnp.int32, (EXTRA, value.shape[1]), 0)
+    rows = jnp.where(row == 0, first, jnp.where(row == 1, second, jnp.where(row == 2, third, 0.0)))
+    return rows.astype(BF16)
+
+
 def side_by_side(refs):
     return jnp.concatenate([ref[...] for ref in refs], axis=1)
 
@@ -138,6 +148,10 @@
     mine_ref, other_ref, whole = refs[-3:]
     fields = refs[:CHUNKS]
     half = whole.shape[0] // 2
+    if mine_ref.shape[0] > half:
+        carried = extra_rows(jnp.full((1, whole.shape[1]), jnp.sum(refs[2 * CHUNKS][...])))
+        mine_ref[half:, :] = carried
+        other_ref[half:, :] = carried
     width = fields[0].shape[1]
     middle = CHUNKS * width // 2
     side = lax.rem(where_ref[0] // mask, 2)
@@ -167,8 +181,8 @@
         whole[middle:used, middle:] = corner[middle // 2 :]
     if used < whole.shape[0]:
         whole[used:, :] = jnp.zeros((whole.shape[0] - used, whole.shape[1]), BF16)
-    mine_ref[...] = whole[pl.ds(pl.multiple_of(side * half, half), half), :]
-    other_ref[...] = whole[pl.ds(pl.multiple_of((1 - side) * half, half), half), :]
+    mine_ref[:half, :] = whole[pl.ds(pl.multiple_of(side * half, half), half), :]
+    other_ref[:half, :] = whole[pl.ds(pl.multiple_of((1 - side) * half, half), half), :]
 
 
 def mix_kernel(pair, masks, first, last, where_ref, *refs):
@@ -261,7 +275,7 @@
 
     jobs = [(stage, c) for stage in range(3) for c in range(CHUNKS)]
     far = {}
-    firsts, squares, pieces = {}, [], [{} for _ in range(CHUNKS)]
+    firsts, squares, pieces = {}, jnp.zeros((8, width), F32), [{} for _ in range(CHUNKS)]
     current = {(0, c): start[c] for c in range(CHUNKS)}
 
     def send_on(job):
@@ -277,17 +291,17 @@
                     pieces[c][d] = to_group(pieces[c][d ^ low], low)
 
     def multiply(job):
+        nonlocal squares
         stage, c = job
         far[job] = order(far[job])
-        old = (None, start[c], firsts.get(c))[stage]
-        out = product(stage, place, blocks, current[job], near[job], far[job], old)
+        old = ((), (start[c],), (firsts.get(c), squares))[stage]
+        out = product(stage, place, blocks, current[job], near[job], far[job], *old)
         if stage == 0:
             firsts[c], out = order(*out)
         elif stage == 1:
             out = order(out)
         else:
-            out, square = order(*out)
-            squares.append(square)
+            out, squares = order(*out)
             pieces[c][0] = out
             bit = groups // 2
             while bit:
@@ -305,7 +319,6 @@
             multiply(jobs[index - 1])
     multiply(jobs[-1])
 
-    squares = sum(squares)
     rows_total = rows * tiles
     level = None
     middle = columns // 2
@@ -314,6 +327,7 @@
     z_masks = [2 << i for i in range(lines.bit_length() - 1)]
     there = {d: 3.0 if d == 1 else 10.5 for d in range(1, groups)}
     mixed, mixes = None, 0
+    squares_ready = False
 
     def is_upper(d):
         return (my_group & (1 << (d.bit_length() - 1))) != 0
@@ -342,41 +356,47 @@
             if d & (d - 1):
                 there[d] = clock.now + 3.5
 
-    def gram_chunk(d, mask):
+    def gram_chunk(d, mask, extra):
         height = middle if d else middle + middle // 2
         height += -height % unit
         fields = all_chunks(0)
         if d:
-            fields += order(*all_chunks(d))
-        half = jax.ShapeDtypeStruct((height // 2, columns), BF16)
+            fields += list(order(*all_chunks(d)))
+        if extra:
+            fields.append(squares)
+        half = jax.ShapeDtypeStruct((height // 2 + extra, columns), BF16)
         scratch = (pltpu.VMEM((height, columns), BF16),)
         name = "gram_pair" if d else "gram_own"
         clock.spend(3.2 if d else 3.0)
         return call(functools.partial(gram_kernel, d > 0, mask), name, (half, half), (where(d),), fields, scratch)
 
     def level_process():
-        nonlocal level
-        yield 4.0
-        total = jnp.full((8, 128), jnp.sum(squares), F32)
-        for axis, peers in (("elem", tiles), ("orb", groups)):
-            bit = 1
-            while bit < peers:
-                total = order(total)
-                other = lax.ppermute(total, axis, [(i, i ^ bit) for i in range(peers)])
-                clock.spend(1.5)
-                yield clock.now + 3.5
-                total = total + order(other)
-                clock.spend(0.6)
-                bit *= 2
-        level = total[0, 0] / (columns * groups * rows_total)
-
-    def process(d, masks):
-        nonlocal mixed, mixes
-        while d and (d not in pieces[-1] or there[d] > clock.now):
+        nonlocal squares
+        bit = 1
+        while bit < groups:
+            other = to_group(order(squares), bit)
+            clock.spend(1.5)
+            yield clock.now + (2.5 if bit == 1 else 7.0)
+            squares = squares + order(other)
+            clock.spend(0.6)
+            bit *= 2
+        nonlocal squares_ready
+        squares_ready = True
+
+    def process(d, masks, extra=0):
+        nonlocal mixed, mixes, level
+        while d and (d not in pieces[-1] or there[d] > clock.now or extra and not squares_ready):
             yield max(there[d], clock.now + 0.5)
-        mine, value = order(*gram_chunk(d, masks[0]))
+        mine, value = order(*gram_chunk(d, masks[0], extra))
         terms = [(mine, 0)]
-        height, offset = mine.shape[0], 0
+        height, offset = mine.shape[0] - extra, 0
+
+        def carried(value):
+            rows = lax.slice_in_dim(value, value.shape[0] - extra, value.shape[0], axis=0)
+            return jnp.sum(rows.astype(F32), axis=0, keepdims=True)
+
+        if extra:
+            total = carried(mine)
 
         def added(first_row, count):
             clock.spend(1.0)
@@ -387,10 +407,18 @@
                 height //= 2
                 keep = (my_tile // mask) % 2
                 value = added(offset + (1 - keep) * height, height).astype(BF16)
+                if extra:
+                    value = jnp.concatenate([value, extra_rows(total)], axis=0)
+                    clock.spend(1.0)
                 offset = offset + keep * height
             received, arrival = over_tiles(value, mask)
-            yield arrival
-            terms.append((order(received), offset))
+            yield arrival if i or mask > 1 else arrival - 3.0
+            received = order(received)
+            terms.append((received, offset))
+            if extra:
+                total = total + carried(received)
+        if extra:
+            level = total[0, 0] / (columns * groups * rows_total)
         while level is None:
             yield clock.now + 0.5
         part = (added(offset, height) / (level * rows_total)).astype(BF16)
@@ -425,14 +453,14 @@
         kernel = functools.partial(mix_kernel, d > 0, masks, first, last)
         name = "mix_pair" if d else "mix_own"
         clock.spend(5.7 if d else 4.5)
-        mixed = call(kernel, name, shape, scalars, args, scratch, {} if first or last else {1: 0})
+        mixed = call(kernel, name, shape, scalars, args, scratch, {} if first or last else {1: 0}, 28)
         if not last:
             mixed = order(mixed)
 
     y_first, z_first, z_then_y = (1, *z_masks), (*z_masks, 1), (*z_masks[:1], 1, *z_masks[1:])
     queue = sorted(range(1, groups), key=lambda d: (d == 1, d))
     processes = [panel_process(), level_process(), process(0, z_first)]
-    processes += [process(d, z_then_y if i == 0 else y_first) for i, d in enumerate(queue)]
+    processes += [process(d, z_then_y if i == 0 else y_first, 0 if i else EXTRA) for i, d in enumerate(queue)]
     clock.run(processes)
     return mixed
 

time: 307 us -> 308 us (level)
  waiting for transfers between devices: 115 us -> 136 us
  starting transfers between devices: 110 us -> 95.9 us
  Pallas kernels: 47.9 us -> 38.9 us
  other arithmetic: 14.9 us -> 22.5 us
    ppermute x18 -> x20, waiting for transfers between devices: 21.2 us -> 34.2 us  [to_group(): return lax.ppermute(value, 'orb', [(i, i ^ d) for i in range(groups)])]
    ppermute x24, waiting for transfers between devices: 51.7 us -> 61.6 us  [over_tiles(): sent = lax.ppermute(value, 'elem', [(i, i ^ mask) for i in range(tiles)])]
    pallas_call x20, Pallas kernels: 47.9 us -> 38.9 us  [call(): pl.pallas_call(kernel, out_shape=outs, in_specs=[pl.BlockSpec(memory_spac...]
    ppermute x5 -> x0, waiting for transfers between devices: 8.81 us -> none  [level_process(): other = lax.ppermute(total, axis, [(i, i ^ bit) for i in range(peers)])]
    ppermute x12, waiting for transfers between devices: 9.16 us -> 15.5 us  [send_on(): far[job] = lax.ppermute(near[job], 'elem', outward)]
    ppermute x5 -> x0, starting transfers between devices: 6.31 us -> none  [level_process(): other = lax.ppermute(total, axis, [(i, i ^ bit) for i in range(peers)])]
    ppermute x8, starting transfers between devices: 27.7 us -> 23.8 us  [multiply(): near[stage + 1, c] = lax.ppermute(out, 'elem', swap)]
    ppermute x24, starting transfers between devices: 33.3 us -> 29.6 us  [over_tiles(): sent = lax.ppermute(value, 'elem', [(i, i ^ mask) for i in range(tiles)])]
  transfers between devices with their start and end apart: 71 -> 68, of which waited for: 34 -> 34; matrix products, arithmetic and copies ran while one was open for 6% -> 8% of each run, Pallas kernels for 14% -> 11%
where the time goes in v6:
time: 308 us; the launch traced here: 305 us
  waiting for transfers between devices  136 us (44%)
  starting transfers between devices  95.9 us (31%)
  Pallas kernels  38.9 us (13%)
  other arithmetic  22.5 us (7%)
  local copies, waits for them, and re-layouts  10.3 us (3%)
    ppermute x24, waiting for transfers between devices, over_tiles(): sent = lax.ppermute(value, 'elem', [(i, i ^ mask) for i in range(tiles)])  61.6 us
    pallas_call x20, Pallas kernels, call(): pl.pallas_call(kernel, out_shape=outs, in_specs=[pl.BlockSpec(memory_spac...  38.9 us
    ppermute x20, waiting for transfers between devices, to_group(): return lax.ppermute(value, 'orb', [(i, i ^ d) for i in range(groups)])  34.2 us
    ppermute x24, starting transfers between devices, over_tiles(): sent = lax.ppermute(value, 'elem', [(i, i ^ mask) for i in range(tiles)])  29.6 us
    ppermute x12, starting transfers between devices, send_on(): far[job] = lax.ppermute(near[job], 'elem', outward)  24 us
    ppermute x8, starting transfers between devices, multiply(): near[stage + 1, c] = lax.ppermute(out, 'elem', swap)  23.8 us
    ppermute x12, waiting for transfers between devices, send_on(): far[job] = lax.ppermute(near[job], 'elem', outward)  15.5 us
    ppermute x20, starting transfers between devices, to_group(): return lax.ppermute(value, 'orb', [(i, i ^ d) for i in range(groups)])  11.7 us
  transfers between devices with their start and end apart: 68, of which 34 were waited for; matrix products, arithmetic and copies ran while one was open for 8% of the time, Pallas kernels for 11%

profile of v6, /device:TPU:0, one launch (start us, length us, event | category | flops | bytes accessed | tf_op | source)
XLA Modules:
  0.0 305.5 jit_solution(15419502829359570775)
XLA Ops:
  1.6 3.0 collective-permute-start
  6.7 2.4 concatenate.40.blocks_ref
  9.4 5.1 %collective-permute-done.near_ref = bf16[768,256]{1,0:T(8,128)(2,1)S(1)} collective-permute-done((bf16[768,256]{1,0:T(8,128)(2,1)S(1)}, bf16[768,256]{1,0:T(8,128)(2,1)S(1)}, u32[]{:S(2)}, u32[]{:S(2)}) %collective-permute-start) | collective-permute-done | bytes 393248 | tf_op jit(solution)/shard_map/ppermute | solution.py:269
  14.6 2.1 collective-permute-start.1
  16.7 3.5 %collective-permute-start.4 = (bf16[768,256]{1,0:T(8,128)(2,1)S(1)}, bf16[768,256]{1,0:T(8,128)(2,1)S(1)}, u32[]{:S(2)}, u32[]{:S(2)}) collective-permute-start(bf16[768,256]{1,0:T(8,128)(2,1)S(1)} %get-tuple-element.221.field_ref.refs_0_), channel_id=1, source_target_pairs={{0,4},{4,0},{8,12},{12,8},{16,20},{20,16},{24,28},{28,24},{1,5},{5... | collective-permute-start | bytes 1179656 | tf_op jit(solution)/shard_map/ppermute | solution.py:274
  20.3 2.7 collective-permute-done.2.near_ref
  23.0 2.1 collective-permute-start.7
  27.1 4.3 %collective-permute-done.4.near_ref = bf16[768,256]{1,0:T(8,128)(2,1)S(1)} collective-permute-done((bf16[768,256]{1,0:T(8,128)(2,1)S(1)}, bf16[768,256]{1,0:T(8,128)(2,1)S(1)}, u32[]{:S(2)}, u32[]{:S(2)}) %collective-permute-start.4) | collective-permute-done | bytes 393248 | tf_op jit(solution)/shard_map/ppermute | solution.py:274
  31.4 2.1 collective-permute-start.5
  33.5 3.5 %collective-permute-start.3 = (bf16[768,256]{1,0:T(8,128)(2,1)S(1)}, bf16[768,256]{1,0:T(8,128)(2,1)S(1)}, u32[]{:S(2)}, u32[]{:S(2)}) collective-permute-start(bf16[768,256]{1,0:T(8,128)(2,1)S(1)} %get-tuple-element.220.field_ref), channel_id=1, source_target_pairs={{0,4},{4,0},{8,12},{12,8},{16,20},{20,16},{24,28},{28,24},{1,5},{5... | collective-permute-start | bytes 1179656 | tf_op jit(solution)/shard_map/ppermute | solution.py:314
  39.9 2.1 collective-permute-start.10
  42.0 3.5 %collective-permute-start.9 = (bf16[768,256]{1,0:T(8,128)(2,1)S(1)}, bf16[768,256]{1,0:T(8,128)(2,1)S(1)}, u32[]{:S(2)}, u32[]{:S(2)}) collective-permute-start(bf16[768,256]{1,0:T(8,128)(2,1)S(1)} %get-tuple-element.239.field_ref), channel_id=1, source_target_pairs={{0,4},{4,0},{8,12},{12,8},{16,20},{20,16},{24,28},{28,24},{1,5},{5... | collective-permute-start | bytes 1179656 | tf_op jit(solution)/shard_map/ppermute | solution.py:314
  48.3 2.1 collective-permute-start.8
  50.4 3.5 %collective-permute-start.12 = (bf16[768,256]{1,0:T(8,128)(2,1)S(1)}, bf16[768,256]{1,0:T(8,128)(2,1)S(1)}, u32[]{:S(2)}, u32[]{:S(2)}) collective-permute-start(bf16[768,256]{1,0:T(8,128)(2,1)S(1)} %get-tuple-element.251.field_ref), channel_id=1, source_target_pairs={{0,4},{4,0},{8,12},{12,8},{16,20},{20,16},{24,28},{28,24},{1,5},{5... | collective-permute-start | bytes 1179656 | tf_op jit(solution)/shard_map/ppermute | solution.py:314
  56.7 2.1 collective-permute-start.15
  58.8 3.5 %collective-permute-start.14 = (bf16[768,256]{1,0:T(8,128)(2,1)S(1)}, bf16[768,256]{1,0:T(8,128)(2,1)S(1)}, u32[]{:S(2)}, u32[]{:S(2)}) collective-permute-start(bf16[768,256]{1,0:T(8,128)(2,1)S(1)} %get-tuple-element.254.field_ref), channel_id=1, source_target_pairs={{0,4},{4,0},{8,12},{12,8},{16,20},{20,16},{24,28},{28,24},{1,5},{5... | collective-permute-start | bytes 1179656 | tf_op jit(solution)/shard_map/ppermute | solution.py:314
  65.1 2.1 collective-permute-start.13
  67.2 3.5 %collective-permute-start.11 = (bf16[768,256]{1,0:T(8,128)(2,1)S(1)}, bf16[768,256]{1,0:T(8,128)(2,1)S(1)}, u32[]{:S(2)}, u32[]{:S(2)}) collective-permute-start(bf16[768,256]{1,0:T(8,128)(2,1)S(1)} %product_1.4.field_ref), channel_id=1, source_target_pairs={{0,4},{4,0},{8,12},{12,8},{16,20},{20,16},{24,28},{28,24},{1,5},{5... | collective-permute-start | bytes 1179656 | tf_op jit(solution)/shard_map/ppermute | solution.py:314
  73.6 2.1 collective-permute-start.17
  78.5 3.5 %collective-permute-done.11.near_ref = bf16[768,256]{1,0:T(8,128)(2,1)S(1)} collective-permute-done((bf16[768,256]{1,0:T(8,128)(2,1)S(1)}, bf16[768,256]{1,0:T(8,128)(2,1)S(1)}, u32[]{:S(2)}, u32[]{:S(2)}) %collective-permute-start.11) | collective-permute-done | bytes 393248 | tf_op jit(solution)/shard_map/ppermute | solution.py:314
  82.0 2.1 collective-permute-start.16
  84.1 3.5 %collective-permute-start.20 = (bf16[768,256]{1,0:T(8,128)(2,1)S(1)}, bf16[768,256]{1,0:T(8,128)(2,1)S(1)}, u32[]{:S(2)}, u32[]{:S(2)}) collective-permute-start(bf16[768,256]{1,0:T(8,128)(2,1)S(1)} %product_1.6.field_ref), channel_id=1, source_target_pairs={{0,4},{4,0},{8,12},{12,8},{16,20},{20,16},{24,28},{28,24},{1,5},{5... | collective-permute-start | bytes 1179656 | tf_op jit(solution)/shard_map/ppermute | solution.py:314
  90.4 2.1 collective-permute-start.19
  92.5 3.1 %collective-permute-done.16.far_ref = bf16[768,256]{1,0:T(8,128)(2,1)S(1)} collective-permute-done((bf16[768,256]{1,0:T(8,128)(2,1)S(1)}, bf16[768,256]{1,0:T(8,128)(2,1)S(1)}, u32[]{:S(2)}, u32[]{:S(2)}) %collective-permute-start.16) | collective-permute-done | bytes 393248 | tf_op jit(solution)/shard_map/ppermute | solution.py:283
  98.9 2.0 collective-permute-start.21
  101.0 3.1 %collective-permute-done.19.far_ref = bf16[768,256]{1,0:T(8,128)(2,1)S(1)} collective-permute-done((bf16[768,256]{1,0:T(8,128)(2,1)S(1)}, bf16[768,256]{1,0:T(8,128)(2,1)S(1)}, u32[]{:S(2)}, u32[]{:S(2)}) %collective-permute-start.19) | collective-permute-done | bytes 393248 | tf_op jit(solution)/shard_map/ppermute | solution.py:283
  108.2 4.8 %collective-permute-done.21.far_ref = bf16[768,256]{1,0:T(8,128)(2,1)S(1)} collective-permute-done((bf16[768,256]{1,0:T(8,128)(2,1)S(1)}, bf16[768,256]{1,0:T(8,128)(2,1)S(1)}, u32[]{:S(2)}, u32[]{:S(2)}) %collective-permute-start.21) | collective-permute-done | bytes 393248 | tf_op jit(solution)/shard_map/ppermute | solution.py:283
  115.9 3.9 %collective-permute-done.24.far_ref = bf16[768,256]{1,0:T(8,128)(2,1)S(1)} collective-permute-done((bf16[768,256]{1,0:T(8,128)(2,1)S(1)}, bf16[768,256]{1,0:T(8,128)(2,1)S(1)}, u32[]{:S(2)}, u32[]{:S(2)}) %collective-permute-start.24) | collective-permute-done | bytes 393248 | tf_op jit(solution)/shard_map/ppermute | solution.py:283
  125.5 3.0 gram_own.1
  130.7 3.2 %gram_pair.3 = (bf16[256,1024]{1,0:T(8,128)(2,1)S(1)}, bf16[256,1024]{1,0:T(8,128)(2,1)}) custom-call(s32[2]{0:T(128)S(1)} %pad_add_fusion.2.where_ref, bf16[768,256]{1,0:T(8,128)(2,1)S(1)} %get-tuple-element.277.refs_0_.refs_1_.refs_10_, bf16[768,256]{1,0:T(8,128)(2,1)S(1)} %get-tuple-element.288.refs_1_.refs_2_.refs_11_, ...), custom_call_target="tpu_custom_call" | custom-call | flops 1024 | bytes 1024 | tf_op jit(solution)/shard_map/gram_pair/pallas_call | solution.py:92
  135.6 2.9 collective-permute-done.33
  140.8 1.8 gram_pair.4
  142.6 2.1 collective-permute-start.34
  144.7 2.3 gram_pair.5
  148.2 6.0 %collective-permute-done.41 = bf16[256,1024]{1,0:T(8,128)(2,1)} collective-permute-done((bf16[256,1024]{1,0:T(8,128)(2,1)}, bf16[256,1024]{1,0:T(8,128)(2,1)}, u32[]{:S(2)}, u32[]{:S(2)}) %collective-permute-start.41) | collective-permute-done | bytes 524320 | tf_op jit(solution)/shard_map/ppermute | solution.py:342
  154.2 1.7 add_convert_fusion.2
  155.9 2.0 collective-permute-start.43
  157.9 1.9 add_convert_fusion
  160.6 3.4 %collective-permute-done.39 = bf16[256,1024]{1,0:T(8,128)(2,1)S(1)} collective-permute-done((bf16[256,1024]{1,0:T(8,128)(2,1)S(1)}, bf16[256,1024]{1,0:T(8,128)(2,1)S(1)}, u32[]{:S(2)}, u32[]{:S(2)}) %collective-permute-start.39) | collective-permute-done | bytes 524320 | tf_op jit(solution)/shard_map/ppermute | solution.py:342
  164.0 3.9 %collective-permute-done.34 = bf16[272,1024]{1,0:T(8,128)(2,1)S(1)} collective-permute-done((bf16[272,1024]{1,0:T(8,128)(2,1)S(1)}, bf16[272,1024]{1,0:T(8,128)(2,1)S(1)}, u32[]{:S(2)}, u32[]{:S(2)}) %collective-permute-start.34) | collective-permute-done | bytes 557088 | tf_op jit(solution)/shard_map/ppermute | solution.py:342
  171.4 2.2 collective-permute-done.43
  175.4 2.9 collective-permute-done.45
  178.3 1.9 add_convert_fusion.4
  180.7 2.4 collective-permute-done.48
  188.1 2.9 collective-permute-start.52
  191.0 8.7 %collective-permute-done.52 = bf16[64,1024]{1,0:T(8,128)(2,1)} collective-permute-done((bf16[64,1024]{1,0:T(8,128)(2,1)}, bf16[64,1024]{1,0:T(8,128)(2,1)}, u32[]{:S(2)}, u32[]{:S(2)}) %collective-permute-start.52) | collective-permute-done | bytes 131104 | tf_op jit(solution)/shard_map/ppermute | solution.py:342
  204.9 3.0 collective-permute-start.51
  207.8 6.2 %collective-permute-done.49 = bf16[64,1024]{1,0:T(8,128)(2,1)S(1)} collective-permute-done((bf16[64,1024]{1,0:T(8,128)(2,1)S(1)}, bf16[64,1024]{1,0:T(8,128)(2,1)S(1)}, u32[]{:S(2)}, u32[]{:S(2)}) %collective-permute-start.49) | collective-permute-done | bytes 131104 | tf_op jit(solution)/shard_map/ppermute | solution.py:342
  215.5 2.0 collective-permute-start.50
  218.7 2.6 collective-permute-start.54
  222.5 3.8 %collective-permute-start.56 = (bf16[256,1024]{1,0:T(8,128)(2,1)S(1)}, bf16[256,1024]{1,0:T(8,128)(2,1)S(1)}, u32[]{:S(2)}, u32[]{:S(2)}) collective-permute-start(bf16[256,1024]{1,0:T(8,128)(2,1)S(1)} %pad_maximum_fusion.1.refs_4_), channel_id=1, source_target_pairs={{0,4},{4,0},{8,12},{12,8},{16,20},{20,16},{24,28},{28,24},{1,5},{5... | collective-permute-start | bytes 1572872 | tf_op jit(solution)/shard_map/ppermute | solution.py:342
  226.9 2.7 collective-permute-start.60
  229.6 12.8 %collective-permute-done.55 = bf16[128,1024]{1,0:T(8,128)(2,1)S(1)} collective-permute-done((bf16[128,1024]{1,0:T(8,128)(2,1)S(1)}, bf16[128,1024]{1,0:T(8,128)(2,1)S(1)}, u32[]{:S(2)}, u32[]{:S(2)}) %collective-permute-start.55) | collective-permute-done | bytes 262176 | tf_op jit(solution)/shard_map/ppermute | solution.py:342
  242.6 1.8 collective-permute-start.65
  246.5 10.9 %collective-permute-done.59.refs_6_ = bf16[256,1024]{1,0:T(8,128)(2,1)S(1)} collective-permute-done((bf16[256,1024]{1,0:T(8,128)(2,1)S(1)}, bf16[256,1024]{1,0:T(8,128)(2,1)S(1)}, u32[]{:S(2)}, u32[]{:S(2)}) %collective-permute-start.59) | collective-permute-done | bytes 524320 | tf_op jit(solution)/shard_map/ppermute | solution.py:342
  257.4 2.0 collective-permute-start.62
  261.9 10.4 %collective-permute-done.61.refs_7_ = bf16[256,1024]{1,0:T(8,128)(2,1)S(1)} collective-permute-done((bf16[256,1024]{1,0:T(8,128)(2,1)S(1)}, bf16[256,1024]{1,0:T(8,128)(2,1)S(1)}, u32[]{:S(2)}, u32[]{:S(2)}) %collective-permute-start.61) | collective-permute-done | bytes 524320 | tf_op jit(solution)/shard_map/ppermute | solution.py:256
  272.3 3.1 %mix_pair.3.refs_0_ = f32[768,1024]{1,0:T(8,128)S(1)} custom-call(s32[2]{0:T(128)S(1)} %pad_add_fusion.2.where_ref, bf16[768,256]{1,0:T(8,128)(2,1)S(1)} %copy-done.2, bf16[768,256]{1,0:T(8,128)(2,1)S(1)} %copy-done.5, bf16[768,256]{1,0:T(8,128)(2,1)} %collective-permute-done.30.refs_6_.refs_2_, bf16[768,256]{1,0:T(8,128)(2,1)} %collective-permute-done.31.refs_7_.refs_3_, ...), custom_call_target="tpu_custom_call" | custom-call | flops 1024 | bytes 1024 | tf_op jit(solution)/shard_map/mix_pair/pallas_call | solution.py:92
  275.4 8.1 %collective-permute-done.62.refs_8_ = bf16[256,1024]{1,0:T(8,128)(2,1)S(1)} collective-permute-done((bf16[256,1024]{1,0:T(8,128)(2,1)S(1)}, bf16[256,1024]{1,0:T(8,128)(2,1)S(1)}, u32[]{:S(2)}, u32[]{:S(2)}) %collective-permute-start.62) | collective-permute-done | bytes 524320 | tf_op jit(solution)/shard_map/ppermute | solution.py:256
  283.5 2.9 mix_pair.4.refs_0_
  286.4 5.8 %collective-permute-done.66.refs_8_ = bf16[256,1024]{1,0:T(8,128)(2,1)S(1)} collective-permute-done((bf16[256,1024]{1,0:T(8,128)(2,1)S(1)}, bf16[256,1024]{1,0:T(8,128)(2,1)S(1)}, u32[]{:S(2)}, u32[]{:S(2)}) %collective-permute-start.66) | collective-permute-done | bytes 524320 | tf_op jit(solution)/shard_map/ppermute | solution.py:256
  292.2 2.6 mix_own.1.refs_1_
  294.9 5.9 %collective-permute-done.67.refs_9_ = bf16[256,1024]{1,0:T(8,128)(2,1)S(1)} collective-permute-done((bf16[256,1024]{1,0:T(8,128)(2,1)S(1)}, bf16[256,1024]{1,0:T(8,128)(2,1)S(1)}, u32[]{:S(2)}, u32[]{:S(2)}) %collective-permute-start.67) | collective-permute-done | bytes 524320 | tf_op jit(solution)/shard_map/ppermute | solution.py:256
  300.8 4.7 %mix_pair.5 = bf16[768,1024]{1,0:T(8,128)(2,1)} custom-call(s32[2]{0:T(128)S(1)} %pad_add_fusion.1.where_ref, f32[1]{0:T(128)} %bitcast.12.refs_0_, f32[768,1024]{1,0:T(8,128)S(1)} %mix_own.1.refs_1_, bf16[768,256]{1,0:T(8,128)(2,1)S(1)} %collective-permute-done.35.refs_4_.refs_2_, bf16[768,256]{1,0:T(8,128)(2,1)} %collective-permute-done.36.refs_5_.refs_3_, ...), custom_call_target="tpu_custom_call" | custom-call | flops 1024 | bytes 1024 | tf_op jit(solution)/shard_map/mix_pair/pallas_call | solution.py:92
  (195 shorter events, 73.1 us)
Async XLA Ops:
  1.6 13.0 %collective-permute-start = (bf16[768,256]{1,0:T(8,128)(2,1)S(1)}, bf16[768,256]{1,0:T(8,128)(2,1)S(1)}, u32[]{:S(2)}, u32[]{:S(2)}) collective-permute-start(bf16[768,256]{1,0:T(8,128)(2,1)S(1)} %get-tuple-element.413.field_ref.refs_0_), channel_id=1, source_target_pairs={{0,4},{4,0},{8,12},{12,8},{16,20},{20,16},{24,28},{28,24},{1,5},{5... | collective-permute-start | bytes 1179656 | tf_op jit(solution)/shard_map/ppermute | solution.py:269
  9.3 13.7 %collective-permute-start.2 = (bf16[768,256]{1,0:T(8,128)(2,1)S(1)}, bf16[768,256]{1,0:T(8,128)(2,1)S(1)}, u32[]{:S(2)}, u32[]{:S(2)}) collective-permute-start(bf16[768,256]{1,0:T(8,128)(2,1)S(1)} %get-tuple-element.213.field_ref.refs_0_), channel_id=1, source_target_pairs={{0,4},{4,0},{8,12},{12,8},{16,20},{20,16},{24,28},{28,24},{1,5},{5... | collective-permute-start | bytes 1179656 | tf_op jit(solution)/shard_map/ppermute | solution.py:274
  14.6 11.3 %collective-permute-start.1 = (bf16[768,256]{1,0:T(8,128)(2,1)S(1)}, bf16[768,256]{1,0:T(8,128)(2,1)S(1)}, u32[]{:S(2)}, u32[]{:S(2)}) collective-permute-start(bf16[768,256]{1,0:T(8,128)(2,1)S(1)} %collective-permute-done.near_ref), channel_id=1, source_target_pairs={{0,8},{4,28},{8,16},{12,4},{16,24},{20,12},{24,0},{28,20},{1,9},{5... | collective-permute-start | bytes 1179656 | tf_op jit(solution)/shard_map/ppermute | solution.py:283
  16.7 14.7 %collective-permute-start.4 = (bf16[768,256]{1,0:T(8,128)(2,1)S(1)}, bf16[768,256]{1,0:T(8,128)(2,1)S(1)}, u32[]{:S(2)}, u32[]{:S(2)}) collective-permute-start(bf16[768,256]{1,0:T(8,128)(2,1)S(1)} %get-tuple-element.221.field_ref.refs_0_), channel_id=1, source_target_pairs={{0,4},{4,0},{8,12},{12,8},{16,20},{20,16},{24,28},{28,24},{1,5},{5... | collective-permute-start | bytes 1179656 | tf_op jit(solution)/shard_map/ppermute | solution.py:274
  20.2 19.6 %collective-permute-start.6 = (bf16[768,256]{1,0:T(8,128)(2,1)S(1)}, bf16[768,256]{1,0:T(8,128)(2,1)S(1)}, u32[]{:S(2)}, u32[]{:S(2)}) collective-permute-start(bf16[768,256]{1,0:T(8,128)(2,1)S(1)} %get-tuple-element.224.field_ref.refs_0_), channel_id=1, source_target_pairs={{0,4},{4,0},{8,12},{12,8},{16,20},{20,16},{24,28},{28,24},{1,5},{5... | collective-permute-start | bytes 1179656 | tf_op jit(solution)/shard_map/ppermute | solution.py:274
  23.0 14.1 %collective-permute-start.7 = (bf16[768,256]{1,0:T(8,128)(2,1)S(1)}, bf16[768,256]{1,0:T(8,128)(2,1)S(1)}, u32[]{:S(2)}, u32[]{:S(2)}) collective-permute-start(bf16[768,256]{1,0:T(8,128)(2,1)S(1)} %collective-permute-done.2.near_ref), channel_id=1, source_target_pairs={{0,8},{4,28},{8,16},{12,4},{16,24},{20,12},{24,0},{28,20},{1,9},{5... | collective-permute-start | bytes 1179656 | tf_op jit(solution)/shard_map/ppermute | solution.py:283
  31.4 14.1 %collective-permute-start.5 = (bf16[768,256]{1,0:T(8,128)(2,1)S(1)}, bf16[768,256]{1,0:T(8,128)(2,1)S(1)}, u32[]{:S(2)}, u32[]{:S(2)}) collective-permute-start(bf16[768,256]{1,0:T(8,128)(2,1)S(1)} %collective-permute-done.4.near_ref), channel_id=1, source_target_pairs={{0,8},{4,28},{8,16},{12,4},{16,24},{20,12},{24,0},{28,20},{1,9},{5... | collective-permute-start | bytes 1179656 | tf_op jit(solution)/shard_map/ppermute | solution.py:283
  33.5 14.7 %collective-permute-start.3 = (bf16[768,256]{1,0:T(8,128)(2,1)S(1)}, bf16[768,256]{1,0:T(8,128)(2,1)S(1)}, u32[]{:S(2)}, u32[]{:S(2)}) collective-permute-start(bf16[768,256]{1,0:T(8,128)(2,1)S(1)} %get-tuple-element.220.field_ref), channel_id=1, source_target_pairs={{0,4},{4,0},{8,12},{12,8},{16,20},{20,16},{24,28},{28,24},{1,5},{5... | collective-permute-start | bytes 1179656 | tf_op jit(solution)/shard_map/ppermute | solution.py:314
  39.9 14.1 %collective-permute-start.10 = (bf16[768,256]{1,0:T(8,128)(2,1)S(1)}, bf16[768,256]{1,0:T(8,128)(2,1)S(1)}, u32[]{:S(2)}, u32[]{:S(2)}) collective-permute-start(bf16[768,256]{1,0:T(8,128)(2,1)S(1)} %collective-permute-done.6.near_ref), channel_id=1, source_target_pairs={{0,8},{4,28},{8,16},{12,4},{16,24},{20,12},{24,0},{28,20},{1,9},{5... | collective-permute-start | bytes 1179656 | tf_op jit(solution)/shard_map/ppermute | solution.py:283
  42.0 14.7 %collective-permute-start.9 = (bf16[768,256]{1,0:T(8,128)(2,1)S(1)}, bf16[768,256]{1,0:T(8,128)(2,1)S(1)}, u32[]{:S(2)}, u32[]{:S(2)}) collective-permute-start(bf16[768,256]{1,0:T(8,128)(2,1)S(1)} %get-tuple-element.239.field_ref), channel_id=1, source_target_pairs={{0,4},{4,0},{8,12},{12,8},{16,20},{20,16},{24,28},{28,24},{1,5},{5... | collective-permute-start | bytes 1179656 | tf_op jit(solution)/shard_map/ppermute | solution.py:314
  48.3 14.1 %collective-permute-start.8 = (bf16[768,256]{1,0:T(8,128)(2,1)S(1)}, bf16[768,256]{1,0:T(8,128)(2,1)S(1)}, u32[]{:S(2)}, u32[]{:S(2)}) collective-permute-start(bf16[768,256]{1,0:T(8,128)(2,1)S(1)} %collective-permute-done.3.near_ref), channel_id=1, source_target_pairs={{0,8},{4,28},{8,16},{12,4},{16,24},{20,12},{24,0},{28,20},{1,9},{5... | collective-permute-start | bytes 1179656 | tf_op jit(solution)/shard_map/ppermute | solution.py:283
  50.4 14.7 %collective-permute-start.12 = (bf16[768,256]{1,0:T(8,128)(2,1)S(1)}, bf16[768,256]{1,0:T(8,128)(2,1)S(1)}, u32[]{:S(2)}, u32[]{:S(2)}) collective-permute-start(bf16[768,256]{1,0:T(8,128)(2,1)S(1)} %get-tuple-element.251.field_ref), channel_id=1, source_target_pairs={{0,4},{4,0},{8,12},{12,8},{16,20},{20,16},{24,28},{28,24},{1,5},{5... | collective-permute-start | bytes 1179656 | tf_op jit(solution)/shard_map/ppermute | solution.py:314
  56.7 14.1 %collective-permute-start.15 = (bf16[768,256]{1,0:T(8,128)(2,1)S(1)}, bf16[768,256]{1,0:T(8,128)(2,1)S(1)}, u32[]{:S(2)}, u32[]{:S(2)}) collective-permute-start(bf16[768,256]{1,0:T(8,128)(2,1)S(1)} %collective-permute-done.9.near_ref), channel_id=1, source_target_pairs={{0,8},{4,28},{8,16},{12,4},{16,24},{20,12},{24,0},{28,20},{1,9},{5... | collective-permute-start | bytes 1179656 | tf_op jit(solution)/shard_map/ppermute | solution.py:283
  58.8 14.7 %collective-permute-start.14 = (bf16[768,256]{1,0:T(8,128)(2,1)S(1)}, bf16[768,256]{1,0:T(8,128)(2,1)S(1)}, u32[]{:S(2)}, u32[]{:S(2)}) collective-permute-start(bf16[768,256]{1,0:T(8,128)(2,1)S(1)} %get-tuple-element.254.field_ref), channel_id=1, source_target_pairs={{0,4},{4,0},{8,12},{12,8},{16,20},{20,16},{24,28},{28,24},{1,5},{5... | collective-permute-start | bytes 1179656 | tf_op jit(solution)/shard_map/ppermute | solution.py:314
  65.1 12.1 %collective-permute-start.13 = (bf16[768,256]{1,0:T(8,128)(2,1)S(1)}, bf16[768,256]{1,0:T(8,128)(2,1)S(1)}, u32[]{:S(2)}, u32[]{:S(2)}) collective-permute-start(bf16[768,256]{1,0:T(8,128)(2,1)S(1)} %collective-permute-done.12.near_ref), channel_id=1, source_target_pairs={{0,8},{4,28},{8,16},{12,4},{16,24},{20,12},{24,0},{28,20},{1,9},{5... | collective-permute-start | bytes 1179656 | tf_op jit(solution)/shard_map/ppermute | solution.py:283
  67.2 14.7 %collective-permute-start.11 = (bf16[768,256]{1,0:T(8,128)(2,1)S(1)}, bf16[768,256]{1,0:T(8,128)(2,1)S(1)}, u32[]{:S(2)}, u32[]{:S(2)}) collective-permute-start(bf16[768,256]{1,0:T(8,128)(2,1)S(1)} %product_1.4.field_ref), channel_id=1, source_target_pairs={{0,4},{4,0},{8,12},{12,8},{16,20},{20,16},{24,28},{28,24},{1,5},{5... | collective-permute-start | bytes 1179656 | tf_op jit(solution)/shard_map/ppermute | solution.py:314
  73.6 16.9 %collective-permute-start.17 = (bf16[768,256]{1,0:T(8,128)(2,1)S(1)}, bf16[768,256]{1,0:T(8,128)(2,1)S(1)}, u32[]{:S(2)}, u32[]{:S(2)}) collective-permute-start(bf16[768,256]{1,0:T(8,128)(2,1)S(1)} %product_1.5.field_ref), channel_id=1, source_target_pairs={{0,4},{4,0},{8,12},{12,8},{16,20},{20,16},{24,28},{28,24},{1,5},{5... | collective-permute-start | bytes 1179656 | tf_op jit(solution)/shard_map/ppermute | solution.py:314
  75.6 12.0 %collective-permute-start.18 = (bf16[768,256]{1,0:T(8,128)(2,1)S(1)}, bf16[768,256]{1,0:T(8,128)(2,1)S(1)}, u32[]{:S(2)}, u32[]{:S(2)}) collective-permute-start(bf16[768,256]{1,0:T(8,128)(2,1)S(1)} %collective-permute-done.14.near_ref), channel_id=1, source_target_pairs={{0,8},{4,28},{8,16},{12,4},{16,24},{20,12},{24,0},{28,20},{1,9},{5... | collective-permute-start | bytes 1179656 | tf_op jit(solution)/shard_map/ppermute | solution.py:283
  82.0 13.6 %collective-permute-start.16 = (bf16[768,256]{1,0:T(8,128)(2,1)S(1)}, bf16[768,256]{1,0:T(8,128)(2,1)S(1)}, u32[]{:S(2)}, u32[]{:S(2)}) collective-permute-start(bf16[768,256]{1,0:T(8,128)(2,1)S(1)} %collective-permute-done.11.near_ref), channel_id=1, source_target_pairs={{0,8},{4,28},{8,16},{12,4},{16,24},{20,12},{24,0},{28,20},{1,9},{5... | collective-permute-start | bytes 1179656 | tf_op jit(solution)/shard_map/ppermute | solution.py:283
  84.1 14.8 %collective-permute-start.20 = (bf16[768,256]{1,0:T(8,128)(2,1)S(1)}, bf16[768,256]{1,0:T(8,128)(2,1)S(1)}, u32[]{:S(2)}, u32[]{:S(2)}) collective-permute-start(bf16[768,256]{1,0:T(8,128)(2,1)S(1)} %product_1.6.field_ref), channel_id=1, source_target_pairs={{0,4},{4,0},{8,12},{12,8},{16,20},{20,16},{24,28},{28,24},{1,5},{5... | collective-permute-start | bytes 1179656 | tf_op jit(solution)/shard_map/ppermute | solution.py:314
  90.4 13.6 %collective-permute-start.19 = (bf16[768,256]{1,0:T(8,128)(2,1)S(1)}, bf16[768,256]{1,0:T(8,128)(2,1)S(1)}, u32[]{:S(2)}, u32[]{:S(2)}) collective-permute-start(bf16[768,256]{1,0:T(8,128)(2,1)S(1)} %collective-permute-done.17.near_ref), channel_id=1, source_target_pairs={{0,8},{4,28},{8,16},{12,4},{16,24},{20,12},{24,0},{28,20},{1,9},{5... | collective-permute-start | bytes 1179656 | tf_op jit(solution)/shard_map/ppermute | solution.py:283
  96.9 10.0 %collective-permute-start.23 = (bf16[768,256]{1,0:T(8,128)(2,1)S(1)}, bf16[768,256]{1,0:T(8,128)(2,1)S(1)}, u32[]{:S(2)}, u32[]{:S(2)}) collective-permute-start(bf16[768,256]{1,0:T(8,128)(2,1)S(1)} %get-tuple-element.277.refs_0_.refs_1_.refs_10_), channel_id=1, source_target_pairs={{0,2},{1,3},{2,0},{3,1},{4,6},{5,7},{6,4},{7,5},{8,10},{9,11},{10,... | collective-permute-start | bytes 1179656 | tf_op jit(solution)/shard_map/ppermute | solution.py:256
  98.5 8.4 %collective-permute-start.22 = (bf16[768,256]{1,0:T(8,128)(2,1)S(1)}, bf16[768,256]{1,0:T(8,128)(2,1)S(1)}, u32[]{:S(2)}, u32[]{:S(2)}) collective-permute-start(bf16[768,256]{1,0:T(8,128)(2,1)S(1)} %product_1.7.field_ref), channel_id=1, source_target_pairs={{0,4},{4,0},{8,12},{12,8},{16,20},{20,16},{24,28},{28,24},{1,5},{5... | collective-permute-start | bytes 1179656 | tf_op jit(solution)/shard_map/ppermute | solution.py:314
  98.9 14.1 %collective-permute-start.21 = (bf16[768,256]{1,0:T(8,128)(2,1)S(1)}, bf16[768,256]{1,0:T(8,128)(2,1)S(1)}, u32[]{:S(2)}, u32[]{:S(2)}) collective-permute-start(bf16[768,256]{1,0:T(8,128)(2,1)S(1)} %collective-permute-done.20.near_ref), channel_id=1, source_target_pairs={{0,8},{4,28},{8,16},{12,4},{16,24},{20,12},{24,0},{28,20},{1,9},{5... | collective-permute-start | bytes 1179656 | tf_op jit(solution)/shard_map/ppermute | solution.py:283
  105.3 10.5 %collective-permute-start.25 = (bf16[768,256]{1,0:T(8,128)(2,1)S(1)}, bf16[768,256]{1,0:T(8,128)(2,1)S(1)}, u32[]{:S(2)}, u32[]{:S(2)}) collective-permute-start(bf16[768,256]{1,0:T(8,128)(2,1)S(1)} %get-tuple-element.288.refs_1_.refs_2_.refs_11_), channel_id=1, source_target_pairs={{0,2},{1,3},{2,0},{3,1},{4,6},{5,7},{6,4},{7,5},{8,10},{9,11},{10,... | collective-permute-start | bytes 1179656 | tf_op jit(solution)/shard_map/ppermute | solution.py:256
  106.9 12.8 %collective-permute-start.24 = (bf16[768,256]{1,0:T(8,128)(2,1)S(1)}, bf16[768,256]{1,0:T(8,128)(2,1)S(1)}, u32[]{:S(2)}, u32[]{:S(2)}) collective-permute-start(bf16[768,256]{1,0:T(8,128)(2,1)S(1)} %collective-permute-done.22.near_ref), channel_id=1, source_target_pairs={{0,8},{4,28},{8,16},{12,4},{16,24},{20,12},{24,0},{28,20},{1,9},{5... | collective-permute-start | bytes 1179656 | tf_op jit(solution)/shard_map/ppermute | solution.py:283
  115.3 8.8 %collective-permute-start.29 = (bf16[768,256]{1,0:T(8,128)(2,1)S(1)}, bf16[768,256]{1,0:T(8,128)(2,1)S(1)}, u32[]{:S(2)}, u32[]{:S(2)}) collective-permute-start(bf16[768,256]{1,0:T(8,128)(2,1)S(1)} %get-tuple-element.288.refs_1_.refs_2_.refs_11_), channel_id=1, source_target_pairs={{0,1},{1,0},{2,3},{3,2},{4,5},{5,4},{6,7},{7,6},{8,9},{9,8},{10,11... | collective-permute-start | bytes 1179656 | tf_op jit(solution)/shard_map/ppermute | solution.py:256
  115.9 14.3 %collective-permute-start.30 = (bf16[768,256]{1,0:T(8,128)(2,1)S(1)}, bf16[768,256]{1,0:T(8,128)(2,1)}, u32[]{:S(2)}, u32[]{:S(2)}) collective-permute-start(bf16[768,256]{1,0:T(8,128)(2,1)S(1)} %get-tuple-element.300.refs_2_.refs_3_.refs_12_), channel_id=1, source_target_pairs={{0,1},{1,0},{2,3},{3,2},{4,5},{5,4},{6,7},{7,6},{8,9},{9,8},{10,11... | collective-permute-start | bytes 1179656 | tf_op jit(solution)/shard_map/ppermute | solution.py:256
  121.0 9.1 %collective-permute-start.31 = (bf16[768,256]{1,0:T(8,128)(2,1)S(1)}, bf16[768,256]{1,0:T(8,128)(2,1)}, u32[]{:S(2)}, u32[]{:S(2)}) collective-permute-start(bf16[768,256]{1,0:T(8,128)(2,1)S(1)} %get-tuple-element.310.refs_3_.refs_4_.refs_13_), channel_id=1, source_target_pairs={{0,1},{1,0},{2,3},{3,2},{4,5},{5,4},{6,7},{7,6},{8,9},{9,8},{10,11... | collective-permute-start | bytes 1179656 | tf_op jit(solution)/shard_map/ppermute | solution.py:256
  122.2 12.5 %collective-permute-start.27 = (bf16[768,256]{1,0:T(8,128)(2,1)S(1)}, bf16[768,256]{1,0:T(8,128)(2,1)S(1)}, u32[]{:S(2)}, u32[]{:S(2)}) collective-permute-start(bf16[768,256]{1,0:T(8,128)(2,1)S(1)} %get-tuple-element.310.refs_3_.refs_4_.refs_13_), channel_id=1, source_target_pairs={{0,2},{1,3},{2,0},{3,1},{4,6},{5,7},{6,4},{7,5},{8,10},{9,11},{10,... | collective-permute-start | bytes 1179656 | tf_op jit(solution)/shard_map/ppermute | solution.py:256
  124.1 10.6 %collective-permute-start.35 = (bf16[768,256]{1,0:T(8,128)(2,1)S(1)}, bf16[768,256]{1,0:T(8,128)(2,1)S(1)}, u32[]{:S(2)}, u32[]{:S(2)}) collective-permute-start(bf16[768,256]{1,0:T(8,128)(2,1)S(1)} %collective-permute-done.23.refs_4_.refs_1_), channel_id=1, source_target_pairs={{0,1},{1,0},{2,3},{3,2},{4,5},{5,4},{6,7},{7,6},{8,9},{9,8},{10,11... | collective-permute-start | bytes 1179656 | tf_op jit(solution)/shard_map/ppermute | solution.py:256
  129.4 24.8 %collective-permute-start.40 = (bf16[384,1024]{1,0:T(8,128)(2,1)}, bf16[384,1024]{1,0:T(8,128)(2,1)}, u32[]{:S(2)}, u32[]{:S(2)}) collective-permute-start(bf16[384,1024]{1,0:T(8,128)(2,1)} %get-tuple-element.356), channel_id=1, source_target_pairs={{0,8},{4,12},{8,0},{12,4},{16,24},{20,28},{24,16},{28,20},{1,9},{5... | collective-permute-start | bytes 2359304 | tf_op jit(solution)/shard_map/ppermute | solution.py:342
  130.1 12.4 %collective-permute-start.36 = (bf16[768,256]{1,0:T(8,128)(2,1)S(1)}, bf16[768,256]{1,0:T(8,128)(2,1)}, u32[]{:S(2)}, u32[]{:S(2)}) collective-permute-start(bf16[768,256]{1,0:T(8,128)(2,1)S(1)} %collective-permute-done.25.refs_5_.refs_2_), channel_id=1, source_target_pairs={{0,1},{1,0},{2,3},{3,2},{4,5},{5,4},{6,7},{7,6},{8,9},{9,8},{10,11... | collective-permute-start | bytes 1179656 | tf_op jit(solution)/shard_map/ppermute | solution.py:256
  130.2 14.5 %collective-permute-start.37 = (bf16[768,256]{1,0:T(8,128)(2,1)S(1)}, bf16[768,256]{1,0:T(8,128)(2,1)}, u32[]{:S(2)}, u32[]{:S(2)}) collective-permute-start(bf16[768,256]{1,0:T(8,128)(2,1)S(1)} %collective-permute-done.26.refs_6_.refs_3_), channel_id=1, source_target_pairs={{0,1},{1,0},{2,3},{3,2},{4,5},{5,4},{6,7},{7,6},{8,9},{9,8},{10,11... | collective-permute-start | bytes 1179656 | tf_op jit(solution)/shard_map/ppermute | solution.py:256
  134.7 10.0 %collective-permute-start.38 = (bf16[768,256]{1,0:T(8,128)(2,1)S(1)}, bf16[768,256]{1,0:T(8,128)(2,1)}, u32[]{:S(2)}, u32[]{:S(2)}) collective-permute-start(bf16[768,256]{1,0:T(8,128)(2,1)S(1)} %collective-permute-done.27.refs_7_.refs_4_), channel_id=1, source_target_pairs={{0,1},{1,0},{2,3},{3,2},{4,5},{5,4},{6,7},{7,6},{8,9},{9,8},{10,11... | collective-permute-start | bytes 1179656 | tf_op jit(solution)/shard_map/ppermute | solution.py:256
  139.0 15.2 %collective-permute-start.41 = (bf16[256,1024]{1,0:T(8,128)(2,1)}, bf16[256,1024]{1,0:T(8,128)(2,1)}, u32[]{:S(2)}, u32[]{:S(2)}) collective-permute-start(bf16[256,1024]{1,0:T(8,128)(2,1)} %get-tuple-element.357), channel_id=1, source_target_pairs={{0,4},{4,0},{8,12},{12,8},{16,20},{20,16},{24,28},{28,24},{1,5},{5... | collective-permute-start | bytes 1572872 | tf_op jit(solution)/shard_map/ppermute | solution.py:342
  142.6 25.3 %collective-permute-start.34 = (bf16[272,1024]{1,0:T(8,128)(2,1)S(1)}, bf16[272,1024]{1,0:T(8,128)(2,1)S(1)}, u32[]{:S(2)}, u32[]{:S(2)}) collective-permute-start(bf16[272,1024]{1,0:T(8,128)(2,1)S(1)} %get-tuple-element.346), channel_id=1, source_target_pairs={{0,8},{4,12},{8,0},{12,4},{16,24},{20,28},{24,16},{28,20},{1,9},{5... | collective-permute-start | bytes 1671176 | tf_op jit(solution)/shard_map/ppermute | solution.py:342
  147.0 17.0 %collective-permute-start.39 = (bf16[256,1024]{1,0:T(8,128)(2,1)S(1)}, bf16[256,1024]{1,0:T(8,128)(2,1)S(1)}, u32[]{:S(2)}, u32[]{:S(2)}) collective-permute-start(bf16[256,1024]{1,0:T(8,128)(2,1)S(1)} %get-tuple-element.355), channel_id=1, source_target_pairs={{0,4},{4,0},{8,12},{12,8},{16,20},{20,16},{24,28},{28,24},{1,5},{5... | collective-permute-start | bytes 1572872 | tf_op jit(solution)/shard_map/ppermute | solution.py:342
  155.9 17.7 %collective-permute-start.43 = (bf16[128,1024]{1,0:T(8,128)(2,1)}, bf16[128,1024]{1,0:T(8,128)(2,1)}, u32[]{:S(2)}, u32[]{:S(2)}) collective-permute-start(bf16[128,1024]{1,0:T(8,128)(2,1)} %add_convert_fusion.2), channel_id=1, source_target_pairs={{0,8},{4,12},{8,0},{12,4},{16,24},{20,28},{24,16},{28,20},{1,9},{5... | collective-permute-start | bytes 786440 | tf_op jit(solution)/shard_map/ppermute | solution.py:342
  159.9 18.4 %collective-permute-start.45 = (bf16[192,1024]{1,0:T(8,128)(2,1)}, bf16[192,1024]{1,0:T(8,128)(2,1)}, u32[]{:S(2)}, u32[]{:S(2)}) collective-permute-start(bf16[192,1024]{1,0:T(8,128)(2,1)} %add_convert_fusion), channel_id=1, source_target_pairs={{0,16},{4,20},{8,24},{12,28},{16,0},{20,4},{24,8},{28,12},{1,17},{... | collective-permute-start | bytes 1179656 | tf_op jit(solution)/shard_map/ppermute | solution.py:342
  168.9 14.2 %collective-permute-start.42 = (bf16[144,1024]{1,0:T(8,128)(2,1)}, bf16[144,1024]{1,0:T(8,128)(2,1)}, u32[]{:S(2)}, u32[]{:S(2)}) collective-permute-start(bf16[144,1024]{1,0:T(8,128)(2,1)} %pad_maximum_fusion.5), channel_id=1, source_target_pairs={{0,4},{4,0},{8,12},{12,8},{16,20},{20,16},{24,28},{28,24},{1,5},{5... | collective-permute-start | bytes 884744 | tf_op jit(solution)/shard_map/ppermute | solution.py:342
  171.3 11.8 %collective-permute-start.48 = (bf16[128,1024]{1,0:T(8,128)(2,1)}, bf16[128,1024]{1,0:T(8,128)(2,1)}, u32[]{:S(2)}, u32[]{:S(2)}) collective-permute-start(bf16[128,1024]{1,0:T(8,128)(2,1)} %add_convert_fusion.1), channel_id=1, source_target_pairs={{0,8},{4,12},{8,0},{12,4},{16,24},{20,28},{24,16},{28,20},{1,9},{5... | collective-permute-start | bytes 786440 | tf_op jit(solution)/shard_map/ppermute | solution.py:342
  175.3 15.7 %collective-permute-start.47 = (bf16[64,1024]{1,0:T(8,128)(2,1)}, bf16[64,1024]{1,0:T(8,128)(2,1)}, u32[]{:S(2)}, u32[]{:S(2)}) collective-permute-start(bf16[64,1024]{1,0:T(8,128)(2,1)} %add_convert_fusion.6), channel_id=1, source_target_pairs={{0,16},{4,20},{8,24},{12,28},{16,0},{20,4},{24,8},{28,12},{1,17},{... | collective-permute-start | bytes 393224 | tf_op jit(solution)/shard_map/ppermute | solution.py:342
  180.2 10.9 %collective-permute-start.46 = (bf16[96,1024]{1,0:T(8,128)(2,1)}, bf16[96,1024]{1,0:T(8,128)(2,1)}, u32[]{:S(2)}, u32[]{:S(2)}) collective-permute-start(bf16[96,1024]{1,0:T(8,128)(2,1)} %add_convert_fusion.4), channel_id=1, source_target_pairs={{0,4},{4,0},{8,12},{12,8},{16,20},{20,16},{24,28},{28,24},{1,5},{5... | collective-permute-start | bytes 589832 | tf_op jit(solution)/shard_map/ppermute | solution.py:342
  186.4 13.3 %collective-permute-start.44 = (bf16[80,1024]{1,0:T(8,128)(2,1)}, bf16[80,1024]{1,0:T(8,128)(2,1)}, u32[]{:S(2)}, u32[]{:S(2)}) collective-permute-start(bf16[80,1024]{1,0:T(8,128)(2,1)} %pad_maximum_fusion.9), channel_id=1, source_target_pairs={{0,16},{4,20},{8,24},{12,28},{16,0},{20,4},{24,8},{28,12},{1,17},{... | collective-permute-start | bytes 491528 | tf_op jit(solution)/shard_map/ppermute | solution.py:342
  188.1 11.6 %collective-permute-start.52 = (bf16[64,1024]{1,0:T(8,128)(2,1)}, bf16[64,1024]{1,0:T(8,128)(2,1)}, u32[]{:S(2)}, u32[]{:S(2)}) collective-permute-start(bf16[64,1024]{1,0:T(8,128)(2,1)} %add_convert_fusion.5), channel_id=1, source_target_pairs={{0,16},{4,20},{8,24},{12,28},{16,0},{20,4},{24,8},{28,12},{1,17},{... | collective-permute-start | bytes 393224 | tf_op jit(solution)/shard_map/ppermute | solution.py:342
  203.6 10.4 %collective-permute-start.49 = (bf16[64,1024]{1,0:T(8,128)(2,1)S(1)}, bf16[64,1024]{1,0:T(8,128)(2,1)S(1)}, u32[]{:S(2)}, u32[]{:S(2)}) collective-permute-start(bf16[64,1024]{1,0:T(8,128)(2,1)S(1)} %divide_convert_fusion.3), channel_id=1, source_target_pairs={{0,16},{4,20},{8,24},{12,28},{16,0},{20,4},{24,8},{28,12},{1,17},{... | collective-permute-start | bytes 393224 | tf_op jit(solution)/shard_map/ppermute | solution.py:342
  204.9 16.4 %collective-permute-start.51 = (bf16[64,1024]{1,0:T(8,128)(2,1)S(1)}, bf16[64,1024]{1,0:T(8,128)(2,1)S(1)}, u32[]{:S(2)}, u32[]{:S(2)}) collective-permute-start(bf16[64,1024]{1,0:T(8,128)(2,1)S(1)} %divide_convert_fusion.2), channel_id=1, source_target_pairs={{0,16},{4,20},{8,24},{12,28},{16,0},{20,4},{24,8},{28,12},{1,17},{... | collective-permute-start | bytes 393224 | tf_op jit(solution)/shard_map/ppermute | solution.py:342
  214.0 8.4 %collective-permute-start.53 = (bf16[128,1024]{1,0:T(8,128)(2,1)S(1)}, bf16[128,1024]{1,0:T(8,128)(2,1)S(1)}, u32[]{:S(2)}, u32[]{:S(2)}) collective-permute-start(bf16[128,1024]{1,0:T(8,128)(2,1)S(1)} %pad_maximum_fusion.6), channel_id=1, source_target_pairs={{0,8},{4,12},{8,0},{12,4},{16,24},{20,28},{24,16},{28,20},{1,9},{5... | collective-permute-start | bytes 786440 | tf_op jit(solution)/shard_map/ppermute | solution.py:342
  215.5 11.3 %collective-permute-start.50 = (bf16[96,1024]{1,0:T(8,128)(2,1)S(1)}, bf16[96,1024]{1,0:T(8,128)(2,1)S(1)}, u32[]{:S(2)}, u32[]{:S(2)}) collective-permute-start(bf16[96,1024]{1,0:T(8,128)(2,1)S(1)} %divide_convert_fusion), channel_id=1, source_target_pairs={{0,4},{4,0},{8,12},{12,8},{16,20},{20,16},{24,28},{28,24},{1,5},{5... | collective-permute-start | bytes 589832 | tf_op jit(solution)/shard_map/ppermute | solution.py:342
  218.7 8.1 %collective-permute-start.54 = (bf16[64,1024]{1,0:T(8,128)(2,1)S(1)}, bf16[64,1024]{1,0:T(8,128)(2,1)S(1)}, u32[]{:S(2)}, u32[]{:S(2)}) collective-permute-start(bf16[64,1024]{1,0:T(8,128)(2,1)S(1)} %divide_convert_fusion.1), channel_id=1, source_target_pairs={{0,16},{4,20},{8,24},{12,28},{16,0},{20,4},{24,8},{28,12},{1,17},{... | collective-permute-start | bytes 393224 | tf_op jit(solution)/shard_map/ppermute | solution.py:342
  222.5 21.9 %collective-permute-start.56 = (bf16[256,1024]{1,0:T(8,128)(2,1)S(1)}, bf16[256,1024]{1,0:T(8,128)(2,1)S(1)}, u32[]{:S(2)}, u32[]{:S(2)}) collective-permute-start(bf16[256,1024]{1,0:T(8,128)(2,1)S(1)} %pad_maximum_fusion.1.refs_4_), channel_id=1, source_target_pairs={{0,4},{4,0},{8,12},{12,8},{16,20},{20,16},{24,28},{28,24},{1,5},{5... | collective-permute-start | bytes 1572872 | tf_op jit(solution)/shard_map/ppermute | solution.py:342
  226.3 16.1 %collective-permute-start.55 = (bf16[128,1024]{1,0:T(8,128)(2,1)S(1)}, bf16[128,1024]{1,0:T(8,128)(2,1)S(1)}, u32[]{:S(2)}, u32[]{:S(2)}) collective-permute-start(bf16[128,1024]{1,0:T(8,128)(2,1)S(1)} %pad_maximum_fusion.7), channel_id=1, source_target_pairs={{0,4},{4,0},{8,12},{12,8},{16,20},{20,16},{24,28},{28,24},{1,5},{5... | collective-permute-start | bytes 786440 | tf_op jit(solution)/shard_map/ppermute | solution.py:342
  226.7 15.8 %collective-permute-start.64 = (bf16[128,1024]{1,0:T(8,128)(2,1)S(1)}, bf16[128,1024]{1,0:T(8,128)(2,1)S(1)}, u32[]{:S(2)}, u32[]{:S(2)}) collective-permute-start(bf16[128,1024]{1,0:T(8,128)(2,1)S(1)} %pad_maximum_fusion.8), channel_id=1, source_target_pairs={{0,8},{4,12},{8,0},{12,4},{16,24},{20,28},{24,16},{28,20},{1,9},{5... | collective-permute-start | bytes 786440 | tf_op jit(solution)/shard_map/ppermute | solution.py:342
  226.9 18.4 %collective-permute-start.60 = (bf16[192,1024]{1,0:T(8,128)(2,1)S(1)}, bf16[192,1024]{1,0:T(8,128)(2,1)S(1)}, u32[]{:S(2)}, u32[]{:S(2)}) collective-permute-start(bf16[192,1024]{1,0:T(8,128)(2,1)S(1)} %pad_maximum_fusion.4), channel_id=1, source_target_pairs={{0,16},{4,20},{8,24},{12,28},{16,0},{20,4},{24,8},{28,12},{1,17},{... | collective-permute-start | bytes 1179656 | tf_op jit(solution)/shard_map/ppermute | solution.py:342
  229.6 27.8 %collective-permute-start.57 = (bf16[256,1024]{1,0:T(8,128)(2,1)S(1)}, bf16[256,1024]{1,0:T(8,128)(2,1)S(1)}, u32[]{:S(2)}, u32[]{:S(2)}) collective-permute-start(bf16[256,1024]{1,0:T(8,128)(2,1)S(1)} %pad_maximum_fusion.1.refs_4_), channel_id=1, source_target_pairs={{0,1},{1,0},{2,3},{3,2},{4,5},{5,4},{6,7},{7,6},{8,9},{9,8},{10,11... | collective-permute-start | bytes 1572872 | tf_op jit(solution)/shard_map/ppermute | solution.py:256
  242.5 14.9 %collective-permute-start.59 = (bf16[256,1024]{1,0:T(8,128)(2,1)S(1)}, bf16[256,1024]{1,0:T(8,128)(2,1)S(1)}, u32[]{:S(2)}, u32[]{:S(2)}) collective-permute-start(bf16[256,1024]{1,0:T(8,128)(2,1)S(1)} %pad_maximum_fusion.2.refs_5_), channel_id=1, source_target_pairs={{0,8},{4,12},{8,0},{12,4},{16,24},{20,28},{24,16},{28,20},{1,9},{5... | collective-permute-start | bytes 1572872 | tf_op jit(solution)/shard_map/ppermute | solution.py:342
  242.6 16.8 %collective-permute-start.65 = (bf16[256,1024]{1,0:T(8,128)(2,1)S(1)}, bf16[256,1024]{1,0:T(8,128)(2,1)S(1)}, u32[]{:S(2)}, u32[]{:S(2)}) collective-permute-start(bf16[256,1024]{1,0:T(8,128)(2,1)S(1)} %pad_maximum_fusion.3.refs_6_), channel_id=1, source_target_pairs={{0,4},{4,0},{8,12},{12,8},{16,20},{20,16},{24,28},{28,24},{1,5},{5... | collective-permute-start | bytes 1572872 | tf_op jit(solution)/shard_map/ppermute | solution.py:342
  244.4 15.0 %collective-permute-start.58 = (bf16[256,1024]{1,0:T(8,128)(2,1)S(1)}, bf16[256,1024]{1,0:T(8,128)(2,1)S(1)}, u32[]{:S(2)}, u32[]{:S(2)}) collective-permute-start(bf16[256,1024]{1,0:T(8,128)(2,1)S(1)} %collective-permute-done.56.refs_5_), channel_id=1, source_target_pairs={{0,1},{1,0},{2,3},{3,2},{4,5},{5,4},{6,7},{7,6},{8,9},{9,8},{10,11... | collective-permute-start | bytes 1572872 | tf_op jit(solution)/shard_map/ppermute | solution.py:256
  245.3 38.2 %collective-permute-start.63 = (bf16[384,1024]{1,0:T(8,128)(2,1)S(1)}, bf16[384,1024]{1,0:T(8,128)(2,1)S(1)}, u32[]{:S(2)}, u32[]{:S(2)}) collective-permute-start(bf16[384,1024]{1,0:T(8,128)(2,1)S(1)} %pad_maximum_fusion.refs_5_), channel_id=1, source_target_pairs={{0,8},{4,12},{8,0},{12,4},{16,24},{20,28},{24,16},{28,20},{1,9},{5... | collective-permute-start | bytes 2359304 | tf_op jit(solution)/shard_map/ppermute | solution.py:342
  257.4 14.9 %collective-permute-start.61 = (bf16[256,1024]{1,0:T(8,128)(2,1)S(1)}, bf16[256,1024]{1,0:T(8,128)(2,1)S(1)}, u32[]{:S(2)}, u32[]{:S(2)}) collective-permute-start(bf16[256,1024]{1,0:T(8,128)(2,1)S(1)} %pad_maximum_fusion.2.refs_5_), channel_id=1, source_target_pairs={{0,2},{1,3},{2,0},{3,1},{4,6},{5,7},{6,4},{7,5},{8,10},{9,11},{10,... | collective-permute-start | bytes 1572872 | tf_op jit(solution)/shard_map/ppermute | solution.py:256
  257.4 26.1 %collective-permute-start.62 = (bf16[256,1024]{1,0:T(8,128)(2,1)S(1)}, bf16[256,1024]{1,0:T(8,128)(2,1)S(1)}, u32[]{:S(2)}, u32[]{:S(2)}) collective-permute-start(bf16[256,1024]{1,0:T(8,128)(2,1)S(1)} %collective-permute-done.59.refs_6_), channel_id=1, source_target_pairs={{0,2},{1,3},{2,0},{3,1},{4,6},{5,7},{6,4},{7,5},{8,10},{9,11},{10,... | collective-permute-start | bytes 1572872 | tf_op jit(solution)/shard_map/ppermute | solution.py:256
  259.4 32.8 %collective-permute-start.66 = (bf16[256,1024]{1,0:T(8,128)(2,1)S(1)}, bf16[256,1024]{1,0:T(8,128)(2,1)S(1)}, u32[]{:S(2)}, u32[]{:S(2)}) collective-permute-start(bf16[256,1024]{1,0:T(8,128)(2,1)S(1)} %pad_maximum_fusion.3.refs_6_), channel_id=1, source_target_pairs={{0,3},{1,2},{2,1},{3,0},{4,7},{5,6},{6,5},{7,4},{8,11},{9,10},{10,... | collective-permute-start | bytes 1572872 | tf_op jit(solution)/shard_map/ppermute | solution.py:256
  259.4 41.4 %collective-permute-start.67 = (bf16[256,1024]{1,0:T(8,128)(2,1)S(1)}, bf16[256,1024]{1,0:T(8,128)(2,1)S(1)}, u32[]{:S(2)}, u32[]{:S(2)}) collective-permute-start(bf16[256,1024]{1,0:T(8,128)(2,1)S(1)} %collective-permute-done.65.refs_7_), channel_id=1, source_target_pairs={{0,3},{1,2},{2,1},{3,0},{4,7},{5,6},{6,5},{7,4},{8,11},{9,10},{10,... | collective-permute-start | bytes 1572872 | tf_op jit(solution)/shard_map/ppermute | solution.py:256
  (29 other events, 304.0 us)

commit v7 on v6

--- a/solution.py
+++ b/solution.py
@@ -79,13 +79,17 @@
             before_ref, half_ref = refs
             half_ref[here, :] = (2.0 * total - before_ref[here, :].astype(F32)).astype(BF16)
         else:
-            before_ref, earlier_ref, half_ref, squares_ref = refs
+            before_ref, earlier_ref, half_ref, *squares_ref = refs
             value = (2.0 * total - before_ref[here, :]).astype(BF16)
             half_ref[here, :] = value
             wide = value.astype(F32)
             squares += jnp.sum((wide * wide).reshape(-1, 8, width), axis=0)
     if stage == 2:
-        squares_ref[...] = earlier_ref[...] + squares
+        squares = earlier_ref[...] + squares
+        if squares_ref:
+            squares_ref[0][...] = squares
+        else:
+            half_ref[elements * size :, :] = extra_rows(jnp.full((1, width), jnp.sum(squares)))
 
 
 def call(kernel, name, outs, scalars, args, scratch=(), aliases=None, vmem=16):
@@ -102,12 +106,13 @@
     )(*scalars, *args)
 
 
-def product(stage, place, blocks, field, by_near, by_far, *before):
+def product(stage, place, blocks, field, by_near, by_far, *before, last=False):
     rows, width = field.shape
+    ended = jax.ShapeDtypeStruct((rows + EXTRA, width), BF16)
     half = jax.ShapeDtypeStruct((rows, width), BF16)
     wide = jax.ShapeDtypeStruct((rows, width), F32)
     squares = jax.ShapeDtypeStruct((8, width), F32)
-    outs = ((wide, half), half, (half, squares))[stage]
+    outs = ((wide, half), half, ended if last else (half, squares))[stage]
     args = (blocks, field, by_near, by_far, *before)
     kernel = functools.partial(product_kernel, stage)
     return call(kernel, f"product_{stage}", outs, (place,), args)
@@ -140,25 +145,21 @@
     return rows.astype(BF16)
 
 
-def side_by_side(refs):
-    return jnp.concatenate([ref[...] for ref in refs], axis=1)
+def side_by_side(refs, rows):
+    return jnp.concatenate([ref[:rows, :] for ref in refs], axis=1)
 
 
 def gram_kernel(pair, mask, where_ref, *refs):
     mine_ref, other_ref, whole = refs[-3:]
     fields = refs[:CHUNKS]
+    rows, width = fields[0].shape
     half = whole.shape[0] // 2
-    if mine_ref.shape[0] > half:
-        carried = extra_rows(jnp.full((1, whole.shape[1]), jnp.sum(refs[2 * CHUNKS][...])))
-        mine_ref[half:, :] = carried
-        other_ref[half:, :] = carried
-    width = fields[0].shape[1]
     middle = CHUNKS * width // 2
     side = lax.rem(where_ref[0] // mask, 2)
 
     def fill(left, rights, count):
         for c, right in enumerate(rights):
-            value = lax.dot_general(left, right[...], TRANSPOSED_LEFT, preferred_element_type=F32)
+            value = lax.dot_general(left, right[:rows, :], TRANSPOSED_LEFT, preferred_element_type=F32)
             whole[:count, c * width : (c + 1) * width] = value.astype(BF16)
 
     if pair:
@@ -167,15 +168,15 @@
 
         @pl.when(where_ref[1] == 0)
         def _():
-            fill(side_by_side(peers[: CHUNKS // 2]), fields, middle)
+            fill(side_by_side(peers[: CHUNKS // 2], rows), fields, middle)
 
         @pl.when(where_ref[1] == 1)
         def _():
-            fill(side_by_side(fields[CHUNKS // 2 :]), peers, middle)
+            fill(side_by_side(fields[CHUNKS // 2 :], rows), peers, middle)
     else:
         used = middle + middle // 2
-        upper = side_by_side(fields[CHUNKS // 2 :])
-        fill(side_by_side(fields[: CHUNKS // 2]), fields, middle)
+        upper = side_by_side(fields[CHUNKS // 2 :], rows)
+        fill(side_by_side(fields[: CHUNKS // 2], rows), fields, middle)
         corner = lax.dot_general(upper, upper, TRANSPOSED_LEFT, preferred_element_type=F32).astype(BF16)
         whole[middle:used, :middle] = corner[: middle // 2]
         whole[middle:used, middle:] = corner[middle // 2 :]
@@ -183,6 +184,47 @@
         whole[used:, :] = jnp.zeros((whole.shape[0] - used, whole.shape[1]), BF16)
     mine_ref[:half, :] = whole[pl.ds(pl.multiple_of(side * half, half), half), :]
     other_ref[:half, :] = whole[pl.ds(pl.multiple_of((1 - side) * half, half), half), :]
+    if mine_ref.shape[0] > half:
+        ends = [fields[-1], *refs[2 * CHUNKS - 1 : -3]]
+        total = sum(jnp.sum(end[rows:, :].astype(F32), axis=0, keepdims=True) for end in ends)
+        carried = extra_rows(jnp.concatenate([total] * CHUNKS, axis=1))
+        mine_ref[half:, :] = carried
+        other_ref[half:, :] = carried
+
+
+def sum_kernel(masks, hop, extra, entries, rows_total, where_ref, *refs):
+    terms, outs = refs[: hop + 1], refs[hop + 1 :]
+    height = terms[0].shape[0] - extra
+    begins, offset = [0, 0], 0
+    final = hop == len(masks)
+    for i, mask in enumerate(masks[1 : hop + 1], 1):
+        height //= 2
+        keep = lax.rem(where_ref[0] // mask, 2)
+        first_row = offset + (1 - keep) * height
+        offset = offset + keep * height
+        begins.append(offset)
+    if final:
+        first_row = offset
+    step = terms[-1].shape[0] - extra if final else height
+    value = 0.0
+    for term, begin in zip(terms, begins):
+        here = pl.ds(pl.multiple_of(first_row - begin, EXTRA), step)
+        value = value + term[here, :].astype(F32)
+    total = None
+    if extra:
+        total = sum(jnp.sum(term[-extra:, :].astype(F32), axis=0, keepdims=True) for term in terms)
+    if not final:
+        outs[0][:step, :] = value.astype(BF16)
+        if extra:
+            outs[0][step:, :] = extra_rows(total)
+        return
+    if extra:
+        level = total / entries
+        outs[1][...] = jnp.broadcast_to(level[:, :1], outs[1].shape)
+    else:
+        level_ref, *outs = outs
+        level = level_ref[:1, :1]
+    outs[0][...] = (value / (level * rows_total)).astype(BF16)
 
 
 def mix_kernel(pair, masks, first, last, where_ref, *refs):
@@ -191,14 +233,14 @@
     fields, refs = refs[:CHUNKS], refs[CHUNKS:]
     out_ref, block = refs[-2:]
     own = refs[-2 - CHUNKS : -2]
-    width = fields[0].shape[1]
+    rows, width = fields[0].shape
     middle = CHUNKS * width // 2
 
     def finish(mixed, here):
         value = mixed if first else total_ref[:, here] + mixed
         if last:
-            filtered = side_by_side(own)[:, here].astype(F32)
-            value = (1.5 * filtered - 0.5 * value) / jnp.sqrt(level_ref[0])
+            filtered = side_by_side(own, rows)[:, here].astype(F32)
+            value = (1.5 * filtered - 0.5 * value) / jnp.sqrt(level_ref[:1, :1])
         out_ref[:, here] = value.astype(out_ref.dtype)
 
     def times(left, right):
@@ -209,7 +251,7 @@
 
     if not pair:
         put_in_place(where_ref, masks, refs[0], refs[1], block, 0)
-        lower, upper = side_by_side(fields[: CHUNKS // 2]), side_by_side(fields[CHUNKS // 2 :])
+        lower, upper = side_by_side(fields[: CHUNKS // 2], rows), side_by_side(fields[CHUNKS // 2 :], rows)
         corner = block[middle : middle + middle // 2, :]
         corner = jnp.concatenate([corner[:, :middle], corner[:, middle:]], axis=0)
         finish(
@@ -225,14 +267,14 @@
 
     @pl.when(is_upper == 0)
     def _():
-        field = side_by_side(fields)
+        field = side_by_side(fields, rows)
         for c in range(CHUNKS):
             here = slice(c * width, (c + 1) * width)
             finish(times(field, jnp.concatenate([block[:middle, here], block[height : height + middle, here]])), here)
 
     @pl.when(is_upper == 1)
     def _():
-        field = side_by_side(fields)
+        field = side_by_side(fields, rows)
         for c in range(CHUNKS):
             row = c * width if c * width < middle else height + c * width - middle
             finish(times_transposed(field, block[row : row + width, :]), slice(c * width, (c + 1) * width))
@@ -295,13 +337,17 @@
         stage, c = job
         far[job] = order(far[job])
         old = ((), (start[c],), (firsts.get(c), squares))[stage]
-        out = product(stage, place, blocks, current[job], near[job], far[job], *old)
+        last = stage == 2 and c == CHUNKS - 1
+        out = product(stage, place, blocks, current[job], near[job], far[job], *old, last=last)
         if stage == 0:
             firsts[c], out = order(*out)
         elif stage == 1:
             out = order(out)
         else:
-            out, squares = order(*out)
+            if last:
+                out = order(out)
+            else:
+                out, squares = order(*out)
             pieces[c][0] = out
             bit = groups // 2
             while bit:
@@ -327,7 +373,6 @@
     z_masks = [2 << i for i in range(lines.bit_length() - 1)]
     there = {d: 3.0 if d == 1 else 10.5 for d in range(1, groups)}
     mixed, mixes = None, 0
-    squares_ready = False
 
     def is_upper(d):
         return (my_group & (1 << (d.bit_length() - 1))) != 0
@@ -363,82 +408,73 @@
         if d:
             fields += list(order(*all_chunks(d)))
         if extra:
-            fields.append(squares)
+            fields += [pieces[-1][other] for other in range(1, groups) if other != d]
         half = jax.ShapeDtypeStruct((height // 2 + extra, columns), BF16)
         scratch = (pltpu.VMEM((height, columns), BF16),)
         name = "gram_pair" if d else "gram_own"
         clock.spend(3.2 if d else 3.0)
         return call(functools.partial(gram_kernel, d > 0, mask), name, (half, half), (where(d),), fields, scratch)
 
-    def level_process():
-        nonlocal squares
-        bit = 1
-        while bit < groups:
-            other = to_group(order(squares), bit)
-            clock.spend(1.5)
-            yield clock.now + (2.5 if bit == 1 else 7.0)
-            squares = squares + order(other)
-            clock.spend(0.6)
-            bit *= 2
-        nonlocal squares_ready
-        squares_ready = True
-
-    def process(d, masks, extra=0):
+    def process(d, masks, extra=0, round_y=False):
         nonlocal mixed, mixes, level
-        while d and (d not in pieces[-1] or there[d] > clock.now or extra and not squares_ready):
-            yield max(there[d], clock.now + 0.5)
+        need = list(there) if extra else [d] if d else []
+        while any(other not in pieces[-1] or there[other] > clock.now for other in need):
+            yield clock.now + 0.5
         mine, value = order(*gram_chunk(d, masks[0], extra))
-        terms = [(mine, 0)]
-        height, offset = mine.shape[0] - extra, 0
-
-        def carried(value):
-            rows = lax.slice_in_dim(value, value.shape[0] - extra, value.shape[0], axis=0)
-            return jnp.sum(rows.astype(F32), axis=0, keepdims=True)
-
+        terms = [mine]
+        height = mine.shape[0] - extra
+
+        def added(hop):
+            clock.spend(0.8)
+            final = hop == len(masks)
+            count = height if final else height + extra
+            outs = jax.ShapeDtypeStruct((count, columns), BF16)
+            args = list(terms)
+            if final and extra:
+                outs = (outs, jax.ShapeDtypeStruct((8, 128), F32))
+            elif final:
+                args.append(level)
+            kernel = functools.partial(
+                sum_kernel, masks, hop, extra, columns * groups * rows_total, rows_total
+            )
+            return call(kernel, "sum_last" if final else "sum_hop", outs, (where(d),), args)
+
+        for hop, mask in enumerate(masks):
+            if hop:
+                height //= 2
+                value = added(hop)
+            received, arrival = over_tiles(value, mask)
+            yield arrival if hop or mask > 1 else arrival - (3.0 if d else 6.0)
+            terms.append(order(received))
+        while level is None and not extra:
+            yield clock.now + 0.5
+        part = added(len(masks))
         if extra:
-            total = carried(mine)
-
-        def added(first_row, count):
-            clock.spend(1.0)
-            return sum(lax.dynamic_slice_in_dim(v, first_row - row, count, 0).astype(F32) for v, row in terms)
-
-        for i, mask in enumerate(masks):
-            if i:
-                height //= 2
-                keep = (my_tile // mask) % 2
-                value = added(offset + (1 - keep) * height, height).astype(BF16)
-                if extra:
-                    value = jnp.concatenate([value, extra_rows(total)], axis=0)
-                    clock.spend(1.0)
-                offset = offset + keep * height
-            received, arrival = over_tiles(value, mask)
-            yield arrival if i or mask > 1 else arrival - 3.0
-            received = order(received)
-            terms.append((received, offset))
-            if extra:
-                total = total + carried(received)
-        if extra:
-            level = total[0, 0] / (columns * groups * rows_total)
-        while level is None:
-            yield clock.now + 0.5
-        part = (added(offset, height) / (level * rows_total)).astype(BF16)
+            part, level = part
         for mask in masks[:0:-1]:
             received, arrival = over_tiles(part, mask)
             yield arrival
             part = jnp.concatenate([part, order(received)], axis=0)
-            clock.spend(0.7)
+            clock.spend(0.5)
         part = order(part)
         far, arrival = over_tiles(part, masks[0])
         if d:
             peer, peer_arrival = over_groups(part, d)
+        if round_y:
+            yield peer_arrival
+            peer = order(peer)
+            peer_far, peer_arrival = over_tiles(peer, masks[0])
         yield arrival
         far = order(far)
         parts = (part, far)
         if d:
-            peer_far, arrival = over_groups(far, d)
-            yield peer_arrival
-            peer = order(peer)
-            yield arrival
+            if not round_y:
+                peer_far, arrival = over_groups(far, d)
+                yield peer_arrival
+                peer = order(peer)
+                yield arrival
+            else:
+                yield peer_arrival
             peer_far = order(peer_far)
             parts += (peer, peer_far)
         first, last = mixes == 0, mixes == groups - 1
@@ -446,21 +482,24 @@
         shape = jax.ShapeDtypeStruct((rows, columns), BF16 if last else F32)
         scratch = (pltpu.VMEM((len(parts) * part.shape[0], columns), BF16),)
         args = (() if first else (mixed,)) + (*all_chunks(d), *parts)
-        scalars = (where(d),)
         if last:
-            scalars += (level.reshape(1),)
-            args += tuple(all_chunks(0))
+            args = (level, *args, *all_chunks(0))
         kernel = functools.partial(mix_kernel, d > 0, masks, first, last)
         name = "mix_pair" if d else "mix_own"
-        clock.spend(5.7 if d else 4.5)
-        mixed = call(kernel, name, shape, scalars, args, scratch, {} if first or last else {1: 0}, 28)
+        clock.spend(3.2)
+        mixed = call(kernel, name, shape, (where(d),), args, scratch, {} if first or last else {1: 0}, 28)
         if not last:
             mixed = order(mixed)
 
-    y_first, z_first, z_then_y = (1, *z_masks), (*z_masks, 1), (*z_masks[:1], 1, *z_masks[1:])
+    y_first, z_then_y, y_then_far = (1, *z_masks), (*z_masks[:1], 1, *z_masks[1:]), (1, *z_masks[::-1])
+    there[1] = 25.0
     queue = sorted(range(1, groups), key=lambda d: (d == 1, d))
-    processes = [panel_process(), level_process(), process(0, z_first)]
-    processes += [process(d, z_then_y if i == 0 else y_first, 0 if i else EXTRA) for i, d in enumerate(queue)]
+    carrier = queue[min(1, len(queue) - 1)]
+    processes = [panel_process()]
+    for d in queue:
+        first = d == queue[0] and d != carrier
+        processes.append(process(d, z_then_y if first else y_first, EXTRA if d == carrier else 0, first))
+    processes.append(process(0, y_then_far))
     clock.run(processes)
     return mixed
 

time: 308 us -> 297 us (0.964)
  other arithmetic: 22.5 us -> 1.68 us
  waiting for transfers between devices: 136 us -> 153 us
  starting transfers between devices: 95.9 us -> 83.9 us
  Pallas kernels: 38.9 us -> 45 us
    ppermute x24 -> x25, waiting for transfers between devices: 61.6 us -> 86.3 us  [over_tiles(): sent = lax.ppermute(value, 'elem', [(i, i ^ mask) for i in range(tiles)])]
    convert_element_type x14 -> x0, other arithmetic: 16 us -> none  [the longest x8 10.9 us: process(): value = added(offset + (1 - keep) * height, height).astype(BF16)]
    ppermute x20 -> x17, waiting for transfers between devices: 34.2 us -> 24.1 us  [to_group(): return lax.ppermute(value, 'orb', [(i, i ^ d) for i in range(groups)])]
    ppermute x24 -> x25, starting transfers between devices: 29.6 us -> 20.2 us  [over_tiles(): sent = lax.ppermute(value, 'elem', [(i, i ^ mask) for i in range(tiles)])]
    pallas_call x20 -> x32, Pallas kernels: 38.9 us -> 45 us  [call(): pl.pallas_call(kernel, out_shape=outs, in_specs=[pl.BlockSpec(memory_spac...]
    ppermute x12, waiting for transfers between devices: 15.5 us -> 19.6 us  [send_on(): far[job] = lax.ppermute(near[job], 'elem', outward)]
    ppermute x20 -> x17, starting transfers between devices: 11.7 us -> 10.7 us  [to_group(): return lax.ppermute(value, 'orb', [(i, i ^ d) for i in range(groups)])]
  transfers between devices with their start and end apart: 68 -> 66, of which waited for: 34 -> 33; matrix products, arithmetic and copies ran while one was open for 8% -> 2% of each run, Pallas kernels for 11% -> 12%
where the time goes in v7:
time: 297 us; the launch traced here: 296 us
  waiting for transfers between devices  153 us (52%)
  starting transfers between devices  83.9 us (28%)
  Pallas kernels  45 us (15%)
  local copies, waits for them, and re-layouts  11.5 us (4%)
    ppermute x25, waiting for transfers between devices, over_tiles(): sent = lax.ppermute(value, 'elem', [(i, i ^ mask) for i in range(tiles)])  86.3 us
    pallas_call x32, Pallas kernels, call(): pl.pallas_call(kernel, out_shape=outs, in_specs=[pl.BlockSpec(memory_spac...  45 us
    ppermute x17, waiting for transfers between devices, to_group(): return lax.ppermute(value, 'orb', [(i, i ^ d) for i in range(groups)])  24.1 us
    ppermute x8, starting transfers between devices, multiply(): near[stage + 1, c] = lax.ppermute(out, 'elem', swap)  23.8 us
    ppermute x12, starting transfers between devices, send_on(): far[job] = lax.ppermute(near[job], 'elem', outward)  22.6 us
    ppermute x25, starting transfers between devices, over_tiles(): sent = lax.ppermute(value, 'elem', [(i, i ^ mask) for i in range(tiles)])  20.2 us
    ppermute x12, waiting for transfers between devices, send_on(): far[job] = lax.ppermute(near[job], 'elem', outward)  19.6 us
    ppermute x8, waiting for transfers between devices, multiply(): near[stage + 1, c] = lax.ppermute(out, 'elem', swap)  10.9 us
  transfers between devices with their start and end apart: 66, of which 33 were waited for; matrix products, arithmetic and copies ran while one was open for 2% of the time, Pallas kernels for 12%

profile of v7, /device:TPU:0, one launch (start us, length us, event | category | flops | bytes accessed | tf_op | source)
XLA Modules:
  0.0 296.0 jit_solution(12265981620853608657)
XLA Ops:
  1.5 3.0 %collective-permute-start = (bf16[768,256]{1,0:T(8,128)(2,1)S(1)}, bf16[768,256]{1,0:T(8,128)(2,1)S(1)}, u32[]{:S(2)}, u32[]{:S(2)}) collective-permute-start(bf16[768,256]{1,0:T(8,128)(2,1)S(1)} %get-tuple-element.391.field_ref.refs_0_), channel_id=1, source_target_pairs={{0,4},{4,0},{8,12},{12,8},{16,20},{20,16},{24,28},{28,24},{1,5},{5... | collective-permute-start | bytes 1179656 | tf_op jit(solution)/shard_map/ppermute | solution.py:311
  4.5 2.2 slice_bitcast_fusion
  8.1 2.3 concatenate.34.blocks_ref
  10.5 3.9 %collective-permute-done.near_ref = bf16[768,256]{1,0:T(8,128)(2,1)S(1)} collective-permute-done((bf16[768,256]{1,0:T(8,128)(2,1)S(1)}, bf16[768,256]{1,0:T(8,128)(2,1)S(1)}, u32[]{:S(2)}, u32[]{:S(2)}) %collective-permute-start) | collective-permute-done | bytes 393248 | tf_op jit(solution)/shard_map/ppermute | solution.py:311
  14.5 2.1 collective-permute-start.1
  16.6 3.5 %collective-permute-start.4 = (bf16[768,256]{1,0:T(8,128)(2,1)S(1)}, bf16[768,256]{1,0:T(8,128)(2,1)S(1)}, u32[]{:S(2)}, u32[]{:S(2)}) collective-permute-start(bf16[768,256]{1,0:T(8,128)(2,1)S(1)} %get-tuple-element.212.field_ref.refs_0_), channel_id=1, source_target_pairs={{0,4},{4,0},{8,12},{12,8},{16,20},{20,16},{24,28},{28,24},{1,5},{5... | collective-permute-start | bytes 1179656 | tf_op jit(solution)/shard_map/ppermute | solution.py:316
  20.2 2.7 collective-permute-done.2.near_ref
  22.9 2.1 collective-permute-start.7
  27.0 4.3 %collective-permute-done.4.near_ref = bf16[768,256]{1,0:T(8,128)(2,1)S(1)} collective-permute-done((bf16[768,256]{1,0:T(8,128)(2,1)S(1)}, bf16[768,256]{1,0:T(8,128)(2,1)S(1)}, u32[]{:S(2)}, u32[]{:S(2)}) %collective-permute-start.4) | collective-permute-done | bytes 393248 | tf_op jit(solution)/shard_map/ppermute | solution.py:316
  31.3 2.1 collective-permute-start.5
  33.4 3.5 %collective-permute-start.3 = (bf16[768,256]{1,0:T(8,128)(2,1)S(1)}, bf16[768,256]{1,0:T(8,128)(2,1)S(1)}, u32[]{:S(2)}, u32[]{:S(2)}) collective-permute-start(bf16[768,256]{1,0:T(8,128)(2,1)S(1)} %get-tuple-element.211.field_ref), channel_id=1, source_target_pairs={{0,4},{4,0},{8,12},{12,8},{16,20},{20,16},{24,28},{28,24},{1,5},{5... | collective-permute-start | bytes 1179656 | tf_op jit(solution)/shard_map/ppermute | solution.py:360
  39.7 2.1 collective-permute-start.10
  41.9 3.5 %collective-permute-start.9 = (bf16[768,256]{1,0:T(8,128)(2,1)S(1)}, bf16[768,256]{1,0:T(8,128)(2,1)S(1)}, u32[]{:S(2)}, u32[]{:S(2)}) collective-permute-start(bf16[768,256]{1,0:T(8,128)(2,1)S(1)} %get-tuple-element.230.field_ref), channel_id=1, source_target_pairs={{0,4},{4,0},{8,12},{12,8},{16,20},{20,16},{24,28},{28,24},{1,5},{5... | collective-permute-start | bytes 1179656 | tf_op jit(solution)/shard_map/ppermute | solution.py:360
  48.2 2.1 collective-permute-start.8
  50.3 3.5 %collective-permute-start.12 = (bf16[768,256]{1,0:T(8,128)(2,1)S(1)}, bf16[768,256]{1,0:T(8,128)(2,1)S(1)}, u32[]{:S(2)}, u32[]{:S(2)}) collective-permute-start(bf16[768,256]{1,0:T(8,128)(2,1)S(1)} %get-tuple-element.242.field_ref), channel_id=1, source_target_pairs={{0,4},{4,0},{8,12},{12,8},{16,20},{20,16},{24,28},{28,24},{1,5},{5... | collective-permute-start | bytes 1179656 | tf_op jit(solution)/shard_map/ppermute | solution.py:360
  56.6 2.1 collective-permute-start.15
  58.7 3.5 %collective-permute-start.14 = (bf16[768,256]{1,0:T(8,128)(2,1)S(1)}, bf16[768,256]{1,0:T(8,128)(2,1)S(1)}, u32[]{:S(2)}, u32[]{:S(2)}) collective-permute-start(bf16[768,256]{1,0:T(8,128)(2,1)S(1)} %get-tuple-element.245.field_ref), channel_id=1, source_target_pairs={{0,4},{4,0},{8,12},{12,8},{16,20},{20,16},{24,28},{28,24},{1,5},{5... | collective-permute-start | bytes 1179656 | tf_op jit(solution)/shard_map/ppermute | solution.py:360
  65.0 2.1 collective-permute-start.13
  67.1 3.5 %collective-permute-start.11 = (bf16[768,256]{1,0:T(8,128)(2,1)S(1)}, bf16[768,256]{1,0:T(8,128)(2,1)S(1)}, u32[]{:S(2)}, u32[]{:S(2)}) collective-permute-start(bf16[768,256]{1,0:T(8,128)(2,1)S(1)} %product_1.4.field_ref), channel_id=1, source_target_pairs={{0,4},{4,0},{8,12},{12,8},{16,20},{20,16},{24,28},{28,24},{1,5},{5... | collective-permute-start | bytes 1179656 | tf_op jit(solution)/shard_map/ppermute | solution.py:360
  73.4 2.1 collective-permute-start.17
  75.5 1.6 collective-permute-start.18
  78.4 3.5 %collective-permute-done.11.near_ref = bf16[768,256]{1,0:T(8,128)(2,1)S(1)} collective-permute-done((bf16[768,256]{1,0:T(8,128)(2,1)S(1)}, bf16[768,256]{1,0:T(8,128)(2,1)S(1)}, u32[]{:S(2)}, u32[]{:S(2)}) %collective-permute-start.11) | collective-permute-done | bytes 393248 | tf_op jit(solution)/shard_map/ppermute | solution.py:360
  81.9 2.1 collective-permute-start.16
  84.0 3.5 %collective-permute-start.20 = (bf16[768,256]{1,0:T(8,128)(2,1)S(1)}, bf16[768,256]{1,0:T(8,128)(2,1)S(1)}, u32[]{:S(2)}, u32[]{:S(2)}) collective-permute-start(bf16[768,256]{1,0:T(8,128)(2,1)S(1)} %product_1.6.field_ref), channel_id=1, source_target_pairs={{0,4},{4,0},{8,12},{12,8},{16,20},{20,16},{24,28},{28,24},{1,5},{5... | collective-permute-start | bytes 1179656 | tf_op jit(solution)/shard_map/ppermute | solution.py:360
  90.3 2.1 collective-permute-start.19
  92.4 3.1 %collective-permute-done.16.far_ref = bf16[768,256]{1,0:T(8,128)(2,1)S(1)} collective-permute-done((bf16[768,256]{1,0:T(8,128)(2,1)S(1)}, bf16[768,256]{1,0:T(8,128)(2,1)S(1)}, u32[]{:S(2)}, u32[]{:S(2)}) %collective-permute-start.16) | collective-permute-done | bytes 393248 | tf_op jit(solution)/shard_map/ppermute | solution.py:325
  96.8 1.6 collective-permute-start.23
  98.8 2.0 collective-permute-start.21
  100.8 3.1 %collective-permute-done.19.far_ref = bf16[768,256]{1,0:T(8,128)(2,1)S(1)} collective-permute-done((bf16[768,256]{1,0:T(8,128)(2,1)S(1)}, bf16[768,256]{1,0:T(8,128)(2,1)S(1)}, u32[]{:S(2)}, u32[]{:S(2)}) %collective-permute-start.19) | collective-permute-done | bytes 393248 | tf_op jit(solution)/shard_map/ppermute | solution.py:325
  105.2 1.6 collective-permute-start.25
  106.8 4.4 %collective-permute-done.21.far_ref = bf16[768,256]{1,0:T(8,128)(2,1)S(1)} collective-permute-done((bf16[768,256]{1,0:T(8,128)(2,1)S(1)}, bf16[768,256]{1,0:T(8,128)(2,1)S(1)}, u32[]{:S(2)}, u32[]{:S(2)}) %collective-permute-start.21) | collective-permute-done | bytes 393248 | tf_op jit(solution)/shard_map/ppermute | solution.py:325
  114.1 8.3 %collective-permute-done.24.far_ref = bf16[768,256]{1,0:T(8,128)(2,1)S(1)} collective-permute-done((bf16[768,256]{1,0:T(8,128)(2,1)S(1)}, bf16[768,256]{1,0:T(8,128)(2,1)S(1)}, u32[]{:S(2)}, u32[]{:S(2)}) %collective-permute-start.24) | collective-permute-done | bytes 393248 | tf_op jit(solution)/shard_map/ppermute | solution.py:325
  123.9 2.1 gram_own.1
  128.7 6.1 %collective-permute-done.30.refs_7_.refs_9_.refs_4_ = bf16[784,256]{1,0:T(8,128)(2,1)S(1)} collective-permute-done((bf16[784,256]{1,0:T(8,128)(2,1)S(1)}, bf16[784,256]{1,0:T(8,128)(2,1)S(1)}, u32[]{:S(2)}, u32[]{:S(2)}) %collective-permute-start.30) | collective-permute-done | bytes 401440 | tf_op jit(solution)/shard_map/ppermute | solution.py:298
  138.1 4.9 %collective-permute-done.32.refs_1_ = bf16[384,1024]{1,0:T(8,128)(2,1)S(1)} collective-permute-done((bf16[384,1024]{1,0:T(8,128)(2,1)S(1)}, bf16[384,1024]{1,0:T(8,128)(2,1)S(1)}, u32[]{:S(2)}, u32[]{:S(2)}) %collective-permute-start.32) | collective-permute-done | bytes 786464 | tf_op jit(solution)/shard_map/ppermute | solution.py:387
  146.1 1.6 gram_pair.3
  147.8 2.4 gram_pair.4
  150.7 2.5 gram_pair.5
  153.2 1.8 collective-permute-start.41
  155.6 2.0 collective-permute-start.35
  157.6 7.2 %collective-permute-done.36.refs_1_ = bf16[256,1024]{1,0:T(8,128)(2,1)S(1)} collective-permute-done((bf16[256,1024]{1,0:T(8,128)(2,1)S(1)}, bf16[256,1024]{1,0:T(8,128)(2,1)S(1)}, u32[]{:S(2)}, u32[]{:S(2)}) %collective-permute-start.36) | collective-permute-done | bytes 524320 | tf_op jit(solution)/shard_map/ppermute | solution.py:387
  164.8 11.2 %collective-permute-done.35.refs_2_ = bf16[192,1024]{1,0:T(8,128)(2,1)S(1)} collective-permute-done((bf16[192,1024]{1,0:T(8,128)(2,1)S(1)}, bf16[192,1024]{1,0:T(8,128)(2,1)S(1)}, u32[]{:S(2)}, u32[]{:S(2)}) %collective-permute-start.35) | collective-permute-done | bytes 393248 | tf_op jit(solution)/shard_map/ppermute | solution.py:387
  177.4 2.1 collective-permute-start.44
  179.5 7.2 %collective-permute-done.40.refs_2_ = bf16[144,1024]{1,0:T(8,128)(2,1)S(1)} collective-permute-done((bf16[144,1024]{1,0:T(8,128)(2,1)S(1)}, bf16[144,1024]{1,0:T(8,128)(2,1)S(1)}, u32[]{:S(2)}, u32[]{:S(2)}) %collective-permute-start.40) | collective-permute-done | bytes 294944 | tf_op jit(solution)/shard_map/ppermute | solution.py:387
  187.4 4.8 %collective-permute-done.44.refs_2_ = bf16[128,1024]{1,0:T(8,128)(2,1)S(1)} collective-permute-done((bf16[128,1024]{1,0:T(8,128)(2,1)S(1)}, bf16[128,1024]{1,0:T(8,128)(2,1)S(1)}, u32[]{:S(2)}, u32[]{:S(2)}) %collective-permute-start.44) | collective-permute-done | bytes 262176 | tf_op jit(solution)/shard_map/ppermute | solution.py:387
  193.0 8.0 %collective-permute-done.46.refs_3_ = bf16[64,1024]{1,0:T(8,128)(2,1)S(1)} collective-permute-done((bf16[64,1024]{1,0:T(8,128)(2,1)S(1)}, bf16[64,1024]{1,0:T(8,128)(2,1)S(1)}, u32[]{:S(2)}, u32[]{:S(2)}) %collective-permute-start.46) | collective-permute-done | bytes 131104 | tf_op jit(solution)/shard_map/ppermute | solution.py:387
  203.4 6.4 %collective-permute-done.48 = bf16[64,1024]{1,0:T(8,128)(2,1)S(1)} collective-permute-done((bf16[64,1024]{1,0:T(8,128)(2,1)S(1)}, bf16[64,1024]{1,0:T(8,128)(2,1)S(1)}, u32[]{:S(2)}, u32[]{:S(2)}) %collective-permute-start.48) | collective-permute-done | bytes 131104 | tf_op jit(solution)/shard_map/ppermute | solution.py:387
  210.5 2.1 collective-permute-start.42
  213.3 2.9 collective-permute-start.50
  216.2 7.4 %collective-permute-done.47.refs_3_ = bf16[64,1024]{1,0:T(8,128)(2,1)S(1)} collective-permute-done((bf16[64,1024]{1,0:T(8,128)(2,1)S(1)}, bf16[64,1024]{1,0:T(8,128)(2,1)S(1)}, u32[]{:S(2)}, u32[]{:S(2)}) %collective-permute-start.47) | collective-permute-done | bytes 131104 | tf_op jit(solution)/shard_map/ppermute | solution.py:387
  223.6 4.0 %collective-permute-done.42.refs_3_ = bf16[96,1024]{1,0:T(8,128)(2,1)S(1)} collective-permute-done((bf16[96,1024]{1,0:T(8,128)(2,1)S(1)}, bf16[96,1024]{1,0:T(8,128)(2,1)S(1)}, u32[]{:S(2)}, u32[]{:S(2)}) %collective-permute-start.42) | collective-permute-done | bytes 196640 | tf_op jit(solution)/shard_map/ppermute | solution.py:387
  231.7 3.3 %collective-permute-done.49 = bf16[64,1024]{1,0:T(8,128)(2,1)S(1)} collective-permute-done((bf16[64,1024]{1,0:T(8,128)(2,1)S(1)}, bf16[64,1024]{1,0:T(8,128)(2,1)S(1)}, u32[]{:S(2)}, u32[]{:S(2)}) %collective-permute-start.49) | collective-permute-done | bytes 131104 | tf_op jit(solution)/shard_map/ppermute | solution.py:387
  235.4 3.0 %collective-permute-done.51 = bf16[96,1024]{1,0:T(8,128)(2,1)S(1)} collective-permute-done((bf16[96,1024]{1,0:T(8,128)(2,1)S(1)}, bf16[96,1024]{1,0:T(8,128)(2,1)S(1)}, u32[]{:S(2)}, u32[]{:S(2)}) %collective-permute-start.51) | collective-permute-done | bytes 196640 | tf_op jit(solution)/shard_map/ppermute | solution.py:387
  238.4 1.6 collective-permute-start.64
  240.0 6.3 %collective-permute-done.54 = bf16[128,1024]{1,0:T(8,128)(2,1)S(1)} collective-permute-done((bf16[128,1024]{1,0:T(8,128)(2,1)S(1)}, bf16[128,1024]{1,0:T(8,128)(2,1)S(1)}, u32[]{:S(2)}, u32[]{:S(2)}) %collective-permute-start.54) | collective-permute-done | bytes 262176 | tf_op jit(solution)/shard_map/ppermute | solution.py:387
  248.9 7.6 %collective-permute-done.64 = bf16[192,1024]{1,0:T(8,128)(2,1)S(1)} collective-permute-done((bf16[192,1024]{1,0:T(8,128)(2,1)S(1)}, bf16[192,1024]{1,0:T(8,128)(2,1)S(1)}, u32[]{:S(2)}, u32[]{:S(2)}) %collective-permute-start.64) | collective-permute-done | bytes 393248 | tf_op jit(solution)/shard_map/ppermute | solution.py:387
  256.9 4.1 %collective-permute-done.58.refs_6_ = bf16[256,1024]{1,0:T(8,128)(2,1)S(1)} collective-permute-done((bf16[256,1024]{1,0:T(8,128)(2,1)S(1)}, bf16[256,1024]{1,0:T(8,128)(2,1)S(1)}, u32[]{:S(2)}, u32[]{:S(2)}) %collective-permute-start.58) | collective-permute-done | bytes 524320 | tf_op jit(solution)/shard_map/ppermute | solution.py:387
  261.0 1.7 collective-permute-start.60
  264.8 10.3 %collective-permute-done.59.refs_7_ = bf16[256,1024]{1,0:T(8,128)(2,1)S(1)} collective-permute-done((bf16[256,1024]{1,0:T(8,128)(2,1)S(1)}, bf16[256,1024]{1,0:T(8,128)(2,1)S(1)}, u32[]{:S(2)}, u32[]{:S(2)}) %collective-permute-start.59) | collective-permute-done | bytes 524320 | tf_op jit(solution)/shard_map/ppermute | solution.py:298
  275.1 3.4 %mix_pair.3.refs_0_ = f32[768,1024]{1,0:T(8,128)S(1)} custom-call(s32[2]{0:T(128)S(1)} %pad_add_fusion.3.where_ref, bf16[768,256]{1,0:T(8,128)(2,1)} %collective-permute-done.37.refs_4_.refs_0_, bf16[768,256]{1,0:T(8,128)(2,1)} %collective-permute-done.38.refs_5_.refs_1_, bf16[768,256]{1,0:T(8,128)(2,1)} %collective-permute-done.39.refs_6_.refs_2_, ...), custom_call_target="tpu_custom_call" | custom-call | flops 1024 | bytes 1024 | tf_op jit(solution)/shard_map/mix_pair/pallas_call | solution.py:96
  278.5 7.6 %collective-permute-done.60.refs_8_ = bf16[256,1024]{1,0:T(8,128)(2,1)S(1)} collective-permute-done((bf16[256,1024]{1,0:T(8,128)(2,1)S(1)}, bf16[256,1024]{1,0:T(8,128)(2,1)S(1)}, u32[]{:S(2)}, u32[]{:S(2)}) %collective-permute-start.60) | collective-permute-done | bytes 524320 | tf_op jit(solution)/shard_map/ppermute | solution.py:298
  286.1 3.4 %mix_pair.4.refs_0_ = f32[768,1024]{1,0:T(8,128)S(1)} custom-call(s32[2]{0:T(128)S(1)} %pad_add_fusion.2.where_ref, f32[768,1024]{1,0:T(8,128)S(1)} %mix_pair.3.refs_0_, bf16[768,256]{1,0:T(8,128)(2,1)S(1)} %copy-done.1, bf16[768,256]{1,0:T(8,128)(2,1)S(1)} %copy-done.3, bf16[768,256]{1,0:T(8,128)(2,1)S(1)} %copy-done.5, ...), custom_call_target="tpu_custom_call", output_to_operand_aliasing={{}: (1, {})} | custom-call | flops 1024 | bytes 1024 | tf_op jit(solution)/shard_map/mix_pair/pallas_call | solution.py:96
  289.5 2.7 mix_pair.5.refs_1_
  292.2 3.8 %mix_own.1 = bf16[768,1024]{1,0:T(8,128)(2,1)} custom-call(s32[2]{0:T(128)S(1)} %copy-done.16, f32[8,128]{1,0:T(8,128)S(1)} %get-tuple-element.358.refs_4_.refs_0_, f32[768,1024]{1,0:T(8,128)S(1)} %mix_pair.5.refs_1_, bf16[768,256]{1,0:T(8,128)(2,1)S(1)} %get-tuple-element.268.refs_0_.refs_2_.refs_8_, ...), custom_call_target="tpu_custom_call" | custom-call | flops 1024 | bytes 1024 | tf_op jit(solution)/shard_map/mix_own/pallas_call | solution.py:96
  (159 shorter events, 56.7 us)
Async XLA Ops:
  1.5 13.0 %collective-permute-start = (bf16[768,256]{1,0:T(8,128)(2,1)S(1)}, bf16[768,256]{1,0:T(8,128)(2,1)S(1)}, u32[]{:S(2)}, u32[]{:S(2)}) collective-permute-start(bf16[768,256]{1,0:T(8,128)(2,1)S(1)} %get-tuple-element.391.field_ref.refs_0_), channel_id=1, source_target_pairs={{0,4},{4,0},{8,12},{12,8},{16,20},{20,16},{24,28},{28,24},{1,5},{5... | collective-permute-start | bytes 1179656 | tf_op jit(solution)/shard_map/ppermute | solution.py:311
  10.5 12.4 %collective-permute-start.2 = (bf16[768,256]{1,0:T(8,128)(2,1)S(1)}, bf16[768,256]{1,0:T(8,128)(2,1)S(1)}, u32[]{:S(2)}, u32[]{:S(2)}) collective-permute-start(bf16[768,256]{1,0:T(8,128)(2,1)S(1)} %get-tuple-element.204.field_ref.refs_0_), channel_id=1, source_target_pairs={{0,4},{4,0},{8,12},{12,8},{16,20},{20,16},{24,28},{28,24},{1,5},{5... | collective-permute-start | bytes 1179656 | tf_op jit(solution)/shard_map/ppermute | solution.py:316
  14.5 11.3 %collective-permute-start.1 = (bf16[768,256]{1,0:T(8,128)(2,1)S(1)}, bf16[768,256]{1,0:T(8,128)(2,1)S(1)}, u32[]{:S(2)}, u32[]{:S(2)}) collective-permute-start(bf16[768,256]{1,0:T(8,128)(2,1)S(1)} %collective-permute-done.near_ref), channel_id=1, source_target_pairs={{0,8},{4,28},{8,16},{12,4},{16,24},{20,12},{24,0},{28,20},{1,9},{5... | collective-permute-start | bytes 1179656 | tf_op jit(solution)/shard_map/ppermute | solution.py:325
  16.6 14.7 %collective-permute-start.4 = (bf16[768,256]{1,0:T(8,128)(2,1)S(1)}, bf16[768,256]{1,0:T(8,128)(2,1)S(1)}, u32[]{:S(2)}, u32[]{:S(2)}) collective-permute-start(bf16[768,256]{1,0:T(8,128)(2,1)S(1)} %get-tuple-element.212.field_ref.refs_0_), channel_id=1, source_target_pairs={{0,4},{4,0},{8,12},{12,8},{16,20},{20,16},{24,28},{28,24},{1,5},{5... | collective-permute-start | bytes 1179656 | tf_op jit(solution)/shard_map/ppermute | solution.py:316
  20.1 19.6 %collective-permute-start.6 = (bf16[768,256]{1,0:T(8,128)(2,1)S(1)}, bf16[768,256]{1,0:T(8,128)(2,1)S(1)}, u32[]{:S(2)}, u32[]{:S(2)}) collective-permute-start(bf16[768,256]{1,0:T(8,128)(2,1)S(1)} %get-tuple-element.215.field_ref.refs_0_), channel_id=1, source_target_pairs={{0,4},{4,0},{8,12},{12,8},{16,20},{20,16},{24,28},{28,24},{1,5},{5... | collective-permute-start | bytes 1179656 | tf_op jit(solution)/shard_map/ppermute | solution.py:316
  22.9 14.1 %collective-permute-start.7 = (bf16[768,256]{1,0:T(8,128)(2,1)S(1)}, bf16[768,256]{1,0:T(8,128)(2,1)S(1)}, u32[]{:S(2)}, u32[]{:S(2)}) collective-permute-start(bf16[768,256]{1,0:T(8,128)(2,1)S(1)} %collective-permute-done.2.near_ref), channel_id=1, source_target_pairs={{0,8},{4,28},{8,16},{12,4},{16,24},{20,12},{24,0},{28,20},{1,9},{5... | collective-permute-start | bytes 1179656 | tf_op jit(solution)/shard_map/ppermute | solution.py:325
  31.3 14.1 %collective-permute-start.5 = (bf16[768,256]{1,0:T(8,128)(2,1)S(1)}, bf16[768,256]{1,0:T(8,128)(2,1)S(1)}, u32[]{:S(2)}, u32[]{:S(2)}) collective-permute-start(bf16[768,256]{1,0:T(8,128)(2,1)S(1)} %collective-permute-done.4.near_ref), channel_id=1, source_target_pairs={{0,8},{4,28},{8,16},{12,4},{16,24},{20,12},{24,0},{28,20},{1,9},{5... | collective-permute-start | bytes 1179656 | tf_op jit(solution)/shard_map/ppermute | solution.py:325
  33.4 14.7 %collective-permute-start.3 = (bf16[768,256]{1,0:T(8,128)(2,1)S(1)}, bf16[768,256]{1,0:T(8,128)(2,1)S(1)}, u32[]{:S(2)}, u32[]{:S(2)}) collective-permute-start(bf16[768,256]{1,0:T(8,128)(2,1)S(1)} %get-tuple-element.211.field_ref), channel_id=1, source_target_pairs={{0,4},{4,0},{8,12},{12,8},{16,20},{20,16},{24,28},{28,24},{1,5},{5... | collective-permute-start | bytes 1179656 | tf_op jit(solution)/shard_map/ppermute | solution.py:360
  39.7 14.1 %collective-permute-start.10 = (bf16[768,256]{1,0:T(8,128)(2,1)S(1)}, bf16[768,256]{1,0:T(8,128)(2,1)S(1)}, u32[]{:S(2)}, u32[]{:S(2)}) collective-permute-start(bf16[768,256]{1,0:T(8,128)(2,1)S(1)} %collective-permute-done.6.near_ref), channel_id=1, source_target_pairs={{0,8},{4,28},{8,16},{12,4},{16,24},{20,12},{24,0},{28,20},{1,9},{5... | collective-permute-start | bytes 1179656 | tf_op jit(solution)/shard_map/ppermute | solution.py:325
  41.9 14.7 %collective-permute-start.9 = (bf16[768,256]{1,0:T(8,128)(2,1)S(1)}, bf16[768,256]{1,0:T(8,128)(2,1)S(1)}, u32[]{:S(2)}, u32[]{:S(2)}) collective-permute-start(bf16[768,256]{1,0:T(8,128)(2,1)S(1)} %get-tuple-element.230.field_ref), channel_id=1, source_target_pairs={{0,4},{4,0},{8,12},{12,8},{16,20},{20,16},{24,28},{28,24},{1,5},{5... | collective-permute-start | bytes 1179656 | tf_op jit(solution)/shard_map/ppermute | solution.py:360
  48.2 14.1 %collective-permute-start.8 = (bf16[768,256]{1,0:T(8,128)(2,1)S(1)}, bf16[768,256]{1,0:T(8,128)(2,1)S(1)}, u32[]{:S(2)}, u32[]{:S(2)}) collective-permute-start(bf16[768,256]{1,0:T(8,128)(2,1)S(1)} %collective-permute-done.3.near_ref), channel_id=1, source_target_pairs={{0,8},{4,28},{8,16},{12,4},{16,24},{20,12},{24,0},{28,20},{1,9},{5... | collective-permute-start | bytes 1179656 | tf_op jit(solution)/shard_map/ppermute | solution.py:325
  50.3 14.7 %collective-permute-start.12 = (bf16[768,256]{1,0:T(8,128)(2,1)S(1)}, bf16[768,256]{1,0:T(8,128)(2,1)S(1)}, u32[]{:S(2)}, u32[]{:S(2)}) collective-permute-start(bf16[768,256]{1,0:T(8,128)(2,1)S(1)} %get-tuple-element.242.field_ref), channel_id=1, source_target_pairs={{0,4},{4,0},{8,12},{12,8},{16,20},{20,16},{24,28},{28,24},{1,5},{5... | collective-permute-start | bytes 1179656 | tf_op jit(solution)/shard_map/ppermute | solution.py:360
  56.6 14.1 %collective-permute-start.15 = (bf16[768,256]{1,0:T(8,128)(2,1)S(1)}, bf16[768,256]{1,0:T(8,128)(2,1)S(1)}, u32[]{:S(2)}, u32[]{:S(2)}) collective-permute-start(bf16[768,256]{1,0:T(8,128)(2,1)S(1)} %collective-permute-done.9.near_ref), channel_id=1, source_target_pairs={{0,8},{4,28},{8,16},{12,4},{16,24},{20,12},{24,0},{28,20},{1,9},{5... | collective-permute-start | bytes 1179656 | tf_op jit(solution)/shard_map/ppermute | solution.py:325
  58.7 14.7 %collective-permute-start.14 = (bf16[768,256]{1,0:T(8,128)(2,1)S(1)}, bf16[768,256]{1,0:T(8,128)(2,1)S(1)}, u32[]{:S(2)}, u32[]{:S(2)}) collective-permute-start(bf16[768,256]{1,0:T(8,128)(2,1)S(1)} %get-tuple-element.245.field_ref), channel_id=1, source_target_pairs={{0,4},{4,0},{8,12},{12,8},{16,20},{20,16},{24,28},{28,24},{1,5},{5... | collective-permute-start | bytes 1179656 | tf_op jit(solution)/shard_map/ppermute | solution.py:360
  65.0 12.1 %collective-permute-start.13 = (bf16[768,256]{1,0:T(8,128)(2,1)S(1)}, bf16[768,256]{1,0:T(8,128)(2,1)S(1)}, u32[]{:S(2)}, u32[]{:S(2)}) collective-permute-start(bf16[768,256]{1,0:T(8,128)(2,1)S(1)} %collective-permute-done.12.near_ref), channel_id=1, source_target_pairs={{0,8},{4,28},{8,16},{12,4},{16,24},{20,12},{24,0},{28,20},{1,9},{5... | collective-permute-start | bytes 1179656 | tf_op jit(solution)/shard_map/ppermute | solution.py:325
  67.1 14.7 %collective-permute-start.11 = (bf16[768,256]{1,0:T(8,128)(2,1)S(1)}, bf16[768,256]{1,0:T(8,128)(2,1)S(1)}, u32[]{:S(2)}, u32[]{:S(2)}) collective-permute-start(bf16[768,256]{1,0:T(8,128)(2,1)S(1)} %product_1.4.field_ref), channel_id=1, source_target_pairs={{0,4},{4,0},{8,12},{12,8},{16,20},{20,16},{24,28},{28,24},{1,5},{5... | collective-permute-start | bytes 1179656 | tf_op jit(solution)/shard_map/ppermute | solution.py:360
  73.4 16.9 %collective-permute-start.17 = (bf16[768,256]{1,0:T(8,128)(2,1)S(1)}, bf16[768,256]{1,0:T(8,128)(2,1)S(1)}, u32[]{:S(2)}, u32[]{:S(2)}) collective-permute-start(bf16[768,256]{1,0:T(8,128)(2,1)S(1)} %product_1.5.field_ref), channel_id=1, source_target_pairs={{0,4},{4,0},{8,12},{12,8},{16,20},{20,16},{24,28},{28,24},{1,5},{5... | collective-permute-start | bytes 1179656 | tf_op jit(solution)/shard_map/ppermute | solution.py:360
  75.5 12.0 %collective-permute-start.18 = (bf16[768,256]{1,0:T(8,128)(2,1)S(1)}, bf16[768,256]{1,0:T(8,128)(2,1)S(1)}, u32[]{:S(2)}, u32[]{:S(2)}) collective-permute-start(bf16[768,256]{1,0:T(8,128)(2,1)S(1)} %collective-permute-done.14.near_ref), channel_id=1, source_target_pairs={{0,8},{4,28},{8,16},{12,4},{16,24},{20,12},{24,0},{28,20},{1,9},{5... | collective-permute-start | bytes 1179656 | tf_op jit(solution)/shard_map/ppermute | solution.py:325
  81.9 13.6 %collective-permute-start.16 = (bf16[768,256]{1,0:T(8,128)(2,1)S(1)}, bf16[768,256]{1,0:T(8,128)(2,1)S(1)}, u32[]{:S(2)}, u32[]{:S(2)}) collective-permute-start(bf16[768,256]{1,0:T(8,128)(2,1)S(1)} %collective-permute-done.11.near_ref), channel_id=1, source_target_pairs={{0,8},{4,28},{8,16},{12,4},{16,24},{20,12},{24,0},{28,20},{1,9},{5... | collective-permute-start | bytes 1179656 | tf_op jit(solution)/shard_map/ppermute | solution.py:325
  84.0 14.8 %collective-permute-start.20 = (bf16[768,256]{1,0:T(8,128)(2,1)S(1)}, bf16[768,256]{1,0:T(8,128)(2,1)S(1)}, u32[]{:S(2)}, u32[]{:S(2)}) collective-permute-start(bf16[768,256]{1,0:T(8,128)(2,1)S(1)} %product_1.6.field_ref), channel_id=1, source_target_pairs={{0,4},{4,0},{8,12},{12,8},{16,20},{20,16},{24,28},{28,24},{1,5},{5... | collective-permute-start | bytes 1179656 | tf_op jit(solution)/shard_map/ppermute | solution.py:360
  90.3 13.6 %collective-permute-start.19 = (bf16[768,256]{1,0:T(8,128)(2,1)S(1)}, bf16[768,256]{1,0:T(8,128)(2,1)S(1)}, u32[]{:S(2)}, u32[]{:S(2)}) collective-permute-start(bf16[768,256]{1,0:T(8,128)(2,1)S(1)} %collective-permute-done.17.near_ref), channel_id=1, source_target_pairs={{0,8},{4,28},{8,16},{12,4},{16,24},{20,12},{24,0},{28,20},{1,9},{5... | collective-permute-start | bytes 1179656 | tf_op jit(solution)/shard_map/ppermute | solution.py:325
  96.8 10.0 %collective-permute-start.23 = (bf16[768,256]{1,0:T(8,128)(2,1)S(1)}, bf16[768,256]{1,0:T(8,128)(2,1)S(1)}, u32[]{:S(2)}, u32[]{:S(2)}) collective-permute-start(bf16[768,256]{1,0:T(8,128)(2,1)S(1)} %get-tuple-element.268.refs_0_.refs_2_.refs_8_), channel_id=1, source_target_pairs={{0,2},{1,3},{2,0},{3,1},{4,6},{5,7},{6,4},{7,5},{8,10},{9,11},{10,... | collective-permute-start | bytes 1179656 | tf_op jit(solution)/shard_map/ppermute | solution.py:298
  98.4 8.4 %collective-permute-start.22 = (bf16[768,256]{1,0:T(8,128)(2,1)S(1)}, bf16[768,256]{1,0:T(8,128)(2,1)S(1)}, u32[]{:S(2)}, u32[]{:S(2)}) collective-permute-start(bf16[768,256]{1,0:T(8,128)(2,1)S(1)} %product_1.7.field_ref), channel_id=1, source_target_pairs={{0,4},{4,0},{8,12},{12,8},{16,20},{20,16},{24,28},{28,24},{1,5},{5... | collective-permute-start | bytes 1179656 | tf_op jit(solution)/shard_map/ppermute | solution.py:360
  98.8 12.4 %collective-permute-start.21 = (bf16[768,256]{1,0:T(8,128)(2,1)S(1)}, bf16[768,256]{1,0:T(8,128)(2,1)S(1)}, u32[]{:S(2)}, u32[]{:S(2)}) collective-permute-start(bf16[768,256]{1,0:T(8,128)(2,1)S(1)} %collective-permute-done.20.near_ref), channel_id=1, source_target_pairs={{0,8},{4,28},{8,16},{12,4},{16,24},{20,12},{24,0},{28,20},{1,9},{5... | collective-permute-start | bytes 1179656 | tf_op jit(solution)/shard_map/ppermute | solution.py:325
  105.2 8.9 %collective-permute-start.25 = (bf16[768,256]{1,0:T(8,128)(2,1)S(1)}, bf16[768,256]{1,0:T(8,128)(2,1)S(1)}, u32[]{:S(2)}, u32[]{:S(2)}) collective-permute-start(bf16[768,256]{1,0:T(8,128)(2,1)S(1)} %get-tuple-element.279.refs_1_.refs_3_.refs_9_), channel_id=1, source_target_pairs={{0,2},{1,3},{2,0},{3,1},{4,6},{5,7},{6,4},{7,5},{8,10},{9,11},{10,... | collective-permute-start | bytes 1179656 | tf_op jit(solution)/shard_map/ppermute | solution.py:298
  111.2 11.2 %collective-permute-start.24 = (bf16[768,256]{1,0:T(8,128)(2,1)S(1)}, bf16[768,256]{1,0:T(8,128)(2,1)S(1)}, u32[]{:S(2)}, u32[]{:S(2)}) collective-permute-start(bf16[768,256]{1,0:T(8,128)(2,1)S(1)} %collective-permute-done.22.near_ref), channel_id=1, source_target_pairs={{0,8},{4,28},{8,16},{12,4},{16,24},{20,12},{24,0},{28,20},{1,9},{5... | collective-permute-start | bytes 1179656 | tf_op jit(solution)/shard_map/ppermute | solution.py:325
  112.5 11.4 %collective-permute-start.28 = (bf16[768,256]{1,0:T(8,128)(2,1)S(1)}, bf16[768,256]{1,0:T(8,128)(2,1)S(1)}, u32[]{:S(2)}, u32[]{:S(2)}) collective-permute-start(bf16[768,256]{1,0:T(8,128)(2,1)S(1)} %get-tuple-element.291.refs_2_.refs_4_.refs_10_), channel_id=1, source_target_pairs={{0,2},{1,3},{2,0},{3,1},{4,6},{5,7},{6,4},{7,5},{8,10},{9,11},{10,... | collective-permute-start | bytes 1179656 | tf_op jit(solution)/shard_map/ppermute | solution.py:298
  126.0 17.0 %collective-permute-start.32 = (bf16[384,1024]{1,0:T(8,128)(2,1)S(1)}, bf16[384,1024]{1,0:T(8,128)(2,1)S(1)}, u32[]{:S(2)}, u32[]{:S(2)}) collective-permute-start(bf16[384,1024]{1,0:T(8,128)(2,1)S(1)} %get-tuple-element.309), channel_id=1, source_target_pairs={{0,4},{4,0},{8,12},{12,8},{16,20},{20,16},{24,28},{28,24},{1,5},{5... | collective-permute-start | bytes 2359304 | tf_op jit(solution)/shard_map/ppermute | solution.py:387
  126.6 8.2 %collective-permute-start.30 = (bf16[784,256]{1,0:T(8,128)(2,1)S(1)}, bf16[784,256]{1,0:T(8,128)(2,1)S(1)}, u32[]{:S(2)}, u32[]{:S(2)}) collective-permute-start(bf16[784,256]{1,0:T(8,128)(2,1)S(1)} %product_2.7.refs_3_.refs_5_.refs_11_), channel_id=1, source_target_pairs={{0,2},{1,3},{2,0},{3,1},{4,6},{5,7},{6,4},{7,5},{8,10},{9,11},{10,... | collective-permute-start | bytes 1204232 | tf_op jit(solution)/shard_map/ppermute | solution.py:298
  128.1 7.9 %collective-permute-start.27 = (bf16[768,256]{1,0:T(8,128)(2,1)S(1)}, bf16[768,256]{1,0:T(8,128)(2,1)S(1)}, u32[]{:S(2)}, u32[]{:S(2)}) collective-permute-start(bf16[768,256]{1,0:T(8,128)(2,1)S(1)} %collective-permute-done.25.refs_5_.refs_2_), channel_id=1, source_target_pairs={{0,1},{1,0},{2,3},{3,2},{4,5},{5,4},{6,7},{7,6},{8,9},{9,8},{10,11... | collective-permute-start | bytes 1179656 | tf_op jit(solution)/shard_map/ppermute | solution.py:298
  128.6 8.2 %collective-permute-start.29 = (bf16[768,256]{1,0:T(8,128)(2,1)S(1)}, bf16[768,256]{1,0:T(8,128)(2,1)S(1)}, u32[]{:S(2)}, u32[]{:S(2)}) collective-permute-start(bf16[768,256]{1,0:T(8,128)(2,1)S(1)} %collective-permute-done.28.refs_6_.refs_3_), channel_id=1, source_target_pairs={{0,1},{1,0},{2,3},{3,2},{4,5},{5,4},{6,7},{7,6},{8,9},{9,8},{10,11... | collective-permute-start | bytes 1179656 | tf_op jit(solution)/shard_map/ppermute | solution.py:298
  134.8 12.9 %collective-permute-start.31 = (bf16[784,256]{1,0:T(8,128)(2,1)S(1)}, bf16[784,256]{1,0:T(8,128)(2,1)}, u32[]{:S(2)}, u32[]{:S(2)}) collective-permute-start(bf16[784,256]{1,0:T(8,128)(2,1)S(1)} %collective-permute-done.30.refs_7_.refs_9_.refs_4_), channel_id=1, source_target_pairs={{0,1},{1,0},{2,3},{3,2},{4,5},{5,4},{6,7},{7,6},{8,9},{9,8},{10,11... | collective-permute-start | bytes 1204232 | tf_op jit(solution)/shard_map/ppermute | solution.py:298
  135.6 12.2 %collective-permute-start.33 = (bf16[784,256]{1,0:T(8,128)(2,1)S(1)}, bf16[784,256]{1,0:T(8,128)(2,1)}, u32[]{:S(2)}, u32[]{:S(2)}) collective-permute-start(bf16[784,256]{1,0:T(8,128)(2,1)S(1)} %product_2.7.refs_3_.refs_5_.refs_11_), channel_id=1, source_target_pairs={{0,1},{1,0},{2,3},{3,2},{4,5},{5,4},{6,7},{7,6},{8,9},{9,8},{10,11... | collective-permute-start | bytes 1204232 | tf_op jit(solution)/shard_map/ppermute | solution.py:298
  136.9 13.8 %collective-permute-start.37 = (bf16[768,256]{1,0:T(8,128)(2,1)S(1)}, bf16[768,256]{1,0:T(8,128)(2,1)}, u32[]{:S(2)}, u32[]{:S(2)}) collective-permute-start(bf16[768,256]{1,0:T(8,128)(2,1)S(1)} %get-tuple-element.268.refs_0_.refs_2_.refs_8_), channel_id=1, source_target_pairs={{0,1},{1,0},{2,3},{3,2},{4,5},{5,4},{6,7},{7,6},{8,9},{9,8},{10,11... | collective-permute-start | bytes 1179656 | tf_op jit(solution)/shard_map/ppermute | solution.py:298
  137.6 13.1 %collective-permute-start.38 = (bf16[768,256]{1,0:T(8,128)(2,1)S(1)}, bf16[768,256]{1,0:T(8,128)(2,1)}, u32[]{:S(2)}, u32[]{:S(2)}) collective-permute-start(bf16[768,256]{1,0:T(8,128)(2,1)S(1)} %get-tuple-element.279.refs_1_.refs_3_.refs_9_), channel_id=1, source_target_pairs={{0,1},{1,0},{2,3},{3,2},{4,5},{5,4},{6,7},{7,6},{8,9},{9,8},{10,11... | collective-permute-start | bytes 1179656 | tf_op jit(solution)/shard_map/ppermute | solution.py:298
  143.0 7.7 %collective-permute-start.39 = (bf16[768,256]{1,0:T(8,128)(2,1)S(1)}, bf16[768,256]{1,0:T(8,128)(2,1)}, u32[]{:S(2)}, u32[]{:S(2)}) collective-permute-start(bf16[768,256]{1,0:T(8,128)(2,1)S(1)} %get-tuple-element.291.refs_2_.refs_4_.refs_10_), channel_id=1, source_target_pairs={{0,1},{1,0},{2,3},{3,2},{4,5},{5,4},{6,7},{7,6},{8,9},{9,8},{10,11... | collective-permute-start | bytes 1179656 | tf_op jit(solution)/shard_map/ppermute | solution.py:298
  147.7 17.1 %collective-permute-start.36 = (bf16[256,1024]{1,0:T(8,128)(2,1)S(1)}, bf16[256,1024]{1,0:T(8,128)(2,1)S(1)}, u32[]{:S(2)}, u32[]{:S(2)}) collective-permute-start(bf16[256,1024]{1,0:T(8,128)(2,1)S(1)} %get-tuple-element.331), channel_id=1, source_target_pairs={{0,8},{4,12},{8,0},{12,4},{16,24},{20,28},{24,16},{28,20},{1,9},{5... | collective-permute-start | bytes 1572872 | tf_op jit(solution)/shard_map/ppermute | solution.py:387
  150.2 25.8 %collective-permute-start.34 = (bf16[272,1024]{1,0:T(8,128)(2,1)S(1)}, bf16[272,1024]{1,0:T(8,128)(2,1)S(1)}, u32[]{:S(2)}, u32[]{:S(2)}) collective-permute-start(bf16[272,1024]{1,0:T(8,128)(2,1)S(1)} %get-tuple-element.328), channel_id=1, source_target_pairs={{0,4},{4,0},{8,12},{12,8},{16,20},{20,16},{24,28},{28,24},{1,5},{5... | collective-permute-start | bytes 1671176 | tf_op jit(solution)/shard_map/ppermute | solution.py:387
  153.2 23.6 %collective-permute-start.41 = (bf16[256,1024]{1,0:T(8,128)(2,1)S(1)}, bf16[256,1024]{1,0:T(8,128)(2,1)S(1)}, u32[]{:S(2)}, u32[]{:S(2)}) collective-permute-start(bf16[256,1024]{1,0:T(8,128)(2,1)S(1)} %get-tuple-element.344), channel_id=1, source_target_pairs={{0,4},{4,0},{8,12},{12,8},{16,20},{20,16},{24,28},{28,24},{1,5},{5... | collective-permute-start | bytes 1572872 | tf_op jit(solution)/shard_map/ppermute | solution.py:387
  155.6 20.4 %collective-permute-start.35 = (bf16[192,1024]{1,0:T(8,128)(2,1)S(1)}, bf16[192,1024]{1,0:T(8,128)(2,1)S(1)}, u32[]{:S(2)}, u32[]{:S(2)}) collective-permute-start(bf16[192,1024]{1,0:T(8,128)(2,1)S(1)} %sum_hop.8), channel_id=1, source_target_pairs={{0,16},{4,20},{8,24},{12,28},{16,0},{20,4},{24,8},{28,12},{1,17},{... | collective-permute-start | bytes 1179656 | tf_op jit(solution)/shard_map/ppermute | solution.py:387
  176.7 10.0 %collective-permute-start.40 = (bf16[144,1024]{1,0:T(8,128)(2,1)S(1)}, bf16[144,1024]{1,0:T(8,128)(2,1)S(1)}, u32[]{:S(2)}, u32[]{:S(2)}) collective-permute-start(bf16[144,1024]{1,0:T(8,128)(2,1)S(1)} %sum_hop.9), channel_id=1, source_target_pairs={{0,8},{4,12},{8,0},{12,4},{16,24},{20,28},{24,16},{28,20},{1,9},{5... | collective-permute-start | bytes 884744 | tf_op jit(solution)/shard_map/ppermute | solution.py:387
  177.4 14.8 %collective-permute-start.44 = (bf16[128,1024]{1,0:T(8,128)(2,1)S(1)}, bf16[128,1024]{1,0:T(8,128)(2,1)S(1)}, u32[]{:S(2)}, u32[]{:S(2)}) collective-permute-start(bf16[128,1024]{1,0:T(8,128)(2,1)S(1)} %sum_hop.12), channel_id=1, source_target_pairs={{0,8},{4,12},{8,0},{12,4},{16,24},{20,28},{24,16},{28,20},{1,9},{5... | collective-permute-start | bytes 786440 | tf_op jit(solution)/shard_map/ppermute | solution.py:387
  187.4 13.6 %collective-permute-start.43 = (bf16[80,1024]{1,0:T(8,128)(2,1)S(1)}, bf16[80,1024]{1,0:T(8,128)(2,1)S(1)}, u32[]{:S(2)}, u32[]{:S(2)}) collective-permute-start(bf16[80,1024]{1,0:T(8,128)(2,1)S(1)} %sum_hop.11), channel_id=1, source_target_pairs={{0,16},{4,20},{8,24},{12,28},{16,0},{20,4},{24,8},{28,12},{1,17},{... | collective-permute-start | bytes 491528 | tf_op jit(solution)/shard_map/ppermute | solution.py:387
  192.8 8.2 %collective-permute-start.46 = (bf16[64,1024]{1,0:T(8,128)(2,1)S(1)}, bf16[64,1024]{1,0:T(8,128)(2,1)S(1)}, u32[]{:S(2)}, u32[]{:S(2)}) collective-permute-start(bf16[64,1024]{1,0:T(8,128)(2,1)S(1)} %sum_hop.14), channel_id=1, source_target_pairs={{0,16},{4,20},{8,24},{12,28},{16,0},{20,4},{24,8},{28,12},{1,17},{... | collective-permute-start | bytes 393224 | tf_op jit(solution)/shard_map/ppermute | solution.py:387
  202.3 7.5 %collective-permute-start.48 = (bf16[64,1024]{1,0:T(8,128)(2,1)S(1)}, bf16[64,1024]{1,0:T(8,128)(2,1)S(1)}, u32[]{:S(2)}, u32[]{:S(2)}) collective-permute-start(bf16[64,1024]{1,0:T(8,128)(2,1)S(1)} %sum_last.5), channel_id=1, source_target_pairs={{0,16},{4,20},{8,24},{12,28},{16,0},{20,4},{24,8},{28,12},{1,17},{... | collective-permute-start | bytes 393224 | tf_op jit(solution)/shard_map/ppermute | solution.py:387
  203.0 9.6 %collective-permute-start.45 = (bf16[128,1024]{1,0:T(8,128)(2,1)S(1)}, bf16[128,1024]{1,0:T(8,128)(2,1)S(1)}, u32[]{:S(2)}, u32[]{:S(2)}) collective-permute-start(bf16[128,1024]{1,0:T(8,128)(2,1)S(1)} %sum_hop.13), channel_id=1, source_target_pairs={{0,4},{4,0},{8,12},{12,8},{16,20},{20,16},{24,28},{28,24},{1,5},{5... | collective-permute-start | bytes 786440 | tf_op jit(solution)/shard_map/ppermute | solution.py:387
  209.8 20.7 %collective-permute-start.52 = (bf16[128,1024]{1,0:T(8,128)(2,1)S(1)}, bf16[128,1024]{1,0:T(8,128)(2,1)S(1)}, u32[]{:S(2)}, u32[]{:S(2)}) collective-permute-start(bf16[128,1024]{1,0:T(8,128)(2,1)S(1)} %pad_maximum_fusion.5), channel_id=1, source_target_pairs={{0,8},{4,12},{8,0},{12,4},{16,24},{20,28},{24,16},{28,20},{1,9},{5... | collective-permute-start | bytes 786440 | tf_op jit(solution)/shard_map/ppermute | solution.py:387
  210.5 17.1 %collective-permute-start.42 = (bf16[96,1024]{1,0:T(8,128)(2,1)S(1)}, bf16[96,1024]{1,0:T(8,128)(2,1)S(1)}, u32[]{:S(2)}, u32[]{:S(2)}) collective-permute-start(bf16[96,1024]{1,0:T(8,128)(2,1)S(1)} %sum_hop.10), channel_id=1, source_target_pairs={{0,8},{4,12},{8,0},{12,4},{16,24},{20,28},{24,16},{28,20},{1,9},{5... | collective-permute-start | bytes 589832 | tf_op jit(solution)/shard_map/ppermute | solution.py:387
  213.2 10.4 %collective-permute-start.47 = (bf16[64,1024]{1,0:T(8,128)(2,1)S(1)}, bf16[64,1024]{1,0:T(8,128)(2,1)S(1)}, u32[]{:S(2)}, u32[]{:S(2)}) collective-permute-start(bf16[64,1024]{1,0:T(8,128)(2,1)S(1)} %sum_hop.15), channel_id=1, source_target_pairs={{0,16},{4,20},{8,24},{12,28},{16,0},{20,4},{24,8},{28,12},{1,17},{... | collective-permute-start | bytes 393224 | tf_op jit(solution)/shard_map/ppermute | solution.py:387
  213.3 17.2 %collective-permute-start.50 = (bf16[64,1024]{1,0:T(8,128)(2,1)S(1)}, bf16[64,1024]{1,0:T(8,128)(2,1)S(1)}, u32[]{:S(2)}, u32[]{:S(2)}) collective-permute-start(bf16[64,1024]{1,0:T(8,128)(2,1)S(1)} %get-tuple-element.365), channel_id=1, source_target_pairs={{0,16},{4,20},{8,24},{12,28},{16,0},{20,4},{24,8},{28,12},{1,17},{... | collective-permute-start | bytes 393224 | tf_op jit(solution)/shard_map/ppermute | solution.py:387
  229.1 9.3 %collective-permute-start.51 = (bf16[96,1024]{1,0:T(8,128)(2,1)S(1)}, bf16[96,1024]{1,0:T(8,128)(2,1)S(1)}, u32[]{:S(2)}, u32[]{:S(2)}) collective-permute-start(bf16[96,1024]{1,0:T(8,128)(2,1)S(1)} %sum_last.7), channel_id=1, source_target_pairs={{0,8},{4,12},{8,0},{12,4},{16,24},{20,28},{24,16},{28,20},{1,9},{5... | collective-permute-start | bytes 589832 | tf_op jit(solution)/shard_map/ppermute | solution.py:387
  230.5 18.3 %collective-permute-start.55 = (bf16[256,1024]{1,0:T(8,128)(2,1)S(1)}, bf16[256,1024]{1,0:T(8,128)(2,1)S(1)}, u32[]{:S(2)}, u32[]{:S(2)}) collective-permute-start(bf16[256,1024]{1,0:T(8,128)(2,1)S(1)} %pad_maximum_fusion.1.refs_4_), channel_id=1, source_target_pairs={{0,4},{4,0},{8,12},{12,8},{16,20},{20,16},{24,28},{28,24},{1,5},{5... | collective-permute-start | bytes 1572872 | tf_op jit(solution)/shard_map/ppermute | solution.py:387
  231.0 15.3 %collective-permute-start.54 = (bf16[128,1024]{1,0:T(8,128)(2,1)S(1)}, bf16[128,1024]{1,0:T(8,128)(2,1)S(1)}, u32[]{:S(2)}, u32[]{:S(2)}) collective-permute-start(bf16[128,1024]{1,0:T(8,128)(2,1)S(1)} %pad_maximum_fusion.6), channel_id=1, source_target_pairs={{0,8},{4,12},{8,0},{12,4},{16,24},{20,28},{24,16},{28,20},{1,9},{5... | collective-permute-start | bytes 786440 | tf_op jit(solution)/shard_map/ppermute | solution.py:387
  235.1 12.6 %collective-permute-start.53 = (bf16[128,1024]{1,0:T(8,128)(2,1)S(1)}, bf16[128,1024]{1,0:T(8,128)(2,1)S(1)}, u32[]{:S(2)}, u32[]{:S(2)}) collective-permute-start(bf16[128,1024]{1,0:T(8,128)(2,1)S(1)} %pad_maximum_fusion.7), channel_id=1, source_target_pairs={{0,4},{4,0},{8,12},{12,8},{16,20},{20,16},{24,28},{28,24},{1,5},{5... | collective-permute-start | bytes 786440 | tf_op jit(solution)/shard_map/ppermute | solution.py:387
  238.4 18.0 %collective-permute-start.64 = (bf16[192,1024]{1,0:T(8,128)(2,1)S(1)}, bf16[192,1024]{1,0:T(8,128)(2,1)S(1)}, u32[]{:S(2)}, u32[]{:S(2)}) collective-permute-start(bf16[192,1024]{1,0:T(8,128)(2,1)S(1)} %pad_maximum_fusion.4), channel_id=1, source_target_pairs={{0,16},{4,20},{8,24},{12,28},{16,0},{20,4},{24,8},{28,12},{1,17},{... | collective-permute-start | bytes 1179656 | tf_op jit(solution)/shard_map/ppermute | solution.py:387
  240.0 21.0 %collective-permute-start.56 = (bf16[256,1024]{1,0:T(8,128)(2,1)S(1)}, bf16[256,1024]{1,0:T(8,128)(2,1)S(1)}, u32[]{:S(2)}, u32[]{:S(2)}) collective-permute-start(bf16[256,1024]{1,0:T(8,128)(2,1)S(1)} %pad_maximum_fusion.1.refs_4_), channel_id=1, source_target_pairs={{0,1},{1,0},{2,3},{3,2},{4,5},{5,4},{6,7},{7,6},{8,9},{9,8},{10,11... | collective-permute-start | bytes 1572872 | tf_op jit(solution)/shard_map/ppermute | solution.py:298
  246.3 14.7 %collective-permute-start.58 = (bf16[256,1024]{1,0:T(8,128)(2,1)S(1)}, bf16[256,1024]{1,0:T(8,128)(2,1)S(1)}, u32[]{:S(2)}, u32[]{:S(2)}) collective-permute-start(bf16[256,1024]{1,0:T(8,128)(2,1)S(1)} %pad_maximum_fusion.2.refs_5_), channel_id=1, source_target_pairs={{0,4},{4,0},{8,12},{12,8},{16,20},{20,16},{24,28},{28,24},{1,5},{5... | collective-permute-start | bytes 1572872 | tf_op jit(solution)/shard_map/ppermute | solution.py:387
  247.7 15.0 %collective-permute-start.62 = (bf16[256,1024]{1,0:T(8,128)(2,1)S(1)}, bf16[256,1024]{1,0:T(8,128)(2,1)S(1)}, u32[]{:S(2)}, u32[]{:S(2)}) collective-permute-start(bf16[256,1024]{1,0:T(8,128)(2,1)S(1)} %pad_maximum_fusion.3.refs_5_), channel_id=1, source_target_pairs={{0,2},{1,3},{2,0},{3,1},{4,6},{5,7},{6,4},{7,5},{8,10},{9,11},{10,... | collective-permute-start | bytes 1572872 | tf_op jit(solution)/shard_map/ppermute | solution.py:298
  248.9 15.0 %collective-permute-start.57 = (bf16[256,1024]{1,0:T(8,128)(2,1)S(1)}, bf16[256,1024]{1,0:T(8,128)(2,1)S(1)}, u32[]{:S(2)}, u32[]{:S(2)}) collective-permute-start(bf16[256,1024]{1,0:T(8,128)(2,1)S(1)} %collective-permute-done.55.refs_5_), channel_id=1, source_target_pairs={{0,1},{1,0},{2,3},{3,2},{4,5},{5,4},{6,7},{7,6},{8,9},{9,8},{10,11... | collective-permute-start | bytes 1572872 | tf_op jit(solution)/shard_map/ppermute | solution.py:298
  256.5 33.0 %collective-permute-start.65 = (bf16[384,1024]{1,0:T(8,128)(2,1)S(1)}, bf16[384,1024]{1,0:T(8,128)(2,1)S(1)}, u32[]{:S(2)}, u32[]{:S(2)}) collective-permute-start(bf16[384,1024]{1,0:T(8,128)(2,1)S(1)} %pad_maximum_fusion.refs_6_), channel_id=1, source_target_pairs={{0,4},{4,0},{8,12},{12,8},{16,20},{20,16},{24,28},{28,24},{1,5},{5... | collective-permute-start | bytes 2359304 | tf_op jit(solution)/shard_map/ppermute | solution.py:387
  261.0 14.1 %collective-permute-start.59 = (bf16[256,1024]{1,0:T(8,128)(2,1)S(1)}, bf16[256,1024]{1,0:T(8,128)(2,1)S(1)}, u32[]{:S(2)}, u32[]{:S(2)}) collective-permute-start(bf16[256,1024]{1,0:T(8,128)(2,1)S(1)} %pad_maximum_fusion.2.refs_5_), channel_id=1, source_target_pairs={{0,3},{1,2},{2,1},{3,0},{4,7},{5,6},{6,5},{7,4},{8,11},{9,10},{10,... | collective-permute-start | bytes 1572872 | tf_op jit(solution)/shard_map/ppermute | solution.py:298
  261.0 25.1 %collective-permute-start.60 = (bf16[256,1024]{1,0:T(8,128)(2,1)S(1)}, bf16[256,1024]{1,0:T(8,128)(2,1)S(1)}, u32[]{:S(2)}, u32[]{:S(2)}) collective-permute-start(bf16[256,1024]{1,0:T(8,128)(2,1)S(1)} %collective-permute-done.58.refs_6_), channel_id=1, source_target_pairs={{0,3},{1,2},{2,1},{3,0},{4,7},{5,6},{6,5},{7,4},{8,11},{9,10},{10,... | collective-permute-start | bytes 1572872 | tf_op jit(solution)/shard_map/ppermute | solution.py:298
  262.7 23.4 %collective-permute-start.61 = (bf16[256,1024]{1,0:T(8,128)(2,1)S(1)}, bf16[256,1024]{1,0:T(8,128)(2,1)S(1)}, u32[]{:S(2)}, u32[]{:S(2)}) collective-permute-start(bf16[256,1024]{1,0:T(8,128)(2,1)S(1)} %pad_maximum_fusion.3.refs_5_), channel_id=1, source_target_pairs={{0,8},{4,12},{8,0},{12,4},{16,24},{20,28},{24,16},{28,20},{1,9},{5... | collective-permute-start | bytes 1572872 | tf_op jit(solution)/shard_map/ppermute | solution.py:387
  263.8 25.6 %collective-permute-start.63 = (bf16[256,1024]{1,0:T(8,128)(2,1)S(1)}, bf16[256,1024]{1,0:T(8,128)(2,1)S(1)}, u32[]{:S(2)}, u32[]{:S(2)}) collective-permute-start(bf16[256,1024]{1,0:T(8,128)(2,1)S(1)} %collective-permute-done.62.refs_7_), channel_id=1, source_target_pairs={{0,8},{4,12},{8,0},{12,4},{16,24},{20,28},{24,16},{28,20},{1,9},{5... | collective-permute-start | bytes 1572872 | tf_op jit(solution)/shard_map/ppermute | solution.py:387
  (20 other events, 131.8 us)

commit v8 on v7

--- a/solution.py
+++ b/solution.py
@@ -92,7 +92,7 @@
             half_ref[elements * size :, :] = extra_rows(jnp.full((1, width), jnp.sum(squares)))
 
 
-def call(kernel, name, outs, scalars, args, scratch=(), aliases=None, vmem=16):
+def call(kernel, name, outs, scalars, args, scratch=(), aliases=None, vmem=16, moved=1024):
     return pl.pallas_call(
         kernel,
         out_shape=outs,
@@ -101,7 +101,7 @@
         scratch_shapes=list(scratch),
         input_output_aliases=aliases or {},
         compiler_params=pltpu.CompilerParams(vmem_limit_bytes=vmem * MIB),
-        cost_estimate=pl.CostEstimate(flops=1024, bytes_accessed=1024, transcendentals=0),
+        cost_estimate=pl.CostEstimate(flops=1024, bytes_accessed=moved, transcendentals=0),
         name=name,
     )(*scalars, *args)
 
@@ -332,6 +332,10 @@
                     pieces[c][d ^ low] = order(pieces[c][d ^ low])
                     pieces[c][d] = to_group(pieces[c][d ^ low], low)
 
+    def settle(c, some=lambda d: True):
+        for d in [d for d in pieces[c] if d and some(d)]:
+            pieces[c][d] = order(pieces[c][d])
+
     def multiply(job):
         nonlocal squares
         stage, c = job
@@ -355,6 +359,9 @@
                 bit //= 2
             if c:
                 more_panel(c - 1)
+                settle(c - 1, lambda d: not d & (d - 1))
+            if c > 1:
+                settle(c - 2)
             return
         current[(stage + 1, c)] = out
         near[(stage + 1, c)] = lax.ppermute(out, "elem", swap)
@@ -396,6 +403,8 @@
     def panel_process():
         yield 10.5
         more_panel(CHUNKS - 1)
+        settle(CHUNKS - 1, lambda d: not d & (d - 1))
+        settle(CHUNKS - 2)
         clock.spend(1.3)
         for d in range(1, groups):
             if d & (d - 1):
@@ -413,7 +422,9 @@
         scratch = (pltpu.VMEM((height, columns), BF16),)
         name = "gram_pair" if d else "gram_own"
         clock.spend(3.2 if d else 3.0)
-        return call(functools.partial(gram_kernel, d > 0, mask), name, (half, half), (where(d),), fields, scratch)
+        return call(
+            functools.partial(gram_kernel, d > 0, mask), name, (half, half), (where(d),), fields, scratch, moved=5 * MIB
+        )
 
     def process(d, masks, extra=0, round_y=False):
         nonlocal mixed, mixes, level
@@ -442,7 +453,7 @@
         for hop, mask in enumerate(masks):
             if hop:
                 height //= 2
-                value = added(hop)
+                value = order(added(hop))
             received, arrival = over_tiles(value, mask)
             yield arrival if hop or mask > 1 else arrival - (3.0 if d else 6.0)
             terms.append(order(received))
@@ -450,13 +461,14 @@
             yield clock.now + 0.5
         part = added(len(masks))
         if extra:
-            part, level = part
+            part, level = order(*part)
+        else:
+            part = order(part)
         for mask in masks[:0:-1]:
             received, arrival = over_tiles(part, mask)
             yield arrival
-            part = jnp.concatenate([part, order(received)], axis=0)
+            part = order(jnp.concatenate([part, order(received)], axis=0))
             clock.spend(0.5)
-        part = order(part)
         far, arrival = over_tiles(part, masks[0])
         if d:
             peer, peer_arrival = over_groups(part, d)
@@ -464,17 +476,16 @@
             yield peer_arrival
             peer = order(peer)
             peer_far, peer_arrival = over_tiles(peer, masks[0])
+        elif d:
+            yield peer_arrival - 3.0
+            peer = order(peer)
         yield arrival
         far = order(far)
         parts = (part, far)
         if d:
             if not round_y:
-                peer_far, arrival = over_groups(far, d)
-                yield peer_arrival
-                peer = order(peer)
-                yield arrival
-            else:
-                yield peer_arrival
+                peer_far, peer_arrival = over_groups(far, d)
+            yield peer_arrival
             peer_far = order(peer_far)
             parts += (peer, peer_far)
         first, last = mixes == 0, mixes == groups - 1
@@ -487,7 +498,7 @@
         kernel = functools.partial(mix_kernel, d > 0, masks, first, last)
         name = "mix_pair" if d else "mix_own"
         clock.spend(3.2)
-        mixed = call(kernel, name, shape, (where(d),), args, scratch, {} if first or last else {1: 0}, 28)
+        mixed = call(kernel, name, shape, (where(d),), args, scratch, {} if first or last else {1: 0}, 28, 5 * MIB)
         if not last:
             mixed = order(mixed)
 

time: 297 us -> 301 us (1.013)
  starting transfers between devices: 83.9 us -> 92 us
  waiting for transfers between devices: 153 us -> 145 us
    ppermute x25, waiting for transfers between devices: 86.3 us -> 100 us  [over_tiles(): sent = lax.ppermute(value, 'elem', [(i, i ^ mask) for i in range(tiles)])]
    ppermute x17, waiting for transfers between devices: 24.1 us -> 12.3 us  [to_group(): return lax.ppermute(value, 'orb', [(i, i ^ d) for i in range(groups)])]
    ppermute x12, waiting for transfers between devices: 19.6 us -> 11.2 us  [send_on(): far[job] = lax.ppermute(near[job], 'elem', outward)]
    ppermute x8, starting transfers between devices: 23.8 us -> 27.7 us  [multiply(): near[stage + 1, c] = lax.ppermute(out, 'elem', swap)]
    ppermute x3, starting transfers between devices: 3.62 us -> 7.13 us  [local(): near[0, c] = lax.ppermute(start[c], 'elem', swap)]
    unnamed x37 -> x39, local copies, waits for them, and re-layouts: 5.4 us -> 6.73 us
  transfers between devices with their start and end apart: 66 -> 66, of which waited for: 33 -> 34; matrix products, arithmetic and copies ran while one was open for 2% -> 2% of each run, Pallas kernels for 12% -> 13%
where the time goes in v8:
time: 301 us; the launch traced here: 300 us
  waiting for transfers between devices  145 us (48%)
  starting transfers between devices  92 us (31%)
  Pallas kernels  47.3 us (16%)
  local copies, waits for them, and re-layouts  12.8 us (4%)
    ppermute x25, waiting for transfers between devices, over_tiles(): sent = lax.ppermute(value, 'elem', [(i, i ^ mask) for i in range(tiles)])  100 us
    pallas_call x32, Pallas kernels, call(): pl.pallas_call(kernel, out_shape=outs, in_specs=[pl.BlockSpec(memory_spac...  47.3 us
    ppermute x8, starting transfers between devices, multiply(): near[stage + 1, c] = lax.ppermute(out, 'elem', swap)  27.7 us
    ppermute x25, starting transfers between devices, over_tiles(): sent = lax.ppermute(value, 'elem', [(i, i ^ mask) for i in range(tiles)])  22.9 us
    ppermute x12, starting transfers between devices, send_on(): far[job] = lax.ppermute(near[job], 'elem', outward)  22 us
    ppermute x17, waiting for transfers between devices, to_group(): return lax.ppermute(value, 'orb', [(i, i ^ d) for i in range(groups)])  12.3 us
    ppermute x8, waiting for transfers between devices, multiply(): near[stage + 1, c] = lax.ppermute(out, 'elem', swap)  11.9 us
    ppermute x12, waiting for transfers between devices, send_on(): far[job] = lax.ppermute(near[job], 'elem', outward)  11.2 us
  transfers between devices with their start and end apart: 66, of which 34 were waited for; matrix products, arithmetic and copies ran while one was open for 2% of the time, Pallas kernels for 13%

profile of v8, /device:TPU:0, one launch (start us, length us, event | category | flops | bytes accessed | tf_op | source)
XLA Modules:
  0.0 300.1 jit_solution(1658015962173586499)
XLA Ops:
  1.5 3.0 %collective-permute-start = (bf16[768,256]{1,0:T(8,128)(2,1)S(1)}, bf16[768,256]{1,0:T(8,128)(2,1)S(1)}, u32[]{:S(2)}, u32[]{:S(2)}) collective-permute-start(bf16[768,256]{1,0:T(8,128)(2,1)S(1)} %get-tuple-element.517.field_ref.refs_0_), channel_id=1, source_target_pairs={{0,4},{4,0},{8,12},{12,8},{16,20},{20,16},{24,28},{28,24},{1,5},{5... | collective-permute-start | bytes 1179656 | tf_op jit(solution)/shard_map/ppermute | solution.py:311
  4.6 2.2 slice_bitcast_fusion
  8.1 2.3 concatenate.30.blocks_ref
  10.5 3.9 %collective-permute-done.near_ref = bf16[768,256]{1,0:T(8,128)(2,1)S(1)} collective-permute-done((bf16[768,256]{1,0:T(8,128)(2,1)S(1)}, bf16[768,256]{1,0:T(8,128)(2,1)S(1)}, u32[]{:S(2)}, u32[]{:S(2)}) %collective-permute-start) | collective-permute-done | bytes 393248 | tf_op jit(solution)/shard_map/ppermute | solution.py:311
  14.5 2.1 collective-permute-start.1
  16.6 3.5 %collective-permute-start.4 = (bf16[768,256]{1,0:T(8,128)(2,1)S(1)}, bf16[768,256]{1,0:T(8,128)(2,1)S(1)}, u32[]{:S(2)}, u32[]{:S(2)}) collective-permute-start(bf16[768,256]{1,0:T(8,128)(2,1)S(1)} %get-tuple-element.275.field_ref.refs_0_), channel_id=1, source_target_pairs={{0,4},{4,0},{8,12},{12,8},{16,20},{20,16},{24,28},{28,24},{1,5},{5... | collective-permute-start | bytes 1179656 | tf_op jit(solution)/shard_map/ppermute | solution.py:316
  20.1 2.8 collective-permute-done.2.near_ref
  22.9 2.1 collective-permute-start.7
  25.0 3.5 %collective-permute-start.6 = (bf16[768,256]{1,0:T(8,128)(2,1)S(1)}, bf16[768,256]{1,0:T(8,128)(2,1)S(1)}, u32[]{:S(2)}, u32[]{:S(2)}) collective-permute-start(bf16[768,256]{1,0:T(8,128)(2,1)S(1)} %get-tuple-element.278.field_ref.refs_0_), channel_id=1, source_target_pairs={{0,4},{4,0},{8,12},{12,8},{16,20},{20,16},{24,28},{28,24},{1,5},{5... | collective-permute-start | bytes 1179656 | tf_op jit(solution)/shard_map/ppermute | solution.py:316
  31.3 2.1 collective-permute-start.5
  33.4 3.5 %collective-permute-start.3 = (bf16[768,256]{1,0:T(8,128)(2,1)S(1)}, bf16[768,256]{1,0:T(8,128)(2,1)S(1)}, u32[]{:S(2)}, u32[]{:S(2)}) collective-permute-start(bf16[768,256]{1,0:T(8,128)(2,1)S(1)} %get-tuple-element.274.field_ref), channel_id=1, source_target_pairs={{0,4},{4,0},{8,12},{12,8},{16,20},{20,16},{24,28},{28,24},{1,5},{5... | collective-permute-start | bytes 1179656 | tf_op jit(solution)/shard_map/ppermute | solution.py:367
  39.7 2.1 collective-permute-start.10
  41.9 3.5 %collective-permute-start.9 = (bf16[768,256]{1,0:T(8,128)(2,1)S(1)}, bf16[768,256]{1,0:T(8,128)(2,1)S(1)}, u32[]{:S(2)}, u32[]{:S(2)}) collective-permute-start(bf16[768,256]{1,0:T(8,128)(2,1)S(1)} %get-tuple-element.293.field_ref), channel_id=1, source_target_pairs={{0,4},{4,0},{8,12},{12,8},{16,20},{20,16},{24,28},{28,24},{1,5},{5... | collective-permute-start | bytes 1179656 | tf_op jit(solution)/shard_map/ppermute | solution.py:367
  48.2 2.1 collective-permute-start.8
  50.3 3.5 %collective-permute-start.12 = (bf16[768,256]{1,0:T(8,128)(2,1)S(1)}, bf16[768,256]{1,0:T(8,128)(2,1)S(1)}, u32[]{:S(2)}, u32[]{:S(2)}) collective-permute-start(bf16[768,256]{1,0:T(8,128)(2,1)S(1)} %get-tuple-element.305.field_ref), channel_id=1, source_target_pairs={{0,4},{4,0},{8,12},{12,8},{16,20},{20,16},{24,28},{28,24},{1,5},{5... | collective-permute-start | bytes 1179656 | tf_op jit(solution)/shard_map/ppermute | solution.py:367
  56.6 2.1 collective-permute-start.15
  58.7 3.5 %collective-permute-start.14 = (bf16[768,256]{1,0:T(8,128)(2,1)S(1)}, bf16[768,256]{1,0:T(8,128)(2,1)S(1)}, u32[]{:S(2)}, u32[]{:S(2)}) collective-permute-start(bf16[768,256]{1,0:T(8,128)(2,1)S(1)} %get-tuple-element.308.field_ref), channel_id=1, source_target_pairs={{0,4},{4,0},{8,12},{12,8},{16,20},{20,16},{24,28},{28,24},{1,5},{5... | collective-permute-start | bytes 1179656 | tf_op jit(solution)/shard_map/ppermute | solution.py:367
  65.0 2.1 collective-permute-start.13
  67.1 3.5 %collective-permute-start.11 = (bf16[768,256]{1,0:T(8,128)(2,1)S(1)}, bf16[768,256]{1,0:T(8,128)(2,1)S(1)}, u32[]{:S(2)}, u32[]{:S(2)}) collective-permute-start(bf16[768,256]{1,0:T(8,128)(2,1)S(1)} %product_1.4.field_ref), channel_id=1, source_target_pairs={{0,4},{4,0},{8,12},{12,8},{16,20},{20,16},{24,28},{28,24},{1,5},{5... | collective-permute-start | bytes 1179656 | tf_op jit(solution)/shard_map/ppermute | solution.py:367
  73.5 2.1 collective-permute-start.18
  75.6 3.5 %collective-permute-start.17 = (bf16[768,256]{1,0:T(8,128)(2,1)S(1)}, bf16[768,256]{1,0:T(8,128)(2,1)S(1)}, u32[]{:S(2)}, u32[]{:S(2)}) collective-permute-start(bf16[768,256]{1,0:T(8,128)(2,1)S(1)} %product_1.5.field_ref), channel_id=1, source_target_pairs={{0,4},{4,0},{8,12},{12,8},{16,20},{20,16},{24,28},{28,24},{1,5},{5... | collective-permute-start | bytes 1179656 | tf_op jit(solution)/shard_map/ppermute | solution.py:367
  81.9 2.1 collective-permute-start.16
  84.0 3.5 %collective-permute-start.20 = (bf16[768,256]{1,0:T(8,128)(2,1)S(1)}, bf16[768,256]{1,0:T(8,128)(2,1)S(1)}, u32[]{:S(2)}, u32[]{:S(2)}) collective-permute-start(bf16[768,256]{1,0:T(8,128)(2,1)S(1)} %product_1.6.field_ref), channel_id=1, source_target_pairs={{0,4},{4,0},{8,12},{12,8},{16,20},{20,16},{24,28},{28,24},{1,5},{5... | collective-permute-start | bytes 1179656 | tf_op jit(solution)/shard_map/ppermute | solution.py:367
  90.3 2.1 collective-permute-start.19
  94.4 1.5 collective-permute-start.24
  96.0 2.9 collective-permute-start.22
  99.7 1.9 collective-permute-done.19.far_ref
  104.9 3.8 %collective-permute-done.22.near_ref = bf16[768,256]{1,0:T(8,128)(2,1)} collective-permute-done((bf16[768,256]{1,0:T(8,128)(2,1)S(1)}, bf16[768,256]{1,0:T(8,128)(2,1)}, u32[]{:S(2)}, u32[]{:S(2)}) %collective-permute-start.22) | collective-permute-done | bytes 393248 | tf_op jit(solution)/shard_map/ppermute | solution.py:367
  108.7 3.2 %collective-permute-done.21.far_ref = bf16[768,256]{1,0:T(8,128)(2,1)S(1)} collective-permute-done((bf16[768,256]{1,0:T(8,128)(2,1)S(1)}, bf16[768,256]{1,0:T(8,128)(2,1)S(1)}, u32[]{:S(2)}, u32[]{:S(2)}) %collective-permute-start.21) | collective-permute-done | bytes 393248 | tf_op jit(solution)/shard_map/ppermute | solution.py:325
  116.4 5.4 %collective-permute-done.25.far_ref = bf16[768,256]{1,0:T(8,128)(2,1)} collective-permute-done((bf16[768,256]{1,0:T(8,128)(2,1)}, bf16[768,256]{1,0:T(8,128)(2,1)}, u32[]{:S(2)}, u32[]{:S(2)}) %collective-permute-start.25) | collective-permute-done | bytes 393248 | tf_op jit(solution)/shard_map/ppermute | solution.py:325
  123.6 1.9 product_2.7.refs_3_.refs_5_.refs_11_
  126.7 3.0 gram_own.1
  131.0 4.9 %collective-permute-done.34.refs_7_.refs_9_.refs_4_ = bf16[784,256]{1,0:T(8,128)(2,1)S(1)} collective-permute-done((bf16[784,256]{1,0:T(8,128)(2,1)S(1)}, bf16[784,256]{1,0:T(8,128)(2,1)S(1)}, u32[]{:S(2)}, u32[]{:S(2)}) %collective-permute-start.34) | collective-permute-done | bytes 401440 | tf_op jit(solution)/shard_map/ppermute | solution.py:298
  136.9 2.4 gram_pair.3
  139.4 9.5 %collective-permute-done.36.refs_1_ = bf16[384,1024]{1,0:T(8,128)(2,1)S(1)} collective-permute-done((bf16[384,1024]{1,0:T(8,128)(2,1)}, bf16[384,1024]{1,0:T(8,128)(2,1)S(1)}, u32[]{:S(2)}, u32[]{:S(2)}) %collective-permute-start.36) | collective-permute-done | bytes 786464 | tf_op jit(solution)/shard_map/ppermute | solution.py:394
  149.6 2.4 gram_pair.4
  152.7 2.2 gram_pair.5
  157.1 13.5 %collective-permute-done.38.refs_2_ = bf16[192,1024]{1,0:T(8,128)(2,1)S(1)} collective-permute-done((bf16[192,1024]{1,0:T(8,128)(2,1)S(1)}, bf16[192,1024]{1,0:T(8,128)(2,1)S(1)}, u32[]{:S(2)}, u32[]{:S(2)}) %collective-permute-start.38) | collective-permute-done | bytes 393248 | tf_op jit(solution)/shard_map/ppermute | solution.py:394
  171.9 2.1 collective-permute-start.40
  175.5 3.6 %collective-permute-done.42.refs_3_ = bf16[96,1024]{1,0:T(8,128)(2,1)S(1)} collective-permute-done((bf16[96,1024]{1,0:T(8,128)(2,1)S(1)}, bf16[96,1024]{1,0:T(8,128)(2,1)S(1)}, u32[]{:S(2)}, u32[]{:S(2)}) %collective-permute-start.42) | collective-permute-done | bytes 196640 | tf_op jit(solution)/shard_map/ppermute | solution.py:394
  179.8 5.6 %collective-permute-done.40.refs_2_ = bf16[144,1024]{1,0:T(8,128)(2,1)S(1)} collective-permute-done((bf16[144,1024]{1,0:T(8,128)(2,1)S(1)}, bf16[144,1024]{1,0:T(8,128)(2,1)S(1)}, u32[]{:S(2)}, u32[]{:S(2)}) %collective-permute-start.40) | collective-permute-done | bytes 294944 | tf_op jit(solution)/shard_map/ppermute | solution.py:394
  187.3 4.3 %collective-permute-done.44.refs_2_ = bf16[128,1024]{1,0:T(8,128)(2,1)S(1)} collective-permute-done((bf16[128,1024]{1,0:T(8,128)(2,1)S(1)}, bf16[128,1024]{1,0:T(8,128)(2,1)S(1)}, u32[]{:S(2)}, u32[]{:S(2)}) %collective-permute-start.44) | collective-permute-done | bytes 262176 | tf_op jit(solution)/shard_map/ppermute | solution.py:394
  192.7 2.5 collective-permute-start.47
  195.1 10.1 %collective-permute-done.46.refs_3_ = bf16[64,1024]{1,0:T(8,128)(2,1)S(1)} collective-permute-done((bf16[64,1024]{1,0:T(8,128)(2,1)S(1)}, bf16[64,1024]{1,0:T(8,128)(2,1)S(1)}, u32[]{:S(2)}, u32[]{:S(2)}) %collective-permute-start.46) | collective-permute-done | bytes 131104 | tf_op jit(solution)/shard_map/ppermute | solution.py:394
  206.7 2.9 collective-permute-start.50
  211.2 1.5 collective-permute-start.51
  212.7 6.5 %collective-permute-done.48 = bf16[64,1024]{1,0:T(8,128)(2,1)S(1)} collective-permute-done((bf16[64,1024]{1,0:T(8,128)(2,1)S(1)}, bf16[64,1024]{1,0:T(8,128)(2,1)S(1)}, u32[]{:S(2)}, u32[]{:S(2)}) %collective-permute-start.48) | collective-permute-done | bytes 131104 | tf_op jit(solution)/shard_map/ppermute | solution.py:394
  219.2 2.8 collective-permute-done.50
  222.0 1.7 collective-permute-done.49
  224.5 1.7 collective-permute-start.64
  226.3 1.7 collective-permute-start.53
  227.9 10.9 %collective-permute-done.52 = bf16[128,1024]{1,0:T(8,128)(2,1)S(1)} collective-permute-done((bf16[128,1024]{1,0:T(8,128)(2,1)S(1)}, bf16[128,1024]{1,0:T(8,128)(2,1)S(1)}, u32[]{:S(2)}, u32[]{:S(2)}) %collective-permute-start.52) | collective-permute-done | bytes 262176 | tf_op jit(solution)/shard_map/ppermute | solution.py:394
  240.4 3.3 %collective-permute-done.54 = bf16[128,1024]{1,0:T(8,128)(2,1)S(1)} collective-permute-done((bf16[128,1024]{1,0:T(8,128)(2,1)S(1)}, bf16[128,1024]{1,0:T(8,128)(2,1)S(1)}, u32[]{:S(2)}, u32[]{:S(2)}) %collective-permute-start.54) | collective-permute-done | bytes 262176 | tf_op jit(solution)/shard_map/ppermute | solution.py:394
  246.4 6.9 %collective-permute-done.55.refs_5_ = bf16[256,1024]{1,0:T(8,128)(2,1)S(1)} collective-permute-done((bf16[256,1024]{1,0:T(8,128)(2,1)S(1)}, bf16[256,1024]{1,0:T(8,128)(2,1)S(1)}, u32[]{:S(2)}, u32[]{:S(2)}) %collective-permute-start.55) | collective-permute-done | bytes 524320 | tf_op jit(solution)/shard_map/ppermute | solution.py:394
  254.3 10.2 %collective-permute-done.58.refs_6_ = bf16[256,1024]{1,0:T(8,128)(2,1)S(1)} collective-permute-done((bf16[256,1024]{1,0:T(8,128)(2,1)S(1)}, bf16[256,1024]{1,0:T(8,128)(2,1)S(1)}, u32[]{:S(2)}, u32[]{:S(2)}) %collective-permute-start.58) | collective-permute-done | bytes 524320 | tf_op jit(solution)/shard_map/ppermute | solution.py:394
  265.9 1.7 collective-permute-done.59.refs_7_
  267.6 2.0 collective-permute-start.63
  269.7 3.2 %mix_pair.3.refs_0_ = f32[768,1024]{1,0:T(8,128)S(1)} custom-call(s32[2]{0:T(128)S(1)} %copy-done.15, bf16[768,256]{1,0:T(8,128)(2,1)S(1)} %copy-done.8, bf16[768,256]{1,0:T(8,128)(2,1)S(1)} %copy-done.10, bf16[768,256]{1,0:T(8,128)(2,1)} %collective-permute-done.30.refs_6_.refs_2_, bf16[784,256]{1,0:T(8,128)(2,1)} %collective-permute-done.33.refs_8_.refs_7_.refs_3_, ...), custom_call_target="tpu_custom_call" | custom-call | flops 1024 | bytes 5242880 | tf_op jit(solution)/shard_map/mix_pair/pallas_call | solution.py:96
  272.8 5.7 %collective-permute-done.60.refs_8_ = bf16[256,1024]{1,0:T(8,128)(2,1)S(1)} collective-permute-done((bf16[256,1024]{1,0:T(8,128)(2,1)S(1)}, bf16[256,1024]{1,0:T(8,128)(2,1)S(1)}, u32[]{:S(2)}, u32[]{:S(2)}) %collective-permute-start.60) | collective-permute-done | bytes 524320 | tf_op jit(solution)/shard_map/ppermute | solution.py:298
  278.5 3.9 %collective-permute-done.61.refs_6_ = bf16[256,1024]{1,0:T(8,128)(2,1)S(1)} collective-permute-done((bf16[256,1024]{1,0:T(8,128)(2,1)S(1)}, bf16[256,1024]{1,0:T(8,128)(2,1)S(1)}, u32[]{:S(2)}, u32[]{:S(2)}) %collective-permute-start.61) | collective-permute-done | bytes 524320 | tf_op jit(solution)/shard_map/ppermute | solution.py:394
  282.4 3.5 %mix_pair.4.refs_0_ = f32[768,1024]{1,0:T(8,128)S(1)} custom-call(s32[2]{0:T(128)S(1)} %pad_add_fusion.2.where_ref, f32[768,1024]{1,0:T(8,128)S(1)} %mix_pair.3.refs_0_, bf16[768,256]{1,0:T(8,128)(2,1)S(1)} %copy-done.1, bf16[768,256]{1,0:T(8,128)(2,1)S(1)} %copy-done.3, ...), custom_call_target="tpu_custom_call", output_to_operand_aliasing={{}: (1, {})} | custom-call | flops 1024 | bytes 5242880 | tf_op jit(solution)/shard_map/mix_pair/pallas_call | solution.py:96
  285.9 7.2 %collective-permute-done.63.refs_8_ = bf16[256,1024]{1,0:T(8,128)(2,1)S(1)} collective-permute-done((bf16[256,1024]{1,0:T(8,128)(2,1)S(1)}, bf16[256,1024]{1,0:T(8,128)(2,1)S(1)}, u32[]{:S(2)}, u32[]{:S(2)}) %collective-permute-start.63) | collective-permute-done | bytes 524320 | tf_op jit(solution)/shard_map/ppermute | solution.py:394
  293.0 3.2 %mix_pair.5.refs_1_ = f32[768,1024]{1,0:T(8,128)S(1)} custom-call(s32[2]{0:T(128)S(1)} %pad_add_fusion.2.where_ref, f32[768,1024]{1,0:T(8,128)S(1)} %mix_pair.4.refs_0_, bf16[768,256]{1,0:T(8,128)(2,1)S(1)} %copy-done.6, bf16[768,256]{1,0:T(8,128)(2,1)} %collective-permute-done.28.refs_5_.refs_2_, ...), custom_call_target="tpu_custom_call", output_to_operand_aliasing={{}: (1, {})} | custom-call | flops 1024 | bytes 5242880 | tf_op jit(solution)/shard_map/mix_pair/pallas_call | solution.py:96
  296.3 3.8 %mix_own.1 = bf16[768,1024]{1,0:T(8,128)(2,1)} custom-call(s32[2]{0:T(128)S(1)} %copy-done.14, f32[8,128]{1,0:T(8,128)S(1)} %get-tuple-element.470.refs_4_.refs_0_, f32[768,1024]{1,0:T(8,128)S(1)} %mix_pair.5.refs_1_, bf16[768,256]{1,0:T(8,128)(2,1)S(1)} %get-tuple-element.331.refs_0_.refs_2_.refs_8_, ...), custom_call_target="tpu_custom_call" | custom-call | flops 1024 | bytes 5242880 | tf_op jit(solution)/shard_map/mix_own/pallas_call | solution.py:96
  (160 shorter events, 61.5 us)
Async XLA Ops:
  1.5 13.0 %collective-permute-start = (bf16[768,256]{1,0:T(8,128)(2,1)S(1)}, bf16[768,256]{1,0:T(8,128)(2,1)S(1)}, u32[]{:S(2)}, u32[]{:S(2)}) collective-permute-start(bf16[768,256]{1,0:T(8,128)(2,1)S(1)} %get-tuple-element.517.field_ref.refs_0_), channel_id=1, source_target_pairs={{0,4},{4,0},{8,12},{12,8},{16,20},{20,16},{24,28},{28,24},{1,5},{5... | collective-permute-start | bytes 1179656 | tf_op jit(solution)/shard_map/ppermute | solution.py:311
  10.5 12.4 %collective-permute-start.2 = (bf16[768,256]{1,0:T(8,128)(2,1)S(1)}, bf16[768,256]{1,0:T(8,128)(2,1)S(1)}, u32[]{:S(2)}, u32[]{:S(2)}) collective-permute-start(bf16[768,256]{1,0:T(8,128)(2,1)S(1)} %get-tuple-element.267.field_ref.refs_0_), channel_id=1, source_target_pairs={{0,4},{4,0},{8,12},{12,8},{16,20},{20,16},{24,28},{28,24},{1,5},{5... | collective-permute-start | bytes 1179656 | tf_op jit(solution)/shard_map/ppermute | solution.py:316
  14.5 14.1 %collective-permute-start.1 = (bf16[768,256]{1,0:T(8,128)(2,1)S(1)}, bf16[768,256]{1,0:T(8,128)(2,1)S(1)}, u32[]{:S(2)}, u32[]{:S(2)}) collective-permute-start(bf16[768,256]{1,0:T(8,128)(2,1)S(1)} %collective-permute-done.near_ref), channel_id=1, source_target_pairs={{0,8},{4,28},{8,16},{12,4},{16,24},{20,12},{24,0},{28,20},{1,9},{5... | collective-permute-start | bytes 1179656 | tf_op jit(solution)/shard_map/ppermute | solution.py:325
  16.6 14.7 %collective-permute-start.4 = (bf16[768,256]{1,0:T(8,128)(2,1)S(1)}, bf16[768,256]{1,0:T(8,128)(2,1)S(1)}, u32[]{:S(2)}, u32[]{:S(2)}) collective-permute-start(bf16[768,256]{1,0:T(8,128)(2,1)S(1)} %get-tuple-element.275.field_ref.refs_0_), channel_id=1, source_target_pairs={{0,4},{4,0},{8,12},{12,8},{16,20},{20,16},{24,28},{28,24},{1,5},{5... | collective-permute-start | bytes 1179656 | tf_op jit(solution)/shard_map/ppermute | solution.py:316
  22.9 14.1 %collective-permute-start.7 = (bf16[768,256]{1,0:T(8,128)(2,1)S(1)}, bf16[768,256]{1,0:T(8,128)(2,1)S(1)}, u32[]{:S(2)}, u32[]{:S(2)}) collective-permute-start(bf16[768,256]{1,0:T(8,128)(2,1)S(1)} %collective-permute-done.2.near_ref), channel_id=1, source_target_pairs={{0,8},{4,28},{8,16},{12,4},{16,24},{20,12},{24,0},{28,20},{1,9},{5... | collective-permute-start | bytes 1179656 | tf_op jit(solution)/shard_map/ppermute | solution.py:325
  25.0 14.7 %collective-permute-start.6 = (bf16[768,256]{1,0:T(8,128)(2,1)S(1)}, bf16[768,256]{1,0:T(8,128)(2,1)S(1)}, u32[]{:S(2)}, u32[]{:S(2)}) collective-permute-start(bf16[768,256]{1,0:T(8,128)(2,1)S(1)} %get-tuple-element.278.field_ref.refs_0_), channel_id=1, source_target_pairs={{0,4},{4,0},{8,12},{12,8},{16,20},{20,16},{24,28},{28,24},{1,5},{5... | collective-permute-start | bytes 1179656 | tf_op jit(solution)/shard_map/ppermute | solution.py:316
  31.3 14.1 %collective-permute-start.5 = (bf16[768,256]{1,0:T(8,128)(2,1)S(1)}, bf16[768,256]{1,0:T(8,128)(2,1)S(1)}, u32[]{:S(2)}, u32[]{:S(2)}) collective-permute-start(bf16[768,256]{1,0:T(8,128)(2,1)S(1)} %collective-permute-done.4.near_ref), channel_id=1, source_target_pairs={{0,8},{4,28},{8,16},{12,4},{16,24},{20,12},{24,0},{28,20},{1,9},{5... | collective-permute-start | bytes 1179656 | tf_op jit(solution)/shard_map/ppermute | solution.py:325
  33.4 14.7 %collective-permute-start.3 = (bf16[768,256]{1,0:T(8,128)(2,1)S(1)}, bf16[768,256]{1,0:T(8,128)(2,1)S(1)}, u32[]{:S(2)}, u32[]{:S(2)}) collective-permute-start(bf16[768,256]{1,0:T(8,128)(2,1)S(1)} %get-tuple-element.274.field_ref), channel_id=1, source_target_pairs={{0,4},{4,0},{8,12},{12,8},{16,20},{20,16},{24,28},{28,24},{1,5},{5... | collective-permute-start | bytes 1179656 | tf_op jit(solution)/shard_map/ppermute | solution.py:367
  39.7 14.1 %collective-permute-start.10 = (bf16[768,256]{1,0:T(8,128)(2,1)S(1)}, bf16[768,256]{1,0:T(8,128)(2,1)S(1)}, u32[]{:S(2)}, u32[]{:S(2)}) collective-permute-start(bf16[768,256]{1,0:T(8,128)(2,1)S(1)} %collective-permute-done.6.near_ref), channel_id=1, source_target_pairs={{0,8},{4,28},{8,16},{12,4},{16,24},{20,12},{24,0},{28,20},{1,9},{5... | collective-permute-start | bytes 1179656 | tf_op jit(solution)/shard_map/ppermute | solution.py:325
  41.9 14.7 %collective-permute-start.9 = (bf16[768,256]{1,0:T(8,128)(2,1)S(1)}, bf16[768,256]{1,0:T(8,128)(2,1)S(1)}, u32[]{:S(2)}, u32[]{:S(2)}) collective-permute-start(bf16[768,256]{1,0:T(8,128)(2,1)S(1)} %get-tuple-element.293.field_ref), channel_id=1, source_target_pairs={{0,4},{4,0},{8,12},{12,8},{16,20},{20,16},{24,28},{28,24},{1,5},{5... | collective-permute-start | bytes 1179656 | tf_op jit(solution)/shard_map/ppermute | solution.py:367
  48.2 14.1 %collective-permute-start.8 = (bf16[768,256]{1,0:T(8,128)(2,1)S(1)}, bf16[768,256]{1,0:T(8,128)(2,1)S(1)}, u32[]{:S(2)}, u32[]{:S(2)}) collective-permute-start(bf16[768,256]{1,0:T(8,128)(2,1)S(1)} %collective-permute-done.3.near_ref), channel_id=1, source_target_pairs={{0,8},{4,28},{8,16},{12,4},{16,24},{20,12},{24,0},{28,20},{1,9},{5... | collective-permute-start | bytes 1179656 | tf_op jit(solution)/shard_map/ppermute | solution.py:325
  50.3 14.7 %collective-permute-start.12 = (bf16[768,256]{1,0:T(8,128)(2,1)S(1)}, bf16[768,256]{1,0:T(8,128)(2,1)S(1)}, u32[]{:S(2)}, u32[]{:S(2)}) collective-permute-start(bf16[768,256]{1,0:T(8,128)(2,1)S(1)} %get-tuple-element.305.field_ref), channel_id=1, source_target_pairs={{0,4},{4,0},{8,12},{12,8},{16,20},{20,16},{24,28},{28,24},{1,5},{5... | collective-permute-start | bytes 1179656 | tf_op jit(solution)/shard_map/ppermute | solution.py:367
  56.6 14.1 %collective-permute-start.15 = (bf16[768,256]{1,0:T(8,128)(2,1)S(1)}, bf16[768,256]{1,0:T(8,128)(2,1)S(1)}, u32[]{:S(2)}, u32[]{:S(2)}) collective-permute-start(bf16[768,256]{1,0:T(8,128)(2,1)S(1)} %collective-permute-done.9.near_ref), channel_id=1, source_target_pairs={{0,8},{4,28},{8,16},{12,4},{16,24},{20,12},{24,0},{28,20},{1,9},{5... | collective-permute-start | bytes 1179656 | tf_op jit(solution)/shard_map/ppermute | solution.py:325
  58.7 14.7 %collective-permute-start.14 = (bf16[768,256]{1,0:T(8,128)(2,1)S(1)}, bf16[768,256]{1,0:T(8,128)(2,1)S(1)}, u32[]{:S(2)}, u32[]{:S(2)}) collective-permute-start(bf16[768,256]{1,0:T(8,128)(2,1)S(1)} %get-tuple-element.308.field_ref), channel_id=1, source_target_pairs={{0,4},{4,0},{8,12},{12,8},{16,20},{20,16},{24,28},{28,24},{1,5},{5... | collective-permute-start | bytes 1179656 | tf_op jit(solution)/shard_map/ppermute | solution.py:367
  65.0 14.1 %collective-permute-start.13 = (bf16[768,256]{1,0:T(8,128)(2,1)S(1)}, bf16[768,256]{1,0:T(8,128)(2,1)S(1)}, u32[]{:S(2)}, u32[]{:S(2)}) collective-permute-start(bf16[768,256]{1,0:T(8,128)(2,1)S(1)} %collective-permute-done.12.near_ref), channel_id=1, source_target_pairs={{0,8},{4,28},{8,16},{12,4},{16,24},{20,12},{24,0},{28,20},{1,9},{5... | collective-permute-start | bytes 1179656 | tf_op jit(solution)/shard_map/ppermute | solution.py:325
  67.1 14.7 %collective-permute-start.11 = (bf16[768,256]{1,0:T(8,128)(2,1)S(1)}, bf16[768,256]{1,0:T(8,128)(2,1)S(1)}, u32[]{:S(2)}, u32[]{:S(2)}) collective-permute-start(bf16[768,256]{1,0:T(8,128)(2,1)S(1)} %product_1.4.field_ref), channel_id=1, source_target_pairs={{0,4},{4,0},{8,12},{12,8},{16,20},{20,16},{24,28},{28,24},{1,5},{5... | collective-permute-start | bytes 1179656 | tf_op jit(solution)/shard_map/ppermute | solution.py:367
  73.5 14.1 %collective-permute-start.18 = (bf16[768,256]{1,0:T(8,128)(2,1)S(1)}, bf16[768,256]{1,0:T(8,128)(2,1)S(1)}, u32[]{:S(2)}, u32[]{:S(2)}) collective-permute-start(bf16[768,256]{1,0:T(8,128)(2,1)S(1)} %collective-permute-done.14.near_ref), channel_id=1, source_target_pairs={{0,8},{4,28},{8,16},{12,4},{16,24},{20,12},{24,0},{28,20},{1,9},{5... | collective-permute-start | bytes 1179656 | tf_op jit(solution)/shard_map/ppermute | solution.py:325
  75.6 14.7 %collective-permute-start.17 = (bf16[768,256]{1,0:T(8,128)(2,1)S(1)}, bf16[768,256]{1,0:T(8,128)(2,1)S(1)}, u32[]{:S(2)}, u32[]{:S(2)}) collective-permute-start(bf16[768,256]{1,0:T(8,128)(2,1)S(1)} %product_1.5.field_ref), channel_id=1, source_target_pairs={{0,4},{4,0},{8,12},{12,8},{16,20},{20,16},{24,28},{28,24},{1,5},{5... | collective-permute-start | bytes 1179656 | tf_op jit(solution)/shard_map/ppermute | solution.py:367
  81.9 11.3 %collective-permute-start.16 = (bf16[768,256]{1,0:T(8,128)(2,1)S(1)}, bf16[768,256]{1,0:T(8,128)(2,1)S(1)}, u32[]{:S(2)}, u32[]{:S(2)}) collective-permute-start(bf16[768,256]{1,0:T(8,128)(2,1)S(1)} %collective-permute-done.11.near_ref), channel_id=1, source_target_pairs={{0,8},{4,28},{8,16},{12,4},{16,24},{20,12},{24,0},{28,20},{1,9},{5... | collective-permute-start | bytes 1179656 | tf_op jit(solution)/shard_map/ppermute | solution.py:325
  84.0 14.8 %collective-permute-start.20 = (bf16[768,256]{1,0:T(8,128)(2,1)S(1)}, bf16[768,256]{1,0:T(8,128)(2,1)S(1)}, u32[]{:S(2)}, u32[]{:S(2)}) collective-permute-start(bf16[768,256]{1,0:T(8,128)(2,1)S(1)} %product_1.6.field_ref), channel_id=1, source_target_pairs={{0,4},{4,0},{8,12},{12,8},{16,20},{20,16},{24,28},{28,24},{1,5},{5... | collective-permute-start | bytes 1179656 | tf_op jit(solution)/shard_map/ppermute | solution.py:367
  90.3 11.3 %collective-permute-start.19 = (bf16[768,256]{1,0:T(8,128)(2,1)S(1)}, bf16[768,256]{1,0:T(8,128)(2,1)S(1)}, u32[]{:S(2)}, u32[]{:S(2)}) collective-permute-start(bf16[768,256]{1,0:T(8,128)(2,1)S(1)} %collective-permute-done.17.near_ref), channel_id=1, source_target_pairs={{0,8},{4,28},{8,16},{12,4},{16,24},{20,12},{24,0},{28,20},{1,9},{5... | collective-permute-start | bytes 1179656 | tf_op jit(solution)/shard_map/ppermute | solution.py:325
  94.4 9.9 %collective-permute-start.24 = (bf16[768,256]{1,0:T(8,128)(2,1)S(1)}, bf16[768,256]{1,0:T(8,128)(2,1)S(1)}, u32[]{:S(2)}, u32[]{:S(2)}) collective-permute-start(bf16[768,256]{1,0:T(8,128)(2,1)S(1)} %get-tuple-element.331.refs_0_.refs_2_.refs_8_), channel_id=1, source_target_pairs={{0,2},{1,3},{2,0},{3,1},{4,6},{5,7},{6,4},{7,5},{8,10},{9,11},{10,... | collective-permute-start | bytes 1179656 | tf_op jit(solution)/shard_map/ppermute | solution.py:298
  96.0 8.4 %collective-permute-start.23 = (bf16[768,256]{1,0:T(8,128)(2,1)S(1)}, bf16[768,256]{1,0:T(8,128)(2,1)S(1)}, u32[]{:S(2)}, u32[]{:S(2)}) collective-permute-start(bf16[768,256]{1,0:T(8,128)(2,1)S(1)} %get-tuple-element.331.refs_0_.refs_2_.refs_8_), channel_id=1, source_target_pairs={{0,1},{1,0},{2,3},{3,2},{4,5},{5,4},{6,7},{7,6},{8,9},{9,8},{10,11... | collective-permute-start | bytes 1179656 | tf_op jit(solution)/shard_map/ppermute | solution.py:298
  96.0 12.7 %collective-permute-start.22 = (bf16[768,256]{1,0:T(8,128)(2,1)S(1)}, bf16[768,256]{1,0:T(8,128)(2,1)}, u32[]{:S(2)}, u32[]{:S(2)}) collective-permute-start(bf16[768,256]{1,0:T(8,128)(2,1)S(1)} %product_1.7.field_ref), channel_id=1, source_target_pairs={{0,4},{4,0},{8,12},{12,8},{16,20},{20,16},{24,28},{28,24},{1,5},{5... | collective-permute-start | bytes 1179656 | tf_op jit(solution)/shard_map/ppermute | solution.py:367
  98.8 13.0 %collective-permute-start.21 = (bf16[768,256]{1,0:T(8,128)(2,1)S(1)}, bf16[768,256]{1,0:T(8,128)(2,1)S(1)}, u32[]{:S(2)}, u32[]{:S(2)}) collective-permute-start(bf16[768,256]{1,0:T(8,128)(2,1)S(1)} %collective-permute-done.20.near_ref), channel_id=1, source_target_pairs={{0,8},{4,28},{8,16},{12,4},{16,24},{20,12},{24,0},{28,20},{1,9},{5... | collective-permute-start | bytes 1179656 | tf_op jit(solution)/shard_map/ppermute | solution.py:325
  102.9 11.4 %collective-permute-start.28 = (bf16[768,256]{1,0:T(8,128)(2,1)S(1)}, bf16[768,256]{1,0:T(8,128)(2,1)}, u32[]{:S(2)}, u32[]{:S(2)}) collective-permute-start(bf16[768,256]{1,0:T(8,128)(2,1)S(1)} %get-tuple-element.342.refs_1_.refs_3_.refs_9_), channel_id=1, source_target_pairs={{0,2},{1,3},{2,0},{3,1},{4,6},{5,7},{6,4},{7,5},{8,10},{9,11},{10,... | collective-permute-start | bytes 1179656 | tf_op jit(solution)/shard_map/ppermute | solution.py:298
  104.4 9.9 %collective-permute-start.27 = (bf16[768,256]{1,0:T(8,128)(2,1)S(1)}, bf16[768,256]{1,0:T(8,128)(2,1)S(1)}, u32[]{:S(2)}, u32[]{:S(2)}) collective-permute-start(bf16[768,256]{1,0:T(8,128)(2,1)S(1)} %get-tuple-element.342.refs_1_.refs_3_.refs_9_), channel_id=1, source_target_pairs={{0,1},{1,0},{2,3},{3,2},{4,5},{5,4},{6,7},{7,6},{8,9},{9,8},{10,11... | collective-permute-start | bytes 1179656 | tf_op jit(solution)/shard_map/ppermute | solution.py:298
  104.4 11.2 %collective-permute-start.26 = (bf16[768,256]{1,0:T(8,128)(2,1)S(1)}, bf16[768,256]{1,0:T(8,128)(2,1)S(1)}, u32[]{:S(2)}, u32[]{:S(2)}) collective-permute-start(bf16[768,256]{1,0:T(8,128)(2,1)S(1)} %collective-permute-done.24.refs_4_.refs_1_), channel_id=1, source_target_pairs={{0,1},{1,0},{2,3},{3,2},{4,5},{5,4},{6,7},{7,6},{8,9},{9,8},{10,11... | collective-permute-start | bytes 1179656 | tf_op jit(solution)/shard_map/ppermute | solution.py:298
  108.7 13.1 %collective-permute-start.25 = (bf16[768,256]{1,0:T(8,128)(2,1)}, bf16[768,256]{1,0:T(8,128)(2,1)}, u32[]{:S(2)}, u32[]{:S(2)}) collective-permute-start(bf16[768,256]{1,0:T(8,128)(2,1)} %collective-permute-done.22.near_ref), channel_id=1, source_target_pairs={{0,8},{4,28},{8,16},{12,4},{16,24},{20,12},{24,0},{28,20},{1,9},{5... | collective-permute-start | bytes 1179656 | tf_op jit(solution)/shard_map/ppermute | solution.py:325
  113.7 15.9 %collective-permute-start.31 = (bf16[768,256]{1,0:T(8,128)(2,1)S(1)}, bf16[768,256]{1,0:T(8,128)(2,1)}, u32[]{:S(2)}, u32[]{:S(2)}) collective-permute-start(bf16[768,256]{1,0:T(8,128)(2,1)S(1)} %get-tuple-element.355.refs_2_.refs_4_.refs_10_), channel_id=1, source_target_pairs={{0,2},{1,3},{2,0},{3,1},{4,6},{5,7},{6,4},{7,5},{8,10},{9,11},{10,... | collective-permute-start | bytes 1179656 | tf_op jit(solution)/shard_map/ppermute | solution.py:298
  114.3 15.4 %collective-permute-start.30 = (bf16[768,256]{1,0:T(8,128)(2,1)S(1)}, bf16[768,256]{1,0:T(8,128)(2,1)}, u32[]{:S(2)}, u32[]{:S(2)}) collective-permute-start(bf16[768,256]{1,0:T(8,128)(2,1)S(1)} %get-tuple-element.355.refs_2_.refs_4_.refs_10_), channel_id=1, source_target_pairs={{0,1},{1,0},{2,3},{3,2},{4,5},{5,4},{6,7},{7,6},{8,9},{9,8},{10,11... | collective-permute-start | bytes 1179656 | tf_op jit(solution)/shard_map/ppermute | solution.py:298
  115.1 14.6 %collective-permute-start.29 = (bf16[768,256]{1,0:T(8,128)(2,1)}, bf16[768,256]{1,0:T(8,128)(2,1)S(1)}, u32[]{:S(2)}, u32[]{:S(2)}) collective-permute-start(bf16[768,256]{1,0:T(8,128)(2,1)} %collective-permute-done.28.refs_5_.refs_2_), channel_id=1, source_target_pairs={{0,1},{1,0},{2,3},{3,2},{4,5},{5,4},{6,7},{7,6},{8,9},{9,8},{10,11... | collective-permute-start | bytes 1179656 | tf_op jit(solution)/shard_map/ppermute | solution.py:298
  125.5 10.3 %collective-permute-start.34 = (bf16[784,256]{1,0:T(8,128)(2,1)S(1)}, bf16[784,256]{1,0:T(8,128)(2,1)S(1)}, u32[]{:S(2)}, u32[]{:S(2)}) collective-permute-start(bf16[784,256]{1,0:T(8,128)(2,1)S(1)} %product_2.7.refs_3_.refs_5_.refs_11_), channel_id=1, source_target_pairs={{0,2},{1,3},{2,0},{3,1},{4,6},{5,7},{6,4},{7,5},{8,10},{9,11},{10,... | collective-permute-start | bytes 1204232 | tf_op jit(solution)/shard_map/ppermute | solution.py:298
  130.4 18.4 %collective-permute-start.36 = (bf16[384,1024]{1,0:T(8,128)(2,1)}, bf16[384,1024]{1,0:T(8,128)(2,1)S(1)}, u32[]{:S(2)}, u32[]{:S(2)}) collective-permute-start(bf16[384,1024]{1,0:T(8,128)(2,1)} %get-tuple-element.395), channel_id=1, source_target_pairs={{0,4},{4,0},{8,12},{12,8},{16,20},{20,16},{24,28},{28,24},{1,5},{5... | collective-permute-start | bytes 2359304 | tf_op jit(solution)/shard_map/ppermute | solution.py:394
  130.4 5.4 %collective-permute-start.33 = (bf16[784,256]{1,0:T(8,128)(2,1)S(1)}, bf16[784,256]{1,0:T(8,128)(2,1)}, u32[]{:S(2)}, u32[]{:S(2)}) collective-permute-start(bf16[784,256]{1,0:T(8,128)(2,1)S(1)} %product_2.7.refs_3_.refs_5_.refs_11_), channel_id=1, source_target_pairs={{0,1},{1,0},{2,3},{3,2},{4,5},{5,4},{6,7},{7,6},{8,9},{9,8},{10,11... | collective-permute-start | bytes 1204232 | tf_op jit(solution)/shard_map/ppermute | solution.py:298
  135.8 13.8 %collective-permute-start.35 = (bf16[784,256]{1,0:T(8,128)(2,1)S(1)}, bf16[784,256]{1,0:T(8,128)(2,1)}, u32[]{:S(2)}, u32[]{:S(2)}) collective-permute-start(bf16[784,256]{1,0:T(8,128)(2,1)S(1)} %collective-permute-done.34.refs_7_.refs_9_.refs_4_), channel_id=1, source_target_pairs={{0,1},{1,0},{2,3},{3,2},{4,5},{5,4},{6,7},{7,6},{8,9},{9,8},{10,11... | collective-permute-start | bytes 1204232 | tf_op jit(solution)/shard_map/ppermute | solution.py:298
  139.3 17.1 %collective-permute-start.39 = (bf16[256,1024]{1,0:T(8,128)(2,1)S(1)}, bf16[256,1024]{1,0:T(8,128)(2,1)S(1)}, u32[]{:S(2)}, u32[]{:S(2)}) collective-permute-start(bf16[256,1024]{1,0:T(8,128)(2,1)S(1)} %get-tuple-element.424), channel_id=1, source_target_pairs={{0,8},{4,12},{8,0},{12,4},{16,24},{20,28},{24,16},{28,20},{1,9},{5... | collective-permute-start | bytes 1572872 | tf_op jit(solution)/shard_map/ppermute | solution.py:394
  152.0 19.3 %collective-permute-start.37 = (bf16[272,1024]{1,0:T(8,128)(2,1)S(1)}, bf16[272,1024]{1,0:T(8,128)(2,1)S(1)}, u32[]{:S(2)}, u32[]{:S(2)}) collective-permute-start(bf16[272,1024]{1,0:T(8,128)(2,1)S(1)} %get-tuple-element.421), channel_id=1, source_target_pairs={{0,4},{4,0},{8,12},{12,8},{16,20},{20,16},{24,28},{28,24},{1,5},{5... | collective-permute-start | bytes 1671176 | tf_op jit(solution)/shard_map/ppermute | solution.py:394
  152.4 18.2 %collective-permute-start.38 = (bf16[192,1024]{1,0:T(8,128)(2,1)S(1)}, bf16[192,1024]{1,0:T(8,128)(2,1)S(1)}, u32[]{:S(2)}, u32[]{:S(2)}) collective-permute-start(bf16[192,1024]{1,0:T(8,128)(2,1)S(1)} %sum_hop.8), channel_id=1, source_target_pairs={{0,16},{4,20},{8,24},{12,28},{16,0},{20,4},{24,8},{28,12},{1,17},{... | collective-permute-start | bytes 1179656 | tf_op jit(solution)/shard_map/ppermute | solution.py:394
  154.9 24.2 %collective-permute-start.41 = (bf16[256,1024]{1,0:T(8,128)(2,1)S(1)}, bf16[256,1024]{1,0:T(8,128)(2,1)S(1)}, u32[]{:S(2)}, u32[]{:S(2)}) collective-permute-start(bf16[256,1024]{1,0:T(8,128)(2,1)S(1)} %get-tuple-element.447), channel_id=1, source_target_pairs={{0,4},{4,0},{8,12},{12,8},{16,20},{20,16},{24,28},{28,24},{1,5},{5... | collective-permute-start | bytes 1572872 | tf_op jit(solution)/shard_map/ppermute | solution.py:394
  171.2 7.9 %collective-permute-start.42 = (bf16[96,1024]{1,0:T(8,128)(2,1)S(1)}, bf16[96,1024]{1,0:T(8,128)(2,1)S(1)}, u32[]{:S(2)}, u32[]{:S(2)}) collective-permute-start(bf16[96,1024]{1,0:T(8,128)(2,1)S(1)} %sum_hop.10), channel_id=1, source_target_pairs={{0,8},{4,12},{8,0},{12,4},{16,24},{20,28},{24,16},{28,20},{1,9},{5... | collective-permute-start | bytes 589832 | tf_op jit(solution)/shard_map/ppermute | solution.py:394
  171.9 13.5 %collective-permute-start.40 = (bf16[144,1024]{1,0:T(8,128)(2,1)S(1)}, bf16[144,1024]{1,0:T(8,128)(2,1)S(1)}, u32[]{:S(2)}, u32[]{:S(2)}) collective-permute-start(bf16[144,1024]{1,0:T(8,128)(2,1)S(1)} %sum_hop.11), channel_id=1, source_target_pairs={{0,8},{4,12},{8,0},{12,4},{16,24},{20,28},{24,16},{28,20},{1,9},{5... | collective-permute-start | bytes 884744 | tf_op jit(solution)/shard_map/ppermute | solution.py:394
  174.0 12.6 %collective-permute-start.45 = (bf16[128,1024]{1,0:T(8,128)(2,1)S(1)}, bf16[128,1024]{1,0:T(8,128)(2,1)S(1)}, u32[]{:S(2)}, u32[]{:S(2)}) collective-permute-start(bf16[128,1024]{1,0:T(8,128)(2,1)S(1)} %sum_hop.9), channel_id=1, source_target_pairs={{0,4},{4,0},{8,12},{12,8},{16,20},{20,16},{24,28},{28,24},{1,5},{5... | collective-permute-start | bytes 786440 | tf_op jit(solution)/shard_map/ppermute | solution.py:394
  179.7 11.8 %collective-permute-start.44 = (bf16[128,1024]{1,0:T(8,128)(2,1)S(1)}, bf16[128,1024]{1,0:T(8,128)(2,1)S(1)}, u32[]{:S(2)}, u32[]{:S(2)}) collective-permute-start(bf16[128,1024]{1,0:T(8,128)(2,1)S(1)} %sum_hop.12), channel_id=1, source_target_pairs={{0,8},{4,12},{8,0},{12,4},{16,24},{20,28},{24,16},{28,20},{1,9},{5... | collective-permute-start | bytes 786440 | tf_op jit(solution)/shard_map/ppermute | solution.py:394
  186.1 19.2 %collective-permute-start.43 = (bf16[80,1024]{1,0:T(8,128)(2,1)S(1)}, bf16[80,1024]{1,0:T(8,128)(2,1)S(1)}, u32[]{:S(2)}, u32[]{:S(2)}) collective-permute-start(bf16[80,1024]{1,0:T(8,128)(2,1)S(1)} %sum_hop.13), channel_id=1, source_target_pairs={{0,16},{4,20},{8,24},{12,28},{16,0},{20,4},{24,8},{28,12},{1,17},{... | collective-permute-start | bytes 491528 | tf_op jit(solution)/shard_map/ppermute | solution.py:394
  192.2 13.1 %collective-permute-start.46 = (bf16[64,1024]{1,0:T(8,128)(2,1)S(1)}, bf16[64,1024]{1,0:T(8,128)(2,1)S(1)}, u32[]{:S(2)}, u32[]{:S(2)}) collective-permute-start(bf16[64,1024]{1,0:T(8,128)(2,1)S(1)} %sum_hop.15), channel_id=1, source_target_pairs={{0,16},{4,20},{8,24},{12,28},{16,0},{20,4},{24,8},{28,12},{1,17},{... | collective-permute-start | bytes 393224 | tf_op jit(solution)/shard_map/ppermute | solution.py:394
  192.7 17.7 %collective-permute-start.47 = (bf16[64,1024]{1,0:T(8,128)(2,1)S(1)}, bf16[64,1024]{1,0:T(8,128)(2,1)S(1)}, u32[]{:S(2)}, u32[]{:S(2)}) collective-permute-start(bf16[64,1024]{1,0:T(8,128)(2,1)S(1)} %sum_hop.14), channel_id=1, source_target_pairs={{0,16},{4,20},{8,24},{12,28},{16,0},{20,4},{24,8},{28,12},{1,17},{... | collective-permute-start | bytes 393224 | tf_op jit(solution)/shard_map/ppermute | solution.py:394
  206.6 12.5 %collective-permute-start.48 = (bf16[64,1024]{1,0:T(8,128)(2,1)S(1)}, bf16[64,1024]{1,0:T(8,128)(2,1)S(1)}, u32[]{:S(2)}, u32[]{:S(2)}) collective-permute-start(bf16[64,1024]{1,0:T(8,128)(2,1)S(1)} %sum_last.7), channel_id=1, source_target_pairs={{0,16},{4,20},{8,24},{12,28},{16,0},{20,4},{24,8},{28,12},{1,17},{... | collective-permute-start | bytes 393224 | tf_op jit(solution)/shard_map/ppermute | solution.py:394
  206.7 15.3 %collective-permute-start.50 = (bf16[64,1024]{1,0:T(8,128)(2,1)S(1)}, bf16[64,1024]{1,0:T(8,128)(2,1)S(1)}, u32[]{:S(2)}, u32[]{:S(2)}) collective-permute-start(bf16[64,1024]{1,0:T(8,128)(2,1)S(1)} %get-tuple-element.483), channel_id=1, source_target_pairs={{0,16},{4,20},{8,24},{12,28},{16,0},{20,4},{24,8},{28,12},{1,17},{... | collective-permute-start | bytes 393224 | tf_op jit(solution)/shard_map/ppermute | solution.py:394
  211.0 12.7 %collective-permute-start.49 = (bf16[64,1024]{1,0:T(8,128)(2,1)S(1)}, bf16[64,1024]{1,0:T(8,128)(2,1)S(1)}, u32[]{:S(2)}, u32[]{:S(2)}) collective-permute-start(bf16[64,1024]{1,0:T(8,128)(2,1)S(1)} %sum_last.6), channel_id=1, source_target_pairs={{0,16},{4,20},{8,24},{12,28},{16,0},{20,4},{24,8},{28,12},{1,17},{... | collective-permute-start | bytes 393224 | tf_op jit(solution)/shard_map/ppermute | solution.py:394
  211.2 13.3 %collective-permute-start.51 = (bf16[96,1024]{1,0:T(8,128)(2,1)S(1)}, bf16[96,1024]{1,0:T(8,128)(2,1)S(1)}, u32[]{:S(2)}, u32[]{:S(2)}) collective-permute-start(bf16[96,1024]{1,0:T(8,128)(2,1)S(1)} %sum_last.5), channel_id=1, source_target_pairs={{0,8},{4,12},{8,0},{12,4},{16,24},{20,28},{24,16},{28,20},{1,9},{5... | collective-permute-start | bytes 589832 | tf_op jit(solution)/shard_map/ppermute | solution.py:394
  222.0 16.9 %collective-permute-start.52 = (bf16[128,1024]{1,0:T(8,128)(2,1)S(1)}, bf16[128,1024]{1,0:T(8,128)(2,1)S(1)}, u32[]{:S(2)}, u32[]{:S(2)}) collective-permute-start(bf16[128,1024]{1,0:T(8,128)(2,1)S(1)} %pad_maximum_fusion.5), channel_id=1, source_target_pairs={{0,8},{4,12},{8,0},{12,4},{16,24},{20,28},{24,16},{28,20},{1,9},{5... | collective-permute-start | bytes 786440 | tf_op jit(solution)/shard_map/ppermute | solution.py:394
  223.7 20.1 %collective-permute-start.54 = (bf16[128,1024]{1,0:T(8,128)(2,1)S(1)}, bf16[128,1024]{1,0:T(8,128)(2,1)S(1)}, u32[]{:S(2)}, u32[]{:S(2)}) collective-permute-start(bf16[128,1024]{1,0:T(8,128)(2,1)S(1)} %pad_maximum_fusion.6), channel_id=1, source_target_pairs={{0,8},{4,12},{8,0},{12,4},{16,24},{20,28},{24,16},{28,20},{1,9},{5... | collective-permute-start | bytes 786440 | tf_op jit(solution)/shard_map/ppermute | solution.py:394
  224.5 21.2 %collective-permute-start.64 = (bf16[192,1024]{1,0:T(8,128)(2,1)S(1)}, bf16[192,1024]{1,0:T(8,128)(2,1)S(1)}, u32[]{:S(2)}, u32[]{:S(2)}) collective-permute-start(bf16[192,1024]{1,0:T(8,128)(2,1)S(1)} %pad_maximum_fusion.4), channel_id=1, source_target_pairs={{0,16},{4,20},{8,24},{12,28},{16,0},{20,4},{24,8},{28,12},{1,17},{... | collective-permute-start | bytes 1179656 | tf_op jit(solution)/shard_map/ppermute | solution.py:394
  226.3 17.5 %collective-permute-start.53 = (bf16[128,1024]{1,0:T(8,128)(2,1)S(1)}, bf16[128,1024]{1,0:T(8,128)(2,1)S(1)}, u32[]{:S(2)}, u32[]{:S(2)}) collective-permute-start(bf16[128,1024]{1,0:T(8,128)(2,1)S(1)} %pad_maximum_fusion.7), channel_id=1, source_target_pairs={{0,4},{4,0},{8,12},{12,8},{16,20},{20,16},{24,28},{28,24},{1,5},{5... | collective-permute-start | bytes 786440 | tf_op jit(solution)/shard_map/ppermute | solution.py:394
  238.9 14.4 %collective-permute-start.55 = (bf16[256,1024]{1,0:T(8,128)(2,1)S(1)}, bf16[256,1024]{1,0:T(8,128)(2,1)S(1)}, u32[]{:S(2)}, u32[]{:S(2)}) collective-permute-start(bf16[256,1024]{1,0:T(8,128)(2,1)S(1)} %pad_maximum_fusion.1.refs_4_), channel_id=1, source_target_pairs={{0,4},{4,0},{8,12},{12,8},{16,20},{20,16},{24,28},{28,24},{1,5},{5... | collective-permute-start | bytes 1572872 | tf_op jit(solution)/shard_map/ppermute | solution.py:394
  243.8 20.7 %collective-permute-start.58 = (bf16[256,1024]{1,0:T(8,128)(2,1)S(1)}, bf16[256,1024]{1,0:T(8,128)(2,1)S(1)}, u32[]{:S(2)}, u32[]{:S(2)}) collective-permute-start(bf16[256,1024]{1,0:T(8,128)(2,1)S(1)} %pad_maximum_fusion.2.refs_5_), channel_id=1, source_target_pairs={{0,4},{4,0},{8,12},{12,8},{16,20},{20,16},{24,28},{28,24},{1,5},{5... | collective-permute-start | bytes 1572872 | tf_op jit(solution)/shard_map/ppermute | solution.py:394
  244.2 20.4 %collective-permute-start.62 = (bf16[256,1024]{1,0:T(8,128)(2,1)S(1)}, bf16[256,1024]{1,0:T(8,128)(2,1)S(1)}, u32[]{:S(2)}, u32[]{:S(2)}) collective-permute-start(bf16[256,1024]{1,0:T(8,128)(2,1)S(1)} %pad_maximum_fusion.3.refs_5_), channel_id=1, source_target_pairs={{0,2},{1,3},{2,0},{3,1},{4,6},{5,7},{6,4},{7,5},{8,10},{9,11},{10,... | collective-permute-start | bytes 1572872 | tf_op jit(solution)/shard_map/ppermute | solution.py:298
  245.7 21.9 %collective-permute-start.59 = (bf16[256,1024]{1,0:T(8,128)(2,1)S(1)}, bf16[256,1024]{1,0:T(8,128)(2,1)S(1)}, u32[]{:S(2)}, u32[]{:S(2)}) collective-permute-start(bf16[256,1024]{1,0:T(8,128)(2,1)S(1)} %pad_maximum_fusion.2.refs_5_), channel_id=1, source_target_pairs={{0,3},{1,2},{2,1},{3,0},{4,7},{5,6},{6,5},{7,4},{8,11},{9,10},{10,... | collective-permute-start | bytes 1572872 | tf_op jit(solution)/shard_map/ppermute | solution.py:298
  245.7 21.9 %collective-permute-start.56 = (bf16[256,1024]{1,0:T(8,128)(2,1)S(1)}, bf16[256,1024]{1,0:T(8,128)(2,1)S(1)}, u32[]{:S(2)}, u32[]{:S(2)}) collective-permute-start(bf16[256,1024]{1,0:T(8,128)(2,1)S(1)} %pad_maximum_fusion.1.refs_4_), channel_id=1, source_target_pairs={{0,1},{1,0},{2,3},{3,2},{4,5},{5,4},{6,7},{7,6},{8,9},{9,8},{10,11... | collective-permute-start | bytes 1572872 | tf_op jit(solution)/shard_map/ppermute | solution.py:298
  253.3 39.7 %collective-permute-start.65 = (bf16[384,1024]{1,0:T(8,128)(2,1)S(1)}, bf16[384,1024]{1,0:T(8,128)(2,1)S(1)}, u32[]{:S(2)}, u32[]{:S(2)}) collective-permute-start(bf16[384,1024]{1,0:T(8,128)(2,1)S(1)} %pad_maximum_fusion.refs_6_), channel_id=1, source_target_pairs={{0,4},{4,0},{8,12},{12,8},{16,20},{20,16},{24,28},{28,24},{1,5},{5... | collective-permute-start | bytes 2359304 | tf_op jit(solution)/shard_map/ppermute | solution.py:394
  264.6 13.9 %collective-permute-start.60 = (bf16[256,1024]{1,0:T(8,128)(2,1)S(1)}, bf16[256,1024]{1,0:T(8,128)(2,1)S(1)}, u32[]{:S(2)}, u32[]{:S(2)}) collective-permute-start(bf16[256,1024]{1,0:T(8,128)(2,1)S(1)} %collective-permute-done.58.refs_6_), channel_id=1, source_target_pairs={{0,3},{1,2},{2,1},{3,0},{4,7},{5,6},{6,5},{7,4},{8,11},{9,10},{10,... | collective-permute-start | bytes 1572872 | tf_op jit(solution)/shard_map/ppermute | solution.py:298
  267.6 14.8 %collective-permute-start.61 = (bf16[256,1024]{1,0:T(8,128)(2,1)S(1)}, bf16[256,1024]{1,0:T(8,128)(2,1)S(1)}, u32[]{:S(2)}, u32[]{:S(2)}) collective-permute-start(bf16[256,1024]{1,0:T(8,128)(2,1)S(1)} %pad_maximum_fusion.3.refs_5_), channel_id=1, source_target_pairs={{0,8},{4,12},{8,0},{12,4},{16,24},{20,28},{24,16},{28,20},{1,9},{5... | collective-permute-start | bytes 1572872 | tf_op jit(solution)/shard_map/ppermute | solution.py:394
  267.6 25.4 %collective-permute-start.63 = (bf16[256,1024]{1,0:T(8,128)(2,1)S(1)}, bf16[256,1024]{1,0:T(8,128)(2,1)S(1)}, u32[]{:S(2)}, u32[]{:S(2)}) collective-permute-start(bf16[256,1024]{1,0:T(8,128)(2,1)S(1)} %collective-permute-done.62.refs_7_), channel_id=1, source_target_pairs={{0,8},{4,12},{8,0},{12,4},{16,24},{20,28},{24,16},{28,20},{1,9},{5... | collective-permute-start | bytes 1572872 | tf_op jit(solution)/shard_map/ppermute | solution.py:394
  (21 other events, 119.8 us)

commit v9 on v8

--- a/solution.py
+++ b/solution.py
@@ -357,11 +357,9 @@
             while bit:
                 pieces[c][bit] = to_group(out, bit)
                 bit //= 2
-            if c:
-                more_panel(c - 1)
-                settle(c - 1, lambda d: not d & (d - 1))
             if c > 1:
-                settle(c - 2)
+                more_panel(c - 2)
+                settle(c - 2, lambda d: not d & (d - 1))
             return
         current[(stage + 1, c)] = out
         near[(stage + 1, c)] = lax.ppermute(out, "elem", swap)
@@ -401,10 +399,13 @@
         return to_group(value, d), clock.transfer(value, "core" if d == 1 else "x")
 
     def panel_process():
+        yield 4.0
+        for c in range(CHUNKS - 1):
+            more_panel(c)
+            settle(c)
         yield 10.5
         more_panel(CHUNKS - 1)
         settle(CHUNKS - 1, lambda d: not d & (d - 1))
-        settle(CHUNKS - 2)
         clock.spend(1.3)
         for d in range(1, groups):
             if d & (d - 1):
@@ -426,7 +427,9 @@
             functools.partial(gram_kernel, d > 0, mask), name, (half, half), (where(d),), fields, scratch, moved=5 * MIB
         )
 
-    def process(d, masks, extra=0, round_y=False):
+    sent = [None]
+
+    def process(d, masks, extra=0, round_y=False, behind=None):
         nonlocal mixed, mixes, level
         need = list(there) if extra else [d] if d else []
         while any(other not in pieces[-1] or there[other] > clock.now for other in need):
@@ -469,18 +472,27 @@
             yield arrival
             part = order(jnp.concatenate([part, order(received)], axis=0))
             clock.spend(0.5)
+        while behind not in sent:
+            yield clock.now + 0.5
+        part = order(part)
         far, arrival = over_tiles(part, masks[0])
+        sent.append(d)
         if d:
             peer, peer_arrival = over_groups(part, d)
         if round_y:
+            clock.now = max(clock.now, arrival)
+            far = order(far)
             yield peer_arrival
             peer = order(peer)
             peer_far, peer_arrival = over_tiles(peer, masks[0])
         elif d:
             yield peer_arrival - 3.0
             peer = order(peer)
-        yield arrival
-        far = order(far)
+            yield arrival
+            far = order(far)
+        else:
+            yield arrival
+            far = order(far)
         parts = (part, far)
         if d:
             if not round_y:
@@ -509,8 +521,9 @@
     processes = [panel_process()]
     for d in queue:
         first = d == queue[0] and d != carrier
-        processes.append(process(d, z_then_y if first else y_first, EXTRA if d == carrier else 0, first))
-    processes.append(process(0, y_then_far))
+        behind = carrier if d == 1 and d != carrier else None
+        processes.append(process(d, z_then_y if first else y_first, EXTRA if d == carrier else 0, first, behind))
+    processes.append(process(0, y_then_far, behind=1))
     clock.run(processes)
     return mixed
 

time: 301 us -> 301 us (level)
  starting transfers between devices: 92 us -> 109 us
  waiting for transfers between devices: 145 us -> 130 us
    ppermute x25, waiting for transfers between devices: 100 us -> 79 us  [over_tiles(): sent = lax.ppermute(value, 'elem', [(i, i ^ mask) for i in range(tiles)])]
    ppermute x25, starting transfers between devices: 22.9 us -> 36.2 us  [over_tiles(): sent = lax.ppermute(value, 'elem', [(i, i ^ mask) for i in range(tiles)])]
    ppermute x17, waiting for transfers between devices: 12.3 us -> 21.7 us  [to_group(): return lax.ppermute(value, 'orb', [(i, i ^ d) for i in range(groups)])]
    ppermute x12, waiting for transfers between devices: 11.2 us -> 6.98 us  [send_on(): far[job] = lax.ppermute(near[job], 'elem', outward)]
    unnamed x39 -> x49, local copies, waits for them, and re-layouts: 6.73 us -> 7.66 us
  transfers between devices with their start and end apart: 66 -> 66, of which waited for: 34 -> 34; matrix products, arithmetic and copies ran while one was open for 2% -> 2% of each run, Pallas kernels for 13% -> 12%
where the time goes in v9:
time: 301 us
  waiting for transfers between devices  130 us (43%)
  starting transfers between devices  109 us (36%)
  Pallas kernels  45.3 us (15%)
  local copies, waits for them, and re-layouts  13.8 us (5%)
    ppermute x25, waiting for transfers between devices, over_tiles(): sent = lax.ppermute(value, 'elem', [(i, i ^ mask) for i in range(tiles)])  79 us
    pallas_call x32, Pallas kernels, call(): pl.pallas_call(kernel, out_shape=outs, in_specs=[pl.BlockSpec(memory_spac...  45.3 us
    ppermute x25, starting transfers between devices, over_tiles(): sent = lax.ppermute(value, 'elem', [(i, i ^ mask) for i in range(tiles)])  36.2 us
    ppermute x8, starting transfers between devices, multiply(): near[stage + 1, c] = lax.ppermute(out, 'elem', swap)  28.9 us
    ppermute x12, starting transfers between devices, send_on(): far[job] = lax.ppermute(near[job], 'elem', outward)  24.3 us
    ppermute x17, waiting for transfers between devices, to_group(): return lax.ppermute(value, 'orb', [(i, i ^ d) for i in range(groups)])  21.7 us
    ppermute x8, waiting for transfers between devices, multiply(): near[stage + 1, c] = lax.ppermute(out, 'elem', swap)  13.2 us
    ppermute x17, starting transfers between devices, to_group(): return lax.ppermute(value, 'orb', [(i, i ^ d) for i in range(groups)])  9.12 us
  transfers between devices with their start and end apart: 66, of which 34 were waited for; matrix products, arithmetic and copies ran while one was open for 2% of the time, Pallas kernels for 12%

profile of v9, /device:TPU:0, one launch (start us, length us, event | category | flops | bytes accessed | tf_op | source)
XLA Modules:
  0.0 300.6 jit_solution(5254047624705416411)
XLA Ops:
  1.5 3.0 %collective-permute-start = (bf16[768,256]{1,0:T(8,128)(2,1)S(1)}, bf16[768,256]{1,0:T(8,128)(2,1)S(1)}, u32[]{:S(2)}, u32[]{:S(2)}) collective-permute-start(bf16[768,256]{1,0:T(8,128)(2,1)S(1)} %get-tuple-element.513.field_ref.refs_0_), channel_id=1, source_target_pairs={{0,4},{4,0},{8,12},{12,8},{16,20},{20,16},{24,28},{28,24},{1,5},{5... | collective-permute-start | bytes 1179656 | tf_op jit(solution)/shard_map/ppermute | solution.py:311
  4.8 2.2 slice_bitcast_fusion
  8.2 2.3 concatenate.30.blocks_ref
  10.6 3.9 %collective-permute-done.near_ref = bf16[768,256]{1,0:T(8,128)(2,1)S(1)} collective-permute-done((bf16[768,256]{1,0:T(8,128)(2,1)S(1)}, bf16[768,256]{1,0:T(8,128)(2,1)S(1)}, u32[]{:S(2)}, u32[]{:S(2)}) %collective-permute-start) | collective-permute-done | bytes 393248 | tf_op jit(solution)/shard_map/ppermute | solution.py:311
  14.5 2.0 collective-permute-start.1
  16.5 3.6 %collective-permute-start.4 = (bf16[768,256]{1,0:T(8,128)(2,1)S(1)}, bf16[768,256]{1,0:T(8,128)(2,1)S(1)}, u32[]{:S(2)}, u32[]{:S(2)}) collective-permute-start(bf16[768,256]{1,0:T(8,128)(2,1)S(1)} %get-tuple-element.273.field_ref.refs_0_), channel_id=1, source_target_pairs={{0,4},{4,0},{8,12},{12,8},{16,20},{20,16},{24,28},{28,24},{1,5},{5... | collective-permute-start | bytes 1179656 | tf_op jit(solution)/shard_map/ppermute | solution.py:316
  20.1 2.8 collective-permute-done.2.near_ref
  22.9 2.0 collective-permute-start.7
  24.9 3.6 %collective-permute-start.6 = (bf16[768,256]{1,0:T(8,128)(2,1)S(1)}, bf16[768,256]{1,0:T(8,128)(2,1)S(1)}, u32[]{:S(2)}, u32[]{:S(2)}) collective-permute-start(bf16[768,256]{1,0:T(8,128)(2,1)S(1)} %get-tuple-element.276.field_ref.refs_0_), channel_id=1, source_target_pairs={{0,4},{4,0},{8,12},{12,8},{16,20},{20,16},{24,28},{28,24},{1,5},{5... | collective-permute-start | bytes 1179656 | tf_op jit(solution)/shard_map/ppermute | solution.py:316
  31.3 2.0 collective-permute-start.5
  33.4 3.6 %collective-permute-start.3 = (bf16[768,256]{1,0:T(8,128)(2,1)S(1)}, bf16[768,256]{1,0:T(8,128)(2,1)S(1)}, u32[]{:S(2)}, u32[]{:S(2)}) collective-permute-start(bf16[768,256]{1,0:T(8,128)(2,1)S(1)} %get-tuple-element.272.field_ref), channel_id=1, source_target_pairs={{0,4},{4,0},{8,12},{12,8},{16,20},{20,16},{24,28},{28,24},{1,5},{5... | collective-permute-start | bytes 1179656 | tf_op jit(solution)/shard_map/ppermute | solution.py:365
  39.7 2.0 collective-permute-start.10
  41.8 3.6 %collective-permute-start.9 = (bf16[768,256]{1,0:T(8,128)(2,1)S(1)}, bf16[768,256]{1,0:T(8,128)(2,1)S(1)}, u32[]{:S(2)}, u32[]{:S(2)}) collective-permute-start(bf16[768,256]{1,0:T(8,128)(2,1)S(1)} %get-tuple-element.291.field_ref), channel_id=1, source_target_pairs={{0,4},{4,0},{8,12},{12,8},{16,20},{20,16},{24,28},{28,24},{1,5},{5... | collective-permute-start | bytes 1179656 | tf_op jit(solution)/shard_map/ppermute | solution.py:365
  48.2 2.0 collective-permute-start.8
  50.2 3.6 %collective-permute-start.12 = (bf16[768,256]{1,0:T(8,128)(2,1)S(1)}, bf16[768,256]{1,0:T(8,128)(2,1)S(1)}, u32[]{:S(2)}, u32[]{:S(2)}) collective-permute-start(bf16[768,256]{1,0:T(8,128)(2,1)S(1)} %get-tuple-element.303.field_ref), channel_id=1, source_target_pairs={{0,4},{4,0},{8,12},{12,8},{16,20},{20,16},{24,28},{28,24},{1,5},{5... | collective-permute-start | bytes 1179656 | tf_op jit(solution)/shard_map/ppermute | solution.py:365
  56.6 2.0 collective-permute-start.15
  58.6 3.6 %collective-permute-start.14 = (bf16[768,256]{1,0:T(8,128)(2,1)S(1)}, bf16[768,256]{1,0:T(8,128)(2,1)S(1)}, u32[]{:S(2)}, u32[]{:S(2)}) collective-permute-start(bf16[768,256]{1,0:T(8,128)(2,1)S(1)} %get-tuple-element.306.field_ref), channel_id=1, source_target_pairs={{0,4},{4,0},{8,12},{12,8},{16,20},{20,16},{24,28},{28,24},{1,5},{5... | collective-permute-start | bytes 1179656 | tf_op jit(solution)/shard_map/ppermute | solution.py:365
  65.0 2.0 collective-permute-start.13
  67.1 3.6 %collective-permute-start.11 = (bf16[768,256]{1,0:T(8,128)(2,1)S(1)}, bf16[768,256]{1,0:T(8,128)(2,1)S(1)}, u32[]{:S(2)}, u32[]{:S(2)}) collective-permute-start(bf16[768,256]{1,0:T(8,128)(2,1)S(1)} %product_1.4.field_ref), channel_id=1, source_target_pairs={{0,4},{4,0},{8,12},{12,8},{16,20},{20,16},{24,28},{28,24},{1,5},{5... | collective-permute-start | bytes 1179656 | tf_op jit(solution)/shard_map/ppermute | solution.py:365
  73.5 2.0 collective-permute-start.18
  75.5 3.6 %collective-permute-start.17 = (bf16[768,256]{1,0:T(8,128)(2,1)S(1)}, bf16[768,256]{1,0:T(8,128)(2,1)S(1)}, u32[]{:S(2)}, u32[]{:S(2)}) collective-permute-start(bf16[768,256]{1,0:T(8,128)(2,1)S(1)} %product_1.5.field_ref), channel_id=1, source_target_pairs={{0,4},{4,0},{8,12},{12,8},{16,20},{20,16},{24,28},{28,24},{1,5},{5... | collective-permute-start | bytes 1179656 | tf_op jit(solution)/shard_map/ppermute | solution.py:365
  81.9 2.0 collective-permute-start.16
  83.9 3.6 %collective-permute-start.20 = (bf16[768,256]{1,0:T(8,128)(2,1)S(1)}, bf16[768,256]{1,0:T(8,128)(2,1)S(1)}, u32[]{:S(2)}, u32[]{:S(2)}) collective-permute-start(bf16[768,256]{1,0:T(8,128)(2,1)S(1)} %product_1.6.field_ref), channel_id=1, source_target_pairs={{0,4},{4,0},{8,12},{12,8},{16,20},{20,16},{24,28},{28,24},{1,5},{5... | collective-permute-start | bytes 1179656 | tf_op jit(solution)/shard_map/ppermute | solution.py:365
  90.3 2.0 collective-permute-start.19
  92.4 3.6 %collective-permute-start.22 = (bf16[768,256]{1,0:T(8,128)(2,1)S(1)}, bf16[768,256]{1,0:T(8,128)(2,1)S(1)}, u32[]{:S(2)}, u32[]{:S(2)}) collective-permute-start(bf16[768,256]{1,0:T(8,128)(2,1)S(1)} %product_1.7.field_ref), channel_id=1, source_target_pairs={{0,4},{4,0},{8,12},{12,8},{16,20},{20,16},{24,28},{28,24},{1,5},{5... | collective-permute-start | bytes 1179656 | tf_op jit(solution)/shard_map/ppermute | solution.py:365
  98.7 2.0 collective-permute-start.21
  103.6 2.8 collective-permute-done.22.near_ref
  106.3 1.8 collective-permute-start.23
  111.9 6.5 %collective-permute-done.23.far_ref = bf16[768,256]{1,0:T(8,128)(2,1)S(1)} collective-permute-done((bf16[768,256]{1,0:T(8,128)(2,1)S(1)}, bf16[768,256]{1,0:T(8,128)(2,1)S(1)}, u32[]{:S(2)}, u32[]{:S(2)}) %collective-permute-start.23) | collective-permute-done | bytes 393248 | tf_op jit(solution)/shard_map/ppermute | solution.py:325
  122.2 3.0 gram_own.1
  127.4 4.6 %collective-permute-done.30.refs_6_.refs_3_ = bf16[768,256]{1,0:T(8,128)(2,1)S(1)} collective-permute-done((bf16[768,256]{1,0:T(8,128)(2,1)S(1)}, bf16[768,256]{1,0:T(8,128)(2,1)S(1)}, u32[]{:S(2)}, u32[]{:S(2)}) %collective-permute-start.30) | collective-permute-done | bytes 393248 | tf_op jit(solution)/shard_map/ppermute | solution.py:298
  135.8 4.3 %collective-permute-done.33.refs_7_.refs_9_.refs_4_ = bf16[784,256]{1,0:T(8,128)(2,1)S(1)} collective-permute-done((bf16[784,256]{1,0:T(8,128)(2,1)S(1)}, bf16[784,256]{1,0:T(8,128)(2,1)S(1)}, u32[]{:S(2)}, u32[]{:S(2)}) %collective-permute-start.33) | collective-permute-done | bytes 401440 | tf_op jit(solution)/shard_map/ppermute | solution.py:298
  143.2 1.8 gram_pair.3
  145.1 7.8 %collective-permute-done.35.refs_1_ = bf16[384,1024]{1,0:T(8,128)(2,1)S(1)} collective-permute-done((bf16[384,1024]{1,0:T(8,128)(2,1)}, bf16[384,1024]{1,0:T(8,128)(2,1)S(1)}, u32[]{:S(2)}, u32[]{:S(2)}) %collective-permute-start.35) | collective-permute-done | bytes 786464 | tf_op jit(solution)/shard_map/ppermute | solution.py:392
  153.6 2.3 gram_pair.4
  157.3 4.2 %collective-permute-start.38 = (bf16[192,1024]{1,0:T(8,128)(2,1)S(1)}, bf16[192,1024]{1,0:T(8,128)(2,1)S(1)}, u32[]{:S(2)}, u32[]{:S(2)}) collective-permute-start(bf16[192,1024]{1,0:T(8,128)(2,1)S(1)} %sum_hop.8), channel_id=1, source_target_pairs={{0,16},{4,20},{8,24},{12,28},{16,0},{20,4},{24,8},{28,12},{1,17},{... | collective-permute-start | bytes 1179656 | tf_op jit(solution)/shard_map/ppermute | solution.py:392
  161.6 2.1 gram_pair.5
  164.0 15.0 %collective-permute-done.39.refs_1_ = bf16[256,1024]{1,0:T(8,128)(2,1)S(1)} collective-permute-done((bf16[256,1024]{1,0:T(8,128)(2,1)S(1)}, bf16[256,1024]{1,0:T(8,128)(2,1)S(1)}, u32[]{:S(2)}, u32[]{:S(2)}) %collective-permute-start.39) | collective-permute-done | bytes 524320 | tf_op jit(solution)/shard_map/ppermute | solution.py:392
  180.3 1.9 collective-permute-start.42
  183.8 4.3 %collective-permute-done.42.refs_3_ = bf16[96,1024]{1,0:T(8,128)(2,1)S(1)} collective-permute-done((bf16[96,1024]{1,0:T(8,128)(2,1)S(1)}, bf16[96,1024]{1,0:T(8,128)(2,1)S(1)}, u32[]{:S(2)}, u32[]{:S(2)}) %collective-permute-start.42) | collective-permute-done | bytes 196640 | tf_op jit(solution)/shard_map/ppermute | solution.py:392
  188.8 2.0 collective-permute-start.44
  190.8 3.7 %collective-permute-done.40.refs_2_ = bf16[144,1024]{1,0:T(8,128)(2,1)S(1)} collective-permute-done((bf16[144,1024]{1,0:T(8,128)(2,1)S(1)}, bf16[144,1024]{1,0:T(8,128)(2,1)S(1)}, u32[]{:S(2)}, u32[]{:S(2)}) %collective-permute-start.40) | collective-permute-done | bytes 294944 | tf_op jit(solution)/shard_map/ppermute | solution.py:392
  195.1 2.3 collective-permute-start.43
  198.1 1.9 collective-permute-done.44.refs_2_
  200.6 2.4 collective-permute-start.48
  203.6 8.2 %collective-permute-done.43.refs_3_ = bf16[80,1024]{1,0:T(8,128)(2,1)S(1)} collective-permute-done((bf16[80,1024]{1,0:T(8,128)(2,1)S(1)}, bf16[80,1024]{1,0:T(8,128)(2,1)S(1)}, u32[]{:S(2)}, u32[]{:S(2)}) %collective-permute-start.43) | collective-permute-done | bytes 163872 | tf_op jit(solution)/shard_map/ppermute | solution.py:392
  212.6 2.0 collective-permute-done.48.refs_3_
  217.0 3.3 %collective-permute-done.49.refs_3_ = bf16[64,1024]{1,0:T(8,128)(2,1)S(1)} collective-permute-done((bf16[64,1024]{1,0:T(8,128)(2,1)S(1)}, bf16[64,1024]{1,0:T(8,128)(2,1)S(1)}, u32[]{:S(2)}, u32[]{:S(2)}) %collective-permute-start.49) | collective-permute-done | bytes 131104 | tf_op jit(solution)/shard_map/ppermute | solution.py:392
  221.0 8.5 %collective-permute-start.47 = (bf16[96,1024]{1,0:T(8,128)(2,1)S(1)}, bf16[96,1024]{1,0:T(8,128)(2,1)S(1)}, u32[]{:S(2)}, u32[]{:S(2)}) collective-permute-start(bf16[96,1024]{1,0:T(8,128)(2,1)S(1)} %sum_last.5), channel_id=1, source_target_pairs={{0,8},{4,12},{8,0},{12,4},{16,24},{20,28},{24,16},{28,20},{1,9},{5... | collective-permute-start | bytes 589832 | tf_op jit(solution)/shard_map/ppermute | solution.py:392
  230.8 1.8 collective-permute-done.52
  232.9 6.9 %collective-permute-done.47 = bf16[96,1024]{1,0:T(8,128)(2,1)S(1)} collective-permute-done((bf16[96,1024]{1,0:T(8,128)(2,1)S(1)}, bf16[96,1024]{1,0:T(8,128)(2,1)S(1)}, u32[]{:S(2)}, u32[]{:S(2)}) %collective-permute-start.47) | collective-permute-done | bytes 196640 | tf_op jit(solution)/shard_map/ppermute | solution.py:392
  239.9 1.6 collective-permute-start.64
  242.1 4.5 %collective-permute-done.50 = bf16[128,1024]{1,0:T(8,128)(2,1)S(1)} collective-permute-done((bf16[128,1024]{1,0:T(8,128)(2,1)S(1)}, bf16[128,1024]{1,0:T(8,128)(2,1)S(1)}, u32[]{:S(2)}, u32[]{:S(2)}) %collective-permute-start.50) | collective-permute-done | bytes 262176 | tf_op jit(solution)/shard_map/ppermute | solution.py:392
  246.9 3.5 %collective-permute-done.58 = bf16[128,1024]{1,0:T(8,128)(2,1)S(1)} collective-permute-done((bf16[128,1024]{1,0:T(8,128)(2,1)S(1)}, bf16[128,1024]{1,0:T(8,128)(2,1)S(1)}, u32[]{:S(2)}, u32[]{:S(2)}) %collective-permute-start.58) | collective-permute-done | bytes 262176 | tf_op jit(solution)/shard_map/ppermute | solution.py:392
  253.1 2.3 collective-permute-start.56
  256.4 5.7 %collective-permute-done.53.refs_5_ = bf16[256,1024]{1,0:T(8,128)(2,1)S(1)} collective-permute-done((bf16[256,1024]{1,0:T(8,128)(2,1)S(1)}, bf16[256,1024]{1,0:T(8,128)(2,1)S(1)}, u32[]{:S(2)}, u32[]{:S(2)}) %collective-permute-start.53) | collective-permute-done | bytes 524320 | tf_op jit(solution)/shard_map/ppermute | solution.py:392
  262.5 1.8 collective-permute-done.62.refs_7_
  264.3 9.0 %collective-permute-done.59.refs_6_ = bf16[256,1024]{1,0:T(8,128)(2,1)S(1)} collective-permute-done((bf16[256,1024]{1,0:T(8,128)(2,1)S(1)}, bf16[256,1024]{1,0:T(8,128)(2,1)S(1)}, u32[]{:S(2)}, u32[]{:S(2)}) %collective-permute-start.59) | collective-permute-done | bytes 524320 | tf_op jit(solution)/shard_map/ppermute | solution.py:392
  274.9 1.6 collective-permute-start.63
  276.5 10.9 %collective-permute-done.57.refs_7_ = bf16[256,1024]{1,0:T(8,128)(2,1)S(1)} collective-permute-done((bf16[256,1024]{1,0:T(8,128)(2,1)S(1)}, bf16[256,1024]{1,0:T(8,128)(2,1)S(1)}, u32[]{:S(2)}, u32[]{:S(2)}) %collective-permute-start.57) | collective-permute-done | bytes 524320 | tf_op jit(solution)/shard_map/ppermute | solution.py:298
  287.5 3.0 %mix_pair.3.refs_0_ = f32[768,1024]{1,0:T(8,128)S(1)} custom-call(s32[2]{0:T(128)S(1)} %get-tuple-element.522.where_ref, bf16[768,256]{1,0:T(8,128)(2,1)S(1)} %copy-done.16, bf16[768,256]{1,0:T(8,128)(2,1)S(1)} %copy-done.18, bf16[768,256]{1,0:T(8,128)(2,1)S(1)} %copy-done.20, bf16[784,256]{1,0:T(8,128)(2,1)} %collective-permute-done.34.refs_7_.refs_3_, ...), custom_call_target="tpu_custom_call" | custom-call | flops 1024 | bytes 5242880 | tf_op jit(solution)/shard_map/mix_pair/pallas_call | solution.py:96
  290.6 3.5 %mix_pair.4.refs_0_ = f32[768,1024]{1,0:T(8,128)S(1)} custom-call(s32[2]{0:T(128)S(1)} %get-tuple-element.523.where_ref, f32[768,1024]{1,0:T(8,128)S(1)} %mix_pair.3.refs_0_, bf16[768,256]{1,0:T(8,128)(2,1)S(1)} %copy-done.4, bf16[768,256]{1,0:T(8,128)(2,1)S(1)} %copy-done.9, bf16[768,256]{1,0:T(8,128)(2,1)S(1)} %copy-done.14, ...), custom_call_target="tpu_custom_call", output_to_operand_aliasing={{}: (1, {})} | custom-call | flops 1024 | bytes 5242880 | tf_op jit(solution)/shard_map/mix_pair/pallas_call | solution.py:96
  294.1 2.7 mix_pair.5.refs_1_
  296.7 3.8 %mix_own.1 = bf16[768,1024]{1,0:T(8,128)(2,1)} custom-call(s32[2]{0:T(128)S(1)} %copy-done.22, f32[8,128]{1,0:T(8,128)S(1)} %get-tuple-element.464.refs_4_.refs_0_, f32[768,1024]{1,0:T(8,128)S(1)} %mix_pair.5.refs_1_, bf16[768,256]{1,0:T(8,128)(2,1)S(1)} %get-tuple-element.329.refs_0_.refs_2_.refs_8_, ...), custom_call_target="tpu_custom_call" | custom-call | flops 1024 | bytes 5242880 | tf_op jit(solution)/shard_map/mix_own/pallas_call | solution.py:96
  (170 shorter events, 67.7 us)
Async XLA Ops:
  1.5 13.0 %collective-permute-start = (bf16[768,256]{1,0:T(8,128)(2,1)S(1)}, bf16[768,256]{1,0:T(8,128)(2,1)S(1)}, u32[]{:S(2)}, u32[]{:S(2)}) collective-permute-start(bf16[768,256]{1,0:T(8,128)(2,1)S(1)} %get-tuple-element.513.field_ref.refs_0_), channel_id=1, source_target_pairs={{0,4},{4,0},{8,12},{12,8},{16,20},{20,16},{24,28},{28,24},{1,5},{5... | collective-permute-start | bytes 1179656 | tf_op jit(solution)/shard_map/ppermute | solution.py:311
  10.5 12.4 %collective-permute-start.2 = (bf16[768,256]{1,0:T(8,128)(2,1)S(1)}, bf16[768,256]{1,0:T(8,128)(2,1)S(1)}, u32[]{:S(2)}, u32[]{:S(2)}) collective-permute-start(bf16[768,256]{1,0:T(8,128)(2,1)S(1)} %get-tuple-element.265.field_ref.refs_0_), channel_id=1, source_target_pairs={{0,4},{4,0},{8,12},{12,8},{16,20},{20,16},{24,28},{28,24},{1,5},{5... | collective-permute-start | bytes 1179656 | tf_op jit(solution)/shard_map/ppermute | solution.py:316
  14.5 14.1 %collective-permute-start.1 = (bf16[768,256]{1,0:T(8,128)(2,1)S(1)}, bf16[768,256]{1,0:T(8,128)(2,1)S(1)}, u32[]{:S(2)}, u32[]{:S(2)}) collective-permute-start(bf16[768,256]{1,0:T(8,128)(2,1)S(1)} %collective-permute-done.near_ref), channel_id=1, source_target_pairs={{0,8},{4,28},{8,16},{12,4},{16,24},{20,12},{24,0},{28,20},{1,9},{5... | collective-permute-start | bytes 1179656 | tf_op jit(solution)/shard_map/ppermute | solution.py:325
  16.5 14.8 %collective-permute-start.4 = (bf16[768,256]{1,0:T(8,128)(2,1)S(1)}, bf16[768,256]{1,0:T(8,128)(2,1)S(1)}, u32[]{:S(2)}, u32[]{:S(2)}) collective-permute-start(bf16[768,256]{1,0:T(8,128)(2,1)S(1)} %get-tuple-element.273.field_ref.refs_0_), channel_id=1, source_target_pairs={{0,4},{4,0},{8,12},{12,8},{16,20},{20,16},{24,28},{28,24},{1,5},{5... | collective-permute-start | bytes 1179656 | tf_op jit(solution)/shard_map/ppermute | solution.py:316
  22.9 14.1 %collective-permute-start.7 = (bf16[768,256]{1,0:T(8,128)(2,1)S(1)}, bf16[768,256]{1,0:T(8,128)(2,1)S(1)}, u32[]{:S(2)}, u32[]{:S(2)}) collective-permute-start(bf16[768,256]{1,0:T(8,128)(2,1)S(1)} %collective-permute-done.2.near_ref), channel_id=1, source_target_pairs={{0,8},{4,28},{8,16},{12,4},{16,24},{20,12},{24,0},{28,20},{1,9},{5... | collective-permute-start | bytes 1179656 | tf_op jit(solution)/shard_map/ppermute | solution.py:325
  24.9 14.8 %collective-permute-start.6 = (bf16[768,256]{1,0:T(8,128)(2,1)S(1)}, bf16[768,256]{1,0:T(8,128)(2,1)S(1)}, u32[]{:S(2)}, u32[]{:S(2)}) collective-permute-start(bf16[768,256]{1,0:T(8,128)(2,1)S(1)} %get-tuple-element.276.field_ref.refs_0_), channel_id=1, source_target_pairs={{0,4},{4,0},{8,12},{12,8},{16,20},{20,16},{24,28},{28,24},{1,5},{5... | collective-permute-start | bytes 1179656 | tf_op jit(solution)/shard_map/ppermute | solution.py:316
  31.3 14.1 %collective-permute-start.5 = (bf16[768,256]{1,0:T(8,128)(2,1)S(1)}, bf16[768,256]{1,0:T(8,128)(2,1)S(1)}, u32[]{:S(2)}, u32[]{:S(2)}) collective-permute-start(bf16[768,256]{1,0:T(8,128)(2,1)S(1)} %collective-permute-done.4.near_ref), channel_id=1, source_target_pairs={{0,8},{4,28},{8,16},{12,4},{16,24},{20,12},{24,0},{28,20},{1,9},{5... | collective-permute-start | bytes 1179656 | tf_op jit(solution)/shard_map/ppermute | solution.py:325
  33.4 14.8 %collective-permute-start.3 = (bf16[768,256]{1,0:T(8,128)(2,1)S(1)}, bf16[768,256]{1,0:T(8,128)(2,1)S(1)}, u32[]{:S(2)}, u32[]{:S(2)}) collective-permute-start(bf16[768,256]{1,0:T(8,128)(2,1)S(1)} %get-tuple-element.272.field_ref), channel_id=1, source_target_pairs={{0,4},{4,0},{8,12},{12,8},{16,20},{20,16},{24,28},{28,24},{1,5},{5... | collective-permute-start | bytes 1179656 | tf_op jit(solution)/shard_map/ppermute | solution.py:365
  39.7 14.1 %collective-permute-start.10 = (bf16[768,256]{1,0:T(8,128)(2,1)S(1)}, bf16[768,256]{1,0:T(8,128)(2,1)S(1)}, u32[]{:S(2)}, u32[]{:S(2)}) collective-permute-start(bf16[768,256]{1,0:T(8,128)(2,1)S(1)} %collective-permute-done.6.near_ref), channel_id=1, source_target_pairs={{0,8},{4,28},{8,16},{12,4},{16,24},{20,12},{24,0},{28,20},{1,9},{5... | collective-permute-start | bytes 1179656 | tf_op jit(solution)/shard_map/ppermute | solution.py:325
  41.8 14.8 %collective-permute-start.9 = (bf16[768,256]{1,0:T(8,128)(2,1)S(1)}, bf16[768,256]{1,0:T(8,128)(2,1)S(1)}, u32[]{:S(2)}, u32[]{:S(2)}) collective-permute-start(bf16[768,256]{1,0:T(8,128)(2,1)S(1)} %get-tuple-element.291.field_ref), channel_id=1, source_target_pairs={{0,4},{4,0},{8,12},{12,8},{16,20},{20,16},{24,28},{28,24},{1,5},{5... | collective-permute-start | bytes 1179656 | tf_op jit(solution)/shard_map/ppermute | solution.py:365
  48.2 14.1 %collective-permute-start.8 = (bf16[768,256]{1,0:T(8,128)(2,1)S(1)}, bf16[768,256]{1,0:T(8,128)(2,1)S(1)}, u32[]{:S(2)}, u32[]{:S(2)}) collective-permute-start(bf16[768,256]{1,0:T(8,128)(2,1)S(1)} %collective-permute-done.3.near_ref), channel_id=1, source_target_pairs={{0,8},{4,28},{8,16},{12,4},{16,24},{20,12},{24,0},{28,20},{1,9},{5... | collective-permute-start | bytes 1179656 | tf_op jit(solution)/shard_map/ppermute | solution.py:325
  50.2 14.8 %collective-permute-start.12 = (bf16[768,256]{1,0:T(8,128)(2,1)S(1)}, bf16[768,256]{1,0:T(8,128)(2,1)S(1)}, u32[]{:S(2)}, u32[]{:S(2)}) collective-permute-start(bf16[768,256]{1,0:T(8,128)(2,1)S(1)} %get-tuple-element.303.field_ref), channel_id=1, source_target_pairs={{0,4},{4,0},{8,12},{12,8},{16,20},{20,16},{24,28},{28,24},{1,5},{5... | collective-permute-start | bytes 1179656 | tf_op jit(solution)/shard_map/ppermute | solution.py:365
  56.6 14.1 %collective-permute-start.15 = (bf16[768,256]{1,0:T(8,128)(2,1)S(1)}, bf16[768,256]{1,0:T(8,128)(2,1)S(1)}, u32[]{:S(2)}, u32[]{:S(2)}) collective-permute-start(bf16[768,256]{1,0:T(8,128)(2,1)S(1)} %collective-permute-done.9.near_ref), channel_id=1, source_target_pairs={{0,8},{4,28},{8,16},{12,4},{16,24},{20,12},{24,0},{28,20},{1,9},{5... | collective-permute-start | bytes 1179656 | tf_op jit(solution)/shard_map/ppermute | solution.py:325
  58.6 14.8 %collective-permute-start.14 = (bf16[768,256]{1,0:T(8,128)(2,1)S(1)}, bf16[768,256]{1,0:T(8,128)(2,1)S(1)}, u32[]{:S(2)}, u32[]{:S(2)}) collective-permute-start(bf16[768,256]{1,0:T(8,128)(2,1)S(1)} %get-tuple-element.306.field_ref), channel_id=1, source_target_pairs={{0,4},{4,0},{8,12},{12,8},{16,20},{20,16},{24,28},{28,24},{1,5},{5... | collective-permute-start | bytes 1179656 | tf_op jit(solution)/shard_map/ppermute | solution.py:365
  65.0 14.1 %collective-permute-start.13 = (bf16[768,256]{1,0:T(8,128)(2,1)S(1)}, bf16[768,256]{1,0:T(8,128)(2,1)S(1)}, u32[]{:S(2)}, u32[]{:S(2)}) collective-permute-start(bf16[768,256]{1,0:T(8,128)(2,1)S(1)} %collective-permute-done.12.near_ref), channel_id=1, source_target_pairs={{0,8},{4,28},{8,16},{12,4},{16,24},{20,12},{24,0},{28,20},{1,9},{5... | collective-permute-start | bytes 1179656 | tf_op jit(solution)/shard_map/ppermute | solution.py:325
  67.1 14.8 %collective-permute-start.11 = (bf16[768,256]{1,0:T(8,128)(2,1)S(1)}, bf16[768,256]{1,0:T(8,128)(2,1)S(1)}, u32[]{:S(2)}, u32[]{:S(2)}) collective-permute-start(bf16[768,256]{1,0:T(8,128)(2,1)S(1)} %product_1.4.field_ref), channel_id=1, source_target_pairs={{0,4},{4,0},{8,12},{12,8},{16,20},{20,16},{24,28},{28,24},{1,5},{5... | collective-permute-start | bytes 1179656 | tf_op jit(solution)/shard_map/ppermute | solution.py:365
  73.5 14.1 %collective-permute-start.18 = (bf16[768,256]{1,0:T(8,128)(2,1)S(1)}, bf16[768,256]{1,0:T(8,128)(2,1)S(1)}, u32[]{:S(2)}, u32[]{:S(2)}) collective-permute-start(bf16[768,256]{1,0:T(8,128)(2,1)S(1)} %collective-permute-done.14.near_ref), channel_id=1, source_target_pairs={{0,8},{4,28},{8,16},{12,4},{16,24},{20,12},{24,0},{28,20},{1,9},{5... | collective-permute-start | bytes 1179656 | tf_op jit(solution)/shard_map/ppermute | solution.py:325
  75.5 14.8 %collective-permute-start.17 = (bf16[768,256]{1,0:T(8,128)(2,1)S(1)}, bf16[768,256]{1,0:T(8,128)(2,1)S(1)}, u32[]{:S(2)}, u32[]{:S(2)}) collective-permute-start(bf16[768,256]{1,0:T(8,128)(2,1)S(1)} %product_1.5.field_ref), channel_id=1, source_target_pairs={{0,4},{4,0},{8,12},{12,8},{16,20},{20,16},{24,28},{28,24},{1,5},{5... | collective-permute-start | bytes 1179656 | tf_op jit(solution)/shard_map/ppermute | solution.py:365
  81.9 14.1 %collective-permute-start.16 = (bf16[768,256]{1,0:T(8,128)(2,1)S(1)}, bf16[768,256]{1,0:T(8,128)(2,1)S(1)}, u32[]{:S(2)}, u32[]{:S(2)}) collective-permute-start(bf16[768,256]{1,0:T(8,128)(2,1)S(1)} %collective-permute-done.11.near_ref), channel_id=1, source_target_pairs={{0,8},{4,28},{8,16},{12,4},{16,24},{20,12},{24,0},{28,20},{1,9},{5... | collective-permute-start | bytes 1179656 | tf_op jit(solution)/shard_map/ppermute | solution.py:325
  83.9 14.8 %collective-permute-start.20 = (bf16[768,256]{1,0:T(8,128)(2,1)S(1)}, bf16[768,256]{1,0:T(8,128)(2,1)S(1)}, u32[]{:S(2)}, u32[]{:S(2)}) collective-permute-start(bf16[768,256]{1,0:T(8,128)(2,1)S(1)} %product_1.6.field_ref), channel_id=1, source_target_pairs={{0,4},{4,0},{8,12},{12,8},{16,20},{20,16},{24,28},{28,24},{1,5},{5... | collective-permute-start | bytes 1179656 | tf_op jit(solution)/shard_map/ppermute | solution.py:365
  90.3 12.0 %collective-permute-start.19 = (bf16[768,256]{1,0:T(8,128)(2,1)S(1)}, bf16[768,256]{1,0:T(8,128)(2,1)S(1)}, u32[]{:S(2)}, u32[]{:S(2)}) collective-permute-start(bf16[768,256]{1,0:T(8,128)(2,1)S(1)} %collective-permute-done.17.near_ref), channel_id=1, source_target_pairs={{0,8},{4,28},{8,16},{12,4},{16,24},{20,12},{24,0},{28,20},{1,9},{5... | collective-permute-start | bytes 1179656 | tf_op jit(solution)/shard_map/ppermute | solution.py:325
  92.4 14.0 %collective-permute-start.22 = (bf16[768,256]{1,0:T(8,128)(2,1)S(1)}, bf16[768,256]{1,0:T(8,128)(2,1)S(1)}, u32[]{:S(2)}, u32[]{:S(2)}) collective-permute-start(bf16[768,256]{1,0:T(8,128)(2,1)S(1)} %product_1.7.field_ref), channel_id=1, source_target_pairs={{0,4},{4,0},{8,12},{12,8},{16,20},{20,16},{24,28},{28,24},{1,5},{5... | collective-permute-start | bytes 1179656 | tf_op jit(solution)/shard_map/ppermute | solution.py:365
  98.7 11.3 %collective-permute-start.21 = (bf16[768,256]{1,0:T(8,128)(2,1)S(1)}, bf16[768,256]{1,0:T(8,128)(2,1)S(1)}, u32[]{:S(2)}, u32[]{:S(2)}) collective-permute-start(bf16[768,256]{1,0:T(8,128)(2,1)S(1)} %collective-permute-done.20.near_ref), channel_id=1, source_target_pairs={{0,8},{4,28},{8,16},{12,4},{16,24},{20,12},{24,0},{28,20},{1,9},{5... | collective-permute-start | bytes 1179656 | tf_op jit(solution)/shard_map/ppermute | solution.py:325
  100.8 10.5 %collective-permute-start.25 = (bf16[768,256]{1,0:T(8,128)(2,1)S(1)}, bf16[768,256]{1,0:T(8,128)(2,1)S(1)}, u32[]{:S(2)}, u32[]{:S(2)}) collective-permute-start(bf16[768,256]{1,0:T(8,128)(2,1)S(1)} %get-tuple-element.329.refs_0_.refs_2_.refs_8_), channel_id=1, source_target_pairs={{0,2},{1,3},{2,0},{3,1},{4,6},{5,7},{6,4},{7,5},{8,10},{9,11},{10,... | collective-permute-start | bytes 1179656 | tf_op jit(solution)/shard_map/ppermute | solution.py:298
  102.3 9.6 %collective-permute-start.24 = (bf16[768,256]{1,0:T(8,128)(2,1)S(1)}, bf16[768,256]{1,0:T(8,128)(2,1)S(1)}, u32[]{:S(2)}, u32[]{:S(2)}) collective-permute-start(bf16[768,256]{1,0:T(8,128)(2,1)S(1)} %get-tuple-element.329.refs_0_.refs_2_.refs_8_), channel_id=1, source_target_pairs={{0,1},{1,0},{2,3},{3,2},{4,5},{5,4},{6,7},{7,6},{8,9},{9,8},{10,11... | collective-permute-start | bytes 1179656 | tf_op jit(solution)/shard_map/ppermute | solution.py:298
  106.3 12.1 %collective-permute-start.23 = (bf16[768,256]{1,0:T(8,128)(2,1)S(1)}, bf16[768,256]{1,0:T(8,128)(2,1)S(1)}, u32[]{:S(2)}, u32[]{:S(2)}) collective-permute-start(bf16[768,256]{1,0:T(8,128)(2,1)S(1)} %collective-permute-done.22.near_ref), channel_id=1, source_target_pairs={{0,8},{4,28},{8,16},{12,4},{16,24},{20,12},{24,0},{28,20},{1,9},{5... | collective-permute-start | bytes 1179656 | tf_op jit(solution)/shard_map/ppermute | solution.py:325
  108.1 11.8 %collective-permute-start.28 = (bf16[768,256]{1,0:T(8,128)(2,1)S(1)}, bf16[768,256]{1,0:T(8,128)(2,1)S(1)}, u32[]{:S(2)}, u32[]{:S(2)}) collective-permute-start(bf16[768,256]{1,0:T(8,128)(2,1)S(1)} %get-tuple-element.340.refs_1_.refs_3_.refs_9_), channel_id=1, source_target_pairs={{0,2},{1,3},{2,0},{3,1},{4,6},{5,7},{6,4},{7,5},{8,10},{9,11},{10,... | collective-permute-start | bytes 1179656 | tf_op jit(solution)/shard_map/ppermute | solution.py:298
  110.0 15.1 %collective-permute-start.27 = (bf16[768,256]{1,0:T(8,128)(2,1)S(1)}, bf16[768,256]{1,0:T(8,128)(2,1)S(1)}, u32[]{:S(2)}, u32[]{:S(2)}) collective-permute-start(bf16[768,256]{1,0:T(8,128)(2,1)S(1)} %get-tuple-element.340.refs_1_.refs_3_.refs_9_), channel_id=1, source_target_pairs={{0,1},{1,0},{2,3},{3,2},{4,5},{5,4},{6,7},{7,6},{8,9},{9,8},{10,11... | collective-permute-start | bytes 1179656 | tf_op jit(solution)/shard_map/ppermute | solution.py:298
  111.3 14.6 %collective-permute-start.26 = (bf16[768,256]{1,0:T(8,128)(2,1)S(1)}, bf16[768,256]{1,0:T(8,128)(2,1)S(1)}, u32[]{:S(2)}, u32[]{:S(2)}) collective-permute-start(bf16[768,256]{1,0:T(8,128)(2,1)S(1)} %collective-permute-done.25.refs_4_.refs_1_), channel_id=1, source_target_pairs={{0,1},{1,0},{2,3},{3,2},{4,5},{5,4},{6,7},{7,6},{8,9},{9,8},{10,11... | collective-permute-start | bytes 1179656 | tf_op jit(solution)/shard_map/ppermute | solution.py:298
  119.9 6.7 %collective-permute-start.29 = (bf16[768,256]{1,0:T(8,128)(2,1)S(1)}, bf16[768,256]{1,0:T(8,128)(2,1)S(1)}, u32[]{:S(2)}, u32[]{:S(2)}) collective-permute-start(bf16[768,256]{1,0:T(8,128)(2,1)S(1)} %collective-permute-done.28.refs_5_.refs_2_), channel_id=1, source_target_pairs={{0,1},{1,0},{2,3},{3,2},{4,5},{5,4},{6,7},{7,6},{8,9},{9,8},{10,11... | collective-permute-start | bytes 1179656 | tf_op jit(solution)/shard_map/ppermute | solution.py:298
  120.0 12.0 %collective-permute-start.30 = (bf16[768,256]{1,0:T(8,128)(2,1)S(1)}, bf16[768,256]{1,0:T(8,128)(2,1)S(1)}, u32[]{:S(2)}, u32[]{:S(2)}) collective-permute-start(bf16[768,256]{1,0:T(8,128)(2,1)S(1)} %get-tuple-element.351.refs_2_.refs_4_.refs_10_), channel_id=1, source_target_pairs={{0,2},{1,3},{2,0},{3,1},{4,6},{5,7},{6,4},{7,5},{8,10},{9,11},{10,... | collective-permute-start | bytes 1179656 | tf_op jit(solution)/shard_map/ppermute | solution.py:298
  121.5 18.6 %collective-permute-start.33 = (bf16[784,256]{1,0:T(8,128)(2,1)S(1)}, bf16[784,256]{1,0:T(8,128)(2,1)S(1)}, u32[]{:S(2)}, u32[]{:S(2)}) collective-permute-start(bf16[784,256]{1,0:T(8,128)(2,1)S(1)} %product_2.7.refs_3_.refs_5_.refs_11_), channel_id=1, source_target_pairs={{0,2},{1,3},{2,0},{3,1},{4,6},{5,7},{6,4},{7,5},{8,10},{9,11},{10,... | collective-permute-start | bytes 1204232 | tf_op jit(solution)/shard_map/ppermute | solution.py:298
  125.9 8.4 %collective-permute-start.32 = (bf16[768,256]{1,0:T(8,128)(2,1)S(1)}, bf16[768,256]{1,0:T(8,128)(2,1)S(1)}, u32[]{:S(2)}, u32[]{:S(2)}) collective-permute-start(bf16[768,256]{1,0:T(8,128)(2,1)S(1)} %get-tuple-element.351.refs_2_.refs_4_.refs_10_), channel_id=1, source_target_pairs={{0,1},{1,0},{2,3},{3,2},{4,5},{5,4},{6,7},{7,6},{8,9},{9,8},{10,11... | collective-permute-start | bytes 1179656 | tf_op jit(solution)/shard_map/ppermute | solution.py:298
  132.7 20.2 %collective-permute-start.35 = (bf16[384,1024]{1,0:T(8,128)(2,1)}, bf16[384,1024]{1,0:T(8,128)(2,1)S(1)}, u32[]{:S(2)}, u32[]{:S(2)}) collective-permute-start(bf16[384,1024]{1,0:T(8,128)(2,1)} %get-tuple-element.388), channel_id=1, source_target_pairs={{0,4},{4,0},{8,12},{12,8},{16,20},{20,16},{24,28},{28,24},{1,5},{5... | collective-permute-start | bytes 2359304 | tf_op jit(solution)/shard_map/ppermute | solution.py:392
  140.1 13.5 %collective-permute-start.34 = (bf16[784,256]{1,0:T(8,128)(2,1)S(1)}, bf16[784,256]{1,0:T(8,128)(2,1)}, u32[]{:S(2)}, u32[]{:S(2)}) collective-permute-start(bf16[784,256]{1,0:T(8,128)(2,1)S(1)} %collective-permute-done.33.refs_7_.refs_9_.refs_4_), channel_id=1, source_target_pairs={{0,1},{1,0},{2,3},{3,2},{4,5},{5,4},{6,7},{7,6},{8,9},{9,8},{10,11... | collective-permute-start | bytes 1204232 | tf_op jit(solution)/shard_map/ppermute | solution.py:298
  155.9 26.3 %collective-permute-start.37 = (bf16[272,1024]{1,0:T(8,128)(2,1)S(1)}, bf16[272,1024]{1,0:T(8,128)(2,1)S(1)}, u32[]{:S(2)}, u32[]{:S(2)}) collective-permute-start(bf16[272,1024]{1,0:T(8,128)(2,1)S(1)} %get-tuple-element.415), channel_id=1, source_target_pairs={{0,4},{4,0},{8,12},{12,8},{16,20},{20,16},{24,28},{28,24},{1,5},{5... | collective-permute-start | bytes 1671176 | tf_op jit(solution)/shard_map/ppermute | solution.py:392
  157.3 21.7 %collective-permute-start.39 = (bf16[256,1024]{1,0:T(8,128)(2,1)S(1)}, bf16[256,1024]{1,0:T(8,128)(2,1)S(1)}, u32[]{:S(2)}, u32[]{:S(2)}) collective-permute-start(bf16[256,1024]{1,0:T(8,128)(2,1)S(1)} %get-tuple-element.418), channel_id=1, source_target_pairs={{0,8},{4,12},{8,0},{12,4},{16,24},{20,28},{24,16},{28,20},{1,9},{5... | collective-permute-start | bytes 1572872 | tf_op jit(solution)/shard_map/ppermute | solution.py:392
  157.3 22.3 %collective-permute-start.38 = (bf16[192,1024]{1,0:T(8,128)(2,1)S(1)}, bf16[192,1024]{1,0:T(8,128)(2,1)S(1)}, u32[]{:S(2)}, u32[]{:S(2)}) collective-permute-start(bf16[192,1024]{1,0:T(8,128)(2,1)S(1)} %sum_hop.8), channel_id=1, source_target_pairs={{0,16},{4,20},{8,24},{12,28},{16,0},{20,4},{24,8},{28,12},{1,17},{... | collective-permute-start | bytes 1179656 | tf_op jit(solution)/shard_map/ppermute | solution.py:392
  163.7 24.5 %collective-permute-start.41 = (bf16[256,1024]{1,0:T(8,128)(2,1)S(1)}, bf16[256,1024]{1,0:T(8,128)(2,1)S(1)}, u32[]{:S(2)}, u32[]{:S(2)}) collective-permute-start(bf16[256,1024]{1,0:T(8,128)(2,1)S(1)} %get-tuple-element.441), channel_id=1, source_target_pairs={{0,4},{4,0},{8,12},{12,8},{16,20},{20,16},{24,28},{28,24},{1,5},{5... | collective-permute-start | bytes 1572872 | tf_op jit(solution)/shard_map/ppermute | solution.py:392
  180.3 7.9 %collective-permute-start.42 = (bf16[96,1024]{1,0:T(8,128)(2,1)S(1)}, bf16[96,1024]{1,0:T(8,128)(2,1)S(1)}, u32[]{:S(2)}, u32[]{:S(2)}) collective-permute-start(bf16[96,1024]{1,0:T(8,128)(2,1)S(1)} %sum_hop.10), channel_id=1, source_target_pairs={{0,8},{4,12},{8,0},{12,4},{16,24},{20,28},{24,16},{28,20},{1,9},{5... | collective-permute-start | bytes 589832 | tf_op jit(solution)/shard_map/ppermute | solution.py:392
  182.9 11.6 %collective-permute-start.40 = (bf16[144,1024]{1,0:T(8,128)(2,1)S(1)}, bf16[144,1024]{1,0:T(8,128)(2,1)S(1)}, u32[]{:S(2)}, u32[]{:S(2)}) collective-permute-start(bf16[144,1024]{1,0:T(8,128)(2,1)S(1)} %sum_hop.11), channel_id=1, source_target_pairs={{0,8},{4,12},{8,0},{12,4},{16,24},{20,28},{24,16},{28,20},{1,9},{5... | collective-permute-start | bytes 884744 | tf_op jit(solution)/shard_map/ppermute | solution.py:392
  183.1 14.4 %collective-permute-start.45 = (bf16[128,1024]{1,0:T(8,128)(2,1)S(1)}, bf16[128,1024]{1,0:T(8,128)(2,1)S(1)}, u32[]{:S(2)}, u32[]{:S(2)}) collective-permute-start(bf16[128,1024]{1,0:T(8,128)(2,1)S(1)} %sum_hop.9), channel_id=1, source_target_pairs={{0,4},{4,0},{8,12},{12,8},{16,20},{20,16},{24,28},{28,24},{1,5},{5... | collective-permute-start | bytes 786440 | tf_op jit(solution)/shard_map/ppermute | solution.py:392
  188.8 11.2 %collective-permute-start.44 = (bf16[128,1024]{1,0:T(8,128)(2,1)S(1)}, bf16[128,1024]{1,0:T(8,128)(2,1)S(1)}, u32[]{:S(2)}, u32[]{:S(2)}) collective-permute-start(bf16[128,1024]{1,0:T(8,128)(2,1)S(1)} %sum_hop.12), channel_id=1, source_target_pairs={{0,8},{4,12},{8,0},{12,4},{16,24},{20,28},{24,16},{28,20},{1,9},{5... | collective-permute-start | bytes 786440 | tf_op jit(solution)/shard_map/ppermute | solution.py:392
  195.1 16.7 %collective-permute-start.43 = (bf16[80,1024]{1,0:T(8,128)(2,1)S(1)}, bf16[80,1024]{1,0:T(8,128)(2,1)S(1)}, u32[]{:S(2)}, u32[]{:S(2)}) collective-permute-start(bf16[80,1024]{1,0:T(8,128)(2,1)S(1)} %sum_hop.13), channel_id=1, source_target_pairs={{0,16},{4,20},{8,24},{12,28},{16,0},{20,4},{24,8},{28,12},{1,17},{... | collective-permute-start | bytes 491528 | tf_op jit(solution)/shard_map/ppermute | solution.py:392
  200.6 14.0 %collective-permute-start.48 = (bf16[64,1024]{1,0:T(8,128)(2,1)S(1)}, bf16[64,1024]{1,0:T(8,128)(2,1)S(1)}, u32[]{:S(2)}, u32[]{:S(2)}) collective-permute-start(bf16[64,1024]{1,0:T(8,128)(2,1)S(1)} %sum_hop.15), channel_id=1, source_target_pairs={{0,16},{4,20},{8,24},{12,28},{16,0},{20,4},{24,8},{28,12},{1,17},{... | collective-permute-start | bytes 393224 | tf_op jit(solution)/shard_map/ppermute | solution.py:392
  203.0 17.2 %collective-permute-start.49 = (bf16[64,1024]{1,0:T(8,128)(2,1)S(1)}, bf16[64,1024]{1,0:T(8,128)(2,1)S(1)}, u32[]{:S(2)}, u32[]{:S(2)}) collective-permute-start(bf16[64,1024]{1,0:T(8,128)(2,1)S(1)} %sum_hop.14), channel_id=1, source_target_pairs={{0,16},{4,20},{8,24},{12,28},{16,0},{20,4},{24,8},{28,12},{1,17},{... | collective-permute-start | bytes 393224 | tf_op jit(solution)/shard_map/ppermute | solution.py:392
  212.5 17.0 %collective-permute-start.46 = (bf16[64,1024]{1,0:T(8,128)(2,1)S(1)}, bf16[64,1024]{1,0:T(8,128)(2,1)S(1)}, u32[]{:S(2)}, u32[]{:S(2)}) collective-permute-start(bf16[64,1024]{1,0:T(8,128)(2,1)S(1)} %get-tuple-element.465), channel_id=1, source_target_pairs={{0,16},{4,20},{8,24},{12,28},{16,0},{20,4},{24,8},{28,12},{1,17},{... | collective-permute-start | bytes 393224 | tf_op jit(solution)/shard_map/ppermute | solution.py:392
  215.3 14.2 %collective-permute-start.51 = (bf16[64,1024]{1,0:T(8,128)(2,1)S(1)}, bf16[64,1024]{1,0:T(8,128)(2,1)S(1)}, u32[]{:S(2)}, u32[]{:S(2)}) collective-permute-start(bf16[64,1024]{1,0:T(8,128)(2,1)S(1)} %sum_last.7), channel_id=1, source_target_pairs={{0,16},{4,20},{8,24},{12,28},{16,0},{20,4},{24,8},{28,12},{1,17},{... | collective-permute-start | bytes 393224 | tf_op jit(solution)/shard_map/ppermute | solution.py:392
  220.9 11.6 %collective-permute-start.52 = (bf16[64,1024]{1,0:T(8,128)(2,1)S(1)}, bf16[64,1024]{1,0:T(8,128)(2,1)S(1)}, u32[]{:S(2)}, u32[]{:S(2)}) collective-permute-start(bf16[64,1024]{1,0:T(8,128)(2,1)S(1)} %sum_last.6), channel_id=1, source_target_pairs={{0,16},{4,20},{8,24},{12,28},{16,0},{20,4},{24,8},{28,12},{1,17},{... | collective-permute-start | bytes 393224 | tf_op jit(solution)/shard_map/ppermute | solution.py:392
  221.0 18.8 %collective-permute-start.47 = (bf16[96,1024]{1,0:T(8,128)(2,1)S(1)}, bf16[96,1024]{1,0:T(8,128)(2,1)S(1)}, u32[]{:S(2)}, u32[]{:S(2)}) collective-permute-start(bf16[96,1024]{1,0:T(8,128)(2,1)S(1)} %sum_last.5), channel_id=1, source_target_pairs={{0,8},{4,12},{8,0},{12,4},{16,24},{20,28},{24,16},{28,20},{1,9},{5... | collective-permute-start | bytes 589832 | tf_op jit(solution)/shard_map/ppermute | solution.py:392
  229.5 17.0 %collective-permute-start.50 = (bf16[128,1024]{1,0:T(8,128)(2,1)S(1)}, bf16[128,1024]{1,0:T(8,128)(2,1)S(1)}, u32[]{:S(2)}, u32[]{:S(2)}) collective-permute-start(bf16[128,1024]{1,0:T(8,128)(2,1)S(1)} %pad_maximum_fusion.5), channel_id=1, source_target_pairs={{0,8},{4,12},{8,0},{12,4},{16,24},{20,28},{24,16},{28,20},{1,9},{5... | collective-permute-start | bytes 786440 | tf_op jit(solution)/shard_map/ppermute | solution.py:392
  232.5 17.8 %collective-permute-start.58 = (bf16[128,1024]{1,0:T(8,128)(2,1)S(1)}, bf16[128,1024]{1,0:T(8,128)(2,1)S(1)}, u32[]{:S(2)}, u32[]{:S(2)}) collective-permute-start(bf16[128,1024]{1,0:T(8,128)(2,1)S(1)} %pad_maximum_fusion.6), channel_id=1, source_target_pairs={{0,8},{4,12},{8,0},{12,4},{16,24},{20,28},{24,16},{28,20},{1,9},{5... | collective-permute-start | bytes 786440 | tf_op jit(solution)/shard_map/ppermute | solution.py:392
  239.9 16.4 %collective-permute-start.64 = (bf16[192,1024]{1,0:T(8,128)(2,1)S(1)}, bf16[192,1024]{1,0:T(8,128)(2,1)S(1)}, u32[]{:S(2)}, u32[]{:S(2)}) collective-permute-start(bf16[192,1024]{1,0:T(8,128)(2,1)S(1)} %pad_maximum_fusion.4), channel_id=1, source_target_pairs={{0,16},{4,20},{8,24},{12,28},{16,0},{20,4},{24,8},{28,12},{1,17},{... | collective-permute-start | bytes 1179656 | tf_op jit(solution)/shard_map/ppermute | solution.py:392
  241.5 9.3 %collective-permute-start.55 = (bf16[128,1024]{1,0:T(8,128)(2,1)S(1)}, bf16[128,1024]{1,0:T(8,128)(2,1)S(1)}, u32[]{:S(2)}, u32[]{:S(2)}) collective-permute-start(bf16[128,1024]{1,0:T(8,128)(2,1)S(1)} %pad_maximum_fusion.7), channel_id=1, source_target_pairs={{0,4},{4,0},{8,12},{12,8},{16,20},{20,16},{24,28},{28,24},{1,5},{5... | collective-permute-start | bytes 786440 | tf_op jit(solution)/shard_map/ppermute | solution.py:392
  246.6 15.5 %collective-permute-start.53 = (bf16[256,1024]{1,0:T(8,128)(2,1)S(1)}, bf16[256,1024]{1,0:T(8,128)(2,1)S(1)}, u32[]{:S(2)}, u32[]{:S(2)}) collective-permute-start(bf16[256,1024]{1,0:T(8,128)(2,1)S(1)} %pad_maximum_fusion.1.refs_4_), channel_id=1, source_target_pairs={{0,4},{4,0},{8,12},{12,8},{16,20},{20,16},{24,28},{28,24},{1,5},{5... | collective-permute-start | bytes 1572872 | tf_op jit(solution)/shard_map/ppermute | solution.py:392
  250.9 13.4 %collective-permute-start.62 = (bf16[256,1024]{1,0:T(8,128)(2,1)S(1)}, bf16[256,1024]{1,0:T(8,128)(2,1)S(1)}, u32[]{:S(2)}, u32[]{:S(2)}) collective-permute-start(bf16[256,1024]{1,0:T(8,128)(2,1)S(1)} %pad_maximum_fusion.3.refs_5_), channel_id=1, source_target_pairs={{0,2},{1,3},{2,0},{3,1},{4,6},{5,7},{6,4},{7,5},{8,10},{9,11},{10,... | collective-permute-start | bytes 1572872 | tf_op jit(solution)/shard_map/ppermute | solution.py:298
  252.4 20.9 %collective-permute-start.59 = (bf16[256,1024]{1,0:T(8,128)(2,1)S(1)}, bf16[256,1024]{1,0:T(8,128)(2,1)S(1)}, u32[]{:S(2)}, u32[]{:S(2)}) collective-permute-start(bf16[256,1024]{1,0:T(8,128)(2,1)S(1)} %pad_maximum_fusion.2.refs_5_), channel_id=1, source_target_pairs={{0,4},{4,0},{8,12},{12,8},{16,20},{20,16},{24,28},{28,24},{1,5},{5... | collective-permute-start | bytes 1572872 | tf_op jit(solution)/shard_map/ppermute | solution.py:392
  253.1 20.2 %collective-permute-start.56 = (bf16[256,1024]{1,0:T(8,128)(2,1)S(1)}, bf16[256,1024]{1,0:T(8,128)(2,1)S(1)}, u32[]{:S(2)}, u32[]{:S(2)}) collective-permute-start(bf16[256,1024]{1,0:T(8,128)(2,1)S(1)} %pad_maximum_fusion.3.refs_5_), channel_id=1, source_target_pairs={{0,8},{4,12},{8,0},{12,4},{16,24},{20,28},{24,16},{28,20},{1,9},{5... | collective-permute-start | bytes 1572872 | tf_op jit(solution)/shard_map/ppermute | solution.py:392
  256.3 18.6 %collective-permute-start.54 = (bf16[256,1024]{1,0:T(8,128)(2,1)S(1)}, bf16[256,1024]{1,0:T(8,128)(2,1)S(1)}, u32[]{:S(2)}, u32[]{:S(2)}) collective-permute-start(bf16[256,1024]{1,0:T(8,128)(2,1)S(1)} %pad_maximum_fusion.1.refs_4_), channel_id=1, source_target_pairs={{0,3},{1,2},{2,1},{3,0},{4,7},{5,6},{6,5},{7,4},{8,11},{9,10},{10,... | collective-permute-start | bytes 1572872 | tf_op jit(solution)/shard_map/ppermute | solution.py:298
  262.1 28.5 %collective-permute-start.65 = (bf16[384,1024]{1,0:T(8,128)(2,1)S(1)}, bf16[384,1024]{1,0:T(8,128)(2,1)S(1)}, u32[]{:S(2)}, u32[]{:S(2)}) collective-permute-start(bf16[384,1024]{1,0:T(8,128)(2,1)S(1)} %pad_maximum_fusion.refs_6_), channel_id=1, source_target_pairs={{0,4},{4,0},{8,12},{12,8},{16,20},{20,16},{24,28},{28,24},{1,5},{5... | collective-permute-start | bytes 2359304 | tf_op jit(solution)/shard_map/ppermute | solution.py:392
  264.3 12.2 %collective-permute-start.60 = (bf16[256,1024]{1,0:T(8,128)(2,1)S(1)}, bf16[256,1024]{1,0:T(8,128)(2,1)S(1)}, u32[]{:S(2)}, u32[]{:S(2)}) collective-permute-start(bf16[256,1024]{1,0:T(8,128)(2,1)S(1)} %pad_maximum_fusion.2.refs_5_), channel_id=1, source_target_pairs={{0,1},{1,0},{2,3},{3,2},{4,5},{5,4},{6,7},{7,6},{8,9},{9,8},{10,11... | collective-permute-start | bytes 1572872 | tf_op jit(solution)/shard_map/ppermute | solution.py:298
  273.3 14.2 %collective-permute-start.57 = (bf16[256,1024]{1,0:T(8,128)(2,1)S(1)}, bf16[256,1024]{1,0:T(8,128)(2,1)S(1)}, u32[]{:S(2)}, u32[]{:S(2)}) collective-permute-start(bf16[256,1024]{1,0:T(8,128)(2,1)S(1)} %collective-permute-done.53.refs_5_), channel_id=1, source_target_pairs={{0,3},{1,2},{2,1},{3,0},{4,7},{5,6},{6,5},{7,4},{8,11},{9,10},{10,... | collective-permute-start | bytes 1572872 | tf_op jit(solution)/shard_map/ppermute | solution.py:298
  273.3 17.2 %collective-permute-start.61 = (bf16[256,1024]{1,0:T(8,128)(2,1)S(1)}, bf16[256,1024]{1,0:T(8,128)(2,1)S(1)}, u32[]{:S(2)}, u32[]{:S(2)}) collective-permute-start(bf16[256,1024]{1,0:T(8,128)(2,1)S(1)} %collective-permute-done.59.refs_6_), channel_id=1, source_target_pairs={{0,1},{1,0},{2,3},{3,2},{4,5},{5,4},{6,7},{7,6},{8,9},{9,8},{10,11... | collective-permute-start | bytes 1572872 | tf_op jit(solution)/shard_map/ppermute | solution.py:298
  274.9 19.1 %collective-permute-start.63 = (bf16[256,1024]{1,0:T(8,128)(2,1)S(1)}, bf16[256,1024]{1,0:T(8,128)(2,1)S(1)}, u32[]{:S(2)}, u32[]{:S(2)}) collective-permute-start(bf16[256,1024]{1,0:T(8,128)(2,1)S(1)} %collective-permute-done.62.refs_7_), channel_id=1, source_target_pairs={{0,8},{4,12},{8,0},{12,4},{16,24},{20,28},{24,16},{28,20},{1,9},{5... | collective-permute-start | bytes 1572872 | tf_op jit(solution)/shard_map/ppermute | solution.py:392
  (26 other events, 137.8 us)

commit v10 on v9

--- a/solution.py
+++ b/solution.py
@@ -145,38 +145,47 @@
     return rows.astype(BF16)
 
 
-def side_by_side(refs, rows):
-    return jnp.concatenate([ref[:rows, :] for ref in refs], axis=1)
-
-
-def gram_kernel(pair, mask, where_ref, *refs):
-    mine_ref, other_ref, whole = refs[-3:]
-    fields = refs[:CHUNKS]
-    rows, width = fields[0].shape
+def gram_kernel(pair, cut, mask, extra, where_ref, *refs):
+    refs = list(refs)
+    whole = refs.pop()
+    field = refs.pop(0) if pair else None
+    chunks = [refs.pop(0) for _ in range(CHUNKS)] if cut else []
+    others = [refs.pop(0) for _ in range(extra)]
+    if cut:
+        joined = refs.pop()
+        rows, width = chunks[0].shape
+        joined[rows:, :] = jnp.zeros((EXTRA, joined.shape[1]), BF16)
+        for c, chunk in enumerate(chunks):
+            joined[: chunk.shape[0], c * width : (c + 1) * width] = chunk[...]
+    else:
+        joined = refs.pop(0)
+        rows, width = joined.shape[0] - EXTRA, joined.shape[1] // CHUNKS
+    field = joined if field is None else field
+    mine_ref, other_ref = refs
     half = whole.shape[0] // 2
     middle = CHUNKS * width // 2
     side = lax.rem(where_ref[0] // mask, 2)
 
-    def fill(left, rights, count):
-        for c, right in enumerate(rights):
-            value = lax.dot_general(left, right[:rows, :], TRANSPOSED_LEFT, preferred_element_type=F32)
-            whole[:count, c * width : (c + 1) * width] = value.astype(BF16)
+    def fill(left, right, count):
+        for c in range(CHUNKS):
+            here = slice(c * width, (c + 1) * width)
+            value = lax.dot_general(left, right[:rows, here], TRANSPOSED_LEFT, preferred_element_type=F32)
+            whole[:count, here] = value.astype(BF16)
 
     if pair:
-        peers = refs[CHUNKS : 2 * CHUNKS]
         used = middle
 
         @pl.when(where_ref[1] == 0)
         def _():
-            fill(side_by_side(peers[: CHUNKS // 2], rows), fields, middle)
+            fill(joined[:rows, :middle], field, middle)
 
         @pl.when(where_ref[1] == 1)
         def _():
-            fill(side_by_side(fields[CHUNKS // 2 :], rows), peers, middle)
+            fill(field[:rows, middle:], joined, middle)
     else:
         used = middle + middle // 2
-        upper = side_by_side(fields[CHUNKS // 2 :], rows)
-        fill(side_by_side(fields[: CHUNKS // 2], rows), fields, middle)
+        upper = field[:rows, middle:]
+        fill(field[:rows, :middle], field, middle)
         corner = lax.dot_general(upper, upper, TRANSPOSED_LEFT, preferred_element_type=F32).astype(BF16)
         whole[middle:used, :middle] = corner[: middle // 2]
         whole[middle:used, middle:] = corner[middle // 2 :]
@@ -185,8 +194,8 @@
     mine_ref[:half, :] = whole[pl.ds(pl.multiple_of(side * half, half), half), :]
     other_ref[:half, :] = whole[pl.ds(pl.multiple_of((1 - side) * half, half), half), :]
     if mine_ref.shape[0] > half:
-        ends = [fields[-1], *refs[2 * CHUNKS - 1 : -3]]
-        total = sum(jnp.sum(end[rows:, :].astype(F32), axis=0, keepdims=True) for end in ends)
+        ends = [field, joined, *others]
+        total = sum(jnp.sum(end[rows:, -width:].astype(F32), axis=0, keepdims=True) for end in ends)
         carried = extra_rows(jnp.concatenate([total] * CHUNKS, axis=1))
         mine_ref[half:, :] = carried
         other_ref[half:, :] = carried
@@ -230,17 +239,16 @@
 def mix_kernel(pair, masks, first, last, where_ref, *refs):
     level_ref, *refs = refs if last else (None, *refs)
     total_ref, *refs = (None, *refs) if first else refs
-    fields, refs = refs[:CHUNKS], refs[CHUNKS:]
+    field, *refs = refs
     out_ref, block = refs[-2:]
-    own = refs[-2 - CHUNKS : -2]
-    rows, width = fields[0].shape
+    own = refs[-3]
+    rows, width = field.shape[0] - EXTRA, field.shape[1] // CHUNKS
     middle = CHUNKS * width // 2
 
     def finish(mixed, here):
         value = mixed if first else total_ref[:, here] + mixed
         if last:
-            filtered = side_by_side(own, rows)[:, here].astype(F32)
-            value = (1.5 * filtered - 0.5 * value) / jnp.sqrt(level_ref[:1, :1])
+            value = (1.5 * own[:rows, here].astype(F32) - 0.5 * value) / jnp.sqrt(level_ref[:1, :1])
         out_ref[:, here] = value.astype(out_ref.dtype)
 
     def times(left, right):
@@ -251,7 +259,7 @@
 
     if not pair:
         put_in_place(where_ref, masks, refs[0], refs[1], block, 0)
-        lower, upper = side_by_side(fields[: CHUNKS // 2], rows), side_by_side(fields[CHUNKS // 2 :], rows)
+        lower, upper = field[:rows, :middle], field[:rows, middle:]
         corner = block[middle : middle + middle // 2, :]
         corner = jnp.concatenate([corner[:, :middle], corner[:, middle:]], axis=0)
         finish(
@@ -267,17 +275,18 @@
 
     @pl.when(is_upper == 0)
     def _():
-        field = side_by_side(fields, rows)
         for c in range(CHUNKS):
             here = slice(c * width, (c + 1) * width)
-            finish(times(field, jnp.concatenate([block[:middle, here], block[height : height + middle, here]])), here)
+            right = jnp.concatenate([block[:middle, here], block[height : height + middle, here]])
+            finish(times(field[:rows, :], right), here)
 
     @pl.when(is_upper == 1)
     def _():
-        field = side_by_side(fields, rows)
         for c in range(CHUNKS):
             row = c * width if c * width < middle else height + c * width - middle
-            finish(times_transposed(field, block[row : row + width, :]), slice(c * width, (c + 1) * width))
+            finish(
+                times_transposed(field[:rows, :], block[row : row + width, :]), slice(c * width, (c + 1) * width)
+            )
 
 
 def local(orbitals, hamiltonian, neighbours):
@@ -324,17 +333,16 @@
         near[job] = order(near[job])
         far[job] = lax.ppermute(near[job], "elem", outward)
 
-    def more_panel(c):
-        for d in range(1, groups):
-            if d & (d - 1):
-                low = d & -d
-                if d ^ low in pieces[c] and d not in pieces[c]:
-                    pieces[c][d ^ low] = order(pieces[c][d ^ low])
-                    pieces[c][d] = to_group(pieces[c][d ^ low], low)
-
-    def settle(c, some=lambda d: True):
-        for d in [d for d in pieces[c] if d and some(d)]:
-            pieces[c][d] = order(pieces[c][d])
+    def pass_on(c):
+        bit = groups // 2
+        while bit > 1:
+            if bit | 1 not in pieces[c]:
+                pieces[c][bit] = order(pieces[c][bit])
+                low = 1
+                while low < bit:
+                    pieces[c][bit | low] = to_group(pieces[c][bit], low)
+                    low *= 2
+            bit //= 2
 
     def multiply(job):
         nonlocal squares
@@ -354,12 +362,11 @@
                 out, squares = order(*out)
             pieces[c][0] = out
             bit = groups // 2
-            while bit:
+            while bit > 1:
                 pieces[c][bit] = to_group(out, bit)
                 bit //= 2
-            if c > 1:
-                more_panel(c - 2)
-                settle(c - 2, lambda d: not d & (d - 1))
+            for earlier in range(max(c - 2, 0), c if c == CHUNKS - 1 else c - 1):
+                pass_on(earlier)
             return
         current[(stage + 1, c)] = out
         near[(stage + 1, c)] = lax.ppermute(out, "elem", swap)
@@ -376,7 +383,7 @@
     unit = 16 * tiles
     clock = Schedule()
     z_masks = [2 << i for i in range(lines.bit_length() - 1)]
-    there = {d: 3.0 if d == 1 else 10.5 for d in range(1, groups)}
+    panel, there = {}, {}
     mixed, mixes = None, 0
 
     def is_upper(d):
@@ -384,9 +391,6 @@
 
     def where(d):
         return jnp.stack([my_tile, is_upper(d) if d else odd]).astype(jnp.int32)
-
-    def all_chunks(d):
-        return [pieces[c][d] for c in range(CHUNKS)]
 
     def over_tiles(value, mask):
         sent = lax.ppermute(value, "elem", [(i, i ^ mask) for i in range(tiles)])
@@ -398,43 +402,53 @@
     def over_groups(value, d):
         return to_group(value, d), clock.transfer(value, "core" if d == 1 else "x")
 
-    def panel_process():
-        yield 4.0
-        for c in range(CHUNKS - 1):
-            more_panel(c)
-            settle(c)
-        yield 10.5
-        more_panel(CHUNKS - 1)
-        settle(CHUNKS - 1, lambda d: not d & (d - 1))
-        clock.spend(1.3)
-        for d in range(1, groups):
-            if d & (d - 1):
-                there[d] = clock.now + 3.5
-
     def gram_chunk(d, mask, extra):
         height = middle if d else middle + middle // 2
         height += -height % unit
-        fields = all_chunks(0)
-        if d:
-            fields += list(order(*all_chunks(d)))
-        if extra:
-            fields += [pieces[-1][other] for other in range(1, groups) if other != d]
+        cut = d not in panel
+        args = [panel[0]] if d else []
+        if cut:
+            if d:
+                pass_on(CHUNKS - 1)
+                for other in pieces[-1]:
+                    there.setdefault(other, max(clock.now + 4.0, 20.0))
+            args += order(*[pieces[c][d] for c in range(CHUNKS)])
+        others = [pieces[-1].get(other, panel.get(other)) for other in range(1, groups) if other != d] if extra else []
+        args += others
+        if not cut:
+            args.append(panel[d])
         half = jax.ShapeDtypeStruct((height // 2 + extra, columns), BF16)
+        outs = (half, half)
+        if cut:
+            outs += (jax.ShapeDtypeStruct((rows + EXTRA, columns), BF16),)
         scratch = (pltpu.VMEM((height, columns), BF16),)
         name = "gram_pair" if d else "gram_own"
         clock.spend(3.2 if d else 3.0)
-        return call(
-            functools.partial(gram_kernel, d > 0, mask), name, (half, half), (where(d),), fields, scratch, moved=5 * MIB
-        )
+        kernel = functools.partial(gram_kernel, d > 0, cut, mask, len(others))
+        outs = order(*call(kernel, name, outs, (where(d),), args, scratch))
+        if cut:
+            panel[d] = outs[2]
+            there[d] = clock.now
+        for low in (1 << i for i in range(groups.bit_length() - 1)):
+            if d | low not in pieces[-1] and (low < d & -d or low == 1 and d == 0):
+                panel[d | low] = to_group(panel[d], low)
+                there[d | low] = clock.transfer(panel[d], "core" if low == 1 else "x")
+                if d == 0:
+                    there[low] = min(there[low], 9.5)
+        return outs[:2]
 
     sent = [None]
 
     def process(d, masks, extra=0, round_y=False, behind=None):
         nonlocal mixed, mixes, level
-        need = list(there) if extra else [d] if d else []
-        while any(other not in pieces[-1] or there[other] > clock.now for other in need):
-            yield clock.now + 0.5
-        mine, value = order(*gram_chunk(d, masks[0], extra))
+        if d:
+            need = range(groups) if extra else (0,) if d != 1 and not d & (d - 1) else (0, d)
+            upper = d != 1 and not d & (d - 1)
+            while upper and clock.now < 10.5 or any(there.get(other, 1e9) > clock.now for other in need):
+                yield clock.now + 0.5
+            if d in panel:
+                panel[d] = order(panel[d])
+        mine, value = gram_chunk(d, masks[0], extra)
         terms = [mine]
         height = mine.shape[0] - extra
 
@@ -458,7 +472,8 @@
                 height //= 2
                 value = order(added(hop))
             received, arrival = over_tiles(value, mask)
-            yield arrival if hop or mask > 1 else arrival - (3.0 if d else 6.0)
+            yield arrival if hop else arrival - (3.0 if d else 6.0)
+            clock.now = max(clock.now, arrival)
             terms.append(order(received))
         while level is None and not extra:
             yield clock.now + 0.5
@@ -504,9 +519,9 @@
         mixes += 1
         shape = jax.ShapeDtypeStruct((rows, columns), BF16 if last else F32)
         scratch = (pltpu.VMEM((len(parts) * part.shape[0], columns), BF16),)
-        args = (() if first else (mixed,)) + (*all_chunks(d), *parts)
+        args = (() if first else (mixed,)) + (panel[d], *parts)
         if last:
-            args = (level, *args, *all_chunks(0))
+            args = (level, *args, panel[0])
         kernel = functools.partial(mix_kernel, d > 0, masks, first, last)
         name = "mix_pair" if d else "mix_own"
         clock.spend(3.2)
@@ -514,16 +529,13 @@
         if not last:
             mixed = order(mixed)
 
-    y_first, z_then_y, y_then_far = (1, *z_masks), (*z_masks[:1], 1, *z_masks[1:]), (1, *z_masks[::-1])
-    there[1] = 25.0
-    queue = sorted(range(1, groups), key=lambda d: (d == 1, d))
+    y_first, z_first, z_then_y = (1, *z_masks), (*z_masks, 1), (*z_masks[:1], 1, *z_masks[1:])
+    queue = sorted(range(1, groups), key=lambda d: (d != 1, -d))
     carrier = queue[min(1, len(queue) - 1)]
-    processes = [panel_process()]
+    processes = []
     for d in queue:
-        first = d == queue[0] and d != carrier
-        behind = carrier if d == 1 and d != carrier else None
-        processes.append(process(d, z_then_y if first else y_first, EXTRA if d == carrier else 0, first, behind))
-    processes.append(process(0, y_then_far, behind=1))
+        processes.append(process(d, z_first if d == 1 else y_first, EXTRA if d == carrier else 0))
+    processes.append(process(0, z_then_y))
     clock.run(processes)
     return mixed
 

time: 301 us -> 331 us (1.100)
  waiting for transfers between devices: 130 us -> 168 us
  starting transfers between devices: 109 us -> 102 us
  local copies, waits for them, and re-layouts: 13.8 us -> 8.38 us
  Pallas kernels: 45.3 us -> 49.3 us
    ppermute x17 -> x15, waiting for transfers between devices: 21.7 us -> 46.6 us  [to_group(): return lax.ppermute(value, 'orb', [(i, i ^ d) for i in range(groups)])]
    ppermute x25 -> x24, waiting for transfers between devices: 79 us -> 96 us  [over_tiles(): sent = lax.ppermute(value, 'elem', [(i, i ^ mask) for i in range(tiles)])]
    ppermute x25 -> x24, starting transfers between devices: 36.2 us -> 29 us  [over_tiles(): sent = lax.ppermute(value, 'elem', [(i, i ^ mask) for i in range(tiles)])]
    unnamed x49 -> x11, local copies, waits for them, and re-layouts: 7.66 us -> 2.29 us
    ppermute x12, waiting for transfers between devices: 6.98 us -> 1.87 us  [send_on(): far[job] = lax.ppermute(near[job], 'elem', outward)]
    pallas_call x32, Pallas kernels: 45.3 us -> 49.3 us  [call(): pl.pallas_call(kernel, out_shape=outs, in_specs=[pl.BlockSpec(memory_spac...]
    ppermute x17 -> x15, starting transfers between devices: 9.12 us -> 9.43 us  [to_group(): return lax.ppermute(value, 'orb', [(i, i ^ d) for i in range(groups)])]
  transfers between devices with their start and end apart: 66 -> 63, of which waited for: 34 -> 39; matrix products, arithmetic and copies ran while one was open for 2% -> 2% of each run, Pallas kernels for 12% -> 12%
where the time goes in v10:
time: 331 us; the launch traced here: 329 us
  waiting for transfers between devices  168 us (51%)
  starting transfers between devices  102 us (31%)
  Pallas kernels  49.3 us (15%)
  local copies, waits for them, and re-layouts  8.38 us (3%)
    ppermute x24, waiting for transfers between devices, over_tiles(): sent = lax.ppermute(value, 'elem', [(i, i ^ mask) for i in range(tiles)])  96 us
    pallas_call x32, Pallas kernels, call(): pl.pallas_call(kernel, out_shape=outs, in_specs=[pl.BlockSpec(memory_spac...  49.3 us
    ppermute x15, waiting for transfers between devices, to_group(): return lax.ppermute(value, 'orb', [(i, i ^ d) for i in range(groups)])  46.6 us
    ppermute x24, starting transfers between devices, over_tiles(): sent = lax.ppermute(value, 'elem', [(i, i ^ mask) for i in range(tiles)])  29 us
    ppermute x8, starting transfers between devices, multiply(): near[stage + 1, c] = lax.ppermute(out, 'elem', swap)  28.4 us
    ppermute x12, starting transfers between devices, send_on(): far[job] = lax.ppermute(near[job], 'elem', outward)  24.8 us
    ppermute x8, waiting for transfers between devices, multiply(): near[stage + 1, c] = lax.ppermute(out, 'elem', swap)  13.8 us
    ppermute x15, starting transfers between devices, to_group(): return lax.ppermute(value, 'orb', [(i, i ^ d) for i in range(groups)])  9.43 us
  transfers between devices with their start and end apart: 63, of which 39 were waited for; matrix products, arithmetic and copies ran while one was open for 2% of the time, Pallas kernels for 12%

profile of v10, /device:TPU:0, one launch (start us, length us, event | category | flops | bytes accessed | tf_op | source)
XLA Modules:
  0.0 329.4 jit_solution(1908592154003052428)
XLA Ops:
  1.5 3.0 collective-permute-start
  4.6 2.2 slice_bitcast_fusion
  8.0 2.3 concatenate.30.blocks_ref
  10.5 4.0 %collective-permute-done.near_ref = bf16[768,256]{1,0:T(8,128)(2,1)S(1)} collective-permute-done((bf16[768,256]{1,0:T(8,128)(2,1)S(1)}, bf16[768,256]{1,0:T(8,128)(2,1)S(1)}, u32[]{:S(2)}, u32[]{:S(2)}) %collective-permute-start) | collective-permute-done | bytes 393248 | tf_op jit(solution)/shard_map/ppermute | solution.py:320
  14.5 2.1 collective-permute-start.1
  16.6 3.5 %collective-permute-start.4 = (bf16[768,256]{1,0:T(8,128)(2,1)S(1)}, bf16[768,256]{1,0:T(8,128)(2,1)S(1)}, u32[]{:S(2)}, u32[]{:S(2)}) collective-permute-start(bf16[768,256]{1,0:T(8,128)(2,1)S(1)} %get-tuple-element.254.field_ref.refs_0_), channel_id=1, source_target_pairs={{0,4},{4,0},{8,12},{12,8},{16,20},{20,16},{24,28},{28,24},{1,5},{5... | collective-permute-start | bytes 1179656 | tf_op jit(solution)/shard_map/ppermute | solution.py:325
  20.1 2.8 collective-permute-done.2.near_ref
  22.9 2.1 collective-permute-start.7
  25.0 3.5 %collective-permute-start.6 = (bf16[768,256]{1,0:T(8,128)(2,1)S(1)}, bf16[768,256]{1,0:T(8,128)(2,1)S(1)}, u32[]{:S(2)}, u32[]{:S(2)}) collective-permute-start(bf16[768,256]{1,0:T(8,128)(2,1)S(1)} %get-tuple-element.257.field_ref.refs_0_), channel_id=1, source_target_pairs={{0,4},{4,0},{8,12},{12,8},{16,20},{20,16},{24,28},{28,24},{1,5},{5... | collective-permute-start | bytes 1179656 | tf_op jit(solution)/shard_map/ppermute | solution.py:325
  31.3 2.1 collective-permute-start.5
  33.4 3.5 %collective-permute-start.3 = (bf16[768,256]{1,0:T(8,128)(2,1)S(1)}, bf16[768,256]{1,0:T(8,128)(2,1)S(1)}, u32[]{:S(2)}, u32[]{:S(2)}) collective-permute-start(bf16[768,256]{1,0:T(8,128)(2,1)S(1)} %get-tuple-element.253.field_ref), channel_id=1, source_target_pairs={{0,4},{4,0},{8,12},{12,8},{16,20},{20,16},{24,28},{28,24},{1,5},{5... | collective-permute-start | bytes 1179656 | tf_op jit(solution)/shard_map/ppermute | solution.py:372
  39.7 2.1 collective-permute-start.10
  41.9 3.5 %collective-permute-start.9 = (bf16[768,256]{1,0:T(8,128)(2,1)S(1)}, bf16[768,256]{1,0:T(8,128)(2,1)S(1)}, u32[]{:S(2)}, u32[]{:S(2)}) collective-permute-start(bf16[768,256]{1,0:T(8,128)(2,1)S(1)} %get-tuple-element.272.field_ref), channel_id=1, source_target_pairs={{0,4},{4,0},{8,12},{12,8},{16,20},{20,16},{24,28},{28,24},{1,5},{5... | collective-permute-start | bytes 1179656 | tf_op jit(solution)/shard_map/ppermute | solution.py:372
  48.2 2.1 collective-permute-start.8
  50.3 3.5 %collective-permute-start.12 = (bf16[768,256]{1,0:T(8,128)(2,1)S(1)}, bf16[768,256]{1,0:T(8,128)(2,1)S(1)}, u32[]{:S(2)}, u32[]{:S(2)}) collective-permute-start(bf16[768,256]{1,0:T(8,128)(2,1)S(1)} %get-tuple-element.284.field_ref), channel_id=1, source_target_pairs={{0,4},{4,0},{8,12},{12,8},{16,20},{20,16},{24,28},{28,24},{1,5},{5... | collective-permute-start | bytes 1179656 | tf_op jit(solution)/shard_map/ppermute | solution.py:372
  56.6 2.1 collective-permute-start.15
  58.7 3.5 %collective-permute-start.14 = (bf16[768,256]{1,0:T(8,128)(2,1)S(1)}, bf16[768,256]{1,0:T(8,128)(2,1)S(1)}, u32[]{:S(2)}, u32[]{:S(2)}) collective-permute-start(bf16[768,256]{1,0:T(8,128)(2,1)S(1)} %get-tuple-element.287.field_ref), channel_id=1, source_target_pairs={{0,4},{4,0},{8,12},{12,8},{16,20},{20,16},{24,28},{28,24},{1,5},{5... | collective-permute-start | bytes 1179656 | tf_op jit(solution)/shard_map/ppermute | solution.py:372
  65.0 2.1 collective-permute-start.13
  67.1 3.5 %collective-permute-start.11 = (bf16[768,256]{1,0:T(8,128)(2,1)S(1)}, bf16[768,256]{1,0:T(8,128)(2,1)S(1)}, u32[]{:S(2)}, u32[]{:S(2)}) collective-permute-start(bf16[768,256]{1,0:T(8,128)(2,1)S(1)} %product_1.4.field_ref), channel_id=1, source_target_pairs={{0,4},{4,0},{8,12},{12,8},{16,20},{20,16},{24,28},{28,24},{1,5},{5... | collective-permute-start | bytes 1179656 | tf_op jit(solution)/shard_map/ppermute | solution.py:372
  73.5 2.1 collective-permute-start.18
  75.6 3.5 %collective-permute-start.17 = (bf16[768,256]{1,0:T(8,128)(2,1)S(1)}, bf16[768,256]{1,0:T(8,128)(2,1)S(1)}, u32[]{:S(2)}, u32[]{:S(2)}) collective-permute-start(bf16[768,256]{1,0:T(8,128)(2,1)S(1)} %product_1.5.field_ref), channel_id=1, source_target_pairs={{0,4},{4,0},{8,12},{12,8},{16,20},{20,16},{24,28},{28,24},{1,5},{5... | collective-permute-start | bytes 1179656 | tf_op jit(solution)/shard_map/ppermute | solution.py:372
  81.9 2.1 collective-permute-start.16
  84.0 3.5 %collective-permute-start.20 = (bf16[768,256]{1,0:T(8,128)(2,1)S(1)}, bf16[768,256]{1,0:T(8,128)(2,1)S(1)}, u32[]{:S(2)}, u32[]{:S(2)}) collective-permute-start(bf16[768,256]{1,0:T(8,128)(2,1)S(1)} %product_1.6.field_ref), channel_id=1, source_target_pairs={{0,4},{4,0},{8,12},{12,8},{16,20},{20,16},{24,28},{28,24},{1,5},{5... | collective-permute-start | bytes 1179656 | tf_op jit(solution)/shard_map/ppermute | solution.py:372
  90.3 2.1 collective-permute-start.19
  92.4 3.5 %collective-permute-start.22 = (bf16[768,256]{1,0:T(8,128)(2,1)S(1)}, bf16[768,256]{1,0:T(8,128)(2,1)S(1)}, u32[]{:S(2)}, u32[]{:S(2)}) collective-permute-start(bf16[768,256]{1,0:T(8,128)(2,1)S(1)} %product_1.7.field_ref), channel_id=1, source_target_pairs={{0,4},{4,0},{8,12},{12,8},{16,20},{20,16},{24,28},{28,24},{1,5},{5... | collective-permute-start | bytes 1179656 | tf_op jit(solution)/shard_map/ppermute | solution.py:372
  98.7 2.1 collective-permute-start.21
  102.9 3.5 %collective-permute-done.22.near_ref = bf16[768,256]{1,0:T(8,128)(2,1)S(1)} collective-permute-done((bf16[768,256]{1,0:T(8,128)(2,1)S(1)}, bf16[768,256]{1,0:T(8,128)(2,1)S(1)}, u32[]{:S(2)}, u32[]{:S(2)}) %collective-permute-start.22) | collective-permute-done | bytes 393248 | tf_op jit(solution)/shard_map/ppermute | solution.py:372
  106.3 1.7 collective-permute-start.24
  110.2 2.0 product_2.6
  114.4 4.1 %collective-permute-done.24.refs_1_ = bf16[768,256]{1,0:T(8,128)(2,1)} collective-permute-done((bf16[768,256]{1,0:T(8,128)(2,1)S(1)}, bf16[768,256]{1,0:T(8,128)(2,1)}, u32[]{:S(2)}, u32[]{:S(2)}) %collective-permute-start.24) | collective-permute-done | bytes 393248 | tf_op jit(solution)/shard_map/ppermute | solution.py:307
  120.3 2.2 product_2.7.refs_3_
  122.5 4.4 %collective-permute-done.26.refs_2_ = bf16[768,256]{1,0:T(8,128)(2,1)} collective-permute-done((bf16[768,256]{1,0:T(8,128)(2,1)S(1)}, bf16[768,256]{1,0:T(8,128)(2,1)}, u32[]{:S(2)}, u32[]{:S(2)}) %collective-permute-start.26) | collective-permute-done | bytes 393248 | tf_op jit(solution)/shard_map/ppermute | solution.py:307
  126.9 6.7 %collective-permute-done.25.refs_3_ = bf16[768,256]{1,0:T(8,128)(2,1)} collective-permute-done((bf16[768,256]{1,0:T(8,128)(2,1)}, bf16[768,256]{1,0:T(8,128)(2,1)}, u32[]{:S(2)}, u32[]{:S(2)}) %collective-permute-start.25) | collective-permute-done | bytes 393248 | tf_op jit(solution)/shard_map/ppermute | solution.py:307
  133.6 3.6 %gram_own.1 = (bf16[384,1024]{1,0:T(8,128)(2,1)S(1)}, bf16[384,1024]{1,0:T(8,128)(2,1)}, bf16[784,1024]{1,0:T(8,128)(2,1)S(1)}) custom-call(s32[2]{0:T(128)S(1)} %get-tuple-element.487.where_ref, bf16[768,256]{1,0:T(8,128)(2,1)S(1)} %get-tuple-element.344.refs_0_, bf16[768,256]{1,0:T(8,128)(2,1)S(1)} %get-tuple-element.345.refs_1_, ...), custom_call_target="tpu_custom_call" | custom-call | flops 1024 | bytes 1024 | tf_op jit(solution)/shard_map/gram_own/pallas_call | solution.py:96
  143.2 8.1 %collective-permute-done.30.refs_4_.refs_6_ = bf16[784,256]{1,0:T(8,128)(2,1)} collective-permute-done((bf16[784,256]{1,0:T(8,128)(2,1)}, bf16[784,256]{1,0:T(8,128)(2,1)}, u32[]{:S(2)}, u32[]{:S(2)}) %collective-permute-start.30) | collective-permute-done | bytes 401440 | tf_op jit(solution)/shard_map/ppermute | solution.py:307
  151.8 2.9 gram_pair.4
  156.3 2.0 collective-permute-done.33.refs_1_
  161.1 2.4 gram_pair.5
  165.6 3.9 %collective-permute-done.35.refs_1_ = bf16[256,1024]{1,0:T(8,128)(2,1)S(1)} collective-permute-done((bf16[256,1024]{1,0:T(8,128)(2,1)S(1)}, bf16[256,1024]{1,0:T(8,128)(2,1)S(1)}, u32[]{:S(2)}, u32[]{:S(2)}) %collective-permute-start.35) | collective-permute-done | bytes 524320 | tf_op jit(solution)/shard_map/ppermute | solution.py:396
  172.5 2.6 collective-permute-start.40
  175.1 14.4 %collective-permute-done.37.refs_2_ = bf16[192,1024]{1,0:T(8,128)(2,1)S(1)} collective-permute-done((bf16[192,1024]{1,0:T(8,128)(2,1)S(1)}, bf16[192,1024]{1,0:T(8,128)(2,1)S(1)}, u32[]{:S(2)}, u32[]{:S(2)}) %collective-permute-start.37) | collective-permute-done | bytes 393248 | tf_op jit(solution)/shard_map/ppermute | solution.py:396
  192.6 2.5 collective-permute-start.42
  197.3 5.7 %collective-permute-done.42.refs_3_ = bf16[96,1024]{1,0:T(8,128)(2,1)S(1)} collective-permute-done((bf16[96,1024]{1,0:T(8,128)(2,1)S(1)}, bf16[96,1024]{1,0:T(8,128)(2,1)S(1)}, u32[]{:S(2)}, u32[]{:S(2)}) %collective-permute-start.42) | collective-permute-done | bytes 196640 | tf_op jit(solution)/shard_map/ppermute | solution.py:396
  203.0 1.9 collective-permute-done.39.refs_2_
  208.6 12.1 %collective-permute-done.44.refs_3_ = bf16[64,1024]{1,0:T(8,128)(2,1)S(1)} collective-permute-done((bf16[64,1024]{1,0:T(8,128)(2,1)S(1)}, bf16[64,1024]{1,0:T(8,128)(2,1)S(1)}, u32[]{:S(2)}, u32[]{:S(2)}) %collective-permute-start.44) | collective-permute-done | bytes 131104 | tf_op jit(solution)/shard_map/ppermute | solution.py:396
  225.7 3.0 collective-permute-start.47
  228.8 10.4 %collective-permute-done.48 = bf16[64,1024]{1,0:T(8,128)(2,1)S(1)} collective-permute-done((bf16[64,1024]{1,0:T(8,128)(2,1)S(1)}, bf16[64,1024]{1,0:T(8,128)(2,1)S(1)}, u32[]{:S(2)}, u32[]{:S(2)}) %collective-permute-start.48) | collective-permute-done | bytes 131104 | tf_op jit(solution)/shard_map/ppermute | solution.py:396
  239.2 2.8 collective-permute-done.47
  242.0 4.0 %collective-permute-start.50 = (bf16[128,1024]{1,0:T(8,128)(2,1)S(1)}, bf16[128,1024]{1,0:T(8,128)(2,1)S(1)}, u32[]{:S(2)}, u32[]{:S(2)}) collective-permute-start(bf16[128,1024]{1,0:T(8,128)(2,1)S(1)} %pad_maximum_fusion.6), channel_id=1, source_target_pairs={{0,8},{4,12},{8,0},{12,4},{16,24},{20,28},{24,16},{28,20},{1,9},{5... | collective-permute-start | bytes 786440 | tf_op jit(solution)/shard_map/ppermute | solution.py:396
  246.0 5.9 %collective-permute-done.51 = bf16[96,1024]{1,0:T(8,128)(2,1)S(1)} collective-permute-done((bf16[96,1024]{1,0:T(8,128)(2,1)S(1)}, bf16[96,1024]{1,0:T(8,128)(2,1)S(1)}, u32[]{:S(2)}, u32[]{:S(2)}) %collective-permute-start.51) | collective-permute-done | bytes 196640 | tf_op jit(solution)/shard_map/ppermute | solution.py:396
  252.6 3.4 %collective-permute-done.46 = bf16[128,1024]{1,0:T(8,128)(2,1)S(1)} collective-permute-done((bf16[128,1024]{1,0:T(8,128)(2,1)S(1)}, bf16[128,1024]{1,0:T(8,128)(2,1)S(1)}, u32[]{:S(2)}, u32[]{:S(2)}) %collective-permute-start.46) | collective-permute-done | bytes 262176 | tf_op jit(solution)/shard_map/ppermute | solution.py:396
  256.2 3.2 collective-permute-done.50
  259.4 5.6 %collective-permute-done.49 = bf16[128,1024]{1,0:T(8,128)(2,1)S(1)} collective-permute-done((bf16[128,1024]{1,0:T(8,128)(2,1)S(1)}, bf16[128,1024]{1,0:T(8,128)(2,1)S(1)}, u32[]{:S(2)}, u32[]{:S(2)}) %collective-permute-start.49) | collective-permute-done | bytes 262176 | tf_op jit(solution)/shard_map/ppermute | solution.py:396
  268.8 6.7 %collective-permute-done.52.refs_2_ = bf16[256,1024]{1,0:T(8,128)(2,1)S(1)} collective-permute-done((bf16[256,1024]{1,0:T(8,128)(2,1)S(1)}, bf16[256,1024]{1,0:T(8,128)(2,1)S(1)}, u32[]{:S(2)}, u32[]{:S(2)}) %collective-permute-start.52) | collective-permute-done | bytes 524320 | tf_op jit(solution)/shard_map/ppermute | solution.py:396
  275.5 4.4 %collective-permute-done.55.refs_3_ = bf16[256,1024]{1,0:T(8,128)(2,1)S(1)} collective-permute-done((bf16[256,1024]{1,0:T(8,128)(2,1)S(1)}, bf16[256,1024]{1,0:T(8,128)(2,1)S(1)}, u32[]{:S(2)}, u32[]{:S(2)}) %collective-permute-start.55) | collective-permute-done | bytes 524320 | tf_op jit(solution)/shard_map/ppermute | solution.py:396
  279.9 8.9 %collective-permute-done.60.refs_4_ = bf16[256,1024]{1,0:T(8,128)(2,1)S(1)} collective-permute-done((bf16[256,1024]{1,0:T(8,128)(2,1)S(1)}, bf16[256,1024]{1,0:T(8,128)(2,1)S(1)}, u32[]{:S(2)}, u32[]{:S(2)}) %collective-permute-start.60) | collective-permute-done | bytes 524320 | tf_op jit(solution)/shard_map/ppermute | solution.py:396
  290.8 3.5 %collective-permute-done.59.refs_3_ = bf16[384,1024]{1,0:T(8,128)(2,1)S(1)} collective-permute-done((bf16[384,1024]{1,0:T(8,128)(2,1)S(1)}, bf16[384,1024]{1,0:T(8,128)(2,1)S(1)}, u32[]{:S(2)}, u32[]{:S(2)}) %collective-permute-start.59) | collective-permute-done | bytes 786464 | tf_op jit(solution)/shard_map/ppermute | solution.py:396
  294.3 2.5 mix_pair.3.refs_0_
  296.9 6.0 %collective-permute-done.57.refs_5_ = bf16[256,1024]{1,0:T(8,128)(2,1)S(1)} collective-permute-done((bf16[256,1024]{1,0:T(8,128)(2,1)S(1)}, bf16[256,1024]{1,0:T(8,128)(2,1)S(1)}, u32[]{:S(2)}, u32[]{:S(2)}) %collective-permute-start.57) | collective-permute-done | bytes 524320 | tf_op jit(solution)/shard_map/ppermute | solution.py:307
  302.9 3.0 mix_pair.4.refs_0_
  305.9 8.3 %collective-permute-done.61.refs_5_ = bf16[256,1024]{1,0:T(8,128)(2,1)S(1)} collective-permute-done((bf16[256,1024]{1,0:T(8,128)(2,1)S(1)}, bf16[256,1024]{1,0:T(8,128)(2,1)S(1)}, u32[]{:S(2)}, u32[]{:S(2)}) %collective-permute-start.61) | collective-permute-done | bytes 524320 | tf_op jit(solution)/shard_map/ppermute | solution.py:307
  314.2 2.7 mix_own.1.refs_1_
  316.9 8.5 %collective-permute-done.62.refs_6_ = bf16[256,1024]{1,0:T(8,128)(2,1)S(1)} collective-permute-done((bf16[256,1024]{1,0:T(8,128)(2,1)S(1)}, bf16[256,1024]{1,0:T(8,128)(2,1)S(1)}, u32[]{:S(2)}, u32[]{:S(2)}) %collective-permute-start.62) | collective-permute-done | bytes 524320 | tf_op jit(solution)/shard_map/ppermute | solution.py:307
  325.4 4.0 %mix_pair.5 = bf16[768,1024]{1,0:T(8,128)(2,1)} custom-call(s32[2]{0:T(128)S(1)} %get-tuple-element.486.where_ref, f32[8,128]{1,0:T(8,128)S(1)} %get-tuple-element.429.refs_4_.refs_0_, f32[768,1024]{1,0:T(8,128)S(1)} %mix_own.1.refs_1_, bf16[784,1024]{1,0:T(8,128)(2,1)S(1)} %get-tuple-element.470.refs_2_, bf16[256,1024]{1,0:T(8,128)(2,1)S(1)} %pad_maximum_fusion.3.refs_3_, ...), custom_call_target="tpu_custom_call" | custom-call | flops 1024 | bytes 5242880 | tf_op jit(solution)/shard_map/mix_pair/pallas_call | solution.py:96
  (126 shorter events, 72.6 us)
Async XLA Ops:
  1.5 13.0 %collective-permute-start = (bf16[768,256]{1,0:T(8,128)(2,1)S(1)}, bf16[768,256]{1,0:T(8,128)(2,1)S(1)}, u32[]{:S(2)}, u32[]{:S(2)}) collective-permute-start(bf16[768,256]{1,0:T(8,128)(2,1)S(1)} %get-tuple-element.477.field_ref.refs_0_), channel_id=1, source_target_pairs={{0,4},{4,0},{8,12},{12,8},{16,20},{20,16},{24,28},{28,24},{1,5},{5... | collective-permute-start | bytes 1179656 | tf_op jit(solution)/shard_map/ppermute | solution.py:320
  10.5 12.4 %collective-permute-start.2 = (bf16[768,256]{1,0:T(8,128)(2,1)S(1)}, bf16[768,256]{1,0:T(8,128)(2,1)S(1)}, u32[]{:S(2)}, u32[]{:S(2)}) collective-permute-start(bf16[768,256]{1,0:T(8,128)(2,1)S(1)} %get-tuple-element.246.field_ref.refs_0_), channel_id=1, source_target_pairs={{0,4},{4,0},{8,12},{12,8},{16,20},{20,16},{24,28},{28,24},{1,5},{5... | collective-permute-start | bytes 1179656 | tf_op jit(solution)/shard_map/ppermute | solution.py:325
  14.5 14.1 %collective-permute-start.1 = (bf16[768,256]{1,0:T(8,128)(2,1)S(1)}, bf16[768,256]{1,0:T(8,128)(2,1)S(1)}, u32[]{:S(2)}, u32[]{:S(2)}) collective-permute-start(bf16[768,256]{1,0:T(8,128)(2,1)S(1)} %collective-permute-done.near_ref), channel_id=1, source_target_pairs={{0,8},{4,28},{8,16},{12,4},{16,24},{20,12},{24,0},{28,20},{1,9},{5... | collective-permute-start | bytes 1179656 | tf_op jit(solution)/shard_map/ppermute | solution.py:334
  16.6 14.7 %collective-permute-start.4 = (bf16[768,256]{1,0:T(8,128)(2,1)S(1)}, bf16[768,256]{1,0:T(8,128)(2,1)S(1)}, u32[]{:S(2)}, u32[]{:S(2)}) collective-permute-start(bf16[768,256]{1,0:T(8,128)(2,1)S(1)} %get-tuple-element.254.field_ref.refs_0_), channel_id=1, source_target_pairs={{0,4},{4,0},{8,12},{12,8},{16,20},{20,16},{24,28},{28,24},{1,5},{5... | collective-permute-start | bytes 1179656 | tf_op jit(solution)/shard_map/ppermute | solution.py:325
  22.9 14.1 %collective-permute-start.7 = (bf16[768,256]{1,0:T(8,128)(2,1)S(1)}, bf16[768,256]{1,0:T(8,128)(2,1)S(1)}, u32[]{:S(2)}, u32[]{:S(2)}) collective-permute-start(bf16[768,256]{1,0:T(8,128)(2,1)S(1)} %collective-permute-done.2.near_ref), channel_id=1, source_target_pairs={{0,8},{4,28},{8,16},{12,4},{16,24},{20,12},{24,0},{28,20},{1,9},{5... | collective-permute-start | bytes 1179656 | tf_op jit(solution)/shard_map/ppermute | solution.py:334
  25.0 14.7 %collective-permute-start.6 = (bf16[768,256]{1,0:T(8,128)(2,1)S(1)}, bf16[768,256]{1,0:T(8,128)(2,1)S(1)}, u32[]{:S(2)}, u32[]{:S(2)}) collective-permute-start(bf16[768,256]{1,0:T(8,128)(2,1)S(1)} %get-tuple-element.257.field_ref.refs_0_), channel_id=1, source_target_pairs={{0,4},{4,0},{8,12},{12,8},{16,20},{20,16},{24,28},{28,24},{1,5},{5... | collective-permute-start | bytes 1179656 | tf_op jit(solution)/shard_map/ppermute | solution.py:325
  31.3 14.1 %collective-permute-start.5 = (bf16[768,256]{1,0:T(8,128)(2,1)S(1)}, bf16[768,256]{1,0:T(8,128)(2,1)S(1)}, u32[]{:S(2)}, u32[]{:S(2)}) collective-permute-start(bf16[768,256]{1,0:T(8,128)(2,1)S(1)} %collective-permute-done.4.near_ref), channel_id=1, source_target_pairs={{0,8},{4,28},{8,16},{12,4},{16,24},{20,12},{24,0},{28,20},{1,9},{5... | collective-permute-start | bytes 1179656 | tf_op jit(solution)/shard_map/ppermute | solution.py:334
  33.4 14.7 %collective-permute-start.3 = (bf16[768,256]{1,0:T(8,128)(2,1)S(1)}, bf16[768,256]{1,0:T(8,128)(2,1)S(1)}, u32[]{:S(2)}, u32[]{:S(2)}) collective-permute-start(bf16[768,256]{1,0:T(8,128)(2,1)S(1)} %get-tuple-element.253.field_ref), channel_id=1, source_target_pairs={{0,4},{4,0},{8,12},{12,8},{16,20},{20,16},{24,28},{28,24},{1,5},{5... | collective-permute-start | bytes 1179656 | tf_op jit(solution)/shard_map/ppermute | solution.py:372
  39.7 14.1 %collective-permute-start.10 = (bf16[768,256]{1,0:T(8,128)(2,1)S(1)}, bf16[768,256]{1,0:T(8,128)(2,1)S(1)}, u32[]{:S(2)}, u32[]{:S(2)}) collective-permute-start(bf16[768,256]{1,0:T(8,128)(2,1)S(1)} %collective-permute-done.6.near_ref), channel_id=1, source_target_pairs={{0,8},{4,28},{8,16},{12,4},{16,24},{20,12},{24,0},{28,20},{1,9},{5... | collective-permute-start | bytes 1179656 | tf_op jit(solution)/shard_map/ppermute | solution.py:334
  41.9 14.7 %collective-permute-start.9 = (bf16[768,256]{1,0:T(8,128)(2,1)S(1)}, bf16[768,256]{1,0:T(8,128)(2,1)S(1)}, u32[]{:S(2)}, u32[]{:S(2)}) collective-permute-start(bf16[768,256]{1,0:T(8,128)(2,1)S(1)} %get-tuple-element.272.field_ref), channel_id=1, source_target_pairs={{0,4},{4,0},{8,12},{12,8},{16,20},{20,16},{24,28},{28,24},{1,5},{5... | collective-permute-start | bytes 1179656 | tf_op jit(solution)/shard_map/ppermute | solution.py:372
  48.2 14.1 %collective-permute-start.8 = (bf16[768,256]{1,0:T(8,128)(2,1)S(1)}, bf16[768,256]{1,0:T(8,128)(2,1)S(1)}, u32[]{:S(2)}, u32[]{:S(2)}) collective-permute-start(bf16[768,256]{1,0:T(8,128)(2,1)S(1)} %collective-permute-done.3.near_ref), channel_id=1, source_target_pairs={{0,8},{4,28},{8,16},{12,4},{16,24},{20,12},{24,0},{28,20},{1,9},{5... | collective-permute-start | bytes 1179656 | tf_op jit(solution)/shard_map/ppermute | solution.py:334
  50.3 14.7 %collective-permute-start.12 = (bf16[768,256]{1,0:T(8,128)(2,1)S(1)}, bf16[768,256]{1,0:T(8,128)(2,1)S(1)}, u32[]{:S(2)}, u32[]{:S(2)}) collective-permute-start(bf16[768,256]{1,0:T(8,128)(2,1)S(1)} %get-tuple-element.284.field_ref), channel_id=1, source_target_pairs={{0,4},{4,0},{8,12},{12,8},{16,20},{20,16},{24,28},{28,24},{1,5},{5... | collective-permute-start | bytes 1179656 | tf_op jit(solution)/shard_map/ppermute | solution.py:372
  56.6 14.1 %collective-permute-start.15 = (bf16[768,256]{1,0:T(8,128)(2,1)S(1)}, bf16[768,256]{1,0:T(8,128)(2,1)S(1)}, u32[]{:S(2)}, u32[]{:S(2)}) collective-permute-start(bf16[768,256]{1,0:T(8,128)(2,1)S(1)} %collective-permute-done.9.near_ref), channel_id=1, source_target_pairs={{0,8},{4,28},{8,16},{12,4},{16,24},{20,12},{24,0},{28,20},{1,9},{5... | collective-permute-start | bytes 1179656 | tf_op jit(solution)/shard_map/ppermute | solution.py:334
  58.7 14.7 %collective-permute-start.14 = (bf16[768,256]{1,0:T(8,128)(2,1)S(1)}, bf16[768,256]{1,0:T(8,128)(2,1)S(1)}, u32[]{:S(2)}, u32[]{:S(2)}) collective-permute-start(bf16[768,256]{1,0:T(8,128)(2,1)S(1)} %get-tuple-element.287.field_ref), channel_id=1, source_target_pairs={{0,4},{4,0},{8,12},{12,8},{16,20},{20,16},{24,28},{28,24},{1,5},{5... | collective-permute-start | bytes 1179656 | tf_op jit(solution)/shard_map/ppermute | solution.py:372
  65.0 14.1 %collective-permute-start.13 = (bf16[768,256]{1,0:T(8,128)(2,1)S(1)}, bf16[768,256]{1,0:T(8,128)(2,1)S(1)}, u32[]{:S(2)}, u32[]{:S(2)}) collective-permute-start(bf16[768,256]{1,0:T(8,128)(2,1)S(1)} %collective-permute-done.12.near_ref), channel_id=1, source_target_pairs={{0,8},{4,28},{8,16},{12,4},{16,24},{20,12},{24,0},{28,20},{1,9},{5... | collective-permute-start | bytes 1179656 | tf_op jit(solution)/shard_map/ppermute | solution.py:334
  67.1 14.7 %collective-permute-start.11 = (bf16[768,256]{1,0:T(8,128)(2,1)S(1)}, bf16[768,256]{1,0:T(8,128)(2,1)S(1)}, u32[]{:S(2)}, u32[]{:S(2)}) collective-permute-start(bf16[768,256]{1,0:T(8,128)(2,1)S(1)} %product_1.4.field_ref), channel_id=1, source_target_pairs={{0,4},{4,0},{8,12},{12,8},{16,20},{20,16},{24,28},{28,24},{1,5},{5... | collective-permute-start | bytes 1179656 | tf_op jit(solution)/shard_map/ppermute | solution.py:372
  73.5 14.1 %collective-permute-start.18 = (bf16[768,256]{1,0:T(8,128)(2,1)S(1)}, bf16[768,256]{1,0:T(8,128)(2,1)S(1)}, u32[]{:S(2)}, u32[]{:S(2)}) collective-permute-start(bf16[768,256]{1,0:T(8,128)(2,1)S(1)} %collective-permute-done.14.near_ref), channel_id=1, source_target_pairs={{0,8},{4,28},{8,16},{12,4},{16,24},{20,12},{24,0},{28,20},{1,9},{5... | collective-permute-start | bytes 1179656 | tf_op jit(solution)/shard_map/ppermute | solution.py:334
  75.6 14.7 %collective-permute-start.17 = (bf16[768,256]{1,0:T(8,128)(2,1)S(1)}, bf16[768,256]{1,0:T(8,128)(2,1)S(1)}, u32[]{:S(2)}, u32[]{:S(2)}) collective-permute-start(bf16[768,256]{1,0:T(8,128)(2,1)S(1)} %product_1.5.field_ref), channel_id=1, source_target_pairs={{0,4},{4,0},{8,12},{12,8},{16,20},{20,16},{24,28},{28,24},{1,5},{5... | collective-permute-start | bytes 1179656 | tf_op jit(solution)/shard_map/ppermute | solution.py:372
  81.9 14.1 %collective-permute-start.16 = (bf16[768,256]{1,0:T(8,128)(2,1)S(1)}, bf16[768,256]{1,0:T(8,128)(2,1)S(1)}, u32[]{:S(2)}, u32[]{:S(2)}) collective-permute-start(bf16[768,256]{1,0:T(8,128)(2,1)S(1)} %collective-permute-done.11.near_ref), channel_id=1, source_target_pairs={{0,8},{4,28},{8,16},{12,4},{16,24},{20,12},{24,0},{28,20},{1,9},{5... | collective-permute-start | bytes 1179656 | tf_op jit(solution)/shard_map/ppermute | solution.py:334
  84.0 14.7 %collective-permute-start.20 = (bf16[768,256]{1,0:T(8,128)(2,1)S(1)}, bf16[768,256]{1,0:T(8,128)(2,1)S(1)}, u32[]{:S(2)}, u32[]{:S(2)}) collective-permute-start(bf16[768,256]{1,0:T(8,128)(2,1)S(1)} %product_1.6.field_ref), channel_id=1, source_target_pairs={{0,4},{4,0},{8,12},{12,8},{16,20},{20,16},{24,28},{28,24},{1,5},{5... | collective-permute-start | bytes 1179656 | tf_op jit(solution)/shard_map/ppermute | solution.py:372
  90.3 11.3 %collective-permute-start.19 = (bf16[768,256]{1,0:T(8,128)(2,1)S(1)}, bf16[768,256]{1,0:T(8,128)(2,1)S(1)}, u32[]{:S(2)}, u32[]{:S(2)}) collective-permute-start(bf16[768,256]{1,0:T(8,128)(2,1)S(1)} %collective-permute-done.17.near_ref), channel_id=1, source_target_pairs={{0,8},{4,28},{8,16},{12,4},{16,24},{20,12},{24,0},{28,20},{1,9},{5... | collective-permute-start | bytes 1179656 | tf_op jit(solution)/shard_map/ppermute | solution.py:334
  92.4 13.9 %collective-permute-start.22 = (bf16[768,256]{1,0:T(8,128)(2,1)S(1)}, bf16[768,256]{1,0:T(8,128)(2,1)S(1)}, u32[]{:S(2)}, u32[]{:S(2)}) collective-permute-start(bf16[768,256]{1,0:T(8,128)(2,1)S(1)} %product_1.7.field_ref), channel_id=1, source_target_pairs={{0,4},{4,0},{8,12},{12,8},{16,20},{20,16},{24,28},{28,24},{1,5},{5... | collective-permute-start | bytes 1179656 | tf_op jit(solution)/shard_map/ppermute | solution.py:372
  98.7 11.4 %collective-permute-start.21 = (bf16[768,256]{1,0:T(8,128)(2,1)S(1)}, bf16[768,256]{1,0:T(8,128)(2,1)S(1)}, u32[]{:S(2)}, u32[]{:S(2)}) collective-permute-start(bf16[768,256]{1,0:T(8,128)(2,1)S(1)} %collective-permute-done.20.near_ref), channel_id=1, source_target_pairs={{0,8},{4,28},{8,16},{12,4},{16,24},{20,12},{24,0},{28,20},{1,9},{5... | collective-permute-start | bytes 1179656 | tf_op jit(solution)/shard_map/ppermute | solution.py:334
  106.3 12.2 %collective-permute-start.24 = (bf16[768,256]{1,0:T(8,128)(2,1)S(1)}, bf16[768,256]{1,0:T(8,128)(2,1)}, u32[]{:S(2)}, u32[]{:S(2)}) collective-permute-start(bf16[768,256]{1,0:T(8,128)(2,1)S(1)} %get-tuple-element.344.refs_0_), channel_id=1, source_target_pairs={{0,2},{1,3},{2,0},{3,1},{4,6},{5,7},{6,4},{7,5},{8,10},{9,11},{10,... | collective-permute-start | bytes 1179656 | tf_op jit(solution)/shard_map/ppermute | solution.py:307
  108.0 11.6 %collective-permute-start.23 = (bf16[768,256]{1,0:T(8,128)(2,1)S(1)}, bf16[768,256]{1,0:T(8,128)(2,1)S(1)}, u32[]{:S(2)}, u32[]{:S(2)}) collective-permute-start(bf16[768,256]{1,0:T(8,128)(2,1)S(1)} %collective-permute-done.22.near_ref), channel_id=1, source_target_pairs={{0,8},{4,28},{8,16},{12,4},{16,24},{20,12},{24,0},{28,20},{1,9},{5... | collective-permute-start | bytes 1179656 | tf_op jit(solution)/shard_map/ppermute | solution.py:334
  109.6 17.3 %collective-permute-start.26 = (bf16[768,256]{1,0:T(8,128)(2,1)S(1)}, bf16[768,256]{1,0:T(8,128)(2,1)}, u32[]{:S(2)}, u32[]{:S(2)}) collective-permute-start(bf16[768,256]{1,0:T(8,128)(2,1)S(1)} %get-tuple-element.345.refs_1_), channel_id=1, source_target_pairs={{0,2},{1,3},{2,0},{3,1},{4,6},{5,7},{6,4},{7,5},{8,10},{9,11},{10,... | collective-permute-start | bytes 1179656 | tf_op jit(solution)/shard_map/ppermute | solution.py:307
  112.8 20.8 %collective-permute-start.25 = (bf16[768,256]{1,0:T(8,128)(2,1)}, bf16[768,256]{1,0:T(8,128)(2,1)}, u32[]{:S(2)}, u32[]{:S(2)}) collective-permute-start(bf16[768,256]{1,0:T(8,128)(2,1)} %get-tuple-element.346.refs_2_), channel_id=1, source_target_pairs={{0,2},{1,3},{2,0},{3,1},{4,6},{5,7},{6,4},{7,5},{8,10},{9,11},{10,... | collective-permute-start | bytes 1179656 | tf_op jit(solution)/shard_map/ppermute | solution.py:307
  138.0 3.5 %collective-permute-start.31 = (bf16[784,1024]{1,0:T(8,128)(2,1)S(1)}, bf16[784,1024]{1,0:T(8,128)(2,1)S(1)}, u32[]{:S(2)}, u32[]{:S(2)}) collective-permute-start(bf16[784,1024]{1,0:T(8,128)(2,1)S(1)} %get-tuple-element.352.refs_0_.refs_1_.refs_7_), channel_id=1, source_target_pairs={{0,1},{1,0},{2,3},{3,2},{4,5},{5,4},{6,7},{7,6},{8,9},{9,8},{10,11... | collective-permute-start | bytes 4816904 | tf_op jit(solution)/shard_map/ppermute | solution.py:307
  138.0 20.3 %collective-permute-start.33 = (bf16[384,1024]{1,0:T(8,128)(2,1)}, bf16[384,1024]{1,0:T(8,128)(2,1)}, u32[]{:S(2)}, u32[]{:S(2)}) collective-permute-start(bf16[384,1024]{1,0:T(8,128)(2,1)} %get-tuple-element.364), channel_id=1, source_target_pairs={{0,8},{4,12},{8,0},{12,4},{16,24},{20,28},{24,16},{28,20},{1,9},{5... | collective-permute-start | bytes 2359304 | tf_op jit(solution)/shard_map/ppermute | solution.py:396
  139.6 11.7 %collective-permute-start.30 = (bf16[784,256]{1,0:T(8,128)(2,1)}, bf16[784,256]{1,0:T(8,128)(2,1)}, u32[]{:S(2)}, u32[]{:S(2)}) collective-permute-start(bf16[784,256]{1,0:T(8,128)(2,1)} %product_2.7.refs_3_), channel_id=1, source_target_pairs={{0,2},{1,3},{2,0},{3,1},{4,6},{5,7},{6,4},{7,5},{8,10},{9,11},{10,... | collective-permute-start | bytes 1204232 | tf_op jit(solution)/shard_map/ppermute | solution.py:307
  141.0 13.7 %collective-permute-start.28 = (bf16[768,256]{1,0:T(8,128)(2,1)}, bf16[768,256]{1,0:T(8,128)(2,1)}, u32[]{:S(2)}, u32[]{:S(2)}) collective-permute-start(bf16[768,256]{1,0:T(8,128)(2,1)} %collective-permute-done.26.refs_2_), channel_id=1, source_target_pairs={{0,1},{1,0},{2,3},{3,2},{4,5},{5,4},{6,7},{7,6},{8,9},{9,8},{10,11... | collective-permute-start | bytes 1179656 | tf_op jit(solution)/shard_map/ppermute | solution.py:307
  151.3 9.8 %collective-permute-start.32 = (bf16[784,256]{1,0:T(8,128)(2,1)}, bf16[784,256]{1,0:T(8,128)(2,1)S(1)}, u32[]{:S(2)}, u32[]{:S(2)}) collective-permute-start(bf16[784,256]{1,0:T(8,128)(2,1)} %collective-permute-done.30.refs_4_.refs_6_), channel_id=1, source_target_pairs={{0,1},{1,0},{2,3},{3,2},{4,5},{5,4},{6,7},{7,6},{8,9},{9,8},{10,11... | collective-permute-start | bytes 1204232 | tf_op jit(solution)/shard_map/ppermute | solution.py:307
  151.3 9.8 %collective-permute-start.27 = (bf16[768,256]{1,0:T(8,128)(2,1)}, bf16[768,256]{1,0:T(8,128)(2,1)S(1)}, u32[]{:S(2)}, u32[]{:S(2)}) collective-permute-start(bf16[768,256]{1,0:T(8,128)(2,1)} %collective-permute-done.24.refs_1_), channel_id=1, source_target_pairs={{0,1},{1,0},{2,3},{3,2},{4,5},{5,4},{6,7},{7,6},{8,9},{9,8},{10,11... | collective-permute-start | bytes 1179656 | tf_op jit(solution)/shard_map/ppermute | solution.py:307
  151.8 9.3 %collective-permute-start.29 = (bf16[768,256]{1,0:T(8,128)(2,1)}, bf16[768,256]{1,0:T(8,128)(2,1)S(1)}, u32[]{:S(2)}, u32[]{:S(2)}) collective-permute-start(bf16[768,256]{1,0:T(8,128)(2,1)} %collective-permute-done.25.refs_3_), channel_id=1, source_target_pairs={{0,1},{1,0},{2,3},{3,2},{4,5},{5,4},{6,7},{7,6},{8,9},{9,8},{10,11... | collective-permute-start | bytes 1179656 | tf_op jit(solution)/shard_map/ppermute | solution.py:307
  151.8 8.0 %copy-start.1 = (bf16[384,1024]{1,0:T(8,128)(2,1)S(1)}, bf16[384,1024]{1,0:T(8,128)(2,1)}, u32[]{:S(2)}) copy-start(bf16[384,1024]{1,0:T(8,128)(2,1)} %copy-done) | copy-start | bytes 2359300
  154.7 14.8 %collective-permute-start.35 = (bf16[256,1024]{1,0:T(8,128)(2,1)S(1)}, bf16[256,1024]{1,0:T(8,128)(2,1)S(1)}, u32[]{:S(2)}, u32[]{:S(2)}) collective-permute-start(bf16[256,1024]{1,0:T(8,128)(2,1)S(1)} %get-tuple-element.389), channel_id=1, source_target_pairs={{0,4},{4,0},{8,12},{12,8},{16,20},{20,16},{24,28},{28,24},{1,5},{5... | collective-permute-start | bytes 1572872 | tf_op jit(solution)/shard_map/ppermute | solution.py:396
  158.3 13.6 %collective-permute-start.38 = (bf16[256,1024]{1,0:T(8,128)(2,1)S(1)}, bf16[256,1024]{1,0:T(8,128)(2,1)S(1)}, u32[]{:S(2)}, u32[]{:S(2)}) collective-permute-start(bf16[256,1024]{1,0:T(8,128)(2,1)S(1)} %get-tuple-element.396), channel_id=1, source_target_pairs={{0,8},{4,12},{8,0},{12,4},{16,24},{20,28},{24,16},{28,20},{1,9},{5... | collective-permute-start | bytes 1572872 | tf_op jit(solution)/shard_map/ppermute | solution.py:396
  163.6 27.8 %collective-permute-start.34 = (bf16[272,1024]{1,0:T(8,128)(2,1)S(1)}, bf16[272,1024]{1,0:T(8,128)(2,1)S(1)}, u32[]{:S(2)}, u32[]{:S(2)}) collective-permute-start(bf16[272,1024]{1,0:T(8,128)(2,1)S(1)} %get-tuple-element.387), channel_id=1, source_target_pairs={{0,4},{4,0},{8,12},{12,8},{16,20},{20,16},{24,28},{28,24},{1,5},{5... | collective-permute-start | bytes 1671176 | tf_op jit(solution)/shard_map/ppermute | solution.py:396
  165.1 24.4 %collective-permute-start.37 = (bf16[192,1024]{1,0:T(8,128)(2,1)S(1)}, bf16[192,1024]{1,0:T(8,128)(2,1)S(1)}, u32[]{:S(2)}, u32[]{:S(2)}) collective-permute-start(bf16[192,1024]{1,0:T(8,128)(2,1)S(1)} %sum_hop.8), channel_id=1, source_target_pairs={{0,4},{4,0},{8,12},{12,8},{16,20},{20,16},{24,28},{28,24},{1,5},{5... | collective-permute-start | bytes 1179656 | tf_op jit(solution)/shard_map/ppermute | solution.py:396
  170.1 20.6 %collective-permute-start.36 = (bf16[128,1024]{1,0:T(8,128)(2,1)S(1)}, bf16[128,1024]{1,0:T(8,128)(2,1)S(1)}, u32[]{:S(2)}, u32[]{:S(2)}) collective-permute-start(bf16[128,1024]{1,0:T(8,128)(2,1)S(1)} %sum_hop.9), channel_id=1, source_target_pairs={{0,8},{4,12},{8,0},{12,4},{16,24},{20,28},{24,16},{28,20},{1,9},{5... | collective-permute-start | bytes 786440 | tf_op jit(solution)/shard_map/ppermute | solution.py:396
  172.5 22.6 %collective-permute-start.40 = (bf16[128,1024]{1,0:T(8,128)(2,1)S(1)}, bf16[128,1024]{1,0:T(8,128)(2,1)S(1)}, u32[]{:S(2)}, u32[]{:S(2)}) collective-permute-start(bf16[128,1024]{1,0:T(8,128)(2,1)S(1)} %sum_hop.10), channel_id=1, source_target_pairs={{0,16},{4,20},{8,24},{12,28},{16,0},{20,4},{24,8},{28,12},{1,17},{... | collective-permute-start | bytes 786440 | tf_op jit(solution)/shard_map/ppermute | solution.py:396
  192.0 12.9 %collective-permute-start.39 = (bf16[144,1024]{1,0:T(8,128)(2,1)S(1)}, bf16[144,1024]{1,0:T(8,128)(2,1)S(1)}, u32[]{:S(2)}, u32[]{:S(2)}) collective-permute-start(bf16[144,1024]{1,0:T(8,128)(2,1)S(1)} %sum_hop.13), channel_id=1, source_target_pairs={{0,8},{4,12},{8,0},{12,4},{16,24},{20,28},{24,16},{28,20},{1,9},{5... | collective-permute-start | bytes 884744 | tf_op jit(solution)/shard_map/ppermute | solution.py:396
  192.6 10.4 %collective-permute-start.42 = (bf16[96,1024]{1,0:T(8,128)(2,1)S(1)}, bf16[96,1024]{1,0:T(8,128)(2,1)S(1)}, u32[]{:S(2)}, u32[]{:S(2)}) collective-permute-start(bf16[96,1024]{1,0:T(8,128)(2,1)S(1)} %sum_hop.11), channel_id=1, source_target_pairs={{0,16},{4,20},{8,24},{12,28},{16,0},{20,4},{24,8},{28,12},{1,17},{... | collective-permute-start | bytes 589832 | tf_op jit(solution)/shard_map/ppermute | solution.py:396
  195.7 7.3 %collective-permute-start.41 = (bf16[64,1024]{1,0:T(8,128)(2,1)S(1)}, bf16[64,1024]{1,0:T(8,128)(2,1)S(1)}, u32[]{:S(2)}, u32[]{:S(2)}) collective-permute-start(bf16[64,1024]{1,0:T(8,128)(2,1)S(1)} %sum_hop.14), channel_id=1, source_target_pairs={{0,4},{4,0},{8,12},{12,8},{16,20},{20,16},{24,28},{28,24},{1,5},{5... | collective-permute-start | bytes 393224 | tf_op jit(solution)/shard_map/ppermute | solution.py:396
  205.6 15.0 %collective-permute-start.43 = (bf16[80,1024]{1,0:T(8,128)(2,1)S(1)}, bf16[80,1024]{1,0:T(8,128)(2,1)S(1)}, u32[]{:S(2)}, u32[]{:S(2)}) collective-permute-start(bf16[80,1024]{1,0:T(8,128)(2,1)S(1)} %sum_hop.15), channel_id=1, source_target_pairs={{0,16},{4,20},{8,24},{12,28},{16,0},{20,4},{24,8},{28,12},{1,17},{... | collective-permute-start | bytes 491528 | tf_op jit(solution)/shard_map/ppermute | solution.py:396
  207.2 13.4 %collective-permute-start.44 = (bf16[64,1024]{1,0:T(8,128)(2,1)S(1)}, bf16[64,1024]{1,0:T(8,128)(2,1)S(1)}, u32[]{:S(2)}, u32[]{:S(2)}) collective-permute-start(bf16[64,1024]{1,0:T(8,128)(2,1)S(1)} %sum_hop.12), channel_id=1, source_target_pairs={{0,16},{4,20},{8,24},{12,28},{16,0},{20,4},{24,8},{28,12},{1,17},{... | collective-permute-start | bytes 393224 | tf_op jit(solution)/shard_map/ppermute | solution.py:396
  222.0 6.7 %collective-permute-start.45 = (bf16[64,1024]{1,0:T(8,128)(2,1)S(1)}, bf16[64,1024]{1,0:T(8,128)(2,1)S(1)}, u32[]{:S(2)}, u32[]{:S(2)}) collective-permute-start(bf16[64,1024]{1,0:T(8,128)(2,1)S(1)} %sum_last.5), channel_id=1, source_target_pairs={{0,4},{4,0},{8,12},{12,8},{16,20},{20,16},{24,28},{28,24},{1,5},{5... | collective-permute-start | bytes 393224 | tf_op jit(solution)/shard_map/ppermute | solution.py:396
  223.7 15.5 %collective-permute-start.48 = (bf16[64,1024]{1,0:T(8,128)(2,1)S(1)}, bf16[64,1024]{1,0:T(8,128)(2,1)S(1)}, u32[]{:S(2)}, u32[]{:S(2)}) collective-permute-start(bf16[64,1024]{1,0:T(8,128)(2,1)S(1)} %get-tuple-element.442), channel_id=1, source_target_pairs={{0,16},{4,20},{8,24},{12,28},{16,0},{20,4},{24,8},{28,12},{1,17},{... | collective-permute-start | bytes 393224 | tf_op jit(solution)/shard_map/ppermute | solution.py:396
  225.7 16.3 %collective-permute-start.47 = (bf16[64,1024]{1,0:T(8,128)(2,1)S(1)}, bf16[64,1024]{1,0:T(8,128)(2,1)S(1)}, u32[]{:S(2)}, u32[]{:S(2)}) collective-permute-start(bf16[64,1024]{1,0:T(8,128)(2,1)S(1)} %sum_last.7), channel_id=1, source_target_pairs={{0,16},{4,20},{8,24},{12,28},{16,0},{20,4},{24,8},{28,12},{1,17},{... | collective-permute-start | bytes 393224 | tf_op jit(solution)/shard_map/ppermute | solution.py:396
  228.7 23.2 %collective-permute-start.51 = (bf16[96,1024]{1,0:T(8,128)(2,1)S(1)}, bf16[96,1024]{1,0:T(8,128)(2,1)S(1)}, u32[]{:S(2)}, u32[]{:S(2)}) collective-permute-start(bf16[96,1024]{1,0:T(8,128)(2,1)S(1)} %sum_last.6), channel_id=1, source_target_pairs={{0,16},{4,20},{8,24},{12,28},{16,0},{20,4},{24,8},{28,12},{1,17},{... | collective-permute-start | bytes 589832 | tf_op jit(solution)/shard_map/ppermute | solution.py:396
  239.2 16.9 %collective-permute-start.46 = (bf16[128,1024]{1,0:T(8,128)(2,1)S(1)}, bf16[128,1024]{1,0:T(8,128)(2,1)S(1)}, u32[]{:S(2)}, u32[]{:S(2)}) collective-permute-start(bf16[128,1024]{1,0:T(8,128)(2,1)S(1)} %pad_maximum_fusion.5), channel_id=1, source_target_pairs={{0,16},{4,20},{8,24},{12,28},{16,0},{20,4},{24,8},{28,12},{1,17},{... | collective-permute-start | bytes 786440 | tf_op jit(solution)/shard_map/ppermute | solution.py:396
  242.0 17.4 %collective-permute-start.50 = (bf16[128,1024]{1,0:T(8,128)(2,1)S(1)}, bf16[128,1024]{1,0:T(8,128)(2,1)S(1)}, u32[]{:S(2)}, u32[]{:S(2)}) collective-permute-start(bf16[128,1024]{1,0:T(8,128)(2,1)S(1)} %pad_maximum_fusion.6), channel_id=1, source_target_pairs={{0,8},{4,12},{8,0},{12,4},{16,24},{20,28},{24,16},{28,20},{1,9},{5... | collective-permute-start | bytes 786440 | tf_op jit(solution)/shard_map/ppermute | solution.py:396
  252.0 15.2 %collective-permute-start.58 = (bf16[192,1024]{1,0:T(8,128)(2,1)S(1)}, bf16[192,1024]{1,0:T(8,128)(2,1)S(1)}, u32[]{:S(2)}, u32[]{:S(2)}) collective-permute-start(bf16[192,1024]{1,0:T(8,128)(2,1)S(1)} %pad_maximum_fusion.4), channel_id=1, source_target_pairs={{0,4},{4,0},{8,12},{12,8},{16,20},{20,16},{24,28},{28,24},{1,5},{5... | collective-permute-start | bytes 1179656 | tf_op jit(solution)/shard_map/ppermute | solution.py:396
  252.5 12.5 %collective-permute-start.49 = (bf16[128,1024]{1,0:T(8,128)(2,1)S(1)}, bf16[128,1024]{1,0:T(8,128)(2,1)S(1)}, u32[]{:S(2)}, u32[]{:S(2)}) collective-permute-start(bf16[128,1024]{1,0:T(8,128)(2,1)S(1)} %pad_maximum_fusion.7), channel_id=1, source_target_pairs={{0,8},{4,12},{8,0},{12,4},{16,24},{20,28},{24,16},{28,20},{1,9},{5... | collective-permute-start | bytes 786440 | tf_op jit(solution)/shard_map/ppermute | solution.py:396
  256.1 19.4 %collective-permute-start.52 = (bf16[256,1024]{1,0:T(8,128)(2,1)S(1)}, bf16[256,1024]{1,0:T(8,128)(2,1)S(1)}, u32[]{:S(2)}, u32[]{:S(2)}) collective-permute-start(bf16[256,1024]{1,0:T(8,128)(2,1)S(1)} %pad_maximum_fusion.1.refs_1_), channel_id=1, source_target_pairs={{0,8},{4,12},{8,0},{12,4},{16,24},{20,28},{24,16},{28,20},{1,9},{5... | collective-permute-start | bytes 1572872 | tf_op jit(solution)/shard_map/ppermute | solution.py:396
  265.0 14.9 %collective-permute-start.55 = (bf16[256,1024]{1,0:T(8,128)(2,1)S(1)}, bf16[256,1024]{1,0:T(8,128)(2,1)S(1)}, u32[]{:S(2)}, u32[]{:S(2)}) collective-permute-start(bf16[256,1024]{1,0:T(8,128)(2,1)S(1)} %pad_maximum_fusion.2.refs_2_), channel_id=1, source_target_pairs={{0,4},{4,0},{8,12},{12,8},{16,20},{20,16},{24,28},{28,24},{1,5},{5... | collective-permute-start | bytes 1572872 | tf_op jit(solution)/shard_map/ppermute | solution.py:396
  265.5 23.2 %collective-permute-start.60 = (bf16[256,1024]{1,0:T(8,128)(2,1)S(1)}, bf16[256,1024]{1,0:T(8,128)(2,1)S(1)}, u32[]{:S(2)}, u32[]{:S(2)}) collective-permute-start(bf16[256,1024]{1,0:T(8,128)(2,1)S(1)} %pad_maximum_fusion.3.refs_3_), channel_id=1, source_target_pairs={{0,4},{4,0},{8,12},{12,8},{16,20},{20,16},{24,28},{28,24},{1,5},{5... | collective-permute-start | bytes 1572872 | tf_op jit(solution)/shard_map/ppermute | solution.py:396
  267.1 21.6 %collective-permute-start.53 = (bf16[256,1024]{1,0:T(8,128)(2,1)S(1)}, bf16[256,1024]{1,0:T(8,128)(2,1)S(1)}, u32[]{:S(2)}, u32[]{:S(2)}) collective-permute-start(bf16[256,1024]{1,0:T(8,128)(2,1)S(1)} %pad_maximum_fusion.1.refs_1_), channel_id=1, source_target_pairs={{0,1},{1,0},{2,3},{3,2},{4,5},{5,4},{6,7},{7,6},{8,9},{9,8},{10,11... | collective-permute-start | bytes 1572872 | tf_op jit(solution)/shard_map/ppermute | solution.py:307
  267.1 23.1 %collective-permute-start.56 = (bf16[256,1024]{1,0:T(8,128)(2,1)S(1)}, bf16[256,1024]{1,0:T(8,128)(2,1)S(1)}, u32[]{:S(2)}, u32[]{:S(2)}) collective-permute-start(bf16[256,1024]{1,0:T(8,128)(2,1)S(1)} %pad_maximum_fusion.2.refs_2_), channel_id=1, source_target_pairs={{0,3},{1,2},{2,1},{3,0},{4,7},{5,6},{6,5},{7,4},{8,11},{9,10},{10,... | collective-permute-start | bytes 1572872 | tf_op jit(solution)/shard_map/ppermute | solution.py:307
  275.5 18.8 %collective-permute-start.59 = (bf16[384,1024]{1,0:T(8,128)(2,1)S(1)}, bf16[384,1024]{1,0:T(8,128)(2,1)S(1)}, u32[]{:S(2)}, u32[]{:S(2)}) collective-permute-start(bf16[384,1024]{1,0:T(8,128)(2,1)S(1)} %pad_maximum_fusion.refs_2_), channel_id=1, source_target_pairs={{0,8},{4,12},{8,0},{12,4},{16,24},{20,28},{24,16},{28,20},{1,9},{5... | collective-permute-start | bytes 2359304 | tf_op jit(solution)/shard_map/ppermute | solution.py:396
  279.9 10.9 %collective-permute-start.54 = (bf16[256,1024]{1,0:T(8,128)(2,1)S(1)}, bf16[256,1024]{1,0:T(8,128)(2,1)S(1)}, u32[]{:S(2)}, u32[]{:S(2)}) collective-permute-start(bf16[256,1024]{1,0:T(8,128)(2,1)S(1)} %collective-permute-done.52.refs_2_), channel_id=1, source_target_pairs={{0,1},{1,0},{2,3},{3,2},{4,5},{5,4},{6,7},{7,6},{8,9},{9,8},{10,11... | collective-permute-start | bytes 1572872 | tf_op jit(solution)/shard_map/ppermute | solution.py:307
  288.7 14.2 %collective-permute-start.57 = (bf16[256,1024]{1,0:T(8,128)(2,1)S(1)}, bf16[256,1024]{1,0:T(8,128)(2,1)S(1)}, u32[]{:S(2)}, u32[]{:S(2)}) collective-permute-start(bf16[256,1024]{1,0:T(8,128)(2,1)S(1)} %collective-permute-done.55.refs_3_), channel_id=1, source_target_pairs={{0,3},{1,2},{2,1},{3,0},{4,7},{5,6},{6,5},{7,4},{8,11},{9,10},{10,... | collective-permute-start | bytes 1572872 | tf_op jit(solution)/shard_map/ppermute | solution.py:307
  288.7 25.5 %collective-permute-start.61 = (bf16[256,1024]{1,0:T(8,128)(2,1)S(1)}, bf16[256,1024]{1,0:T(8,128)(2,1)S(1)}, u32[]{:S(2)}, u32[]{:S(2)}) collective-permute-start(bf16[256,1024]{1,0:T(8,128)(2,1)S(1)} %pad_maximum_fusion.3.refs_3_), channel_id=1, source_target_pairs={{0,2},{1,3},{2,0},{3,1},{4,6},{5,7},{6,4},{7,5},{8,10},{9,11},{10,... | collective-permute-start | bytes 1572872 | tf_op jit(solution)/shard_map/ppermute | solution.py:307
  290.3 35.2 %collective-permute-start.62 = (bf16[256,1024]{1,0:T(8,128)(2,1)S(1)}, bf16[256,1024]{1,0:T(8,128)(2,1)S(1)}, u32[]{:S(2)}, u32[]{:S(2)}) collective-permute-start(bf16[256,1024]{1,0:T(8,128)(2,1)S(1)} %collective-permute-done.60.refs_4_), channel_id=1, source_target_pairs={{0,2},{1,3},{2,0},{3,1},{4,6},{5,7},{6,4},{7,5},{8,10},{9,11},{10,... | collective-permute-start | bytes 1572872 | tf_op jit(solution)/shard_map/ppermute | solution.py:307
  (4 other events, 6.7 us)

commit v11 on v9

--- a/solution.py
+++ b/solution.py
@@ -399,11 +399,10 @@
         return to_group(value, d), clock.transfer(value, "core" if d == 1 else "x")
 
     def panel_process():
-        yield 4.0
+        yield 10.5
         for c in range(CHUNKS - 1):
             more_panel(c)
-            settle(c)
-        yield 10.5
+            settle(c, lambda d: not d & (d - 1))
         more_panel(CHUNKS - 1)
         settle(CHUNKS - 1, lambda d: not d & (d - 1))
         clock.spend(1.3)
@@ -488,7 +487,7 @@
         elif d:
             yield peer_arrival - 3.0
             peer = order(peer)
-            yield arrival
+            yield arrival + (6.0 if d == 1 else 0.0)
             far = order(far)
         else:
             yield arrival
@@ -498,6 +497,9 @@
             if not round_y:
                 peer_far, peer_arrival = over_groups(far, d)
             yield peer_arrival
+        while mixes < turn[d]:
+            yield clock.now + 0.5
+        if d:
             peer_far = order(peer_far)
             parts += (peer, peer_far)
         first, last = mixes == 0, mixes == groups - 1
@@ -517,6 +519,7 @@
     y_first, z_then_y, y_then_far = (1, *z_masks), (*z_masks[:1], 1, *z_masks[1:]), (1, *z_masks[::-1])
     there[1] = 25.0
     queue = sorted(range(1, groups), key=lambda d: (d == 1, d))
+    turn = {d: place for place, d in enumerate(sorted(range(groups), key=lambda d: (d != 1, d)))}
     carrier = queue[min(1, len(queue) - 1)]
     processes = [panel_process()]
     for d in queue:

time: 301 us -> 288 us (0.957)
  waiting for transfers between devices: 130 us -> 118 us
  starting transfers between devices: 109 us -> 103 us
    ppermute x25, waiting for transfers between devices: 79 us -> 70.6 us  [over_tiles(): sent = lax.ppermute(value, 'elem', [(i, i ^ mask) for i in range(tiles)])]
    ppermute x25, starting transfers between devices: 36.2 us -> 31.5 us  [over_tiles(): sent = lax.ppermute(value, 'elem', [(i, i ^ mask) for i in range(tiles)])]
    ppermute x12, waiting for transfers between devices: 6.98 us -> 3.18 us  [send_on(): far[job] = lax.ppermute(near[job], 'elem', outward)]
    unnamed x49 -> x41, local copies, waits for them, and re-layouts: 7.66 us -> 9.63 us
  transfers between devices with their start and end apart: 66 -> 66, of which waited for: 34 -> 32; matrix products, arithmetic and copies ran while one was open for 2% -> 2% of each run, Pallas kernels for 12% -> 14%
where the time goes in v11:
time: 288 us
  waiting for transfers between devices  118 us (41%)
  starting transfers between devices  103 us (36%)
  Pallas kernels  47.5 us (16%)
  local copies, waits for them, and re-layouts  15.7 us (5%)
    ppermute x25, waiting for transfers between devices, over_tiles(): sent = lax.ppermute(value, 'elem', [(i, i ^ mask) for i in range(tiles)])  70.6 us
    pallas_call x32, Pallas kernels, call(): pl.pallas_call(kernel, out_shape=outs, in_specs=[pl.BlockSpec(memory_spac...  47.5 us
    ppermute x25, starting transfers between devices, over_tiles(): sent = lax.ppermute(value, 'elem', [(i, i ^ mask) for i in range(tiles)])  31.5 us
    ppermute x8, starting transfers between devices, multiply(): near[stage + 1, c] = lax.ppermute(out, 'elem', swap)  28.4 us
    ppermute x12, starting transfers between devices, send_on(): far[job] = lax.ppermute(near[job], 'elem', outward)  25.1 us
    ppermute x17, waiting for transfers between devices, to_group(): return lax.ppermute(value, 'orb', [(i, i ^ d) for i in range(groups)])  23.4 us
    ppermute x8, waiting for transfers between devices, multiply(): near[stage + 1, c] = lax.ppermute(out, 'elem', swap)  11.4 us
    unnamed x41, local copies, waits for them, and re-layouts  9.63 us
  transfers between devices with their start and end apart: 66, of which 32 were waited for; matrix products, arithmetic and copies ran while one was open for 2% of the time, Pallas kernels for 14%

profile of v11, /device:TPU:0, one launch (start us, length us, event | category | flops | bytes accessed | tf_op | source)
XLA Modules:
  0.0 287.5 jit_solution(13147627261616702790)
XLA Ops:
  1.5 3.0 %collective-permute-start = (bf16[768,256]{1,0:T(8,128)(2,1)S(1)}, bf16[768,256]{1,0:T(8,128)(2,1)S(1)}, u32[]{:S(2)}, u32[]{:S(2)}) collective-permute-start(bf16[768,256]{1,0:T(8,128)(2,1)S(1)} %get-tuple-element.501.field_ref.refs_0_), channel_id=1, source_target_pairs={{0,4},{4,0},{8,12},{12,8},{16,20},{20,16},{24,28},{28,24},{1,5},{5... | collective-permute-start | bytes 1179656 | tf_op jit(solution)/shard_map/ppermute | solution.py:311
  4.5 2.2 slice_bitcast_fusion
  8.1 2.3 concatenate.30.blocks_ref
  10.5 3.9 %collective-permute-done.near_ref = bf16[768,256]{1,0:T(8,128)(2,1)S(1)} collective-permute-done((bf16[768,256]{1,0:T(8,128)(2,1)S(1)}, bf16[768,256]{1,0:T(8,128)(2,1)S(1)}, u32[]{:S(2)}, u32[]{:S(2)}) %collective-permute-start) | collective-permute-done | bytes 393248 | tf_op jit(solution)/shard_map/ppermute | solution.py:311
  14.5 2.1 collective-permute-start.1
  16.6 3.5 %collective-permute-start.4 = (bf16[768,256]{1,0:T(8,128)(2,1)S(1)}, bf16[768,256]{1,0:T(8,128)(2,1)S(1)}, u32[]{:S(2)}, u32[]{:S(2)}) collective-permute-start(bf16[768,256]{1,0:T(8,128)(2,1)S(1)} %get-tuple-element.267.field_ref.refs_0_), channel_id=1, source_target_pairs={{0,4},{4,0},{8,12},{12,8},{16,20},{20,16},{24,28},{28,24},{1,5},{5... | collective-permute-start | bytes 1179656 | tf_op jit(solution)/shard_map/ppermute | solution.py:316
  20.1 2.8 collective-permute-done.2.near_ref
  22.9 2.1 collective-permute-start.7
  25.0 3.5 %collective-permute-start.6 = (bf16[768,256]{1,0:T(8,128)(2,1)S(1)}, bf16[768,256]{1,0:T(8,128)(2,1)S(1)}, u32[]{:S(2)}, u32[]{:S(2)}) collective-permute-start(bf16[768,256]{1,0:T(8,128)(2,1)S(1)} %get-tuple-element.270.field_ref.refs_0_), channel_id=1, source_target_pairs={{0,4},{4,0},{8,12},{12,8},{16,20},{20,16},{24,28},{28,24},{1,5},{5... | collective-permute-start | bytes 1179656 | tf_op jit(solution)/shard_map/ppermute | solution.py:316
  31.3 2.1 collective-permute-start.5
  33.4 3.5 %collective-permute-start.3 = (bf16[768,256]{1,0:T(8,128)(2,1)S(1)}, bf16[768,256]{1,0:T(8,128)(2,1)S(1)}, u32[]{:S(2)}, u32[]{:S(2)}) collective-permute-start(bf16[768,256]{1,0:T(8,128)(2,1)S(1)} %get-tuple-element.266.field_ref), channel_id=1, source_target_pairs={{0,4},{4,0},{8,12},{12,8},{16,20},{20,16},{24,28},{28,24},{1,5},{5... | collective-permute-start | bytes 1179656 | tf_op jit(solution)/shard_map/ppermute | solution.py:365
  39.7 2.1 collective-permute-start.10
  41.9 3.5 %collective-permute-start.9 = (bf16[768,256]{1,0:T(8,128)(2,1)S(1)}, bf16[768,256]{1,0:T(8,128)(2,1)S(1)}, u32[]{:S(2)}, u32[]{:S(2)}) collective-permute-start(bf16[768,256]{1,0:T(8,128)(2,1)S(1)} %get-tuple-element.285.field_ref), channel_id=1, source_target_pairs={{0,4},{4,0},{8,12},{12,8},{16,20},{20,16},{24,28},{28,24},{1,5},{5... | collective-permute-start | bytes 1179656 | tf_op jit(solution)/shard_map/ppermute | solution.py:365
  48.2 2.1 collective-permute-start.8
  50.3 3.5 %collective-permute-start.12 = (bf16[768,256]{1,0:T(8,128)(2,1)S(1)}, bf16[768,256]{1,0:T(8,128)(2,1)S(1)}, u32[]{:S(2)}, u32[]{:S(2)}) collective-permute-start(bf16[768,256]{1,0:T(8,128)(2,1)S(1)} %get-tuple-element.297.field_ref), channel_id=1, source_target_pairs={{0,4},{4,0},{8,12},{12,8},{16,20},{20,16},{24,28},{28,24},{1,5},{5... | collective-permute-start | bytes 1179656 | tf_op jit(solution)/shard_map/ppermute | solution.py:365
  56.6 2.1 collective-permute-start.15
  58.7 3.5 %collective-permute-start.14 = (bf16[768,256]{1,0:T(8,128)(2,1)S(1)}, bf16[768,256]{1,0:T(8,128)(2,1)S(1)}, u32[]{:S(2)}, u32[]{:S(2)}) collective-permute-start(bf16[768,256]{1,0:T(8,128)(2,1)S(1)} %get-tuple-element.300.field_ref), channel_id=1, source_target_pairs={{0,4},{4,0},{8,12},{12,8},{16,20},{20,16},{24,28},{28,24},{1,5},{5... | collective-permute-start | bytes 1179656 | tf_op jit(solution)/shard_map/ppermute | solution.py:365
  65.0 2.1 collective-permute-start.13
  67.1 3.5 %collective-permute-start.11 = (bf16[768,256]{1,0:T(8,128)(2,1)S(1)}, bf16[768,256]{1,0:T(8,128)(2,1)S(1)}, u32[]{:S(2)}, u32[]{:S(2)}) collective-permute-start(bf16[768,256]{1,0:T(8,128)(2,1)S(1)} %product_1.4.field_ref), channel_id=1, source_target_pairs={{0,4},{4,0},{8,12},{12,8},{16,20},{20,16},{24,28},{28,24},{1,5},{5... | collective-permute-start | bytes 1179656 | tf_op jit(solution)/shard_map/ppermute | solution.py:365
  73.4 2.1 collective-permute-start.18
  75.6 3.5 %collective-permute-start.17 = (bf16[768,256]{1,0:T(8,128)(2,1)S(1)}, bf16[768,256]{1,0:T(8,128)(2,1)S(1)}, u32[]{:S(2)}, u32[]{:S(2)}) collective-permute-start(bf16[768,256]{1,0:T(8,128)(2,1)S(1)} %product_1.5.field_ref), channel_id=1, source_target_pairs={{0,4},{4,0},{8,12},{12,8},{16,20},{20,16},{24,28},{28,24},{1,5},{5... | collective-permute-start | bytes 1179656 | tf_op jit(solution)/shard_map/ppermute | solution.py:365
  81.9 2.1 collective-permute-start.16
  84.0 3.5 %collective-permute-start.20 = (bf16[768,256]{1,0:T(8,128)(2,1)S(1)}, bf16[768,256]{1,0:T(8,128)(2,1)S(1)}, u32[]{:S(2)}, u32[]{:S(2)}) collective-permute-start(bf16[768,256]{1,0:T(8,128)(2,1)S(1)} %product_1.6.field_ref), channel_id=1, source_target_pairs={{0,4},{4,0},{8,12},{12,8},{16,20},{20,16},{24,28},{28,24},{1,5},{5... | collective-permute-start | bytes 1179656 | tf_op jit(solution)/shard_map/ppermute | solution.py:365
  90.3 2.1 collective-permute-start.19
  92.4 3.5 %collective-permute-start.22 = (bf16[768,256]{1,0:T(8,128)(2,1)S(1)}, bf16[768,256]{1,0:T(8,128)(2,1)S(1)}, u32[]{:S(2)}, u32[]{:S(2)}) collective-permute-start(bf16[768,256]{1,0:T(8,128)(2,1)S(1)} %product_1.7.field_ref), channel_id=1, source_target_pairs={{0,4},{4,0},{8,12},{12,8},{16,20},{20,16},{24,28},{28,24},{1,5},{5... | collective-permute-start | bytes 1179656 | tf_op jit(solution)/shard_map/ppermute | solution.py:365
  98.7 2.1 collective-permute-start.21
  103.6 2.7 collective-permute-done.22.near_ref
  106.3 1.8 collective-permute-start.23
  115.9 2.8 collective-permute-done.23.far_ref
  122.6 3.0 %gram_own.1 = (bf16[384,1024]{1,0:T(8,128)(2,1)S(1)}, bf16[384,1024]{1,0:T(8,128)(2,1)}) custom-call(s32[2]{0:T(128)S(1)} %get-tuple-element.510.where_ref, bf16[768,256]{1,0:T(8,128)(2,1)S(1)} %get-tuple-element.323.refs_0_.refs_1_.refs_10_, bf16[768,256]{1,0:T(8,128)(2,1)S(1)} %get-tuple-element.334.refs_1_.refs_2_.refs_11_, ...), custom_call_target="tpu_custom_call" | custom-call | flops 1024 | bytes 5242880 | tf_op jit(solution)/shard_map/gram_own/pallas_call | solution.py:96
  125.6 1.9 collective-permute-start.35
  130.0 16.6 %collective-permute-done.29.refs_6_.refs_3_ = bf16[768,256]{1,0:T(8,128)(2,1)} collective-permute-done((bf16[768,256]{1,0:T(8,128)(2,1)S(1)}, bf16[768,256]{1,0:T(8,128)(2,1)}, u32[]{:S(2)}, u32[]{:S(2)}) %collective-permute-start.29) | collective-permute-done | bytes 393248 | tf_op jit(solution)/shard_map/ppermute | solution.py:298
  149.3 2.5 gram_pair.3
  152.8 2.5 gram_pair.4
  155.6 2.0 collective-permute-start.38
  157.6 2.1 gram_pair.5
  159.7 1.8 collective-permute-start.41
  161.5 10.9 %collective-permute-done.39.refs_1_ = bf16[256,1024]{1,0:T(8,128)(2,1)S(1)} collective-permute-done((bf16[256,1024]{1,0:T(8,128)(2,1)S(1)}, bf16[256,1024]{1,0:T(8,128)(2,1)S(1)}, u32[]{:S(2)}, u32[]{:S(2)}) %collective-permute-start.39) | collective-permute-done | bytes 524320 | tf_op jit(solution)/shard_map/ppermute | solution.py:392
  173.0 2.7 collective-permute-done.38.refs_2_
  177.2 2.1 collective-permute-start.40
  180.9 3.4 %collective-permute-done.42.refs_3_ = bf16[96,1024]{1,0:T(8,128)(2,1)S(1)} collective-permute-done((bf16[96,1024]{1,0:T(8,128)(2,1)S(1)}, bf16[96,1024]{1,0:T(8,128)(2,1)S(1)}, u32[]{:S(2)}, u32[]{:S(2)}) %collective-permute-start.42) | collective-permute-done | bytes 196640 | tf_op jit(solution)/shard_map/ppermute | solution.py:392
  185.0 5.6 %collective-permute-done.40.refs_2_ = bf16[144,1024]{1,0:T(8,128)(2,1)S(1)} collective-permute-done((bf16[144,1024]{1,0:T(8,128)(2,1)S(1)}, bf16[144,1024]{1,0:T(8,128)(2,1)S(1)}, u32[]{:S(2)}, u32[]{:S(2)}) %collective-permute-start.40) | collective-permute-done | bytes 294944 | tf_op jit(solution)/shard_map/ppermute | solution.py:392
  192.3 3.7 %collective-permute-done.44.refs_2_ = bf16[128,1024]{1,0:T(8,128)(2,1)S(1)} collective-permute-done((bf16[128,1024]{1,0:T(8,128)(2,1)S(1)}, bf16[128,1024]{1,0:T(8,128)(2,1)S(1)}, u32[]{:S(2)}, u32[]{:S(2)}) %collective-permute-start.44) | collective-permute-done | bytes 262176 | tf_op jit(solution)/shard_map/ppermute | solution.py:392
  196.7 2.8 collective-permute-start.47
  199.6 9.2 %collective-permute-done.46.refs_3_ = bf16[64,1024]{1,0:T(8,128)(2,1)S(1)} collective-permute-done((bf16[64,1024]{1,0:T(8,128)(2,1)S(1)}, bf16[64,1024]{1,0:T(8,128)(2,1)S(1)}, u32[]{:S(2)}, u32[]{:S(2)}) %collective-permute-start.46) | collective-permute-done | bytes 131104 | tf_op jit(solution)/shard_map/ppermute | solution.py:392
  215.1 2.2 collective-permute-start.50
  217.3 4.8 %collective-permute-done.48 = bf16[64,1024]{1,0:T(8,128)(2,1)S(1)} collective-permute-done((bf16[64,1024]{1,0:T(8,128)(2,1)S(1)}, bf16[64,1024]{1,0:T(8,128)(2,1)S(1)}, u32[]{:S(2)}, u32[]{:S(2)}) %collective-permute-start.48) | collective-permute-done | bytes 131104 | tf_op jit(solution)/shard_map/ppermute | solution.py:392
  222.2 2.3 collective-permute-done.49
  224.4 2.2 collective-permute-start.58
  227.3 2.0 collective-permute-start.56
  229.9 6.2 %collective-permute-done.52 = bf16[128,1024]{1,0:T(8,128)(2,1)S(1)} collective-permute-done((bf16[128,1024]{1,0:T(8,128)(2,1)S(1)}, bf16[128,1024]{1,0:T(8,128)(2,1)S(1)}, u32[]{:S(2)}, u32[]{:S(2)}) %collective-permute-start.52) | collective-permute-done | bytes 262176 | tf_op jit(solution)/shard_map/ppermute | solution.py:392
  236.1 1.9 collective-permute-start.53
  239.6 2.7 collective-permute-done.59
  242.4 2.0 collective-permute-start.63
  244.3 2.5 collective-permute-start.60
  248.1 2.1 collective-permute-start.57
  250.2 2.2 collective-permute-done.61.refs_7_
  252.4 6.9 %collective-permute-done.63.refs_7_ = bf16[256,1024]{1,0:T(8,128)(2,1)S(1)} collective-permute-done((bf16[256,1024]{1,0:T(8,128)(2,1)S(1)}, bf16[256,1024]{1,0:T(8,128)(2,1)S(1)}, u32[]{:S(2)}, u32[]{:S(2)}) %collective-permute-start.63) | collective-permute-done | bytes 524320 | tf_op jit(solution)/shard_map/ppermute | solution.py:392
  259.8 4.6 %collective-permute-done.64.refs_8_ = bf16[256,1024]{1,0:T(8,128)(2,1)S(1)} collective-permute-done((bf16[256,1024]{1,0:T(8,128)(2,1)S(1)}, bf16[256,1024]{1,0:T(8,128)(2,1)S(1)}, u32[]{:S(2)}, u32[]{:S(2)}) %collective-permute-start.64) | collective-permute-done | bytes 524320 | tf_op jit(solution)/shard_map/ppermute | solution.py:298
  264.3 9.1 %collective-permute-done.57.refs_6_ = bf16[384,1024]{1,0:T(8,128)(2,1)S(1)} collective-permute-done((bf16[384,1024]{1,0:T(8,128)(2,1)S(1)}, bf16[384,1024]{1,0:T(8,128)(2,1)S(1)}, u32[]{:S(2)}, u32[]{:S(2)}) %collective-permute-start.57) | collective-permute-done | bytes 786464 | tf_op jit(solution)/shard_map/ppermute | solution.py:392
  273.4 3.0 %mix_pair.3.refs_0_ = f32[768,1024]{1,0:T(8,128)S(1)} custom-call(s32[2]{0:T(128)S(1)} %copy-done.18, bf16[768,256]{1,0:T(8,128)(2,1)S(1)} %copy-done.3, bf16[768,256]{1,0:T(8,128)(2,1)} %collective-permute-done.30.refs_5_.refs_1_, bf16[768,256]{1,0:T(8,128)(2,1)S(1)} %copy-done.5, bf16[784,256]{1,0:T(8,128)(2,1)S(1)} %copy-done.1, ...), custom_call_target="tpu_custom_call" | custom-call | flops 1024 | bytes 5242880 | tf_op jit(solution)/shard_map/mix_pair/pallas_call | solution.py:96
  276.5 2.6 mix_own.1.refs_0_
  279.1 3.6 %mix_pair.4.refs_1_ = f32[768,1024]{1,0:T(8,128)S(1)} custom-call(s32[2]{0:T(128)S(1)} %pad_add_fusion.1.where_ref, f32[768,1024]{1,0:T(8,128)S(1)} %mix_own.1.refs_0_, bf16[768,256]{1,0:T(8,128)(2,1)} %collective-permute-done.25.refs_4_.refs_1_, bf16[768,256]{1,0:T(8,128)(2,1)} %collective-permute-done.27.refs_5_.refs_2_, ...), custom_call_target="tpu_custom_call", output_to_operand_aliasing={{}: (1, {})} | custom-call | flops 1024 | bytes 5242880 | tf_op jit(solution)/shard_map/mix_pair/pallas_call | solution.py:96
  282.7 4.8 %mix_pair.5 = bf16[768,1024]{1,0:T(8,128)(2,1)} custom-call(s32[2]{0:T(128)S(1)} %pad_add_fusion.1.where_ref, f32[8,128]{1,0:T(8,128)S(1)} %get-tuple-element.452.refs_4_.refs_0_, f32[768,1024]{1,0:T(8,128)S(1)} %mix_pair.4.refs_1_, bf16[768,256]{1,0:T(8,128)(2,1)} %collective-permute-done.26.refs_4_.refs_2_, ...), custom_call_target="tpu_custom_call" | custom-call | flops 1024 | bytes 5242880 | tf_op jit(solution)/shard_map/mix_pair/pallas_call | solution.py:96
  (162 shorter events, 66.4 us)
Async XLA Ops:
  1.5 13.0 %collective-permute-start = (bf16[768,256]{1,0:T(8,128)(2,1)S(1)}, bf16[768,256]{1,0:T(8,128)(2,1)S(1)}, u32[]{:S(2)}, u32[]{:S(2)}) collective-permute-start(bf16[768,256]{1,0:T(8,128)(2,1)S(1)} %get-tuple-element.501.field_ref.refs_0_), channel_id=1, source_target_pairs={{0,4},{4,0},{8,12},{12,8},{16,20},{20,16},{24,28},{28,24},{1,5},{5... | collective-permute-start | bytes 1179656 | tf_op jit(solution)/shard_map/ppermute | solution.py:311
  10.5 12.4 %collective-permute-start.2 = (bf16[768,256]{1,0:T(8,128)(2,1)S(1)}, bf16[768,256]{1,0:T(8,128)(2,1)S(1)}, u32[]{:S(2)}, u32[]{:S(2)}) collective-permute-start(bf16[768,256]{1,0:T(8,128)(2,1)S(1)} %get-tuple-element.259.field_ref.refs_0_), channel_id=1, source_target_pairs={{0,4},{4,0},{8,12},{12,8},{16,20},{20,16},{24,28},{28,24},{1,5},{5... | collective-permute-start | bytes 1179656 | tf_op jit(solution)/shard_map/ppermute | solution.py:316
  14.5 14.1 %collective-permute-start.1 = (bf16[768,256]{1,0:T(8,128)(2,1)S(1)}, bf16[768,256]{1,0:T(8,128)(2,1)S(1)}, u32[]{:S(2)}, u32[]{:S(2)}) collective-permute-start(bf16[768,256]{1,0:T(8,128)(2,1)S(1)} %collective-permute-done.near_ref), channel_id=1, source_target_pairs={{0,8},{4,28},{8,16},{12,4},{16,24},{20,12},{24,0},{28,20},{1,9},{5... | collective-permute-start | bytes 1179656 | tf_op jit(solution)/shard_map/ppermute | solution.py:325
  16.6 14.7 %collective-permute-start.4 = (bf16[768,256]{1,0:T(8,128)(2,1)S(1)}, bf16[768,256]{1,0:T(8,128)(2,1)S(1)}, u32[]{:S(2)}, u32[]{:S(2)}) collective-permute-start(bf16[768,256]{1,0:T(8,128)(2,1)S(1)} %get-tuple-element.267.field_ref.refs_0_), channel_id=1, source_target_pairs={{0,4},{4,0},{8,12},{12,8},{16,20},{20,16},{24,28},{28,24},{1,5},{5... | collective-permute-start | bytes 1179656 | tf_op jit(solution)/shard_map/ppermute | solution.py:316
  22.9 14.1 %collective-permute-start.7 = (bf16[768,256]{1,0:T(8,128)(2,1)S(1)}, bf16[768,256]{1,0:T(8,128)(2,1)S(1)}, u32[]{:S(2)}, u32[]{:S(2)}) collective-permute-start(bf16[768,256]{1,0:T(8,128)(2,1)S(1)} %collective-permute-done.2.near_ref), channel_id=1, source_target_pairs={{0,8},{4,28},{8,16},{12,4},{16,24},{20,12},{24,0},{28,20},{1,9},{5... | collective-permute-start | bytes 1179656 | tf_op jit(solution)/shard_map/ppermute | solution.py:325
  25.0 14.7 %collective-permute-start.6 = (bf16[768,256]{1,0:T(8,128)(2,1)S(1)}, bf16[768,256]{1,0:T(8,128)(2,1)S(1)}, u32[]{:S(2)}, u32[]{:S(2)}) collective-permute-start(bf16[768,256]{1,0:T(8,128)(2,1)S(1)} %get-tuple-element.270.field_ref.refs_0_), channel_id=1, source_target_pairs={{0,4},{4,0},{8,12},{12,8},{16,20},{20,16},{24,28},{28,24},{1,5},{5... | collective-permute-start | bytes 1179656 | tf_op jit(solution)/shard_map/ppermute | solution.py:316
  31.3 14.1 %collective-permute-start.5 = (bf16[768,256]{1,0:T(8,128)(2,1)S(1)}, bf16[768,256]{1,0:T(8,128)(2,1)S(1)}, u32[]{:S(2)}, u32[]{:S(2)}) collective-permute-start(bf16[768,256]{1,0:T(8,128)(2,1)S(1)} %collective-permute-done.4.near_ref), channel_id=1, source_target_pairs={{0,8},{4,28},{8,16},{12,4},{16,24},{20,12},{24,0},{28,20},{1,9},{5... | collective-permute-start | bytes 1179656 | tf_op jit(solution)/shard_map/ppermute | solution.py:325
  33.4 14.7 %collective-permute-start.3 = (bf16[768,256]{1,0:T(8,128)(2,1)S(1)}, bf16[768,256]{1,0:T(8,128)(2,1)S(1)}, u32[]{:S(2)}, u32[]{:S(2)}) collective-permute-start(bf16[768,256]{1,0:T(8,128)(2,1)S(1)} %get-tuple-element.266.field_ref), channel_id=1, source_target_pairs={{0,4},{4,0},{8,12},{12,8},{16,20},{20,16},{24,28},{28,24},{1,5},{5... | collective-permute-start | bytes 1179656 | tf_op jit(solution)/shard_map/ppermute | solution.py:365
  39.7 14.1 %collective-permute-start.10 = (bf16[768,256]{1,0:T(8,128)(2,1)S(1)}, bf16[768,256]{1,0:T(8,128)(2,1)S(1)}, u32[]{:S(2)}, u32[]{:S(2)}) collective-permute-start(bf16[768,256]{1,0:T(8,128)(2,1)S(1)} %collective-permute-done.6.near_ref), channel_id=1, source_target_pairs={{0,8},{4,28},{8,16},{12,4},{16,24},{20,12},{24,0},{28,20},{1,9},{5... | collective-permute-start | bytes 1179656 | tf_op jit(solution)/shard_map/ppermute | solution.py:325
  41.9 14.7 %collective-permute-start.9 = (bf16[768,256]{1,0:T(8,128)(2,1)S(1)}, bf16[768,256]{1,0:T(8,128)(2,1)S(1)}, u32[]{:S(2)}, u32[]{:S(2)}) collective-permute-start(bf16[768,256]{1,0:T(8,128)(2,1)S(1)} %get-tuple-element.285.field_ref), channel_id=1, source_target_pairs={{0,4},{4,0},{8,12},{12,8},{16,20},{20,16},{24,28},{28,24},{1,5},{5... | collective-permute-start | bytes 1179656 | tf_op jit(solution)/shard_map/ppermute | solution.py:365
  48.2 14.1 %collective-permute-start.8 = (bf16[768,256]{1,0:T(8,128)(2,1)S(1)}, bf16[768,256]{1,0:T(8,128)(2,1)S(1)}, u32[]{:S(2)}, u32[]{:S(2)}) collective-permute-start(bf16[768,256]{1,0:T(8,128)(2,1)S(1)} %collective-permute-done.3.near_ref), channel_id=1, source_target_pairs={{0,8},{4,28},{8,16},{12,4},{16,24},{20,12},{24,0},{28,20},{1,9},{5... | collective-permute-start | bytes 1179656 | tf_op jit(solution)/shard_map/ppermute | solution.py:325
  50.3 14.7 %collective-permute-start.12 = (bf16[768,256]{1,0:T(8,128)(2,1)S(1)}, bf16[768,256]{1,0:T(8,128)(2,1)S(1)}, u32[]{:S(2)}, u32[]{:S(2)}) collective-permute-start(bf16[768,256]{1,0:T(8,128)(2,1)S(1)} %get-tuple-element.297.field_ref), channel_id=1, source_target_pairs={{0,4},{4,0},{8,12},{12,8},{16,20},{20,16},{24,28},{28,24},{1,5},{5... | collective-permute-start | bytes 1179656 | tf_op jit(solution)/shard_map/ppermute | solution.py:365
  56.6 14.1 %collective-permute-start.15 = (bf16[768,256]{1,0:T(8,128)(2,1)S(1)}, bf16[768,256]{1,0:T(8,128)(2,1)S(1)}, u32[]{:S(2)}, u32[]{:S(2)}) collective-permute-start(bf16[768,256]{1,0:T(8,128)(2,1)S(1)} %collective-permute-done.9.near_ref), channel_id=1, source_target_pairs={{0,8},{4,28},{8,16},{12,4},{16,24},{20,12},{24,0},{28,20},{1,9},{5... | collective-permute-start | bytes 1179656 | tf_op jit(solution)/shard_map/ppermute | solution.py:325
  58.7 14.7 %collective-permute-start.14 = (bf16[768,256]{1,0:T(8,128)(2,1)S(1)}, bf16[768,256]{1,0:T(8,128)(2,1)S(1)}, u32[]{:S(2)}, u32[]{:S(2)}) collective-permute-start(bf16[768,256]{1,0:T(8,128)(2,1)S(1)} %get-tuple-element.300.field_ref), channel_id=1, source_target_pairs={{0,4},{4,0},{8,12},{12,8},{16,20},{20,16},{24,28},{28,24},{1,5},{5... | collective-permute-start | bytes 1179656 | tf_op jit(solution)/shard_map/ppermute | solution.py:365
  65.0 14.1 %collective-permute-start.13 = (bf16[768,256]{1,0:T(8,128)(2,1)S(1)}, bf16[768,256]{1,0:T(8,128)(2,1)S(1)}, u32[]{:S(2)}, u32[]{:S(2)}) collective-permute-start(bf16[768,256]{1,0:T(8,128)(2,1)S(1)} %collective-permute-done.12.near_ref), channel_id=1, source_target_pairs={{0,8},{4,28},{8,16},{12,4},{16,24},{20,12},{24,0},{28,20},{1,9},{5... | collective-permute-start | bytes 1179656 | tf_op jit(solution)/shard_map/ppermute | solution.py:325
  67.1 14.7 %collective-permute-start.11 = (bf16[768,256]{1,0:T(8,128)(2,1)S(1)}, bf16[768,256]{1,0:T(8,128)(2,1)S(1)}, u32[]{:S(2)}, u32[]{:S(2)}) collective-permute-start(bf16[768,256]{1,0:T(8,128)(2,1)S(1)} %product_1.4.field_ref), channel_id=1, source_target_pairs={{0,4},{4,0},{8,12},{12,8},{16,20},{20,16},{24,28},{28,24},{1,5},{5... | collective-permute-start | bytes 1179656 | tf_op jit(solution)/shard_map/ppermute | solution.py:365
  73.4 14.1 %collective-permute-start.18 = (bf16[768,256]{1,0:T(8,128)(2,1)S(1)}, bf16[768,256]{1,0:T(8,128)(2,1)S(1)}, u32[]{:S(2)}, u32[]{:S(2)}) collective-permute-start(bf16[768,256]{1,0:T(8,128)(2,1)S(1)} %collective-permute-done.14.near_ref), channel_id=1, source_target_pairs={{0,8},{4,28},{8,16},{12,4},{16,24},{20,12},{24,0},{28,20},{1,9},{5... | collective-permute-start | bytes 1179656 | tf_op jit(solution)/shard_map/ppermute | solution.py:325
  75.6 14.7 %collective-permute-start.17 = (bf16[768,256]{1,0:T(8,128)(2,1)S(1)}, bf16[768,256]{1,0:T(8,128)(2,1)S(1)}, u32[]{:S(2)}, u32[]{:S(2)}) collective-permute-start(bf16[768,256]{1,0:T(8,128)(2,1)S(1)} %product_1.5.field_ref), channel_id=1, source_target_pairs={{0,4},{4,0},{8,12},{12,8},{16,20},{20,16},{24,28},{28,24},{1,5},{5... | collective-permute-start | bytes 1179656 | tf_op jit(solution)/shard_map/ppermute | solution.py:365
  81.9 14.1 %collective-permute-start.16 = (bf16[768,256]{1,0:T(8,128)(2,1)S(1)}, bf16[768,256]{1,0:T(8,128)(2,1)S(1)}, u32[]{:S(2)}, u32[]{:S(2)}) collective-permute-start(bf16[768,256]{1,0:T(8,128)(2,1)S(1)} %collective-permute-done.11.near_ref), channel_id=1, source_target_pairs={{0,8},{4,28},{8,16},{12,4},{16,24},{20,12},{24,0},{28,20},{1,9},{5... | collective-permute-start | bytes 1179656 | tf_op jit(solution)/shard_map/ppermute | solution.py:325
  84.0 14.7 %collective-permute-start.20 = (bf16[768,256]{1,0:T(8,128)(2,1)S(1)}, bf16[768,256]{1,0:T(8,128)(2,1)S(1)}, u32[]{:S(2)}, u32[]{:S(2)}) collective-permute-start(bf16[768,256]{1,0:T(8,128)(2,1)S(1)} %product_1.6.field_ref), channel_id=1, source_target_pairs={{0,4},{4,0},{8,12},{12,8},{16,20},{20,16},{24,28},{28,24},{1,5},{5... | collective-permute-start | bytes 1179656 | tf_op jit(solution)/shard_map/ppermute | solution.py:365
  90.3 12.0 %collective-permute-start.19 = (bf16[768,256]{1,0:T(8,128)(2,1)S(1)}, bf16[768,256]{1,0:T(8,128)(2,1)S(1)}, u32[]{:S(2)}, u32[]{:S(2)}) collective-permute-start(bf16[768,256]{1,0:T(8,128)(2,1)S(1)} %collective-permute-done.17.near_ref), channel_id=1, source_target_pairs={{0,8},{4,28},{8,16},{12,4},{16,24},{20,12},{24,0},{28,20},{1,9},{5... | collective-permute-start | bytes 1179656 | tf_op jit(solution)/shard_map/ppermute | solution.py:325
  92.4 13.9 %collective-permute-start.22 = (bf16[768,256]{1,0:T(8,128)(2,1)S(1)}, bf16[768,256]{1,0:T(8,128)(2,1)S(1)}, u32[]{:S(2)}, u32[]{:S(2)}) collective-permute-start(bf16[768,256]{1,0:T(8,128)(2,1)S(1)} %product_1.7.field_ref), channel_id=1, source_target_pairs={{0,4},{4,0},{8,12},{12,8},{16,20},{20,16},{24,28},{28,24},{1,5},{5... | collective-permute-start | bytes 1179656 | tf_op jit(solution)/shard_map/ppermute | solution.py:365
  98.7 11.3 %collective-permute-start.21 = (bf16[768,256]{1,0:T(8,128)(2,1)S(1)}, bf16[768,256]{1,0:T(8,128)(2,1)S(1)}, u32[]{:S(2)}, u32[]{:S(2)}) collective-permute-start(bf16[768,256]{1,0:T(8,128)(2,1)S(1)} %collective-permute-done.20.near_ref), channel_id=1, source_target_pairs={{0,8},{4,28},{8,16},{12,4},{16,24},{20,12},{24,0},{28,20},{1,9},{5... | collective-permute-start | bytes 1179656 | tf_op jit(solution)/shard_map/ppermute | solution.py:325
  100.8 15.0 %collective-permute-start.24 = (bf16[768,256]{1,0:T(8,128)(2,1)S(1)}, bf16[768,256]{1,0:T(8,128)(2,1)S(1)}, u32[]{:S(2)}, u32[]{:S(2)}) collective-permute-start(bf16[768,256]{1,0:T(8,128)(2,1)S(1)} %get-tuple-element.323.refs_0_.refs_1_.refs_10_), channel_id=1, source_target_pairs={{0,1},{1,0},{2,3},{3,2},{4,5},{5,4},{6,7},{7,6},{8,9},{9,8},{10,11... | collective-permute-start | bytes 1179656 | tf_op jit(solution)/shard_map/ppermute | solution.py:298
  100.8 15.0 %collective-permute-start.25 = (bf16[768,256]{1,0:T(8,128)(2,1)S(1)}, bf16[768,256]{1,0:T(8,128)(2,1)}, u32[]{:S(2)}, u32[]{:S(2)}) collective-permute-start(bf16[768,256]{1,0:T(8,128)(2,1)S(1)} %get-tuple-element.323.refs_0_.refs_1_.refs_10_), channel_id=1, source_target_pairs={{0,2},{1,3},{2,0},{3,1},{4,6},{5,7},{6,4},{7,5},{8,10},{9,11},{10,... | collective-permute-start | bytes 1179656 | tf_op jit(solution)/shard_map/ppermute | solution.py:298
  106.3 12.3 %collective-permute-start.23 = (bf16[768,256]{1,0:T(8,128)(2,1)S(1)}, bf16[768,256]{1,0:T(8,128)(2,1)}, u32[]{:S(2)}, u32[]{:S(2)}) collective-permute-start(bf16[768,256]{1,0:T(8,128)(2,1)S(1)} %collective-permute-done.22.near_ref), channel_id=1, source_target_pairs={{0,8},{4,28},{8,16},{12,4},{16,24},{20,12},{24,0},{28,20},{1,9},{5... | collective-permute-start | bytes 1179656 | tf_op jit(solution)/shard_map/ppermute | solution.py:325
  108.1 14.4 %collective-permute-start.27 = (bf16[768,256]{1,0:T(8,128)(2,1)S(1)}, bf16[768,256]{1,0:T(8,128)(2,1)}, u32[]{:S(2)}, u32[]{:S(2)}) collective-permute-start(bf16[768,256]{1,0:T(8,128)(2,1)S(1)} %get-tuple-element.334.refs_1_.refs_2_.refs_11_), channel_id=1, source_target_pairs={{0,2},{1,3},{2,0},{3,1},{4,6},{5,7},{6,4},{7,5},{8,10},{9,11},{10,... | collective-permute-start | bytes 1179656 | tf_op jit(solution)/shard_map/ppermute | solution.py:298
  110.8 11.8 %collective-permute-start.30 = (bf16[768,256]{1,0:T(8,128)(2,1)S(1)}, bf16[768,256]{1,0:T(8,128)(2,1)}, u32[]{:S(2)}, u32[]{:S(2)}) collective-permute-start(bf16[768,256]{1,0:T(8,128)(2,1)S(1)} %get-tuple-element.334.refs_1_.refs_2_.refs_11_), channel_id=1, source_target_pairs={{0,1},{1,0},{2,3},{3,2},{4,5},{5,4},{6,7},{7,6},{8,9},{9,8},{10,11... | collective-permute-start | bytes 1179656 | tf_op jit(solution)/shard_map/ppermute | solution.py:298
  125.6 26.2 %collective-permute-start.35 = (bf16[384,1024]{1,0:T(8,128)(2,1)}, bf16[384,1024]{1,0:T(8,128)(2,1)S(1)}, u32[]{:S(2)}, u32[]{:S(2)}) collective-permute-start(bf16[384,1024]{1,0:T(8,128)(2,1)} %get-tuple-element.376), channel_id=1, source_target_pairs={{0,4},{4,0},{8,12},{12,8},{16,20},{20,16},{24,28},{28,24},{1,5},{5... | collective-permute-start | bytes 2359304 | tf_op jit(solution)/shard_map/ppermute | solution.py:392
  127.4 19.9 %collective-permute-start.32 = (bf16[784,256]{1,0:T(8,128)(2,1)S(1)}, bf16[784,256]{1,0:T(8,128)(2,1)S(1)}, u32[]{:S(2)}, u32[]{:S(2)}) collective-permute-start(bf16[784,256]{1,0:T(8,128)(2,1)S(1)} %product_2.7.refs_3_.refs_4_.refs_13_), channel_id=1, source_target_pairs={{0,2},{1,3},{2,0},{3,1},{4,6},{5,7},{6,4},{7,5},{8,10},{9,11},{10,... | collective-permute-start | bytes 1204232 | tf_op jit(solution)/shard_map/ppermute | solution.py:298
  128.9 17.7 %collective-permute-start.29 = (bf16[768,256]{1,0:T(8,128)(2,1)S(1)}, bf16[768,256]{1,0:T(8,128)(2,1)}, u32[]{:S(2)}, u32[]{:S(2)}) collective-permute-start(bf16[768,256]{1,0:T(8,128)(2,1)S(1)} %get-tuple-element.345.refs_2_.refs_3_.refs_12_), channel_id=1, source_target_pairs={{0,2},{1,3},{2,0},{3,1},{4,6},{5,7},{6,4},{7,5},{8,10},{9,11},{10,... | collective-permute-start | bytes 1179656 | tf_op jit(solution)/shard_map/ppermute | solution.py:298
  129.5 17.2 %collective-permute-start.33 = (bf16[768,256]{1,0:T(8,128)(2,1)S(1)}, bf16[768,256]{1,0:T(8,128)(2,1)S(1)}, u32[]{:S(2)}, u32[]{:S(2)}) collective-permute-start(bf16[768,256]{1,0:T(8,128)(2,1)S(1)} %get-tuple-element.345.refs_2_.refs_3_.refs_12_), channel_id=1, source_target_pairs={{0,1},{1,0},{2,3},{3,2},{4,5},{5,4},{6,7},{7,6},{8,9},{9,8},{10,11... | collective-permute-start | bytes 1179656 | tf_op jit(solution)/shard_map/ppermute | solution.py:298
  129.5 18.4 %collective-permute-start.36 = (bf16[784,256]{1,0:T(8,128)(2,1)S(1)}, bf16[784,256]{1,0:T(8,128)(2,1)S(1)}, u32[]{:S(2)}, u32[]{:S(2)}) collective-permute-start(bf16[784,256]{1,0:T(8,128)(2,1)S(1)} %product_2.7.refs_3_.refs_4_.refs_13_), channel_id=1, source_target_pairs={{0,1},{1,0},{2,3},{3,2},{4,5},{5,4},{6,7},{7,6},{8,9},{9,8},{10,11... | collective-permute-start | bytes 1204232 | tf_op jit(solution)/shard_map/ppermute | solution.py:298
  147.4 5.2 %collective-permute-start.34 = (bf16[784,256]{1,0:T(8,128)(2,1)S(1)}, bf16[784,256]{1,0:T(8,128)(2,1)}, u32[]{:S(2)}, u32[]{:S(2)}) collective-permute-start(bf16[784,256]{1,0:T(8,128)(2,1)S(1)} %collective-permute-done.32.refs_7_.refs_9_.refs_4_), channel_id=1, source_target_pairs={{0,1},{1,0},{2,3},{3,2},{4,5},{5,4},{6,7},{7,6},{8,9},{9,8},{10,11... | collective-permute-start | bytes 1204232 | tf_op jit(solution)/shard_map/ppermute | solution.py:298
  147.4 5.2 %collective-permute-start.26 = (bf16[768,256]{1,0:T(8,128)(2,1)}, bf16[768,256]{1,0:T(8,128)(2,1)}, u32[]{:S(2)}, u32[]{:S(2)}) collective-permute-start(bf16[768,256]{1,0:T(8,128)(2,1)} %collective-permute-done.25.refs_4_.refs_1_), channel_id=1, source_target_pairs={{0,1},{1,0},{2,3},{3,2},{4,5},{5,4},{6,7},{7,6},{8,9},{9,8},{10,11... | collective-permute-start | bytes 1179656 | tf_op jit(solution)/shard_map/ppermute | solution.py:298
  151.8 20.6 %collective-permute-start.39 = (bf16[256,1024]{1,0:T(8,128)(2,1)S(1)}, bf16[256,1024]{1,0:T(8,128)(2,1)S(1)}, u32[]{:S(2)}, u32[]{:S(2)}) collective-permute-start(bf16[256,1024]{1,0:T(8,128)(2,1)S(1)} %get-tuple-element.406), channel_id=1, source_target_pairs={{0,8},{4,12},{8,0},{12,4},{16,24},{20,28},{24,16},{28,20},{1,9},{5... | collective-permute-start | bytes 1572872 | tf_op jit(solution)/shard_map/ppermute | solution.py:392
  155.2 21.3 %collective-permute-start.37 = (bf16[272,1024]{1,0:T(8,128)(2,1)S(1)}, bf16[272,1024]{1,0:T(8,128)(2,1)S(1)}, u32[]{:S(2)}, u32[]{:S(2)}) collective-permute-start(bf16[272,1024]{1,0:T(8,128)(2,1)S(1)} %get-tuple-element.403), channel_id=1, source_target_pairs={{0,4},{4,0},{8,12},{12,8},{16,20},{20,16},{24,28},{28,24},{1,5},{5... | collective-permute-start | bytes 1671176 | tf_op jit(solution)/shard_map/ppermute | solution.py:392
  155.6 20.2 %collective-permute-start.38 = (bf16[192,1024]{1,0:T(8,128)(2,1)S(1)}, bf16[192,1024]{1,0:T(8,128)(2,1)S(1)}, u32[]{:S(2)}, u32[]{:S(2)}) collective-permute-start(bf16[192,1024]{1,0:T(8,128)(2,1)S(1)} %sum_hop.8), channel_id=1, source_target_pairs={{0,16},{4,20},{8,24},{12,28},{16,0},{20,4},{24,8},{28,12},{1,17},{... | collective-permute-start | bytes 1179656 | tf_op jit(solution)/shard_map/ppermute | solution.py:392
  159.7 24.6 %collective-permute-start.41 = (bf16[256,1024]{1,0:T(8,128)(2,1)S(1)}, bf16[256,1024]{1,0:T(8,128)(2,1)S(1)}, u32[]{:S(2)}, u32[]{:S(2)}) collective-permute-start(bf16[256,1024]{1,0:T(8,128)(2,1)S(1)} %get-tuple-element.429), channel_id=1, source_target_pairs={{0,4},{4,0},{8,12},{12,8},{16,20},{20,16},{24,28},{28,24},{1,5},{5... | collective-permute-start | bytes 1572872 | tf_op jit(solution)/shard_map/ppermute | solution.py:392
  176.4 7.9 %collective-permute-start.42 = (bf16[96,1024]{1,0:T(8,128)(2,1)S(1)}, bf16[96,1024]{1,0:T(8,128)(2,1)S(1)}, u32[]{:S(2)}, u32[]{:S(2)}) collective-permute-start(bf16[96,1024]{1,0:T(8,128)(2,1)S(1)} %sum_hop.10), channel_id=1, source_target_pairs={{0,8},{4,12},{8,0},{12,4},{16,24},{20,28},{24,16},{28,20},{1,9},{5... | collective-permute-start | bytes 589832 | tf_op jit(solution)/shard_map/ppermute | solution.py:392
  177.2 13.5 %collective-permute-start.40 = (bf16[144,1024]{1,0:T(8,128)(2,1)S(1)}, bf16[144,1024]{1,0:T(8,128)(2,1)S(1)}, u32[]{:S(2)}, u32[]{:S(2)}) collective-permute-start(bf16[144,1024]{1,0:T(8,128)(2,1)S(1)} %sum_hop.11), channel_id=1, source_target_pairs={{0,8},{4,12},{8,0},{12,4},{16,24},{20,28},{24,16},{28,20},{1,9},{5... | collective-permute-start | bytes 884744 | tf_op jit(solution)/shard_map/ppermute | solution.py:392
  179.2 12.4 %collective-permute-start.45 = (bf16[128,1024]{1,0:T(8,128)(2,1)S(1)}, bf16[128,1024]{1,0:T(8,128)(2,1)S(1)}, u32[]{:S(2)}, u32[]{:S(2)}) collective-permute-start(bf16[128,1024]{1,0:T(8,128)(2,1)S(1)} %sum_hop.9), channel_id=1, source_target_pairs={{0,4},{4,0},{8,12},{12,8},{16,20},{20,16},{24,28},{28,24},{1,5},{5... | collective-permute-start | bytes 786440 | tf_op jit(solution)/shard_map/ppermute | solution.py:392
  185.0 11.0 %collective-permute-start.44 = (bf16[128,1024]{1,0:T(8,128)(2,1)S(1)}, bf16[128,1024]{1,0:T(8,128)(2,1)S(1)}, u32[]{:S(2)}, u32[]{:S(2)}) collective-permute-start(bf16[128,1024]{1,0:T(8,128)(2,1)S(1)} %sum_hop.12), channel_id=1, source_target_pairs={{0,8},{4,12},{8,0},{12,4},{16,24},{20,28},{24,16},{28,20},{1,9},{5... | collective-permute-start | bytes 786440 | tf_op jit(solution)/shard_map/ppermute | solution.py:392
  191.3 17.5 %collective-permute-start.43 = (bf16[80,1024]{1,0:T(8,128)(2,1)S(1)}, bf16[80,1024]{1,0:T(8,128)(2,1)S(1)}, u32[]{:S(2)}, u32[]{:S(2)}) collective-permute-start(bf16[80,1024]{1,0:T(8,128)(2,1)S(1)} %sum_hop.13), channel_id=1, source_target_pairs={{0,16},{4,20},{8,24},{12,28},{16,0},{20,4},{24,8},{28,12},{1,17},{... | collective-permute-start | bytes 491528 | tf_op jit(solution)/shard_map/ppermute | solution.py:392
  196.6 12.2 %collective-permute-start.46 = (bf16[64,1024]{1,0:T(8,128)(2,1)S(1)}, bf16[64,1024]{1,0:T(8,128)(2,1)S(1)}, u32[]{:S(2)}, u32[]{:S(2)}) collective-permute-start(bf16[64,1024]{1,0:T(8,128)(2,1)S(1)} %sum_hop.15), channel_id=1, source_target_pairs={{0,16},{4,20},{8,24},{12,28},{16,0},{20,4},{24,8},{28,12},{1,17},{... | collective-permute-start | bytes 393224 | tf_op jit(solution)/shard_map/ppermute | solution.py:392
  196.7 15.5 %collective-permute-start.47 = (bf16[64,1024]{1,0:T(8,128)(2,1)S(1)}, bf16[64,1024]{1,0:T(8,128)(2,1)S(1)}, u32[]{:S(2)}, u32[]{:S(2)}) collective-permute-start(bf16[64,1024]{1,0:T(8,128)(2,1)S(1)} %sum_hop.14), channel_id=1, source_target_pairs={{0,16},{4,20},{8,24},{12,28},{16,0},{20,4},{24,8},{28,12},{1,17},{... | collective-permute-start | bytes 393224 | tf_op jit(solution)/shard_map/ppermute | solution.py:392
  210.2 11.9 %collective-permute-start.48 = (bf16[64,1024]{1,0:T(8,128)(2,1)S(1)}, bf16[64,1024]{1,0:T(8,128)(2,1)S(1)}, u32[]{:S(2)}, u32[]{:S(2)}) collective-permute-start(bf16[64,1024]{1,0:T(8,128)(2,1)S(1)} %sum_last.7), channel_id=1, source_target_pairs={{0,16},{4,20},{8,24},{12,28},{16,0},{20,4},{24,8},{28,12},{1,17},{... | collective-permute-start | bytes 393224 | tf_op jit(solution)/shard_map/ppermute | solution.py:392
  212.9 11.6 %collective-permute-start.49 = (bf16[64,1024]{1,0:T(8,128)(2,1)S(1)}, bf16[64,1024]{1,0:T(8,128)(2,1)S(1)}, u32[]{:S(2)}, u32[]{:S(2)}) collective-permute-start(bf16[64,1024]{1,0:T(8,128)(2,1)S(1)} %sum_last.6), channel_id=1, source_target_pairs={{0,16},{4,20},{8,24},{12,28},{16,0},{20,4},{24,8},{28,12},{1,17},{... | collective-permute-start | bytes 393224 | tf_op jit(solution)/shard_map/ppermute | solution.py:392
  214.7 12.6 %collective-permute-start.51 = (bf16[96,1024]{1,0:T(8,128)(2,1)S(1)}, bf16[96,1024]{1,0:T(8,128)(2,1)S(1)}, u32[]{:S(2)}, u32[]{:S(2)}) collective-permute-start(bf16[96,1024]{1,0:T(8,128)(2,1)S(1)} %sum_last.5), channel_id=1, source_target_pairs={{0,8},{4,12},{8,0},{12,4},{16,24},{20,28},{24,16},{28,20},{1,9},{5... | collective-permute-start | bytes 589832 | tf_op jit(solution)/shard_map/ppermute | solution.py:392
  215.1 11.5 %collective-permute-start.50 = (bf16[64,1024]{1,0:T(8,128)(2,1)S(1)}, bf16[64,1024]{1,0:T(8,128)(2,1)S(1)}, u32[]{:S(2)}, u32[]{:S(2)}) collective-permute-start(bf16[64,1024]{1,0:T(8,128)(2,1)S(1)} %get-tuple-element.465), channel_id=1, source_target_pairs={{0,16},{4,20},{8,24},{12,28},{16,0},{20,4},{24,8},{28,12},{1,17},{... | collective-permute-start | bytes 393224 | tf_op jit(solution)/shard_map/ppermute | solution.py:392
  222.1 14.0 %collective-permute-start.52 = (bf16[128,1024]{1,0:T(8,128)(2,1)S(1)}, bf16[128,1024]{1,0:T(8,128)(2,1)S(1)}, u32[]{:S(2)}, u32[]{:S(2)}) collective-permute-start(bf16[128,1024]{1,0:T(8,128)(2,1)S(1)} %pad_maximum_fusion.5), channel_id=1, source_target_pairs={{0,8},{4,12},{8,0},{12,4},{16,24},{20,28},{24,16},{28,20},{1,9},{5... | collective-permute-start | bytes 786440 | tf_op jit(solution)/shard_map/ppermute | solution.py:392
  224.4 13.5 %collective-permute-start.58 = (bf16[128,1024]{1,0:T(8,128)(2,1)S(1)}, bf16[128,1024]{1,0:T(8,128)(2,1)S(1)}, u32[]{:S(2)}, u32[]{:S(2)}) collective-permute-start(bf16[128,1024]{1,0:T(8,128)(2,1)S(1)} %pad_maximum_fusion.6), channel_id=1, source_target_pairs={{0,4},{4,0},{8,12},{12,8},{16,20},{20,16},{24,28},{28,24},{1,5},{5... | collective-permute-start | bytes 786440 | tf_op jit(solution)/shard_map/ppermute | solution.py:392
  227.3 17.1 %collective-permute-start.56 = (bf16[192,1024]{1,0:T(8,128)(2,1)S(1)}, bf16[192,1024]{1,0:T(8,128)(2,1)S(1)}, u32[]{:S(2)}, u32[]{:S(2)}) collective-permute-start(bf16[192,1024]{1,0:T(8,128)(2,1)S(1)} %pad_maximum_fusion.4), channel_id=1, source_target_pairs={{0,16},{4,20},{8,24},{12,28},{16,0},{20,4},{24,8},{28,12},{1,17},{... | collective-permute-start | bytes 1179656 | tf_op jit(solution)/shard_map/ppermute | solution.py:392
  229.3 13.1 %collective-permute-start.59 = (bf16[128,1024]{1,0:T(8,128)(2,1)S(1)}, bf16[128,1024]{1,0:T(8,128)(2,1)S(1)}, u32[]{:S(2)}, u32[]{:S(2)}) collective-permute-start(bf16[128,1024]{1,0:T(8,128)(2,1)S(1)} %pad_maximum_fusion.7), channel_id=1, source_target_pairs={{0,8},{4,12},{8,0},{12,4},{16,24},{20,28},{24,16},{28,20},{1,9},{5... | collective-permute-start | bytes 786440 | tf_op jit(solution)/shard_map/ppermute | solution.py:392
  236.1 12.0 %collective-permute-start.53 = (bf16[256,1024]{1,0:T(8,128)(2,1)S(1)}, bf16[256,1024]{1,0:T(8,128)(2,1)S(1)}, u32[]{:S(2)}, u32[]{:S(2)}) collective-permute-start(bf16[256,1024]{1,0:T(8,128)(2,1)S(1)} %pad_maximum_fusion.1.refs_4_), channel_id=1, source_target_pairs={{0,4},{4,0},{8,12},{12,8},{16,20},{20,16},{24,28},{28,24},{1,5},{5... | collective-permute-start | bytes 1572872 | tf_op jit(solution)/shard_map/ppermute | solution.py:392
  238.0 12.2 %collective-permute-start.54 = (bf16[256,1024]{1,0:T(8,128)(2,1)S(1)}, bf16[256,1024]{1,0:T(8,128)(2,1)S(1)}, u32[]{:S(2)}, u32[]{:S(2)}) collective-permute-start(bf16[256,1024]{1,0:T(8,128)(2,1)S(1)} %pad_maximum_fusion.1.refs_4_), channel_id=1, source_target_pairs={{0,1},{1,0},{2,3},{3,2},{4,5},{5,4},{6,7},{7,6},{8,9},{9,8},{10,11... | collective-permute-start | bytes 1572872 | tf_op jit(solution)/shard_map/ppermute | solution.py:298
  238.0 14.4 %collective-permute-start.61 = (bf16[256,1024]{1,0:T(8,128)(2,1)S(1)}, bf16[256,1024]{1,0:T(8,128)(2,1)S(1)}, u32[]{:S(2)}, u32[]{:S(2)}) collective-permute-start(bf16[256,1024]{1,0:T(8,128)(2,1)S(1)} %pad_maximum_fusion.2.refs_5_), channel_id=1, source_target_pairs={{0,2},{1,3},{2,0},{3,1},{4,6},{5,7},{6,4},{7,5},{8,10},{9,11},{10,... | collective-permute-start | bytes 1572872 | tf_op jit(solution)/shard_map/ppermute | solution.py:298
  242.4 17.0 %collective-permute-start.63 = (bf16[256,1024]{1,0:T(8,128)(2,1)S(1)}, bf16[256,1024]{1,0:T(8,128)(2,1)S(1)}, u32[]{:S(2)}, u32[]{:S(2)}) collective-permute-start(bf16[256,1024]{1,0:T(8,128)(2,1)S(1)} %pad_maximum_fusion.3.refs_6_), channel_id=1, source_target_pairs={{0,4},{4,0},{8,12},{12,8},{16,20},{20,16},{24,28},{28,24},{1,5},{5... | collective-permute-start | bytes 1572872 | tf_op jit(solution)/shard_map/ppermute | solution.py:392
  244.3 15.4 %collective-permute-start.60 = (bf16[256,1024]{1,0:T(8,128)(2,1)S(1)}, bf16[256,1024]{1,0:T(8,128)(2,1)S(1)}, u32[]{:S(2)}, u32[]{:S(2)}) collective-permute-start(bf16[256,1024]{1,0:T(8,128)(2,1)S(1)} %pad_maximum_fusion.2.refs_5_), channel_id=1, source_target_pairs={{0,8},{4,12},{8,0},{12,4},{16,24},{20,28},{24,16},{28,20},{1,9},{5... | collective-permute-start | bytes 1572872 | tf_op jit(solution)/shard_map/ppermute | solution.py:392
  248.1 25.3 %collective-permute-start.57 = (bf16[384,1024]{1,0:T(8,128)(2,1)S(1)}, bf16[384,1024]{1,0:T(8,128)(2,1)S(1)}, u32[]{:S(2)}, u32[]{:S(2)}) collective-permute-start(bf16[384,1024]{1,0:T(8,128)(2,1)S(1)} %pad_maximum_fusion.refs_5_), channel_id=1, source_target_pairs={{0,4},{4,0},{8,12},{12,8},{16,20},{20,16},{24,28},{28,24},{1,5},{5... | collective-permute-start | bytes 2359304 | tf_op jit(solution)/shard_map/ppermute | solution.py:392
  250.2 14.1 %collective-permute-start.64 = (bf16[256,1024]{1,0:T(8,128)(2,1)S(1)}, bf16[256,1024]{1,0:T(8,128)(2,1)S(1)}, u32[]{:S(2)}, u32[]{:S(2)}) collective-permute-start(bf16[256,1024]{1,0:T(8,128)(2,1)S(1)} %pad_maximum_fusion.3.refs_6_), channel_id=1, source_target_pairs={{0,3},{1,2},{2,1},{3,0},{4,7},{5,6},{6,5},{7,4},{8,11},{9,10},{10,... | collective-permute-start | bytes 1572872 | tf_op jit(solution)/shard_map/ppermute | solution.py:298
  252.4 11.9 %collective-permute-start.55 = (bf16[256,1024]{1,0:T(8,128)(2,1)S(1)}, bf16[256,1024]{1,0:T(8,128)(2,1)S(1)}, u32[]{:S(2)}, u32[]{:S(2)}) collective-permute-start(bf16[256,1024]{1,0:T(8,128)(2,1)S(1)} %collective-permute-done.53.refs_5_), channel_id=1, source_target_pairs={{0,1},{1,0},{2,3},{3,2},{4,5},{5,4},{6,7},{7,6},{8,9},{9,8},{10,11... | collective-permute-start | bytes 1572872 | tf_op jit(solution)/shard_map/ppermute | solution.py:298
  259.3 19.7 %collective-permute-start.62 = (bf16[256,1024]{1,0:T(8,128)(2,1)S(1)}, bf16[256,1024]{1,0:T(8,128)(2,1)S(1)}, u32[]{:S(2)}, u32[]{:S(2)}) collective-permute-start(bf16[256,1024]{1,0:T(8,128)(2,1)S(1)} %collective-permute-done.61.refs_7_), channel_id=1, source_target_pairs={{0,8},{4,12},{8,0},{12,4},{16,24},{20,28},{24,16},{28,20},{1,9},{5... | collective-permute-start | bytes 1572872 | tf_op jit(solution)/shard_map/ppermute | solution.py:392
  259.8 22.9 %collective-permute-start.65 = (bf16[256,1024]{1,0:T(8,128)(2,1)S(1)}, bf16[256,1024]{1,0:T(8,128)(2,1)S(1)}, u32[]{:S(2)}, u32[]{:S(2)}) collective-permute-start(bf16[256,1024]{1,0:T(8,128)(2,1)S(1)} %collective-permute-done.63.refs_7_), channel_id=1, source_target_pairs={{0,3},{1,2},{2,1},{3,0},{4,7},{5,6},{6,5},{7,4},{8,11},{9,10},{10,... | collective-permute-start | bytes 1572872 | tf_op jit(solution)/shard_map/ppermute | solution.py:298
  (22 other events, 78.2 us)

commit v12 on v11

--- a/solution.py
+++ b/solution.py
@@ -360,6 +360,8 @@
             if c > 1:
                 more_panel(c - 2)
                 settle(c - 2, lambda d: not d & (d - 1))
+            if last:
+                more_panel(c - 1)
             return
         current[(stage + 1, c)] = out
         near[(stage + 1, c)] = lax.ppermute(out, "elem", swap)
@@ -491,6 +493,8 @@
             far = order(far)
         else:
             yield arrival
+            while mixes < turn[d]:
+                yield clock.now + 0.5
             far = order(far)
         parts = (part, far)
         if d:
@@ -519,7 +523,7 @@
     y_first, z_then_y, y_then_far = (1, *z_masks), (*z_masks[:1], 1, *z_masks[1:]), (1, *z_masks[::-1])
     there[1] = 25.0
     queue = sorted(range(1, groups), key=lambda d: (d == 1, d))
-    turn = {d: place for place, d in enumerate(sorted(range(groups), key=lambda d: (d != 1, d)))}
+    turn = {d: place for place, d in enumerate([queue[-1], *queue[:-2], 0, *queue[-2:-1]])}
     carrier = queue[min(1, len(queue) - 1)]
     processes = [panel_process()]
     for d in queue:

time: 288 us -> 284 us (0.986)
  waiting for transfers between devices: 118 us -> 102 us
  starting transfers between devices: 103 us -> 114 us
    ppermute x17, waiting for transfers between devices: 23.4 us -> 12.5 us  [to_group(): return lax.ppermute(value, 'orb', [(i, i ^ d) for i in range(groups)])]
    ppermute x25, starting transfers between devices: 31.5 us -> 41.6 us  [over_tiles(): sent = lax.ppermute(value, 'elem', [(i, i ^ mask) for i in range(tiles)])]
    ppermute x25, waiting for transfers between devices: 70.6 us -> 62.3 us  [over_tiles(): sent = lax.ppermute(value, 'elem', [(i, i ^ mask) for i in range(tiles)])]
    unnamed x41 -> x53, local copies, waits for them, and re-layouts: 9.63 us -> 11.1 us
  transfers between devices with their start and end apart: 66 -> 66, of which waited for: 32 -> 33; matrix products, arithmetic and copies ran while one was open for 2% -> 2% of each run, Pallas kernels for 14% -> 15%
where the time goes in v12:
time: 284 us; the launch traced here: 283 us
  starting transfers between devices  114 us (40%)
  waiting for transfers between devices  102 us (36%)
  Pallas kernels  47.1 us (17%)
  local copies, waits for them, and re-layouts  17.2 us (6%)
    ppermute x25, waiting for transfers between devices, over_tiles(): sent = lax.ppermute(value, 'elem', [(i, i ^ mask) for i in range(tiles)])  62.3 us
    pallas_call x32, Pallas kernels, call(): pl.pallas_call(kernel, out_shape=outs, in_specs=[pl.BlockSpec(memory_spac...  47.1 us
    ppermute x25, starting transfers between devices, over_tiles(): sent = lax.ppermute(value, 'elem', [(i, i ^ mask) for i in range(tiles)])  41.6 us
    ppermute x8, starting transfers between devices, multiply(): near[stage + 1, c] = lax.ppermute(out, 'elem', swap)  28.4 us
    ppermute x12, starting transfers between devices, send_on(): far[job] = lax.ppermute(near[job], 'elem', outward)  25.1 us
    ppermute x17, waiting for transfers between devices, to_group(): return lax.ppermute(value, 'orb', [(i, i ^ d) for i in range(groups)])  12.5 us
    ppermute x8, waiting for transfers between devices, multiply(): near[stage + 1, c] = lax.ppermute(out, 'elem', swap)  12.2 us
    unnamed x53, local copies, waits for them, and re-layouts  11.1 us
  transfers between devices with their start and end apart: 66, of which 33 were waited for; matrix products, arithmetic and copies ran while one was open for 2% of the time, Pallas kernels for 15%

profile of v12, /device:TPU:0, one launch (start us, length us, event | category | flops | bytes accessed | tf_op | source)
XLA Modules:
  0.0 282.9 jit_solution(10368026997355678301)
XLA Ops:
  1.5 3.0 %collective-permute-start = (bf16[768,256]{1,0:T(8,128)(2,1)S(1)}, bf16[768,256]{1,0:T(8,128)(2,1)S(1)}, u32[]{:S(2)}, u32[]{:S(2)}) collective-permute-start(bf16[768,256]{1,0:T(8,128)(2,1)S(1)} %get-tuple-element.503.field_ref.refs_0_), channel_id=1, source_target_pairs={{0,4},{4,0},{8,12},{12,8},{16,20},{20,16},{24,28},{28,24},{1,5},{5... | collective-permute-start | bytes 1179656 | tf_op jit(solution)/shard_map/ppermute | solution.py:311
  4.5 2.2 slice_bitcast_fusion
  8.1 2.3 concatenate.30.blocks_ref
  10.5 3.9 %collective-permute-done.near_ref = bf16[768,256]{1,0:T(8,128)(2,1)S(1)} collective-permute-done((bf16[768,256]{1,0:T(8,128)(2,1)S(1)}, bf16[768,256]{1,0:T(8,128)(2,1)S(1)}, u32[]{:S(2)}, u32[]{:S(2)}) %collective-permute-start) | collective-permute-done | bytes 393248 | tf_op jit(solution)/shard_map/ppermute | solution.py:311
  14.5 2.1 collective-permute-start.1
  16.6 3.5 %collective-permute-start.4 = (bf16[768,256]{1,0:T(8,128)(2,1)S(1)}, bf16[768,256]{1,0:T(8,128)(2,1)S(1)}, u32[]{:S(2)}, u32[]{:S(2)}) collective-permute-start(bf16[768,256]{1,0:T(8,128)(2,1)S(1)} %get-tuple-element.268.field_ref.refs_0_), channel_id=1, source_target_pairs={{0,4},{4,0},{8,12},{12,8},{16,20},{20,16},{24,28},{28,24},{1,5},{5... | collective-permute-start | bytes 1179656 | tf_op jit(solution)/shard_map/ppermute | solution.py:316
  20.1 2.8 collective-permute-done.2.near_ref
  22.9 2.1 collective-permute-start.7
  25.0 3.5 %collective-permute-start.6 = (bf16[768,256]{1,0:T(8,128)(2,1)S(1)}, bf16[768,256]{1,0:T(8,128)(2,1)S(1)}, u32[]{:S(2)}, u32[]{:S(2)}) collective-permute-start(bf16[768,256]{1,0:T(8,128)(2,1)S(1)} %get-tuple-element.271.field_ref.refs_0_), channel_id=1, source_target_pairs={{0,4},{4,0},{8,12},{12,8},{16,20},{20,16},{24,28},{28,24},{1,5},{5... | collective-permute-start | bytes 1179656 | tf_op jit(solution)/shard_map/ppermute | solution.py:316
  31.3 2.1 collective-permute-start.5
  33.4 3.5 %collective-permute-start.3 = (bf16[768,256]{1,0:T(8,128)(2,1)S(1)}, bf16[768,256]{1,0:T(8,128)(2,1)S(1)}, u32[]{:S(2)}, u32[]{:S(2)}) collective-permute-start(bf16[768,256]{1,0:T(8,128)(2,1)S(1)} %get-tuple-element.267.field_ref), channel_id=1, source_target_pairs={{0,4},{4,0},{8,12},{12,8},{16,20},{20,16},{24,28},{28,24},{1,5},{5... | collective-permute-start | bytes 1179656 | tf_op jit(solution)/shard_map/ppermute | solution.py:367
  39.7 2.1 collective-permute-start.10
  41.9 3.5 %collective-permute-start.9 = (bf16[768,256]{1,0:T(8,128)(2,1)S(1)}, bf16[768,256]{1,0:T(8,128)(2,1)S(1)}, u32[]{:S(2)}, u32[]{:S(2)}) collective-permute-start(bf16[768,256]{1,0:T(8,128)(2,1)S(1)} %get-tuple-element.286.field_ref), channel_id=1, source_target_pairs={{0,4},{4,0},{8,12},{12,8},{16,20},{20,16},{24,28},{28,24},{1,5},{5... | collective-permute-start | bytes 1179656 | tf_op jit(solution)/shard_map/ppermute | solution.py:367
  48.2 2.1 collective-permute-start.8
  50.3 3.5 %collective-permute-start.12 = (bf16[768,256]{1,0:T(8,128)(2,1)S(1)}, bf16[768,256]{1,0:T(8,128)(2,1)S(1)}, u32[]{:S(2)}, u32[]{:S(2)}) collective-permute-start(bf16[768,256]{1,0:T(8,128)(2,1)S(1)} %get-tuple-element.298.field_ref), channel_id=1, source_target_pairs={{0,4},{4,0},{8,12},{12,8},{16,20},{20,16},{24,28},{28,24},{1,5},{5... | collective-permute-start | bytes 1179656 | tf_op jit(solution)/shard_map/ppermute | solution.py:367
  56.6 2.1 collective-permute-start.15
  58.7 3.5 %collective-permute-start.14 = (bf16[768,256]{1,0:T(8,128)(2,1)S(1)}, bf16[768,256]{1,0:T(8,128)(2,1)S(1)}, u32[]{:S(2)}, u32[]{:S(2)}) collective-permute-start(bf16[768,256]{1,0:T(8,128)(2,1)S(1)} %get-tuple-element.301.field_ref), channel_id=1, source_target_pairs={{0,4},{4,0},{8,12},{12,8},{16,20},{20,16},{24,28},{28,24},{1,5},{5... | collective-permute-start | bytes 1179656 | tf_op jit(solution)/shard_map/ppermute | solution.py:367
  65.0 2.1 collective-permute-start.13
  67.1 3.5 %collective-permute-start.11 = (bf16[768,256]{1,0:T(8,128)(2,1)S(1)}, bf16[768,256]{1,0:T(8,128)(2,1)S(1)}, u32[]{:S(2)}, u32[]{:S(2)}) collective-permute-start(bf16[768,256]{1,0:T(8,128)(2,1)S(1)} %product_1.4.field_ref), channel_id=1, source_target_pairs={{0,4},{4,0},{8,12},{12,8},{16,20},{20,16},{24,28},{28,24},{1,5},{5... | collective-permute-start | bytes 1179656 | tf_op jit(solution)/shard_map/ppermute | solution.py:367
  73.4 2.1 collective-permute-start.18
  75.6 3.5 %collective-permute-start.17 = (bf16[768,256]{1,0:T(8,128)(2,1)S(1)}, bf16[768,256]{1,0:T(8,128)(2,1)S(1)}, u32[]{:S(2)}, u32[]{:S(2)}) collective-permute-start(bf16[768,256]{1,0:T(8,128)(2,1)S(1)} %product_1.5.field_ref), channel_id=1, source_target_pairs={{0,4},{4,0},{8,12},{12,8},{16,20},{20,16},{24,28},{28,24},{1,5},{5... | collective-permute-start | bytes 1179656 | tf_op jit(solution)/shard_map/ppermute | solution.py:367
  81.9 2.1 collective-permute-start.16
  84.0 3.5 %collective-permute-start.20 = (bf16[768,256]{1,0:T(8,128)(2,1)S(1)}, bf16[768,256]{1,0:T(8,128)(2,1)S(1)}, u32[]{:S(2)}, u32[]{:S(2)}) collective-permute-start(bf16[768,256]{1,0:T(8,128)(2,1)S(1)} %product_1.6.field_ref), channel_id=1, source_target_pairs={{0,4},{4,0},{8,12},{12,8},{16,20},{20,16},{24,28},{28,24},{1,5},{5... | collective-permute-start | bytes 1179656 | tf_op jit(solution)/shard_map/ppermute | solution.py:367
  90.3 2.1 collective-permute-start.19
  92.4 3.5 %collective-permute-start.22 = (bf16[768,256]{1,0:T(8,128)(2,1)S(1)}, bf16[768,256]{1,0:T(8,128)(2,1)S(1)}, u32[]{:S(2)}, u32[]{:S(2)}) collective-permute-start(bf16[768,256]{1,0:T(8,128)(2,1)S(1)} %product_1.7.field_ref), channel_id=1, source_target_pairs={{0,4},{4,0},{8,12},{12,8},{16,20},{20,16},{24,28},{28,24},{1,5},{5... | collective-permute-start | bytes 1179656 | tf_op jit(solution)/shard_map/ppermute | solution.py:367
  98.7 2.1 collective-permute-start.21
  103.6 2.7 collective-permute-done.22.near_ref
  106.3 1.8 collective-permute-start.23
  114.2 4.5 %collective-permute-done.23.far_ref = bf16[768,256]{1,0:T(8,128)(2,1)} collective-permute-done((bf16[768,256]{1,0:T(8,128)(2,1)S(1)}, bf16[768,256]{1,0:T(8,128)(2,1)}, u32[]{:S(2)}, u32[]{:S(2)}) %collective-permute-start.23) | collective-permute-done | bytes 393248 | tf_op jit(solution)/shard_map/ppermute | solution.py:325
  123.2 1.8 product_2.7.refs_3_.refs_4_.refs_13_
  124.9 3.0 %gram_own.1 = (bf16[384,1024]{1,0:T(8,128)(2,1)S(1)}, bf16[384,1024]{1,0:T(8,128)(2,1)}) custom-call(s32[2]{0:T(128)S(1)} %get-tuple-element.512.where_ref, bf16[768,256]{1,0:T(8,128)(2,1)S(1)} %get-tuple-element.324.refs_0_.refs_1_.refs_10_, bf16[768,256]{1,0:T(8,128)(2,1)S(1)} %get-tuple-element.335.refs_1_.refs_2_.refs_11_, ...), custom_call_target="tpu_custom_call" | custom-call | flops 1024 | bytes 5242880 | tf_op jit(solution)/shard_map/gram_own/pallas_call | solution.py:96
  134.6 4.8 %collective-permute-done.32.refs_7_.refs_9_.refs_4_ = bf16[784,256]{1,0:T(8,128)(2,1)S(1)} collective-permute-done((bf16[784,256]{1,0:T(8,128)(2,1)S(1)}, bf16[784,256]{1,0:T(8,128)(2,1)S(1)}, u32[]{:S(2)}, u32[]{:S(2)}) %collective-permute-start.32) | collective-permute-done | bytes 401440 | tf_op jit(solution)/shard_map/ppermute | solution.py:298
  143.3 2.3 gram_pair.3
  145.6 1.9 collective-permute-done.35.refs_1_
  148.2 2.5 gram_pair.4
  151.6 4.4 %collective-permute-start.38 = (bf16[192,1024]{1,0:T(8,128)(2,1)S(1)}, bf16[192,1024]{1,0:T(8,128)(2,1)S(1)}, u32[]{:S(2)}, u32[]{:S(2)}) collective-permute-start(bf16[192,1024]{1,0:T(8,128)(2,1)S(1)} %sum_hop.8), channel_id=1, source_target_pairs={{0,16},{4,20},{8,24},{12,28},{16,0},{20,4},{24,8},{28,12},{1,17},{... | collective-permute-start | bytes 1179656 | tf_op jit(solution)/shard_map/ppermute | solution.py:394
  156.0 2.1 gram_pair.5
  158.5 8.6 %collective-permute-done.39.refs_1_ = bf16[256,1024]{1,0:T(8,128)(2,1)S(1)} collective-permute-done((bf16[256,1024]{1,0:T(8,128)(2,1)S(1)}, bf16[256,1024]{1,0:T(8,128)(2,1)S(1)}, u32[]{:S(2)}, u32[]{:S(2)}) %collective-permute-start.39) | collective-permute-done | bytes 524320 | tf_op jit(solution)/shard_map/ppermute | solution.py:394
  167.7 3.4 %collective-permute-done.38.refs_2_ = bf16[192,1024]{1,0:T(8,128)(2,1)S(1)} collective-permute-done((bf16[192,1024]{1,0:T(8,128)(2,1)S(1)}, bf16[192,1024]{1,0:T(8,128)(2,1)S(1)}, u32[]{:S(2)}, u32[]{:S(2)}) %collective-permute-start.38) | collective-permute-done | bytes 393248 | tf_op jit(solution)/shard_map/ppermute | solution.py:394
  172.5 2.1 collective-permute-start.40
  174.5 1.6 collective-permute-start.45
  176.2 3.4 %collective-permute-done.42.refs_3_ = bf16[96,1024]{1,0:T(8,128)(2,1)S(1)} collective-permute-done((bf16[96,1024]{1,0:T(8,128)(2,1)S(1)}, bf16[96,1024]{1,0:T(8,128)(2,1)S(1)}, u32[]{:S(2)}, u32[]{:S(2)}) %collective-permute-start.42) | collective-permute-done | bytes 196640 | tf_op jit(solution)/shard_map/ppermute | solution.py:394
  180.3 5.8 %collective-permute-done.40.refs_2_ = bf16[144,1024]{1,0:T(8,128)(2,1)S(1)} collective-permute-done((bf16[144,1024]{1,0:T(8,128)(2,1)S(1)}, bf16[144,1024]{1,0:T(8,128)(2,1)S(1)}, u32[]{:S(2)}, u32[]{:S(2)}) %collective-permute-start.40) | collective-permute-done | bytes 294944 | tf_op jit(solution)/shard_map/ppermute | solution.py:394
  189.6 2.4 collective-permute-start.46
  192.6 11.1 %collective-permute-done.46.refs_3_ = bf16[64,1024]{1,0:T(8,128)(2,1)S(1)} collective-permute-done((bf16[64,1024]{1,0:T(8,128)(2,1)S(1)}, bf16[64,1024]{1,0:T(8,128)(2,1)S(1)}, u32[]{:S(2)}, u32[]{:S(2)}) %collective-permute-start.46) | collective-permute-done | bytes 131104 | tf_op jit(solution)/shard_map/ppermute | solution.py:394
  206.5 3.0 %collective-permute-start.49 = (bf16[64,1024]{1,0:T(8,128)(2,1)S(1)}, bf16[64,1024]{1,0:T(8,128)(2,1)S(1)}, u32[]{:S(2)}, u32[]{:S(2)}) collective-permute-start(bf16[64,1024]{1,0:T(8,128)(2,1)S(1)} %sum_last.6), channel_id=1, source_target_pairs={{0,16},{4,20},{8,24},{12,28},{16,0},{20,4},{24,8},{28,12},{1,17},{... | collective-permute-start | bytes 393224 | tf_op jit(solution)/shard_map/ppermute | solution.py:394
  209.5 4.1 %collective-permute-start.51 = (bf16[96,1024]{1,0:T(8,128)(2,1)S(1)}, bf16[96,1024]{1,0:T(8,128)(2,1)S(1)}, u32[]{:S(2)}, u32[]{:S(2)}) collective-permute-start(bf16[96,1024]{1,0:T(8,128)(2,1)S(1)} %sum_last.5), channel_id=1, source_target_pairs={{0,8},{4,12},{8,0},{12,4},{16,24},{20,28},{24,16},{28,20},{1,9},{5... | collective-permute-start | bytes 589832 | tf_op jit(solution)/shard_map/ppermute | solution.py:394
  214.5 2.4 collective-permute-done.48
  217.0 2.2 collective-permute-done.49
  219.2 3.1 %collective-permute-start.56 = (bf16[128,1024]{1,0:T(8,128)(2,1)S(1)}, bf16[128,1024]{1,0:T(8,128)(2,1)S(1)}, u32[]{:S(2)}, u32[]{:S(2)}) collective-permute-start(bf16[128,1024]{1,0:T(8,128)(2,1)S(1)} %pad_maximum_fusion.6), channel_id=1, source_target_pairs={{0,4},{4,0},{8,12},{12,8},{16,20},{20,16},{24,28},{28,24},{1,5},{5... | collective-permute-start | bytes 786440 | tf_op jit(solution)/shard_map/ppermute | solution.py:394
  222.9 2.3 collective-permute-start.61
  225.3 3.0 %collective-permute-start.57 = (bf16[128,1024]{1,0:T(8,128)(2,1)S(1)}, bf16[128,1024]{1,0:T(8,128)(2,1)S(1)}, u32[]{:S(2)}, u32[]{:S(2)}) collective-permute-start(bf16[128,1024]{1,0:T(8,128)(2,1)S(1)} %pad_maximum_fusion.7), channel_id=1, source_target_pairs={{0,8},{4,12},{8,0},{12,4},{16,24},{20,28},{24,16},{28,20},{1,9},{5... | collective-permute-start | bytes 786440 | tf_op jit(solution)/shard_map/ppermute | solution.py:394
  228.3 3.3 %collective-permute-done.52 = bf16[128,1024]{1,0:T(8,128)(2,1)S(1)} collective-permute-done((bf16[128,1024]{1,0:T(8,128)(2,1)S(1)}, bf16[128,1024]{1,0:T(8,128)(2,1)S(1)}, u32[]{:S(2)}, u32[]{:S(2)}) %collective-permute-start.52) | collective-permute-done | bytes 262176 | tf_op jit(solution)/shard_map/ppermute | solution.py:394
  231.7 1.7 collective-permute-start.53
  236.4 3.7 %collective-permute-start.63 = (bf16[256,1024]{1,0:T(8,128)(2,1)S(1)}, bf16[256,1024]{1,0:T(8,128)(2,1)S(1)}, u32[]{:S(2)}, u32[]{:S(2)}) collective-permute-start(bf16[256,1024]{1,0:T(8,128)(2,1)S(1)} %pad_maximum_fusion.3.refs_6_), channel_id=1, source_target_pairs={{0,4},{4,0},{8,12},{12,8},{16,20},{20,16},{24,28},{28,24},{1,5},{5... | collective-permute-start | bytes 1572872 | tf_op jit(solution)/shard_map/ppermute | solution.py:394
  240.1 2.5 collective-permute-start.58
  245.4 2.5 collective-permute-done.59.refs_7_
  247.9 7.1 %collective-permute-done.63.refs_7_ = bf16[256,1024]{1,0:T(8,128)(2,1)S(1)} collective-permute-done((bf16[256,1024]{1,0:T(8,128)(2,1)S(1)}, bf16[256,1024]{1,0:T(8,128)(2,1)S(1)}, u32[]{:S(2)}, u32[]{:S(2)}) %collective-permute-start.63) | collective-permute-done | bytes 524320 | tf_op jit(solution)/shard_map/ppermute | solution.py:394
  255.5 4.0 %collective-permute-done.64.refs_8_ = bf16[256,1024]{1,0:T(8,128)(2,1)S(1)} collective-permute-done((bf16[256,1024]{1,0:T(8,128)(2,1)S(1)}, bf16[256,1024]{1,0:T(8,128)(2,1)S(1)}, u32[]{:S(2)}, u32[]{:S(2)}) %collective-permute-start.64) | collective-permute-done | bytes 524320 | tf_op jit(solution)/shard_map/ppermute | solution.py:298
  259.4 9.6 %collective-permute-done.62.refs_6_ = bf16[384,1024]{1,0:T(8,128)(2,1)S(1)} collective-permute-done((bf16[384,1024]{1,0:T(8,128)(2,1)S(1)}, bf16[384,1024]{1,0:T(8,128)(2,1)S(1)}, u32[]{:S(2)}, u32[]{:S(2)}) %collective-permute-start.62) | collective-permute-done | bytes 786464 | tf_op jit(solution)/shard_map/ppermute | solution.py:394
  269.0 3.0 %mix_pair.3.refs_0_ = f32[768,1024]{1,0:T(8,128)S(1)} custom-call(s32[2]{0:T(128)S(1)} %copy-done.22, bf16[768,256]{1,0:T(8,128)(2,1)S(1)} %copy-done.11, bf16[768,256]{1,0:T(8,128)(2,1)} %collective-permute-done.30.refs_5_.refs_1_, bf16[768,256]{1,0:T(8,128)(2,1)S(1)} %copy-done.13, bf16[784,256]{1,0:T(8,128)(2,1)S(1)} %copy-done.1, ...), custom_call_target="tpu_custom_call" | custom-call | flops 1024 | bytes 5242880 | tf_op jit(solution)/shard_map/mix_pair/pallas_call | solution.py:96
  272.1 3.4 %mix_pair.4.refs_0_ = f32[768,1024]{1,0:T(8,128)S(1)} custom-call(s32[2]{0:T(128)S(1)} %pad_add_fusion.1.where_ref, f32[768,1024]{1,0:T(8,128)S(1)} %mix_pair.3.refs_0_, bf16[768,256]{1,0:T(8,128)(2,1)} %collective-permute-done.25.refs_4_.refs_1_, bf16[768,256]{1,0:T(8,128)(2,1)S(1)} %copy-done.4, ...), custom_call_target="tpu_custom_call", output_to_operand_aliasing={{}: (1, {})} | custom-call | flops 1024 | bytes 5242880 | tf_op jit(solution)/shard_map/mix_pair/pallas_call | solution.py:96
  275.5 2.6 mix_own.1.refs_1_
  278.1 4.8 %mix_pair.5 = bf16[768,1024]{1,0:T(8,128)(2,1)} custom-call(s32[2]{0:T(128)S(1)} %pad_add_fusion.1.where_ref, f32[8,128]{1,0:T(8,128)S(1)} %get-tuple-element.454.refs_4_.refs_0_, f32[768,1024]{1,0:T(8,128)S(1)} %mix_own.1.refs_1_, bf16[768,256]{1,0:T(8,128)(2,1)} %collective-permute-done.26.refs_4_.refs_2_, ...), custom_call_target="tpu_custom_call" | custom-call | flops 1024 | bytes 5242880 | tf_op jit(solution)/shard_map/mix_pair/pallas_call | solution.py:96
  (174 shorter events, 71.1 us)
Async XLA Ops:
  1.5 13.0 %collective-permute-start = (bf16[768,256]{1,0:T(8,128)(2,1)S(1)}, bf16[768,256]{1,0:T(8,128)(2,1)S(1)}, u32[]{:S(2)}, u32[]{:S(2)}) collective-permute-start(bf16[768,256]{1,0:T(8,128)(2,1)S(1)} %get-tuple-element.503.field_ref.refs_0_), channel_id=1, source_target_pairs={{0,4},{4,0},{8,12},{12,8},{16,20},{20,16},{24,28},{28,24},{1,5},{5... | collective-permute-start | bytes 1179656 | tf_op jit(solution)/shard_map/ppermute | solution.py:311
  10.5 12.4 %collective-permute-start.2 = (bf16[768,256]{1,0:T(8,128)(2,1)S(1)}, bf16[768,256]{1,0:T(8,128)(2,1)S(1)}, u32[]{:S(2)}, u32[]{:S(2)}) collective-permute-start(bf16[768,256]{1,0:T(8,128)(2,1)S(1)} %get-tuple-element.260.field_ref.refs_0_), channel_id=1, source_target_pairs={{0,4},{4,0},{8,12},{12,8},{16,20},{20,16},{24,28},{28,24},{1,5},{5... | collective-permute-start | bytes 1179656 | tf_op jit(solution)/shard_map/ppermute | solution.py:316
  14.5 14.1 %collective-permute-start.1 = (bf16[768,256]{1,0:T(8,128)(2,1)S(1)}, bf16[768,256]{1,0:T(8,128)(2,1)S(1)}, u32[]{:S(2)}, u32[]{:S(2)}) collective-permute-start(bf16[768,256]{1,0:T(8,128)(2,1)S(1)} %collective-permute-done.near_ref), channel_id=1, source_target_pairs={{0,8},{4,28},{8,16},{12,4},{16,24},{20,12},{24,0},{28,20},{1,9},{5... | collective-permute-start | bytes 1179656 | tf_op jit(solution)/shard_map/ppermute | solution.py:325
  16.6 14.7 %collective-permute-start.4 = (bf16[768,256]{1,0:T(8,128)(2,1)S(1)}, bf16[768,256]{1,0:T(8,128)(2,1)S(1)}, u32[]{:S(2)}, u32[]{:S(2)}) collective-permute-start(bf16[768,256]{1,0:T(8,128)(2,1)S(1)} %get-tuple-element.268.field_ref.refs_0_), channel_id=1, source_target_pairs={{0,4},{4,0},{8,12},{12,8},{16,20},{20,16},{24,28},{28,24},{1,5},{5... | collective-permute-start | bytes 1179656 | tf_op jit(solution)/shard_map/ppermute | solution.py:316
  22.9 14.1 %collective-permute-start.7 = (bf16[768,256]{1,0:T(8,128)(2,1)S(1)}, bf16[768,256]{1,0:T(8,128)(2,1)S(1)}, u32[]{:S(2)}, u32[]{:S(2)}) collective-permute-start(bf16[768,256]{1,0:T(8,128)(2,1)S(1)} %collective-permute-done.2.near_ref), channel_id=1, source_target_pairs={{0,8},{4,28},{8,16},{12,4},{16,24},{20,12},{24,0},{28,20},{1,9},{5... | collective-permute-start | bytes 1179656 | tf_op jit(solution)/shard_map/ppermute | solution.py:325
  25.0 14.7 %collective-permute-start.6 = (bf16[768,256]{1,0:T(8,128)(2,1)S(1)}, bf16[768,256]{1,0:T(8,128)(2,1)S(1)}, u32[]{:S(2)}, u32[]{:S(2)}) collective-permute-start(bf16[768,256]{1,0:T(8,128)(2,1)S(1)} %get-tuple-element.271.field_ref.refs_0_), channel_id=1, source_target_pairs={{0,4},{4,0},{8,12},{12,8},{16,20},{20,16},{24,28},{28,24},{1,5},{5... | collective-permute-start | bytes 1179656 | tf_op jit(solution)/shard_map/ppermute | solution.py:316
  31.3 14.1 %collective-permute-start.5 = (bf16[768,256]{1,0:T(8,128)(2,1)S(1)}, bf16[768,256]{1,0:T(8,128)(2,1)S(1)}, u32[]{:S(2)}, u32[]{:S(2)}) collective-permute-start(bf16[768,256]{1,0:T(8,128)(2,1)S(1)} %collective-permute-done.4.near_ref), channel_id=1, source_target_pairs={{0,8},{4,28},{8,16},{12,4},{16,24},{20,12},{24,0},{28,20},{1,9},{5... | collective-permute-start | bytes 1179656 | tf_op jit(solution)/shard_map/ppermute | solution.py:325
  33.4 14.7 %collective-permute-start.3 = (bf16[768,256]{1,0:T(8,128)(2,1)S(1)}, bf16[768,256]{1,0:T(8,128)(2,1)S(1)}, u32[]{:S(2)}, u32[]{:S(2)}) collective-permute-start(bf16[768,256]{1,0:T(8,128)(2,1)S(1)} %get-tuple-element.267.field_ref), channel_id=1, source_target_pairs={{0,4},{4,0},{8,12},{12,8},{16,20},{20,16},{24,28},{28,24},{1,5},{5... | collective-permute-start | bytes 1179656 | tf_op jit(solution)/shard_map/ppermute | solution.py:367
  39.7 14.1 %collective-permute-start.10 = (bf16[768,256]{1,0:T(8,128)(2,1)S(1)}, bf16[768,256]{1,0:T(8,128)(2,1)S(1)}, u32[]{:S(2)}, u32[]{:S(2)}) collective-permute-start(bf16[768,256]{1,0:T(8,128)(2,1)S(1)} %collective-permute-done.6.near_ref), channel_id=1, source_target_pairs={{0,8},{4,28},{8,16},{12,4},{16,24},{20,12},{24,0},{28,20},{1,9},{5... | collective-permute-start | bytes 1179656 | tf_op jit(solution)/shard_map/ppermute | solution.py:325
  41.9 14.7 %collective-permute-start.9 = (bf16[768,256]{1,0:T(8,128)(2,1)S(1)}, bf16[768,256]{1,0:T(8,128)(2,1)S(1)}, u32[]{:S(2)}, u32[]{:S(2)}) collective-permute-start(bf16[768,256]{1,0:T(8,128)(2,1)S(1)} %get-tuple-element.286.field_ref), channel_id=1, source_target_pairs={{0,4},{4,0},{8,12},{12,8},{16,20},{20,16},{24,28},{28,24},{1,5},{5... | collective-permute-start | bytes 1179656 | tf_op jit(solution)/shard_map/ppermute | solution.py:367
  48.2 14.1 %collective-permute-start.8 = (bf16[768,256]{1,0:T(8,128)(2,1)S(1)}, bf16[768,256]{1,0:T(8,128)(2,1)S(1)}, u32[]{:S(2)}, u32[]{:S(2)}) collective-permute-start(bf16[768,256]{1,0:T(8,128)(2,1)S(1)} %collective-permute-done.3.near_ref), channel_id=1, source_target_pairs={{0,8},{4,28},{8,16},{12,4},{16,24},{20,12},{24,0},{28,20},{1,9},{5... | collective-permute-start | bytes 1179656 | tf_op jit(solution)/shard_map/ppermute | solution.py:325
  50.3 14.7 %collective-permute-start.12 = (bf16[768,256]{1,0:T(8,128)(2,1)S(1)}, bf16[768,256]{1,0:T(8,128)(2,1)S(1)}, u32[]{:S(2)}, u32[]{:S(2)}) collective-permute-start(bf16[768,256]{1,0:T(8,128)(2,1)S(1)} %get-tuple-element.298.field_ref), channel_id=1, source_target_pairs={{0,4},{4,0},{8,12},{12,8},{16,20},{20,16},{24,28},{28,24},{1,5},{5... | collective-permute-start | bytes 1179656 | tf_op jit(solution)/shard_map/ppermute | solution.py:367
  56.6 14.1 %collective-permute-start.15 = (bf16[768,256]{1,0:T(8,128)(2,1)S(1)}, bf16[768,256]{1,0:T(8,128)(2,1)S(1)}, u32[]{:S(2)}, u32[]{:S(2)}) collective-permute-start(bf16[768,256]{1,0:T(8,128)(2,1)S(1)} %collective-permute-done.9.near_ref), channel_id=1, source_target_pairs={{0,8},{4,28},{8,16},{12,4},{16,24},{20,12},{24,0},{28,20},{1,9},{5... | collective-permute-start | bytes 1179656 | tf_op jit(solution)/shard_map/ppermute | solution.py:325
  58.7 14.7 %collective-permute-start.14 = (bf16[768,256]{1,0:T(8,128)(2,1)S(1)}, bf16[768,256]{1,0:T(8,128)(2,1)S(1)}, u32[]{:S(2)}, u32[]{:S(2)}) collective-permute-start(bf16[768,256]{1,0:T(8,128)(2,1)S(1)} %get-tuple-element.301.field_ref), channel_id=1, source_target_pairs={{0,4},{4,0},{8,12},{12,8},{16,20},{20,16},{24,28},{28,24},{1,5},{5... | collective-permute-start | bytes 1179656 | tf_op jit(solution)/shard_map/ppermute | solution.py:367
  65.0 14.1 %collective-permute-start.13 = (bf16[768,256]{1,0:T(8,128)(2,1)S(1)}, bf16[768,256]{1,0:T(8,128)(2,1)S(1)}, u32[]{:S(2)}, u32[]{:S(2)}) collective-permute-start(bf16[768,256]{1,0:T(8,128)(2,1)S(1)} %collective-permute-done.12.near_ref), channel_id=1, source_target_pairs={{0,8},{4,28},{8,16},{12,4},{16,24},{20,12},{24,0},{28,20},{1,9},{5... | collective-permute-start | bytes 1179656 | tf_op jit(solution)/shard_map/ppermute | solution.py:325
  67.1 14.7 %collective-permute-start.11 = (bf16[768,256]{1,0:T(8,128)(2,1)S(1)}, bf16[768,256]{1,0:T(8,128)(2,1)S(1)}, u32[]{:S(2)}, u32[]{:S(2)}) collective-permute-start(bf16[768,256]{1,0:T(8,128)(2,1)S(1)} %product_1.4.field_ref), channel_id=1, source_target_pairs={{0,4},{4,0},{8,12},{12,8},{16,20},{20,16},{24,28},{28,24},{1,5},{5... | collective-permute-start | bytes 1179656 | tf_op jit(solution)/shard_map/ppermute | solution.py:367
  73.4 14.1 %collective-permute-start.18 = (bf16[768,256]{1,0:T(8,128)(2,1)S(1)}, bf16[768,256]{1,0:T(8,128)(2,1)S(1)}, u32[]{:S(2)}, u32[]{:S(2)}) collective-permute-start(bf16[768,256]{1,0:T(8,128)(2,1)S(1)} %collective-permute-done.14.near_ref), channel_id=1, source_target_pairs={{0,8},{4,28},{8,16},{12,4},{16,24},{20,12},{24,0},{28,20},{1,9},{5... | collective-permute-start | bytes 1179656 | tf_op jit(solution)/shard_map/ppermute | solution.py:325
  75.6 14.7 %collective-permute-start.17 = (bf16[768,256]{1,0:T(8,128)(2,1)S(1)}, bf16[768,256]{1,0:T(8,128)(2,1)S(1)}, u32[]{:S(2)}, u32[]{:S(2)}) collective-permute-start(bf16[768,256]{1,0:T(8,128)(2,1)S(1)} %product_1.5.field_ref), channel_id=1, source_target_pairs={{0,4},{4,0},{8,12},{12,8},{16,20},{20,16},{24,28},{28,24},{1,5},{5... | collective-permute-start | bytes 1179656 | tf_op jit(solution)/shard_map/ppermute | solution.py:367
  81.9 14.1 %collective-permute-start.16 = (bf16[768,256]{1,0:T(8,128)(2,1)S(1)}, bf16[768,256]{1,0:T(8,128)(2,1)S(1)}, u32[]{:S(2)}, u32[]{:S(2)}) collective-permute-start(bf16[768,256]{1,0:T(8,128)(2,1)S(1)} %collective-permute-done.11.near_ref), channel_id=1, source_target_pairs={{0,8},{4,28},{8,16},{12,4},{16,24},{20,12},{24,0},{28,20},{1,9},{5... | collective-permute-start | bytes 1179656 | tf_op jit(solution)/shard_map/ppermute | solution.py:325
  84.0 14.7 %collective-permute-start.20 = (bf16[768,256]{1,0:T(8,128)(2,1)S(1)}, bf16[768,256]{1,0:T(8,128)(2,1)S(1)}, u32[]{:S(2)}, u32[]{:S(2)}) collective-permute-start(bf16[768,256]{1,0:T(8,128)(2,1)S(1)} %product_1.6.field_ref), channel_id=1, source_target_pairs={{0,4},{4,0},{8,12},{12,8},{16,20},{20,16},{24,28},{28,24},{1,5},{5... | collective-permute-start | bytes 1179656 | tf_op jit(solution)/shard_map/ppermute | solution.py:367
  90.3 12.0 %collective-permute-start.19 = (bf16[768,256]{1,0:T(8,128)(2,1)S(1)}, bf16[768,256]{1,0:T(8,128)(2,1)S(1)}, u32[]{:S(2)}, u32[]{:S(2)}) collective-permute-start(bf16[768,256]{1,0:T(8,128)(2,1)S(1)} %collective-permute-done.17.near_ref), channel_id=1, source_target_pairs={{0,8},{4,28},{8,16},{12,4},{16,24},{20,12},{24,0},{28,20},{1,9},{5... | collective-permute-start | bytes 1179656 | tf_op jit(solution)/shard_map/ppermute | solution.py:325
  92.4 13.9 %collective-permute-start.22 = (bf16[768,256]{1,0:T(8,128)(2,1)S(1)}, bf16[768,256]{1,0:T(8,128)(2,1)S(1)}, u32[]{:S(2)}, u32[]{:S(2)}) collective-permute-start(bf16[768,256]{1,0:T(8,128)(2,1)S(1)} %product_1.7.field_ref), channel_id=1, source_target_pairs={{0,4},{4,0},{8,12},{12,8},{16,20},{20,16},{24,28},{28,24},{1,5},{5... | collective-permute-start | bytes 1179656 | tf_op jit(solution)/shard_map/ppermute | solution.py:367
  98.7 11.3 %collective-permute-start.21 = (bf16[768,256]{1,0:T(8,128)(2,1)S(1)}, bf16[768,256]{1,0:T(8,128)(2,1)S(1)}, u32[]{:S(2)}, u32[]{:S(2)}) collective-permute-start(bf16[768,256]{1,0:T(8,128)(2,1)S(1)} %collective-permute-done.20.near_ref), channel_id=1, source_target_pairs={{0,8},{4,28},{8,16},{12,4},{16,24},{20,12},{24,0},{28,20},{1,9},{5... | collective-permute-start | bytes 1179656 | tf_op jit(solution)/shard_map/ppermute | solution.py:325
  100.8 10.5 %collective-permute-start.25 = (bf16[768,256]{1,0:T(8,128)(2,1)S(1)}, bf16[768,256]{1,0:T(8,128)(2,1)}, u32[]{:S(2)}, u32[]{:S(2)}) collective-permute-start(bf16[768,256]{1,0:T(8,128)(2,1)S(1)} %get-tuple-element.324.refs_0_.refs_1_.refs_10_), channel_id=1, source_target_pairs={{0,2},{1,3},{2,0},{3,1},{4,6},{5,7},{6,4},{7,5},{8,10},{9,11},{10,... | collective-permute-start | bytes 1179656 | tf_op jit(solution)/shard_map/ppermute | solution.py:298
  102.3 11.1 %collective-permute-start.24 = (bf16[768,256]{1,0:T(8,128)(2,1)S(1)}, bf16[768,256]{1,0:T(8,128)(2,1)S(1)}, u32[]{:S(2)}, u32[]{:S(2)}) collective-permute-start(bf16[768,256]{1,0:T(8,128)(2,1)S(1)} %get-tuple-element.324.refs_0_.refs_1_.refs_10_), channel_id=1, source_target_pairs={{0,1},{1,0},{2,3},{3,2},{4,5},{5,4},{6,7},{7,6},{8,9},{9,8},{10,11... | collective-permute-start | bytes 1179656 | tf_op jit(solution)/shard_map/ppermute | solution.py:298
  106.3 12.3 %collective-permute-start.23 = (bf16[768,256]{1,0:T(8,128)(2,1)S(1)}, bf16[768,256]{1,0:T(8,128)(2,1)}, u32[]{:S(2)}, u32[]{:S(2)}) collective-permute-start(bf16[768,256]{1,0:T(8,128)(2,1)S(1)} %collective-permute-done.22.near_ref), channel_id=1, source_target_pairs={{0,8},{4,28},{8,16},{12,4},{16,24},{20,12},{24,0},{28,20},{1,9},{5... | collective-permute-start | bytes 1179656 | tf_op jit(solution)/shard_map/ppermute | solution.py:325
  108.1 20.3 %collective-permute-start.27 = (bf16[768,256]{1,0:T(8,128)(2,1)S(1)}, bf16[768,256]{1,0:T(8,128)(2,1)S(1)}, u32[]{:S(2)}, u32[]{:S(2)}) collective-permute-start(bf16[768,256]{1,0:T(8,128)(2,1)S(1)} %get-tuple-element.335.refs_1_.refs_2_.refs_11_), channel_id=1, source_target_pairs={{0,2},{1,3},{2,0},{3,1},{4,6},{5,7},{6,4},{7,5},{8,10},{9,11},{10,... | collective-permute-start | bytes 1179656 | tf_op jit(solution)/shard_map/ppermute | solution.py:298
  110.0 18.4 %collective-permute-start.30 = (bf16[768,256]{1,0:T(8,128)(2,1)S(1)}, bf16[768,256]{1,0:T(8,128)(2,1)}, u32[]{:S(2)}, u32[]{:S(2)}) collective-permute-start(bf16[768,256]{1,0:T(8,128)(2,1)S(1)} %get-tuple-element.335.refs_1_.refs_2_.refs_11_), channel_id=1, source_target_pairs={{0,1},{1,0},{2,3},{3,2},{4,5},{5,4},{6,7},{7,6},{8,9},{9,8},{10,11... | collective-permute-start | bytes 1179656 | tf_op jit(solution)/shard_map/ppermute | solution.py:298
  111.3 17.1 %collective-permute-start.29 = (bf16[768,256]{1,0:T(8,128)(2,1)S(1)}, bf16[768,256]{1,0:T(8,128)(2,1)S(1)}, u32[]{:S(2)}, u32[]{:S(2)}) collective-permute-start(bf16[768,256]{1,0:T(8,128)(2,1)S(1)} %get-tuple-element.346.refs_2_.refs_3_.refs_12_), channel_id=1, source_target_pairs={{0,2},{1,3},{2,0},{3,1},{4,6},{5,7},{6,4},{7,5},{8,10},{9,11},{10,... | collective-permute-start | bytes 1179656 | tf_op jit(solution)/shard_map/ppermute | solution.py:298
  129.3 18.1 %collective-permute-start.35 = (bf16[384,1024]{1,0:T(8,128)(2,1)}, bf16[384,1024]{1,0:T(8,128)(2,1)S(1)}, u32[]{:S(2)}, u32[]{:S(2)}) collective-permute-start(bf16[384,1024]{1,0:T(8,128)(2,1)} %get-tuple-element.378), channel_id=1, source_target_pairs={{0,4},{4,0},{8,12},{12,8},{16,20},{20,16},{24,28},{28,24},{1,5},{5... | collective-permute-start | bytes 2359304 | tf_op jit(solution)/shard_map/ppermute | solution.py:394
  130.7 8.8 %collective-permute-start.32 = (bf16[784,256]{1,0:T(8,128)(2,1)S(1)}, bf16[784,256]{1,0:T(8,128)(2,1)S(1)}, u32[]{:S(2)}, u32[]{:S(2)}) collective-permute-start(bf16[784,256]{1,0:T(8,128)(2,1)S(1)} %product_2.7.refs_3_.refs_4_.refs_13_), channel_id=1, source_target_pairs={{0,2},{1,3},{2,0},{3,1},{4,6},{5,7},{6,4},{7,5},{8,10},{9,11},{10,... | collective-permute-start | bytes 1204232 | tf_op jit(solution)/shard_map/ppermute | solution.py:298
  132.2 7.8 %collective-permute-start.36 = (bf16[784,256]{1,0:T(8,128)(2,1)S(1)}, bf16[784,256]{1,0:T(8,128)(2,1)S(1)}, u32[]{:S(2)}, u32[]{:S(2)}) collective-permute-start(bf16[784,256]{1,0:T(8,128)(2,1)S(1)} %product_2.7.refs_3_.refs_4_.refs_13_), channel_id=1, source_target_pairs={{0,1},{1,0},{2,3},{3,2},{4,5},{5,4},{6,7},{7,6},{8,9},{9,8},{10,11... | collective-permute-start | bytes 1204232 | tf_op jit(solution)/shard_map/ppermute | solution.py:298
  139.4 8.7 %collective-permute-start.34 = (bf16[784,256]{1,0:T(8,128)(2,1)S(1)}, bf16[784,256]{1,0:T(8,128)(2,1)}, u32[]{:S(2)}, u32[]{:S(2)}) collective-permute-start(bf16[784,256]{1,0:T(8,128)(2,1)S(1)} %collective-permute-done.32.refs_7_.refs_9_.refs_4_), channel_id=1, source_target_pairs={{0,1},{1,0},{2,3},{3,2},{4,5},{5,4},{6,7},{7,6},{8,9},{9,8},{10,11... | collective-permute-start | bytes 1204232 | tf_op jit(solution)/shard_map/ppermute | solution.py:298
  139.5 8.7 %collective-permute-start.26 = (bf16[768,256]{1,0:T(8,128)(2,1)}, bf16[768,256]{1,0:T(8,128)(2,1)}, u32[]{:S(2)}, u32[]{:S(2)}) collective-permute-start(bf16[768,256]{1,0:T(8,128)(2,1)} %collective-permute-done.25.refs_4_.refs_1_), channel_id=1, source_target_pairs={{0,1},{1,0},{2,3},{3,2},{4,5},{5,4},{6,7},{7,6},{8,9},{9,8},{10,11... | collective-permute-start | bytes 1179656 | tf_op jit(solution)/shard_map/ppermute | solution.py:298
  140.0 8.2 %collective-permute-start.28 = (bf16[768,256]{1,0:T(8,128)(2,1)}, bf16[768,256]{1,0:T(8,128)(2,1)}, u32[]{:S(2)}, u32[]{:S(2)}) collective-permute-start(bf16[768,256]{1,0:T(8,128)(2,1)} %copy-done.2), channel_id=1, source_target_pairs={{0,1},{1,0},{2,3},{3,2},{4,5},{5,4},{6,7},{7,6},{8,9},{9,8},{10,11... | collective-permute-start | bytes 1179656 | tf_op jit(solution)/shard_map/ppermute | solution.py:298
  147.4 19.7 %collective-permute-start.39 = (bf16[256,1024]{1,0:T(8,128)(2,1)S(1)}, bf16[256,1024]{1,0:T(8,128)(2,1)S(1)}, u32[]{:S(2)}, u32[]{:S(2)}) collective-permute-start(bf16[256,1024]{1,0:T(8,128)(2,1)S(1)} %get-tuple-element.408), channel_id=1, source_target_pairs={{0,8},{4,12},{8,0},{12,4},{16,24},{20,28},{24,16},{28,20},{1,9},{5... | collective-permute-start | bytes 1572872 | tf_op jit(solution)/shard_map/ppermute | solution.py:394
  150.7 21.1 %collective-permute-start.37 = (bf16[272,1024]{1,0:T(8,128)(2,1)S(1)}, bf16[272,1024]{1,0:T(8,128)(2,1)S(1)}, u32[]{:S(2)}, u32[]{:S(2)}) collective-permute-start(bf16[272,1024]{1,0:T(8,128)(2,1)S(1)} %get-tuple-element.405), channel_id=1, source_target_pairs={{0,4},{4,0},{8,12},{12,8},{16,20},{20,16},{24,28},{28,24},{1,5},{5... | collective-permute-start | bytes 1671176 | tf_op jit(solution)/shard_map/ppermute | solution.py:394
  151.6 19.4 %collective-permute-start.38 = (bf16[192,1024]{1,0:T(8,128)(2,1)S(1)}, bf16[192,1024]{1,0:T(8,128)(2,1)S(1)}, u32[]{:S(2)}, u32[]{:S(2)}) collective-permute-start(bf16[192,1024]{1,0:T(8,128)(2,1)S(1)} %sum_hop.8), channel_id=1, source_target_pairs={{0,16},{4,20},{8,24},{12,28},{16,0},{20,4},{24,8},{28,12},{1,17},{... | collective-permute-start | bytes 1179656 | tf_op jit(solution)/shard_map/ppermute | solution.py:394
  158.1 21.5 %collective-permute-start.41 = (bf16[256,1024]{1,0:T(8,128)(2,1)S(1)}, bf16[256,1024]{1,0:T(8,128)(2,1)S(1)}, u32[]{:S(2)}, u32[]{:S(2)}) collective-permute-start(bf16[256,1024]{1,0:T(8,128)(2,1)S(1)} %get-tuple-element.431), channel_id=1, source_target_pairs={{0,4},{4,0},{8,12},{12,8},{16,20},{20,16},{24,28},{28,24},{1,5},{5... | collective-permute-start | bytes 1572872 | tf_op jit(solution)/shard_map/ppermute | solution.py:394
  171.7 7.9 %collective-permute-start.42 = (bf16[96,1024]{1,0:T(8,128)(2,1)S(1)}, bf16[96,1024]{1,0:T(8,128)(2,1)S(1)}, u32[]{:S(2)}, u32[]{:S(2)}) collective-permute-start(bf16[96,1024]{1,0:T(8,128)(2,1)S(1)} %sum_hop.10), channel_id=1, source_target_pairs={{0,8},{4,12},{8,0},{12,4},{16,24},{20,28},{24,16},{28,20},{1,9},{5... | collective-permute-start | bytes 589832 | tf_op jit(solution)/shard_map/ppermute | solution.py:394
  172.5 13.7 %collective-permute-start.40 = (bf16[144,1024]{1,0:T(8,128)(2,1)S(1)}, bf16[144,1024]{1,0:T(8,128)(2,1)S(1)}, u32[]{:S(2)}, u32[]{:S(2)}) collective-permute-start(bf16[144,1024]{1,0:T(8,128)(2,1)S(1)} %sum_hop.11), channel_id=1, source_target_pairs={{0,8},{4,12},{8,0},{12,4},{16,24},{20,28},{24,16},{28,20},{1,9},{5... | collective-permute-start | bytes 884744 | tf_op jit(solution)/shard_map/ppermute | solution.py:394
  174.5 13.4 %collective-permute-start.45 = (bf16[128,1024]{1,0:T(8,128)(2,1)S(1)}, bf16[128,1024]{1,0:T(8,128)(2,1)S(1)}, u32[]{:S(2)}, u32[]{:S(2)}) collective-permute-start(bf16[128,1024]{1,0:T(8,128)(2,1)S(1)} %sum_hop.9), channel_id=1, source_target_pairs={{0,4},{4,0},{8,12},{12,8},{16,20},{20,16},{24,28},{28,24},{1,5},{5... | collective-permute-start | bytes 786440 | tf_op jit(solution)/shard_map/ppermute | solution.py:394
  180.2 8.7 %collective-permute-start.44 = (bf16[128,1024]{1,0:T(8,128)(2,1)S(1)}, bf16[128,1024]{1,0:T(8,128)(2,1)S(1)}, u32[]{:S(2)}, u32[]{:S(2)}) collective-permute-start(bf16[128,1024]{1,0:T(8,128)(2,1)S(1)} %sum_hop.12), channel_id=1, source_target_pairs={{0,8},{4,12},{8,0},{12,4},{16,24},{20,28},{24,16},{28,20},{1,9},{5... | collective-permute-start | bytes 786440 | tf_op jit(solution)/shard_map/ppermute | solution.py:394
  186.8 16.8 %collective-permute-start.43 = (bf16[80,1024]{1,0:T(8,128)(2,1)S(1)}, bf16[80,1024]{1,0:T(8,128)(2,1)S(1)}, u32[]{:S(2)}, u32[]{:S(2)}) collective-permute-start(bf16[80,1024]{1,0:T(8,128)(2,1)S(1)} %sum_hop.13), channel_id=1, source_target_pairs={{0,16},{4,20},{8,24},{12,28},{16,0},{20,4},{24,8},{28,12},{1,17},{... | collective-permute-start | bytes 491528 | tf_op jit(solution)/shard_map/ppermute | solution.py:394
  189.6 14.1 %collective-permute-start.46 = (bf16[64,1024]{1,0:T(8,128)(2,1)S(1)}, bf16[64,1024]{1,0:T(8,128)(2,1)S(1)}, u32[]{:S(2)}, u32[]{:S(2)}) collective-permute-start(bf16[64,1024]{1,0:T(8,128)(2,1)S(1)} %sum_hop.15), channel_id=1, source_target_pairs={{0,16},{4,20},{8,24},{12,28},{16,0},{20,4},{24,8},{28,12},{1,17},{... | collective-permute-start | bytes 393224 | tf_op jit(solution)/shard_map/ppermute | solution.py:394
  192.0 13.8 %collective-permute-start.47 = (bf16[64,1024]{1,0:T(8,128)(2,1)S(1)}, bf16[64,1024]{1,0:T(8,128)(2,1)S(1)}, u32[]{:S(2)}, u32[]{:S(2)}) collective-permute-start(bf16[64,1024]{1,0:T(8,128)(2,1)S(1)} %sum_hop.14), channel_id=1, source_target_pairs={{0,16},{4,20},{8,24},{12,28},{16,0},{20,4},{24,8},{28,12},{1,17},{... | collective-permute-start | bytes 393224 | tf_op jit(solution)/shard_map/ppermute | solution.py:394
  205.0 11.9 %collective-permute-start.48 = (bf16[64,1024]{1,0:T(8,128)(2,1)S(1)}, bf16[64,1024]{1,0:T(8,128)(2,1)S(1)}, u32[]{:S(2)}, u32[]{:S(2)}) collective-permute-start(bf16[64,1024]{1,0:T(8,128)(2,1)S(1)} %sum_last.7), channel_id=1, source_target_pairs={{0,16},{4,20},{8,24},{12,28},{16,0},{20,4},{24,8},{28,12},{1,17},{... | collective-permute-start | bytes 393224 | tf_op jit(solution)/shard_map/ppermute | solution.py:394
  206.5 12.7 %collective-permute-start.49 = (bf16[64,1024]{1,0:T(8,128)(2,1)S(1)}, bf16[64,1024]{1,0:T(8,128)(2,1)S(1)}, u32[]{:S(2)}, u32[]{:S(2)}) collective-permute-start(bf16[64,1024]{1,0:T(8,128)(2,1)S(1)} %sum_last.6), channel_id=1, source_target_pairs={{0,16},{4,20},{8,24},{12,28},{16,0},{20,4},{24,8},{28,12},{1,17},{... | collective-permute-start | bytes 393224 | tf_op jit(solution)/shard_map/ppermute | solution.py:394
  209.5 13.4 %collective-permute-start.51 = (bf16[96,1024]{1,0:T(8,128)(2,1)S(1)}, bf16[96,1024]{1,0:T(8,128)(2,1)S(1)}, u32[]{:S(2)}, u32[]{:S(2)}) collective-permute-start(bf16[96,1024]{1,0:T(8,128)(2,1)S(1)} %sum_last.5), channel_id=1, source_target_pairs={{0,8},{4,12},{8,0},{12,4},{16,24},{20,28},{24,16},{28,20},{1,9},{5... | collective-permute-start | bytes 589832 | tf_op jit(solution)/shard_map/ppermute | solution.py:394
  213.6 8.7 %collective-permute-start.50 = (bf16[64,1024]{1,0:T(8,128)(2,1)S(1)}, bf16[64,1024]{1,0:T(8,128)(2,1)S(1)}, u32[]{:S(2)}, u32[]{:S(2)}) collective-permute-start(bf16[64,1024]{1,0:T(8,128)(2,1)S(1)} %get-tuple-element.467), channel_id=1, source_target_pairs={{0,16},{4,20},{8,24},{12,28},{16,0},{20,4},{24,8},{28,12},{1,17},{... | collective-permute-start | bytes 393224 | tf_op jit(solution)/shard_map/ppermute | solution.py:394
  216.9 14.7 %collective-permute-start.52 = (bf16[128,1024]{1,0:T(8,128)(2,1)S(1)}, bf16[128,1024]{1,0:T(8,128)(2,1)S(1)}, u32[]{:S(2)}, u32[]{:S(2)}) collective-permute-start(bf16[128,1024]{1,0:T(8,128)(2,1)S(1)} %pad_maximum_fusion.5), channel_id=1, source_target_pairs={{0,8},{4,12},{8,0},{12,4},{16,24},{20,28},{24,16},{28,20},{1,9},{5... | collective-permute-start | bytes 786440 | tf_op jit(solution)/shard_map/ppermute | solution.py:394
  219.2 14.2 %collective-permute-start.56 = (bf16[128,1024]{1,0:T(8,128)(2,1)S(1)}, bf16[128,1024]{1,0:T(8,128)(2,1)S(1)}, u32[]{:S(2)}, u32[]{:S(2)}) collective-permute-start(bf16[128,1024]{1,0:T(8,128)(2,1)S(1)} %pad_maximum_fusion.6), channel_id=1, source_target_pairs={{0,4},{4,0},{8,12},{12,8},{16,20},{20,16},{24,28},{28,24},{1,5},{5... | collective-permute-start | bytes 786440 | tf_op jit(solution)/shard_map/ppermute | solution.py:394
  222.9 17.2 %collective-permute-start.61 = (bf16[192,1024]{1,0:T(8,128)(2,1)S(1)}, bf16[192,1024]{1,0:T(8,128)(2,1)S(1)}, u32[]{:S(2)}, u32[]{:S(2)}) collective-permute-start(bf16[192,1024]{1,0:T(8,128)(2,1)S(1)} %pad_maximum_fusion.4), channel_id=1, source_target_pairs={{0,16},{4,20},{8,24},{12,28},{16,0},{20,4},{24,8},{28,12},{1,17},{... | collective-permute-start | bytes 1179656 | tf_op jit(solution)/shard_map/ppermute | solution.py:394
  225.3 11.1 %collective-permute-start.57 = (bf16[128,1024]{1,0:T(8,128)(2,1)S(1)}, bf16[128,1024]{1,0:T(8,128)(2,1)S(1)}, u32[]{:S(2)}, u32[]{:S(2)}) collective-permute-start(bf16[128,1024]{1,0:T(8,128)(2,1)S(1)} %pad_maximum_fusion.7), channel_id=1, source_target_pairs={{0,8},{4,12},{8,0},{12,4},{16,24},{20,28},{24,16},{28,20},{1,9},{5... | collective-permute-start | bytes 786440 | tf_op jit(solution)/shard_map/ppermute | solution.py:394
  231.7 12.1 %collective-permute-start.53 = (bf16[256,1024]{1,0:T(8,128)(2,1)S(1)}, bf16[256,1024]{1,0:T(8,128)(2,1)S(1)}, u32[]{:S(2)}, u32[]{:S(2)}) collective-permute-start(bf16[256,1024]{1,0:T(8,128)(2,1)S(1)} %pad_maximum_fusion.1.refs_4_), channel_id=1, source_target_pairs={{0,4},{4,0},{8,12},{12,8},{16,20},{20,16},{24,28},{28,24},{1,5},{5... | collective-permute-start | bytes 1572872 | tf_op jit(solution)/shard_map/ppermute | solution.py:394
  233.4 12.0 %collective-permute-start.54 = (bf16[256,1024]{1,0:T(8,128)(2,1)S(1)}, bf16[256,1024]{1,0:T(8,128)(2,1)S(1)}, u32[]{:S(2)}, u32[]{:S(2)}) collective-permute-start(bf16[256,1024]{1,0:T(8,128)(2,1)S(1)} %pad_maximum_fusion.1.refs_4_), channel_id=1, source_target_pairs={{0,1},{1,0},{2,3},{3,2},{4,5},{5,4},{6,7},{7,6},{8,9},{9,8},{10,11... | collective-permute-start | bytes 1572872 | tf_op jit(solution)/shard_map/ppermute | solution.py:298
  233.5 14.4 %collective-permute-start.59 = (bf16[256,1024]{1,0:T(8,128)(2,1)S(1)}, bf16[256,1024]{1,0:T(8,128)(2,1)S(1)}, u32[]{:S(2)}, u32[]{:S(2)}) collective-permute-start(bf16[256,1024]{1,0:T(8,128)(2,1)S(1)} %pad_maximum_fusion.2.refs_5_), channel_id=1, source_target_pairs={{0,2},{1,3},{2,0},{3,1},{4,6},{5,7},{6,4},{7,5},{8,10},{9,11},{10,... | collective-permute-start | bytes 1572872 | tf_op jit(solution)/shard_map/ppermute | solution.py:298
  236.4 18.6 %collective-permute-start.63 = (bf16[256,1024]{1,0:T(8,128)(2,1)S(1)}, bf16[256,1024]{1,0:T(8,128)(2,1)S(1)}, u32[]{:S(2)}, u32[]{:S(2)}) collective-permute-start(bf16[256,1024]{1,0:T(8,128)(2,1)S(1)} %pad_maximum_fusion.3.refs_6_), channel_id=1, source_target_pairs={{0,4},{4,0},{8,12},{12,8},{16,20},{20,16},{24,28},{28,24},{1,5},{5... | collective-permute-start | bytes 1572872 | tf_op jit(solution)/shard_map/ppermute | solution.py:394
  240.1 15.3 %collective-permute-start.58 = (bf16[256,1024]{1,0:T(8,128)(2,1)S(1)}, bf16[256,1024]{1,0:T(8,128)(2,1)S(1)}, u32[]{:S(2)}, u32[]{:S(2)}) collective-permute-start(bf16[256,1024]{1,0:T(8,128)(2,1)S(1)} %pad_maximum_fusion.2.refs_5_), channel_id=1, source_target_pairs={{0,8},{4,12},{8,0},{12,4},{16,24},{20,28},{24,16},{28,20},{1,9},{5... | collective-permute-start | bytes 1572872 | tf_op jit(solution)/shard_map/ppermute | solution.py:394
  243.8 25.2 %collective-permute-start.62 = (bf16[384,1024]{1,0:T(8,128)(2,1)S(1)}, bf16[384,1024]{1,0:T(8,128)(2,1)S(1)}, u32[]{:S(2)}, u32[]{:S(2)}) collective-permute-start(bf16[384,1024]{1,0:T(8,128)(2,1)S(1)} %pad_maximum_fusion.refs_5_), channel_id=1, source_target_pairs={{0,4},{4,0},{8,12},{12,8},{16,20},{20,16},{24,28},{28,24},{1,5},{5... | collective-permute-start | bytes 2359304 | tf_op jit(solution)/shard_map/ppermute | solution.py:394
  245.4 14.0 %collective-permute-start.64 = (bf16[256,1024]{1,0:T(8,128)(2,1)S(1)}, bf16[256,1024]{1,0:T(8,128)(2,1)S(1)}, u32[]{:S(2)}, u32[]{:S(2)}) collective-permute-start(bf16[256,1024]{1,0:T(8,128)(2,1)S(1)} %pad_maximum_fusion.3.refs_6_), channel_id=1, source_target_pairs={{0,3},{1,2},{2,1},{3,0},{4,7},{5,6},{6,5},{7,4},{8,11},{9,10},{10,... | collective-permute-start | bytes 1572872 | tf_op jit(solution)/shard_map/ppermute | solution.py:298
  247.9 11.6 %collective-permute-start.55 = (bf16[256,1024]{1,0:T(8,128)(2,1)S(1)}, bf16[256,1024]{1,0:T(8,128)(2,1)S(1)}, u32[]{:S(2)}, u32[]{:S(2)}) collective-permute-start(bf16[256,1024]{1,0:T(8,128)(2,1)S(1)} %collective-permute-done.53.refs_5_), channel_id=1, source_target_pairs={{0,1},{1,0},{2,3},{3,2},{4,5},{5,4},{6,7},{7,6},{8,9},{9,8},{10,11... | collective-permute-start | bytes 1572872 | tf_op jit(solution)/shard_map/ppermute | solution.py:298
  255.0 17.0 %collective-permute-start.60 = (bf16[256,1024]{1,0:T(8,128)(2,1)S(1)}, bf16[256,1024]{1,0:T(8,128)(2,1)S(1)}, u32[]{:S(2)}, u32[]{:S(2)}) collective-permute-start(bf16[256,1024]{1,0:T(8,128)(2,1)S(1)} %collective-permute-done.59.refs_7_), channel_id=1, source_target_pairs={{0,8},{4,12},{8,0},{12,4},{16,24},{20,28},{24,16},{28,20},{1,9},{5... | collective-permute-start | bytes 1572872 | tf_op jit(solution)/shard_map/ppermute | solution.py:394
  255.5 22.6 %collective-permute-start.65 = (bf16[256,1024]{1,0:T(8,128)(2,1)S(1)}, bf16[256,1024]{1,0:T(8,128)(2,1)S(1)}, u32[]{:S(2)}, u32[]{:S(2)}) collective-permute-start(bf16[256,1024]{1,0:T(8,128)(2,1)S(1)} %collective-permute-done.63.refs_7_), channel_id=1, source_target_pairs={{0,3},{1,2},{2,1},{3,0},{4,7},{5,6},{6,5},{7,4},{8,11},{9,10},{10,... | collective-permute-start | bytes 1572872 | tf_op jit(solution)/shard_map/ppermute | solution.py:298
  (28 other events, 240.1 us)

commit v13 on v12

--- a/solution.py
+++ b/solution.py
@@ -92,7 +92,7 @@
             half_ref[elements * size :, :] = extra_rows(jnp.full((1, width), jnp.sum(squares)))
 
 
-def call(kernel, name, outs, scalars, args, scratch=(), aliases=None, vmem=16, moved=1024):
+def call(kernel, name, outs, scalars, args, scratch=(), aliases=None, vmem=10, moved=1024):
     return pl.pallas_call(
         kernel,
         out_shape=outs,
@@ -190,6 +190,12 @@
         carried = extra_rows(jnp.concatenate([total] * CHUNKS, axis=1))
         mine_ref[half:, :] = carried
         other_ref[half:, :] = carried
+
+
+def join_kernel(upper_ref, lower_ref, out_ref):
+    height = upper_ref.shape[0]
+    out_ref[:height, :] = upper_ref[...]
+    out_ref[height:, :] = lower_ref[...]
 
 
 def sum_kernel(masks, hop, extra, entries, rows_total, where_ref, *refs):
@@ -310,7 +316,10 @@
     start = [lax.slice_in_dim(orbitals, c * width, (c + 1) * width, axis=1) for c in range(CHUNKS)]
     near = {(0, 0): lax.ppermute(start[0], "elem", swap)}
     order = Order(jnp.zeros((8, 128), F32))
-    blocks, place = order(blocks, place)
+    positions = [
+        jnp.stack([my_tile, my_group >> max(d.bit_length() - 1, 0) & 1]).astype(jnp.int32) for d in range(groups)
+    ]
+    blocks, place, *positions = order(blocks, place, *positions)
     start = [start[0]] + [order(field) for field in start[1:]]
     for c in range(1, CHUNKS):
         near[(0, c)] = lax.ppermute(start[c], "elem", swap)
@@ -381,11 +390,8 @@
     there = {d: 3.0 if d == 1 else 10.5 for d in range(1, groups)}
     mixed, mixes = None, 0
 
-    def is_upper(d):
-        return (my_group & (1 << (d.bit_length() - 1))) != 0
-
     def where(d):
-        return jnp.stack([my_tile, is_upper(d) if d else odd]).astype(jnp.int32)
+        return positions[d]
 
     def all_chunks(d):
         return [pieces[c][d] for c in range(CHUNKS)]
@@ -471,7 +477,8 @@
         for mask in masks[:0:-1]:
             received, arrival = over_tiles(part, mask)
             yield arrival
-            part = order(jnp.concatenate([part, order(received)], axis=0))
+            joined = jax.ShapeDtypeStruct((2 * part.shape[0], columns), BF16)
+            part = order(call(join_kernel, "join", joined, (), (part, order(received))))
             clock.spend(0.5)
         while behind not in sent:
             yield clock.now + 0.5
@@ -516,7 +523,7 @@
         kernel = functools.partial(mix_kernel, d > 0, masks, first, last)
         name = "mix_pair" if d else "mix_own"
         clock.spend(3.2)
-        mixed = call(kernel, name, shape, (where(d),), args, scratch, {} if first or last else {1: 0}, 28, 5 * MIB)
+        mixed = call(kernel, name, shape, (where(d),), args, scratch, {} if first or last else {1: 0}, 20, 5 * MIB)
         if not last:
             mixed = order(mixed)
 

time: 284 us -> 282 us (level)
  waiting for transfers between devices: 102 us -> 138 us
  starting transfers between devices: 114 us -> 91.1 us
  local copies, waits for them, and re-layouts: 17.2 us -> 6.77 us
  Pallas kernels: 47.1 us -> 42.7 us
    ppermute x25, waiting for transfers between devices: 62.3 us -> 86.1 us  [over_tiles(): sent = lax.ppermute(value, 'elem', [(i, i ^ mask) for i in range(tiles)])]
    ppermute x25, starting transfers between devices: 41.6 us -> 27.2 us  [over_tiles(): sent = lax.ppermute(value, 'elem', [(i, i ^ mask) for i in range(tiles)])]
    unnamed x53 -> x3, local copies, waits for them, and re-layouts: 11.1 us -> 0.1 us
    ppermute x8, waiting for transfers between devices: 12.2 us -> 20.8 us  [multiply(): near[stage + 1, c] = lax.ppermute(out, 'elem', swap)]
    ppermute x12, starting transfers between devices: 25.1 us -> 18.9 us  [send_on(): far[job] = lax.ppermute(near[job], 'elem', outward)]
    ppermute x8, starting transfers between devices: 28.4 us -> 23.7 us  [multiply(): near[stage + 1, c] = lax.ppermute(out, 'elem', swap)]
    pallas_call x32 -> x40, Pallas kernels: 47.1 us -> 42.7 us  [call(): pl.pallas_call(kernel, out_shape=outs, in_specs=[pl.BlockSpec(memory_spac...]
    ppermute x3, waiting for transfers between devices: 5.75 us -> 9.11 us  [local(): near[0, c] = lax.ppermute(start[c], 'elem', swap)]
  transfers between devices with their start and end apart: 66 -> 66, of which waited for: 33 -> 35; matrix products, arithmetic and copies ran while one was open for 2% -> 3% of each run, Pallas kernels for 15% -> 13%
where the time goes in v13:
time: 282 us; the launch traced here: 281 us
  waiting for transfers between devices  138 us (49%)
  starting transfers between devices  91.1 us (32%)
  Pallas kernels  42.7 us (15%)
  local copies, waits for them, and re-layouts  6.77 us (2%)
    ppermute x25, waiting for transfers between devices, over_tiles(): sent = lax.ppermute(value, 'elem', [(i, i ^ mask) for i in range(tiles)])  86.1 us
    pallas_call x40, Pallas kernels, call(): pl.pallas_call(kernel, out_shape=outs, in_specs=[pl.BlockSpec(memory_spac...  42.7 us
    ppermute x25, starting transfers between devices, over_tiles(): sent = lax.ppermute(value, 'elem', [(i, i ^ mask) for i in range(tiles)])  27.2 us
    ppermute x8, starting transfers between devices, multiply(): near[stage + 1, c] = lax.ppermute(out, 'elem', swap)  23.7 us
    ppermute x8, waiting for transfers between devices, multiply(): near[stage + 1, c] = lax.ppermute(out, 'elem', swap)  20.8 us
    ppermute x12, starting transfers between devices, send_on(): far[job] = lax.ppermute(near[job], 'elem', outward)  18.9 us
    ppermute x17, waiting for transfers between devices, to_group(): return lax.ppermute(value, 'orb', [(i, i ^ d) for i in range(groups)])  14.3 us
    ppermute x17, starting transfers between devices, to_group(): return lax.ppermute(value, 'orb', [(i, i ^ d) for i in range(groups)])  10.7 us
  transfers between devices with their start and end apart: 66, of which 35 were waited for; matrix products, arithmetic and copies ran while one was open for 3% of the time, Pallas kernels for 13%

profile of v13, /device:TPU:0, one launch (start us, length us, event | category | flops | bytes accessed | tf_op | source)
XLA Modules:
  0.0 281.3 jit_solution(1747255074712496092)
XLA Ops:
  1.5 3.0 %collective-permute-start = (bf16[768,256]{1,0:T(8,128)(2,1)S(1)}, bf16[768,256]{1,0:T(8,128)(2,1)S(1)}, u32[]{:S(2)}, u32[]{:S(2)}) collective-permute-start(bf16[768,256]{1,0:T(8,128)(2,1)S(1)} %get-tuple-element.511.field_ref.refs_0_), channel_id=1, source_target_pairs={{0,4},{4,0},{8,12},{12,8},{16,20},{20,16},{24,28},{28,24},{1,5},{5... | collective-permute-start | bytes 1179656 | tf_op jit(solution)/shard_map/ppermute | solution.py:317
  4.5 2.2 slice_bitcast_fusion
  8.7 2.3 concatenate.6.blocks_ref
  11.9 2.1 collective-permute-done.near_ref
  13.9 1.6 collective-permute-start.1
  15.5 4.5 %collective-permute-start.4 = (bf16[768,256]{1,0:T(8,128)(2,1)S(1)}, bf16[768,256]{1,0:T(8,128)(2,1)S(1)}, u32[]{:S(2)}, u32[]{:S(2)}) collective-permute-start(bf16[768,256]{1,0:T(8,128)(2,1)S(1)} %get-tuple-element.273.field_ref.refs_0_), channel_id=1, source_target_pairs={{0,4},{4,0},{8,12},{12,8},{16,20},{20,16},{24,28},{28,24},{1,5},{5... | collective-permute-start | bytes 1179656 | tf_op jit(solution)/shard_map/ppermute | solution.py:325
  20.0 3.9 %collective-permute-done.2.near_ref = bf16[768,256]{1,0:T(8,128)(2,1)S(1)} collective-permute-done((bf16[768,256]{1,0:T(8,128)(2,1)S(1)}, bf16[768,256]{1,0:T(8,128)(2,1)S(1)}, u32[]{:S(2)}, u32[]{:S(2)}) %collective-permute-start.2) | collective-permute-done | bytes 393248 | tf_op jit(solution)/shard_map/ppermute | solution.py:325
  23.9 1.6 collective-permute-start.7
  25.5 3.0 %collective-permute-start.6 = (bf16[768,256]{1,0:T(8,128)(2,1)S(1)}, bf16[768,256]{1,0:T(8,128)(2,1)S(1)}, u32[]{:S(2)}, u32[]{:S(2)}) collective-permute-start(bf16[768,256]{1,0:T(8,128)(2,1)S(1)} %get-tuple-element.276.field_ref.refs_0_), channel_id=1, source_target_pairs={{0,4},{4,0},{8,12},{12,8},{16,20},{20,16},{24,28},{28,24},{1,5},{5... | collective-permute-start | bytes 1179656 | tf_op jit(solution)/shard_map/ppermute | solution.py:325
  29.7 2.6 collective-permute-done.4.near_ref
  33.9 3.0 %collective-permute-start.3 = (bf16[768,256]{1,0:T(8,128)(2,1)S(1)}, bf16[768,256]{1,0:T(8,128)(2,1)S(1)}, u32[]{:S(2)}, u32[]{:S(2)}) collective-permute-start(bf16[768,256]{1,0:T(8,128)(2,1)S(1)} %get-tuple-element.272.field_ref), channel_id=1, source_target_pairs={{0,4},{4,0},{8,12},{12,8},{16,20},{20,16},{24,28},{28,24},{1,5},{5... | collective-permute-start | bytes 1179656 | tf_op jit(solution)/shard_map/ppermute | solution.py:376
  38.1 2.6 collective-permute-done.6.near_ref
  42.3 3.0 %collective-permute-start.9 = (bf16[768,256]{1,0:T(8,128)(2,1)S(1)}, bf16[768,256]{1,0:T(8,128)(2,1)S(1)}, u32[]{:S(2)}, u32[]{:S(2)}) collective-permute-start(bf16[768,256]{1,0:T(8,128)(2,1)S(1)} %get-tuple-element.291.field_ref), channel_id=1, source_target_pairs={{0,4},{4,0},{8,12},{12,8},{16,20},{20,16},{24,28},{28,24},{1,5},{5... | collective-permute-start | bytes 1179656 | tf_op jit(solution)/shard_map/ppermute | solution.py:376
  46.6 2.6 collective-permute-done.3.near_ref
  49.2 1.6 collective-permute-start.8
  50.7 3.0 %collective-permute-start.12 = (bf16[768,256]{1,0:T(8,128)(2,1)S(1)}, bf16[768,256]{1,0:T(8,128)(2,1)S(1)}, u32[]{:S(2)}, u32[]{:S(2)}) collective-permute-start(bf16[768,256]{1,0:T(8,128)(2,1)S(1)} %get-tuple-element.303.field_ref), channel_id=1, source_target_pairs={{0,4},{4,0},{8,12},{12,8},{16,20},{20,16},{24,28},{28,24},{1,5},{5... | collective-permute-start | bytes 1179656 | tf_op jit(solution)/shard_map/ppermute | solution.py:376
  55.0 2.6 collective-permute-done.9.near_ref
  59.2 3.0 %collective-permute-start.14 = (bf16[768,256]{1,0:T(8,128)(2,1)S(1)}, bf16[768,256]{1,0:T(8,128)(2,1)S(1)}, u32[]{:S(2)}, u32[]{:S(2)}) collective-permute-start(bf16[768,256]{1,0:T(8,128)(2,1)S(1)} %get-tuple-element.306.field_ref), channel_id=1, source_target_pairs={{0,4},{4,0},{8,12},{12,8},{16,20},{20,16},{24,28},{28,24},{1,5},{5... | collective-permute-start | bytes 1179656 | tf_op jit(solution)/shard_map/ppermute | solution.py:376
  63.4 2.6 collective-permute-done.12.near_ref
  67.6 3.0 %collective-permute-start.11 = (bf16[768,256]{1,0:T(8,128)(2,1)S(1)}, bf16[768,256]{1,0:T(8,128)(2,1)S(1)}, u32[]{:S(2)}, u32[]{:S(2)}) collective-permute-start(bf16[768,256]{1,0:T(8,128)(2,1)S(1)} %product_1.4.field_ref), channel_id=1, source_target_pairs={{0,4},{4,0},{8,12},{12,8},{16,20},{20,16},{24,28},{28,24},{1,5},{5... | collective-permute-start | bytes 1179656 | tf_op jit(solution)/shard_map/ppermute | solution.py:376
  71.8 2.6 collective-permute-done.14.near_ref
  76.0 3.0 %collective-permute-start.17 = (bf16[768,256]{1,0:T(8,128)(2,1)S(1)}, bf16[768,256]{1,0:T(8,128)(2,1)S(1)}, u32[]{:S(2)}, u32[]{:S(2)}) collective-permute-start(bf16[768,256]{1,0:T(8,128)(2,1)S(1)} %product_1.5.field_ref), channel_id=1, source_target_pairs={{0,4},{4,0},{8,12},{12,8},{16,20},{20,16},{24,28},{28,24},{1,5},{5... | collective-permute-start | bytes 1179656 | tf_op jit(solution)/shard_map/ppermute | solution.py:376
  80.3 2.6 collective-permute-done.11.near_ref
  84.5 3.0 %collective-permute-start.20 = (bf16[768,256]{1,0:T(8,128)(2,1)S(1)}, bf16[768,256]{1,0:T(8,128)(2,1)S(1)}, u32[]{:S(2)}, u32[]{:S(2)}) collective-permute-start(bf16[768,256]{1,0:T(8,128)(2,1)S(1)} %product_1.6.field_ref), channel_id=1, source_target_pairs={{0,4},{4,0},{8,12},{12,8},{16,20},{20,16},{24,28},{28,24},{1,5},{5... | collective-permute-start | bytes 1179656 | tf_op jit(solution)/shard_map/ppermute | solution.py:376
  88.7 2.6 collective-permute-done.17.near_ref
  92.9 3.0 %collective-permute-start.22 = (bf16[768,256]{1,0:T(8,128)(2,1)S(1)}, bf16[768,256]{1,0:T(8,128)(2,1)S(1)}, u32[]{:S(2)}, u32[]{:S(2)}) collective-permute-start(bf16[768,256]{1,0:T(8,128)(2,1)S(1)} %product_1.7.field_ref), channel_id=1, source_target_pairs={{0,4},{4,0},{8,12},{12,8},{16,20},{20,16},{24,28},{28,24},{1,5},{5... | collective-permute-start | bytes 1179656 | tf_op jit(solution)/shard_map/ppermute | solution.py:376
  97.1 2.6 collective-permute-done.20.near_ref
  104.1 2.6 collective-permute-done.22.near_ref
  113.0 5.5 %collective-permute-done.23.far_ref = bf16[768,256]{1,0:T(8,128)(2,1)S(1)} collective-permute-done((bf16[768,256]{1,0:T(8,128)(2,1)S(1)}, bf16[768,256]{1,0:T(8,128)(2,1)S(1)}, u32[]{:S(2)}, u32[]{:S(2)}) %collective-permute-start.23) | collective-permute-done | bytes 393248 | tf_op jit(solution)/shard_map/ppermute | solution.py:334
  119.9 2.1 gram_own.1
  122.0 4.1 %collective-permute-done.29.refs_6_.refs_3_ = bf16[768,256]{1,0:T(8,128)(2,1)S(1)} collective-permute-done((bf16[768,256]{1,0:T(8,128)(2,1)S(1)}, bf16[768,256]{1,0:T(8,128)(2,1)S(1)}, u32[]{:S(2)}, u32[]{:S(2)}) %collective-permute-start.29) | collective-permute-done | bytes 393248 | tf_op jit(solution)/shard_map/ppermute | solution.py:304
  126.1 3.8 %collective-permute-start.35 = (bf16[384,1024]{1,0:T(8,128)(2,1)S(1)}, bf16[384,1024]{1,0:T(8,128)(2,1)S(1)}, u32[]{:S(2)}, u32[]{:S(2)}) collective-permute-start(bf16[384,1024]{1,0:T(8,128)(2,1)S(1)} %get-tuple-element.384), channel_id=1, source_target_pairs={{0,4},{4,0},{8,12},{12,8},{16,20},{20,16},{24,28},{28,24},{1,5},{5... | collective-permute-start | bytes 2359304 | tf_op jit(solution)/shard_map/ppermute | solution.py:400
  133.1 5.6 %collective-permute-done.32.refs_7_.refs_9_.refs_4_ = bf16[784,256]{1,0:T(8,128)(2,1)S(1)} collective-permute-done((bf16[784,256]{1,0:T(8,128)(2,1)S(1)}, bf16[784,256]{1,0:T(8,128)(2,1)S(1)}, u32[]{:S(2)}, u32[]{:S(2)}) %collective-permute-start.32) | collective-permute-done | bytes 401440 | tf_op jit(solution)/shard_map/ppermute | solution.py:304
  139.7 1.6 gram_pair.3
  141.4 4.1 %collective-permute-done.35.refs_1_ = bf16[384,1024]{1,0:T(8,128)(2,1)S(1)} collective-permute-done((bf16[384,1024]{1,0:T(8,128)(2,1)S(1)}, bf16[384,1024]{1,0:T(8,128)(2,1)S(1)}, u32[]{:S(2)}, u32[]{:S(2)}) %collective-permute-start.35) | collective-permute-done | bytes 786464 | tf_op jit(solution)/shard_map/ppermute | solution.py:400
  146.2 1.8 gram_pair.4
  148.0 1.8 collective-permute-start.37
  150.9 1.6 gram_pair.5
  152.8 9.1 %collective-permute-done.39.refs_1_ = bf16[256,1024]{1,0:T(8,128)(2,1)S(1)} collective-permute-done((bf16[256,1024]{1,0:T(8,128)(2,1)S(1)}, bf16[256,1024]{1,0:T(8,128)(2,1)S(1)}, u32[]{:S(2)}, u32[]{:S(2)}) %collective-permute-start.39) | collective-permute-done | bytes 524320 | tf_op jit(solution)/shard_map/ppermute | solution.py:400
  162.6 4.4 %collective-permute-done.38.refs_2_ = bf16[192,1024]{1,0:T(8,128)(2,1)S(1)} collective-permute-done((bf16[192,1024]{1,0:T(8,128)(2,1)S(1)}, bf16[192,1024]{1,0:T(8,128)(2,1)S(1)}, u32[]{:S(2)}, u32[]{:S(2)}) %collective-permute-start.38) | collective-permute-done | bytes 393248 | tf_op jit(solution)/shard_map/ppermute | solution.py:400
  168.3 2.1 collective-permute-start.40
  171.1 4.4 %collective-permute-done.42.refs_3_ = bf16[96,1024]{1,0:T(8,128)(2,1)S(1)} collective-permute-done((bf16[96,1024]{1,0:T(8,128)(2,1)S(1)}, bf16[96,1024]{1,0:T(8,128)(2,1)S(1)}, u32[]{:S(2)}, u32[]{:S(2)}) %collective-permute-start.42) | collective-permute-done | bytes 196640 | tf_op jit(solution)/shard_map/ppermute | solution.py:400
  176.2 6.4 %collective-permute-done.40.refs_2_ = bf16[144,1024]{1,0:T(8,128)(2,1)S(1)} collective-permute-done((bf16[144,1024]{1,0:T(8,128)(2,1)S(1)}, bf16[144,1024]{1,0:T(8,128)(2,1)S(1)}, u32[]{:S(2)}, u32[]{:S(2)}) %collective-permute-start.40) | collective-permute-done | bytes 294944 | tf_op jit(solution)/shard_map/ppermute | solution.py:400
  187.6 8.1 %collective-permute-done.46.refs_3_ = bf16[64,1024]{1,0:T(8,128)(2,1)S(1)} collective-permute-done((bf16[64,1024]{1,0:T(8,128)(2,1)S(1)}, bf16[64,1024]{1,0:T(8,128)(2,1)S(1)}, u32[]{:S(2)}, u32[]{:S(2)}) %collective-permute-start.46) | collective-permute-done | bytes 131104 | tf_op jit(solution)/shard_map/ppermute | solution.py:400
  197.9 2.7 collective-permute-start.51
  200.9 5.3 %collective-permute-done.48.lower_ref = bf16[64,1024]{1,0:T(8,128)(2,1)S(1)} collective-permute-done((bf16[64,1024]{1,0:T(8,128)(2,1)S(1)}, bf16[64,1024]{1,0:T(8,128)(2,1)S(1)}, u32[]{:S(2)}, u32[]{:S(2)}) %collective-permute-start.48) | collective-permute-done | bytes 131104 | tf_op jit(solution)/shard_map/ppermute | solution.py:400
  206.3 8.3 %collective-permute-done.47.refs_3_ = bf16[64,1024]{1,0:T(8,128)(2,1)S(1)} collective-permute-done((bf16[64,1024]{1,0:T(8,128)(2,1)S(1)}, bf16[64,1024]{1,0:T(8,128)(2,1)S(1)}, u32[]{:S(2)}, u32[]{:S(2)}) %collective-permute-start.47) | collective-permute-done | bytes 131104 | tf_op jit(solution)/shard_map/ppermute | solution.py:400
  215.3 2.9 %collective-permute-start.50 = (bf16[64,1024]{1,0:T(8,128)(2,1)S(1)}, bf16[64,1024]{1,0:T(8,128)(2,1)S(1)}, u32[]{:S(2)}, u32[]{:S(2)}) collective-permute-start(bf16[64,1024]{1,0:T(8,128)(2,1)S(1)} %get-tuple-element.475.upper_ref), channel_id=1, source_target_pairs={{0,16},{4,20},{8,24},{12,28},{16,0},{20,4},{24,8},{28,12},{1,17},{... | collective-permute-start | bytes 393224 | tf_op jit(solution)/shard_map/ppermute | solution.py:400
  218.4 10.6 %collective-permute-done.49.lower_ref = bf16[64,1024]{1,0:T(8,128)(2,1)S(1)} collective-permute-done((bf16[64,1024]{1,0:T(8,128)(2,1)S(1)}, bf16[64,1024]{1,0:T(8,128)(2,1)S(1)}, u32[]{:S(2)}, u32[]{:S(2)}) %collective-permute-start.49) | collective-permute-done | bytes 131104 | tf_op jit(solution)/shard_map/ppermute | solution.py:400
  229.1 1.6 collective-permute-done.50.lower_ref
  230.9 2.4 collective-permute-start.53
  233.2 2.2 collective-permute-done.56.lower_ref
  237.8 2.6 collective-permute-start.63
  240.4 4.0 %collective-permute-done.53.refs_5_ = bf16[256,1024]{1,0:T(8,128)(2,1)S(1)} collective-permute-done((bf16[256,1024]{1,0:T(8,128)(2,1)S(1)}, bf16[256,1024]{1,0:T(8,128)(2,1)S(1)}, u32[]{:S(2)}, u32[]{:S(2)}) %collective-permute-start.53) | collective-permute-done | bytes 524320 | tf_op jit(solution)/shard_map/ppermute | solution.py:400
  244.3 2.4 collective-permute-start.62
  247.7 1.7 collective-permute-start.55
  249.3 6.3 %collective-permute-done.63.refs_7_ = bf16[256,1024]{1,0:T(8,128)(2,1)S(1)} collective-permute-done((bf16[256,1024]{1,0:T(8,128)(2,1)S(1)}, bf16[256,1024]{1,0:T(8,128)(2,1)S(1)}, u32[]{:S(2)}, u32[]{:S(2)}) %collective-permute-start.63) | collective-permute-done | bytes 524320 | tf_op jit(solution)/shard_map/ppermute | solution.py:400
  255.6 1.9 collective-permute-start.60
  257.5 2.4 collective-permute-done.64.refs_8_
  259.9 9.2 %collective-permute-done.62.refs_6_ = bf16[384,1024]{1,0:T(8,128)(2,1)S(1)} collective-permute-done((bf16[384,1024]{1,0:T(8,128)(2,1)S(1)}, bf16[384,1024]{1,0:T(8,128)(2,1)S(1)}, u32[]{:S(2)}, u32[]{:S(2)}) %collective-permute-start.62) | collective-permute-done | bytes 786464 | tf_op jit(solution)/shard_map/ppermute | solution.py:400
  269.2 2.6 mix_pair.3.refs_0_
  271.8 2.9 %mix_pair.4.refs_0_ = f32[768,1024]{1,0:T(8,128)S(1)} custom-call(s32[2]{0:T(128)S(1)} %get-tuple-element.385.where_ref, f32[768,1024]{1,0:T(8,128)S(1)} %mix_pair.3.refs_0_, bf16[768,256]{1,0:T(8,128)(2,1)S(1)} %collective-permute-done.25.refs_4_.refs_1_, ...), custom_call_target="tpu_custom_call", output_to_operand_aliasing={{}: (1, {})} | custom-call | flops 1024 | bytes 5242880 | tf_op jit(solution)/shard_map/mix_pair/pallas_call | solution.py:96
  274.7 2.6 mix_own.1.refs_1_
  277.3 4.0 %mix_pair.5 = bf16[768,1024]{1,0:T(8,128)(2,1)} custom-call(s32[2]{0:T(128)S(1)} %get-tuple-element.385.where_ref, f32[8,128]{1,0:T(8,128)S(1)} %get-tuple-element.462.refs_4_.refs_0_, f32[768,1024]{1,0:T(8,128)S(1)} %mix_own.1.refs_1_, bf16[768,256]{1,0:T(8,128)(2,1)S(1)} %collective-permute-done.26.refs_4_.refs_2_, ...), custom_call_target="tpu_custom_call" | custom-call | flops 1024 | bytes 5242880 | tf_op jit(solution)/shard_map/mix_pair/pallas_call | solution.py:96
  (123 shorter events, 60.4 us)
Async XLA Ops:
  1.5 12.4 %collective-permute-start = (bf16[768,256]{1,0:T(8,128)(2,1)S(1)}, bf16[768,256]{1,0:T(8,128)(2,1)S(1)}, u32[]{:S(2)}, u32[]{:S(2)}) collective-permute-start(bf16[768,256]{1,0:T(8,128)(2,1)S(1)} %get-tuple-element.511.field_ref.refs_0_), channel_id=1, source_target_pairs={{0,4},{4,0},{8,12},{12,8},{16,20},{20,16},{24,28},{28,24},{1,5},{5... | collective-permute-start | bytes 1179656 | tf_op jit(solution)/shard_map/ppermute | solution.py:317
  11.8 12.0 %collective-permute-start.2 = (bf16[768,256]{1,0:T(8,128)(2,1)S(1)}, bf16[768,256]{1,0:T(8,128)(2,1)S(1)}, u32[]{:S(2)}, u32[]{:S(2)}) collective-permute-start(bf16[768,256]{1,0:T(8,128)(2,1)S(1)} %get-tuple-element.265.field_ref.refs_0_), channel_id=1, source_target_pairs={{0,4},{4,0},{8,12},{12,8},{16,20},{20,16},{24,28},{28,24},{1,5},{5... | collective-permute-start | bytes 1179656 | tf_op jit(solution)/shard_map/ppermute | solution.py:325
  13.9 14.5 %collective-permute-start.1 = (bf16[768,256]{1,0:T(8,128)(2,1)S(1)}, bf16[768,256]{1,0:T(8,128)(2,1)S(1)}, u32[]{:S(2)}, u32[]{:S(2)}) collective-permute-start(bf16[768,256]{1,0:T(8,128)(2,1)S(1)} %collective-permute-done.near_ref), channel_id=1, source_target_pairs={{0,8},{4,28},{8,16},{12,4},{16,24},{20,12},{24,0},{28,20},{1,9},{5... | collective-permute-start | bytes 1179656 | tf_op jit(solution)/shard_map/ppermute | solution.py:334
  15.5 16.8 %collective-permute-start.4 = (bf16[768,256]{1,0:T(8,128)(2,1)S(1)}, bf16[768,256]{1,0:T(8,128)(2,1)S(1)}, u32[]{:S(2)}, u32[]{:S(2)}) collective-permute-start(bf16[768,256]{1,0:T(8,128)(2,1)S(1)} %get-tuple-element.273.field_ref.refs_0_), channel_id=1, source_target_pairs={{0,4},{4,0},{8,12},{12,8},{16,20},{20,16},{24,28},{28,24},{1,5},{5... | collective-permute-start | bytes 1179656 | tf_op jit(solution)/shard_map/ppermute | solution.py:325
  23.9 13.0 %collective-permute-start.7 = (bf16[768,256]{1,0:T(8,128)(2,1)S(1)}, bf16[768,256]{1,0:T(8,128)(2,1)S(1)}, u32[]{:S(2)}, u32[]{:S(2)}) collective-permute-start(bf16[768,256]{1,0:T(8,128)(2,1)S(1)} %collective-permute-done.2.near_ref), channel_id=1, source_target_pairs={{0,8},{4,28},{8,16},{12,4},{16,24},{20,12},{24,0},{28,20},{1,9},{5... | collective-permute-start | bytes 1179656 | tf_op jit(solution)/shard_map/ppermute | solution.py:334
  25.5 15.3 %collective-permute-start.6 = (bf16[768,256]{1,0:T(8,128)(2,1)S(1)}, bf16[768,256]{1,0:T(8,128)(2,1)S(1)}, u32[]{:S(2)}, u32[]{:S(2)}) collective-permute-start(bf16[768,256]{1,0:T(8,128)(2,1)S(1)} %get-tuple-element.276.field_ref.refs_0_), channel_id=1, source_target_pairs={{0,4},{4,0},{8,12},{12,8},{16,20},{20,16},{24,28},{28,24},{1,5},{5... | collective-permute-start | bytes 1179656 | tf_op jit(solution)/shard_map/ppermute | solution.py:325
  32.3 13.0 %collective-permute-start.5 = (bf16[768,256]{1,0:T(8,128)(2,1)S(1)}, bf16[768,256]{1,0:T(8,128)(2,1)S(1)}, u32[]{:S(2)}, u32[]{:S(2)}) collective-permute-start(bf16[768,256]{1,0:T(8,128)(2,1)S(1)} %collective-permute-done.4.near_ref), channel_id=1, source_target_pairs={{0,8},{4,28},{8,16},{12,4},{16,24},{20,12},{24,0},{28,20},{1,9},{5... | collective-permute-start | bytes 1179656 | tf_op jit(solution)/shard_map/ppermute | solution.py:334
  33.9 15.3 %collective-permute-start.3 = (bf16[768,256]{1,0:T(8,128)(2,1)S(1)}, bf16[768,256]{1,0:T(8,128)(2,1)S(1)}, u32[]{:S(2)}, u32[]{:S(2)}) collective-permute-start(bf16[768,256]{1,0:T(8,128)(2,1)S(1)} %get-tuple-element.272.field_ref), channel_id=1, source_target_pairs={{0,4},{4,0},{8,12},{12,8},{16,20},{20,16},{24,28},{28,24},{1,5},{5... | collective-permute-start | bytes 1179656 | tf_op jit(solution)/shard_map/ppermute | solution.py:376
  40.7 13.0 %collective-permute-start.10 = (bf16[768,256]{1,0:T(8,128)(2,1)S(1)}, bf16[768,256]{1,0:T(8,128)(2,1)S(1)}, u32[]{:S(2)}, u32[]{:S(2)}) collective-permute-start(bf16[768,256]{1,0:T(8,128)(2,1)S(1)} %collective-permute-done.6.near_ref), channel_id=1, source_target_pairs={{0,8},{4,28},{8,16},{12,4},{16,24},{20,12},{24,0},{28,20},{1,9},{5... | collective-permute-start | bytes 1179656 | tf_op jit(solution)/shard_map/ppermute | solution.py:334
  42.3 15.3 %collective-permute-start.9 = (bf16[768,256]{1,0:T(8,128)(2,1)S(1)}, bf16[768,256]{1,0:T(8,128)(2,1)S(1)}, u32[]{:S(2)}, u32[]{:S(2)}) collective-permute-start(bf16[768,256]{1,0:T(8,128)(2,1)S(1)} %get-tuple-element.291.field_ref), channel_id=1, source_target_pairs={{0,4},{4,0},{8,12},{12,8},{16,20},{20,16},{24,28},{28,24},{1,5},{5... | collective-permute-start | bytes 1179656 | tf_op jit(solution)/shard_map/ppermute | solution.py:376
  49.2 13.0 %collective-permute-start.8 = (bf16[768,256]{1,0:T(8,128)(2,1)S(1)}, bf16[768,256]{1,0:T(8,128)(2,1)S(1)}, u32[]{:S(2)}, u32[]{:S(2)}) collective-permute-start(bf16[768,256]{1,0:T(8,128)(2,1)S(1)} %collective-permute-done.3.near_ref), channel_id=1, source_target_pairs={{0,8},{4,28},{8,16},{12,4},{16,24},{20,12},{24,0},{28,20},{1,9},{5... | collective-permute-start | bytes 1179656 | tf_op jit(solution)/shard_map/ppermute | solution.py:334
  50.7 15.3 %collective-permute-start.12 = (bf16[768,256]{1,0:T(8,128)(2,1)S(1)}, bf16[768,256]{1,0:T(8,128)(2,1)S(1)}, u32[]{:S(2)}, u32[]{:S(2)}) collective-permute-start(bf16[768,256]{1,0:T(8,128)(2,1)S(1)} %get-tuple-element.303.field_ref), channel_id=1, source_target_pairs={{0,4},{4,0},{8,12},{12,8},{16,20},{20,16},{24,28},{28,24},{1,5},{5... | collective-permute-start | bytes 1179656 | tf_op jit(solution)/shard_map/ppermute | solution.py:376
  57.6 13.0 %collective-permute-start.15 = (bf16[768,256]{1,0:T(8,128)(2,1)S(1)}, bf16[768,256]{1,0:T(8,128)(2,1)S(1)}, u32[]{:S(2)}, u32[]{:S(2)}) collective-permute-start(bf16[768,256]{1,0:T(8,128)(2,1)S(1)} %collective-permute-done.9.near_ref), channel_id=1, source_target_pairs={{0,8},{4,28},{8,16},{12,4},{16,24},{20,12},{24,0},{28,20},{1,9},{5... | collective-permute-start | bytes 1179656 | tf_op jit(solution)/shard_map/ppermute | solution.py:334
  59.2 15.3 %collective-permute-start.14 = (bf16[768,256]{1,0:T(8,128)(2,1)S(1)}, bf16[768,256]{1,0:T(8,128)(2,1)S(1)}, u32[]{:S(2)}, u32[]{:S(2)}) collective-permute-start(bf16[768,256]{1,0:T(8,128)(2,1)S(1)} %get-tuple-element.306.field_ref), channel_id=1, source_target_pairs={{0,4},{4,0},{8,12},{12,8},{16,20},{20,16},{24,28},{28,24},{1,5},{5... | collective-permute-start | bytes 1179656 | tf_op jit(solution)/shard_map/ppermute | solution.py:376
  66.0 13.0 %collective-permute-start.13 = (bf16[768,256]{1,0:T(8,128)(2,1)S(1)}, bf16[768,256]{1,0:T(8,128)(2,1)S(1)}, u32[]{:S(2)}, u32[]{:S(2)}) collective-permute-start(bf16[768,256]{1,0:T(8,128)(2,1)S(1)} %collective-permute-done.12.near_ref), channel_id=1, source_target_pairs={{0,8},{4,28},{8,16},{12,4},{16,24},{20,12},{24,0},{28,20},{1,9},{5... | collective-permute-start | bytes 1179656 | tf_op jit(solution)/shard_map/ppermute | solution.py:334
  67.6 15.3 %collective-permute-start.11 = (bf16[768,256]{1,0:T(8,128)(2,1)S(1)}, bf16[768,256]{1,0:T(8,128)(2,1)S(1)}, u32[]{:S(2)}, u32[]{:S(2)}) collective-permute-start(bf16[768,256]{1,0:T(8,128)(2,1)S(1)} %product_1.4.field_ref), channel_id=1, source_target_pairs={{0,4},{4,0},{8,12},{12,8},{16,20},{20,16},{24,28},{28,24},{1,5},{5... | collective-permute-start | bytes 1179656 | tf_op jit(solution)/shard_map/ppermute | solution.py:376
  74.4 13.0 %collective-permute-start.18 = (bf16[768,256]{1,0:T(8,128)(2,1)S(1)}, bf16[768,256]{1,0:T(8,128)(2,1)S(1)}, u32[]{:S(2)}, u32[]{:S(2)}) collective-permute-start(bf16[768,256]{1,0:T(8,128)(2,1)S(1)} %collective-permute-done.14.near_ref), channel_id=1, source_target_pairs={{0,8},{4,28},{8,16},{12,4},{16,24},{20,12},{24,0},{28,20},{1,9},{5... | collective-permute-start | bytes 1179656 | tf_op jit(solution)/shard_map/ppermute | solution.py:334
  76.0 15.3 %collective-permute-start.17 = (bf16[768,256]{1,0:T(8,128)(2,1)S(1)}, bf16[768,256]{1,0:T(8,128)(2,1)S(1)}, u32[]{:S(2)}, u32[]{:S(2)}) collective-permute-start(bf16[768,256]{1,0:T(8,128)(2,1)S(1)} %product_1.5.field_ref), channel_id=1, source_target_pairs={{0,4},{4,0},{8,12},{12,8},{16,20},{20,16},{24,28},{28,24},{1,5},{5... | collective-permute-start | bytes 1179656 | tf_op jit(solution)/shard_map/ppermute | solution.py:376
  82.9 13.0 %collective-permute-start.16 = (bf16[768,256]{1,0:T(8,128)(2,1)S(1)}, bf16[768,256]{1,0:T(8,128)(2,1)S(1)}, u32[]{:S(2)}, u32[]{:S(2)}) collective-permute-start(bf16[768,256]{1,0:T(8,128)(2,1)S(1)} %collective-permute-done.11.near_ref), channel_id=1, source_target_pairs={{0,8},{4,28},{8,16},{12,4},{16,24},{20,12},{24,0},{28,20},{1,9},{5... | collective-permute-start | bytes 1179656 | tf_op jit(solution)/shard_map/ppermute | solution.py:334
  84.5 15.3 %collective-permute-start.20 = (bf16[768,256]{1,0:T(8,128)(2,1)S(1)}, bf16[768,256]{1,0:T(8,128)(2,1)S(1)}, u32[]{:S(2)}, u32[]{:S(2)}) collective-permute-start(bf16[768,256]{1,0:T(8,128)(2,1)S(1)} %product_1.6.field_ref), channel_id=1, source_target_pairs={{0,4},{4,0},{8,12},{12,8},{16,20},{20,16},{24,28},{28,24},{1,5},{5... | collective-permute-start | bytes 1179656 | tf_op jit(solution)/shard_map/ppermute | solution.py:376
  91.3 11.5 %collective-permute-start.19 = (bf16[768,256]{1,0:T(8,128)(2,1)S(1)}, bf16[768,256]{1,0:T(8,128)(2,1)S(1)}, u32[]{:S(2)}, u32[]{:S(2)}) collective-permute-start(bf16[768,256]{1,0:T(8,128)(2,1)S(1)} %collective-permute-done.17.near_ref), channel_id=1, source_target_pairs={{0,8},{4,28},{8,16},{12,4},{16,24},{20,12},{24,0},{28,20},{1,9},{5... | collective-permute-start | bytes 1179656 | tf_op jit(solution)/shard_map/ppermute | solution.py:334
  92.9 13.8 %collective-permute-start.22 = (bf16[768,256]{1,0:T(8,128)(2,1)S(1)}, bf16[768,256]{1,0:T(8,128)(2,1)S(1)}, u32[]{:S(2)}, u32[]{:S(2)}) collective-permute-start(bf16[768,256]{1,0:T(8,128)(2,1)S(1)} %product_1.7.field_ref), channel_id=1, source_target_pairs={{0,4},{4,0},{8,12},{12,8},{16,20},{20,16},{24,28},{28,24},{1,5},{5... | collective-permute-start | bytes 1179656 | tf_op jit(solution)/shard_map/ppermute | solution.py:376
  99.7 10.4 %collective-permute-start.21 = (bf16[768,256]{1,0:T(8,128)(2,1)S(1)}, bf16[768,256]{1,0:T(8,128)(2,1)S(1)}, u32[]{:S(2)}, u32[]{:S(2)}) collective-permute-start(bf16[768,256]{1,0:T(8,128)(2,1)S(1)} %collective-permute-done.20.near_ref), channel_id=1, source_target_pairs={{0,8},{4,28},{8,16},{12,4},{16,24},{20,12},{24,0},{28,20},{1,9},{5... | collective-permute-start | bytes 1179656 | tf_op jit(solution)/shard_map/ppermute | solution.py:334
  101.3 10.2 %collective-permute-start.25 = (bf16[768,256]{1,0:T(8,128)(2,1)S(1)}, bf16[768,256]{1,0:T(8,128)(2,1)S(1)}, u32[]{:S(2)}, u32[]{:S(2)}) collective-permute-start(bf16[768,256]{1,0:T(8,128)(2,1)S(1)} %get-tuple-element.329.refs_0_.refs_1_.refs_10_), channel_id=1, source_target_pairs={{0,2},{1,3},{2,0},{3,1},{4,6},{5,7},{6,4},{7,5},{8,10},{9,11},{10,... | collective-permute-start | bytes 1179656 | tf_op jit(solution)/shard_map/ppermute | solution.py:304
  102.8 10.2 %collective-permute-start.24 = (bf16[768,256]{1,0:T(8,128)(2,1)S(1)}, bf16[768,256]{1,0:T(8,128)(2,1)S(1)}, u32[]{:S(2)}, u32[]{:S(2)}) collective-permute-start(bf16[768,256]{1,0:T(8,128)(2,1)S(1)} %get-tuple-element.329.refs_0_.refs_1_.refs_10_), channel_id=1, source_target_pairs={{0,1},{1,0},{2,3},{3,2},{4,5},{5,4},{6,7},{7,6},{8,9},{9,8},{10,11... | collective-permute-start | bytes 1179656 | tf_op jit(solution)/shard_map/ppermute | solution.py:304
  106.7 11.7 %collective-permute-start.23 = (bf16[768,256]{1,0:T(8,128)(2,1)S(1)}, bf16[768,256]{1,0:T(8,128)(2,1)S(1)}, u32[]{:S(2)}, u32[]{:S(2)}) collective-permute-start(bf16[768,256]{1,0:T(8,128)(2,1)S(1)} %collective-permute-done.22.near_ref), channel_id=1, source_target_pairs={{0,8},{4,28},{8,16},{12,4},{16,24},{20,12},{24,0},{28,20},{1,9},{5... | collective-permute-start | bytes 1179656 | tf_op jit(solution)/shard_map/ppermute | solution.py:334
  108.3 13.7 %collective-permute-start.27 = (bf16[768,256]{1,0:T(8,128)(2,1)S(1)}, bf16[768,256]{1,0:T(8,128)(2,1)S(1)}, u32[]{:S(2)}, u32[]{:S(2)}) collective-permute-start(bf16[768,256]{1,0:T(8,128)(2,1)S(1)} %get-tuple-element.340.refs_1_.refs_2_.refs_11_), channel_id=1, source_target_pairs={{0,2},{1,3},{2,0},{3,1},{4,6},{5,7},{6,4},{7,5},{8,10},{9,11},{10,... | collective-permute-start | bytes 1179656 | tf_op jit(solution)/shard_map/ppermute | solution.py:304
  110.1 11.8 %collective-permute-start.30 = (bf16[768,256]{1,0:T(8,128)(2,1)S(1)}, bf16[768,256]{1,0:T(8,128)(2,1)S(1)}, u32[]{:S(2)}, u32[]{:S(2)}) collective-permute-start(bf16[768,256]{1,0:T(8,128)(2,1)S(1)} %get-tuple-element.340.refs_1_.refs_2_.refs_11_), channel_id=1, source_target_pairs={{0,1},{1,0},{2,3},{3,2},{4,5},{5,4},{6,7},{7,6},{8,9},{9,8},{10,11... | collective-permute-start | bytes 1179656 | tf_op jit(solution)/shard_map/ppermute | solution.py:304
  111.5 14.6 %collective-permute-start.29 = (bf16[768,256]{1,0:T(8,128)(2,1)S(1)}, bf16[768,256]{1,0:T(8,128)(2,1)S(1)}, u32[]{:S(2)}, u32[]{:S(2)}) collective-permute-start(bf16[768,256]{1,0:T(8,128)(2,1)S(1)} %get-tuple-element.351.refs_2_.refs_3_.refs_12_), channel_id=1, source_target_pairs={{0,2},{1,3},{2,0},{3,1},{4,6},{5,7},{6,4},{7,5},{8,10},{9,11},{10,... | collective-permute-start | bytes 1179656 | tf_op jit(solution)/shard_map/ppermute | solution.py:304
  126.1 19.4 %collective-permute-start.35 = (bf16[384,1024]{1,0:T(8,128)(2,1)S(1)}, bf16[384,1024]{1,0:T(8,128)(2,1)S(1)}, u32[]{:S(2)}, u32[]{:S(2)}) collective-permute-start(bf16[384,1024]{1,0:T(8,128)(2,1)S(1)} %get-tuple-element.384), channel_id=1, source_target_pairs={{0,4},{4,0},{8,12},{12,8},{16,20},{20,16},{24,28},{28,24},{1,5},{5... | collective-permute-start | bytes 2359304 | tf_op jit(solution)/shard_map/ppermute | solution.py:400
  129.9 8.8 %collective-permute-start.32 = (bf16[784,256]{1,0:T(8,128)(2,1)S(1)}, bf16[784,256]{1,0:T(8,128)(2,1)S(1)}, u32[]{:S(2)}, u32[]{:S(2)}) collective-permute-start(bf16[784,256]{1,0:T(8,128)(2,1)S(1)} %product_2.7.refs_3_.refs_4_.refs_13_), channel_id=1, source_target_pairs={{0,2},{1,3},{2,0},{3,1},{4,6},{5,7},{6,4},{7,5},{8,10},{9,11},{10,... | collective-permute-start | bytes 1204232 | tf_op jit(solution)/shard_map/ppermute | solution.py:304
  131.4 7.8 %collective-permute-start.36 = (bf16[784,256]{1,0:T(8,128)(2,1)S(1)}, bf16[784,256]{1,0:T(8,128)(2,1)S(1)}, u32[]{:S(2)}, u32[]{:S(2)}) collective-permute-start(bf16[784,256]{1,0:T(8,128)(2,1)S(1)} %product_2.7.refs_3_.refs_4_.refs_13_), channel_id=1, source_target_pairs={{0,1},{1,0},{2,3},{3,2},{4,5},{5,4},{6,7},{7,6},{8,9},{9,8},{10,11... | collective-permute-start | bytes 1204232 | tf_op jit(solution)/shard_map/ppermute | solution.py:304
  138.7 7.5 %collective-permute-start.34 = (bf16[784,256]{1,0:T(8,128)(2,1)S(1)}, bf16[784,256]{1,0:T(8,128)(2,1)S(1)}, u32[]{:S(2)}, u32[]{:S(2)}) collective-permute-start(bf16[784,256]{1,0:T(8,128)(2,1)S(1)} %collective-permute-done.32.refs_7_.refs_9_.refs_4_), channel_id=1, source_target_pairs={{0,1},{1,0},{2,3},{3,2},{4,5},{5,4},{6,7},{7,6},{8,9},{9,8},{10,11... | collective-permute-start | bytes 1204232 | tf_op jit(solution)/shard_map/ppermute | solution.py:304
  138.7 7.4 %collective-permute-start.26 = (bf16[768,256]{1,0:T(8,128)(2,1)S(1)}, bf16[768,256]{1,0:T(8,128)(2,1)S(1)}, u32[]{:S(2)}, u32[]{:S(2)}) collective-permute-start(bf16[768,256]{1,0:T(8,128)(2,1)S(1)} %collective-permute-done.25.refs_4_.refs_1_), channel_id=1, source_target_pairs={{0,1},{1,0},{2,3},{3,2},{4,5},{5,4},{6,7},{7,6},{8,9},{9,8},{10,11... | collective-permute-start | bytes 1179656 | tf_op jit(solution)/shard_map/ppermute | solution.py:304
  139.2 6.9 %collective-permute-start.28 = (bf16[768,256]{1,0:T(8,128)(2,1)S(1)}, bf16[768,256]{1,0:T(8,128)(2,1)S(1)}, u32[]{:S(2)}, u32[]{:S(2)}) collective-permute-start(bf16[768,256]{1,0:T(8,128)(2,1)S(1)} %collective-permute-done.27.refs_5_.refs_2_), channel_id=1, source_target_pairs={{0,1},{1,0},{2,3},{3,2},{4,5},{5,4},{6,7},{7,6},{8,9},{9,8},{10,11... | collective-permute-start | bytes 1179656 | tf_op jit(solution)/shard_map/ppermute | solution.py:304
  139.2 7.0 %collective-permute-start.31 = (bf16[768,256]{1,0:T(8,128)(2,1)S(1)}, bf16[768,256]{1,0:T(8,128)(2,1)S(1)}, u32[]{:S(2)}, u32[]{:S(2)}) collective-permute-start(bf16[768,256]{1,0:T(8,128)(2,1)S(1)} %collective-permute-done.29.refs_6_.refs_3_), channel_id=1, source_target_pairs={{0,1},{1,0},{2,3},{3,2},{4,5},{5,4},{6,7},{7,6},{8,9},{9,8},{10,11... | collective-permute-start | bytes 1179656 | tf_op jit(solution)/shard_map/ppermute | solution.py:304
  145.5 16.4 %collective-permute-start.39 = (bf16[256,1024]{1,0:T(8,128)(2,1)S(1)}, bf16[256,1024]{1,0:T(8,128)(2,1)S(1)}, u32[]{:S(2)}, u32[]{:S(2)}) collective-permute-start(bf16[256,1024]{1,0:T(8,128)(2,1)S(1)} %get-tuple-element.415), channel_id=1, source_target_pairs={{0,8},{4,12},{8,0},{12,4},{16,24},{20,28},{24,16},{28,20},{1,9},{5... | collective-permute-start | bytes 1572872 | tf_op jit(solution)/shard_map/ppermute | solution.py:400
  148.0 19.6 %collective-permute-start.37 = (bf16[272,1024]{1,0:T(8,128)(2,1)S(1)}, bf16[272,1024]{1,0:T(8,128)(2,1)S(1)}, u32[]{:S(2)}, u32[]{:S(2)}) collective-permute-start(bf16[272,1024]{1,0:T(8,128)(2,1)S(1)} %get-tuple-element.412), channel_id=1, source_target_pairs={{0,4},{4,0},{8,12},{12,8},{16,20},{20,16},{24,28},{28,24},{1,5},{5... | collective-permute-start | bytes 1671176 | tf_op jit(solution)/shard_map/ppermute | solution.py:400
  149.8 17.1 %collective-permute-start.38 = (bf16[192,1024]{1,0:T(8,128)(2,1)S(1)}, bf16[192,1024]{1,0:T(8,128)(2,1)S(1)}, u32[]{:S(2)}, u32[]{:S(2)}) collective-permute-start(bf16[192,1024]{1,0:T(8,128)(2,1)S(1)} %sum_hop.8), channel_id=1, source_target_pairs={{0,16},{4,20},{8,24},{12,28},{16,0},{20,4},{24,8},{28,12},{1,17},{... | collective-permute-start | bytes 1179656 | tf_op jit(solution)/shard_map/ppermute | solution.py:400
  152.5 23.0 %collective-permute-start.41 = (bf16[256,1024]{1,0:T(8,128)(2,1)S(1)}, bf16[256,1024]{1,0:T(8,128)(2,1)S(1)}, u32[]{:S(2)}, u32[]{:S(2)}) collective-permute-start(bf16[256,1024]{1,0:T(8,128)(2,1)S(1)} %get-tuple-element.439), channel_id=1, source_target_pairs={{0,4},{4,0},{8,12},{12,8},{16,20},{20,16},{24,28},{28,24},{1,5},{5... | collective-permute-start | bytes 1572872 | tf_op jit(solution)/shard_map/ppermute | solution.py:400
  167.6 7.9 %collective-permute-start.42 = (bf16[96,1024]{1,0:T(8,128)(2,1)S(1)}, bf16[96,1024]{1,0:T(8,128)(2,1)S(1)}, u32[]{:S(2)}, u32[]{:S(2)}) collective-permute-start(bf16[96,1024]{1,0:T(8,128)(2,1)S(1)} %sum_hop.10), channel_id=1, source_target_pairs={{0,8},{4,12},{8,0},{12,4},{16,24},{20,28},{24,16},{28,20},{1,9},{5... | collective-permute-start | bytes 589832 | tf_op jit(solution)/shard_map/ppermute | solution.py:400
  168.3 14.3 %collective-permute-start.40 = (bf16[144,1024]{1,0:T(8,128)(2,1)S(1)}, bf16[144,1024]{1,0:T(8,128)(2,1)S(1)}, u32[]{:S(2)}, u32[]{:S(2)}) collective-permute-start(bf16[144,1024]{1,0:T(8,128)(2,1)S(1)} %sum_hop.11), channel_id=1, source_target_pairs={{0,8},{4,12},{8,0},{12,4},{16,24},{20,28},{24,16},{28,20},{1,9},{5... | collective-permute-start | bytes 884744 | tf_op jit(solution)/shard_map/ppermute | solution.py:400
  170.4 13.0 %collective-permute-start.45 = (bf16[128,1024]{1,0:T(8,128)(2,1)S(1)}, bf16[128,1024]{1,0:T(8,128)(2,1)S(1)}, u32[]{:S(2)}, u32[]{:S(2)}) collective-permute-start(bf16[128,1024]{1,0:T(8,128)(2,1)S(1)} %sum_hop.9), channel_id=1, source_target_pairs={{0,4},{4,0},{8,12},{12,8},{16,20},{20,16},{24,28},{28,24},{1,5},{5... | collective-permute-start | bytes 786440 | tf_op jit(solution)/shard_map/ppermute | solution.py:400
  176.1 9.4 %collective-permute-start.44 = (bf16[128,1024]{1,0:T(8,128)(2,1)S(1)}, bf16[128,1024]{1,0:T(8,128)(2,1)S(1)}, u32[]{:S(2)}, u32[]{:S(2)}) collective-permute-start(bf16[128,1024]{1,0:T(8,128)(2,1)S(1)} %sum_hop.12), channel_id=1, source_target_pairs={{0,8},{4,12},{8,0},{12,4},{16,24},{20,28},{24,16},{28,20},{1,9},{5... | collective-permute-start | bytes 786440 | tf_op jit(solution)/shard_map/ppermute | solution.py:400
  183.3 12.4 %collective-permute-start.43 = (bf16[80,1024]{1,0:T(8,128)(2,1)S(1)}, bf16[80,1024]{1,0:T(8,128)(2,1)S(1)}, u32[]{:S(2)}, u32[]{:S(2)}) collective-permute-start(bf16[80,1024]{1,0:T(8,128)(2,1)S(1)} %sum_hop.13), channel_id=1, source_target_pairs={{0,16},{4,20},{8,24},{12,28},{16,0},{20,4},{24,8},{28,12},{1,17},{... | collective-permute-start | bytes 491528 | tf_op jit(solution)/shard_map/ppermute | solution.py:400
  186.1 9.6 %collective-permute-start.46 = (bf16[64,1024]{1,0:T(8,128)(2,1)S(1)}, bf16[64,1024]{1,0:T(8,128)(2,1)S(1)}, u32[]{:S(2)}, u32[]{:S(2)}) collective-permute-start(bf16[64,1024]{1,0:T(8,128)(2,1)S(1)} %sum_hop.15), channel_id=1, source_target_pairs={{0,16},{4,20},{8,24},{12,28},{16,0},{20,4},{24,8},{28,12},{1,17},{... | collective-permute-start | bytes 393224 | tf_op jit(solution)/shard_map/ppermute | solution.py:400
  197.1 9.2 %collective-permute-start.48 = (bf16[64,1024]{1,0:T(8,128)(2,1)S(1)}, bf16[64,1024]{1,0:T(8,128)(2,1)S(1)}, u32[]{:S(2)}, u32[]{:S(2)}) collective-permute-start(bf16[64,1024]{1,0:T(8,128)(2,1)S(1)} %sum_last.7.upper_ref), channel_id=1, source_target_pairs={{0,16},{4,20},{8,24},{12,28},{16,0},{20,4},{24,8},{28,12},{1,17},{... | collective-permute-start | bytes 393224 | tf_op jit(solution)/shard_map/ppermute | solution.py:400
  197.9 20.4 %collective-permute-start.51 = (bf16[96,1024]{1,0:T(8,128)(2,1)S(1)}, bf16[96,1024]{1,0:T(8,128)(2,1)S(1)}, u32[]{:S(2)}, u32[]{:S(2)}) collective-permute-start(bf16[96,1024]{1,0:T(8,128)(2,1)S(1)} %sum_last.5.upper_ref), channel_id=1, source_target_pairs={{0,8},{4,12},{8,0},{12,4},{16,24},{20,28},{24,16},{28,20},{1,9},{5... | collective-permute-start | bytes 589832 | tf_op jit(solution)/shard_map/ppermute | solution.py:400
  200.6 14.0 %collective-permute-start.47 = (bf16[64,1024]{1,0:T(8,128)(2,1)S(1)}, bf16[64,1024]{1,0:T(8,128)(2,1)S(1)}, u32[]{:S(2)}, u32[]{:S(2)}) collective-permute-start(bf16[64,1024]{1,0:T(8,128)(2,1)S(1)} %sum_hop.14), channel_id=1, source_target_pairs={{0,16},{4,20},{8,24},{12,28},{16,0},{20,4},{24,8},{28,12},{1,17},{... | collective-permute-start | bytes 393224 | tf_op jit(solution)/shard_map/ppermute | solution.py:400
  206.2 24.6 %collective-permute-start.52 = (bf16[128,1024]{1,0:T(8,128)(2,1)S(1)}, bf16[128,1024]{1,0:T(8,128)(2,1)S(1)}, u32[]{:S(2)}, u32[]{:S(2)}) collective-permute-start(bf16[128,1024]{1,0:T(8,128)(2,1)S(1)} %join.11.upper_ref), channel_id=1, source_target_pairs={{0,8},{4,12},{8,0},{12,4},{16,24},{20,28},{24,16},{28,20},{1,9},{5... | collective-permute-start | bytes 786440 | tf_op jit(solution)/shard_map/ppermute | solution.py:400
  215.3 13.7 %collective-permute-start.49 = (bf16[64,1024]{1,0:T(8,128)(2,1)S(1)}, bf16[64,1024]{1,0:T(8,128)(2,1)S(1)}, u32[]{:S(2)}, u32[]{:S(2)}) collective-permute-start(bf16[64,1024]{1,0:T(8,128)(2,1)S(1)} %sum_last.6.upper_ref), channel_id=1, source_target_pairs={{0,16},{4,20},{8,24},{12,28},{16,0},{20,4},{24,8},{28,12},{1,17},{... | collective-permute-start | bytes 393224 | tf_op jit(solution)/shard_map/ppermute | solution.py:400
  215.3 15.4 %collective-permute-start.50 = (bf16[64,1024]{1,0:T(8,128)(2,1)S(1)}, bf16[64,1024]{1,0:T(8,128)(2,1)S(1)}, u32[]{:S(2)}, u32[]{:S(2)}) collective-permute-start(bf16[64,1024]{1,0:T(8,128)(2,1)S(1)} %get-tuple-element.475.upper_ref), channel_id=1, source_target_pairs={{0,16},{4,20},{8,24},{12,28},{16,0},{20,4},{24,8},{28,12},{1,17},{... | collective-permute-start | bytes 393224 | tf_op jit(solution)/shard_map/ppermute | solution.py:400
  218.3 22.0 %collective-permute-start.61 = (bf16[192,1024]{1,0:T(8,128)(2,1)S(1)}, bf16[192,1024]{1,0:T(8,128)(2,1)S(1)}, u32[]{:S(2)}, u32[]{:S(2)}) collective-permute-start(bf16[192,1024]{1,0:T(8,128)(2,1)S(1)} %join.8.upper_ref), channel_id=1, source_target_pairs={{0,16},{4,20},{8,24},{12,28},{16,0},{20,4},{24,8},{28,12},{1,17},{... | collective-permute-start | bytes 1179656 | tf_op jit(solution)/shard_map/ppermute | solution.py:400
  230.7 7.0 %collective-permute-start.57 = (bf16[128,1024]{1,0:T(8,128)(2,1)S(1)}, bf16[128,1024]{1,0:T(8,128)(2,1)S(1)}, u32[]{:S(2)}, u32[]{:S(2)}) collective-permute-start(bf16[128,1024]{1,0:T(8,128)(2,1)S(1)} %join.9.upper_ref), channel_id=1, source_target_pairs={{0,8},{4,12},{8,0},{12,4},{16,24},{20,28},{24,16},{28,20},{1,9},{5... | collective-permute-start | bytes 786440 | tf_op jit(solution)/shard_map/ppermute | solution.py:400
  230.9 13.5 %collective-permute-start.53 = (bf16[256,1024]{1,0:T(8,128)(2,1)S(1)}, bf16[256,1024]{1,0:T(8,128)(2,1)S(1)}, u32[]{:S(2)}, u32[]{:S(2)}) collective-permute-start(bf16[256,1024]{1,0:T(8,128)(2,1)S(1)} %join.12.refs_4_), channel_id=1, source_target_pairs={{0,4},{4,0},{8,12},{12,8},{16,20},{20,16},{24,28},{28,24},{1,5},{5... | collective-permute-start | bytes 1572872 | tf_op jit(solution)/shard_map/ppermute | solution.py:400
  233.2 13.5 %collective-permute-start.54 = (bf16[256,1024]{1,0:T(8,128)(2,1)S(1)}, bf16[256,1024]{1,0:T(8,128)(2,1)S(1)}, u32[]{:S(2)}, u32[]{:S(2)}) collective-permute-start(bf16[256,1024]{1,0:T(8,128)(2,1)S(1)} %join.12.refs_4_), channel_id=1, source_target_pairs={{0,1},{1,0},{2,3},{3,2},{4,5},{5,4},{6,7},{7,6},{8,9},{9,8},{10,11... | collective-permute-start | bytes 1572872 | tf_op jit(solution)/shard_map/ppermute | solution.py:304
  235.5 12.2 %collective-permute-start.59 = (bf16[256,1024]{1,0:T(8,128)(2,1)S(1)}, bf16[256,1024]{1,0:T(8,128)(2,1)S(1)}, u32[]{:S(2)}, u32[]{:S(2)}) collective-permute-start(bf16[256,1024]{1,0:T(8,128)(2,1)S(1)} %join.14.refs_5_), channel_id=1, source_target_pairs={{0,2},{1,3},{2,0},{3,1},{4,6},{5,7},{6,4},{7,5},{8,10},{9,11},{10,... | collective-permute-start | bytes 1572872 | tf_op jit(solution)/shard_map/ppermute | solution.py:304
  237.8 17.8 %collective-permute-start.63 = (bf16[256,1024]{1,0:T(8,128)(2,1)S(1)}, bf16[256,1024]{1,0:T(8,128)(2,1)S(1)}, u32[]{:S(2)}, u32[]{:S(2)}) collective-permute-start(bf16[256,1024]{1,0:T(8,128)(2,1)S(1)} %join.13.refs_6_), channel_id=1, source_target_pairs={{0,4},{4,0},{8,12},{12,8},{16,20},{20,16},{24,28},{28,24},{1,5},{5... | collective-permute-start | bytes 1572872 | tf_op jit(solution)/shard_map/ppermute | solution.py:400
  240.3 17.2 %collective-permute-start.58 = (bf16[256,1024]{1,0:T(8,128)(2,1)S(1)}, bf16[256,1024]{1,0:T(8,128)(2,1)S(1)}, u32[]{:S(2)}, u32[]{:S(2)}) collective-permute-start(bf16[256,1024]{1,0:T(8,128)(2,1)S(1)} %join.14.refs_5_), channel_id=1, source_target_pairs={{0,8},{4,12},{8,0},{12,4},{16,24},{20,28},{24,16},{28,20},{1,9},{5... | collective-permute-start | bytes 1572872 | tf_op jit(solution)/shard_map/ppermute | solution.py:400
  244.3 24.8 %collective-permute-start.62 = (bf16[384,1024]{1,0:T(8,128)(2,1)S(1)}, bf16[384,1024]{1,0:T(8,128)(2,1)S(1)}, u32[]{:S(2)}, u32[]{:S(2)}) collective-permute-start(bf16[384,1024]{1,0:T(8,128)(2,1)S(1)} %join.15.refs_5_), channel_id=1, source_target_pairs={{0,4},{4,0},{8,12},{12,8},{16,20},{20,16},{24,28},{28,24},{1,5},{5... | collective-permute-start | bytes 2359304 | tf_op jit(solution)/shard_map/ppermute | solution.py:400
  246.7 13.2 %collective-permute-start.64 = (bf16[256,1024]{1,0:T(8,128)(2,1)S(1)}, bf16[256,1024]{1,0:T(8,128)(2,1)S(1)}, u32[]{:S(2)}, u32[]{:S(2)}) collective-permute-start(bf16[256,1024]{1,0:T(8,128)(2,1)S(1)} %join.13.refs_6_), channel_id=1, source_target_pairs={{0,3},{1,2},{2,1},{3,0},{4,7},{5,6},{6,5},{7,4},{8,11},{9,10},{10,... | collective-permute-start | bytes 1572872 | tf_op jit(solution)/shard_map/ppermute | solution.py:304
  247.7 12.3 %collective-permute-start.55 = (bf16[256,1024]{1,0:T(8,128)(2,1)S(1)}, bf16[256,1024]{1,0:T(8,128)(2,1)S(1)}, u32[]{:S(2)}, u32[]{:S(2)}) collective-permute-start(bf16[256,1024]{1,0:T(8,128)(2,1)S(1)} %collective-permute-done.53.refs_5_), channel_id=1, source_target_pairs={{0,1},{1,0},{2,3},{3,2},{4,5},{5,4},{6,7},{7,6},{8,9},{9,8},{10,11... | collective-permute-start | bytes 1572872 | tf_op jit(solution)/shard_map/ppermute | solution.py:304
  255.6 16.2 %collective-permute-start.60 = (bf16[256,1024]{1,0:T(8,128)(2,1)S(1)}, bf16[256,1024]{1,0:T(8,128)(2,1)S(1)}, u32[]{:S(2)}, u32[]{:S(2)}) collective-permute-start(bf16[256,1024]{1,0:T(8,128)(2,1)S(1)} %collective-permute-done.59.refs_7_), channel_id=1, source_target_pairs={{0,8},{4,12},{8,0},{12,4},{16,24},{20,28},{24,16},{28,20},{1,9},{5... | collective-permute-start | bytes 1572872 | tf_op jit(solution)/shard_map/ppermute | solution.py:400
  257.5 19.8 %collective-permute-start.65 = (bf16[256,1024]{1,0:T(8,128)(2,1)S(1)}, bf16[256,1024]{1,0:T(8,128)(2,1)S(1)}, u32[]{:S(2)}, u32[]{:S(2)}) collective-permute-start(bf16[256,1024]{1,0:T(8,128)(2,1)S(1)} %collective-permute-done.63.refs_7_), channel_id=1, source_target_pairs={{0,3},{1,2},{2,1},{3,0},{4,7},{5,6},{6,5},{7,4},{8,11},{9,10},{10,... | collective-permute-start | bytes 1572872 | tf_op jit(solution)/shard_map/ppermute | solution.py:304
  (3 other events, 14.4 us)

commit v14 on v13

--- a/solution.py
+++ b/solution.py
@@ -441,7 +441,9 @@
         need = list(there) if extra else [d] if d else []
         while any(other not in pieces[-1] or there[other] > clock.now for other in need):
             yield clock.now + 0.5
-        mine, value = order(*gram_chunk(d, masks[0], extra))
+        mine, value = gram_chunk(d, masks[0], extra)
+        if d:
+            mine, value = order(mine, value)
         terms = [mine]
         height = mine.shape[0] - extra
 
@@ -475,7 +477,9 @@
         else:
             part = order(part)
         for mask in masks[:0:-1]:
-            received, arrival = over_tiles(part, mask)
+            while mask != masks[-1] and d == 0 and behind not in sent:
+                yield clock.now + 0.5
+            received, arrival = over_tiles(order(part), mask)
             yield arrival
             joined = jax.ShapeDtypeStruct((2 * part.shape[0], columns), BF16)
             part = order(call(join_kernel, "join", joined, (), (part, order(received))))

time: 282 us -> 291 us (1.032)
  waiting for transfers between devices: 138 us -> 148 us
    ppermute x25, waiting for transfers between devices: 86.1 us -> 91.5 us  [over_tiles(): sent = lax.ppermute(value, 'elem', [(i, i ^ mask) for i in range(tiles)])]
    ppermute x17, waiting for transfers between devices: 14.3 us -> 19.2 us  [to_group(): return lax.ppermute(value, 'orb', [(i, i ^ d) for i in range(groups)])]
  transfers between devices with their start and end apart: 66 -> 66, of which waited for: 35 -> 32; matrix products, arithmetic and copies ran while one was open for 3% -> 3% of each run, Pallas kernels for 13% -> 13%
where the time goes in v14:
time: 291 us
  waiting for transfers between devices  148 us (51%)
  starting transfers between devices  90.6 us (31%)
  Pallas kernels  42.7 us (15%)
  local copies, waits for them, and re-layouts  6.77 us (2%)
    ppermute x25, waiting for transfers between devices, over_tiles(): sent = lax.ppermute(value, 'elem', [(i, i ^ mask) for i in range(tiles)])  91.5 us
    pallas_call x40, Pallas kernels, call(): pl.pallas_call(kernel, out_shape=outs, in_specs=[pl.BlockSpec(memory_spac...  42.7 us
    ppermute x25, starting transfers between devices, over_tiles(): sent = lax.ppermute(value, 'elem', [(i, i ^ mask) for i in range(tiles)])  28.6 us
    ppermute x8, starting transfers between devices, multiply(): near[stage + 1, c] = lax.ppermute(out, 'elem', swap)  23.7 us
    ppermute x8, waiting for transfers between devices, multiply(): near[stage + 1, c] = lax.ppermute(out, 'elem', swap)  20.8 us
    ppermute x17, waiting for transfers between devices, to_group(): return lax.ppermute(value, 'orb', [(i, i ^ d) for i in range(groups)])  19.2 us
    ppermute x12, starting transfers between devices, send_on(): far[job] = lax.ppermute(near[job], 'elem', outward)  18.9 us
    ppermute x3, waiting for transfers between devices, local(): near[0, c] = lax.ppermute(start[c], 'elem', swap)  9.1 us
  transfers between devices with their start and end apart: 66, of which 32 were waited for; matrix products, arithmetic and copies ran while one was open for 3% of the time, Pallas kernels for 13%

profile of v14, /device:TPU:0, one launch (start us, length us, event | category | flops | bytes accessed | tf_op | source)
XLA Modules:
  0.0 290.8 jit_solution(13787012669553798288)
XLA Ops:
  1.5 3.0 %collective-permute-start = (bf16[768,256]{1,0:T(8,128)(2,1)S(1)}, bf16[768,256]{1,0:T(8,128)(2,1)S(1)}, u32[]{:S(2)}, u32[]{:S(2)}) collective-permute-start(bf16[768,256]{1,0:T(8,128)(2,1)S(1)} %get-tuple-element.529.field_ref.refs_0_), channel_id=1, source_target_pairs={{0,4},{4,0},{8,12},{12,8},{16,20},{20,16},{24,28},{28,24},{1,5},{5... | collective-permute-start | bytes 1179656 | tf_op jit(solution)/shard_map/ppermute | solution.py:317
  4.5 2.2 slice_bitcast_fusion
  8.7 2.3 concatenate.6.blocks_ref
  11.9 2.1 collective-permute-done.near_ref
  15.5 4.5 %collective-permute-start.4 = (bf16[768,256]{1,0:T(8,128)(2,1)S(1)}, bf16[768,256]{1,0:T(8,128)(2,1)S(1)}, u32[]{:S(2)}, u32[]{:S(2)}) collective-permute-start(bf16[768,256]{1,0:T(8,128)(2,1)S(1)} %get-tuple-element.280.field_ref.refs_0_), channel_id=1, source_target_pairs={{0,4},{4,0},{8,12},{12,8},{16,20},{20,16},{24,28},{28,24},{1,5},{5... | collective-permute-start | bytes 1179656 | tf_op jit(solution)/shard_map/ppermute | solution.py:325
  20.0 3.9 %collective-permute-done.2.near_ref = bf16[768,256]{1,0:T(8,128)(2,1)S(1)} collective-permute-done((bf16[768,256]{1,0:T(8,128)(2,1)S(1)}, bf16[768,256]{1,0:T(8,128)(2,1)S(1)}, u32[]{:S(2)}, u32[]{:S(2)}) %collective-permute-start.2) | collective-permute-done | bytes 393248 | tf_op jit(solution)/shard_map/ppermute | solution.py:325
  23.9 1.6 collective-permute-start.7
  25.5 3.0 %collective-permute-start.6 = (bf16[768,256]{1,0:T(8,128)(2,1)S(1)}, bf16[768,256]{1,0:T(8,128)(2,1)S(1)}, u32[]{:S(2)}, u32[]{:S(2)}) collective-permute-start(bf16[768,256]{1,0:T(8,128)(2,1)S(1)} %get-tuple-element.283.field_ref.refs_0_), channel_id=1, source_target_pairs={{0,4},{4,0},{8,12},{12,8},{16,20},{20,16},{24,28},{28,24},{1,5},{5... | collective-permute-start | bytes 1179656 | tf_op jit(solution)/shard_map/ppermute | solution.py:325
  29.7 2.6 collective-permute-done.4.near_ref
  32.3 1.6 collective-permute-start.5
  33.9 3.0 %collective-permute-start.3 = (bf16[768,256]{1,0:T(8,128)(2,1)S(1)}, bf16[768,256]{1,0:T(8,128)(2,1)S(1)}, u32[]{:S(2)}, u32[]{:S(2)}) collective-permute-start(bf16[768,256]{1,0:T(8,128)(2,1)S(1)} %get-tuple-element.279.field_ref), channel_id=1, source_target_pairs={{0,4},{4,0},{8,12},{12,8},{16,20},{20,16},{24,28},{28,24},{1,5},{5... | collective-permute-start | bytes 1179656 | tf_op jit(solution)/shard_map/ppermute | solution.py:376
  38.1 2.6 collective-permute-done.6.near_ref
  40.7 1.6 collective-permute-start.10
  42.3 3.0 %collective-permute-start.9 = (bf16[768,256]{1,0:T(8,128)(2,1)S(1)}, bf16[768,256]{1,0:T(8,128)(2,1)S(1)}, u32[]{:S(2)}, u32[]{:S(2)}) collective-permute-start(bf16[768,256]{1,0:T(8,128)(2,1)S(1)} %get-tuple-element.298.field_ref), channel_id=1, source_target_pairs={{0,4},{4,0},{8,12},{12,8},{16,20},{20,16},{24,28},{28,24},{1,5},{5... | collective-permute-start | bytes 1179656 | tf_op jit(solution)/shard_map/ppermute | solution.py:376
  46.6 2.6 collective-permute-done.3.near_ref
  49.2 1.6 collective-permute-start.8
  50.7 3.0 %collective-permute-start.12 = (bf16[768,256]{1,0:T(8,128)(2,1)S(1)}, bf16[768,256]{1,0:T(8,128)(2,1)S(1)}, u32[]{:S(2)}, u32[]{:S(2)}) collective-permute-start(bf16[768,256]{1,0:T(8,128)(2,1)S(1)} %get-tuple-element.310.field_ref), channel_id=1, source_target_pairs={{0,4},{4,0},{8,12},{12,8},{16,20},{20,16},{24,28},{28,24},{1,5},{5... | collective-permute-start | bytes 1179656 | tf_op jit(solution)/shard_map/ppermute | solution.py:376
  55.0 2.6 collective-permute-done.9.near_ref
  57.6 1.6 collective-permute-start.15
  59.2 3.0 %collective-permute-start.14 = (bf16[768,256]{1,0:T(8,128)(2,1)S(1)}, bf16[768,256]{1,0:T(8,128)(2,1)S(1)}, u32[]{:S(2)}, u32[]{:S(2)}) collective-permute-start(bf16[768,256]{1,0:T(8,128)(2,1)S(1)} %get-tuple-element.313.field_ref), channel_id=1, source_target_pairs={{0,4},{4,0},{8,12},{12,8},{16,20},{20,16},{24,28},{28,24},{1,5},{5... | collective-permute-start | bytes 1179656 | tf_op jit(solution)/shard_map/ppermute | solution.py:376
  63.4 2.6 collective-permute-done.12.near_ref
  66.0 1.6 collective-permute-start.13
  67.6 3.0 %collective-permute-start.11 = (bf16[768,256]{1,0:T(8,128)(2,1)S(1)}, bf16[768,256]{1,0:T(8,128)(2,1)S(1)}, u32[]{:S(2)}, u32[]{:S(2)}) collective-permute-start(bf16[768,256]{1,0:T(8,128)(2,1)S(1)} %product_1.4.field_ref), channel_id=1, source_target_pairs={{0,4},{4,0},{8,12},{12,8},{16,20},{20,16},{24,28},{28,24},{1,5},{5... | collective-permute-start | bytes 1179656 | tf_op jit(solution)/shard_map/ppermute | solution.py:376
  71.8 2.6 collective-permute-done.14.near_ref
  76.0 3.0 %collective-permute-start.17 = (bf16[768,256]{1,0:T(8,128)(2,1)S(1)}, bf16[768,256]{1,0:T(8,128)(2,1)S(1)}, u32[]{:S(2)}, u32[]{:S(2)}) collective-permute-start(bf16[768,256]{1,0:T(8,128)(2,1)S(1)} %product_1.5.field_ref), channel_id=1, source_target_pairs={{0,4},{4,0},{8,12},{12,8},{16,20},{20,16},{24,28},{28,24},{1,5},{5... | collective-permute-start | bytes 1179656 | tf_op jit(solution)/shard_map/ppermute | solution.py:376
  80.3 2.6 collective-permute-done.11.near_ref
  84.4 3.0 %collective-permute-start.20 = (bf16[768,256]{1,0:T(8,128)(2,1)S(1)}, bf16[768,256]{1,0:T(8,128)(2,1)S(1)}, u32[]{:S(2)}, u32[]{:S(2)}) collective-permute-start(bf16[768,256]{1,0:T(8,128)(2,1)S(1)} %product_1.6.field_ref), channel_id=1, source_target_pairs={{0,4},{4,0},{8,12},{12,8},{16,20},{20,16},{24,28},{28,24},{1,5},{5... | collective-permute-start | bytes 1179656 | tf_op jit(solution)/shard_map/ppermute | solution.py:376
  88.7 2.6 collective-permute-done.17.near_ref
  92.9 3.0 %collective-permute-start.22 = (bf16[768,256]{1,0:T(8,128)(2,1)S(1)}, bf16[768,256]{1,0:T(8,128)(2,1)S(1)}, u32[]{:S(2)}, u32[]{:S(2)}) collective-permute-start(bf16[768,256]{1,0:T(8,128)(2,1)S(1)} %product_1.7.field_ref), channel_id=1, source_target_pairs={{0,4},{4,0},{8,12},{12,8},{16,20},{20,16},{24,28},{28,24},{1,5},{5... | collective-permute-start | bytes 1179656 | tf_op jit(solution)/shard_map/ppermute | solution.py:376
  97.1 2.6 collective-permute-done.20.near_ref
  104.1 2.6 collective-permute-done.22.near_ref
  111.5 1.8 collective-permute-done.25.refs_4_.refs_1_
  113.2 5.2 %collective-permute-done.23.far_ref = bf16[768,256]{1,0:T(8,128)(2,1)S(1)} collective-permute-done((bf16[768,256]{1,0:T(8,128)(2,1)S(1)}, bf16[768,256]{1,0:T(8,128)(2,1)S(1)}, u32[]{:S(2)}, u32[]{:S(2)}) %collective-permute-start.23) | collective-permute-done | bytes 393248 | tf_op jit(solution)/shard_map/ppermute | solution.py:334
  119.9 2.1 gram_own.1
  125.4 15.0 %collective-permute-done.29.refs_6_.refs_3_ = bf16[768,256]{1,0:T(8,128)(2,1)S(1)} collective-permute-done((bf16[768,256]{1,0:T(8,128)(2,1)S(1)}, bf16[768,256]{1,0:T(8,128)(2,1)S(1)}, u32[]{:S(2)}, u32[]{:S(2)}) %collective-permute-start.29) | collective-permute-done | bytes 393248 | tf_op jit(solution)/shard_map/ppermute | solution.py:304
  141.4 1.6 gram_pair.3
  144.3 1.8 gram_pair.4
  146.7 4.2 %collective-permute-start.38 = (bf16[192,1024]{1,0:T(8,128)(2,1)S(1)}, bf16[192,1024]{1,0:T(8,128)(2,1)S(1)}, u32[]{:S(2)}, u32[]{:S(2)}) collective-permute-start(bf16[192,1024]{1,0:T(8,128)(2,1)S(1)} %sum_hop.8), channel_id=1, source_target_pairs={{0,16},{4,20},{8,24},{12,28},{16,0},{20,4},{24,8},{28,12},{1,17},{... | collective-permute-start | bytes 1179656 | tf_op jit(solution)/shard_map/ppermute | solution.py:400
  150.9 1.6 gram_pair.5
  152.6 1.7 collective-permute-start.41
  154.3 11.1 %collective-permute-done.39.refs_1_ = bf16[256,1024]{1,0:T(8,128)(2,1)S(1)} collective-permute-done((bf16[256,1024]{1,0:T(8,128)(2,1)S(1)}, bf16[256,1024]{1,0:T(8,128)(2,1)S(1)}, u32[]{:S(2)}, u32[]{:S(2)}) %collective-permute-start.39) | collective-permute-done | bytes 524320 | tf_op jit(solution)/shard_map/ppermute | solution.py:400
  166.0 2.2 collective-permute-done.38.refs_2_
  170.1 1.6 collective-permute-start.40
  171.7 1.7 collective-permute-start.45
  173.3 3.3 %collective-permute-done.42.refs_3_ = bf16[96,1024]{1,0:T(8,128)(2,1)S(1)} collective-permute-done((bf16[96,1024]{1,0:T(8,128)(2,1)S(1)}, bf16[96,1024]{1,0:T(8,128)(2,1)S(1)}, u32[]{:S(2)}, u32[]{:S(2)}) %collective-permute-start.42) | collective-permute-done | bytes 196640 | tf_op jit(solution)/shard_map/ppermute | solution.py:400
  177.9 6.8 %collective-permute-done.40.refs_2_ = bf16[144,1024]{1,0:T(8,128)(2,1)S(1)} collective-permute-done((bf16[144,1024]{1,0:T(8,128)(2,1)S(1)}, bf16[144,1024]{1,0:T(8,128)(2,1)S(1)}, u32[]{:S(2)}, u32[]{:S(2)}) %collective-permute-start.40) | collective-permute-done | bytes 294944 | tf_op jit(solution)/shard_map/ppermute | solution.py:400
  186.1 1.7 collective-permute-done.44.refs_2_
  188.4 2.0 collective-permute-start.46
  190.3 7.9 %collective-permute-done.46.refs_3_ = bf16[64,1024]{1,0:T(8,128)(2,1)S(1)} collective-permute-done((bf16[64,1024]{1,0:T(8,128)(2,1)S(1)}, bf16[64,1024]{1,0:T(8,128)(2,1)S(1)}, u32[]{:S(2)}, u32[]{:S(2)}) %collective-permute-start.46) | collective-permute-done | bytes 131104 | tf_op jit(solution)/shard_map/ppermute | solution.py:400
  200.4 2.6 collective-permute-start.50
  203.5 5.2 %collective-permute-done.48.lower_ref = bf16[64,1024]{1,0:T(8,128)(2,1)S(1)} collective-permute-done((bf16[64,1024]{1,0:T(8,128)(2,1)S(1)}, bf16[64,1024]{1,0:T(8,128)(2,1)S(1)}, u32[]{:S(2)}, u32[]{:S(2)}) %collective-permute-start.48) | collective-permute-done | bytes 131104 | tf_op jit(solution)/shard_map/ppermute | solution.py:400
  208.7 2.4 collective-permute-done.47.refs_3_
  211.8 3.4 %collective-permute-start.52 = (bf16[64,1024]{1,0:T(8,128)(2,1)S(1)}, bf16[64,1024]{1,0:T(8,128)(2,1)S(1)}, u32[]{:S(2)}, u32[]{:S(2)}) collective-permute-start(bf16[64,1024]{1,0:T(8,128)(2,1)S(1)} %sum_last.6.upper_ref), channel_id=1, source_target_pairs={{0,16},{4,20},{8,24},{12,28},{16,0},{20,4},{24,8},{28,12},{1,17},{... | collective-permute-start | bytes 393224 | tf_op jit(solution)/shard_map/ppermute | solution.py:400
  215.4 2.9 %collective-permute-start.63 = (bf16[192,1024]{1,0:T(8,128)(2,1)S(1)}, bf16[192,1024]{1,0:T(8,128)(2,1)S(1)}, u32[]{:S(2)}, u32[]{:S(2)}) collective-permute-start(bf16[192,1024]{1,0:T(8,128)(2,1)S(1)} %join.8.upper_ref), channel_id=1, source_target_pairs={{0,16},{4,20},{8,24},{12,28},{16,0},{20,4},{24,8},{28,12},{1,17},{... | collective-permute-start | bytes 1179656 | tf_op jit(solution)/shard_map/ppermute | solution.py:400
  218.3 14.7 %collective-permute-done.52.lower_ref = bf16[64,1024]{1,0:T(8,128)(2,1)S(1)} collective-permute-done((bf16[64,1024]{1,0:T(8,128)(2,1)S(1)}, bf16[64,1024]{1,0:T(8,128)(2,1)S(1)}, u32[]{:S(2)}, u32[]{:S(2)}) %collective-permute-start.52) | collective-permute-done | bytes 131104 | tf_op jit(solution)/shard_map/ppermute | solution.py:400
  234.1 1.8 collective-permute-done.49.lower_ref
  237.1 5.2 %collective-permute-done.56.lower_ref = bf16[128,1024]{1,0:T(8,128)(2,1)S(1)} collective-permute-done((bf16[128,1024]{1,0:T(8,128)(2,1)S(1)}, bf16[128,1024]{1,0:T(8,128)(2,1)S(1)}, u32[]{:S(2)}, u32[]{:S(2)}) %collective-permute-start.56) | collective-permute-done | bytes 262176 | tf_op jit(solution)/shard_map/ppermute | solution.py:400
  243.9 4.0 %collective-permute-done.51.lower_ref = bf16[128,1024]{1,0:T(8,128)(2,1)S(1)} collective-permute-done((bf16[128,1024]{1,0:T(8,128)(2,1)S(1)}, bf16[128,1024]{1,0:T(8,128)(2,1)S(1)}, u32[]{:S(2)}, u32[]{:S(2)}) %collective-permute-start.51) | collective-permute-done | bytes 262176 | tf_op jit(solution)/shard_map/ppermute | solution.py:400
  251.8 11.0 %collective-permute-done.54.refs_7_ = bf16[256,1024]{1,0:T(8,128)(2,1)S(1)} collective-permute-done((bf16[256,1024]{1,0:T(8,128)(2,1)S(1)}, bf16[256,1024]{1,0:T(8,128)(2,1)S(1)}, u32[]{:S(2)}, u32[]{:S(2)}) %collective-permute-start.54) | collective-permute-done | bytes 524320 | tf_op jit(solution)/shard_map/ppermute | solution.py:400
  264.3 14.4 %collective-permute-done.64.refs_6_ = bf16[384,1024]{1,0:T(8,128)(2,1)S(1)} collective-permute-done((bf16[384,1024]{1,0:T(8,128)(2,1)S(1)}, bf16[384,1024]{1,0:T(8,128)(2,1)S(1)}, u32[]{:S(2)}, u32[]{:S(2)}) %collective-permute-start.64) | collective-permute-done | bytes 786464 | tf_op jit(solution)/shard_map/ppermute | solution.py:400
  278.7 2.6 mix_pair.3.refs_0_
  281.3 2.9 %mix_pair.4.refs_0_ = f32[768,1024]{1,0:T(8,128)S(1)} custom-call(s32[2]{0:T(128)S(1)} %get-tuple-element.389.where_ref, f32[768,1024]{1,0:T(8,128)S(1)} %mix_pair.3.refs_0_, bf16[768,256]{1,0:T(8,128)(2,1)S(1)} %collective-permute-done.25.refs_4_.refs_1_, ...), custom_call_target="tpu_custom_call", output_to_operand_aliasing={{}: (1, {})} | custom-call | flops 1024 | bytes 5242880 | tf_op jit(solution)/shard_map/mix_pair/pallas_call | solution.py:96
  284.2 2.6 mix_own.1.refs_1_
  286.8 4.0 %mix_pair.5 = bf16[768,1024]{1,0:T(8,128)(2,1)} custom-call(s32[2]{0:T(128)S(1)} %get-tuple-element.389.where_ref, f32[8,128]{1,0:T(8,128)S(1)} %get-tuple-element.466.refs_4_.refs_0_, f32[768,1024]{1,0:T(8,128)S(1)} %mix_own.1.refs_1_, bf16[768,256]{1,0:T(8,128)(2,1)S(1)} %collective-permute-done.26.refs_4_.refs_2_, ...), custom_call_target="tpu_custom_call" | custom-call | flops 1024 | bytes 5242880 | tf_op jit(solution)/shard_map/mix_pair/pallas_call | solution.py:96
  (123 shorter events, 57.5 us)
Async XLA Ops:
  1.5 12.4 %collective-permute-start = (bf16[768,256]{1,0:T(8,128)(2,1)S(1)}, bf16[768,256]{1,0:T(8,128)(2,1)S(1)}, u32[]{:S(2)}, u32[]{:S(2)}) collective-permute-start(bf16[768,256]{1,0:T(8,128)(2,1)S(1)} %get-tuple-element.529.field_ref.refs_0_), channel_id=1, source_target_pairs={{0,4},{4,0},{8,12},{12,8},{16,20},{20,16},{24,28},{28,24},{1,5},{5... | collective-permute-start | bytes 1179656 | tf_op jit(solution)/shard_map/ppermute | solution.py:317
  11.8 12.0 %collective-permute-start.2 = (bf16[768,256]{1,0:T(8,128)(2,1)S(1)}, bf16[768,256]{1,0:T(8,128)(2,1)S(1)}, u32[]{:S(2)}, u32[]{:S(2)}) collective-permute-start(bf16[768,256]{1,0:T(8,128)(2,1)S(1)} %get-tuple-element.272.field_ref.refs_0_), channel_id=1, source_target_pairs={{0,4},{4,0},{8,12},{12,8},{16,20},{20,16},{24,28},{28,24},{1,5},{5... | collective-permute-start | bytes 1179656 | tf_op jit(solution)/shard_map/ppermute | solution.py:325
  13.9 14.5 %collective-permute-start.1 = (bf16[768,256]{1,0:T(8,128)(2,1)S(1)}, bf16[768,256]{1,0:T(8,128)(2,1)S(1)}, u32[]{:S(2)}, u32[]{:S(2)}) collective-permute-start(bf16[768,256]{1,0:T(8,128)(2,1)S(1)} %collective-permute-done.near_ref), channel_id=1, source_target_pairs={{0,8},{4,28},{8,16},{12,4},{16,24},{20,12},{24,0},{28,20},{1,9},{5... | collective-permute-start | bytes 1179656 | tf_op jit(solution)/shard_map/ppermute | solution.py:334
  15.5 16.8 %collective-permute-start.4 = (bf16[768,256]{1,0:T(8,128)(2,1)S(1)}, bf16[768,256]{1,0:T(8,128)(2,1)S(1)}, u32[]{:S(2)}, u32[]{:S(2)}) collective-permute-start(bf16[768,256]{1,0:T(8,128)(2,1)S(1)} %get-tuple-element.280.field_ref.refs_0_), channel_id=1, source_target_pairs={{0,4},{4,0},{8,12},{12,8},{16,20},{20,16},{24,28},{28,24},{1,5},{5... | collective-permute-start | bytes 1179656 | tf_op jit(solution)/shard_map/ppermute | solution.py:325
  23.9 13.0 %collective-permute-start.7 = (bf16[768,256]{1,0:T(8,128)(2,1)S(1)}, bf16[768,256]{1,0:T(8,128)(2,1)S(1)}, u32[]{:S(2)}, u32[]{:S(2)}) collective-permute-start(bf16[768,256]{1,0:T(8,128)(2,1)S(1)} %collective-permute-done.2.near_ref), channel_id=1, source_target_pairs={{0,8},{4,28},{8,16},{12,4},{16,24},{20,12},{24,0},{28,20},{1,9},{5... | collective-permute-start | bytes 1179656 | tf_op jit(solution)/shard_map/ppermute | solution.py:334
  25.5 15.3 %collective-permute-start.6 = (bf16[768,256]{1,0:T(8,128)(2,1)S(1)}, bf16[768,256]{1,0:T(8,128)(2,1)S(1)}, u32[]{:S(2)}, u32[]{:S(2)}) collective-permute-start(bf16[768,256]{1,0:T(8,128)(2,1)S(1)} %get-tuple-element.283.field_ref.refs_0_), channel_id=1, source_target_pairs={{0,4},{4,0},{8,12},{12,8},{16,20},{20,16},{24,28},{28,24},{1,5},{5... | collective-permute-start | bytes 1179656 | tf_op jit(solution)/shard_map/ppermute | solution.py:325
  32.3 13.0 %collective-permute-start.5 = (bf16[768,256]{1,0:T(8,128)(2,1)S(1)}, bf16[768,256]{1,0:T(8,128)(2,1)S(1)}, u32[]{:S(2)}, u32[]{:S(2)}) collective-permute-start(bf16[768,256]{1,0:T(8,128)(2,1)S(1)} %collective-permute-done.4.near_ref), channel_id=1, source_target_pairs={{0,8},{4,28},{8,16},{12,4},{16,24},{20,12},{24,0},{28,20},{1,9},{5... | collective-permute-start | bytes 1179656 | tf_op jit(solution)/shard_map/ppermute | solution.py:334
  33.9 15.3 %collective-permute-start.3 = (bf16[768,256]{1,0:T(8,128)(2,1)S(1)}, bf16[768,256]{1,0:T(8,128)(2,1)S(1)}, u32[]{:S(2)}, u32[]{:S(2)}) collective-permute-start(bf16[768,256]{1,0:T(8,128)(2,1)S(1)} %get-tuple-element.279.field_ref), channel_id=1, source_target_pairs={{0,4},{4,0},{8,12},{12,8},{16,20},{20,16},{24,28},{28,24},{1,5},{5... | collective-permute-start | bytes 1179656 | tf_op jit(solution)/shard_map/ppermute | solution.py:376
  40.7 13.0 %collective-permute-start.10 = (bf16[768,256]{1,0:T(8,128)(2,1)S(1)}, bf16[768,256]{1,0:T(8,128)(2,1)S(1)}, u32[]{:S(2)}, u32[]{:S(2)}) collective-permute-start(bf16[768,256]{1,0:T(8,128)(2,1)S(1)} %collective-permute-done.6.near_ref), channel_id=1, source_target_pairs={{0,8},{4,28},{8,16},{12,4},{16,24},{20,12},{24,0},{28,20},{1,9},{5... | collective-permute-start | bytes 1179656 | tf_op jit(solution)/shard_map/ppermute | solution.py:334
  42.3 15.3 %collective-permute-start.9 = (bf16[768,256]{1,0:T(8,128)(2,1)S(1)}, bf16[768,256]{1,0:T(8,128)(2,1)S(1)}, u32[]{:S(2)}, u32[]{:S(2)}) collective-permute-start(bf16[768,256]{1,0:T(8,128)(2,1)S(1)} %get-tuple-element.298.field_ref), channel_id=1, source_target_pairs={{0,4},{4,0},{8,12},{12,8},{16,20},{20,16},{24,28},{28,24},{1,5},{5... | collective-permute-start | bytes 1179656 | tf_op jit(solution)/shard_map/ppermute | solution.py:376
  49.2 13.0 %collective-permute-start.8 = (bf16[768,256]{1,0:T(8,128)(2,1)S(1)}, bf16[768,256]{1,0:T(8,128)(2,1)S(1)}, u32[]{:S(2)}, u32[]{:S(2)}) collective-permute-start(bf16[768,256]{1,0:T(8,128)(2,1)S(1)} %collective-permute-done.3.near_ref), channel_id=1, source_target_pairs={{0,8},{4,28},{8,16},{12,4},{16,24},{20,12},{24,0},{28,20},{1,9},{5... | collective-permute-start | bytes 1179656 | tf_op jit(solution)/shard_map/ppermute | solution.py:334
  50.7 15.3 %collective-permute-start.12 = (bf16[768,256]{1,0:T(8,128)(2,1)S(1)}, bf16[768,256]{1,0:T(8,128)(2,1)S(1)}, u32[]{:S(2)}, u32[]{:S(2)}) collective-permute-start(bf16[768,256]{1,0:T(8,128)(2,1)S(1)} %get-tuple-element.310.field_ref), channel_id=1, source_target_pairs={{0,4},{4,0},{8,12},{12,8},{16,20},{20,16},{24,28},{28,24},{1,5},{5... | collective-permute-start | bytes 1179656 | tf_op jit(solution)/shard_map/ppermute | solution.py:376
  57.6 13.0 %collective-permute-start.15 = (bf16[768,256]{1,0:T(8,128)(2,1)S(1)}, bf16[768,256]{1,0:T(8,128)(2,1)S(1)}, u32[]{:S(2)}, u32[]{:S(2)}) collective-permute-start(bf16[768,256]{1,0:T(8,128)(2,1)S(1)} %collective-permute-done.9.near_ref), channel_id=1, source_target_pairs={{0,8},{4,28},{8,16},{12,4},{16,24},{20,12},{24,0},{28,20},{1,9},{5... | collective-permute-start | bytes 1179656 | tf_op jit(solution)/shard_map/ppermute | solution.py:334
  59.2 15.3 %collective-permute-start.14 = (bf16[768,256]{1,0:T(8,128)(2,1)S(1)}, bf16[768,256]{1,0:T(8,128)(2,1)S(1)}, u32[]{:S(2)}, u32[]{:S(2)}) collective-permute-start(bf16[768,256]{1,0:T(8,128)(2,1)S(1)} %get-tuple-element.313.field_ref), channel_id=1, source_target_pairs={{0,4},{4,0},{8,12},{12,8},{16,20},{20,16},{24,28},{28,24},{1,5},{5... | collective-permute-start | bytes 1179656 | tf_op jit(solution)/shard_map/ppermute | solution.py:376
  66.0 13.0 %collective-permute-start.13 = (bf16[768,256]{1,0:T(8,128)(2,1)S(1)}, bf16[768,256]{1,0:T(8,128)(2,1)S(1)}, u32[]{:S(2)}, u32[]{:S(2)}) collective-permute-start(bf16[768,256]{1,0:T(8,128)(2,1)S(1)} %collective-permute-done.12.near_ref), channel_id=1, source_target_pairs={{0,8},{4,28},{8,16},{12,4},{16,24},{20,12},{24,0},{28,20},{1,9},{5... | collective-permute-start | bytes 1179656 | tf_op jit(solution)/shard_map/ppermute | solution.py:334
  67.6 15.3 %collective-permute-start.11 = (bf16[768,256]{1,0:T(8,128)(2,1)S(1)}, bf16[768,256]{1,0:T(8,128)(2,1)S(1)}, u32[]{:S(2)}, u32[]{:S(2)}) collective-permute-start(bf16[768,256]{1,0:T(8,128)(2,1)S(1)} %product_1.4.field_ref), channel_id=1, source_target_pairs={{0,4},{4,0},{8,12},{12,8},{16,20},{20,16},{24,28},{28,24},{1,5},{5... | collective-permute-start | bytes 1179656 | tf_op jit(solution)/shard_map/ppermute | solution.py:376
  74.4 13.0 %collective-permute-start.18 = (bf16[768,256]{1,0:T(8,128)(2,1)S(1)}, bf16[768,256]{1,0:T(8,128)(2,1)S(1)}, u32[]{:S(2)}, u32[]{:S(2)}) collective-permute-start(bf16[768,256]{1,0:T(8,128)(2,1)S(1)} %collective-permute-done.14.near_ref), channel_id=1, source_target_pairs={{0,8},{4,28},{8,16},{12,4},{16,24},{20,12},{24,0},{28,20},{1,9},{5... | collective-permute-start | bytes 1179656 | tf_op jit(solution)/shard_map/ppermute | solution.py:334
  76.0 15.3 %collective-permute-start.17 = (bf16[768,256]{1,0:T(8,128)(2,1)S(1)}, bf16[768,256]{1,0:T(8,128)(2,1)S(1)}, u32[]{:S(2)}, u32[]{:S(2)}) collective-permute-start(bf16[768,256]{1,0:T(8,128)(2,1)S(1)} %product_1.5.field_ref), channel_id=1, source_target_pairs={{0,4},{4,0},{8,12},{12,8},{16,20},{20,16},{24,28},{28,24},{1,5},{5... | collective-permute-start | bytes 1179656 | tf_op jit(solution)/shard_map/ppermute | solution.py:376
  82.9 13.0 %collective-permute-start.16 = (bf16[768,256]{1,0:T(8,128)(2,1)S(1)}, bf16[768,256]{1,0:T(8,128)(2,1)S(1)}, u32[]{:S(2)}, u32[]{:S(2)}) collective-permute-start(bf16[768,256]{1,0:T(8,128)(2,1)S(1)} %collective-permute-done.11.near_ref), channel_id=1, source_target_pairs={{0,8},{4,28},{8,16},{12,4},{16,24},{20,12},{24,0},{28,20},{1,9},{5... | collective-permute-start | bytes 1179656 | tf_op jit(solution)/shard_map/ppermute | solution.py:334
  84.4 15.3 %collective-permute-start.20 = (bf16[768,256]{1,0:T(8,128)(2,1)S(1)}, bf16[768,256]{1,0:T(8,128)(2,1)S(1)}, u32[]{:S(2)}, u32[]{:S(2)}) collective-permute-start(bf16[768,256]{1,0:T(8,128)(2,1)S(1)} %product_1.6.field_ref), channel_id=1, source_target_pairs={{0,4},{4,0},{8,12},{12,8},{16,20},{20,16},{24,28},{28,24},{1,5},{5... | collective-permute-start | bytes 1179656 | tf_op jit(solution)/shard_map/ppermute | solution.py:376
  91.3 11.5 %collective-permute-start.19 = (bf16[768,256]{1,0:T(8,128)(2,1)S(1)}, bf16[768,256]{1,0:T(8,128)(2,1)S(1)}, u32[]{:S(2)}, u32[]{:S(2)}) collective-permute-start(bf16[768,256]{1,0:T(8,128)(2,1)S(1)} %collective-permute-done.17.near_ref), channel_id=1, source_target_pairs={{0,8},{4,28},{8,16},{12,4},{16,24},{20,12},{24,0},{28,20},{1,9},{5... | collective-permute-start | bytes 1179656 | tf_op jit(solution)/shard_map/ppermute | solution.py:334
  92.9 13.8 %collective-permute-start.22 = (bf16[768,256]{1,0:T(8,128)(2,1)S(1)}, bf16[768,256]{1,0:T(8,128)(2,1)S(1)}, u32[]{:S(2)}, u32[]{:S(2)}) collective-permute-start(bf16[768,256]{1,0:T(8,128)(2,1)S(1)} %product_1.7.field_ref), channel_id=1, source_target_pairs={{0,4},{4,0},{8,12},{12,8},{16,20},{20,16},{24,28},{28,24},{1,5},{5... | collective-permute-start | bytes 1179656 | tf_op jit(solution)/shard_map/ppermute | solution.py:376
  99.7 10.4 %collective-permute-start.21 = (bf16[768,256]{1,0:T(8,128)(2,1)S(1)}, bf16[768,256]{1,0:T(8,128)(2,1)S(1)}, u32[]{:S(2)}, u32[]{:S(2)}) collective-permute-start(bf16[768,256]{1,0:T(8,128)(2,1)S(1)} %collective-permute-done.20.near_ref), channel_id=1, source_target_pairs={{0,8},{4,28},{8,16},{12,4},{16,24},{20,12},{24,0},{28,20},{1,9},{5... | collective-permute-start | bytes 1179656 | tf_op jit(solution)/shard_map/ppermute | solution.py:334
  101.3 11.9 %collective-permute-start.24 = (bf16[768,256]{1,0:T(8,128)(2,1)S(1)}, bf16[768,256]{1,0:T(8,128)(2,1)S(1)}, u32[]{:S(2)}, u32[]{:S(2)}) collective-permute-start(bf16[768,256]{1,0:T(8,128)(2,1)S(1)} %get-tuple-element.336.refs_0_.refs_1_.refs_10_), channel_id=1, source_target_pairs={{0,1},{1,0},{2,3},{3,2},{4,5},{5,4},{6,7},{7,6},{8,9},{9,8},{10,11... | collective-permute-start | bytes 1179656 | tf_op jit(solution)/shard_map/ppermute | solution.py:304
  101.3 11.9 %collective-permute-start.25 = (bf16[768,256]{1,0:T(8,128)(2,1)S(1)}, bf16[768,256]{1,0:T(8,128)(2,1)S(1)}, u32[]{:S(2)}, u32[]{:S(2)}) collective-permute-start(bf16[768,256]{1,0:T(8,128)(2,1)S(1)} %get-tuple-element.336.refs_0_.refs_1_.refs_10_), channel_id=1, source_target_pairs={{0,2},{1,3},{2,0},{3,1},{4,6},{5,7},{6,4},{7,5},{8,10},{9,11},{10,... | collective-permute-start | bytes 1179656 | tf_op jit(solution)/shard_map/ppermute | solution.py:304
  106.7 11.7 %collective-permute-start.23 = (bf16[768,256]{1,0:T(8,128)(2,1)S(1)}, bf16[768,256]{1,0:T(8,128)(2,1)S(1)}, u32[]{:S(2)}, u32[]{:S(2)}) collective-permute-start(bf16[768,256]{1,0:T(8,128)(2,1)S(1)} %collective-permute-done.22.near_ref), channel_id=1, source_target_pairs={{0,8},{4,28},{8,16},{12,4},{16,24},{20,12},{24,0},{28,20},{1,9},{5... | collective-permute-start | bytes 1179656 | tf_op jit(solution)/shard_map/ppermute | solution.py:334
  108.3 16.7 %collective-permute-start.27 = (bf16[768,256]{1,0:T(8,128)(2,1)S(1)}, bf16[768,256]{1,0:T(8,128)(2,1)S(1)}, u32[]{:S(2)}, u32[]{:S(2)}) collective-permute-start(bf16[768,256]{1,0:T(8,128)(2,1)S(1)} %get-tuple-element.347.refs_1_.refs_2_.refs_11_), channel_id=1, source_target_pairs={{0,2},{1,3},{2,0},{3,1},{4,6},{5,7},{6,4},{7,5},{8,10},{9,11},{10,... | collective-permute-start | bytes 1179656 | tf_op jit(solution)/shard_map/ppermute | solution.py:304
  110.1 14.8 %collective-permute-start.30 = (bf16[768,256]{1,0:T(8,128)(2,1)S(1)}, bf16[768,256]{1,0:T(8,128)(2,1)S(1)}, u32[]{:S(2)}, u32[]{:S(2)}) collective-permute-start(bf16[768,256]{1,0:T(8,128)(2,1)S(1)} %get-tuple-element.347.refs_1_.refs_2_.refs_11_), channel_id=1, source_target_pairs={{0,1},{1,0},{2,3},{3,2},{4,5},{5,4},{6,7},{7,6},{8,9},{9,8},{10,11... | collective-permute-start | bytes 1179656 | tf_op jit(solution)/shard_map/ppermute | solution.py:304
  122.0 21.1 %collective-permute-start.35 = (bf16[384,1024]{1,0:T(8,128)(2,1)S(1)}, bf16[384,1024]{1,0:T(8,128)(2,1)S(1)}, u32[]{:S(2)}, u32[]{:S(2)}) collective-permute-start(bf16[384,1024]{1,0:T(8,128)(2,1)S(1)} %get-tuple-element.388), channel_id=1, source_target_pairs={{0,4},{4,0},{8,12},{12,8},{16,20},{20,16},{24,28},{28,24},{1,5},{5... | collective-permute-start | bytes 2359304 | tf_op jit(solution)/shard_map/ppermute | solution.py:400
  122.9 17.5 %collective-permute-start.32 = (bf16[784,256]{1,0:T(8,128)(2,1)S(1)}, bf16[784,256]{1,0:T(8,128)(2,1)S(1)}, u32[]{:S(2)}, u32[]{:S(2)}) collective-permute-start(bf16[784,256]{1,0:T(8,128)(2,1)S(1)} %product_2.7.refs_3_.refs_4_.refs_13_), channel_id=1, source_target_pairs={{0,2},{1,3},{2,0},{3,1},{4,6},{5,7},{6,4},{7,5},{8,10},{9,11},{10,... | collective-permute-start | bytes 1204232 | tf_op jit(solution)/shard_map/ppermute | solution.py:304
  124.4 16.0 %collective-permute-start.29 = (bf16[768,256]{1,0:T(8,128)(2,1)S(1)}, bf16[768,256]{1,0:T(8,128)(2,1)S(1)}, u32[]{:S(2)}, u32[]{:S(2)}) collective-permute-start(bf16[768,256]{1,0:T(8,128)(2,1)S(1)} %get-tuple-element.358.refs_2_.refs_3_.refs_12_), channel_id=1, source_target_pairs={{0,2},{1,3},{2,0},{3,1},{4,6},{5,7},{6,4},{7,5},{8,10},{9,11},{10,... | collective-permute-start | bytes 1179656 | tf_op jit(solution)/shard_map/ppermute | solution.py:304
  124.9 15.5 %collective-permute-start.33 = (bf16[768,256]{1,0:T(8,128)(2,1)S(1)}, bf16[768,256]{1,0:T(8,128)(2,1)S(1)}, u32[]{:S(2)}, u32[]{:S(2)}) collective-permute-start(bf16[768,256]{1,0:T(8,128)(2,1)S(1)} %get-tuple-element.358.refs_2_.refs_3_.refs_12_), channel_id=1, source_target_pairs={{0,1},{1,0},{2,3},{3,2},{4,5},{5,4},{6,7},{7,6},{8,9},{9,8},{10,11... | collective-permute-start | bytes 1179656 | tf_op jit(solution)/shard_map/ppermute | solution.py:304
  124.9 16.1 %collective-permute-start.36 = (bf16[784,256]{1,0:T(8,128)(2,1)S(1)}, bf16[784,256]{1,0:T(8,128)(2,1)S(1)}, u32[]{:S(2)}, u32[]{:S(2)}) collective-permute-start(bf16[784,256]{1,0:T(8,128)(2,1)S(1)} %product_2.7.refs_3_.refs_4_.refs_13_), channel_id=1, source_target_pairs={{0,1},{1,0},{2,3},{3,2},{4,5},{5,4},{6,7},{7,6},{8,9},{9,8},{10,11... | collective-permute-start | bytes 1204232 | tf_op jit(solution)/shard_map/ppermute | solution.py:304
  140.4 3.9 %collective-permute-start.34 = (bf16[784,256]{1,0:T(8,128)(2,1)S(1)}, bf16[784,256]{1,0:T(8,128)(2,1)S(1)}, u32[]{:S(2)}, u32[]{:S(2)}) collective-permute-start(bf16[784,256]{1,0:T(8,128)(2,1)S(1)} %collective-permute-done.32.refs_7_.refs_9_.refs_4_), channel_id=1, source_target_pairs={{0,1},{1,0},{2,3},{3,2},{4,5},{5,4},{6,7},{7,6},{8,9},{9,8},{10,11... | collective-permute-start | bytes 1204232 | tf_op jit(solution)/shard_map/ppermute | solution.py:304
  140.4 3.8 %collective-permute-start.26 = (bf16[768,256]{1,0:T(8,128)(2,1)S(1)}, bf16[768,256]{1,0:T(8,128)(2,1)S(1)}, u32[]{:S(2)}, u32[]{:S(2)}) collective-permute-start(bf16[768,256]{1,0:T(8,128)(2,1)S(1)} %collective-permute-done.25.refs_4_.refs_1_), channel_id=1, source_target_pairs={{0,1},{1,0},{2,3},{3,2},{4,5},{5,4},{6,7},{7,6},{8,9},{9,8},{10,11... | collective-permute-start | bytes 1179656 | tf_op jit(solution)/shard_map/ppermute | solution.py:304
  143.1 22.3 %collective-permute-start.39 = (bf16[256,1024]{1,0:T(8,128)(2,1)S(1)}, bf16[256,1024]{1,0:T(8,128)(2,1)S(1)}, u32[]{:S(2)}, u32[]{:S(2)}) collective-permute-start(bf16[256,1024]{1,0:T(8,128)(2,1)S(1)} %get-tuple-element.419), channel_id=1, source_target_pairs={{0,8},{4,12},{8,0},{12,4},{16,24},{20,28},{24,16},{28,20},{1,9},{5... | collective-permute-start | bytes 1572872 | tf_op jit(solution)/shard_map/ppermute | solution.py:400
  146.1 23.3 %collective-permute-start.37 = (bf16[272,1024]{1,0:T(8,128)(2,1)S(1)}, bf16[272,1024]{1,0:T(8,128)(2,1)S(1)}, u32[]{:S(2)}, u32[]{:S(2)}) collective-permute-start(bf16[272,1024]{1,0:T(8,128)(2,1)S(1)} %get-tuple-element.416), channel_id=1, source_target_pairs={{0,4},{4,0},{8,12},{12,8},{16,20},{20,16},{24,28},{28,24},{1,5},{5... | collective-permute-start | bytes 1671176 | tf_op jit(solution)/shard_map/ppermute | solution.py:400
  146.7 21.5 %collective-permute-start.38 = (bf16[192,1024]{1,0:T(8,128)(2,1)S(1)}, bf16[192,1024]{1,0:T(8,128)(2,1)S(1)}, u32[]{:S(2)}, u32[]{:S(2)}) collective-permute-start(bf16[192,1024]{1,0:T(8,128)(2,1)S(1)} %sum_hop.8), channel_id=1, source_target_pairs={{0,16},{4,20},{8,24},{12,28},{16,0},{20,4},{24,8},{28,12},{1,17},{... | collective-permute-start | bytes 1179656 | tf_op jit(solution)/shard_map/ppermute | solution.py:400
  152.6 24.0 %collective-permute-start.41 = (bf16[256,1024]{1,0:T(8,128)(2,1)S(1)}, bf16[256,1024]{1,0:T(8,128)(2,1)S(1)}, u32[]{:S(2)}, u32[]{:S(2)}) collective-permute-start(bf16[256,1024]{1,0:T(8,128)(2,1)S(1)} %get-tuple-element.443), channel_id=1, source_target_pairs={{0,4},{4,0},{8,12},{12,8},{16,20},{20,16},{24,28},{28,24},{1,5},{5... | collective-permute-start | bytes 1572872 | tf_op jit(solution)/shard_map/ppermute | solution.py:400
  168.8 7.8 %collective-permute-start.42 = (bf16[96,1024]{1,0:T(8,128)(2,1)S(1)}, bf16[96,1024]{1,0:T(8,128)(2,1)S(1)}, u32[]{:S(2)}, u32[]{:S(2)}) collective-permute-start(bf16[96,1024]{1,0:T(8,128)(2,1)S(1)} %sum_hop.10), channel_id=1, source_target_pairs={{0,8},{4,12},{8,0},{12,4},{16,24},{20,28},{24,16},{28,20},{1,9},{5... | collective-permute-start | bytes 589832 | tf_op jit(solution)/shard_map/ppermute | solution.py:400
  170.1 14.6 %collective-permute-start.40 = (bf16[144,1024]{1,0:T(8,128)(2,1)S(1)}, bf16[144,1024]{1,0:T(8,128)(2,1)S(1)}, u32[]{:S(2)}, u32[]{:S(2)}) collective-permute-start(bf16[144,1024]{1,0:T(8,128)(2,1)S(1)} %sum_hop.11), channel_id=1, source_target_pairs={{0,8},{4,12},{8,0},{12,4},{16,24},{20,28},{24,16},{28,20},{1,9},{5... | collective-permute-start | bytes 884744 | tf_op jit(solution)/shard_map/ppermute | solution.py:400
  171.7 13.8 %collective-permute-start.45 = (bf16[128,1024]{1,0:T(8,128)(2,1)S(1)}, bf16[128,1024]{1,0:T(8,128)(2,1)S(1)}, u32[]{:S(2)}, u32[]{:S(2)}) collective-permute-start(bf16[128,1024]{1,0:T(8,128)(2,1)S(1)} %sum_hop.9), channel_id=1, source_target_pairs={{0,4},{4,0},{8,12},{12,8},{16,20},{20,16},{24,28},{28,24},{1,5},{5... | collective-permute-start | bytes 786440 | tf_op jit(solution)/shard_map/ppermute | solution.py:400
  177.3 10.5 %collective-permute-start.44 = (bf16[128,1024]{1,0:T(8,128)(2,1)S(1)}, bf16[128,1024]{1,0:T(8,128)(2,1)S(1)}, u32[]{:S(2)}, u32[]{:S(2)}) collective-permute-start(bf16[128,1024]{1,0:T(8,128)(2,1)S(1)} %sum_hop.12), channel_id=1, source_target_pairs={{0,8},{4,12},{8,0},{12,4},{16,24},{20,28},{24,16},{28,20},{1,9},{5... | collective-permute-start | bytes 786440 | tf_op jit(solution)/shard_map/ppermute | solution.py:400
  185.4 12.9 %collective-permute-start.43 = (bf16[80,1024]{1,0:T(8,128)(2,1)S(1)}, bf16[80,1024]{1,0:T(8,128)(2,1)S(1)}, u32[]{:S(2)}, u32[]{:S(2)}) collective-permute-start(bf16[80,1024]{1,0:T(8,128)(2,1)S(1)} %sum_hop.13), channel_id=1, source_target_pairs={{0,16},{4,20},{8,24},{12,28},{16,0},{20,4},{24,8},{28,12},{1,17},{... | collective-permute-start | bytes 491528 | tf_op jit(solution)/shard_map/ppermute | solution.py:400
  188.4 9.9 %collective-permute-start.46 = (bf16[64,1024]{1,0:T(8,128)(2,1)S(1)}, bf16[64,1024]{1,0:T(8,128)(2,1)S(1)}, u32[]{:S(2)}, u32[]{:S(2)}) collective-permute-start(bf16[64,1024]{1,0:T(8,128)(2,1)S(1)} %sum_hop.15), channel_id=1, source_target_pairs={{0,16},{4,20},{8,24},{12,28},{16,0},{20,4},{24,8},{28,12},{1,17},{... | collective-permute-start | bytes 393224 | tf_op jit(solution)/shard_map/ppermute | solution.py:400
  199.6 9.1 %collective-permute-start.48 = (bf16[64,1024]{1,0:T(8,128)(2,1)S(1)}, bf16[64,1024]{1,0:T(8,128)(2,1)S(1)}, u32[]{:S(2)}, u32[]{:S(2)}) collective-permute-start(bf16[64,1024]{1,0:T(8,128)(2,1)S(1)} %sum_last.7.upper_ref), channel_id=1, source_target_pairs={{0,16},{4,20},{8,24},{12,28},{16,0},{20,4},{24,8},{28,12},{1,17},{... | collective-permute-start | bytes 393224 | tf_op jit(solution)/shard_map/ppermute | solution.py:400
  200.4 14.9 %collective-permute-start.50 = (bf16[96,1024]{1,0:T(8,128)(2,1)S(1)}, bf16[96,1024]{1,0:T(8,128)(2,1)S(1)}, u32[]{:S(2)}, u32[]{:S(2)}) collective-permute-start(bf16[96,1024]{1,0:T(8,128)(2,1)S(1)} %sum_last.5.upper_ref), channel_id=1, source_target_pairs={{0,8},{4,12},{8,0},{12,4},{16,24},{20,28},{24,16},{28,20},{1,9},{5... | collective-permute-start | bytes 589832 | tf_op jit(solution)/shard_map/ppermute | solution.py:400
  203.0 8.2 %collective-permute-start.47 = (bf16[64,1024]{1,0:T(8,128)(2,1)S(1)}, bf16[64,1024]{1,0:T(8,128)(2,1)S(1)}, u32[]{:S(2)}, u32[]{:S(2)}) collective-permute-start(bf16[64,1024]{1,0:T(8,128)(2,1)S(1)} %sum_hop.14), channel_id=1, source_target_pairs={{0,16},{4,20},{8,24},{12,28},{16,0},{20,4},{24,8},{28,12},{1,17},{... | collective-permute-start | bytes 393224 | tf_op jit(solution)/shard_map/ppermute | solution.py:400
  208.7 27.3 %collective-permute-start.53 = (bf16[128,1024]{1,0:T(8,128)(2,1)S(1)}, bf16[128,1024]{1,0:T(8,128)(2,1)S(1)}, u32[]{:S(2)}, u32[]{:S(2)}) collective-permute-start(bf16[128,1024]{1,0:T(8,128)(2,1)S(1)} %join.12.upper_ref), channel_id=1, source_target_pairs={{0,8},{4,12},{8,0},{12,4},{16,24},{20,28},{24,16},{28,20},{1,9},{5... | collective-permute-start | bytes 786440 | tf_op jit(solution)/shard_map/ppermute | solution.py:400
  211.8 21.2 %collective-permute-start.52 = (bf16[64,1024]{1,0:T(8,128)(2,1)S(1)}, bf16[64,1024]{1,0:T(8,128)(2,1)S(1)}, u32[]{:S(2)}, u32[]{:S(2)}) collective-permute-start(bf16[64,1024]{1,0:T(8,128)(2,1)S(1)} %sum_last.6.upper_ref), channel_id=1, source_target_pairs={{0,16},{4,20},{8,24},{12,28},{16,0},{20,4},{24,8},{28,12},{1,17},{... | collective-permute-start | bytes 393224 | tf_op jit(solution)/shard_map/ppermute | solution.py:400
  215.2 20.6 %collective-permute-start.49 = (bf16[64,1024]{1,0:T(8,128)(2,1)S(1)}, bf16[64,1024]{1,0:T(8,128)(2,1)S(1)}, u32[]{:S(2)}, u32[]{:S(2)}) collective-permute-start(bf16[64,1024]{1,0:T(8,128)(2,1)S(1)} %get-tuple-element.481.upper_ref), channel_id=1, source_target_pairs={{0,16},{4,20},{8,24},{12,28},{16,0},{20,4},{24,8},{28,12},{1,17},{... | collective-permute-start | bytes 393224 | tf_op jit(solution)/shard_map/ppermute | solution.py:400
  215.4 33.7 %collective-permute-start.63 = (bf16[192,1024]{1,0:T(8,128)(2,1)S(1)}, bf16[192,1024]{1,0:T(8,128)(2,1)S(1)}, u32[]{:S(2)}, u32[]{:S(2)}) collective-permute-start(bf16[192,1024]{1,0:T(8,128)(2,1)S(1)} %join.8.upper_ref), channel_id=1, source_target_pairs={{0,16},{4,20},{8,24},{12,28},{16,0},{20,4},{24,8},{28,12},{1,17},{... | collective-permute-start | bytes 1179656 | tf_op jit(solution)/shard_map/ppermute | solution.py:400
  233.0 9.3 %collective-permute-start.56 = (bf16[128,1024]{1,0:T(8,128)(2,1)S(1)}, bf16[128,1024]{1,0:T(8,128)(2,1)S(1)}, u32[]{:S(2)}, u32[]{:S(2)}) collective-permute-start(bf16[128,1024]{1,0:T(8,128)(2,1)S(1)} %join.10.upper_ref), channel_id=1, source_target_pairs={{0,4},{4,0},{8,12},{12,8},{16,20},{20,16},{24,28},{28,24},{1,5},{5... | collective-permute-start | bytes 786440 | tf_op jit(solution)/shard_map/ppermute | solution.py:400
  235.9 12.0 %collective-permute-start.51 = (bf16[128,1024]{1,0:T(8,128)(2,1)S(1)}, bf16[128,1024]{1,0:T(8,128)(2,1)S(1)}, u32[]{:S(2)}, u32[]{:S(2)}) collective-permute-start(bf16[128,1024]{1,0:T(8,128)(2,1)S(1)} %join.9.upper_ref), channel_id=1, source_target_pairs={{0,8},{4,12},{8,0},{12,4},{16,24},{20,28},{24,16},{28,20},{1,9},{5... | collective-permute-start | bytes 786440 | tf_op jit(solution)/shard_map/ppermute | solution.py:400
  236.0 13.1 %collective-permute-start.58 = (bf16[256,1024]{1,0:T(8,128)(2,1)S(1)}, bf16[256,1024]{1,0:T(8,128)(2,1)S(1)}, u32[]{:S(2)}, u32[]{:S(2)}) collective-permute-start(bf16[256,1024]{1,0:T(8,128)(2,1)S(1)} %join.14.refs_4_), channel_id=1, source_target_pairs={{0,4},{4,0},{8,12},{12,8},{16,20},{20,16},{24,28},{28,24},{1,5},{5... | collective-permute-start | bytes 1572872 | tf_op jit(solution)/shard_map/ppermute | solution.py:400
  237.1 13.0 %collective-permute-start.59 = (bf16[256,1024]{1,0:T(8,128)(2,1)S(1)}, bf16[256,1024]{1,0:T(8,128)(2,1)S(1)}, u32[]{:S(2)}, u32[]{:S(2)}) collective-permute-start(bf16[256,1024]{1,0:T(8,128)(2,1)S(1)} %join.14.refs_4_), channel_id=1, source_target_pairs={{0,1},{1,0},{2,3},{3,2},{4,5},{5,4},{6,7},{7,6},{8,9},{9,8},{10,11... | collective-permute-start | bytes 1572872 | tf_op jit(solution)/shard_map/ppermute | solution.py:304
  242.3 9.2 %collective-permute-start.61 = (bf16[256,1024]{1,0:T(8,128)(2,1)S(1)}, bf16[256,1024]{1,0:T(8,128)(2,1)S(1)}, u32[]{:S(2)}, u32[]{:S(2)}) collective-permute-start(bf16[256,1024]{1,0:T(8,128)(2,1)S(1)} %join.13.refs_5_), channel_id=1, source_target_pairs={{0,2},{1,3},{2,0},{3,1},{4,6},{5,7},{6,4},{7,5},{8,10},{9,11},{10,... | collective-permute-start | bytes 1572872 | tf_op jit(solution)/shard_map/ppermute | solution.py:304
  247.9 14.8 %collective-permute-start.54 = (bf16[256,1024]{1,0:T(8,128)(2,1)S(1)}, bf16[256,1024]{1,0:T(8,128)(2,1)S(1)}, u32[]{:S(2)}, u32[]{:S(2)}) collective-permute-start(bf16[256,1024]{1,0:T(8,128)(2,1)S(1)} %join.11.refs_6_), channel_id=1, source_target_pairs={{0,4},{4,0},{8,12},{12,8},{16,20},{20,16},{24,28},{28,24},{1,5},{5... | collective-permute-start | bytes 1572872 | tf_op jit(solution)/shard_map/ppermute | solution.py:400
  249.1 13.7 %collective-permute-start.57 = (bf16[256,1024]{1,0:T(8,128)(2,1)S(1)}, bf16[256,1024]{1,0:T(8,128)(2,1)S(1)}, u32[]{:S(2)}, u32[]{:S(2)}) collective-permute-start(bf16[256,1024]{1,0:T(8,128)(2,1)S(1)} %join.13.refs_5_), channel_id=1, source_target_pairs={{0,8},{4,12},{8,0},{12,4},{16,24},{20,28},{24,16},{28,20},{1,9},{5... | collective-permute-start | bytes 1572872 | tf_op jit(solution)/shard_map/ppermute | solution.py:400
  249.1 29.6 %collective-permute-start.64 = (bf16[384,1024]{1,0:T(8,128)(2,1)S(1)}, bf16[384,1024]{1,0:T(8,128)(2,1)S(1)}, u32[]{:S(2)}, u32[]{:S(2)}) collective-permute-start(bf16[384,1024]{1,0:T(8,128)(2,1)S(1)} %join.15.refs_5_), channel_id=1, source_target_pairs={{0,4},{4,0},{8,12},{12,8},{16,20},{20,16},{24,28},{28,24},{1,5},{5... | collective-permute-start | bytes 2359304 | tf_op jit(solution)/shard_map/ppermute | solution.py:400
  250.2 14.2 %collective-permute-start.55 = (bf16[256,1024]{1,0:T(8,128)(2,1)S(1)}, bf16[256,1024]{1,0:T(8,128)(2,1)S(1)}, u32[]{:S(2)}, u32[]{:S(2)}) collective-permute-start(bf16[256,1024]{1,0:T(8,128)(2,1)S(1)} %join.11.refs_6_), channel_id=1, source_target_pairs={{0,3},{1,2},{2,1},{3,0},{4,7},{5,6},{6,5},{7,4},{8,11},{9,10},{10,... | collective-permute-start | bytes 1572872 | tf_op jit(solution)/shard_map/ppermute | solution.py:304
  251.6 12.8 %collective-permute-start.60 = (bf16[256,1024]{1,0:T(8,128)(2,1)S(1)}, bf16[256,1024]{1,0:T(8,128)(2,1)S(1)}, u32[]{:S(2)}, u32[]{:S(2)}) collective-permute-start(bf16[256,1024]{1,0:T(8,128)(2,1)S(1)} %collective-permute-done.58.refs_5_), channel_id=1, source_target_pairs={{0,1},{1,0},{2,3},{3,2},{4,5},{5,4},{6,7},{7,6},{8,9},{9,8},{10,11... | collective-permute-start | bytes 1572872 | tf_op jit(solution)/shard_map/ppermute | solution.py:304
  262.8 18.5 %collective-permute-start.62 = (bf16[256,1024]{1,0:T(8,128)(2,1)S(1)}, bf16[256,1024]{1,0:T(8,128)(2,1)S(1)}, u32[]{:S(2)}, u32[]{:S(2)}) collective-permute-start(bf16[256,1024]{1,0:T(8,128)(2,1)S(1)} %collective-permute-done.61.refs_7_), channel_id=1, source_target_pairs={{0,8},{4,12},{8,0},{12,4},{16,24},{20,28},{24,16},{28,20},{1,9},{5... | collective-permute-start | bytes 1572872 | tf_op jit(solution)/shard_map/ppermute | solution.py:400
  262.8 24.0 %collective-permute-start.65 = (bf16[256,1024]{1,0:T(8,128)(2,1)S(1)}, bf16[256,1024]{1,0:T(8,128)(2,1)S(1)}, u32[]{:S(2)}, u32[]{:S(2)}) collective-permute-start(bf16[256,1024]{1,0:T(8,128)(2,1)S(1)} %collective-permute-done.54.refs_7_), channel_id=1, source_target_pairs={{0,3},{1,2},{2,1},{3,0},{4,7},{5,6},{6,5},{7,4},{8,11},{9,10},{10,... | collective-permute-start | bytes 1572872 | tf_op jit(solution)/shard_map/ppermute | solution.py:304
  (3 other events, 12.9 us)

commit v15 on v13

--- a/solution.py
+++ b/solution.py
@@ -527,7 +527,7 @@
         if not last:
             mixed = order(mixed)
 
-    y_first, z_then_y, y_then_far = (1, *z_masks), (*z_masks[:1], 1, *z_masks[1:]), (1, *z_masks[::-1])
+    y_first, z_then_y = (1, *z_masks), (*z_masks[:1], 1, *z_masks[1:])
     there[1] = 25.0
     queue = sorted(range(1, groups), key=lambda d: (d == 1, d))
     turn = {d: place for place, d in enumerate([queue[-1], *queue[:-2], 0, *queue[-2:-1]])}
@@ -537,7 +537,7 @@
         first = d == queue[0] and d != carrier
         behind = carrier if d == 1 and d != carrier else None
         processes.append(process(d, z_then_y if first else y_first, EXTRA if d == carrier else 0, first, behind))
-    processes.append(process(0, y_then_far, behind=1))
+    processes.append(process(0, y_first, behind=1))
     clock.run(processes)
     return mixed
 

time: 282 us -> 292 us (1.035)
  waiting for transfers between devices: 138 us -> 156 us
  starting transfers between devices: 91.1 us -> 83.3 us
    ppermute x25, waiting for transfers between devices: 86.1 us -> 110 us  [over_tiles(): sent = lax.ppermute(value, 'elem', [(i, i ^ mask) for i in range(tiles)])]
    ppermute x25, starting transfers between devices: 27.2 us -> 21 us  [over_tiles(): sent = lax.ppermute(value, 'elem', [(i, i ^ mask) for i in range(tiles)])]
    ppermute x17, waiting for transfers between devices: 14.3 us -> 8.35 us  [to_group(): return lax.ppermute(value, 'orb', [(i, i ^ d) for i in range(groups)])]
  transfers between devices with their start and end apart: 66 -> 66, of which waited for: 35 -> 32; matrix products, arithmetic and copies ran while one was open for 3% -> 3% of each run, Pallas kernels for 13% -> 12%
where the time goes in v15:
time: 292 us; the launch traced here: 291 us
  waiting for transfers between devices  156 us (53%)
  starting transfers between devices  83.3 us (29%)
  Pallas kernels  42.7 us (15%)
  local copies, waits for them, and re-layouts  6.78 us (2%)
    ppermute x25, waiting for transfers between devices, over_tiles(): sent = lax.ppermute(value, 'elem', [(i, i ^ mask) for i in range(tiles)])  110 us
    pallas_call x40, Pallas kernels, call(): pl.pallas_call(kernel, out_shape=outs, in_specs=[pl.BlockSpec(memory_spac...  42.7 us
    ppermute x8, starting transfers between devices, multiply(): near[stage + 1, c] = lax.ppermute(out, 'elem', swap)  23.7 us
    ppermute x25, starting transfers between devices, over_tiles(): sent = lax.ppermute(value, 'elem', [(i, i ^ mask) for i in range(tiles)])  21 us
    ppermute x8, waiting for transfers between devices, multiply(): near[stage + 1, c] = lax.ppermute(out, 'elem', swap)  20.8 us
    ppermute x12, starting transfers between devices, send_on(): far[job] = lax.ppermute(near[job], 'elem', outward)  18.9 us
    ppermute x3, waiting for transfers between devices, local(): near[0, c] = lax.ppermute(start[c], 'elem', swap)  9.1 us
    ppermute x17, starting transfers between devices, to_group(): return lax.ppermute(value, 'orb', [(i, i ^ d) for i in range(groups)])  9.08 us
  transfers between devices with their start and end apart: 66, of which 32 were waited for; matrix products, arithmetic and copies ran while one was open for 3% of the time, Pallas kernels for 12%

profile of v15, /device:TPU:0, one launch (start us, length us, event | category | flops | bytes accessed | tf_op | source)
XLA Modules:
  0.0 291.5 jit_solution(4812731460626750376)
XLA Ops:
  1.5 3.0 %collective-permute-start = (bf16[768,256]{1,0:T(8,128)(2,1)S(1)}, bf16[768,256]{1,0:T(8,128)(2,1)S(1)}, u32[]{:S(2)}, u32[]{:S(2)}) collective-permute-start(bf16[768,256]{1,0:T(8,128)(2,1)S(1)} %get-tuple-element.514.field_ref.refs_0_), channel_id=1, source_target_pairs={{0,4},{4,0},{8,12},{12,8},{16,20},{20,16},{24,28},{28,24},{1,5},{5... | collective-permute-start | bytes 1179656 | tf_op jit(solution)/shard_map/ppermute | solution.py:317
  4.6 2.2 slice_bitcast_fusion
  8.7 2.3 concatenate.6.blocks_ref
  11.9 2.1 collective-permute-done.near_ref
  13.9 1.6 collective-permute-start.1
  15.5 4.5 %collective-permute-start.4 = (bf16[768,256]{1,0:T(8,128)(2,1)S(1)}, bf16[768,256]{1,0:T(8,128)(2,1)S(1)}, u32[]{:S(2)}, u32[]{:S(2)}) collective-permute-start(bf16[768,256]{1,0:T(8,128)(2,1)S(1)} %get-tuple-element.274.field_ref.refs_0_), channel_id=1, source_target_pairs={{0,4},{4,0},{8,12},{12,8},{16,20},{20,16},{24,28},{28,24},{1,5},{5... | collective-permute-start | bytes 1179656 | tf_op jit(solution)/shard_map/ppermute | solution.py:325
  20.0 3.9 %collective-permute-done.2.near_ref = bf16[768,256]{1,0:T(8,128)(2,1)S(1)} collective-permute-done((bf16[768,256]{1,0:T(8,128)(2,1)S(1)}, bf16[768,256]{1,0:T(8,128)(2,1)S(1)}, u32[]{:S(2)}, u32[]{:S(2)}) %collective-permute-start.2) | collective-permute-done | bytes 393248 | tf_op jit(solution)/shard_map/ppermute | solution.py:325
  25.5 3.0 %collective-permute-start.6 = (bf16[768,256]{1,0:T(8,128)(2,1)S(1)}, bf16[768,256]{1,0:T(8,128)(2,1)S(1)}, u32[]{:S(2)}, u32[]{:S(2)}) collective-permute-start(bf16[768,256]{1,0:T(8,128)(2,1)S(1)} %get-tuple-element.277.field_ref.refs_0_), channel_id=1, source_target_pairs={{0,4},{4,0},{8,12},{12,8},{16,20},{20,16},{24,28},{28,24},{1,5},{5... | collective-permute-start | bytes 1179656 | tf_op jit(solution)/shard_map/ppermute | solution.py:325
  29.7 2.6 collective-permute-done.4.near_ref
  32.3 1.6 collective-permute-start.5
  33.9 3.0 %collective-permute-start.3 = (bf16[768,256]{1,0:T(8,128)(2,1)S(1)}, bf16[768,256]{1,0:T(8,128)(2,1)S(1)}, u32[]{:S(2)}, u32[]{:S(2)}) collective-permute-start(bf16[768,256]{1,0:T(8,128)(2,1)S(1)} %get-tuple-element.273.field_ref), channel_id=1, source_target_pairs={{0,4},{4,0},{8,12},{12,8},{16,20},{20,16},{24,28},{28,24},{1,5},{5... | collective-permute-start | bytes 1179656 | tf_op jit(solution)/shard_map/ppermute | solution.py:376
  38.1 2.6 collective-permute-done.6.near_ref
  40.7 1.6 collective-permute-start.10
  42.3 3.0 %collective-permute-start.9 = (bf16[768,256]{1,0:T(8,128)(2,1)S(1)}, bf16[768,256]{1,0:T(8,128)(2,1)S(1)}, u32[]{:S(2)}, u32[]{:S(2)}) collective-permute-start(bf16[768,256]{1,0:T(8,128)(2,1)S(1)} %get-tuple-element.292.field_ref), channel_id=1, source_target_pairs={{0,4},{4,0},{8,12},{12,8},{16,20},{20,16},{24,28},{28,24},{1,5},{5... | collective-permute-start | bytes 1179656 | tf_op jit(solution)/shard_map/ppermute | solution.py:376
  46.6 2.6 collective-permute-done.3.near_ref
  49.2 1.6 collective-permute-start.8
  50.7 3.0 %collective-permute-start.12 = (bf16[768,256]{1,0:T(8,128)(2,1)S(1)}, bf16[768,256]{1,0:T(8,128)(2,1)S(1)}, u32[]{:S(2)}, u32[]{:S(2)}) collective-permute-start(bf16[768,256]{1,0:T(8,128)(2,1)S(1)} %get-tuple-element.304.field_ref), channel_id=1, source_target_pairs={{0,4},{4,0},{8,12},{12,8},{16,20},{20,16},{24,28},{28,24},{1,5},{5... | collective-permute-start | bytes 1179656 | tf_op jit(solution)/shard_map/ppermute | solution.py:376
  55.0 2.6 collective-permute-done.9.near_ref
  57.6 1.6 collective-permute-start.15
  59.2 3.0 %collective-permute-start.14 = (bf16[768,256]{1,0:T(8,128)(2,1)S(1)}, bf16[768,256]{1,0:T(8,128)(2,1)S(1)}, u32[]{:S(2)}, u32[]{:S(2)}) collective-permute-start(bf16[768,256]{1,0:T(8,128)(2,1)S(1)} %get-tuple-element.307.field_ref), channel_id=1, source_target_pairs={{0,4},{4,0},{8,12},{12,8},{16,20},{20,16},{24,28},{28,24},{1,5},{5... | collective-permute-start | bytes 1179656 | tf_op jit(solution)/shard_map/ppermute | solution.py:376
  63.4 2.6 collective-permute-done.12.near_ref
  66.0 1.6 collective-permute-start.13
  67.6 3.0 %collective-permute-start.11 = (bf16[768,256]{1,0:T(8,128)(2,1)S(1)}, bf16[768,256]{1,0:T(8,128)(2,1)S(1)}, u32[]{:S(2)}, u32[]{:S(2)}) collective-permute-start(bf16[768,256]{1,0:T(8,128)(2,1)S(1)} %product_1.4.field_ref), channel_id=1, source_target_pairs={{0,4},{4,0},{8,12},{12,8},{16,20},{20,16},{24,28},{28,24},{1,5},{5... | collective-permute-start | bytes 1179656 | tf_op jit(solution)/shard_map/ppermute | solution.py:376
  71.8 2.6 collective-permute-done.14.near_ref
  74.4 1.6 collective-permute-start.18
  76.0 3.0 %collective-permute-start.17 = (bf16[768,256]{1,0:T(8,128)(2,1)S(1)}, bf16[768,256]{1,0:T(8,128)(2,1)S(1)}, u32[]{:S(2)}, u32[]{:S(2)}) collective-permute-start(bf16[768,256]{1,0:T(8,128)(2,1)S(1)} %product_1.5.field_ref), channel_id=1, source_target_pairs={{0,4},{4,0},{8,12},{12,8},{16,20},{20,16},{24,28},{28,24},{1,5},{5... | collective-permute-start | bytes 1179656 | tf_op jit(solution)/shard_map/ppermute | solution.py:376
  80.3 2.6 collective-permute-done.11.near_ref
  84.5 3.0 %collective-permute-start.20 = (bf16[768,256]{1,0:T(8,128)(2,1)S(1)}, bf16[768,256]{1,0:T(8,128)(2,1)S(1)}, u32[]{:S(2)}, u32[]{:S(2)}) collective-permute-start(bf16[768,256]{1,0:T(8,128)(2,1)S(1)} %product_1.6.field_ref), channel_id=1, source_target_pairs={{0,4},{4,0},{8,12},{12,8},{16,20},{20,16},{24,28},{28,24},{1,5},{5... | collective-permute-start | bytes 1179656 | tf_op jit(solution)/shard_map/ppermute | solution.py:376
  88.7 2.6 collective-permute-done.17.near_ref
  92.9 3.0 %collective-permute-start.22 = (bf16[768,256]{1,0:T(8,128)(2,1)S(1)}, bf16[768,256]{1,0:T(8,128)(2,1)S(1)}, u32[]{:S(2)}, u32[]{:S(2)}) collective-permute-start(bf16[768,256]{1,0:T(8,128)(2,1)S(1)} %product_1.7.field_ref), channel_id=1, source_target_pairs={{0,4},{4,0},{8,12},{12,8},{16,20},{20,16},{24,28},{28,24},{1,5},{5... | collective-permute-start | bytes 1179656 | tf_op jit(solution)/shard_map/ppermute | solution.py:376
  97.1 2.6 collective-permute-done.20.near_ref
  104.1 2.6 collective-permute-done.22.near_ref
  113.0 5.5 %collective-permute-done.23.far_ref = bf16[768,256]{1,0:T(8,128)(2,1)S(1)} collective-permute-done((bf16[768,256]{1,0:T(8,128)(2,1)S(1)}, bf16[768,256]{1,0:T(8,128)(2,1)S(1)}, u32[]{:S(2)}, u32[]{:S(2)}) %collective-permute-start.23) | collective-permute-done | bytes 393248 | tf_op jit(solution)/shard_map/ppermute | solution.py:334
  121.9 2.1 gram_own.1
  124.0 4.7 %collective-permute-done.29.refs_6_.refs_3_ = bf16[768,256]{1,0:T(8,128)(2,1)S(1)} collective-permute-done((bf16[768,256]{1,0:T(8,128)(2,1)S(1)}, bf16[768,256]{1,0:T(8,128)(2,1)S(1)}, u32[]{:S(2)}, u32[]{:S(2)}) %collective-permute-start.29) | collective-permute-done | bytes 393248 | tf_op jit(solution)/shard_map/ppermute | solution.py:304
  128.7 3.4 %collective-permute-start.35 = (bf16[384,1024]{1,0:T(8,128)(2,1)S(1)}, bf16[384,1024]{1,0:T(8,128)(2,1)S(1)}, u32[]{:S(2)}, u32[]{:S(2)}) collective-permute-start(bf16[384,1024]{1,0:T(8,128)(2,1)S(1)} %get-tuple-element.385), channel_id=1, source_target_pairs={{0,4},{4,0},{8,12},{12,8},{16,20},{20,16},{24,28},{28,24},{1,5},{5... | collective-permute-start | bytes 2359304 | tf_op jit(solution)/shard_map/ppermute | solution.py:400
  132.2 2.5 collective-permute-done.32.refs_7_.refs_9_.refs_4_
  135.7 1.6 gram_pair.3
  137.3 8.2 %collective-permute-done.35.refs_1_ = bf16[384,1024]{1,0:T(8,128)(2,1)S(1)} collective-permute-done((bf16[384,1024]{1,0:T(8,128)(2,1)S(1)}, bf16[384,1024]{1,0:T(8,128)(2,1)S(1)}, u32[]{:S(2)}, u32[]{:S(2)}) %collective-permute-start.35) | collective-permute-done | bytes 786464 | tf_op jit(solution)/shard_map/ppermute | solution.py:400
  146.2 1.8 gram_pair.4
  148.0 1.8 collective-permute-start.37
  149.9 2.0 collective-permute-start.38
  151.9 1.6 gram_pair.5
  153.8 8.5 %collective-permute-done.39.refs_1_ = bf16[256,1024]{1,0:T(8,128)(2,1)S(1)} collective-permute-done((bf16[256,1024]{1,0:T(8,128)(2,1)S(1)}, bf16[256,1024]{1,0:T(8,128)(2,1)S(1)}, u32[]{:S(2)}, u32[]{:S(2)}) %collective-permute-start.39) | collective-permute-done | bytes 524320 | tf_op jit(solution)/shard_map/ppermute | solution.py:400
  163.0 8.1 %collective-permute-done.38.refs_2_ = bf16[192,1024]{1,0:T(8,128)(2,1)S(1)} collective-permute-done((bf16[192,1024]{1,0:T(8,128)(2,1)S(1)}, bf16[192,1024]{1,0:T(8,128)(2,1)S(1)}, u32[]{:S(2)}, u32[]{:S(2)}) %collective-permute-start.38) | collective-permute-done | bytes 393248 | tf_op jit(solution)/shard_map/ppermute | solution.py:400
  172.5 2.0 collective-permute-start.41
  174.8 8.5 %collective-permute-done.41.refs_3_ = bf16[96,1024]{1,0:T(8,128)(2,1)S(1)} collective-permute-done((bf16[96,1024]{1,0:T(8,128)(2,1)S(1)}, bf16[96,1024]{1,0:T(8,128)(2,1)S(1)}, u32[]{:S(2)}, u32[]{:S(2)}) %collective-permute-start.41) | collective-permute-done | bytes 196640 | tf_op jit(solution)/shard_map/ppermute | solution.py:400
  183.3 2.8 collective-permute-done.40.refs_2_
  187.4 3.1 %collective-permute-start.42 = (bf16[80,1024]{1,0:T(8,128)(2,1)S(1)}, bf16[80,1024]{1,0:T(8,128)(2,1)S(1)}, u32[]{:S(2)}, u32[]{:S(2)}) collective-permute-start(bf16[80,1024]{1,0:T(8,128)(2,1)S(1)} %sum_hop.12), channel_id=1, source_target_pairs={{0,16},{4,20},{8,24},{12,28},{16,0},{20,4},{24,8},{28,12},{1,17},{... | collective-permute-start | bytes 491528 | tf_op jit(solution)/shard_map/ppermute | solution.py:400
  191.2 13.6 %collective-permute-done.42.refs_3_ = bf16[80,1024]{1,0:T(8,128)(2,1)S(1)} collective-permute-done((bf16[80,1024]{1,0:T(8,128)(2,1)S(1)}, bf16[80,1024]{1,0:T(8,128)(2,1)S(1)}, u32[]{:S(2)}, u32[]{:S(2)}) %collective-permute-start.42) | collective-permute-done | bytes 163872 | tf_op jit(solution)/shard_map/ppermute | solution.py:400
  208.4 2.9 collective-permute-start.53
  211.3 9.1 %collective-permute-done.52.lower_ref = bf16[64,1024]{1,0:T(8,128)(2,1)S(1)} collective-permute-done((bf16[64,1024]{1,0:T(8,128)(2,1)S(1)}, bf16[64,1024]{1,0:T(8,128)(2,1)S(1)}, u32[]{:S(2)}, u32[]{:S(2)}) %collective-permute-start.52) | collective-permute-done | bytes 131104 | tf_op jit(solution)/shard_map/ppermute | solution.py:400
  220.6 5.2 %collective-permute-done.46.refs_3_ = bf16[64,1024]{1,0:T(8,128)(2,1)S(1)} collective-permute-done((bf16[64,1024]{1,0:T(8,128)(2,1)S(1)}, bf16[64,1024]{1,0:T(8,128)(2,1)S(1)}, u32[]{:S(2)}, u32[]{:S(2)}) %collective-permute-start.46) | collective-permute-done | bytes 131104 | tf_op jit(solution)/shard_map/ppermute | solution.py:400
  228.8 4.0 %collective-permute-done.49.lower_ref = bf16[64,1024]{1,0:T(8,128)(2,1)S(1)} collective-permute-done((bf16[64,1024]{1,0:T(8,128)(2,1)S(1)}, bf16[64,1024]{1,0:T(8,128)(2,1)S(1)}, u32[]{:S(2)}, u32[]{:S(2)}) %collective-permute-start.49) | collective-permute-done | bytes 131104 | tf_op jit(solution)/shard_map/ppermute | solution.py:400
  233.7 5.2 %collective-permute-done.50.lower_ref = bf16[128,1024]{1,0:T(8,128)(2,1)S(1)} collective-permute-done((bf16[128,1024]{1,0:T(8,128)(2,1)S(1)}, bf16[128,1024]{1,0:T(8,128)(2,1)S(1)}, u32[]{:S(2)}, u32[]{:S(2)}) %collective-permute-start.50) | collective-permute-done | bytes 262176 | tf_op jit(solution)/shard_map/ppermute | solution.py:400
  238.9 2.8 collective-permute-done.54.lower_ref
  241.9 1.8 collective-permute-start.60
  244.1 10.4 %collective-permute-done.55.refs_5_ = bf16[256,1024]{1,0:T(8,128)(2,1)S(1)} collective-permute-done((bf16[256,1024]{1,0:T(8,128)(2,1)S(1)}, bf16[256,1024]{1,0:T(8,128)(2,1)S(1)}, u32[]{:S(2)}, u32[]{:S(2)}) %collective-permute-start.55) | collective-permute-done | bytes 524320 | tf_op jit(solution)/shard_map/ppermute | solution.py:400
  254.5 10.5 %collective-permute-done.60.refs_7_ = bf16[256,1024]{1,0:T(8,128)(2,1)S(1)} collective-permute-done((bf16[256,1024]{1,0:T(8,128)(2,1)S(1)}, bf16[256,1024]{1,0:T(8,128)(2,1)S(1)}, u32[]{:S(2)}, u32[]{:S(2)}) %collective-permute-start.60) | collective-permute-done | bytes 524320 | tf_op jit(solution)/shard_map/ppermute | solution.py:400
  266.9 12.4 %collective-permute-done.63.refs_8_ = bf16[256,1024]{1,0:T(8,128)(2,1)S(1)} collective-permute-done((bf16[256,1024]{1,0:T(8,128)(2,1)S(1)}, bf16[256,1024]{1,0:T(8,128)(2,1)S(1)}, u32[]{:S(2)}, u32[]{:S(2)}) %collective-permute-start.63) | collective-permute-done | bytes 524320 | tf_op jit(solution)/shard_map/ppermute | solution.py:400
  279.3 2.6 mix_pair.3.refs_0_
  281.9 2.9 mix_pair.4.refs_0_
  284.8 2.6 mix_own.1.refs_1_
  287.5 4.0 %mix_pair.5 = bf16[768,1024]{1,0:T(8,128)(2,1)} custom-call(s32[2]{0:T(128)S(1)} %get-tuple-element.386.where_ref, f32[8,128]{1,0:T(8,128)S(1)} %get-tuple-element.459.refs_4_.refs_0_, f32[768,1024]{1,0:T(8,128)S(1)} %mix_own.1.refs_1_, bf16[768,256]{1,0:T(8,128)(2,1)S(1)} %collective-permute-done.26.refs_4_.refs_2_, ...), custom_call_target="tpu_custom_call" | custom-call | flops 1024 | bytes 5242880 | tf_op jit(solution)/shard_map/mix_pair/pallas_call | solution.py:96
  (123 shorter events, 51.0 us)
Async XLA Ops:
  1.5 12.4 %collective-permute-start = (bf16[768,256]{1,0:T(8,128)(2,1)S(1)}, bf16[768,256]{1,0:T(8,128)(2,1)S(1)}, u32[]{:S(2)}, u32[]{:S(2)}) collective-permute-start(bf16[768,256]{1,0:T(8,128)(2,1)S(1)} %get-tuple-element.514.field_ref.refs_0_), channel_id=1, source_target_pairs={{0,4},{4,0},{8,12},{12,8},{16,20},{20,16},{24,28},{28,24},{1,5},{5... | collective-permute-start | bytes 1179656 | tf_op jit(solution)/shard_map/ppermute | solution.py:317
  11.8 12.0 %collective-permute-start.2 = (bf16[768,256]{1,0:T(8,128)(2,1)S(1)}, bf16[768,256]{1,0:T(8,128)(2,1)S(1)}, u32[]{:S(2)}, u32[]{:S(2)}) collective-permute-start(bf16[768,256]{1,0:T(8,128)(2,1)S(1)} %get-tuple-element.266.field_ref.refs_0_), channel_id=1, source_target_pairs={{0,4},{4,0},{8,12},{12,8},{16,20},{20,16},{24,28},{28,24},{1,5},{5... | collective-permute-start | bytes 1179656 | tf_op jit(solution)/shard_map/ppermute | solution.py:325
  13.9 14.5 %collective-permute-start.1 = (bf16[768,256]{1,0:T(8,128)(2,1)S(1)}, bf16[768,256]{1,0:T(8,128)(2,1)S(1)}, u32[]{:S(2)}, u32[]{:S(2)}) collective-permute-start(bf16[768,256]{1,0:T(8,128)(2,1)S(1)} %collective-permute-done.near_ref), channel_id=1, source_target_pairs={{0,8},{4,28},{8,16},{12,4},{16,24},{20,12},{24,0},{28,20},{1,9},{5... | collective-permute-start | bytes 1179656 | tf_op jit(solution)/shard_map/ppermute | solution.py:334
  15.5 16.8 %collective-permute-start.4 = (bf16[768,256]{1,0:T(8,128)(2,1)S(1)}, bf16[768,256]{1,0:T(8,128)(2,1)S(1)}, u32[]{:S(2)}, u32[]{:S(2)}) collective-permute-start(bf16[768,256]{1,0:T(8,128)(2,1)S(1)} %get-tuple-element.274.field_ref.refs_0_), channel_id=1, source_target_pairs={{0,4},{4,0},{8,12},{12,8},{16,20},{20,16},{24,28},{28,24},{1,5},{5... | collective-permute-start | bytes 1179656 | tf_op jit(solution)/shard_map/ppermute | solution.py:325
  23.9 13.0 %collective-permute-start.7 = (bf16[768,256]{1,0:T(8,128)(2,1)S(1)}, bf16[768,256]{1,0:T(8,128)(2,1)S(1)}, u32[]{:S(2)}, u32[]{:S(2)}) collective-permute-start(bf16[768,256]{1,0:T(8,128)(2,1)S(1)} %collective-permute-done.2.near_ref), channel_id=1, source_target_pairs={{0,8},{4,28},{8,16},{12,4},{16,24},{20,12},{24,0},{28,20},{1,9},{5... | collective-permute-start | bytes 1179656 | tf_op jit(solution)/shard_map/ppermute | solution.py:334
  25.5 15.3 %collective-permute-start.6 = (bf16[768,256]{1,0:T(8,128)(2,1)S(1)}, bf16[768,256]{1,0:T(8,128)(2,1)S(1)}, u32[]{:S(2)}, u32[]{:S(2)}) collective-permute-start(bf16[768,256]{1,0:T(8,128)(2,1)S(1)} %get-tuple-element.277.field_ref.refs_0_), channel_id=1, source_target_pairs={{0,4},{4,0},{8,12},{12,8},{16,20},{20,16},{24,28},{28,24},{1,5},{5... | collective-permute-start | bytes 1179656 | tf_op jit(solution)/shard_map/ppermute | solution.py:325
  32.3 13.0 %collective-permute-start.5 = (bf16[768,256]{1,0:T(8,128)(2,1)S(1)}, bf16[768,256]{1,0:T(8,128)(2,1)S(1)}, u32[]{:S(2)}, u32[]{:S(2)}) collective-permute-start(bf16[768,256]{1,0:T(8,128)(2,1)S(1)} %collective-permute-done.4.near_ref), channel_id=1, source_target_pairs={{0,8},{4,28},{8,16},{12,4},{16,24},{20,12},{24,0},{28,20},{1,9},{5... | collective-permute-start | bytes 1179656 | tf_op jit(solution)/shard_map/ppermute | solution.py:334
  33.9 15.3 %collective-permute-start.3 = (bf16[768,256]{1,0:T(8,128)(2,1)S(1)}, bf16[768,256]{1,0:T(8,128)(2,1)S(1)}, u32[]{:S(2)}, u32[]{:S(2)}) collective-permute-start(bf16[768,256]{1,0:T(8,128)(2,1)S(1)} %get-tuple-element.273.field_ref), channel_id=1, source_target_pairs={{0,4},{4,0},{8,12},{12,8},{16,20},{20,16},{24,28},{28,24},{1,5},{5... | collective-permute-start | bytes 1179656 | tf_op jit(solution)/shard_map/ppermute | solution.py:376
  40.7 13.0 %collective-permute-start.10 = (bf16[768,256]{1,0:T(8,128)(2,1)S(1)}, bf16[768,256]{1,0:T(8,128)(2,1)S(1)}, u32[]{:S(2)}, u32[]{:S(2)}) collective-permute-start(bf16[768,256]{1,0:T(8,128)(2,1)S(1)} %collective-permute-done.6.near_ref), channel_id=1, source_target_pairs={{0,8},{4,28},{8,16},{12,4},{16,24},{20,12},{24,0},{28,20},{1,9},{5... | collective-permute-start | bytes 1179656 | tf_op jit(solution)/shard_map/ppermute | solution.py:334
  42.3 15.3 %collective-permute-start.9 = (bf16[768,256]{1,0:T(8,128)(2,1)S(1)}, bf16[768,256]{1,0:T(8,128)(2,1)S(1)}, u32[]{:S(2)}, u32[]{:S(2)}) collective-permute-start(bf16[768,256]{1,0:T(8,128)(2,1)S(1)} %get-tuple-element.292.field_ref), channel_id=1, source_target_pairs={{0,4},{4,0},{8,12},{12,8},{16,20},{20,16},{24,28},{28,24},{1,5},{5... | collective-permute-start | bytes 1179656 | tf_op jit(solution)/shard_map/ppermute | solution.py:376
  49.2 13.0 %collective-permute-start.8 = (bf16[768,256]{1,0:T(8,128)(2,1)S(1)}, bf16[768,256]{1,0:T(8,128)(2,1)S(1)}, u32[]{:S(2)}, u32[]{:S(2)}) collective-permute-start(bf16[768,256]{1,0:T(8,128)(2,1)S(1)} %collective-permute-done.3.near_ref), channel_id=1, source_target_pairs={{0,8},{4,28},{8,16},{12,4},{16,24},{20,12},{24,0},{28,20},{1,9},{5... | collective-permute-start | bytes 1179656 | tf_op jit(solution)/shard_map/ppermute | solution.py:334
  50.7 15.3 %collective-permute-start.12 = (bf16[768,256]{1,0:T(8,128)(2,1)S(1)}, bf16[768,256]{1,0:T(8,128)(2,1)S(1)}, u32[]{:S(2)}, u32[]{:S(2)}) collective-permute-start(bf16[768,256]{1,0:T(8,128)(2,1)S(1)} %get-tuple-element.304.field_ref), channel_id=1, source_target_pairs={{0,4},{4,0},{8,12},{12,8},{16,20},{20,16},{24,28},{28,24},{1,5},{5... | collective-permute-start | bytes 1179656 | tf_op jit(solution)/shard_map/ppermute | solution.py:376
  57.6 13.0 %collective-permute-start.15 = (bf16[768,256]{1,0:T(8,128)(2,1)S(1)}, bf16[768,256]{1,0:T(8,128)(2,1)S(1)}, u32[]{:S(2)}, u32[]{:S(2)}) collective-permute-start(bf16[768,256]{1,0:T(8,128)(2,1)S(1)} %collective-permute-done.9.near_ref), channel_id=1, source_target_pairs={{0,8},{4,28},{8,16},{12,4},{16,24},{20,12},{24,0},{28,20},{1,9},{5... | collective-permute-start | bytes 1179656 | tf_op jit(solution)/shard_map/ppermute | solution.py:334
  59.2 15.3 %collective-permute-start.14 = (bf16[768,256]{1,0:T(8,128)(2,1)S(1)}, bf16[768,256]{1,0:T(8,128)(2,1)S(1)}, u32[]{:S(2)}, u32[]{:S(2)}) collective-permute-start(bf16[768,256]{1,0:T(8,128)(2,1)S(1)} %get-tuple-element.307.field_ref), channel_id=1, source_target_pairs={{0,4},{4,0},{8,12},{12,8},{16,20},{20,16},{24,28},{28,24},{1,5},{5... | collective-permute-start | bytes 1179656 | tf_op jit(solution)/shard_map/ppermute | solution.py:376
  66.0 13.0 %collective-permute-start.13 = (bf16[768,256]{1,0:T(8,128)(2,1)S(1)}, bf16[768,256]{1,0:T(8,128)(2,1)S(1)}, u32[]{:S(2)}, u32[]{:S(2)}) collective-permute-start(bf16[768,256]{1,0:T(8,128)(2,1)S(1)} %collective-permute-done.12.near_ref), channel_id=1, source_target_pairs={{0,8},{4,28},{8,16},{12,4},{16,24},{20,12},{24,0},{28,20},{1,9},{5... | collective-permute-start | bytes 1179656 | tf_op jit(solution)/shard_map/ppermute | solution.py:334
  67.6 15.3 %collective-permute-start.11 = (bf16[768,256]{1,0:T(8,128)(2,1)S(1)}, bf16[768,256]{1,0:T(8,128)(2,1)S(1)}, u32[]{:S(2)}, u32[]{:S(2)}) collective-permute-start(bf16[768,256]{1,0:T(8,128)(2,1)S(1)} %product_1.4.field_ref), channel_id=1, source_target_pairs={{0,4},{4,0},{8,12},{12,8},{16,20},{20,16},{24,28},{28,24},{1,5},{5... | collective-permute-start | bytes 1179656 | tf_op jit(solution)/shard_map/ppermute | solution.py:376
  74.4 13.0 %collective-permute-start.18 = (bf16[768,256]{1,0:T(8,128)(2,1)S(1)}, bf16[768,256]{1,0:T(8,128)(2,1)S(1)}, u32[]{:S(2)}, u32[]{:S(2)}) collective-permute-start(bf16[768,256]{1,0:T(8,128)(2,1)S(1)} %collective-permute-done.14.near_ref), channel_id=1, source_target_pairs={{0,8},{4,28},{8,16},{12,4},{16,24},{20,12},{24,0},{28,20},{1,9},{5... | collective-permute-start | bytes 1179656 | tf_op jit(solution)/shard_map/ppermute | solution.py:334
  76.0 15.3 %collective-permute-start.17 = (bf16[768,256]{1,0:T(8,128)(2,1)S(1)}, bf16[768,256]{1,0:T(8,128)(2,1)S(1)}, u32[]{:S(2)}, u32[]{:S(2)}) collective-permute-start(bf16[768,256]{1,0:T(8,128)(2,1)S(1)} %product_1.5.field_ref), channel_id=1, source_target_pairs={{0,4},{4,0},{8,12},{12,8},{16,20},{20,16},{24,28},{28,24},{1,5},{5... | collective-permute-start | bytes 1179656 | tf_op jit(solution)/shard_map/ppermute | solution.py:376
  82.9 13.0 %collective-permute-start.16 = (bf16[768,256]{1,0:T(8,128)(2,1)S(1)}, bf16[768,256]{1,0:T(8,128)(2,1)S(1)}, u32[]{:S(2)}, u32[]{:S(2)}) collective-permute-start(bf16[768,256]{1,0:T(8,128)(2,1)S(1)} %collective-permute-done.11.near_ref), channel_id=1, source_target_pairs={{0,8},{4,28},{8,16},{12,4},{16,24},{20,12},{24,0},{28,20},{1,9},{5... | collective-permute-start | bytes 1179656 | tf_op jit(solution)/shard_map/ppermute | solution.py:334
  84.5 15.3 %collective-permute-start.20 = (bf16[768,256]{1,0:T(8,128)(2,1)S(1)}, bf16[768,256]{1,0:T(8,128)(2,1)S(1)}, u32[]{:S(2)}, u32[]{:S(2)}) collective-permute-start(bf16[768,256]{1,0:T(8,128)(2,1)S(1)} %product_1.6.field_ref), channel_id=1, source_target_pairs={{0,4},{4,0},{8,12},{12,8},{16,20},{20,16},{24,28},{28,24},{1,5},{5... | collective-permute-start | bytes 1179656 | tf_op jit(solution)/shard_map/ppermute | solution.py:376
  91.3 11.5 %collective-permute-start.19 = (bf16[768,256]{1,0:T(8,128)(2,1)S(1)}, bf16[768,256]{1,0:T(8,128)(2,1)S(1)}, u32[]{:S(2)}, u32[]{:S(2)}) collective-permute-start(bf16[768,256]{1,0:T(8,128)(2,1)S(1)} %collective-permute-done.17.near_ref), channel_id=1, source_target_pairs={{0,8},{4,28},{8,16},{12,4},{16,24},{20,12},{24,0},{28,20},{1,9},{5... | collective-permute-start | bytes 1179656 | tf_op jit(solution)/shard_map/ppermute | solution.py:334
  92.9 13.8 %collective-permute-start.22 = (bf16[768,256]{1,0:T(8,128)(2,1)S(1)}, bf16[768,256]{1,0:T(8,128)(2,1)S(1)}, u32[]{:S(2)}, u32[]{:S(2)}) collective-permute-start(bf16[768,256]{1,0:T(8,128)(2,1)S(1)} %product_1.7.field_ref), channel_id=1, source_target_pairs={{0,4},{4,0},{8,12},{12,8},{16,20},{20,16},{24,28},{28,24},{1,5},{5... | collective-permute-start | bytes 1179656 | tf_op jit(solution)/shard_map/ppermute | solution.py:376
  99.7 10.4 %collective-permute-start.21 = (bf16[768,256]{1,0:T(8,128)(2,1)S(1)}, bf16[768,256]{1,0:T(8,128)(2,1)S(1)}, u32[]{:S(2)}, u32[]{:S(2)}) collective-permute-start(bf16[768,256]{1,0:T(8,128)(2,1)S(1)} %collective-permute-done.20.near_ref), channel_id=1, source_target_pairs={{0,8},{4,28},{8,16},{12,4},{16,24},{20,12},{24,0},{28,20},{1,9},{5... | collective-permute-start | bytes 1179656 | tf_op jit(solution)/shard_map/ppermute | solution.py:334
  101.3 10.2 %collective-permute-start.25 = (bf16[768,256]{1,0:T(8,128)(2,1)S(1)}, bf16[768,256]{1,0:T(8,128)(2,1)S(1)}, u32[]{:S(2)}, u32[]{:S(2)}) collective-permute-start(bf16[768,256]{1,0:T(8,128)(2,1)S(1)} %get-tuple-element.330.refs_0_.refs_1_.refs_10_), channel_id=1, source_target_pairs={{0,2},{1,3},{2,0},{3,1},{4,6},{5,7},{6,4},{7,5},{8,10},{9,11},{10,... | collective-permute-start | bytes 1179656 | tf_op jit(solution)/shard_map/ppermute | solution.py:304
  102.8 10.2 %collective-permute-start.24 = (bf16[768,256]{1,0:T(8,128)(2,1)S(1)}, bf16[768,256]{1,0:T(8,128)(2,1)S(1)}, u32[]{:S(2)}, u32[]{:S(2)}) collective-permute-start(bf16[768,256]{1,0:T(8,128)(2,1)S(1)} %get-tuple-element.330.refs_0_.refs_1_.refs_10_), channel_id=1, source_target_pairs={{0,1},{1,0},{2,3},{3,2},{4,5},{5,4},{6,7},{7,6},{8,9},{9,8},{10,11... | collective-permute-start | bytes 1179656 | tf_op jit(solution)/shard_map/ppermute | solution.py:304
  106.7 11.7 %collective-permute-start.23 = (bf16[768,256]{1,0:T(8,128)(2,1)S(1)}, bf16[768,256]{1,0:T(8,128)(2,1)S(1)}, u32[]{:S(2)}, u32[]{:S(2)}) collective-permute-start(bf16[768,256]{1,0:T(8,128)(2,1)S(1)} %collective-permute-done.22.near_ref), channel_id=1, source_target_pairs={{0,8},{4,28},{8,16},{12,4},{16,24},{20,12},{24,0},{28,20},{1,9},{5... | collective-permute-start | bytes 1179656 | tf_op jit(solution)/shard_map/ppermute | solution.py:334
  108.3 13.1 %collective-permute-start.27 = (bf16[768,256]{1,0:T(8,128)(2,1)S(1)}, bf16[768,256]{1,0:T(8,128)(2,1)S(1)}, u32[]{:S(2)}, u32[]{:S(2)}) collective-permute-start(bf16[768,256]{1,0:T(8,128)(2,1)S(1)} %get-tuple-element.341.refs_1_.refs_2_.refs_11_), channel_id=1, source_target_pairs={{0,2},{1,3},{2,0},{3,1},{4,6},{5,7},{6,4},{7,5},{8,10},{9,11},{10,... | collective-permute-start | bytes 1179656 | tf_op jit(solution)/shard_map/ppermute | solution.py:304
  110.2 13.9 %collective-permute-start.30 = (bf16[768,256]{1,0:T(8,128)(2,1)S(1)}, bf16[768,256]{1,0:T(8,128)(2,1)S(1)}, u32[]{:S(2)}, u32[]{:S(2)}) collective-permute-start(bf16[768,256]{1,0:T(8,128)(2,1)S(1)} %get-tuple-element.341.refs_1_.refs_2_.refs_11_), channel_id=1, source_target_pairs={{0,1},{1,0},{2,3},{3,2},{4,5},{5,4},{6,7},{7,6},{8,9},{9,8},{10,11... | collective-permute-start | bytes 1179656 | tf_op jit(solution)/shard_map/ppermute | solution.py:304
  111.5 17.3 %collective-permute-start.29 = (bf16[768,256]{1,0:T(8,128)(2,1)S(1)}, bf16[768,256]{1,0:T(8,128)(2,1)S(1)}, u32[]{:S(2)}, u32[]{:S(2)}) collective-permute-start(bf16[768,256]{1,0:T(8,128)(2,1)S(1)} %get-tuple-element.352.refs_2_.refs_3_.refs_12_), channel_id=1, source_target_pairs={{0,2},{1,3},{2,0},{3,1},{4,6},{5,7},{6,4},{7,5},{8,10},{9,11},{10,... | collective-permute-start | bytes 1179656 | tf_op jit(solution)/shard_map/ppermute | solution.py:304
  119.9 14.8 %collective-permute-start.32 = (bf16[784,256]{1,0:T(8,128)(2,1)S(1)}, bf16[784,256]{1,0:T(8,128)(2,1)S(1)}, u32[]{:S(2)}, u32[]{:S(2)}) collective-permute-start(bf16[784,256]{1,0:T(8,128)(2,1)S(1)} %product_2.7.refs_3_.refs_4_.refs_13_), channel_id=1, source_target_pairs={{0,2},{1,3},{2,0},{3,1},{4,6},{5,7},{6,4},{7,5},{8,10},{9,11},{10,... | collective-permute-start | bytes 1204232 | tf_op jit(solution)/shard_map/ppermute | solution.py:304
  121.4 10.8 %collective-permute-start.33 = (bf16[768,256]{1,0:T(8,128)(2,1)S(1)}, bf16[768,256]{1,0:T(8,128)(2,1)S(1)}, u32[]{:S(2)}, u32[]{:S(2)}) collective-permute-start(bf16[768,256]{1,0:T(8,128)(2,1)S(1)} %get-tuple-element.352.refs_2_.refs_3_.refs_12_), channel_id=1, source_target_pairs={{0,1},{1,0},{2,3},{3,2},{4,5},{5,4},{6,7},{7,6},{8,9},{9,8},{10,11... | collective-permute-start | bytes 1179656 | tf_op jit(solution)/shard_map/ppermute | solution.py:304
  121.4 13.8 %collective-permute-start.36 = (bf16[784,256]{1,0:T(8,128)(2,1)S(1)}, bf16[784,256]{1,0:T(8,128)(2,1)S(1)}, u32[]{:S(2)}, u32[]{:S(2)}) collective-permute-start(bf16[784,256]{1,0:T(8,128)(2,1)S(1)} %product_2.7.refs_3_.refs_4_.refs_13_), channel_id=1, source_target_pairs={{0,1},{1,0},{2,3},{3,2},{4,5},{5,4},{6,7},{7,6},{8,9},{9,8},{10,11... | collective-permute-start | bytes 1204232 | tf_op jit(solution)/shard_map/ppermute | solution.py:304
  128.7 16.8 %collective-permute-start.35 = (bf16[384,1024]{1,0:T(8,128)(2,1)S(1)}, bf16[384,1024]{1,0:T(8,128)(2,1)S(1)}, u32[]{:S(2)}, u32[]{:S(2)}) collective-permute-start(bf16[384,1024]{1,0:T(8,128)(2,1)S(1)} %get-tuple-element.385), channel_id=1, source_target_pairs={{0,4},{4,0},{8,12},{12,8},{16,20},{20,16},{24,28},{28,24},{1,5},{5... | collective-permute-start | bytes 2359304 | tf_op jit(solution)/shard_map/ppermute | solution.py:400
  134.7 11.5 %collective-permute-start.34 = (bf16[784,256]{1,0:T(8,128)(2,1)S(1)}, bf16[784,256]{1,0:T(8,128)(2,1)S(1)}, u32[]{:S(2)}, u32[]{:S(2)}) collective-permute-start(bf16[784,256]{1,0:T(8,128)(2,1)S(1)} %collective-permute-done.32.refs_7_.refs_9_.refs_4_), channel_id=1, source_target_pairs={{0,1},{1,0},{2,3},{3,2},{4,5},{5,4},{6,7},{7,6},{8,9},{9,8},{10,11... | collective-permute-start | bytes 1204232 | tf_op jit(solution)/shard_map/ppermute | solution.py:304
  134.7 11.5 %collective-permute-start.26 = (bf16[768,256]{1,0:T(8,128)(2,1)S(1)}, bf16[768,256]{1,0:T(8,128)(2,1)S(1)}, u32[]{:S(2)}, u32[]{:S(2)}) collective-permute-start(bf16[768,256]{1,0:T(8,128)(2,1)S(1)} %collective-permute-done.25.refs_4_.refs_1_), channel_id=1, source_target_pairs={{0,1},{1,0},{2,3},{3,2},{4,5},{5,4},{6,7},{7,6},{8,9},{9,8},{10,11... | collective-permute-start | bytes 1179656 | tf_op jit(solution)/shard_map/ppermute | solution.py:304
  135.2 11.0 %collective-permute-start.28 = (bf16[768,256]{1,0:T(8,128)(2,1)S(1)}, bf16[768,256]{1,0:T(8,128)(2,1)S(1)}, u32[]{:S(2)}, u32[]{:S(2)}) collective-permute-start(bf16[768,256]{1,0:T(8,128)(2,1)S(1)} %collective-permute-done.27.refs_5_.refs_2_), channel_id=1, source_target_pairs={{0,1},{1,0},{2,3},{3,2},{4,5},{5,4},{6,7},{7,6},{8,9},{9,8},{10,11... | collective-permute-start | bytes 1179656 | tf_op jit(solution)/shard_map/ppermute | solution.py:304
  135.2 11.0 %collective-permute-start.31 = (bf16[768,256]{1,0:T(8,128)(2,1)S(1)}, bf16[768,256]{1,0:T(8,128)(2,1)S(1)}, u32[]{:S(2)}, u32[]{:S(2)}) collective-permute-start(bf16[768,256]{1,0:T(8,128)(2,1)S(1)} %collective-permute-done.29.refs_6_.refs_3_), channel_id=1, source_target_pairs={{0,1},{1,0},{2,3},{3,2},{4,5},{5,4},{6,7},{7,6},{8,9},{9,8},{10,11... | collective-permute-start | bytes 1179656 | tf_op jit(solution)/shard_map/ppermute | solution.py:304
  148.0 23.7 %collective-permute-start.37 = (bf16[272,1024]{1,0:T(8,128)(2,1)S(1)}, bf16[272,1024]{1,0:T(8,128)(2,1)S(1)}, u32[]{:S(2)}, u32[]{:S(2)}) collective-permute-start(bf16[272,1024]{1,0:T(8,128)(2,1)S(1)} %get-tuple-element.413), channel_id=1, source_target_pairs={{0,4},{4,0},{8,12},{12,8},{16,20},{20,16},{24,28},{28,24},{1,5},{5... | collective-permute-start | bytes 1671176 | tf_op jit(solution)/shard_map/ppermute | solution.py:400
  149.8 12.5 %collective-permute-start.39 = (bf16[256,1024]{1,0:T(8,128)(2,1)S(1)}, bf16[256,1024]{1,0:T(8,128)(2,1)S(1)}, u32[]{:S(2)}, u32[]{:S(2)}) collective-permute-start(bf16[256,1024]{1,0:T(8,128)(2,1)S(1)} %get-tuple-element.416), channel_id=1, source_target_pairs={{0,8},{4,12},{8,0},{12,4},{16,24},{20,28},{24,16},{28,20},{1,9},{5... | collective-permute-start | bytes 1572872 | tf_op jit(solution)/shard_map/ppermute | solution.py:400
  149.9 21.2 %collective-permute-start.38 = (bf16[192,1024]{1,0:T(8,128)(2,1)S(1)}, bf16[192,1024]{1,0:T(8,128)(2,1)S(1)}, u32[]{:S(2)}, u32[]{:S(2)}) collective-permute-start(bf16[192,1024]{1,0:T(8,128)(2,1)S(1)} %sum_hop.8), channel_id=1, source_target_pairs={{0,8},{4,12},{8,0},{12,4},{16,24},{20,28},{24,16},{28,20},{1,9},{5... | collective-permute-start | bytes 1179656 | tf_op jit(solution)/shard_map/ppermute | solution.py:400
  153.5 33.2 %collective-permute-start.44 = (bf16[256,1024]{1,0:T(8,128)(2,1)S(1)}, bf16[256,1024]{1,0:T(8,128)(2,1)S(1)}, u32[]{:S(2)}, u32[]{:S(2)}) collective-permute-start(bf16[256,1024]{1,0:T(8,128)(2,1)S(1)} %get-tuple-element.447), channel_id=1, source_target_pairs={{0,4},{4,0},{8,12},{12,8},{16,20},{20,16},{24,28},{28,24},{1,5},{5... | collective-permute-start | bytes 1572872 | tf_op jit(solution)/shard_map/ppermute | solution.py:400
  172.4 13.6 %collective-permute-start.40 = (bf16[144,1024]{1,0:T(8,128)(2,1)S(1)}, bf16[144,1024]{1,0:T(8,128)(2,1)S(1)}, u32[]{:S(2)}, u32[]{:S(2)}) collective-permute-start(bf16[144,1024]{1,0:T(8,128)(2,1)S(1)} %sum_hop.11), channel_id=1, source_target_pairs={{0,8},{4,12},{8,0},{12,4},{16,24},{20,28},{24,16},{28,20},{1,9},{5... | collective-permute-start | bytes 884744 | tf_op jit(solution)/shard_map/ppermute | solution.py:400
  172.5 10.8 %collective-permute-start.41 = (bf16[96,1024]{1,0:T(8,128)(2,1)S(1)}, bf16[96,1024]{1,0:T(8,128)(2,1)S(1)}, u32[]{:S(2)}, u32[]{:S(2)}) collective-permute-start(bf16[96,1024]{1,0:T(8,128)(2,1)S(1)} %sum_hop.10), channel_id=1, source_target_pairs={{0,16},{4,20},{8,24},{12,28},{16,0},{20,4},{24,8},{28,12},{1,17},{... | collective-permute-start | bytes 589832 | tf_op jit(solution)/shard_map/ppermute | solution.py:400
  174.5 16.0 %collective-permute-start.43 = (bf16[128,1024]{1,0:T(8,128)(2,1)S(1)}, bf16[128,1024]{1,0:T(8,128)(2,1)S(1)}, u32[]{:S(2)}, u32[]{:S(2)}) collective-permute-start(bf16[128,1024]{1,0:T(8,128)(2,1)S(1)} %sum_hop.9), channel_id=1, source_target_pairs={{0,4},{4,0},{8,12},{12,8},{16,20},{20,16},{24,28},{28,24},{1,5},{5... | collective-permute-start | bytes 786440 | tf_op jit(solution)/shard_map/ppermute | solution.py:400
  187.3 18.9 %collective-permute-start.45 = (bf16[128,1024]{1,0:T(8,128)(2,1)S(1)}, bf16[128,1024]{1,0:T(8,128)(2,1)S(1)}, u32[]{:S(2)}, u32[]{:S(2)}) collective-permute-start(bf16[128,1024]{1,0:T(8,128)(2,1)S(1)} %sum_hop.13), channel_id=1, source_target_pairs={{0,8},{4,12},{8,0},{12,4},{16,24},{20,28},{24,16},{28,20},{1,9},{5... | collective-permute-start | bytes 786440 | tf_op jit(solution)/shard_map/ppermute | solution.py:400
  187.4 17.4 %collective-permute-start.42 = (bf16[80,1024]{1,0:T(8,128)(2,1)S(1)}, bf16[80,1024]{1,0:T(8,128)(2,1)S(1)}, u32[]{:S(2)}, u32[]{:S(2)}) collective-permute-start(bf16[80,1024]{1,0:T(8,128)(2,1)S(1)} %sum_hop.12), channel_id=1, source_target_pairs={{0,16},{4,20},{8,24},{12,28},{16,0},{20,4},{24,8},{28,12},{1,17},{... | collective-permute-start | bytes 491528 | tf_op jit(solution)/shard_map/ppermute | solution.py:400
  191.1 16.5 %collective-permute-start.48 = (bf16[64,1024]{1,0:T(8,128)(2,1)S(1)}, bf16[64,1024]{1,0:T(8,128)(2,1)S(1)}, u32[]{:S(2)}, u32[]{:S(2)}) collective-permute-start(bf16[64,1024]{1,0:T(8,128)(2,1)S(1)} %sum_hop.14), channel_id=1, source_target_pairs={{0,16},{4,20},{8,24},{12,28},{16,0},{20,4},{24,8},{28,12},{1,17},{... | collective-permute-start | bytes 393224 | tf_op jit(solution)/shard_map/ppermute | solution.py:400
  208.3 12.2 %collective-permute-start.52 = (bf16[64,1024]{1,0:T(8,128)(2,1)S(1)}, bf16[64,1024]{1,0:T(8,128)(2,1)S(1)}, u32[]{:S(2)}, u32[]{:S(2)}) collective-permute-start(bf16[64,1024]{1,0:T(8,128)(2,1)S(1)} %sum_last.6.upper_ref), channel_id=1, source_target_pairs={{0,16},{4,20},{8,24},{12,28},{16,0},{20,4},{24,8},{28,12},{1,17},{... | collective-permute-start | bytes 393224 | tf_op jit(solution)/shard_map/ppermute | solution.py:400
  208.4 18.2 %collective-permute-start.53 = (bf16[96,1024]{1,0:T(8,128)(2,1)S(1)}, bf16[96,1024]{1,0:T(8,128)(2,1)S(1)}, u32[]{:S(2)}, u32[]{:S(2)}) collective-permute-start(bf16[96,1024]{1,0:T(8,128)(2,1)S(1)} %sum_last.5.upper_ref), channel_id=1, source_target_pairs={{0,16},{4,20},{8,24},{12,28},{16,0},{20,4},{24,8},{28,12},{1,17},{... | collective-permute-start | bytes 589832 | tf_op jit(solution)/shard_map/ppermute | solution.py:400
  211.3 14.5 %collective-permute-start.46 = (bf16[64,1024]{1,0:T(8,128)(2,1)S(1)}, bf16[64,1024]{1,0:T(8,128)(2,1)S(1)}, u32[]{:S(2)}, u32[]{:S(2)}) collective-permute-start(bf16[64,1024]{1,0:T(8,128)(2,1)S(1)} %sum_hop.15), channel_id=1, source_target_pairs={{0,16},{4,20},{8,24},{12,28},{16,0},{20,4},{24,8},{28,12},{1,17},{... | collective-permute-start | bytes 393224 | tf_op jit(solution)/shard_map/ppermute | solution.py:400
  220.5 12.4 %collective-permute-start.58 = (bf16[128,1024]{1,0:T(8,128)(2,1)S(1)}, bf16[128,1024]{1,0:T(8,128)(2,1)S(1)}, u32[]{:S(2)}, u32[]{:S(2)}) collective-permute-start(bf16[128,1024]{1,0:T(8,128)(2,1)S(1)} %join.11.upper_ref), channel_id=1, source_target_pairs={{0,4},{4,0},{8,12},{12,8},{16,20},{20,16},{24,28},{28,24},{1,5},{5... | collective-permute-start | bytes 786440 | tf_op jit(solution)/shard_map/ppermute | solution.py:400
  220.5 7.5 %collective-permute-start.47 = (bf16[64,1024]{1,0:T(8,128)(2,1)S(1)}, bf16[64,1024]{1,0:T(8,128)(2,1)S(1)}, u32[]{:S(2)}, u32[]{:S(2)}) collective-permute-start(bf16[64,1024]{1,0:T(8,128)(2,1)S(1)} %get-tuple-element.465.upper_ref), channel_id=1, source_target_pairs={{0,16},{4,20},{8,24},{12,28},{16,0},{20,4},{24,8},{28,12},{1,17},{... | collective-permute-start | bytes 393224 | tf_op jit(solution)/shard_map/ppermute | solution.py:400
  226.6 17.2 %collective-permute-start.59 = (bf16[192,1024]{1,0:T(8,128)(2,1)S(1)}, bf16[192,1024]{1,0:T(8,128)(2,1)S(1)}, u32[]{:S(2)}, u32[]{:S(2)}) collective-permute-start(bf16[192,1024]{1,0:T(8,128)(2,1)S(1)} %join.10.upper_ref), channel_id=1, source_target_pairs={{0,8},{4,12},{8,0},{12,4},{16,24},{20,28},{24,16},{28,20},{1,9},{5... | collective-permute-start | bytes 1179656 | tf_op jit(solution)/shard_map/ppermute | solution.py:400
  228.1 10.8 %collective-permute-start.50 = (bf16[128,1024]{1,0:T(8,128)(2,1)S(1)}, bf16[128,1024]{1,0:T(8,128)(2,1)S(1)}, u32[]{:S(2)}, u32[]{:S(2)}) collective-permute-start(bf16[128,1024]{1,0:T(8,128)(2,1)S(1)} %join.8.upper_ref), channel_id=1, source_target_pairs={{0,8},{4,12},{8,0},{12,4},{16,24},{20,28},{24,16},{28,20},{1,9},{5... | collective-permute-start | bytes 786440 | tf_op jit(solution)/shard_map/ppermute | solution.py:400
  232.8 8.8 %collective-permute-start.54 = (bf16[128,1024]{1,0:T(8,128)(2,1)S(1)}, bf16[128,1024]{1,0:T(8,128)(2,1)S(1)}, u32[]{:S(2)}, u32[]{:S(2)}) collective-permute-start(bf16[128,1024]{1,0:T(8,128)(2,1)S(1)} %join.12.upper_ref), channel_id=1, source_target_pairs={{0,8},{4,12},{8,0},{12,4},{16,24},{20,28},{24,16},{28,20},{1,9},{5... | collective-permute-start | bytes 786440 | tf_op jit(solution)/shard_map/ppermute | solution.py:400
  232.9 10.9 %collective-permute-start.62 = (bf16[256,1024]{1,0:T(8,128)(2,1)S(1)}, bf16[256,1024]{1,0:T(8,128)(2,1)S(1)}, u32[]{:S(2)}, u32[]{:S(2)}) collective-permute-start(bf16[256,1024]{1,0:T(8,128)(2,1)S(1)} %join.15.refs_5_), channel_id=1, source_target_pairs={{0,2},{1,3},{2,0},{3,1},{4,6},{5,7},{6,4},{7,5},{8,10},{9,11},{10,... | collective-permute-start | bytes 1572872 | tf_op jit(solution)/shard_map/ppermute | solution.py:304
  241.7 12.8 %collective-permute-start.55 = (bf16[256,1024]{1,0:T(8,128)(2,1)S(1)}, bf16[256,1024]{1,0:T(8,128)(2,1)S(1)}, u32[]{:S(2)}, u32[]{:S(2)}) collective-permute-start(bf16[256,1024]{1,0:T(8,128)(2,1)S(1)} %join.13.refs_4_), channel_id=1, source_target_pairs={{0,4},{4,0},{8,12},{12,8},{16,20},{20,16},{24,28},{28,24},{1,5},{5... | collective-permute-start | bytes 1572872 | tf_op jit(solution)/shard_map/ppermute | solution.py:400
  241.9 23.0 %collective-permute-start.60 = (bf16[256,1024]{1,0:T(8,128)(2,1)S(1)}, bf16[256,1024]{1,0:T(8,128)(2,1)S(1)}, u32[]{:S(2)}, u32[]{:S(2)}) collective-permute-start(bf16[256,1024]{1,0:T(8,128)(2,1)S(1)} %join.9.refs_6_), channel_id=1, source_target_pairs={{0,4},{4,0},{8,12},{12,8},{16,20},{20,16},{24,28},{28,24},{1,5},{5... | collective-permute-start | bytes 1572872 | tf_op jit(solution)/shard_map/ppermute | solution.py:400
  243.8 21.2 %collective-permute-start.51 = (bf16[256,1024]{1,0:T(8,128)(2,1)S(1)}, bf16[256,1024]{1,0:T(8,128)(2,1)S(1)}, u32[]{:S(2)}, u32[]{:S(2)}) collective-permute-start(bf16[256,1024]{1,0:T(8,128)(2,1)S(1)} %join.9.refs_6_), channel_id=1, source_target_pairs={{0,3},{1,2},{2,1},{3,0},{4,7},{5,6},{6,5},{7,4},{8,11},{9,10},{10,... | collective-permute-start | bytes 1572872 | tf_op jit(solution)/shard_map/ppermute | solution.py:304
  243.8 21.2 %collective-permute-start.61 = (bf16[256,1024]{1,0:T(8,128)(2,1)S(1)}, bf16[256,1024]{1,0:T(8,128)(2,1)S(1)}, u32[]{:S(2)}, u32[]{:S(2)}) collective-permute-start(bf16[256,1024]{1,0:T(8,128)(2,1)S(1)} %join.15.refs_5_), channel_id=1, source_target_pairs={{0,8},{4,12},{8,0},{12,4},{16,24},{20,28},{24,16},{28,20},{1,9},{5... | collective-permute-start | bytes 1572872 | tf_op jit(solution)/shard_map/ppermute | solution.py:400
  243.9 38.0 %collective-permute-start.64 = (bf16[384,1024]{1,0:T(8,128)(2,1)S(1)}, bf16[384,1024]{1,0:T(8,128)(2,1)S(1)}, u32[]{:S(2)}, u32[]{:S(2)}) collective-permute-start(bf16[384,1024]{1,0:T(8,128)(2,1)S(1)} %join.14.refs_5_), channel_id=1, source_target_pairs={{0,4},{4,0},{8,12},{12,8},{16,20},{20,16},{24,28},{28,24},{1,5},{5... | collective-permute-start | bytes 2359304 | tf_op jit(solution)/shard_map/ppermute | solution.py:400
  254.5 11.3 %collective-permute-start.56 = (bf16[256,1024]{1,0:T(8,128)(2,1)S(1)}, bf16[256,1024]{1,0:T(8,128)(2,1)S(1)}, u32[]{:S(2)}, u32[]{:S(2)}) collective-permute-start(bf16[256,1024]{1,0:T(8,128)(2,1)S(1)} %join.13.refs_4_), channel_id=1, source_target_pairs={{0,1},{1,0},{2,3},{3,2},{4,5},{5,4},{6,7},{7,6},{8,9},{9,8},{10,11... | collective-permute-start | bytes 1572872 | tf_op jit(solution)/shard_map/ppermute | solution.py:304
  265.0 14.3 %collective-permute-start.63 = (bf16[256,1024]{1,0:T(8,128)(2,1)S(1)}, bf16[256,1024]{1,0:T(8,128)(2,1)S(1)}, u32[]{:S(2)}, u32[]{:S(2)}) collective-permute-start(bf16[256,1024]{1,0:T(8,128)(2,1)S(1)} %collective-permute-done.62.refs_7_), channel_id=1, source_target_pairs={{0,8},{4,12},{8,0},{12,4},{16,24},{20,28},{24,16},{28,20},{1,9},{5... | collective-permute-start | bytes 1572872 | tf_op jit(solution)/shard_map/ppermute | solution.py:400
  265.0 19.8 %collective-permute-start.65 = (bf16[256,1024]{1,0:T(8,128)(2,1)S(1)}, bf16[256,1024]{1,0:T(8,128)(2,1)S(1)}, u32[]{:S(2)}, u32[]{:S(2)}) collective-permute-start(bf16[256,1024]{1,0:T(8,128)(2,1)S(1)} %collective-permute-done.60.refs_7_), channel_id=1, source_target_pairs={{0,3},{1,2},{2,1},{3,0},{4,7},{5,6},{6,5},{7,4},{8,11},{9,10},{10,... | collective-permute-start | bytes 1572872 | tf_op jit(solution)/shard_map/ppermute | solution.py:304
  (3 other events, 12.7 us)

commit v16 on v13

--- a/solution.py
+++ b/solution.py
@@ -431,7 +431,7 @@
         name = "gram_pair" if d else "gram_own"
         clock.spend(3.2 if d else 3.0)
         return call(
-            functools.partial(gram_kernel, d > 0, mask), name, (half, half), (where(d),), fields, scratch, moved=5 * MIB
+            functools.partial(gram_kernel, d > 0, mask), name, (half, half), (where(d),), fields, scratch
         )
 
     sent = [None]

time: 282 us -> 282 us (level)
  no operation moved by 1% of the time
where the time goes in v16:
time: 282 us; the launch traced here: 281 us
  waiting for transfers between devices  138 us (49%)
  starting transfers between devices  91.1 us (32%)
  Pallas kernels  42.7 us (15%)
  local copies, waits for them, and re-layouts  6.77 us (2%)
    ppermute x25, waiting for transfers between devices, over_tiles(): sent = lax.ppermute(value, 'elem', [(i, i ^ mask) for i in range(tiles)])  86.1 us
    pallas_call x40, Pallas kernels, call(): pl.pallas_call(kernel, out_shape=outs, in_specs=[pl.BlockSpec(memory_spac...  42.7 us
    ppermute x25, starting transfers between devices, over_tiles(): sent = lax.ppermute(value, 'elem', [(i, i ^ mask) for i in range(tiles)])  27.2 us
    ppermute x8, starting transfers between devices, multiply(): near[stage + 1, c] = lax.ppermute(out, 'elem', swap)  23.7 us
    ppermute x8, waiting for transfers between devices, multiply(): near[stage + 1, c] = lax.ppermute(out, 'elem', swap)  20.8 us
    ppermute x12, starting transfers between devices, send_on(): far[job] = lax.ppermute(near[job], 'elem', outward)  18.9 us
    ppermute x17, waiting for transfers between devices, to_group(): return lax.ppermute(value, 'orb', [(i, i ^ d) for i in range(groups)])  14.3 us
    ppermute x17, starting transfers between devices, to_group(): return lax.ppermute(value, 'orb', [(i, i ^ d) for i in range(groups)])  10.7 us
  transfers between devices with their start and end apart: 66, of which 35 were waited for; matrix products, arithmetic and copies ran while one was open for 3% of the time, Pallas kernels for 13%

profile of v16, /device:TPU:0, one launch (start us, length us, event | category | flops | bytes accessed | tf_op | source)
XLA Modules:
  0.0 281.3 jit_solution(1747255074712496092)
XLA Ops:
  1.5 3.0 %collective-permute-start = (bf16[768,256]{1,0:T(8,128)(2,1)S(1)}, bf16[768,256]{1,0:T(8,128)(2,1)S(1)}, u32[]{:S(2)}, u32[]{:S(2)}) collective-permute-start(bf16[768,256]{1,0:T(8,128)(2,1)S(1)} %get-tuple-element.511.field_ref.refs_0_), channel_id=1, source_target_pairs={{0,4},{4,0},{8,12},{12,8},{16,20},{20,16},{24,28},{28,24},{1,5},{5... | collective-permute-start | bytes 1179656 | tf_op jit(solution)/shard_map/ppermute | solution.py:317
  4.5 2.2 slice_bitcast_fusion
  8.7 2.3 concatenate.6.blocks_ref
  11.9 2.1 collective-permute-done.near_ref
  13.9 1.6 collective-permute-start.1
  15.5 4.5 %collective-permute-start.4 = (bf16[768,256]{1,0:T(8,128)(2,1)S(1)}, bf16[768,256]{1,0:T(8,128)(2,1)S(1)}, u32[]{:S(2)}, u32[]{:S(2)}) collective-permute-start(bf16[768,256]{1,0:T(8,128)(2,1)S(1)} %get-tuple-element.273.field_ref.refs_0_), channel_id=1, source_target_pairs={{0,4},{4,0},{8,12},{12,8},{16,20},{20,16},{24,28},{28,24},{1,5},{5... | collective-permute-start | bytes 1179656 | tf_op jit(solution)/shard_map/ppermute | solution.py:325
  20.0 3.9 %collective-permute-done.2.near_ref = bf16[768,256]{1,0:T(8,128)(2,1)S(1)} collective-permute-done((bf16[768,256]{1,0:T(8,128)(2,1)S(1)}, bf16[768,256]{1,0:T(8,128)(2,1)S(1)}, u32[]{:S(2)}, u32[]{:S(2)}) %collective-permute-start.2) | collective-permute-done | bytes 393248 | tf_op jit(solution)/shard_map/ppermute | solution.py:325
  23.9 1.6 collective-permute-start.7
  25.5 3.0 %collective-permute-start.6 = (bf16[768,256]{1,0:T(8,128)(2,1)S(1)}, bf16[768,256]{1,0:T(8,128)(2,1)S(1)}, u32[]{:S(2)}, u32[]{:S(2)}) collective-permute-start(bf16[768,256]{1,0:T(8,128)(2,1)S(1)} %get-tuple-element.276.field_ref.refs_0_), channel_id=1, source_target_pairs={{0,4},{4,0},{8,12},{12,8},{16,20},{20,16},{24,28},{28,24},{1,5},{5... | collective-permute-start | bytes 1179656 | tf_op jit(solution)/shard_map/ppermute | solution.py:325
  29.7 2.6 collective-permute-done.4.near_ref
  33.9 3.0 %collective-permute-start.3 = (bf16[768,256]{1,0:T(8,128)(2,1)S(1)}, bf16[768,256]{1,0:T(8,128)(2,1)S(1)}, u32[]{:S(2)}, u32[]{:S(2)}) collective-permute-start(bf16[768,256]{1,0:T(8,128)(2,1)S(1)} %get-tuple-element.272.field_ref), channel_id=1, source_target_pairs={{0,4},{4,0},{8,12},{12,8},{16,20},{20,16},{24,28},{28,24},{1,5},{5... | collective-permute-start | bytes 1179656 | tf_op jit(solution)/shard_map/ppermute | solution.py:376
  38.1 2.6 collective-permute-done.6.near_ref
  42.3 3.0 %collective-permute-start.9 = (bf16[768,256]{1,0:T(8,128)(2,1)S(1)}, bf16[768,256]{1,0:T(8,128)(2,1)S(1)}, u32[]{:S(2)}, u32[]{:S(2)}) collective-permute-start(bf16[768,256]{1,0:T(8,128)(2,1)S(1)} %get-tuple-element.291.field_ref), channel_id=1, source_target_pairs={{0,4},{4,0},{8,12},{12,8},{16,20},{20,16},{24,28},{28,24},{1,5},{5... | collective-permute-start | bytes 1179656 | tf_op jit(solution)/shard_map/ppermute | solution.py:376
  46.6 2.6 collective-permute-done.3.near_ref
  49.2 1.6 collective-permute-start.8
  50.7 3.0 %collective-permute-start.12 = (bf16[768,256]{1,0:T(8,128)(2,1)S(1)}, bf16[768,256]{1,0:T(8,128)(2,1)S(1)}, u32[]{:S(2)}, u32[]{:S(2)}) collective-permute-start(bf16[768,256]{1,0:T(8,128)(2,1)S(1)} %get-tuple-element.303.field_ref), channel_id=1, source_target_pairs={{0,4},{4,0},{8,12},{12,8},{16,20},{20,16},{24,28},{28,24},{1,5},{5... | collective-permute-start | bytes 1179656 | tf_op jit(solution)/shard_map/ppermute | solution.py:376
  55.0 2.6 collective-permute-done.9.near_ref
  59.2 3.0 %collective-permute-start.14 = (bf16[768,256]{1,0:T(8,128)(2,1)S(1)}, bf16[768,256]{1,0:T(8,128)(2,1)S(1)}, u32[]{:S(2)}, u32[]{:S(2)}) collective-permute-start(bf16[768,256]{1,0:T(8,128)(2,1)S(1)} %get-tuple-element.306.field_ref), channel_id=1, source_target_pairs={{0,4},{4,0},{8,12},{12,8},{16,20},{20,16},{24,28},{28,24},{1,5},{5... | collective-permute-start | bytes 1179656 | tf_op jit(solution)/shard_map/ppermute | solution.py:376
  63.4 2.6 collective-permute-done.12.near_ref
  67.6 3.0 %collective-permute-start.11 = (bf16[768,256]{1,0:T(8,128)(2,1)S(1)}, bf16[768,256]{1,0:T(8,128)(2,1)S(1)}, u32[]{:S(2)}, u32[]{:S(2)}) collective-permute-start(bf16[768,256]{1,0:T(8,128)(2,1)S(1)} %product_1.4.field_ref), channel_id=1, source_target_pairs={{0,4},{4,0},{8,12},{12,8},{16,20},{20,16},{24,28},{28,24},{1,5},{5... | collective-permute-start | bytes 1179656 | tf_op jit(solution)/shard_map/ppermute | solution.py:376
  71.8 2.6 collective-permute-done.14.near_ref
  76.0 3.0 %collective-permute-start.17 = (bf16[768,256]{1,0:T(8,128)(2,1)S(1)}, bf16[768,256]{1,0:T(8,128)(2,1)S(1)}, u32[]{:S(2)}, u32[]{:S(2)}) collective-permute-start(bf16[768,256]{1,0:T(8,128)(2,1)S(1)} %product_1.5.field_ref), channel_id=1, source_target_pairs={{0,4},{4,0},{8,12},{12,8},{16,20},{20,16},{24,28},{28,24},{1,5},{5... | collective-permute-start | bytes 1179656 | tf_op jit(solution)/shard_map/ppermute | solution.py:376
  80.3 2.6 collective-permute-done.11.near_ref
  84.5 3.0 %collective-permute-start.20 = (bf16[768,256]{1,0:T(8,128)(2,1)S(1)}, bf16[768,256]{1,0:T(8,128)(2,1)S(1)}, u32[]{:S(2)}, u32[]{:S(2)}) collective-permute-start(bf16[768,256]{1,0:T(8,128)(2,1)S(1)} %product_1.6.field_ref), channel_id=1, source_target_pairs={{0,4},{4,0},{8,12},{12,8},{16,20},{20,16},{24,28},{28,24},{1,5},{5... | collective-permute-start | bytes 1179656 | tf_op jit(solution)/shard_map/ppermute | solution.py:376
  88.7 2.6 collective-permute-done.17.near_ref
  92.9 3.0 %collective-permute-start.22 = (bf16[768,256]{1,0:T(8,128)(2,1)S(1)}, bf16[768,256]{1,0:T(8,128)(2,1)S(1)}, u32[]{:S(2)}, u32[]{:S(2)}) collective-permute-start(bf16[768,256]{1,0:T(8,128)(2,1)S(1)} %product_1.7.field_ref), channel_id=1, source_target_pairs={{0,4},{4,0},{8,12},{12,8},{16,20},{20,16},{24,28},{28,24},{1,5},{5... | collective-permute-start | bytes 1179656 | tf_op jit(solution)/shard_map/ppermute | solution.py:376
  97.1 2.6 collective-permute-done.20.near_ref
  104.1 2.6 collective-permute-done.22.near_ref
  113.0 5.5 %collective-permute-done.23.far_ref = bf16[768,256]{1,0:T(8,128)(2,1)S(1)} collective-permute-done((bf16[768,256]{1,0:T(8,128)(2,1)S(1)}, bf16[768,256]{1,0:T(8,128)(2,1)S(1)}, u32[]{:S(2)}, u32[]{:S(2)}) %collective-permute-start.23) | collective-permute-done | bytes 393248 | tf_op jit(solution)/shard_map/ppermute | solution.py:334
  119.9 2.1 gram_own.1
  122.0 4.1 %collective-permute-done.29.refs_6_.refs_3_ = bf16[768,256]{1,0:T(8,128)(2,1)S(1)} collective-permute-done((bf16[768,256]{1,0:T(8,128)(2,1)S(1)}, bf16[768,256]{1,0:T(8,128)(2,1)S(1)}, u32[]{:S(2)}, u32[]{:S(2)}) %collective-permute-start.29) | collective-permute-done | bytes 393248 | tf_op jit(solution)/shard_map/ppermute | solution.py:304
  126.1 3.8 %collective-permute-start.35 = (bf16[384,1024]{1,0:T(8,128)(2,1)S(1)}, bf16[384,1024]{1,0:T(8,128)(2,1)S(1)}, u32[]{:S(2)}, u32[]{:S(2)}) collective-permute-start(bf16[384,1024]{1,0:T(8,128)(2,1)S(1)} %get-tuple-element.384), channel_id=1, source_target_pairs={{0,4},{4,0},{8,12},{12,8},{16,20},{20,16},{24,28},{28,24},{1,5},{5... | collective-permute-start | bytes 2359304 | tf_op jit(solution)/shard_map/ppermute | solution.py:400
  133.1 5.6 %collective-permute-done.32.refs_7_.refs_9_.refs_4_ = bf16[784,256]{1,0:T(8,128)(2,1)S(1)} collective-permute-done((bf16[784,256]{1,0:T(8,128)(2,1)S(1)}, bf16[784,256]{1,0:T(8,128)(2,1)S(1)}, u32[]{:S(2)}, u32[]{:S(2)}) %collective-permute-start.32) | collective-permute-done | bytes 401440 | tf_op jit(solution)/shard_map/ppermute | solution.py:304
  139.7 1.6 gram_pair.3
  141.4 4.1 %collective-permute-done.35.refs_1_ = bf16[384,1024]{1,0:T(8,128)(2,1)S(1)} collective-permute-done((bf16[384,1024]{1,0:T(8,128)(2,1)S(1)}, bf16[384,1024]{1,0:T(8,128)(2,1)S(1)}, u32[]{:S(2)}, u32[]{:S(2)}) %collective-permute-start.35) | collective-permute-done | bytes 786464 | tf_op jit(solution)/shard_map/ppermute | solution.py:400
  146.2 1.8 gram_pair.4
  148.0 1.8 collective-permute-start.37
  150.9 1.6 gram_pair.5
  152.8 9.1 %collective-permute-done.39.refs_1_ = bf16[256,1024]{1,0:T(8,128)(2,1)S(1)} collective-permute-done((bf16[256,1024]{1,0:T(8,128)(2,1)S(1)}, bf16[256,1024]{1,0:T(8,128)(2,1)S(1)}, u32[]{:S(2)}, u32[]{:S(2)}) %collective-permute-start.39) | collective-permute-done | bytes 524320 | tf_op jit(solution)/shard_map/ppermute | solution.py:400
  162.6 4.4 %collective-permute-done.38.refs_2_ = bf16[192,1024]{1,0:T(8,128)(2,1)S(1)} collective-permute-done((bf16[192,1024]{1,0:T(8,128)(2,1)S(1)}, bf16[192,1024]{1,0:T(8,128)(2,1)S(1)}, u32[]{:S(2)}, u32[]{:S(2)}) %collective-permute-start.38) | collective-permute-done | bytes 393248 | tf_op jit(solution)/shard_map/ppermute | solution.py:400
  168.3 2.1 collective-permute-start.40
  171.1 4.4 %collective-permute-done.42.refs_3_ = bf16[96,1024]{1,0:T(8,128)(2,1)S(1)} collective-permute-done((bf16[96,1024]{1,0:T(8,128)(2,1)S(1)}, bf16[96,1024]{1,0:T(8,128)(2,1)S(1)}, u32[]{:S(2)}, u32[]{:S(2)}) %collective-permute-start.42) | collective-permute-done | bytes 196640 | tf_op jit(solution)/shard_map/ppermute | solution.py:400
  176.2 6.4 %collective-permute-done.40.refs_2_ = bf16[144,1024]{1,0:T(8,128)(2,1)S(1)} collective-permute-done((bf16[144,1024]{1,0:T(8,128)(2,1)S(1)}, bf16[144,1024]{1,0:T(8,128)(2,1)S(1)}, u32[]{:S(2)}, u32[]{:S(2)}) %collective-permute-start.40) | collective-permute-done | bytes 294944 | tf_op jit(solution)/shard_map/ppermute | solution.py:400
  187.6 8.1 %collective-permute-done.46.refs_3_ = bf16[64,1024]{1,0:T(8,128)(2,1)S(1)} collective-permute-done((bf16[64,1024]{1,0:T(8,128)(2,1)S(1)}, bf16[64,1024]{1,0:T(8,128)(2,1)S(1)}, u32[]{:S(2)}, u32[]{:S(2)}) %collective-permute-start.46) | collective-permute-done | bytes 131104 | tf_op jit(solution)/shard_map/ppermute | solution.py:400
  197.9 2.7 collective-permute-start.51
  200.9 5.3 %collective-permute-done.48.lower_ref = bf16[64,1024]{1,0:T(8,128)(2,1)S(1)} collective-permute-done((bf16[64,1024]{1,0:T(8,128)(2,1)S(1)}, bf16[64,1024]{1,0:T(8,128)(2,1)S(1)}, u32[]{:S(2)}, u32[]{:S(2)}) %collective-permute-start.48) | collective-permute-done | bytes 131104 | tf_op jit(solution)/shard_map/ppermute | solution.py:400
  206.3 8.3 %collective-permute-done.47.refs_3_ = bf16[64,1024]{1,0:T(8,128)(2,1)S(1)} collective-permute-done((bf16[64,1024]{1,0:T(8,128)(2,1)S(1)}, bf16[64,1024]{1,0:T(8,128)(2,1)S(1)}, u32[]{:S(2)}, u32[]{:S(2)}) %collective-permute-start.47) | collective-permute-done | bytes 131104 | tf_op jit(solution)/shard_map/ppermute | solution.py:400
  215.3 2.9 %collective-permute-start.50 = (bf16[64,1024]{1,0:T(8,128)(2,1)S(1)}, bf16[64,1024]{1,0:T(8,128)(2,1)S(1)}, u32[]{:S(2)}, u32[]{:S(2)}) collective-permute-start(bf16[64,1024]{1,0:T(8,128)(2,1)S(1)} %get-tuple-element.475.upper_ref), channel_id=1, source_target_pairs={{0,16},{4,20},{8,24},{12,28},{16,0},{20,4},{24,8},{28,12},{1,17},{... | collective-permute-start | bytes 393224 | tf_op jit(solution)/shard_map/ppermute | solution.py:400
  218.4 10.6 %collective-permute-done.49.lower_ref = bf16[64,1024]{1,0:T(8,128)(2,1)S(1)} collective-permute-done((bf16[64,1024]{1,0:T(8,128)(2,1)S(1)}, bf16[64,1024]{1,0:T(8,128)(2,1)S(1)}, u32[]{:S(2)}, u32[]{:S(2)}) %collective-permute-start.49) | collective-permute-done | bytes 131104 | tf_op jit(solution)/shard_map/ppermute | solution.py:400
  229.1 1.6 collective-permute-done.50.lower_ref
  230.9 2.4 collective-permute-start.53
  233.2 2.2 collective-permute-done.56.lower_ref
  237.8 2.6 collective-permute-start.63
  240.4 4.0 %collective-permute-done.53.refs_5_ = bf16[256,1024]{1,0:T(8,128)(2,1)S(1)} collective-permute-done((bf16[256,1024]{1,0:T(8,128)(2,1)S(1)}, bf16[256,1024]{1,0:T(8,128)(2,1)S(1)}, u32[]{:S(2)}, u32[]{:S(2)}) %collective-permute-start.53) | collective-permute-done | bytes 524320 | tf_op jit(solution)/shard_map/ppermute | solution.py:400
  244.3 2.4 collective-permute-start.62
  247.7 1.7 collective-permute-start.55
  249.3 6.3 %collective-permute-done.63.refs_7_ = bf16[256,1024]{1,0:T(8,128)(2,1)S(1)} collective-permute-done((bf16[256,1024]{1,0:T(8,128)(2,1)S(1)}, bf16[256,1024]{1,0:T(8,128)(2,1)S(1)}, u32[]{:S(2)}, u32[]{:S(2)}) %collective-permute-start.63) | collective-permute-done | bytes 524320 | tf_op jit(solution)/shard_map/ppermute | solution.py:400
  255.6 1.9 collective-permute-start.60
  257.5 2.4 collective-permute-done.64.refs_8_
  259.9 9.2 %collective-permute-done.62.refs_6_ = bf16[384,1024]{1,0:T(8,128)(2,1)S(1)} collective-permute-done((bf16[384,1024]{1,0:T(8,128)(2,1)S(1)}, bf16[384,1024]{1,0:T(8,128)(2,1)S(1)}, u32[]{:S(2)}, u32[]{:S(2)}) %collective-permute-start.62) | collective-permute-done | bytes 786464 | tf_op jit(solution)/shard_map/ppermute | solution.py:400
  269.2 2.6 mix_pair.3.refs_0_
  271.8 2.9 %mix_pair.4.refs_0_ = f32[768,1024]{1,0:T(8,128)S(1)} custom-call(s32[2]{0:T(128)S(1)} %get-tuple-element.385.where_ref, f32[768,1024]{1,0:T(8,128)S(1)} %mix_pair.3.refs_0_, bf16[768,256]{1,0:T(8,128)(2,1)S(1)} %collective-permute-done.25.refs_4_.refs_1_, ...), custom_call_target="tpu_custom_call", output_to_operand_aliasing={{}: (1, {})} | custom-call | flops 1024 | bytes 5242880 | tf_op jit(solution)/shard_map/mix_pair/pallas_call | solution.py:96
  274.7 2.6 mix_own.1.refs_1_
  277.3 4.0 %mix_pair.5 = bf16[768,1024]{1,0:T(8,128)(2,1)} custom-call(s32[2]{0:T(128)S(1)} %get-tuple-element.385.where_ref, f32[8,128]{1,0:T(8,128)S(1)} %get-tuple-element.462.refs_4_.refs_0_, f32[768,1024]{1,0:T(8,128)S(1)} %mix_own.1.refs_1_, bf16[768,256]{1,0:T(8,128)(2,1)S(1)} %collective-permute-done.26.refs_4_.refs_2_, ...), custom_call_target="tpu_custom_call" | custom-call | flops 1024 | bytes 5242880 | tf_op jit(solution)/shard_map/mix_pair/pallas_call | solution.py:96
  (123 shorter events, 60.4 us)
Async XLA Ops:
  1.5 12.4 %collective-permute-start = (bf16[768,256]{1,0:T(8,128)(2,1)S(1)}, bf16[768,256]{1,0:T(8,128)(2,1)S(1)}, u32[]{:S(2)}, u32[]{:S(2)}) collective-permute-start(bf16[768,256]{1,0:T(8,128)(2,1)S(1)} %get-tuple-element.511.field_ref.refs_0_), channel_id=1, source_target_pairs={{0,4},{4,0},{8,12},{12,8},{16,20},{20,16},{24,28},{28,24},{1,5},{5... | collective-permute-start | bytes 1179656 | tf_op jit(solution)/shard_map/ppermute | solution.py:317
  11.8 12.0 %collective-permute-start.2 = (bf16[768,256]{1,0:T(8,128)(2,1)S(1)}, bf16[768,256]{1,0:T(8,128)(2,1)S(1)}, u32[]{:S(2)}, u32[]{:S(2)}) collective-permute-start(bf16[768,256]{1,0:T(8,128)(2,1)S(1)} %get-tuple-element.265.field_ref.refs_0_), channel_id=1, source_target_pairs={{0,4},{4,0},{8,12},{12,8},{16,20},{20,16},{24,28},{28,24},{1,5},{5... | collective-permute-start | bytes 1179656 | tf_op jit(solution)/shard_map/ppermute | solution.py:325
  13.9 14.5 %collective-permute-start.1 = (bf16[768,256]{1,0:T(8,128)(2,1)S(1)}, bf16[768,256]{1,0:T(8,128)(2,1)S(1)}, u32[]{:S(2)}, u32[]{:S(2)}) collective-permute-start(bf16[768,256]{1,0:T(8,128)(2,1)S(1)} %collective-permute-done.near_ref), channel_id=1, source_target_pairs={{0,8},{4,28},{8,16},{12,4},{16,24},{20,12},{24,0},{28,20},{1,9},{5... | collective-permute-start | bytes 1179656 | tf_op jit(solution)/shard_map/ppermute | solution.py:334
  15.5 16.8 %collective-permute-start.4 = (bf16[768,256]{1,0:T(8,128)(2,1)S(1)}, bf16[768,256]{1,0:T(8,128)(2,1)S(1)}, u32[]{:S(2)}, u32[]{:S(2)}) collective-permute-start(bf16[768,256]{1,0:T(8,128)(2,1)S(1)} %get-tuple-element.273.field_ref.refs_0_), channel_id=1, source_target_pairs={{0,4},{4,0},{8,12},{12,8},{16,20},{20,16},{24,28},{28,24},{1,5},{5... | collective-permute-start | bytes 1179656 | tf_op jit(solution)/shard_map/ppermute | solution.py:325
  23.9 13.0 %collective-permute-start.7 = (bf16[768,256]{1,0:T(8,128)(2,1)S(1)}, bf16[768,256]{1,0:T(8,128)(2,1)S(1)}, u32[]{:S(2)}, u32[]{:S(2)}) collective-permute-start(bf16[768,256]{1,0:T(8,128)(2,1)S(1)} %collective-permute-done.2.near_ref), channel_id=1, source_target_pairs={{0,8},{4,28},{8,16},{12,4},{16,24},{20,12},{24,0},{28,20},{1,9},{5... | collective-permute-start | bytes 1179656 | tf_op jit(solution)/shard_map/ppermute | solution.py:334
  25.5 15.3 %collective-permute-start.6 = (bf16[768,256]{1,0:T(8,128)(2,1)S(1)}, bf16[768,256]{1,0:T(8,128)(2,1)S(1)}, u32[]{:S(2)}, u32[]{:S(2)}) collective-permute-start(bf16[768,256]{1,0:T(8,128)(2,1)S(1)} %get-tuple-element.276.field_ref.refs_0_), channel_id=1, source_target_pairs={{0,4},{4,0},{8,12},{12,8},{16,20},{20,16},{24,28},{28,24},{1,5},{5... | collective-permute-start | bytes 1179656 | tf_op jit(solution)/shard_map/ppermute | solution.py:325
  32.3 13.0 %collective-permute-start.5 = (bf16[768,256]{1,0:T(8,128)(2,1)S(1)}, bf16[768,256]{1,0:T(8,128)(2,1)S(1)}, u32[]{:S(2)}, u32[]{:S(2)}) collective-permute-start(bf16[768,256]{1,0:T(8,128)(2,1)S(1)} %collective-permute-done.4.near_ref), channel_id=1, source_target_pairs={{0,8},{4,28},{8,16},{12,4},{16,24},{20,12},{24,0},{28,20},{1,9},{5... | collective-permute-start | bytes 1179656 | tf_op jit(solution)/shard_map/ppermute | solution.py:334
  33.9 15.3 %collective-permute-start.3 = (bf16[768,256]{1,0:T(8,128)(2,1)S(1)}, bf16[768,256]{1,0:T(8,128)(2,1)S(1)}, u32[]{:S(2)}, u32[]{:S(2)}) collective-permute-start(bf16[768,256]{1,0:T(8,128)(2,1)S(1)} %get-tuple-element.272.field_ref), channel_id=1, source_target_pairs={{0,4},{4,0},{8,12},{12,8},{16,20},{20,16},{24,28},{28,24},{1,5},{5... | collective-permute-start | bytes 1179656 | tf_op jit(solution)/shard_map/ppermute | solution.py:376
  40.7 13.0 %collective-permute-start.10 = (bf16[768,256]{1,0:T(8,128)(2,1)S(1)}, bf16[768,256]{1,0:T(8,128)(2,1)S(1)}, u32[]{:S(2)}, u32[]{:S(2)}) collective-permute-start(bf16[768,256]{1,0:T(8,128)(2,1)S(1)} %collective-permute-done.6.near_ref), channel_id=1, source_target_pairs={{0,8},{4,28},{8,16},{12,4},{16,24},{20,12},{24,0},{28,20},{1,9},{5... | collective-permute-start | bytes 1179656 | tf_op jit(solution)/shard_map/ppermute | solution.py:334
  42.3 15.3 %collective-permute-start.9 = (bf16[768,256]{1,0:T(8,128)(2,1)S(1)}, bf16[768,256]{1,0:T(8,128)(2,1)S(1)}, u32[]{:S(2)}, u32[]{:S(2)}) collective-permute-start(bf16[768,256]{1,0:T(8,128)(2,1)S(1)} %get-tuple-element.291.field_ref), channel_id=1, source_target_pairs={{0,4},{4,0},{8,12},{12,8},{16,20},{20,16},{24,28},{28,24},{1,5},{5... | collective-permute-start | bytes 1179656 | tf_op jit(solution)/shard_map/ppermute | solution.py:376
  49.2 13.0 %collective-permute-start.8 = (bf16[768,256]{1,0:T(8,128)(2,1)S(1)}, bf16[768,256]{1,0:T(8,128)(2,1)S(1)}, u32[]{:S(2)}, u32[]{:S(2)}) collective-permute-start(bf16[768,256]{1,0:T(8,128)(2,1)S(1)} %collective-permute-done.3.near_ref), channel_id=1, source_target_pairs={{0,8},{4,28},{8,16},{12,4},{16,24},{20,12},{24,0},{28,20},{1,9},{5... | collective-permute-start | bytes 1179656 | tf_op jit(solution)/shard_map/ppermute | solution.py:334
  50.7 15.3 %collective-permute-start.12 = (bf16[768,256]{1,0:T(8,128)(2,1)S(1)}, bf16[768,256]{1,0:T(8,128)(2,1)S(1)}, u32[]{:S(2)}, u32[]{:S(2)}) collective-permute-start(bf16[768,256]{1,0:T(8,128)(2,1)S(1)} %get-tuple-element.303.field_ref), channel_id=1, source_target_pairs={{0,4},{4,0},{8,12},{12,8},{16,20},{20,16},{24,28},{28,24},{1,5},{5... | collective-permute-start | bytes 1179656 | tf_op jit(solution)/shard_map/ppermute | solution.py:376
  57.6 13.0 %collective-permute-start.15 = (bf16[768,256]{1,0:T(8,128)(2,1)S(1)}, bf16[768,256]{1,0:T(8,128)(2,1)S(1)}, u32[]{:S(2)}, u32[]{:S(2)}) collective-permute-start(bf16[768,256]{1,0:T(8,128)(2,1)S(1)} %collective-permute-done.9.near_ref), channel_id=1, source_target_pairs={{0,8},{4,28},{8,16},{12,4},{16,24},{20,12},{24,0},{28,20},{1,9},{5... | collective-permute-start | bytes 1179656 | tf_op jit(solution)/shard_map/ppermute | solution.py:334
  59.2 15.3 %collective-permute-start.14 = (bf16[768,256]{1,0:T(8,128)(2,1)S(1)}, bf16[768,256]{1,0:T(8,128)(2,1)S(1)}, u32[]{:S(2)}, u32[]{:S(2)}) collective-permute-start(bf16[768,256]{1,0:T(8,128)(2,1)S(1)} %get-tuple-element.306.field_ref), channel_id=1, source_target_pairs={{0,4},{4,0},{8,12},{12,8},{16,20},{20,16},{24,28},{28,24},{1,5},{5... | collective-permute-start | bytes 1179656 | tf_op jit(solution)/shard_map/ppermute | solution.py:376
  66.0 13.0 %collective-permute-start.13 = (bf16[768,256]{1,0:T(8,128)(2,1)S(1)}, bf16[768,256]{1,0:T(8,128)(2,1)S(1)}, u32[]{:S(2)}, u32[]{:S(2)}) collective-permute-start(bf16[768,256]{1,0:T(8,128)(2,1)S(1)} %collective-permute-done.12.near_ref), channel_id=1, source_target_pairs={{0,8},{4,28},{8,16},{12,4},{16,24},{20,12},{24,0},{28,20},{1,9},{5... | collective-permute-start | bytes 1179656 | tf_op jit(solution)/shard_map/ppermute | solution.py:334
  67.6 15.3 %collective-permute-start.11 = (bf16[768,256]{1,0:T(8,128)(2,1)S(1)}, bf16[768,256]{1,0:T(8,128)(2,1)S(1)}, u32[]{:S(2)}, u32[]{:S(2)}) collective-permute-start(bf16[768,256]{1,0:T(8,128)(2,1)S(1)} %product_1.4.field_ref), channel_id=1, source_target_pairs={{0,4},{4,0},{8,12},{12,8},{16,20},{20,16},{24,28},{28,24},{1,5},{5... | collective-permute-start | bytes 1179656 | tf_op jit(solution)/shard_map/ppermute | solution.py:376
  74.4 13.0 %collective-permute-start.18 = (bf16[768,256]{1,0:T(8,128)(2,1)S(1)}, bf16[768,256]{1,0:T(8,128)(2,1)S(1)}, u32[]{:S(2)}, u32[]{:S(2)}) collective-permute-start(bf16[768,256]{1,0:T(8,128)(2,1)S(1)} %collective-permute-done.14.near_ref), channel_id=1, source_target_pairs={{0,8},{4,28},{8,16},{12,4},{16,24},{20,12},{24,0},{28,20},{1,9},{5... | collective-permute-start | bytes 1179656 | tf_op jit(solution)/shard_map/ppermute | solution.py:334
  76.0 15.3 %collective-permute-start.17 = (bf16[768,256]{1,0:T(8,128)(2,1)S(1)}, bf16[768,256]{1,0:T(8,128)(2,1)S(1)}, u32[]{:S(2)}, u32[]{:S(2)}) collective-permute-start(bf16[768,256]{1,0:T(8,128)(2,1)S(1)} %product_1.5.field_ref), channel_id=1, source_target_pairs={{0,4},{4,0},{8,12},{12,8},{16,20},{20,16},{24,28},{28,24},{1,5},{5... | collective-permute-start | bytes 1179656 | tf_op jit(solution)/shard_map/ppermute | solution.py:376
  82.9 13.0 %collective-permute-start.16 = (bf16[768,256]{1,0:T(8,128)(2,1)S(1)}, bf16[768,256]{1,0:T(8,128)(2,1)S(1)}, u32[]{:S(2)}, u32[]{:S(2)}) collective-permute-start(bf16[768,256]{1,0:T(8,128)(2,1)S(1)} %collective-permute-done.11.near_ref), channel_id=1, source_target_pairs={{0,8},{4,28},{8,16},{12,4},{16,24},{20,12},{24,0},{28,20},{1,9},{5... | collective-permute-start | bytes 1179656 | tf_op jit(solution)/shard_map/ppermute | solution.py:334
  84.5 15.3 %collective-permute-start.20 = (bf16[768,256]{1,0:T(8,128)(2,1)S(1)}, bf16[768,256]{1,0:T(8,128)(2,1)S(1)}, u32[]{:S(2)}, u32[]{:S(2)}) collective-permute-start(bf16[768,256]{1,0:T(8,128)(2,1)S(1)} %product_1.6.field_ref), channel_id=1, source_target_pairs={{0,4},{4,0},{8,12},{12,8},{16,20},{20,16},{24,28},{28,24},{1,5},{5... | collective-permute-start | bytes 1179656 | tf_op jit(solution)/shard_map/ppermute | solution.py:376
  91.3 11.5 %collective-permute-start.19 = (bf16[768,256]{1,0:T(8,128)(2,1)S(1)}, bf16[768,256]{1,0:T(8,128)(2,1)S(1)}, u32[]{:S(2)}, u32[]{:S(2)}) collective-permute-start(bf16[768,256]{1,0:T(8,128)(2,1)S(1)} %collective-permute-done.17.near_ref), channel_id=1, source_target_pairs={{0,8},{4,28},{8,16},{12,4},{16,24},{20,12},{24,0},{28,20},{1,9},{5... | collective-permute-start | bytes 1179656 | tf_op jit(solution)/shard_map/ppermute | solution.py:334
  92.9 13.8 %collective-permute-start.22 = (bf16[768,256]{1,0:T(8,128)(2,1)S(1)}, bf16[768,256]{1,0:T(8,128)(2,1)S(1)}, u32[]{:S(2)}, u32[]{:S(2)}) collective-permute-start(bf16[768,256]{1,0:T(8,128)(2,1)S(1)} %product_1.7.field_ref), channel_id=1, source_target_pairs={{0,4},{4,0},{8,12},{12,8},{16,20},{20,16},{24,28},{28,24},{1,5},{5... | collective-permute-start | bytes 1179656 | tf_op jit(solution)/shard_map/ppermute | solution.py:376
  99.7 10.4 %collective-permute-start.21 = (bf16[768,256]{1,0:T(8,128)(2,1)S(1)}, bf16[768,256]{1,0:T(8,128)(2,1)S(1)}, u32[]{:S(2)}, u32[]{:S(2)}) collective-permute-start(bf16[768,256]{1,0:T(8,128)(2,1)S(1)} %collective-permute-done.20.near_ref), channel_id=1, source_target_pairs={{0,8},{4,28},{8,16},{12,4},{16,24},{20,12},{24,0},{28,20},{1,9},{5... | collective-permute-start | bytes 1179656 | tf_op jit(solution)/shard_map/ppermute | solution.py:334
  101.3 10.2 %collective-permute-start.25 = (bf16[768,256]{1,0:T(8,128)(2,1)S(1)}, bf16[768,256]{1,0:T(8,128)(2,1)S(1)}, u32[]{:S(2)}, u32[]{:S(2)}) collective-permute-start(bf16[768,256]{1,0:T(8,128)(2,1)S(1)} %get-tuple-element.329.refs_0_.refs_1_.refs_10_), channel_id=1, source_target_pairs={{0,2},{1,3},{2,0},{3,1},{4,6},{5,7},{6,4},{7,5},{8,10},{9,11},{10,... | collective-permute-start | bytes 1179656 | tf_op jit(solution)/shard_map/ppermute | solution.py:304
  102.8 10.2 %collective-permute-start.24 = (bf16[768,256]{1,0:T(8,128)(2,1)S(1)}, bf16[768,256]{1,0:T(8,128)(2,1)S(1)}, u32[]{:S(2)}, u32[]{:S(2)}) collective-permute-start(bf16[768,256]{1,0:T(8,128)(2,1)S(1)} %get-tuple-element.329.refs_0_.refs_1_.refs_10_), channel_id=1, source_target_pairs={{0,1},{1,0},{2,3},{3,2},{4,5},{5,4},{6,7},{7,6},{8,9},{9,8},{10,11... | collective-permute-start | bytes 1179656 | tf_op jit(solution)/shard_map/ppermute | solution.py:304
  106.7 11.7 %collective-permute-start.23 = (bf16[768,256]{1,0:T(8,128)(2,1)S(1)}, bf16[768,256]{1,0:T(8,128)(2,1)S(1)}, u32[]{:S(2)}, u32[]{:S(2)}) collective-permute-start(bf16[768,256]{1,0:T(8,128)(2,1)S(1)} %collective-permute-done.22.near_ref), channel_id=1, source_target_pairs={{0,8},{4,28},{8,16},{12,4},{16,24},{20,12},{24,0},{28,20},{1,9},{5... | collective-permute-start | bytes 1179656 | tf_op jit(solution)/shard_map/ppermute | solution.py:334
  108.3 13.7 %collective-permute-start.27 = (bf16[768,256]{1,0:T(8,128)(2,1)S(1)}, bf16[768,256]{1,0:T(8,128)(2,1)S(1)}, u32[]{:S(2)}, u32[]{:S(2)}) collective-permute-start(bf16[768,256]{1,0:T(8,128)(2,1)S(1)} %get-tuple-element.340.refs_1_.refs_2_.refs_11_), channel_id=1, source_target_pairs={{0,2},{1,3},{2,0},{3,1},{4,6},{5,7},{6,4},{7,5},{8,10},{9,11},{10,... | collective-permute-start | bytes 1179656 | tf_op jit(solution)/shard_map/ppermute | solution.py:304
  110.1 11.8 %collective-permute-start.30 = (bf16[768,256]{1,0:T(8,128)(2,1)S(1)}, bf16[768,256]{1,0:T(8,128)(2,1)S(1)}, u32[]{:S(2)}, u32[]{:S(2)}) collective-permute-start(bf16[768,256]{1,0:T(8,128)(2,1)S(1)} %get-tuple-element.340.refs_1_.refs_2_.refs_11_), channel_id=1, source_target_pairs={{0,1},{1,0},{2,3},{3,2},{4,5},{5,4},{6,7},{7,6},{8,9},{9,8},{10,11... | collective-permute-start | bytes 1179656 | tf_op jit(solution)/shard_map/ppermute | solution.py:304
  111.5 14.6 %collective-permute-start.29 = (bf16[768,256]{1,0:T(8,128)(2,1)S(1)}, bf16[768,256]{1,0:T(8,128)(2,1)S(1)}, u32[]{:S(2)}, u32[]{:S(2)}) collective-permute-start(bf16[768,256]{1,0:T(8,128)(2,1)S(1)} %get-tuple-element.351.refs_2_.refs_3_.refs_12_), channel_id=1, source_target_pairs={{0,2},{1,3},{2,0},{3,1},{4,6},{5,7},{6,4},{7,5},{8,10},{9,11},{10,... | collective-permute-start | bytes 1179656 | tf_op jit(solution)/shard_map/ppermute | solution.py:304
  126.1 19.4 %collective-permute-start.35 = (bf16[384,1024]{1,0:T(8,128)(2,1)S(1)}, bf16[384,1024]{1,0:T(8,128)(2,1)S(1)}, u32[]{:S(2)}, u32[]{:S(2)}) collective-permute-start(bf16[384,1024]{1,0:T(8,128)(2,1)S(1)} %get-tuple-element.384), channel_id=1, source_target_pairs={{0,4},{4,0},{8,12},{12,8},{16,20},{20,16},{24,28},{28,24},{1,5},{5... | collective-permute-start | bytes 2359304 | tf_op jit(solution)/shard_map/ppermute | solution.py:400
  129.9 8.8 %collective-permute-start.32 = (bf16[784,256]{1,0:T(8,128)(2,1)S(1)}, bf16[784,256]{1,0:T(8,128)(2,1)S(1)}, u32[]{:S(2)}, u32[]{:S(2)}) collective-permute-start(bf16[784,256]{1,0:T(8,128)(2,1)S(1)} %product_2.7.refs_3_.refs_4_.refs_13_), channel_id=1, source_target_pairs={{0,2},{1,3},{2,0},{3,1},{4,6},{5,7},{6,4},{7,5},{8,10},{9,11},{10,... | collective-permute-start | bytes 1204232 | tf_op jit(solution)/shard_map/ppermute | solution.py:304
  131.4 7.8 %collective-permute-start.36 = (bf16[784,256]{1,0:T(8,128)(2,1)S(1)}, bf16[784,256]{1,0:T(8,128)(2,1)S(1)}, u32[]{:S(2)}, u32[]{:S(2)}) collective-permute-start(bf16[784,256]{1,0:T(8,128)(2,1)S(1)} %product_2.7.refs_3_.refs_4_.refs_13_), channel_id=1, source_target_pairs={{0,1},{1,0},{2,3},{3,2},{4,5},{5,4},{6,7},{7,6},{8,9},{9,8},{10,11... | collective-permute-start | bytes 1204232 | tf_op jit(solution)/shard_map/ppermute | solution.py:304
  138.7 7.5 %collective-permute-start.34 = (bf16[784,256]{1,0:T(8,128)(2,1)S(1)}, bf16[784,256]{1,0:T(8,128)(2,1)S(1)}, u32[]{:S(2)}, u32[]{:S(2)}) collective-permute-start(bf16[784,256]{1,0:T(8,128)(2,1)S(1)} %collective-permute-done.32.refs_7_.refs_9_.refs_4_), channel_id=1, source_target_pairs={{0,1},{1,0},{2,3},{3,2},{4,5},{5,4},{6,7},{7,6},{8,9},{9,8},{10,11... | collective-permute-start | bytes 1204232 | tf_op jit(solution)/shard_map/ppermute | solution.py:304
  138.7 7.4 %collective-permute-start.26 = (bf16[768,256]{1,0:T(8,128)(2,1)S(1)}, bf16[768,256]{1,0:T(8,128)(2,1)S(1)}, u32[]{:S(2)}, u32[]{:S(2)}) collective-permute-start(bf16[768,256]{1,0:T(8,128)(2,1)S(1)} %collective-permute-done.25.refs_4_.refs_1_), channel_id=1, source_target_pairs={{0,1},{1,0},{2,3},{3,2},{4,5},{5,4},{6,7},{7,6},{8,9},{9,8},{10,11... | collective-permute-start | bytes 1179656 | tf_op jit(solution)/shard_map/ppermute | solution.py:304
  139.2 6.9 %collective-permute-start.28 = (bf16[768,256]{1,0:T(8,128)(2,1)S(1)}, bf16[768,256]{1,0:T(8,128)(2,1)S(1)}, u32[]{:S(2)}, u32[]{:S(2)}) collective-permute-start(bf16[768,256]{1,0:T(8,128)(2,1)S(1)} %collective-permute-done.27.refs_5_.refs_2_), channel_id=1, source_target_pairs={{0,1},{1,0},{2,3},{3,2},{4,5},{5,4},{6,7},{7,6},{8,9},{9,8},{10,11... | collective-permute-start | bytes 1179656 | tf_op jit(solution)/shard_map/ppermute | solution.py:304
  139.2 7.0 %collective-permute-start.31 = (bf16[768,256]{1,0:T(8,128)(2,1)S(1)}, bf16[768,256]{1,0:T(8,128)(2,1)S(1)}, u32[]{:S(2)}, u32[]{:S(2)}) collective-permute-start(bf16[768,256]{1,0:T(8,128)(2,1)S(1)} %collective-permute-done.29.refs_6_.refs_3_), channel_id=1, source_target_pairs={{0,1},{1,0},{2,3},{3,2},{4,5},{5,4},{6,7},{7,6},{8,9},{9,8},{10,11... | collective-permute-start | bytes 1179656 | tf_op jit(solution)/shard_map/ppermute | solution.py:304
  145.5 16.4 %collective-permute-start.39 = (bf16[256,1024]{1,0:T(8,128)(2,1)S(1)}, bf16[256,1024]{1,0:T(8,128)(2,1)S(1)}, u32[]{:S(2)}, u32[]{:S(2)}) collective-permute-start(bf16[256,1024]{1,0:T(8,128)(2,1)S(1)} %get-tuple-element.415), channel_id=1, source_target_pairs={{0,8},{4,12},{8,0},{12,4},{16,24},{20,28},{24,16},{28,20},{1,9},{5... | collective-permute-start | bytes 1572872 | tf_op jit(solution)/shard_map/ppermute | solution.py:400
  148.0 19.6 %collective-permute-start.37 = (bf16[272,1024]{1,0:T(8,128)(2,1)S(1)}, bf16[272,1024]{1,0:T(8,128)(2,1)S(1)}, u32[]{:S(2)}, u32[]{:S(2)}) collective-permute-start(bf16[272,1024]{1,0:T(8,128)(2,1)S(1)} %get-tuple-element.412), channel_id=1, source_target_pairs={{0,4},{4,0},{8,12},{12,8},{16,20},{20,16},{24,28},{28,24},{1,5},{5... | collective-permute-start | bytes 1671176 | tf_op jit(solution)/shard_map/ppermute | solution.py:400
  149.8 17.1 %collective-permute-start.38 = (bf16[192,1024]{1,0:T(8,128)(2,1)S(1)}, bf16[192,1024]{1,0:T(8,128)(2,1)S(1)}, u32[]{:S(2)}, u32[]{:S(2)}) collective-permute-start(bf16[192,1024]{1,0:T(8,128)(2,1)S(1)} %sum_hop.8), channel_id=1, source_target_pairs={{0,16},{4,20},{8,24},{12,28},{16,0},{20,4},{24,8},{28,12},{1,17},{... | collective-permute-start | bytes 1179656 | tf_op jit(solution)/shard_map/ppermute | solution.py:400
  152.5 23.0 %collective-permute-start.41 = (bf16[256,1024]{1,0:T(8,128)(2,1)S(1)}, bf16[256,1024]{1,0:T(8,128)(2,1)S(1)}, u32[]{:S(2)}, u32[]{:S(2)}) collective-permute-start(bf16[256,1024]{1,0:T(8,128)(2,1)S(1)} %get-tuple-element.439), channel_id=1, source_target_pairs={{0,4},{4,0},{8,12},{12,8},{16,20},{20,16},{24,28},{28,24},{1,5},{5... | collective-permute-start | bytes 1572872 | tf_op jit(solution)/shard_map/ppermute | solution.py:400
  167.6 7.9 %collective-permute-start.42 = (bf16[96,1024]{1,0:T(8,128)(2,1)S(1)}, bf16[96,1024]{1,0:T(8,128)(2,1)S(1)}, u32[]{:S(2)}, u32[]{:S(2)}) collective-permute-start(bf16[96,1024]{1,0:T(8,128)(2,1)S(1)} %sum_hop.10), channel_id=1, source_target_pairs={{0,8},{4,12},{8,0},{12,4},{16,24},{20,28},{24,16},{28,20},{1,9},{5... | collective-permute-start | bytes 589832 | tf_op jit(solution)/shard_map/ppermute | solution.py:400
  168.3 14.3 %collective-permute-start.40 = (bf16[144,1024]{1,0:T(8,128)(2,1)S(1)}, bf16[144,1024]{1,0:T(8,128)(2,1)S(1)}, u32[]{:S(2)}, u32[]{:S(2)}) collective-permute-start(bf16[144,1024]{1,0:T(8,128)(2,1)S(1)} %sum_hop.11), channel_id=1, source_target_pairs={{0,8},{4,12},{8,0},{12,4},{16,24},{20,28},{24,16},{28,20},{1,9},{5... | collective-permute-start | bytes 884744 | tf_op jit(solution)/shard_map/ppermute | solution.py:400
  170.4 13.0 %collective-permute-start.45 = (bf16[128,1024]{1,0:T(8,128)(2,1)S(1)}, bf16[128,1024]{1,0:T(8,128)(2,1)S(1)}, u32[]{:S(2)}, u32[]{:S(2)}) collective-permute-start(bf16[128,1024]{1,0:T(8,128)(2,1)S(1)} %sum_hop.9), channel_id=1, source_target_pairs={{0,4},{4,0},{8,12},{12,8},{16,20},{20,16},{24,28},{28,24},{1,5},{5... | collective-permute-start | bytes 786440 | tf_op jit(solution)/shard_map/ppermute | solution.py:400
  176.1 9.4 %collective-permute-start.44 = (bf16[128,1024]{1,0:T(8,128)(2,1)S(1)}, bf16[128,1024]{1,0:T(8,128)(2,1)S(1)}, u32[]{:S(2)}, u32[]{:S(2)}) collective-permute-start(bf16[128,1024]{1,0:T(8,128)(2,1)S(1)} %sum_hop.12), channel_id=1, source_target_pairs={{0,8},{4,12},{8,0},{12,4},{16,24},{20,28},{24,16},{28,20},{1,9},{5... | collective-permute-start | bytes 786440 | tf_op jit(solution)/shard_map/ppermute | solution.py:400
  183.3 12.4 %collective-permute-start.43 = (bf16[80,1024]{1,0:T(8,128)(2,1)S(1)}, bf16[80,1024]{1,0:T(8,128)(2,1)S(1)}, u32[]{:S(2)}, u32[]{:S(2)}) collective-permute-start(bf16[80,1024]{1,0:T(8,128)(2,1)S(1)} %sum_hop.13), channel_id=1, source_target_pairs={{0,16},{4,20},{8,24},{12,28},{16,0},{20,4},{24,8},{28,12},{1,17},{... | collective-permute-start | bytes 491528 | tf_op jit(solution)/shard_map/ppermute | solution.py:400
  186.1 9.6 %collective-permute-start.46 = (bf16[64,1024]{1,0:T(8,128)(2,1)S(1)}, bf16[64,1024]{1,0:T(8,128)(2,1)S(1)}, u32[]{:S(2)}, u32[]{:S(2)}) collective-permute-start(bf16[64,1024]{1,0:T(8,128)(2,1)S(1)} %sum_hop.15), channel_id=1, source_target_pairs={{0,16},{4,20},{8,24},{12,28},{16,0},{20,4},{24,8},{28,12},{1,17},{... | collective-permute-start | bytes 393224 | tf_op jit(solution)/shard_map/ppermute | solution.py:400
  197.1 9.2 %collective-permute-start.48 = (bf16[64,1024]{1,0:T(8,128)(2,1)S(1)}, bf16[64,1024]{1,0:T(8,128)(2,1)S(1)}, u32[]{:S(2)}, u32[]{:S(2)}) collective-permute-start(bf16[64,1024]{1,0:T(8,128)(2,1)S(1)} %sum_last.7.upper_ref), channel_id=1, source_target_pairs={{0,16},{4,20},{8,24},{12,28},{16,0},{20,4},{24,8},{28,12},{1,17},{... | collective-permute-start | bytes 393224 | tf_op jit(solution)/shard_map/ppermute | solution.py:400
  197.9 20.4 %collective-permute-start.51 = (bf16[96,1024]{1,0:T(8,128)(2,1)S(1)}, bf16[96,1024]{1,0:T(8,128)(2,1)S(1)}, u32[]{:S(2)}, u32[]{:S(2)}) collective-permute-start(bf16[96,1024]{1,0:T(8,128)(2,1)S(1)} %sum_last.5.upper_ref), channel_id=1, source_target_pairs={{0,8},{4,12},{8,0},{12,4},{16,24},{20,28},{24,16},{28,20},{1,9},{5... | collective-permute-start | bytes 589832 | tf_op jit(solution)/shard_map/ppermute | solution.py:400
  200.6 14.0 %collective-permute-start.47 = (bf16[64,1024]{1,0:T(8,128)(2,1)S(1)}, bf16[64,1024]{1,0:T(8,128)(2,1)S(1)}, u32[]{:S(2)}, u32[]{:S(2)}) collective-permute-start(bf16[64,1024]{1,0:T(8,128)(2,1)S(1)} %sum_hop.14), channel_id=1, source_target_pairs={{0,16},{4,20},{8,24},{12,28},{16,0},{20,4},{24,8},{28,12},{1,17},{... | collective-permute-start | bytes 393224 | tf_op jit(solution)/shard_map/ppermute | solution.py:400
  206.2 24.6 %collective-permute-start.52 = (bf16[128,1024]{1,0:T(8,128)(2,1)S(1)}, bf16[128,1024]{1,0:T(8,128)(2,1)S(1)}, u32[]{:S(2)}, u32[]{:S(2)}) collective-permute-start(bf16[128,1024]{1,0:T(8,128)(2,1)S(1)} %join.11.upper_ref), channel_id=1, source_target_pairs={{0,8},{4,12},{8,0},{12,4},{16,24},{20,28},{24,16},{28,20},{1,9},{5... | collective-permute-start | bytes 786440 | tf_op jit(solution)/shard_map/ppermute | solution.py:400
  215.3 13.7 %collective-permute-start.49 = (bf16[64,1024]{1,0:T(8,128)(2,1)S(1)}, bf16[64,1024]{1,0:T(8,128)(2,1)S(1)}, u32[]{:S(2)}, u32[]{:S(2)}) collective-permute-start(bf16[64,1024]{1,0:T(8,128)(2,1)S(1)} %sum_last.6.upper_ref), channel_id=1, source_target_pairs={{0,16},{4,20},{8,24},{12,28},{16,0},{20,4},{24,8},{28,12},{1,17},{... | collective-permute-start | bytes 393224 | tf_op jit(solution)/shard_map/ppermute | solution.py:400
  215.3 15.4 %collective-permute-start.50 = (bf16[64,1024]{1,0:T(8,128)(2,1)S(1)}, bf16[64,1024]{1,0:T(8,128)(2,1)S(1)}, u32[]{:S(2)}, u32[]{:S(2)}) collective-permute-start(bf16[64,1024]{1,0:T(8,128)(2,1)S(1)} %get-tuple-element.475.upper_ref), channel_id=1, source_target_pairs={{0,16},{4,20},{8,24},{12,28},{16,0},{20,4},{24,8},{28,12},{1,17},{... | collective-permute-start | bytes 393224 | tf_op jit(solution)/shard_map/ppermute | solution.py:400
  218.3 22.0 %collective-permute-start.61 = (bf16[192,1024]{1,0:T(8,128)(2,1)S(1)}, bf16[192,1024]{1,0:T(8,128)(2,1)S(1)}, u32[]{:S(2)}, u32[]{:S(2)}) collective-permute-start(bf16[192,1024]{1,0:T(8,128)(2,1)S(1)} %join.8.upper_ref), channel_id=1, source_target_pairs={{0,16},{4,20},{8,24},{12,28},{16,0},{20,4},{24,8},{28,12},{1,17},{... | collective-permute-start | bytes 1179656 | tf_op jit(solution)/shard_map/ppermute | solution.py:400
  230.7 7.0 %collective-permute-start.57 = (bf16[128,1024]{1,0:T(8,128)(2,1)S(1)}, bf16[128,1024]{1,0:T(8,128)(2,1)S(1)}, u32[]{:S(2)}, u32[]{:S(2)}) collective-permute-start(bf16[128,1024]{1,0:T(8,128)(2,1)S(1)} %join.9.upper_ref), channel_id=1, source_target_pairs={{0,8},{4,12},{8,0},{12,4},{16,24},{20,28},{24,16},{28,20},{1,9},{5... | collective-permute-start | bytes 786440 | tf_op jit(solution)/shard_map/ppermute | solution.py:400
  230.9 13.5 %collective-permute-start.53 = (bf16[256,1024]{1,0:T(8,128)(2,1)S(1)}, bf16[256,1024]{1,0:T(8,128)(2,1)S(1)}, u32[]{:S(2)}, u32[]{:S(2)}) collective-permute-start(bf16[256,1024]{1,0:T(8,128)(2,1)S(1)} %join.12.refs_4_), channel_id=1, source_target_pairs={{0,4},{4,0},{8,12},{12,8},{16,20},{20,16},{24,28},{28,24},{1,5},{5... | collective-permute-start | bytes 1572872 | tf_op jit(solution)/shard_map/ppermute | solution.py:400
  233.2 13.5 %collective-permute-start.54 = (bf16[256,1024]{1,0:T(8,128)(2,1)S(1)}, bf16[256,1024]{1,0:T(8,128)(2,1)S(1)}, u32[]{:S(2)}, u32[]{:S(2)}) collective-permute-start(bf16[256,1024]{1,0:T(8,128)(2,1)S(1)} %join.12.refs_4_), channel_id=1, source_target_pairs={{0,1},{1,0},{2,3},{3,2},{4,5},{5,4},{6,7},{7,6},{8,9},{9,8},{10,11... | collective-permute-start | bytes 1572872 | tf_op jit(solution)/shard_map/ppermute | solution.py:304
  235.5 12.2 %collective-permute-start.59 = (bf16[256,1024]{1,0:T(8,128)(2,1)S(1)}, bf16[256,1024]{1,0:T(8,128)(2,1)S(1)}, u32[]{:S(2)}, u32[]{:S(2)}) collective-permute-start(bf16[256,1024]{1,0:T(8,128)(2,1)S(1)} %join.14.refs_5_), channel_id=1, source_target_pairs={{0,2},{1,3},{2,0},{3,1},{4,6},{5,7},{6,4},{7,5},{8,10},{9,11},{10,... | collective-permute-start | bytes 1572872 | tf_op jit(solution)/shard_map/ppermute | solution.py:304
  237.8 17.8 %collective-permute-start.63 = (bf16[256,1024]{1,0:T(8,128)(2,1)S(1)}, bf16[256,1024]{1,0:T(8,128)(2,1)S(1)}, u32[]{:S(2)}, u32[]{:S(2)}) collective-permute-start(bf16[256,1024]{1,0:T(8,128)(2,1)S(1)} %join.13.refs_6_), channel_id=1, source_target_pairs={{0,4},{4,0},{8,12},{12,8},{16,20},{20,16},{24,28},{28,24},{1,5},{5... | collective-permute-start | bytes 1572872 | tf_op jit(solution)/shard_map/ppermute | solution.py:400
  240.3 17.2 %collective-permute-start.58 = (bf16[256,1024]{1,0:T(8,128)(2,1)S(1)}, bf16[256,1024]{1,0:T(8,128)(2,1)S(1)}, u32[]{:S(2)}, u32[]{:S(2)}) collective-permute-start(bf16[256,1024]{1,0:T(8,128)(2,1)S(1)} %join.14.refs_5_), channel_id=1, source_target_pairs={{0,8},{4,12},{8,0},{12,4},{16,24},{20,28},{24,16},{28,20},{1,9},{5... | collective-permute-start | bytes 1572872 | tf_op jit(solution)/shard_map/ppermute | solution.py:400
  244.3 24.8 %collective-permute-start.62 = (bf16[384,1024]{1,0:T(8,128)(2,1)S(1)}, bf16[384,1024]{1,0:T(8,128)(2,1)S(1)}, u32[]{:S(2)}, u32[]{:S(2)}) collective-permute-start(bf16[384,1024]{1,0:T(8,128)(2,1)S(1)} %join.15.refs_5_), channel_id=1, source_target_pairs={{0,4},{4,0},{8,12},{12,8},{16,20},{20,16},{24,28},{28,24},{1,5},{5... | collective-permute-start | bytes 2359304 | tf_op jit(solution)/shard_map/ppermute | solution.py:400
  246.7 13.2 %collective-permute-start.64 = (bf16[256,1024]{1,0:T(8,128)(2,1)S(1)}, bf16[256,1024]{1,0:T(8,128)(2,1)S(1)}, u32[]{:S(2)}, u32[]{:S(2)}) collective-permute-start(bf16[256,1024]{1,0:T(8,128)(2,1)S(1)} %join.13.refs_6_), channel_id=1, source_target_pairs={{0,3},{1,2},{2,1},{3,0},{4,7},{5,6},{6,5},{7,4},{8,11},{9,10},{10,... | collective-permute-start | bytes 1572872 | tf_op jit(solution)/shard_map/ppermute | solution.py:304
  247.7 12.3 %collective-permute-start.55 = (bf16[256,1024]{1,0:T(8,128)(2,1)S(1)}, bf16[256,1024]{1,0:T(8,128)(2,1)S(1)}, u32[]{:S(2)}, u32[]{:S(2)}) collective-permute-start(bf16[256,1024]{1,0:T(8,128)(2,1)S(1)} %collective-permute-done.53.refs_5_), channel_id=1, source_target_pairs={{0,1},{1,0},{2,3},{3,2},{4,5},{5,4},{6,7},{7,6},{8,9},{9,8},{10,11... | collective-permute-start | bytes 1572872 | tf_op jit(solution)/shard_map/ppermute | solution.py:304
  255.6 16.2 %collective-permute-start.60 = (bf16[256,1024]{1,0:T(8,128)(2,1)S(1)}, bf16[256,1024]{1,0:T(8,128)(2,1)S(1)}, u32[]{:S(2)}, u32[]{:S(2)}) collective-permute-start(bf16[256,1024]{1,0:T(8,128)(2,1)S(1)} %collective-permute-done.59.refs_7_), channel_id=1, source_target_pairs={{0,8},{4,12},{8,0},{12,4},{16,24},{20,28},{24,16},{28,20},{1,9},{5... | collective-permute-start | bytes 1572872 | tf_op jit(solution)/shard_map/ppermute | solution.py:400
  257.5 19.8 %collective-permute-start.65 = (bf16[256,1024]{1,0:T(8,128)(2,1)S(1)}, bf16[256,1024]{1,0:T(8,128)(2,1)S(1)}, u32[]{:S(2)}, u32[]{:S(2)}) collective-permute-start(bf16[256,1024]{1,0:T(8,128)(2,1)S(1)} %collective-permute-done.63.refs_7_), channel_id=1, source_target_pairs={{0,3},{1,2},{2,1},{3,0},{4,7},{5,6},{6,5},{7,4},{8,11},{9,10},{10,... | collective-permute-start | bytes 1572872 | tf_op jit(solution)/shard_map/ppermute | solution.py:304
  (3 other events, 14.4 us)
